TPU v7x, 32 devices: a whole 2x2x4 slice. The times are simulated.
32 devices in a mesh: groups: 2 (over x), pair: 16 (over z, y, core).
Axes of the slice: x: 2, y: 2, z: 4, core: 2. Of those that a mesh axis runs over, the one named last changes fastest.
Arguments:
- ray_blocks: bfloat16 [256, 16, 128, 128], P(('groups', 'pair')), parts along dimension 0, may hold values from -0.125 to 0.125
- block_cells: int32 [256, 16], P(('groups', 'pair')), parts along dimension 0, may hold values from 0 to 1023, as said below
- block_counts: int32 [256], P(('groups', 'pair')), parts along dimension 0, may hold values from 1 to 16
- travel_times: float32 [32768, 64], P(('groups', 'pair')), parts along dimension 0, may hold values from -6 to 6
Outputs:
- estimate: float32 [262144, 64], P(('groups', 'pair')), parts along dimension 0
- model_vec: float32 [262144, 64], P(('groups', 'pair')), parts along dimension 0
There are 2 independent parts, one for each index of `groups`. A program takes and returns all parts, laid end to end along the dimension named above; each array names one. Nothing has to cross between parts.
Inputs may be any that keep to these rules, and one draw needn't show every extreme that they name: Slots of pair block p at or past block_counts[p] are ignored. `block_cells`: cell block b belongs to the device holding output rows b * 128 to b * 128 + 127, that is device b // 64; among all slots of the pair blocks on one device, at most 8 name cell blocks of one owning device, and these name at most 4 distinct cell blocks.
All inputs are finite; a program needn't handle non-finite values.
Results may differ from a plain program's by a relative error of at most 0.0075.
Values may be sent and summed in bfloat16 or wider, within the bound.
No kernel may reach another device: no remote copies, remote signals or barrier semaphores. Data moves between devices by JAX's collectives and lax.ppermute only.
A program may use at most 128 MiB of HBM per device.

v0:
```python
import jax
import jax.numpy as jnp
from jax import lax
from jax.sharding import PartitionSpec as P

CELL_DEV = 8192
SCAP = 8
ITERS = 2


def place(owner_of, takes_place, peer_count, capacity):
    onehot = (owner_of[:, None] == jnp.arange(peer_count)[None, :]).astype(jnp.int32) * takes_place[
        :, None
    ]
    place_rank = jnp.sum((jnp.cumsum(onehot, axis=0) - 1) * onehot, axis=1)
    return owner_of * capacity + place_rank


def on_device(ray_blocks, block_cells, block_counts, travel_times):
    pair_count, slot_count, block_size, unused = ray_blocks.shape
    columns = travel_times.shape[1]
    peer_count = lax.axis_size("pair")
    owned_blocks = CELL_DEV // block_size
    flat_cells = block_cells.reshape(-1)
    owner_of = flat_cells // owned_blocks
    local_block = flat_cells % owned_blocks
    live_slot = (jnp.arange(slot_count)[None, :] < block_counts[:, None]).reshape(-1)
    capacity = SCAP
    target = place(owner_of, jnp.ones_like(flat_cells), peer_count, capacity)
    request = jnp.zeros((peer_count * capacity,), jnp.int32).at[target].set(local_block)
    asked = lax.all_to_all(
        request.reshape(peer_count, capacity), "pair", split_axis=0, concat_axis=0, tiled=True
    ).reshape(-1)
    gather_table = (jnp.arange(owned_blocks)[:, None] == asked[None, :]).astype(jnp.float32)
    live_bf = live_slot.astype(jnp.bfloat16).reshape(pair_count, slot_count, 1, 1)
    live_float = live_slot.astype(jnp.float32).reshape(-1, 1, 1)

    def transpose(data_vec):
        data_bf = data_vec.astype(jnp.bfloat16).reshape(pair_count, block_size, columns)
        contrib = jnp.einsum(
            "pkij,pic->pkjc", ray_blocks, data_bf, preferred_element_type=jnp.float32
        )
        contrib = contrib.reshape(-1, block_size, columns) * live_float
        outgoing = (
            jnp.zeros((peer_count * capacity, block_size, columns), jnp.float32)
            .at[target]
            .add(contrib)
        )
        incoming = lax.all_to_all(
            outgoing.reshape(peer_count, capacity, block_size, columns),
            "pair",
            split_axis=0,
            concat_axis=0,
            tiled=True,
        )
        incoming = incoming.reshape(peer_count * capacity, block_size * columns)
        summed = jnp.dot(
            gather_table,
            incoming,
            precision=lax.Precision.HIGHEST,
            preferred_element_type=jnp.float32,
        )
        return summed.reshape(CELL_DEV, columns)

    def pair_norm(values):
        return jnp.sqrt(lax.psum(jnp.sum(values * values, axis=0), "pair") + 1e-12)

    def settle(partial_value, beta_norm, model_own, first):
        if not first:
            partial_value = partial_value - beta_norm * model_own
        alpha_norm = jnp.sqrt(
            lax.psum(jnp.sum(partial_value * partial_value, axis=0), "pair") + 1e-12
        )
        return (partial_value / alpha_norm, alpha_norm)

    beta_norm = pair_norm(travel_times)
    data_vec = travel_times / beta_norm
    model_own, alpha_norm = settle(transpose(data_vec), beta_norm, None, True)
    search = model_own
    estimate = jnp.zeros_like(model_own)
    phi_bar = beta_norm
    rho_bar = alpha_norm
    for step in range(ITERS):
        model_tiles = model_own.astype(jnp.bfloat16).reshape(owned_blocks, block_size, columns)
        replies = model_tiles[asked].reshape(peer_count, capacity, block_size, columns)
        fetched = lax.all_to_all(replies, "pair", split_axis=0, concat_axis=0, tiled=True).reshape(
            -1, block_size, columns
        )
        chosen = fetched[target].reshape(pair_count, slot_count, block_size, columns) * live_bf
        product = jnp.einsum(
            "pkij,pkjc->pic", ray_blocks, chosen, preferred_element_type=jnp.float32
        )
        raw = product.reshape(-1, columns) - alpha_norm * data_vec
        beta_norm = pair_norm(raw)
        data_vec = raw / beta_norm
        model_own, alpha_norm = settle(transpose(data_vec), beta_norm, model_own, False)
        rho_next = jnp.sqrt(rho_bar * rho_bar + beta_norm * beta_norm)
        cosine = rho_bar / rho_next
        sine_value = beta_norm / rho_next
        theta_step = sine_value * alpha_norm
        rho_bar = -cosine * alpha_norm
        phi_step = cosine * phi_bar
        phi_bar = sine_value * phi_bar
        estimate = estimate + phi_step / rho_next * search
        search = model_own - theta_step / rho_next * search
    return (estimate, model_own)


def solution(mesh):
    return jax.shard_map(
        on_device,
        mesh=mesh,
        in_specs=(
            P(("groups", "pair"), None, None, None),
            P(("groups", "pair"), None),
            P(("groups", "pair")),
            P(("groups", "pair"), None),
        ),
        out_specs=(P(("groups", "pair"), None), P(("groups", "pair"), None)),
        check_vma=False,
    )
```

profile of v0, /device:TPU:0, one launch (start us, length us, event | category | flops | bytes accessed | tf_op | source)
XLA Modules:
  0.0 826.7 jit_solution(8900876756062320096)
XLA Ops:
  0.6 0.8 reshape.289
  1.4 0.8 reshape.288
  2.6 1.0 scatter_custom_fusion
  3.6 0.7 all_to_all.21
  4.3 7.4 all-to-all-start
  11.7 1.1 multiply_reduce_fusion.5
  12.8 33.9 %psum.42 = f32[64]{0:T(128)S(1)} all-reduce(f32[64]{0:T(128)S(1)} %multiply_reduce_fusion.5), channel_id=1, replica_groups=mesh['groups'=2,'pair'=16] {'pair'}, use_global_device_ids=true, to_apply=%region_4.5 | all-reduce | flops 64 | bytes 512 | tf_op jit(solution)/shard_map/psum | solution.py:66
  46.7 0.7 fusion.27
  47.5 1.0 convert_bitcast_fusion.1
  48.5 2.9 fusion.17
  51.4 2.3 bitcast_multiply_fusion.2
  53.7 2.5 broadcast.181.clone
  56.2 20.1 %scatter_fusion = f32[128,128,64]{1,2,0:T(8,128)} fusion(f32[128,128,64]{1,2,0:T(8,128)} %broadcast.181.clone, s32[128]{0:T(128)S(1)} %fusion.29, f32[128,128,64]{1,2,0:T(8,128)} %bitcast_multiply_fusion.2), kind=kCustom, calls=%fused_computation.5 | custom fusion | flops 1048576 | bytes 12583424 | tf_op jit(solution)/shard_map/scatter-add | solution.py:47
  76.3 4.5 all-to-all-start.1
  82.3 76.2 %all-to-all-done.1 = f32[16,8,128,64]{2,3,1,0:T(8,128)} async-done(((f32[16,8,128,64]{2,3,1,0:T(8,128)}), f32[16,8,128,64]{2,3,1,0:T(8,128)}, u32[]{:S(2)}, u32[]{:S(2)}) %all-to-all-start.1) | async-done | bytes 4194336 | tf_op jit(solution)/shard_map/all_to_all | solution.py:49
  158.5 6.9 copy.26
  165.4 7.9 reshape.293
  173.3 3.9 fusion.23
  177.2 3.0 reshape.294
  180.2 3.0 reshape.295
  183.2 3.3 multiply_reduce_fusion.2
  186.5 47.6 %psum.43 = f32[64]{0:T(128)S(1)} all-reduce(f32[64]{0:T(128)S(1)} %multiply_reduce_fusion.2), channel_id=1, replica_groups=mesh['groups'=2,'pair'=16] {'pair'}, use_global_device_ids=true, to_apply=%region_7.8 | all-reduce | flops 64 | bytes 512 | tf_op jit(solution)/shard_map/psum | solution.py:72
  234.1 2.7 fusion.4
  236.9 3.0 gather_fusion
  239.9 4.8 copy.27
  244.6 3.7 all-to-all-start.2
  248.4 41.0 %all-to-all-done.2 = bf16[16,8,128,64]{2,3,1,0:T(8,128)(2,1)S(1)} async-done(((bf16[16,8,128,64]{2,3,1,0:T(8,128)(2,1)}), bf16[16,8,128,64]{2,3,1,0:T(8,128)(2,1)S(1)}, u32[]{:S(2)}, u32[]{:S(2)}) %all-to-all-start.2) | async-done | bytes 2097184 | tf_op jit(solution)/shard_map/all_to_all | solution.py:86
  289.4 2.1 gather_fusion.1
  291.5 4.5 fusion.5
  296.2 39.4 %psum.44 = f32[64]{0:T(128)S(1)} all-reduce(f32[64]{0:T(128)S(1)} %get-tuple-element.15), channel_id=1, replica_groups=mesh['groups'=2,'pair'=16] {'pair'}, use_global_device_ids=true, to_apply=%region_9.10 | all-reduce | flops 64 | bytes 512 | tf_op jit(solution)/shard_map/psum | solution.py:66
  335.7 2.9 fusion.15
  338.6 2.3 bitcast_multiply_fusion.1
  340.9 2.5 broadcast.181.clone.1
  343.4 20.1 %scatter_fusion.1 = f32[128,128,64]{1,2,0:T(8,128)} fusion(f32[128,128,64]{1,2,0:T(8,128)} %broadcast.181.clone.1, s32[128]{0:T(128)S(1)} %fusion.29, f32[128,128,64]{1,2,0:T(8,128)} %bitcast_multiply_fusion.1), kind=kCustom, calls=%fused_computation.6 | custom fusion | flops 1048576 | bytes 12583424 | tf_op jit(solution)/shard_map/scatter-add | solution.py:47
  363.5 96.8 %all_to_all.34 = f32[16,8,128,64]{2,3,1,0:T(8,128)} all-to-all(f32[16,8,128,64]{2,3,1,0:T(8,128)} %bitcast.87), channel_id=1, replica_groups=mesh['groups'=2,'pair'=16] {'pair'}, dimensions={0} | all-to-all | bytes 8388608 | tf_op jit(solution)/shard_map/all_to_all | solution.py:49
  460.3 6.9 copy.30
  467.2 7.9 reshape.304
  475.1 3.9 fusion.22
  479.0 3.0 reshape.306
  482.0 3.0 reshape.305
  485.0 6.4 multiply_reduce_fusion.1
  491.4 33.0 %psum.45 = f32[64]{0:T(128)S(1)} all-reduce(f32[64]{0:T(128)S(1)} %get-tuple-element.13), channel_id=1, replica_groups=mesh['groups'=2,'pair'=16] {'pair'}, use_global_device_ids=true, to_apply=%region_12.13 | all-reduce | flops 64 | bytes 512 | tf_op jit(solution)/shard_map/psum | solution.py:72
  524.4 4.5 divide_convert_fusion
  528.9 3.0 gather_fusion.2
  531.9 4.8 copy.31
  536.7 50.9 %all_to_all.35 = bf16[16,8,128,64]{2,3,1,0:T(8,128)(2,1)S(1)} all-to-all(bf16[16,8,128,64]{2,3,1,0:T(8,128)(2,1)} %copy.31), channel_id=1, replica_groups=mesh['groups'=2,'pair'=16] {'pair'}, dimensions={0} | all-to-all | bytes 4194304 | tf_op jit(solution)/shard_map/all_to_all | solution.py:86
  587.6 2.1 gather_fusion.3
  589.8 4.4 fusion.8
  594.4 33.2 %psum.46 = f32[64]{0:T(128)S(1)} all-reduce(f32[64]{0:T(128)S(1)} %get-tuple-element.11), channel_id=1, replica_groups=mesh['groups'=2,'pair'=16] {'pair'}, use_global_device_ids=true, to_apply=%region_14.15 | all-reduce | flops 64 | bytes 512 | tf_op jit(solution)/shard_map/psum | solution.py:66
  627.8 2.9 fusion.13
  630.6 2.3 bitcast_multiply_fusion
  633.0 2.5 broadcast.181
  635.4 20.1 %scatter_fusion.2 = f32[128,128,64]{1,2,0:T(8,128)} fusion(f32[128,128,64]{1,2,0:T(8,128)} %broadcast.181, s32[128]{0:T(128)S(1)} %fusion.29, f32[128,128,64]{1,2,0:T(8,128)} %bitcast_multiply_fusion), kind=kCustom, calls=%fused_computation.7 | custom fusion | flops 1048576 | bytes 12583424 | tf_op jit(solution)/shard_map/scatter-add | solution.py:47
  655.5 4.5 all-to-all-start.5
  660.1 77.6 %all-to-all-done.5 = f32[16,8,128,64]{2,3,1,0:T(8,128)} async-done(((f32[16,8,128,64]{2,3,1,0:T(8,128)}), f32[16,8,128,64]{2,3,1,0:T(8,128)}, u32[]{:S(2)}, u32[]{:S(2)}) %all-to-all-start.5) | async-done | bytes 4194336 | tf_op jit(solution)/shard_map/all_to_all | solution.py:49
  737.7 6.9 copy.34
  744.6 7.9 reshape.314
  752.5 3.9 fusion.21
  756.4 3.0 reshape.315
  759.5 4.6 multiply_reduce_fusion
  764.0 47.6 %psum.47 = f32[64]{0:T(128)S(1)} all-reduce(f32[64]{0:T(128)S(1)} %multiply_reduce_fusion), channel_id=1, replica_groups=mesh['groups'=2,'pair'=16] {'pair'}, use_global_device_ids=true, to_apply=%region_17.18 | all-reduce | flops 64 | bytes 512 | tf_op jit(solution)/shard_map/psum | solution.py:72
  811.6 7.5 broadcast_divide_fusion
  819.2 3.8 copy.36
  822.9 3.8 copy.35
  (30 shorter events, 2.7 us)
Async XLA Ops:
  4.3 72.0 %all-to-all-start = ((s32[16,1,8]{2,1,0:T(1,128)}), s32[16,1,8]{2,1,0:T(1,128)S(1)}, u32[]{:S(2)}, u32[]{:S(2)}) async-start(s32[16,1,8]{2,1,0:T(1,128)} %bitcast.2), calls=%async_computation | async-start | bytes 16384 | tf_op jit(solution)/shard_map/all_to_all | solution.py:31
  76.3 82.2 %all-to-all-start.1 = ((f32[16,8,128,64]{2,3,1,0:T(8,128)}), f32[16,8,128,64]{2,3,1,0:T(8,128)}, u32[]{:S(2)}, u32[]{:S(2)}) async-start(f32[16,8,128,64]{2,3,1,0:T(8,128)} %bitcast.86), calls=%async_computation.1 | async-start | bytes 8388608 | tf_op jit(solution)/shard_map/all_to_all | solution.py:49
  244.6 44.8 %all-to-all-start.2 = ((bf16[16,8,128,64]{2,3,1,0:T(8,128)(2,1)}), bf16[16,8,128,64]{2,3,1,0:T(8,128)(2,1)S(1)}, u32[]{:S(2)}, u32[]{:S(2)}) async-start(bf16[16,8,128,64]{2,3,1,0:T(8,128)(2,1)} %copy.27), calls=%async_computation.2 | async-start | bytes 4194304 | tf_op jit(solution)/shard_map/all_to_all | solution.py:86
  291.5 4.5 copy-start
  655.5 82.2 %all-to-all-start.5 = ((f32[16,8,128,64]{2,3,1,0:T(8,128)}), f32[16,8,128,64]{2,3,1,0:T(8,128)}, u32[]{:S(2)}, u32[]{:S(2)}) async-start(f32[16,8,128,64]{2,3,1,0:T(8,128)} %bitcast.85), calls=%async_computation.5 | async-start | bytes 8388608 | tf_op jit(solution)/shard_map/all_to_all | solution.py:49
where the time goes:
time: 829 us; the launch traced here: 827 us
  blocking collectives  382 us (46%)
  waiting for transfers between devices  195 us (24%)
  other arithmetic  101 us (12%)
  local copies, waits for them, and re-layouts  98.2 us (12%)
  matrix products  29.2 us (4%)
  starting transfers between devices  20.2 us (2%)
    all_to_all x2, waiting for transfers between devices, transpose(): lax.all_to_all(outgoing.reshape(peer_count, capacity, block_size, columns...  154 us
    psum x3, blocking collectives, settle(): lax.psum(jnp.sum(partial_value * partial_value, axis=0), 'pair') + 1e-12  128 us
    psum x3, blocking collectives, pair_norm(): return jnp.sqrt(lax.psum(jnp.sum(values * values, axis=0), 'pair') + 1e-12)  106 us
    all_to_all x1, blocking collectives, transpose(): lax.all_to_all(outgoing.reshape(peer_count, capacity, block_size, columns...  96.8 us
    scatter-add x3, other arithmetic, transpose(): outgoing = jnp.zeros((peer_count * capacity, block_size, columns), jnp.fl...  60.4 us
    all_to_all x1, blocking collectives, on_device(): lax.all_to_all(replies, 'pair', split_axis=0, concat_axis=0, tiled=True)  50.9 us
    all_to_all x1, waiting for transfers between devices, on_device(): lax.all_to_all(replies, 'pair', split_axis=0, concat_axis=0, tiled=True)  41 us
    reshape x3, local copies, waits for them, and re-layouts, transpose(): incoming = incoming.reshape(peer_count * capacity, block_size * columns)  23.7 us
  transfers between devices with their start and end apart: 4, of which 3 were waited for; matrix products, arithmetic and copies ran while one was open for 4% of the time, Pallas kernels for 0%

commit v1 on v0

v1 whole, which is shorter than its diff:
```python
import functools

import jax
import jax.numpy as jnp
from jax import lax
from jax.experimental import pallas as pl
from jax.experimental.pallas import tpu as pltpu
from jax.sharding import PartitionSpec as P

CELL_DEV = 8192
BCAP = 4
BS = 128
TAIL = 16
ITERS = 2
EPS = 1e-12
F32 = jnp.float32
BF16 = jnp.bfloat16
VMEM = pltpu.VMEM
SMEM = pltpu.SMEM


def diagonal(cols):
    shape = (cols, BS)
    return lax.broadcasted_iota(jnp.int32, shape, 0) == lax.broadcasted_iota(jnp.int32, shape, 1)


def squares_tail(squares):
    cols = squares.shape[0]
    total = jnp.sum(squares, axis=1, keepdims=True)
    row = jnp.sum(jnp.where(diagonal(cols), total, 0.0), axis=0, keepdims=True)
    high = row.astype(BF16).astype(F32)
    middle = (row - high).astype(BF16).astype(F32)
    low = row - high - middle
    place = lax.broadcasted_iota(jnp.int32, (TAIL, BS), 0)
    return jnp.where(
        place == 0, high, jnp.where(place == 1, middle, jnp.where(place == 2, low, 0.0))
    )


def norm_of_tails(message_ref, cols):
    tails = message_ref[:, BCAP * cols :, :].astype(F32)
    summed = jnp.sum(tails, axis=0)
    row = summed[0:1] + summed[1:2] + summed[2:3]
    column = jnp.sum(jnp.where(diagonal(cols), row, 0.0), axis=1, keepdims=True)
    return jnp.broadcast_to(jnp.sqrt(column + EPS), (cols, BS))


def lanes(block):
    return pl.ds(pl.multiple_of(block * BS, BS), BS)


def transposed(data_ref, rays_ref, target_ref, total_ref, message_ref):
    pair_count, slot_count = rays_ref.shape[:2]
    cols = data_ref.shape[0]
    peers = message_ref.shape[0]
    spots = peers * BCAP

    def clear(index, carry):
        total_ref[index] = jnp.zeros((cols, BS), F32)
        return carry

    lax.fori_loop(0, spots, clear, 0, unroll=8)

    def one_pair(pair, carry):
        data = data_ref[:, lanes(pair)].astype(BF16)
        for slot in range(0, slot_count, 2):
            rays = jnp.concatenate([rays_ref[pair, slot], rays_ref[pair, slot + 1]], axis=1)
            part = jnp.dot(data, rays, preferred_element_type=F32)
            for half in range(2):
                spot = target_ref[pair * slot_count + slot + half]
                total_ref[spot] += part[:, half * BS : (half + 1) * BS]
        return carry

    lax.fori_loop(0, pair_count, one_pair, 0)

    def pack(peer, carry):
        for rank in range(BCAP):
            message_ref[peer, rank * cols : (rank + 1) * cols, :] = total_ref[
                peer * BCAP + rank
            ].astype(BF16)
        return carry

    lax.fori_loop(0, peers, pack, 0, unroll=2)


def start_kernel(
    cells_ref, counts_ref, times_ref, rays_ref, message_ref, target_ref, total_ref, table_ref, used_ref
):
    pair_count, slot_count = rays_ref.shape[:2]
    peers = message_ref.shape[0]
    cols = times_ref.shape[0]
    owned = CELL_DEV // BS

    def clear(peer, carry):
        used_ref[peer] = 0
        for rank in range(BCAP):
            table_ref[peer * BCAP + rank] = 0
        return carry

    lax.fori_loop(0, peers, clear, 0)

    def one_pair(pair, carry):
        count = counts_ref[pair]
        for slot in range(slot_count):
            cell = cells_ref[pair, slot]
            owner = cell // owned
            local = cell % owned
            used = used_ref[owner]
            rank = used
            for other in range(BCAP - 1, -1, -1):
                same = (table_ref[owner * BCAP + other] == local) & (other < used)
                rank = jnp.where(same, other, rank)
            spot = owner * BCAP + rank
            table_ref[spot] = local
            used_ref[owner] = jnp.maximum(used, rank + 1)
            target_ref[pair * slot_count + slot] = jnp.where(slot < count, spot, peers * BCAP)
        return carry

    lax.fori_loop(0, pair_count, one_pair, 0)
    transposed(times_ref, rays_ref, target_ref, total_ref, message_ref)
    squares = jnp.zeros((cols, BS), F32)
    for pair in range(pair_count):
        part = times_ref[:, pair * BS : (pair + 1) * BS]
        squares += part * part
    tail = squares_tail(squares)
    place = lax.broadcasted_iota(jnp.int32, (TAIL, BS), 0)
    lane = lax.broadcasted_iota(jnp.int32, (TAIL, BS), 1)

    def ask(peer, carry):
        rows = tail
        for rank in range(BCAP):
            asked = table_ref[peer * BCAP + rank].astype(F32)
            rows = jnp.where((place == 3) & (lane == rank), asked, rows)
        message_ref[peer, BCAP * cols :, :] = rows.astype(BF16)
        return carry

    lax.fori_loop(0, peers, ask, 0)


def pair_kernel(
    target_ref, fetched_ref, data_ref, beta_ref, rays_ref,
    message_ref, raw_ref, alpha_ref, total_ref,
):
    pair_count, slot_count = rays_ref.shape[:2]
    peers = message_ref.shape[0]
    cols = data_ref.shape[0]
    spots = peers * BCAP
    alpha = norm_of_tails(fetched_ref, cols)
    alpha_ref[...] = alpha
    model_scale = 1.0 / alpha
    data_scale = alpha / beta_ref[...]

    def one_pair(pair, squares):
        chosen = []
        for slot in range(slot_count):
            spot = target_ref[pair * slot_count + slot]
            live = spot < spots
            spot = jnp.where(live, spot, 0)
            rows = pl.ds(pl.multiple_of((spot % BCAP) * cols, cols), cols)
            block = fetched_ref[spot // BCAP, rows, :]
            chosen.append(jnp.where(live, block, jnp.zeros_like(block)))
        rays = jnp.concatenate([rays_ref[pair, slot] for slot in range(slot_count)], axis=1)
        product = lax.dot_general(
            jnp.concatenate(chosen, axis=1), rays, (((1,), (1,)), ((), ())),
            preferred_element_type=F32,
        )
        raw = product * model_scale - data_ref[:, lanes(pair)] * data_scale
        raw_ref[:, lanes(pair)] = raw
        return squares + raw * raw

    squares = lax.fori_loop(0, pair_count, one_pair, jnp.zeros((cols, BS), F32))
    transposed(raw_ref, rays_ref, target_ref, total_ref, message_ref)
    tail = squares_tail(squares).astype(BF16)
    message_ref[:, BCAP * cols :, :] = jnp.broadcast_to(tail[None], (peers, TAIL, BS))


def cell_kernel(first, last, *refs):
    if first:
        arrived_ref, raw_ref, beta_ref, out_ref, asked_ref, table_ref, sem = refs
    else:
        asked_ref, arrived_ref, model_ref, alpha_ref, raw_ref, beta_ref, out_ref = refs
    peers = arrived_ref.shape[0]
    cols, cells = raw_ref.shape
    if first:
        table_ref[...] = arrived_ref[:, BCAP * cols :, :].astype(F32)[:, 3, :].astype(jnp.int32)
        copy = pltpu.make_async_copy(table_ref, asked_ref, sem)
        copy.start()
    beta = norm_of_tails(arrived_ref, cols)
    beta_ref[...] = beta
    raw_ref[...] = jnp.zeros((cols, cells), F32)
    if first:
        copy.wait()

    def add(peer, carry):
        for rank in range(BCAP):
            where = lanes(asked_ref[peer, rank])
            raw_ref[:, where] += arrived_ref[peer, rank * cols : (rank + 1) * cols, :].astype(F32)
        return carry

    lax.fori_loop(0, peers, add, 0, unroll=2)
    scale = 1.0 / beta
    if not first:
        model_scale = beta / alpha_ref[...]

    def settle(block, squares):
        raw = raw_ref[:, lanes(block)] * scale
        if not first:
            raw = raw - model_ref[:, lanes(block)] * model_scale
        raw_ref[:, lanes(block)] = raw
        return squares + raw * raw

    squares = lax.fori_loop(0, cells // BS, settle, jnp.zeros((cols, BS), F32), unroll=4)
    tail = squares_tail(squares)
    if last:
        out_ref[...] = jnp.broadcast_to(tail[None], out_ref.shape).astype(out_ref.dtype)
        return
    out_ref[:, BCAP * cols :, :] = jnp.broadcast_to(tail[None], (peers, TAIL, BS)).astype(BF16)

    def reply(peer, carry):
        for rank in range(BCAP):
            block = raw_ref[:, lanes(asked_ref[peer, rank])]
            out_ref[peer, rank * cols : (rank + 1) * cols, :] = block.astype(BF16)
        return carry

    lax.fori_loop(0, peers, reply, 0, unroll=2)


def estimate_kernel(*refs):
    betas = refs[0 : ITERS + 1]
    alphas = refs[ITERS + 1 : 2 * ITERS + 1]
    models = refs[2 * ITERS + 1 : 3 * ITERS + 1]
    estimate_ref = refs[-1]
    cols, cells = estimate_ref.shape
    phi_bar = betas[0][...]
    rho_bar = alphas[0][...]
    trace = [1.0 / alphas[0][...]]
    weight = [jnp.zeros((cols, BS), F32)] * ITERS
    for step in range(ITERS):
        beta = betas[step + 1][...]
        rho = jnp.sqrt(rho_bar * rho_bar + beta * beta)
        cosine = rho_bar / rho
        sine = beta / rho
        gain = cosine * phi_bar / rho
        weight = [
            weight[i] + gain * trace[i] if i < len(trace) else weight[i] for i in range(ITERS)
        ]
        if step + 1 < ITERS:
            alpha = alphas[step + 1][...]
            theta = sine * alpha
            rho_bar = -cosine * alpha
            phi_bar = sine * phi_bar
            trace = [-(theta / rho) * value for value in trace] + [1.0 / alpha]

    def one_block(block, carry):
        where = lanes(block)
        total = weight[0] * models[0][:, where]
        for i in range(1, ITERS):
            total += weight[i] * models[i][:, where]
        estimate_ref[:, where] = total
        return carry

    lax.fori_loop(0, cells // BS, one_block, 0, unroll=4)


def model_kernel(tails_ref, raw_ref, model_ref):
    cols, cells = raw_ref.shape
    summed = jnp.sum(tails_ref[...], axis=0)
    row = summed[0:1] + summed[1:2] + summed[2:3]
    column = jnp.sum(jnp.where(diagonal(cols), row, 0.0), axis=1, keepdims=True)
    scale = jnp.broadcast_to(1.0 / jnp.sqrt(column + EPS), (cols, BS))

    def one_block(block, carry):
        model_ref[:, lanes(block)] = raw_ref[:, lanes(block)] * scale
        return carry

    lax.fori_loop(0, cells // BS, one_block, 0, unroll=4)


def call(kernel, name, in_spaces, outs, scratch=(), flops=0, moved=0):
    return pl.pallas_call(
        kernel,
        name=name,
        in_specs=[pl.BlockSpec(memory_space=space) for space in in_spaces],
        out_specs=[pl.BlockSpec(memory_space=space) for _, _, space in outs],
        out_shape=[jax.ShapeDtypeStruct(shape, dtype) for shape, dtype, _ in outs],
        scratch_shapes=list(scratch),
        compiler_params=pltpu.CompilerParams(vmem_limit_bytes=24 * 1024 * 1024),
        cost_estimate=pl.CostEstimate(flops=flops, bytes_accessed=moved, transcendentals=0),
    )


def on_device(ray_blocks, block_cells, block_counts, travel_times):
    pair_count, slot_count = ray_blocks.shape[:2]
    slots = pair_count * slot_count
    peers = lax.axis_size("pair")
    spots = peers * BCAP
    times = travel_times.T
    cols, pairs = times.shape
    message = ((peers, BCAP * cols + TAIL, BS), BF16, VMEM)
    tile = ((cols, BS), F32, VMEM)
    data = ((cols, pairs), F32, VMEM)
    model = ((cols, CELL_DEV), F32, VMEM)
    totals = VMEM((spots + 1, cols, BS), F32)
    flops = 2 * slots * BS * BS * cols

    def exchange(values):
        return lax.all_to_all(values, "pair", split_axis=0, concat_axis=0, tiled=True)

    outgoing, target = call(
        start_kernel, "start", [SMEM, SMEM, VMEM, VMEM],
        [message, ((slots,), jnp.int32, SMEM)],
        [totals, SMEM((spots,), jnp.int32), SMEM((peers,), jnp.int32)],
        flops, 6 << 20,
    )(block_cells, block_counts, times, ray_blocks)
    arrived = exchange(outgoing)
    raw, beta, reply, asked = call(
        functools.partial(cell_kernel, True, False), "cells_first", [VMEM],
        [model, tile, message, ((peers, BS), jnp.int32, SMEM)],
        [VMEM((peers, BS), jnp.int32), pltpu.SemaphoreType.DMA],
        0, 6 << 20,
    )(arrived)
    models, betas, alphas = [raw], [beta], []
    current = times
    for step in range(ITERS):
        fetched = exchange(reply)
        outgoing, current, alpha = call(
            pair_kernel, "pairs", [SMEM, VMEM, VMEM, VMEM, VMEM],
            [message, data, tile], [totals], 2 * flops, 8 << 20,
        )(target, fetched, current, betas[-1], ray_blocks)
        alphas.append(alpha)
        arrived = exchange(outgoing)
        last = step + 1 == ITERS
        out = ((peers, TAIL, BS), F32, VMEM) if last else message
        raw, beta, reply = call(
            functools.partial(cell_kernel, False, last), "cells_last" if last else "cells",
            [SMEM, VMEM, VMEM, VMEM], [model, tile, out], (), 0, 8 << 20,
        )(asked, arrived, models[-1], alpha)
        betas.append(beta)
        models.append(raw)
    tails = exchange(reply)
    (estimate,) = call(
        estimate_kernel, "estimate", [VMEM] * (3 * ITERS + 1), [model], (), 0, 6 << 20
    )(*betas, *alphas, *models[:ITERS])
    (model_vec,) = call(model_kernel, "model", [VMEM, VMEM], [model], (), 0, 4 << 20)(
        tails, models[-1]
    )
    return (estimate.T, model_vec.T)


def solution(mesh):
    return jax.shard_map(
        on_device,
        mesh=mesh,
        in_specs=(
            P(("groups", "pair"), None, None, None),
            P(("groups", "pair"), None),
            P(("groups", "pair")),
            P(("groups", "pair"), None),
        ),
        out_specs=(P(("groups", "pair"), None), P(("groups", "pair"), None)),
        check_vma=False,
    )
```

time: 829 us -> 209 us (0.25)
  blocking collectives: 382 us -> 161 us
  waiting for transfers between devices: 195 us -> 4.22 us
  other arithmetic: 101 us -> 0 us
  local copies, waits for them, and re-layouts: 98.2 us -> 8.99 us
  Pallas kernels: 0 us -> 30 us
  matrix products: 29.2 us -> 0 us
  starting transfers between devices: 20.2 us -> 3.51 us
    psum x6 -> x0, blocking collectives: 235 us -> none  [the longest x3 128 us: settle(): lax.psum(jnp.sum(partial_value * partial_value, axis=0), 'pair') + 1e-12]
    all_to_all x4 -> x1, waiting for transfers between devices: 195 us -> 4.22 us  [exchange(): lax.all_to_all(values, 'pair', split_axis=0, concat_axis=0, tiled=True)]
    scatter-add x3 -> x0, other arithmetic: 60.4 us -> none  [transpose(): outgoing = jnp.zeros((peer_count * capacity, block_size, columns), jnp.fl...]
    reshape x13 -> x0, local copies, waits for them, and re-layouts: 49.9 us -> none  [the longest x3 23.7 us: transpose(): incoming = incoming.reshape(peer_count * capacity, block_size * columns)]
    pallas_call x0 -> x8, Pallas kernels: none -> 30 us  [the longest x2 11.9 us: on_device(): call(pair_kernel, 'pairs', [SMEM, VMEM, VMEM, VMEM, VMEM], [message, data...]
    dot_general x8 -> x0, matrix products: 29.2 us -> none  [the longest x3 11.7 us: transpose(): jnp.dot(gather_table, incoming, precision=lax.Precision.HIGHEST, preferre...]
    all_to_all x5 -> x0, local copies, waits for them, and re-layouts: 21.9 us -> none  [the longest x3 20.7 us: transpose(): lax.all_to_all(outgoing.reshape(peer_count, capacity, block_size, columns...]
    all_to_all x4 -> x1, starting transfers between devices: 20.2 us -> 3.51 us  [exchange(): lax.all_to_all(values, 'pair', split_axis=0, concat_axis=0, tiled=True)]
  transfers between devices with their start and end apart: 4 -> 1, of which waited for: 3 -> 1; matrix products, arithmetic and copies ran while one was open for 4% -> 0% of each run, Pallas kernels for 0% -> 1%
where the time goes in v1:
time: 209 us
  blocking collectives  161 us (77%)
  Pallas kernels  30 us (14%)
  local copies, waits for them, and re-layouts  8.99 us (4%)
  waiting for transfers between devices  4.22 us (2%)
  starting transfers between devices  3.51 us (2%)
    all_to_all x5, blocking collectives, exchange(): lax.all_to_all(values, 'pair', split_axis=0, concat_axis=0, tiled=True)  161 us
    pallas_call x2, Pallas kernels, on_device(): call(pair_kernel, 'pairs', [SMEM, VMEM, VMEM, VMEM, VMEM], [message, data...  11.9 us
    unnamed x18, local copies, waits for them, and re-layouts  8.99 us
    pallas_call x1, Pallas kernels, on_device(): call(start_kernel, 'start', [SMEM, SMEM, VMEM, VMEM], [message, ((slots,)...  6.08 us
    pallas_call x2, Pallas kernels, on_device(): call(functools.partial(cell_kernel, False, last), 'cells_last' if last el...  5.08 us
    all_to_all x1, waiting for transfers between devices, exchange(): lax.all_to_all(values, 'pair', split_axis=0, concat_axis=0, tiled=True)  4.22 us
  transfers between devices with their start and end apart: 1, of which 1 were waited for; matrix products, arithmetic and copies ran while one was open for 0% of the time, Pallas kernels for 1%

profile of v1, /device:TPU:0, one launch (start us, length us, event | category | flops | bytes accessed | tf_op | source)
XLA Modules:
  0.0 208.6 jit_solution(6387402642326150922)
XLA Ops:
  0.6 0.0 copy-start
  0.6 2.2 %copy-done = bf16[8,16,128,128]{3,2,1,0:T(8,128)(2,1)S(1)} copy-done((bf16[8,16,128,128]{3,2,1,0:T(8,128)(2,1)S(1)}, bf16[8,16,128,128]{3,2,1,0:T(8,128)(2,1)}, u32[]{:S(2)}) %copy-start) | copy-done | bytes 4194328
  2.8 0.0 copy-start.6
  2.8 0.9 copy-done.6
  3.8 0.0 copy-start.7
  3.8 0.7 copy-done.7
  4.5 0.0 copy-start.8
  4.5 0.7 copy-done.8
  5.1 6.1 %start.1 = (bf16[16,272,128]{2,1,0:T(8,128)(2,1)S(1)}, s32[128]{0:T(128)S(1)}) custom-call(s32[8,16]{1,0:T(8,128)S(1)} %copy-done.7, s32[8]{0:T(128)S(1)} %copy-done.8, f32[64,1024]{1,0:T(8,128)S(1)} %bitcast.3, bf16[8,16,128,128]{3,2,1,0:T(8,128)(2,1)S(1)} %copy-done), custom_call_target="tpu_custom_call" | custom-call | flops 268435456 | bytes 6291456 | tf_op jit(solution)/shard_map/start/pallas_call | solution.py:309
  11.2 0.0 copy-start.1
  11.2 35.9 %all_to_all.30.refs_0_ = bf16[16,272,128]{2,1,0:T(8,128)(2,1)S(1)} all-to-all(bf16[16,272,128]{2,1,0:T(8,128)(2,1)S(1)} %get-tuple-element.19), channel_id=1, replica_groups=mesh['groups'=2,'pair'=16] {'pair'}, dimensions={0} | all-to-all | bytes 2228224 | tf_op jit(solution)/shard_map/all_to_all | solution.py:307
  47.1 2.9 %cells_first.1 = (f32[64,8192]{1,0:T(8,128)S(1)}, f32[64,128]{1,0:T(8,128)S(1)}, bf16[16,272,128]{2,1,0:T(8,128)(2,1)S(1)}, s32[16,128]{1,0:T(8,128)S(1)}) custom-call(bf16[16,272,128]{2,1,0:T(8,128)(2,1)S(1)} %all_to_all.30.refs_0_), custom_call_target="tpu_custom_call" | custom-call | bytes 6291456 | tf_op jit(solution)/shard_map/cells_first/pallas_call | solution.py:316
  50.1 31.3 %all_to_all.31.fetched_ref = bf16[16,272,128]{2,1,0:T(8,128)(2,1)S(1)} all-to-all(bf16[16,272,128]{2,1,0:T(8,128)(2,1)S(1)} %get-tuple-element.23), channel_id=1, replica_groups=mesh['groups'=2,'pair'=16] {'pair'}, dimensions={0} | all-to-all | bytes 2228224 | tf_op jit(solution)/shard_map/all_to_all | solution.py:307
  81.4 0.0 copy-done.1
  81.4 5.7 %pairs.2 = (bf16[16,272,128]{2,1,0:T(8,128)(2,1)S(1)}, f32[64,1024]{1,0:T(8,128)S(1)}, f32[64,128]{1,0:T(8,128)S(1)}) custom-call(s32[128]{0:T(128)S(1)} %get-tuple-element.22.target_ref, bf16[16,272,128]{2,1,0:T(8,128)(2,1)S(1)} %all_to_all.31.fetched_ref, f32[64,1024]{1,0:T(8,128)S(1)} %bitcast.4, f32[64,128]{1,0:T(8,128)S(1)} %get-tuple-element.20.beta_ref.refs_0_, ...), custom_call_target="tpu_custom_call" | custom-call | flops 536870912 | bytes 8388608 | tf_op jit(solution)/shard_map/pairs/pallas_call | solution.py:326
  87.1 31.3 %all_to_all.32.refs_1_ = bf16[16,272,128]{2,1,0:T(8,128)(2,1)S(1)} all-to-all(bf16[16,272,128]{2,1,0:T(8,128)(2,1)S(1)} %get-tuple-element.24), channel_id=1, replica_groups=mesh['groups'=2,'pair'=16] {'pair'}, dimensions={0} | all-to-all | bytes 2228224 | tf_op jit(solution)/shard_map/all_to_all | solution.py:307
  118.4 2.4 %cells.1 = (f32[64,8192]{1,0:T(8,128)S(1)}, f32[64,128]{1,0:T(8,128)S(1)}, bf16[16,272,128]{2,1,0:T(8,128)(2,1)S(1)}) custom-call(s32[16,128]{1,0:T(8,128)S(1)} %get-tuple-element.21.refs_0_, bf16[16,272,128]{2,1,0:T(8,128)(2,1)S(1)} %all_to_all.32.refs_1_, f32[64,8192]{1,0:T(8,128)S(1)} %get-tuple-element.25.refs_2_.refs_5_, ...), custom_call_target="tpu_custom_call" | custom-call | bytes 8388608 | tf_op jit(solution)/shard_map/cells/pallas_call | solution.py:334
  120.8 0.0 copy-start.2
  120.8 31.3 %all_to_all.33.fetched_ref = bf16[16,272,128]{2,1,0:T(8,128)(2,1)S(1)} all-to-all(bf16[16,272,128]{2,1,0:T(8,128)(2,1)S(1)} %get-tuple-element.28), channel_id=1, replica_groups=mesh['groups'=2,'pair'=16] {'pair'}, dimensions={0} | all-to-all | bytes 2228224 | tf_op jit(solution)/shard_map/all_to_all | solution.py:307
  152.1 6.3 %pairs.3 = (bf16[16,272,128]{2,1,0:T(8,128)(2,1)S(1)}, f32[64,1024]{1,0:T(8,128)}, f32[64,128]{1,0:T(8,128)S(1)}) custom-call(s32[128]{0:T(128)S(1)} %get-tuple-element.22.target_ref, bf16[16,272,128]{2,1,0:T(8,128)(2,1)S(1)} %all_to_all.33.fetched_ref, f32[64,1024]{1,0:T(8,128)S(1)} %get-tuple-element.29.data_ref, ...), custom_call_target="tpu_custom_call" | custom-call | flops 536870912 | bytes 8388608 | tf_op jit(solution)/shard_map/pairs/pallas_call | solution.py:326
  158.4 31.3 %all_to_all.34.refs_1_ = bf16[16,272,128]{2,1,0:T(8,128)(2,1)S(1)} all-to-all(bf16[16,272,128]{2,1,0:T(8,128)(2,1)S(1)} %get-tuple-element.30), channel_id=1, replica_groups=mesh['groups'=2,'pair'=16] {'pair'}, dimensions={0} | all-to-all | bytes 2228224 | tf_op jit(solution)/shard_map/all_to_all | solution.py:307
  189.7 0.0 copy-done.2
  189.7 2.7 %cells_last.1 = (f32[64,8192]{1,0:T(8,128)S(1)}, f32[64,128]{1,0:T(8,128)S(1)}, f32[16,16,128]{2,1,0:T(8,128)}) custom-call(s32[16,128]{1,0:T(8,128)S(1)} %get-tuple-element.21.refs_0_, bf16[16,272,128]{2,1,0:T(8,128)(2,1)S(1)} %all_to_all.34.refs_1_, f32[64,8192]{1,0:T(8,128)S(1)} %get-tuple-element.31.refs_2_.refs_6_, ...), custom_call_target="tpu_custom_call" | custom-call | bytes 8388608 | tf_op jit(solution)/shard_map/cells_last/pallas_call | solution.py:334
  192.4 0.0 copy-start.4
  192.4 1.3 copy-done.4
  193.7 3.5 %all-to-all-start.5 = ((f32[16,16,128]{2,1,0:T(8,128)}), f32[16,16,128]{2,1,0:T(8,128)S(1)}, u32[]{:S(2)}, u32[]{:S(2)}) async-start(f32[16,16,128]{2,1,0:T(8,128)} %get-tuple-element.34), calls=%async_computation.5 | async-start | bytes 262144 | tf_op jit(solution)/shard_map/all_to_all | solution.py:307
  197.2 0.0 copy-start.3
  197.2 1.6 copy-done.3
  198.8 2.1 %estimate.1 = f32[64,8192]{1,0:T(8,128)} custom-call(f32[64,128]{1,0:T(8,128)S(1)} %get-tuple-element.20.beta_ref.refs_0_, f32[64,128]{1,0:T(8,128)S(1)} %get-tuple-element.27.beta_ref.refs_1_, f32[64,128]{1,0:T(8,128)S(1)} %get-tuple-element.33.refs_2_, f32[64,128]{1,0:T(8,128)S(1)} %get-tuple-element.26.refs_3_, ...), custom_call_target="tpu_custom_call" | custom-call | bytes 6291456 | tf_op jit(solution)/shard_map/estimate/pallas_call | solution.py:341
  200.9 4.2 %all-to-all-done.5.tails_ref = f32[16,16,128]{2,1,0:T(8,128)S(1)} async-done(((f32[16,16,128]{2,1,0:T(8,128)}), f32[16,16,128]{2,1,0:T(8,128)S(1)}, u32[]{:S(2)}, u32[]{:S(2)}) %all-to-all-start.5) | async-done | bytes 131104 | tf_op jit(solution)/shard_map/all_to_all | solution.py:307
  205.1 0.0 copy-start.5
  205.1 1.6 copy-done.5
  206.7 1.9 model.1
Async XLA Ops:
  0.6 2.2 %copy-start = (bf16[8,16,128,128]{3,2,1,0:T(8,128)(2,1)S(1)}, bf16[8,16,128,128]{3,2,1,0:T(8,128)(2,1)}, u32[]{:S(2)}) copy-start(bf16[8,16,128,128]{3,2,1,0:T(8,128)(2,1)} %rays_ref.5) | copy-start | bytes 12582916
  2.8 0.9 copy-start.6
  3.8 0.7 copy-start.7
  4.5 0.7 copy-start.8
  11.2 70.2 %copy-start.1 = (bf16[8,16,128,128]{3,2,1,0:T(8,128)(2,1)S(1)}, bf16[8,16,128,128]{3,2,1,0:T(8,128)(2,1)}, u32[]{:S(2)}) copy-start(bf16[8,16,128,128]{3,2,1,0:T(8,128)(2,1)} %rays_ref.5) | copy-start | bytes 12582916
  120.8 68.9 %copy-start.2 = (f32[64,8192]{1,0:T(8,128)}, f32[64,8192]{1,0:T(8,128)S(1)}, u32[]{:S(2)}) copy-start(f32[64,8192]{1,0:T(8,128)S(1)} %get-tuple-element.31.refs_2_.refs_6_) | copy-start | bytes 6291460
  192.4 1.3 copy-start.4
  193.7 11.4 %all-to-all-start.5 = ((f32[16,16,128]{2,1,0:T(8,128)}), f32[16,16,128]{2,1,0:T(8,128)S(1)}, u32[]{:S(2)}, u32[]{:S(2)}) async-start(f32[16,16,128]{2,1,0:T(8,128)} %get-tuple-element.34), calls=%async_computation.5 | async-start | bytes 262144 | tf_op jit(solution)/shard_map/all_to_all | solution.py:307
  197.2 1.6 copy-start.3
  205.1 1.6 copy-start.5

commit v2 on v1

--- a/solution.py
+++ b/solution.py
@@ -12,6 +12,7 @@
 BS = 128
 TAIL = 16
 ITERS = 2
+PARTS = 2
 EPS = 1e-12
 F32 = jnp.float32
 BF16 = jnp.bfloat16
@@ -49,9 +50,9 @@
     return pl.ds(pl.multiple_of(block * BS, BS), BS)
 
 
-def transposed(data_ref, rays_ref, target_ref, total_ref, message_ref):
+def transposed(data_ref, rows, rays_ref, target_ref, total_ref, message_ref):
     pair_count, slot_count = rays_ref.shape[:2]
-    cols = data_ref.shape[0]
+    cols = total_ref.shape[1]
     peers = message_ref.shape[0]
     spots = peers * BCAP
 
@@ -62,10 +63,14 @@
     lax.fori_loop(0, spots, clear, 0, unroll=8)
 
     def one_pair(pair, carry):
-        data = data_ref[:, lanes(pair)].astype(BF16)
+        data = data_ref[rows, lanes(pair)]
+        high = data.astype(BF16)
+        low = (data - high.astype(F32)).astype(BF16)
+        pieces = jnp.concatenate([high, low], axis=0)
         for slot in range(0, slot_count, 2):
             rays = jnp.concatenate([rays_ref[pair, slot], rays_ref[pair, slot + 1]], axis=1)
-            part = jnp.dot(data, rays, preferred_element_type=F32)
+            part = jnp.dot(pieces, rays, preferred_element_type=F32)
+            part = part[:cols] + part[cols:]
             for half in range(2):
                 spot = target_ref[pair * slot_count + slot + half]
                 total_ref[spot] += part[:, half * BS : (half + 1) * BS]
@@ -83,12 +88,46 @@
     lax.fori_loop(0, peers, pack, 0, unroll=2)
 
 
-def start_kernel(
-    cells_ref, counts_ref, times_ref, rays_ref, message_ref, target_ref, total_ref, table_ref, used_ref
-):
+def start_kernel(part, *refs):
+    if part == 0:
+        cells_ref, counts_ref, times_ref, rays_ref, message_ref, target_ref = refs[:6]
+        total_ref, table_ref, used_ref = refs[6:]
+    else:
+        target_ref, times_ref, rays_ref, message_ref, total_ref = refs
     pair_count, slot_count = rays_ref.shape[:2]
     peers = message_ref.shape[0]
-    cols = times_ref.shape[0]
+    cols = total_ref.shape[1]
+    columns = slice(part * cols, (part + 1) * cols)
+    if part == 0:
+        find_places(cells_ref, counts_ref, target_ref, table_ref, used_ref)
+    transposed(times_ref, columns, rays_ref, target_ref, total_ref, message_ref)
+    squares = jnp.zeros((cols, BS), F32)
+    for pair in range(pair_count):
+        values = times_ref[columns, pair * BS : (pair + 1) * BS]
+        squares += values * values
+    tail = squares_tail(squares)
+    if part != 0:
+        message_ref[:, BCAP * cols :, :] = jnp.broadcast_to(
+            tail.astype(BF16)[None], (peers, TAIL, BS)
+        )
+        return
+    place = lax.broadcasted_iota(jnp.int32, (TAIL, BS), 0)
+    lane = lax.broadcasted_iota(jnp.int32, (TAIL, BS), 1)
+
+    def ask(peer, carry):
+        rows = tail
+        for rank in range(BCAP):
+            asked = table_ref[peer * BCAP + rank].astype(F32)
+            rows = jnp.where((place == 3) & (lane == rank), asked, rows)
+        message_ref[peer, BCAP * cols :, :] = rows.astype(BF16)
+        return carry
+
+    lax.fori_loop(0, peers, ask, 0)
+
+
+def find_places(cells_ref, counts_ref, target_ref, table_ref, used_ref):
+    pair_count, slot_count = cells_ref.shape
+    peers = used_ref.shape[0]
     owned = CELL_DEV // BS
 
     def clear(peer, carry):
@@ -117,33 +156,15 @@
         return carry
 
     lax.fori_loop(0, pair_count, one_pair, 0)
-    transposed(times_ref, rays_ref, target_ref, total_ref, message_ref)
-    squares = jnp.zeros((cols, BS), F32)
-    for pair in range(pair_count):
-        part = times_ref[:, pair * BS : (pair + 1) * BS]
-        squares += part * part
-    tail = squares_tail(squares)
-    place = lax.broadcasted_iota(jnp.int32, (TAIL, BS), 0)
-    lane = lax.broadcasted_iota(jnp.int32, (TAIL, BS), 1)
-
-    def ask(peer, carry):
-        rows = tail
-        for rank in range(BCAP):
-            asked = table_ref[peer * BCAP + rank].astype(F32)
-            rows = jnp.where((place == 3) & (lane == rank), asked, rows)
-        message_ref[peer, BCAP * cols :, :] = rows.astype(BF16)
-        return carry
-
-    lax.fori_loop(0, peers, ask, 0)
 
 
 def pair_kernel(
-    target_ref, fetched_ref, data_ref, beta_ref, rays_ref,
+    rows, target_ref, fetched_ref, data_ref, beta_ref, rays_ref,
     message_ref, raw_ref, alpha_ref, total_ref,
 ):
     pair_count, slot_count = rays_ref.shape[:2]
     peers = message_ref.shape[0]
-    cols = data_ref.shape[0]
+    cols = raw_ref.shape[0]
     spots = peers * BCAP
     alpha = norm_of_tails(fetched_ref, cols)
     alpha_ref[...] = alpha
@@ -156,39 +177,42 @@
             spot = target_ref[pair * slot_count + slot]
             live = spot < spots
             spot = jnp.where(live, spot, 0)
-            rows = pl.ds(pl.multiple_of((spot % BCAP) * cols, cols), cols)
-            block = fetched_ref[spot // BCAP, rows, :]
+            inside = pl.ds(pl.multiple_of((spot % BCAP) * cols, cols), cols)
+            block = fetched_ref[spot // BCAP, inside, :]
             chosen.append(jnp.where(live, block, jnp.zeros_like(block)))
         rays = jnp.concatenate([rays_ref[pair, slot] for slot in range(slot_count)], axis=1)
         product = lax.dot_general(
             jnp.concatenate(chosen, axis=1), rays, (((1,), (1,)), ((), ())),
             preferred_element_type=F32,
         )
-        raw = product * model_scale - data_ref[:, lanes(pair)] * data_scale
+        raw = product * model_scale - data_ref[rows, lanes(pair)] * data_scale
         raw_ref[:, lanes(pair)] = raw
         return squares + raw * raw
 
     squares = lax.fori_loop(0, pair_count, one_pair, jnp.zeros((cols, BS), F32))
-    transposed(raw_ref, rays_ref, target_ref, total_ref, message_ref)
+    transposed(raw_ref, slice(0, cols), rays_ref, target_ref, total_ref, message_ref)
     tail = squares_tail(squares).astype(BF16)
     message_ref[:, BCAP * cols :, :] = jnp.broadcast_to(tail[None], (peers, TAIL, BS))
 
 
 def cell_kernel(first, last, *refs):
-    if first:
+    finds = first and len(refs) == 7
+    if finds:
         arrived_ref, raw_ref, beta_ref, out_ref, asked_ref, table_ref, sem = refs
+    elif first:
+        asked_ref, arrived_ref, raw_ref, beta_ref, out_ref = refs
     else:
-        asked_ref, arrived_ref, model_ref, alpha_ref, raw_ref, beta_ref, out_ref = refs
+        asked_ref, arrived_ref, model_ref, alpha_ref, *others, raw_ref, beta_ref, out_ref = refs
     peers = arrived_ref.shape[0]
     cols, cells = raw_ref.shape
-    if first:
+    if finds:
         table_ref[...] = arrived_ref[:, BCAP * cols :, :].astype(F32)[:, 3, :].astype(jnp.int32)
         copy = pltpu.make_async_copy(table_ref, asked_ref, sem)
         copy.start()
     beta = norm_of_tails(arrived_ref, cols)
     beta_ref[...] = beta
     raw_ref[...] = jnp.zeros((cols, cells), F32)
-    if first:
+    if finds:
         copy.wait()
 
     def add(peer, carry):
@@ -212,7 +236,8 @@
     squares = lax.fori_loop(0, cells // BS, settle, jnp.zeros((cols, BS), F32), unroll=4)
     tail = squares_tail(squares)
     if last:
-        out_ref[...] = jnp.broadcast_to(tail[None], out_ref.shape).astype(out_ref.dtype)
+        tails = jnp.concatenate([other[...] for other in others] + [tail], axis=0)
+        out_ref[...] = jnp.broadcast_to(tails, out_ref.shape)
         return
     out_ref[:, BCAP * cols :, :] = jnp.broadcast_to(tail[None], (peers, TAIL, BS)).astype(BF16)
 
@@ -226,11 +251,19 @@
 
 
 def estimate_kernel(*refs):
-    betas = refs[0 : ITERS + 1]
-    alphas = refs[ITERS + 1 : 2 * ITERS + 1]
-    models = refs[2 * ITERS + 1 : 3 * ITERS + 1]
     estimate_ref = refs[-1]
-    cols, cells = estimate_ref.shape
+    each = 3 * ITERS + 1
+    for part in range(len(refs) // each):
+        some = refs[part * each : (part + 1) * each]
+        estimate_part(
+            some[: ITERS + 1], some[ITERS + 1 : 2 * ITERS + 1], some[2 * ITERS + 1 :],
+            estimate_ref, part,
+        )
+
+
+def estimate_part(betas, alphas, models, estimate_ref, part):
+    cols, cells = models[0].shape
+    rows = slice(part * cols, (part + 1) * cols)
     phi_bar = betas[0][...]
     rho_bar = alphas[0][...]
     trace = [1.0 / alphas[0][...]]
@@ -256,24 +289,28 @@
         total = weight[0] * models[0][:, where]
         for i in range(1, ITERS):
             total += weight[i] * models[i][:, where]
-        estimate_ref[:, where] = total
+        estimate_ref[rows, where] = total
         return carry
 
     lax.fori_loop(0, cells // BS, one_block, 0, unroll=4)
 
 
-def model_kernel(tails_ref, raw_ref, model_ref):
-    cols, cells = raw_ref.shape
+def model_kernel(tails_ref, *refs):
+    model_ref = refs[-1]
     summed = jnp.sum(tails_ref[...], axis=0)
-    row = summed[0:1] + summed[1:2] + summed[2:3]
-    column = jnp.sum(jnp.where(diagonal(cols), row, 0.0), axis=1, keepdims=True)
-    scale = jnp.broadcast_to(1.0 / jnp.sqrt(column + EPS), (cols, BS))
-
-    def one_block(block, carry):
-        model_ref[:, lanes(block)] = raw_ref[:, lanes(block)] * scale
-        return carry
-
-    lax.fori_loop(0, cells // BS, one_block, 0, unroll=4)
+    for part, raw_ref in enumerate(refs[:-1]):
+        cols, cells = raw_ref.shape
+        rows = slice(part * cols, (part + 1) * cols)
+        some = summed[part * TAIL : (part + 1) * TAIL]
+        row = some[0:1] + some[1:2] + some[2:3]
+        column = jnp.sum(jnp.where(diagonal(cols), row, 0.0), axis=1, keepdims=True)
+        scale = jnp.broadcast_to(1.0 / jnp.sqrt(column + EPS), (cols, BS))
+
+        def one_block(block, carry):
+            model_ref[rows, lanes(block)] = raw_ref[:, lanes(block)] * scale
+            return carry
+
+        lax.fori_loop(0, cells // BS, one_block, 0, unroll=4)
 
 
 def call(kernel, name, in_spaces, outs, scratch=(), flops=0, moved=0):
@@ -295,55 +332,88 @@
     peers = lax.axis_size("pair")
     spots = peers * BCAP
     times = travel_times.T
-    cols, pairs = times.shape
+    pairs = times.shape[1]
+    cols = times.shape[0] // PARTS
+    parts = range(PARTS)
     message = ((peers, BCAP * cols + TAIL, BS), BF16, VMEM)
     tile = ((cols, BS), F32, VMEM)
     data = ((cols, pairs), F32, VMEM)
     model = ((cols, CELL_DEV), F32, VMEM)
+    whole = ((times.shape[0], CELL_DEV), F32, VMEM)
     totals = VMEM((spots + 1, cols, BS), F32)
-    flops = 2 * slots * BS * BS * cols
+    flops = 4 * slots * BS * BS * cols
 
     def exchange(values):
         return lax.all_to_all(values, "pair", split_axis=0, concat_axis=0, tiled=True)
 
-    outgoing, target = call(
-        start_kernel, "start", [SMEM, SMEM, VMEM, VMEM],
-        [message, ((slots,), jnp.int32, SMEM)],
-        [totals, SMEM((spots,), jnp.int32), SMEM((peers,), jnp.int32)],
-        flops, 6 << 20,
-    )(block_cells, block_counts, times, ray_blocks)
-    arrived = exchange(outgoing)
-    raw, beta, reply, asked = call(
-        functools.partial(cell_kernel, True, False), "cells_first", [VMEM],
-        [model, tile, message, ((peers, BS), jnp.int32, SMEM)],
-        [VMEM((peers, BS), jnp.int32), pltpu.SemaphoreType.DMA],
-        0, 6 << 20,
-    )(arrived)
-    models, betas, alphas = [raw], [beta], []
-    current = times
+    arrived, fetched = [None] * PARTS, [None] * PARTS
+    models, betas, alphas = ([[] for _ in parts] for _ in range(3))
+    for part in parts:
+        if part == 0:
+            outgoing, target = call(
+                functools.partial(start_kernel, part), "start", [SMEM, SMEM, VMEM, VMEM],
+                [message, ((slots,), jnp.int32, SMEM)],
+                [totals, SMEM((spots,), jnp.int32), SMEM((peers,), jnp.int32)], flops, 6 << 20,
+            )(block_cells, block_counts, times, ray_blocks)
+        else:
+            (outgoing,) = call(
+                functools.partial(start_kernel, part), "start_more", [SMEM, VMEM, VMEM],
+                [message], [totals], flops, 6 << 20,
+            )(target, times, ray_blocks)
+        arrived[part] = exchange(outgoing)
+    for part in parts:
+        if part == 0:
+            raw, beta, reply, asked = call(
+                functools.partial(cell_kernel, True, False), "cells_first", [VMEM],
+                [model, tile, message, ((peers, BS), jnp.int32, SMEM)],
+                [VMEM((peers, BS), jnp.int32), pltpu.SemaphoreType.DMA], 0, 6 << 20,
+            )(arrived[part])
+        else:
+            raw, beta, reply = call(
+                functools.partial(cell_kernel, True, False), "cells_more", [SMEM, VMEM],
+                [model, tile, message], (), 0, 6 << 20,
+            )(asked, arrived[part])
+        models[part].append(raw)
+        betas[part].append(beta)
+        fetched[part] = exchange(reply)
+    current = [times] * PARTS
+    tails = []
     for step in range(ITERS):
-        fetched = exchange(reply)
-        outgoing, current, alpha = call(
-            pair_kernel, "pairs", [SMEM, VMEM, VMEM, VMEM, VMEM],
-            [message, data, tile], [totals], 2 * flops, 8 << 20,
-        )(target, fetched, current, betas[-1], ray_blocks)
-        alphas.append(alpha)
-        arrived = exchange(outgoing)
+        for part in parts:
+            rows = slice(part * cols, (part + 1) * cols) if step == 0 else slice(0, cols)
+            outgoing, current[part], alpha = call(
+                functools.partial(pair_kernel, rows), "pairs", [SMEM, VMEM, VMEM, VMEM, VMEM],
+                [message, data, tile], [totals], 2 * flops, 8 << 20,
+            )(target, fetched[part], current[part], betas[part][-1], ray_blocks)
+            alphas[part].append(alpha)
+            arrived[part] = exchange(outgoing)
         last = step + 1 == ITERS
-        out = ((peers, TAIL, BS), F32, VMEM) if last else message
-        raw, beta, reply = call(
-            functools.partial(cell_kernel, False, last), "cells_last" if last else "cells",
-            [SMEM, VMEM, VMEM, VMEM], [model, tile, out], (), 0, 8 << 20,
-        )(asked, arrived, models[-1], alpha)
-        betas.append(beta)
-        models.append(raw)
-    tails = exchange(reply)
-    (estimate,) = call(
-        estimate_kernel, "estimate", [VMEM] * (3 * ITERS + 1), [model], (), 0, 6 << 20
-    )(*betas, *alphas, *models[:ITERS])
-    (model_vec,) = call(model_kernel, "model", [VMEM, VMEM], [model], (), 0, 4 << 20)(
-        tails, models[-1]
+        for part in parts:
+            out, others = message, []
+            if last and part + 1 < PARTS:
+                out = ((TAIL, BS), F32, VMEM)
+            elif last:
+                out, others = ((peers, PARTS * TAIL, BS), F32, VMEM), tails
+            raw, beta, reply = call(
+                functools.partial(cell_kernel, False, last), "cells_last" if last else "cells",
+                [SMEM] + [VMEM] * (3 + len(others)), [model, tile, out], (), 0, 8 << 20,
+            )(asked, arrived[part], models[part][-1], alphas[part][-1], *others)
+            betas[part].append(beta)
+            models[part].append(raw)
+            if not last:
+                fetched[part] = exchange(reply)
+            elif part + 1 < PARTS:
+                tails.append(reply)
+    summed = exchange(reply)
+    given = [
+        ref for part in parts for ref in betas[part] + alphas[part] + models[part][:ITERS]
+    ]
+    (estimate,) = call(estimate_kernel, "estimate", [VMEM] * len(given), [whole], (), 0, 6 << 20)(
+        *given
     )
+    (model_vec,) = call(
+        model_kernel, "model", [VMEM] * (PARTS + 1), [whole], (), 0, 4 << 20
+    )(summed, *[models[part][-1] for part in parts])
     return (estimate.T, model_vec.T)
 
 

time: 209 us -> 242 us (1.16)
  blocking collectives: 161 us -> 0 us
  waiting for transfers between devices: 4.22 us -> 98.6 us
  starting transfers between devices: 3.51 us -> 51.9 us
  local copies, waits for them, and re-layouts: 8.99 us -> 37.7 us
  Pallas kernels: 30 us -> 50.7 us
    all_to_all x5 -> x0, blocking collectives: 161 us -> none  [exchange(): lax.all_to_all(values, 'pair', split_axis=0, concat_axis=0, tiled=True)]
    all_to_all x1 -> x11, waiting for transfers between devices: 4.22 us -> 98.6 us  [exchange(): lax.all_to_all(values, 'pair', split_axis=0, concat_axis=0, tiled=True)]
    all_to_all x1 -> x11, starting transfers between devices: 3.51 us -> 51.9 us  [exchange(): lax.all_to_all(values, 'pair', split_axis=0, concat_axis=0, tiled=True)]
    unnamed x18 -> x84, local copies, waits for them, and re-layouts: 8.99 us -> 37.7 us
    pallas_call x5 -> x9, Pallas kernels: 22 us -> 39.8 us  [the longest x4 24 us: on_device(): call(functools.partial(pair_kernel, rows), 'pairs', [SMEM, VMEM, VMEM, VM...]
    pallas_call x2 -> x4, Pallas kernels: 5.08 us -> 8.32 us  [on_device(): call(functools.partial(cell_kernel, False, last), 'cells_last' if last el...]
  transfers between devices with their start and end apart: 1 -> 11, of which waited for: 1 -> 11; matrix products, arithmetic and copies ran while one was open for 0% -> 0% of each run, Pallas kernels for 1% -> 17%
where the time goes in v2:
time: 242 us; the launch traced here: 240 us
  waiting for transfers between devices  98.6 us (41%)
  starting transfers between devices  51.9 us (21%)
  Pallas kernels  50.7 us (21%)
  local copies, waits for them, and re-layouts  37.7 us (16%)
    all_to_all x11, waiting for transfers between devices, exchange(): lax.all_to_all(values, 'pair', split_axis=0, concat_axis=0, tiled=True)  98.6 us
    all_to_all x11, starting transfers between devices, exchange(): lax.all_to_all(values, 'pair', split_axis=0, concat_axis=0, tiled=True)  51.9 us
    unnamed x84, local copies, waits for them, and re-layouts  37.7 us
    pallas_call x4, Pallas kernels, on_device(): call(functools.partial(pair_kernel, rows), 'pairs', [SMEM, VMEM, VMEM, VM...  24 us
    pallas_call x4, Pallas kernels, on_device(): call(functools.partial(cell_kernel, False, last), 'cells_last' if last el...  8.32 us
    pallas_call x1, Pallas kernels, on_device(): call(functools.partial(start_kernel, part), 'start', [SMEM, SMEM, VMEM, V...  6.12 us
  transfers between devices with their start and end apart: 11, of which 11 were waited for; matrix products, arithmetic and copies ran while one was open for 0% of the time, Pallas kernels for 17%

profile of v2, /device:TPU:0, one launch (start us, length us, event | category | flops | bytes accessed | tf_op | source)
XLA Modules:
  0.0 239.9 jit_solution(16813481122419289233)
XLA Ops:
  0.6 2.2 copy-done
  2.8 0.9 copy-done.9
  5.1 6.1 %start.1 = (bf16[16,144,128]{2,1,0:T(8,128)(2,1)}, s32[128]{0:T(128)S(1)}) custom-call(s32[8,16]{1,0:T(8,128)S(1)} %copy-done.40, s32[8]{0:T(128)S(1)} %copy-done.41, f32[64,1024]{1,0:T(8,128)S(1)} %bitcast.3, bf16[8,16,128,128]{3,2,1,0:T(8,128)(2,1)S(1)} %copy-done), custom_call_target="tpu_custom_call" | custom-call | flops 268435456 | bytes 6291456 | tf_op jit(solution)/shard_map/start/pallas_call | solution.py:353
  11.2 7.4 %all-to-all-start = ((bf16[16,144,128]{2,1,0:T(8,128)(2,1)}), bf16[16,144,128]{2,1,0:T(8,128)(2,1)S(1)}, u32[]{:S(2)}, u32[]{:S(2)}) async-start(bf16[16,144,128]{2,1,0:T(8,128)(2,1)} %get-tuple-element.33), calls=%async_computation | async-start | bytes 1179648 | tf_op jit(solution)/shard_map/all_to_all | solution.py:347
  18.7 2.2 copy-done.1
  20.9 3.7 %start_more.1 = bf16[16,144,128]{2,1,0:T(8,128)(2,1)} custom-call(s32[128]{0:T(128)S(1)} %get-tuple-element.36.target_ref.refs_0_, f32[64,1024]{1,0:T(8,128)S(1)} %bitcast.4, bf16[8,16,128,128]{3,2,1,0:T(8,128)(2,1)S(1)} %copy-done.1), custom_call_target="tpu_custom_call" | custom-call | flops 268435456 | bytes 6291456 | tf_op jit(solution)/shard_map/start_more/pallas_call | solution.py:359
  24.6 9.6 %all-to-all-done.refs_0_ = bf16[16,144,128]{2,1,0:T(8,128)(2,1)S(1)} async-done(((bf16[16,144,128]{2,1,0:T(8,128)(2,1)}), bf16[16,144,128]{2,1,0:T(8,128)(2,1)S(1)}, u32[]{:S(2)}, u32[]{:S(2)}) %all-to-all-start) | async-done | bytes 589856 | tf_op jit(solution)/shard_map/all_to_all | solution.py:347
  34.2 4.4 %all-to-all-start.5 = ((bf16[16,144,128]{2,1,0:T(8,128)(2,1)}), bf16[16,144,128]{2,1,0:T(8,128)(2,1)S(1)}, u32[]{:S(2)}, u32[]{:S(2)}) async-start(bf16[16,144,128]{2,1,0:T(8,128)(2,1)} %start_more.1), calls=%async_computation.5 | async-start | bytes 1179648 | tf_op jit(solution)/shard_map/all_to_all | solution.py:347
  38.7 2.6 %cells_first.1 = (f32[32,8192]{1,0:T(8,128)S(1)}, f32[32,128]{1,0:T(8,128)S(1)}, bf16[16,144,128]{2,1,0:T(8,128)(2,1)}, s32[16,128]{1,0:T(8,128)S(1)}) custom-call(bf16[16,144,128]{2,1,0:T(8,128)(2,1)S(1)} %all-to-all-done.refs_0_), custom_call_target="tpu_custom_call" | custom-call | bytes 6291456 | tf_op jit(solution)/shard_map/cells_first/pallas_call | solution.py:366
  41.2 13.0 %all-to-all-done.5.refs_1_ = bf16[16,144,128]{2,1,0:T(8,128)(2,1)S(1)} async-done(((bf16[16,144,128]{2,1,0:T(8,128)(2,1)}), bf16[16,144,128]{2,1,0:T(8,128)(2,1)S(1)}, u32[]{:S(2)}, u32[]{:S(2)}) %all-to-all-start.5) | async-done | bytes 589856 | tf_op jit(solution)/shard_map/all_to_all | solution.py:347
  54.2 4.4 %all-to-all-start.1 = ((bf16[16,144,128]{2,1,0:T(8,128)(2,1)}), bf16[16,144,128]{2,1,0:T(8,128)(2,1)S(1)}, u32[]{:S(2)}, u32[]{:S(2)}) async-start(bf16[16,144,128]{2,1,0:T(8,128)(2,1)} %get-tuple-element.37), calls=%async_computation.1 | async-start | bytes 1179648 | tf_op jit(solution)/shard_map/all_to_all | solution.py:347
  58.6 1.8 cells_more.1
  60.5 0.8 copy-done.23
  61.9 12.3 %all-to-all-done.1.fetched_ref = bf16[16,144,128]{2,1,0:T(8,128)(2,1)S(1)} async-done(((bf16[16,144,128]{2,1,0:T(8,128)(2,1)}), bf16[16,144,128]{2,1,0:T(8,128)(2,1)S(1)}, u32[]{:S(2)}, u32[]{:S(2)}) %all-to-all-start.1) | async-done | bytes 589856 | tf_op jit(solution)/shard_map/all_to_all | solution.py:347
  74.2 4.4 %all-to-all-start.6 = ((bf16[16,144,128]{2,1,0:T(8,128)(2,1)}), bf16[16,144,128]{2,1,0:T(8,128)(2,1)S(1)}, u32[]{:S(2)}, u32[]{:S(2)}) async-start(bf16[16,144,128]{2,1,0:T(8,128)(2,1)} %copy-done.23), calls=%async_computation.6 | async-start | bytes 1179648 | tf_op jit(solution)/shard_map/all_to_all | solution.py:347
  78.6 2.2 copy-done.2
  80.8 0.7 copy-done.29
  81.5 5.2 %pairs.4 = (bf16[16,144,128]{2,1,0:T(8,128)(2,1)S(1)}, f32[32,1024]{1,0:T(8,128)S(1)}, f32[32,128]{1,0:T(8,128)S(1)}) custom-call(s32[128]{0:T(128)S(1)} %get-tuple-element.36.target_ref.refs_0_, bf16[16,144,128]{2,1,0:T(8,128)(2,1)S(1)} %all-to-all-done.1.fetched_ref, f32[64,1024]{1,0:T(8,128)S(1)} %bitcast.5, f32[32,128]{1,0:T(8,128)S(1)} %copy-done.29, ...), custom_call_target="tpu_custom_call" | custom-call | flops 536870912 | bytes 8388608 | tf_op jit(solution)/shard_map/pairs/pallas_call | solution.py:384
  86.8 0.8 copy-done.24
  88.8 5.3 %all-to-all-done.6.fetched_ref = bf16[16,144,128]{2,1,0:T(8,128)(2,1)S(1)} async-done(((bf16[16,144,128]{2,1,0:T(8,128)(2,1)}), bf16[16,144,128]{2,1,0:T(8,128)(2,1)S(1)}, u32[]{:S(2)}, u32[]{:S(2)}) %all-to-all-start.6) | async-done | bytes 589856 | tf_op jit(solution)/shard_map/all_to_all | solution.py:347
  94.2 0.8 copy-done.13
  95.0 4.4 %all-to-all-start.2 = ((bf16[16,144,128]{2,1,0:T(8,128)(2,1)}), bf16[16,144,128]{2,1,0:T(8,128)(2,1)S(1)}, u32[]{:S(2)}, u32[]{:S(2)}) async-start(bf16[16,144,128]{2,1,0:T(8,128)(2,1)} %copy-done.24), calls=%async_computation.2 | async-start | bytes 1179648 | tf_op jit(solution)/shard_map/all_to_all | solution.py:347
  99.4 2.2 copy-done.3
  101.6 1.1 copy-done.14
  102.7 0.7 copy-done.32
  103.4 6.1 %pairs.6 = (bf16[16,144,128]{2,1,0:T(8,128)(2,1)}, f32[32,1024]{1,0:T(8,128)S(1)}, f32[32,128]{1,0:T(8,128)S(1)}) custom-call(s32[128]{0:T(128)S(1)} %get-tuple-element.36.target_ref.refs_0_, bf16[16,144,128]{2,1,0:T(8,128)(2,1)S(1)} %copy-done.14, f32[64,1024]{1,0:T(8,128)S(1)} %bitcast.6, f32[32,128]{1,0:T(8,128)S(1)} %copy-done.32, ...), custom_call_target="tpu_custom_call" | custom-call | flops 536870912 | bytes 8388608 | tf_op jit(solution)/shard_map/pairs/pallas_call | solution.py:384
  109.5 5.5 %all-to-all-done.2.refs_1_ = bf16[16,144,128]{2,1,0:T(8,128)(2,1)S(1)} async-done(((bf16[16,144,128]{2,1,0:T(8,128)(2,1)}), bf16[16,144,128]{2,1,0:T(8,128)(2,1)S(1)}, u32[]{:S(2)}, u32[]{:S(2)}) %all-to-all-start.2) | async-done | bytes 589856 | tf_op jit(solution)/shard_map/all_to_all | solution.py:347
  115.0 4.5 %all-to-all-start.7 = ((bf16[16,144,128]{2,1,0:T(8,128)(2,1)}), bf16[16,144,128]{2,1,0:T(8,128)(2,1)}, u32[]{:S(2)}, u32[]{:S(2)}) async-start(bf16[16,144,128]{2,1,0:T(8,128)(2,1)} %get-tuple-element.50), calls=%async_computation.7 | async-start | bytes 1179648 | tf_op jit(solution)/shard_map/all_to_all | solution.py:347
  119.5 1.1 copy-done.12
  120.5 1.8 cells.2
  122.4 0.8 copy-done.22
  123.2 11.8 %all-to-all-done.7.refs_1_ = bf16[16,144,128]{2,1,0:T(8,128)(2,1)} async-done(((bf16[16,144,128]{2,1,0:T(8,128)(2,1)}), bf16[16,144,128]{2,1,0:T(8,128)(2,1)}, u32[]{:S(2)}, u32[]{:S(2)}) %all-to-all-start.7) | async-done | bytes 589856 | tf_op jit(solution)/shard_map/all_to_all | solution.py:347
  135.0 4.5 %all-to-all-start.3 = ((bf16[16,144,128]{2,1,0:T(8,128)(2,1)}), bf16[16,144,128]{2,1,0:T(8,128)(2,1)}, u32[]{:S(2)}, u32[]{:S(2)}) async-start(bf16[16,144,128]{2,1,0:T(8,128)(2,1)} %copy-done.22), calls=%async_computation.3 | async-start | bytes 1179648 | tf_op jit(solution)/shard_map/all_to_all | solution.py:347
  139.5 2.3 cells.3
  141.8 1.0 copy-done.6
  142.8 0.8 copy-done.21
  143.6 11.5 %all-to-all-done.3.fetched_ref = bf16[16,144,128]{2,1,0:T(8,128)(2,1)} async-done(((bf16[16,144,128]{2,1,0:T(8,128)(2,1)}), bf16[16,144,128]{2,1,0:T(8,128)(2,1)}, u32[]{:S(2)}, u32[]{:S(2)}) %all-to-all-start.3) | async-done | bytes 589856 | tf_op jit(solution)/shard_map/all_to_all | solution.py:347
  155.1 4.5 %all-to-all-start.8 = ((bf16[16,144,128]{2,1,0:T(8,128)(2,1)}), bf16[16,144,128]{2,1,0:T(8,128)(2,1)}, u32[]{:S(2)}, u32[]{:S(2)}) async-start(bf16[16,144,128]{2,1,0:T(8,128)(2,1)} %copy-done.21), calls=%async_computation.8 | async-start | bytes 1179648 | tf_op jit(solution)/shard_map/all_to_all | solution.py:347
  159.6 2.2 copy-done.4
  161.8 6.3 %pairs.5 = (bf16[16,144,128]{2,1,0:T(8,128)(2,1)S(1)}, f32[32,1024]{1,0:T(8,128)}, f32[32,128]{1,0:T(8,128)S(1)}) custom-call(s32[128]{0:T(128)S(1)} %get-tuple-element.36.target_ref.refs_0_, bf16[16,144,128]{2,1,0:T(8,128)(2,1)} %all-to-all-done.3.fetched_ref, f32[32,1024]{1,0:T(8,128)S(1)} %copy-done.27, f32[32,128]{1,0:T(8,128)S(1)} %get-tuple-element.41.beta_ref.refs_1_, ...), custom_call_target="tpu_custom_call" | custom-call | flops 536870912 | bytes 8388608 | tf_op jit(solution)/shard_map/pairs/pallas_call | solution.py:384
  168.1 0.8 copy-done.19
  169.0 6.2 %all-to-all-done.8.fetched_ref = bf16[16,144,128]{2,1,0:T(8,128)(2,1)} async-done(((bf16[16,144,128]{2,1,0:T(8,128)(2,1)}), bf16[16,144,128]{2,1,0:T(8,128)(2,1)}, u32[]{:S(2)}, u32[]{:S(2)}) %all-to-all-start.8) | async-done | bytes 589856 | tf_op jit(solution)/shard_map/all_to_all | solution.py:347
  175.2 4.5 %all-to-all-start.4 = ((bf16[16,144,128]{2,1,0:T(8,128)(2,1)}), bf16[16,144,128]{2,1,0:T(8,128)(2,1)}, u32[]{:S(2)}, u32[]{:S(2)}) async-start(bf16[16,144,128]{2,1,0:T(8,128)(2,1)} %copy-done.19), calls=%async_computation.4 | async-start | bytes 1179648 | tf_op jit(solution)/shard_map/all_to_all | solution.py:347
  179.7 2.2 copy-done.5
  181.9 6.3 %pairs.7 = (bf16[16,144,128]{2,1,0:T(8,128)(2,1)S(1)}, f32[32,1024]{1,0:T(8,128)}, f32[32,128]{1,0:T(8,128)S(1)}) custom-call(s32[128]{0:T(128)S(1)} %get-tuple-element.36.target_ref.refs_0_, bf16[16,144,128]{2,1,0:T(8,128)(2,1)} %all-to-all-done.8.fetched_ref, f32[32,1024]{1,0:T(8,128)S(1)} %get-tuple-element.55.data_ref, ...), custom_call_target="tpu_custom_call" | custom-call | flops 536870912 | bytes 8388608 | tf_op jit(solution)/shard_map/pairs/pallas_call | solution.py:384
  188.2 0.8 copy-done.20
  189.0 6.3 %all-to-all-done.4.refs_1_ = bf16[16,144,128]{2,1,0:T(8,128)(2,1)} async-done(((bf16[16,144,128]{2,1,0:T(8,128)(2,1)}), bf16[16,144,128]{2,1,0:T(8,128)(2,1)}, u32[]{:S(2)}, u32[]{:S(2)}) %all-to-all-start.4) | async-done | bytes 589856 | tf_op jit(solution)/shard_map/all_to_all | solution.py:347
  195.3 4.5 %all-to-all-start.9 = ((bf16[16,144,128]{2,1,0:T(8,128)(2,1)}), bf16[16,144,128]{2,1,0:T(8,128)(2,1)}, u32[]{:S(2)}, u32[]{:S(2)}) async-start(bf16[16,144,128]{2,1,0:T(8,128)(2,1)} %copy-done.20), calls=%async_computation.9 | async-start | bytes 1179648 | tf_op jit(solution)/shard_map/all_to_all | solution.py:347
  199.8 2.1 cells_last.2
  201.9 1.0 copy-done.15
  203.5 11.9 %all-to-all-done.9.refs_1_ = bf16[16,144,128]{2,1,0:T(8,128)(2,1)} async-done(((bf16[16,144,128]{2,1,0:T(8,128)(2,1)}), bf16[16,144,128]{2,1,0:T(8,128)(2,1)}, u32[]{:S(2)}, u32[]{:S(2)}) %all-to-all-start.9) | async-done | bytes 589856 | tf_op jit(solution)/shard_map/all_to_all | solution.py:347
  215.4 1.2 copy-done.7
  216.6 2.1 cells_last.3
  218.7 1.0 copy-done.17
  219.7 0.7 copy-done.25
  221.0 4.4 %all-to-all-start.10 = ((f32[16,32,128]{2,1,0:T(8,128)}), f32[16,32,128]{2,1,0:T(8,128)S(1)}, u32[]{:S(2)}, u32[]{:S(2)}) async-start(f32[16,32,128]{2,1,0:T(8,128)} %copy-done.25), calls=%async_computation.10 | async-start | bytes 524288 | tf_op jit(solution)/shard_map/all_to_all | solution.py:347
  225.4 1.2 copy-done.8
  226.6 0.7 copy-done.37
  227.4 0.7 copy-done.39
  228.1 2.2 estimate.1
  230.2 5.2 %all-to-all-done.10.tails_ref = f32[16,32,128]{2,1,0:T(8,128)S(1)} async-done(((f32[16,32,128]{2,1,0:T(8,128)}), f32[16,32,128]{2,1,0:T(8,128)S(1)}, u32[]{:S(2)}, u32[]{:S(2)}) %all-to-all-start.10) | async-done | bytes 262176 | tf_op jit(solution)/shard_map/all_to_all | solution.py:347
  235.4 1.2 copy-done.16
  236.7 1.2 copy-done.18
  237.9 2.0 model.1
  (56 shorter events, 4.5 us)
Async XLA Ops:
  0.6 2.2 copy-start
  2.8 0.9 copy-start.9
  3.8 0.7 copy-start.40
  4.5 0.7 copy-start.41
  5.1 13.6 %copy-start.10 = (f32[1024,64]{0,1:T(8,128)S(1)}, f32[1024,64]{0,1:T(8,128)}, u32[]{:S(2)}) copy-start(f32[1024,64]{0,1:T(8,128)} %param.7) | copy-start | bytes 786436
  11.2 23.0 %all-to-all-start = ((bf16[16,144,128]{2,1,0:T(8,128)(2,1)}), bf16[16,144,128]{2,1,0:T(8,128)(2,1)S(1)}, u32[]{:S(2)}, u32[]{:S(2)}) async-start(bf16[16,144,128]{2,1,0:T(8,128)(2,1)} %get-tuple-element.33), calls=%async_computation | async-start | bytes 1179648 | tf_op jit(solution)/shard_map/all_to_all | solution.py:347
  18.7 2.2 copy-start.1
  34.2 20.0 %all-to-all-start.5 = ((bf16[16,144,128]{2,1,0:T(8,128)(2,1)}), bf16[16,144,128]{2,1,0:T(8,128)(2,1)S(1)}, u32[]{:S(2)}, u32[]{:S(2)}) async-start(bf16[16,144,128]{2,1,0:T(8,128)(2,1)} %start_more.1), calls=%async_computation.5 | async-start | bytes 1179648 | tf_op jit(solution)/shard_map/all_to_all | solution.py:347
  41.2 17.4 %copy-start.28 = (f32[32,128]{1,0:T(8,128)}, f32[32,128]{1,0:T(8,128)S(1)}, u32[]{:S(2)}) copy-start(f32[32,128]{1,0:T(8,128)S(1)} %get-tuple-element.34.beta_ref.refs_0_) | copy-start | bytes 49156
  54.2 20.0 %all-to-all-start.1 = ((bf16[16,144,128]{2,1,0:T(8,128)(2,1)}), bf16[16,144,128]{2,1,0:T(8,128)(2,1)S(1)}, u32[]{:S(2)}, u32[]{:S(2)}) async-start(bf16[16,144,128]{2,1,0:T(8,128)(2,1)} %get-tuple-element.37), calls=%async_computation.1 | async-start | bytes 1179648 | tf_op jit(solution)/shard_map/all_to_all | solution.py:347
  60.4 0.8 copy-start.23
  61.3 0.6 copy-start.31
  74.2 20.0 %all-to-all-start.6 = ((bf16[16,144,128]{2,1,0:T(8,128)(2,1)}), bf16[16,144,128]{2,1,0:T(8,128)(2,1)S(1)}, u32[]{:S(2)}, u32[]{:S(2)}) async-start(bf16[16,144,128]{2,1,0:T(8,128)(2,1)} %copy-done.23), calls=%async_computation.6 | async-start | bytes 1179648 | tf_op jit(solution)/shard_map/all_to_all | solution.py:347
  78.6 2.2 copy-start.2
  80.8 0.7 copy-start.29
  86.8 0.8 copy-start.24
  87.6 0.7 copy-start.26
  88.2 0.6 copy-start.34
  94.2 0.8 copy-start.13
  95.0 20.0 %all-to-all-start.2 = ((bf16[16,144,128]{2,1,0:T(8,128)(2,1)}), bf16[16,144,128]{2,1,0:T(8,128)(2,1)S(1)}, u32[]{:S(2)}, u32[]{:S(2)}) async-start(bf16[16,144,128]{2,1,0:T(8,128)(2,1)} %copy-done.24), calls=%async_computation.2 | async-start | bytes 1179648 | tf_op jit(solution)/shard_map/all_to_all | solution.py:347
  99.4 2.2 copy-start.3
  101.6 1.1 copy-start.14
  102.7 0.7 copy-start.32
  103.4 16.1 %copy-start.35 = (f32[32,128]{1,0:T(8,128)S(1)}, f32[32,128]{1,0:T(8,128)}, u32[]{:S(2)}) copy-start(f32[32,128]{1,0:T(8,128)} %copy-done.34) | copy-start | bytes 49156
  115.0 4.5 %copy-start.11 = (bf16[16,144,128]{2,1,0:T(8,128)(2,1)}, bf16[16,144,128]{2,1,0:T(8,128)(2,1)S(1)}, u32[]{:S(2)}) copy-start(bf16[16,144,128]{2,1,0:T(8,128)(2,1)S(1)} %all-to-all-done.2.refs_1_) | copy-start | bytes 1769476
  115.0 20.1 %all-to-all-start.7 = ((bf16[16,144,128]{2,1,0:T(8,128)(2,1)}), bf16[16,144,128]{2,1,0:T(8,128)(2,1)}, u32[]{:S(2)}, u32[]{:S(2)}) async-start(bf16[16,144,128]{2,1,0:T(8,128)(2,1)} %get-tuple-element.50), calls=%async_computation.7 | async-start | bytes 1179648 | tf_op jit(solution)/shard_map/all_to_all | solution.py:347
  119.4 1.1 copy-start.12
  122.4 0.8 copy-start.22
  123.2 36.4 %copy-start.27 = (f32[32,1024]{1,0:T(8,128)S(1)}, f32[32,1024]{1,0:T(8,128)}, u32[]{:S(2)}) copy-start(f32[32,1024]{1,0:T(8,128)} %copy-done.26) | copy-start | bytes 393220
  135.0 20.1 %all-to-all-start.3 = ((bf16[16,144,128]{2,1,0:T(8,128)(2,1)}), bf16[16,144,128]{2,1,0:T(8,128)(2,1)}, u32[]{:S(2)}, u32[]{:S(2)}) async-start(bf16[16,144,128]{2,1,0:T(8,128)(2,1)} %copy-done.22), calls=%async_computation.3 | async-start | bytes 1179648 | tf_op jit(solution)/shard_map/all_to_all | solution.py:347
  141.8 1.0 copy-start.6
  142.8 0.8 copy-start.21
  155.1 20.1 %all-to-all-start.8 = ((bf16[16,144,128]{2,1,0:T(8,128)(2,1)}), bf16[16,144,128]{2,1,0:T(8,128)(2,1)}, u32[]{:S(2)}, u32[]{:S(2)}) async-start(bf16[16,144,128]{2,1,0:T(8,128)(2,1)} %copy-done.21), calls=%async_computation.8 | async-start | bytes 1179648 | tf_op jit(solution)/shard_map/all_to_all | solution.py:347
  159.6 2.2 copy-start.4
  168.1 0.8 copy-start.19
  175.2 20.1 %all-to-all-start.4 = ((bf16[16,144,128]{2,1,0:T(8,128)(2,1)}), bf16[16,144,128]{2,1,0:T(8,128)(2,1)}, u32[]{:S(2)}, u32[]{:S(2)}) async-start(bf16[16,144,128]{2,1,0:T(8,128)(2,1)} %copy-done.19), calls=%async_computation.4 | async-start | bytes 1179648 | tf_op jit(solution)/shard_map/all_to_all | solution.py:347
  179.7 2.2 copy-start.5
  188.2 0.8 copy-start.20
  195.3 20.1 %all-to-all-start.9 = ((bf16[16,144,128]{2,1,0:T(8,128)(2,1)}), bf16[16,144,128]{2,1,0:T(8,128)(2,1)}, u32[]{:S(2)}, u32[]{:S(2)}) async-start(bf16[16,144,128]{2,1,0:T(8,128)(2,1)} %copy-done.20), calls=%async_computation.9 | async-start | bytes 1179648 | tf_op jit(solution)/shard_map/all_to_all | solution.py:347
  199.8 25.6 %copy-start.30 = (f32[32,128]{1,0:T(8,128)S(1)}, f32[32,128]{1,0:T(8,128)}, u32[]{:S(2)}) copy-start(f32[32,128]{1,0:T(8,128)} %copy-done.28) | copy-start | bytes 49156
  199.8 25.6 %copy-start.33 = (f32[32,128]{1,0:T(8,128)S(1)}, f32[32,128]{1,0:T(8,128)}, u32[]{:S(2)}) copy-start(f32[32,128]{1,0:T(8,128)} %copy-done.31) | copy-start | bytes 49156
  201.9 1.0 copy-start.15
  202.9 0.6 copy-start.36
  215.4 1.2 copy-start.7
  218.7 1.0 copy-start.17
  219.7 0.7 copy-start.25
  220.4 0.6 copy-start.38
  221.0 14.5 %all-to-all-start.10 = ((f32[16,32,128]{2,1,0:T(8,128)}), f32[16,32,128]{2,1,0:T(8,128)S(1)}, u32[]{:S(2)}, u32[]{:S(2)}) async-start(f32[16,32,128]{2,1,0:T(8,128)} %copy-done.25), calls=%async_computation.10 | async-start | bytes 524288 | tf_op jit(solution)/shard_map/all_to_all | solution.py:347
  225.4 1.2 copy-start.8
  226.6 0.7 copy-start.37
  227.4 0.7 copy-start.39
  235.4 1.2 copy-start.16
  236.7 1.2 copy-start.18

commit v3 on v2

--- a/solution.py
+++ b/solution.py
@@ -12,7 +12,7 @@
 BS = 128
 TAIL = 16
 ITERS = 2
-PARTS = 2
+PARTS = 1
 EPS = 1e-12
 F32 = jnp.float32
 BF16 = jnp.bfloat16
@@ -38,9 +38,8 @@
     )
 
 
-def norm_of_tails(message_ref, cols):
-    tails = message_ref[:, BCAP * cols :, :].astype(F32)
-    summed = jnp.sum(tails, axis=0)
+def norm_of_tails(message_refs, cols):
+    summed = sum(message_ref[BCAP * cols :, :].astype(F32) for message_ref in message_refs)
     row = summed[0:1] + summed[1:2] + summed[2:3]
     column = jnp.sum(jnp.where(diagonal(cols), row, 0.0), axis=1, keepdims=True)
     return jnp.broadcast_to(jnp.sqrt(column + EPS), (cols, BS))
@@ -50,11 +49,10 @@
     return pl.ds(pl.multiple_of(block * BS, BS), BS)
 
 
-def transposed(data_ref, rows, rays_ref, target_ref, total_ref, message_ref):
+def transposed(data_ref, rows, rays_ref, target_ref, total_ref, message_refs):
     pair_count, slot_count = rays_ref.shape[:2]
     cols = total_ref.shape[1]
-    peers = message_ref.shape[0]
-    spots = peers * BCAP
+    spots = len(message_refs) * BCAP
 
     def clear(index, carry):
         total_ref[index] = jnp.zeros((cols, BS), F32)
@@ -78,54 +76,45 @@
 
     lax.fori_loop(0, pair_count, one_pair, 0)
 
-    def pack(peer, carry):
+    for peer, message_ref in enumerate(message_refs):
         for rank in range(BCAP):
-            message_ref[peer, rank * cols : (rank + 1) * cols, :] = total_ref[
+            message_ref[rank * cols : (rank + 1) * cols, :] = total_ref[
                 peer * BCAP + rank
             ].astype(BF16)
-        return carry
-
-    lax.fori_loop(0, peers, pack, 0, unroll=2)
-
-
-def start_kernel(part, *refs):
+
+
+def start_kernel(part, peers, *refs):
     if part == 0:
-        cells_ref, counts_ref, times_ref, rays_ref, message_ref, target_ref = refs[:6]
-        total_ref, table_ref, used_ref = refs[6:]
+        me_ref, cells_ref, counts_ref, times_ref, rays_ref = refs[:5]
+        message_refs = refs[5 : 5 + peers]
+        target_ref, total_ref, table_ref, used_ref = refs[5 + peers :]
     else:
-        target_ref, times_ref, rays_ref, message_ref, total_ref = refs
+        target_ref, times_ref, rays_ref = refs[:3]
+        message_refs = refs[3 : 3 + peers]
+        total_ref = refs[-1]
     pair_count, slot_count = rays_ref.shape[:2]
-    peers = message_ref.shape[0]
     cols = total_ref.shape[1]
     columns = slice(part * cols, (part + 1) * cols)
     if part == 0:
-        find_places(cells_ref, counts_ref, target_ref, table_ref, used_ref)
-    transposed(times_ref, columns, rays_ref, target_ref, total_ref, message_ref)
+        find_places(me_ref, cells_ref, counts_ref, target_ref, table_ref, used_ref)
+    transposed(times_ref, columns, rays_ref, target_ref, total_ref, message_refs)
     squares = jnp.zeros((cols, BS), F32)
     for pair in range(pair_count):
         values = times_ref[columns, pair * BS : (pair + 1) * BS]
         squares += values * values
     tail = squares_tail(squares)
-    if part != 0:
-        message_ref[:, BCAP * cols :, :] = jnp.broadcast_to(
-            tail.astype(BF16)[None], (peers, TAIL, BS)
-        )
-        return
     place = lax.broadcasted_iota(jnp.int32, (TAIL, BS), 0)
     lane = lax.broadcasted_iota(jnp.int32, (TAIL, BS), 1)
-
-    def ask(peer, carry):
+    for peer, message_ref in enumerate(message_refs):
         rows = tail
-        for rank in range(BCAP):
-            asked = table_ref[peer * BCAP + rank].astype(F32)
-            rows = jnp.where((place == 3) & (lane == rank), asked, rows)
-        message_ref[peer, BCAP * cols :, :] = rows.astype(BF16)
-        return carry
-
-    lax.fori_loop(0, peers, ask, 0)
-
-
-def find_places(cells_ref, counts_ref, target_ref, table_ref, used_ref):
+        if part == 0:
+            for rank in range(BCAP):
+                asked = table_ref[peer * BCAP + rank].astype(F32)
+                rows = jnp.where((place == 3) & (lane == rank), asked, rows)
+        message_ref[BCAP * cols :, :] = rows.astype(BF16)
+
+
+def find_places(me_ref, cells_ref, counts_ref, target_ref, table_ref, used_ref):
     pair_count, slot_count = cells_ref.shape
     peers = used_ref.shape[0]
     owned = CELL_DEV // BS
@@ -142,7 +131,7 @@
         count = counts_ref[pair]
         for slot in range(slot_count):
             cell = cells_ref[pair, slot]
-            owner = cell // owned
+            owner = (cell // owned) ^ me_ref[0]
             local = cell % owned
             used = used_ref[owner]
             rank = used
@@ -158,15 +147,17 @@
     lax.fori_loop(0, pair_count, one_pair, 0)
 
 
-def pair_kernel(
-    rows, target_ref, fetched_ref, data_ref, beta_ref, rays_ref,
-    message_ref, raw_ref, alpha_ref, total_ref,
-):
+def pair_kernel(rows, peers, target_ref, *refs):
+    fetched_refs = refs[:peers]
+    data_ref, beta_ref, rays_ref = refs[peers : peers + 3]
+    message_refs = refs[peers + 3 : 2 * peers + 3]
+    raw_ref, alpha_ref, total_ref, fetched_ref = refs[2 * peers + 3 :]
     pair_count, slot_count = rays_ref.shape[:2]
-    peers = message_ref.shape[0]
     cols = raw_ref.shape[0]
     spots = peers * BCAP
-    alpha = norm_of_tails(fetched_ref, cols)
+    for peer in range(peers):
+        fetched_ref[peer] = fetched_refs[peer][: BCAP * cols, :]
+    alpha = norm_of_tails(fetched_refs, cols)
     alpha_ref[...] = alpha
     model_scale = 1.0 / alpha
     data_scale = alpha / beta_ref[...]
@@ -190,38 +181,43 @@
         return squares + raw * raw
 
     squares = lax.fori_loop(0, pair_count, one_pair, jnp.zeros((cols, BS), F32))
-    transposed(raw_ref, slice(0, cols), rays_ref, target_ref, total_ref, message_ref)
+    transposed(raw_ref, slice(0, cols), rays_ref, target_ref, total_ref, message_refs)
     tail = squares_tail(squares).astype(BF16)
-    message_ref[:, BCAP * cols :, :] = jnp.broadcast_to(tail[None], (peers, TAIL, BS))
-
-
-def cell_kernel(first, last, *refs):
-    finds = first and len(refs) == 7
-    if finds:
-        arrived_ref, raw_ref, beta_ref, out_ref, asked_ref, table_ref, sem = refs
-    elif first:
-        asked_ref, arrived_ref, raw_ref, beta_ref, out_ref = refs
+    for message_ref in message_refs:
+        message_ref[BCAP * cols :, :] = tail
+
+
+def cell_kernel(first, last, peers, *refs):
+    finds = first and refs[0].dtype == BF16
+    if not finds:
+        asked_ref, *refs = refs
+    arrived_refs, refs = refs[:peers], refs[peers:]
+    if not first:
+        model_ref, alpha_ref, *refs = refs
+    if last:
+        *others, raw_ref, beta_ref, out_ref = refs
     else:
-        asked_ref, arrived_ref, model_ref, alpha_ref, *others, raw_ref, beta_ref, out_ref = refs
-    peers = arrived_ref.shape[0]
+        raw_ref, beta_ref, *refs = refs
+        out_refs = refs[:peers]
     cols, cells = raw_ref.shape
     if finds:
-        table_ref[...] = arrived_ref[:, BCAP * cols :, :].astype(F32)[:, 3, :].astype(jnp.int32)
+        asked_ref, table_ref, sem = refs[peers:]
+        for peer in range(peers):
+            table_ref[peer : peer + 1, :] = (
+                arrived_refs[peer][BCAP * cols :, :].astype(F32)[3:4].astype(jnp.int32)
+            )
         copy = pltpu.make_async_copy(table_ref, asked_ref, sem)
         copy.start()
-    beta = norm_of_tails(arrived_ref, cols)
+    beta = norm_of_tails(arrived_refs, cols)
     beta_ref[...] = beta
     raw_ref[...] = jnp.zeros((cols, cells), F32)
     if finds:
         copy.wait()
-
-    def add(peer, carry):
+    for peer in range(peers):
         for rank in range(BCAP):
             where = lanes(asked_ref[peer, rank])
-            raw_ref[:, where] += arrived_ref[peer, rank * cols : (rank + 1) * cols, :].astype(F32)
-        return carry
-
-    lax.fori_loop(0, peers, add, 0, unroll=2)
+            block = arrived_refs[peer][rank * cols : (rank + 1) * cols, :]
+            raw_ref[:, where] += block.astype(F32)
     scale = 1.0 / beta
     if not first:
         model_scale = beta / alpha_ref[...]
@@ -239,15 +235,11 @@
         tails = jnp.concatenate([other[...] for other in others] + [tail], axis=0)
         out_ref[...] = jnp.broadcast_to(tails, out_ref.shape)
         return
-    out_ref[:, BCAP * cols :, :] = jnp.broadcast_to(tail[None], (peers, TAIL, BS)).astype(BF16)
-
-    def reply(peer, carry):
+    for peer, out_ref in enumerate(out_refs):
+        out_ref[BCAP * cols :, :] = tail.astype(BF16)
         for rank in range(BCAP):
             block = raw_ref[:, lanes(asked_ref[peer, rank])]
-            out_ref[peer, rank * cols : (rank + 1) * cols, :] = block.astype(BF16)
-        return carry
-
-    lax.fori_loop(0, peers, reply, 0, unroll=2)
+            out_ref[rank * cols : (rank + 1) * cols, :] = block.astype(BF16)
 
 
 def estimate_kernel(*refs):
@@ -326,6 +318,14 @@
     )
 
 
+def exchange(values):
+    peers = len(values)
+    return [values[0]] + [
+        lax.ppermute(values[step], "pair", [(i, i ^ step) for i in range(peers)])
+        for step in range(1, peers)
+    ]
+
+
 def on_device(ray_blocks, block_cells, block_counts, travel_times):
     pair_count, slot_count = ray_blocks.shape[:2]
     slots = pair_count * slot_count
@@ -335,44 +335,44 @@
     pairs = times.shape[1]
     cols = times.shape[0] // PARTS
     parts = range(PARTS)
-    message = ((peers, BCAP * cols + TAIL, BS), BF16, VMEM)
+    messages = [((BCAP * cols + TAIL, BS), BF16, VMEM)] * peers
+    ins = [VMEM] * peers
     tile = ((cols, BS), F32, VMEM)
     data = ((cols, pairs), F32, VMEM)
     model = ((cols, CELL_DEV), F32, VMEM)
     whole = ((times.shape[0], CELL_DEV), F32, VMEM)
     totals = VMEM((spots + 1, cols, BS), F32)
+    gathered = VMEM((peers, BCAP * cols, BS), BF16)
     flops = 4 * slots * BS * BS * cols
-
-    def exchange(values):
-        return lax.all_to_all(values, "pair", split_axis=0, concat_axis=0, tiled=True)
+    me = lax.axis_index("pair").astype(jnp.int32).reshape(1)
 
     arrived, fetched = [None] * PARTS, [None] * PARTS
     models, betas, alphas = ([[] for _ in parts] for _ in range(3))
     for part in parts:
+        kernel = functools.partial(start_kernel, part, peers)
         if part == 0:
-            outgoing, target = call(
-                functools.partial(start_kernel, part), "start", [SMEM, SMEM, VMEM, VMEM],
-                [message, ((slots,), jnp.int32, SMEM)],
+            *outgoing, target = call(
+                kernel, "start", [SMEM, SMEM, SMEM, VMEM, VMEM],
+                messages + [((slots,), jnp.int32, SMEM)],
                 [totals, SMEM((spots,), jnp.int32), SMEM((peers,), jnp.int32)], flops, 6 << 20,
-            )(block_cells, block_counts, times, ray_blocks)
+            )(me, block_cells, block_counts, times, ray_blocks)
         else:
-            (outgoing,) = call(
-                functools.partial(start_kernel, part), "start_more", [SMEM, VMEM, VMEM],
-                [message], [totals], flops, 6 << 20,
+            outgoing = call(
+                kernel, "start_more", [SMEM, VMEM, VMEM], messages, [totals], flops, 6 << 20,
             )(target, times, ray_blocks)
         arrived[part] = exchange(outgoing)
     for part in parts:
+        kernel = functools.partial(cell_kernel, True, False, peers)
         if part == 0:
-            raw, beta, reply, asked = call(
-                functools.partial(cell_kernel, True, False), "cells_first", [VMEM],
-                [model, tile, message, ((peers, BS), jnp.int32, SMEM)],
+            raw, beta, *reply, asked = call(
+                kernel, "cells_first", ins,
+                [model, tile] + messages + [((peers, BS), jnp.int32, SMEM)],
                 [VMEM((peers, BS), jnp.int32), pltpu.SemaphoreType.DMA], 0, 6 << 20,
-            )(arrived[part])
+            )(*arrived[part])
         else:
-            raw, beta, reply = call(
-                functools.partial(cell_kernel, True, False), "cells_more", [SMEM, VMEM],
-                [model, tile, message], (), 0, 6 << 20,
-            )(asked, arrived[part])
+            raw, beta, *reply = call(
+                kernel, "cells_more", [SMEM] + ins, [model, tile] + messages, (), 0, 6 << 20,
+            )(asked, *arrived[part])
         models[part].append(raw)
         betas[part].append(beta)
         fetched[part] = exchange(reply)
@@ -381,30 +381,32 @@
     for step in range(ITERS):
         for part in parts:
             rows = slice(part * cols, (part + 1) * cols) if step == 0 else slice(0, cols)
-            outgoing, current[part], alpha = call(
-                functools.partial(pair_kernel, rows), "pairs", [SMEM, VMEM, VMEM, VMEM, VMEM],
-                [message, data, tile], [totals], 2 * flops, 8 << 20,
-            )(target, fetched[part], current[part], betas[part][-1], ray_blocks)
+            *outgoing, current[part], alpha = call(
+                functools.partial(pair_kernel, rows, peers), "pairs",
+                [SMEM] + ins + [VMEM, VMEM, VMEM],
+                messages + [data, tile], [totals, gathered], 2 * flops, 8 << 20,
+            )(target, *fetched[part], current[part], betas[part][-1], ray_blocks)
             alphas[part].append(alpha)
             arrived[part] = exchange(outgoing)
         last = step + 1 == ITERS
         for part in parts:
-            out, others = message, []
+            out, others = messages, []
             if last and part + 1 < PARTS:
-                out = ((TAIL, BS), F32, VMEM)
+                out = [((TAIL, BS), F32, VMEM)]
             elif last:
-                out, others = ((peers, PARTS * TAIL, BS), F32, VMEM), tails
-            raw, beta, reply = call(
-                functools.partial(cell_kernel, False, last), "cells_last" if last else "cells",
-                [SMEM] + [VMEM] * (3 + len(others)), [model, tile, out], (), 0, 8 << 20,
-            )(asked, arrived[part], models[part][-1], alphas[part][-1], *others)
+                out, others = [((peers, PARTS * TAIL, BS), F32, VMEM)], tails
+            raw, beta, *reply = call(
+                functools.partial(cell_kernel, False, last, peers),
+                "cells_last" if last else "cells",
+                [SMEM] + ins + [VMEM] * (2 + len(others)), [model, tile] + out, (), 0, 8 << 20,
+            )(asked, *arrived[part], models[part][-1], alphas[part][-1], *others)
             betas[part].append(beta)
             models[part].append(raw)
             if not last:
                 fetched[part] = exchange(reply)
             elif part + 1 < PARTS:
-                tails.append(reply)
-    summed = exchange(reply)
+                tails.append(reply[0])
+    summed = lax.all_to_all(reply[0], "pair", split_axis=0, concat_axis=0, tiled=True)
     given = [
         ref for part in parts for ref in betas[part] + alphas[part] + models[part][:ITERS]
     ]

time: 242 us -> 220 us (0.909)
  starting transfers between devices: 51.9 us -> 128 us
  waiting for transfers between devices: 98.6 us -> 51.9 us
  local copies, waits for them, and re-layouts: 37.7 us -> 8.96 us
  Pallas kernels: 50.7 us -> 30.1 us
    ppermute x0 -> x75, starting transfers between devices: none -> 122 us  [exchange(): lax.ppermute(values[step], 'pair', [(i, i ^ step) for i in range(peers)])]
    all_to_all x11 -> x1, waiting for transfers between devices: 98.6 us -> 4.25 us  [on_device(): lax.all_to_all(reply[0], 'pair', split_axis=0, concat_axis=0, tiled=True)]
    ppermute x0 -> x75, waiting for transfers between devices: none -> 47.7 us  [exchange(): lax.ppermute(values[step], 'pair', [(i, i ^ step) for i in range(peers)])]
    all_to_all x11 -> x1, starting transfers between devices: 51.9 us -> 5.46 us  [on_device(): lax.all_to_all(reply[0], 'pair', split_axis=0, concat_axis=0, tiled=True)]
    unnamed x84 -> x20, local copies, waits for them, and re-layouts: 37.7 us -> 8.96 us
    pallas_call x12 -> x6, Pallas kernels: 46.6 us -> 26.1 us  [the longest x2 12.3 us: on_device(): call(functools.partial(pair_kernel, rows, peers), 'pairs', [SMEM] + ins +...]
  transfers between devices with their start and end apart: 11 -> 76, of which waited for: 11 -> 20; matrix products, arithmetic and copies ran while one was open for 0% -> 0% of each run, Pallas kernels for 17% -> 1%
where the time goes in v3:
time: 220 us; the launch traced here: 219 us
  starting transfers between devices  128 us (58%)
  waiting for transfers between devices  51.9 us (24%)
  Pallas kernels  30.1 us (14%)
  local copies, waits for them, and re-layouts  8.96 us (4%)
    ppermute x75, starting transfers between devices, exchange(): lax.ppermute(values[step], 'pair', [(i, i ^ step) for i in range(peers)])  122 us
    ppermute x75, waiting for transfers between devices, exchange(): lax.ppermute(values[step], 'pair', [(i, i ^ step) for i in range(peers)])  47.7 us
    pallas_call x2, Pallas kernels, on_device(): call(functools.partial(pair_kernel, rows, peers), 'pairs', [SMEM] + ins +...  12.3 us
    unnamed x20, local copies, waits for them, and re-layouts  8.96 us
    pallas_call x1, Pallas kernels, on_device(): call(kernel, 'start', [SMEM, SMEM, SMEM, VMEM, VMEM], messages + [((slots...  6.16 us
    all_to_all x1, starting transfers between devices, on_device(): lax.all_to_all(reply[0], 'pair', split_axis=0, concat_axis=0, tiled=True)  5.46 us
    pallas_call x2, Pallas kernels, on_device(): call(functools.partial(cell_kernel, False, last, peers), 'cells_last' if...  4.94 us
  transfers between devices with their start and end apart: 76, of which 20 were waited for; matrix products, arithmetic and copies ran while one was open for 0% of the time, Pallas kernels for 1%

profile of v3, /device:TPU:0, one launch (start us, length us, event | category | flops | bytes accessed | tf_op | source)
XLA Modules:
  0.0 219.4 jit_solution(15972804333261595471)
XLA Ops:
  0.6 2.2 copy-done
  5.1 6.2 %start.1 = (bf16[272,128]{1,0:T(8,128)(2,1)S(1)}, bf16[272,128]{1,0:T(8,128)(2,1)S(1)}, bf16[272,128]{1,0:T(8,128)(2,1)S(1)}, bf16[272,128]{1,0:T(8,128)(2,1)S(1...) custom-call(s32[1]{0:T(128)} %bitcast.refs_0_, ...), custom_call_target="tpu_custom_call" | custom-call | flops 536870912 | bytes 6291456 | tf_op jit(solution)/shard_map/start/pallas_call | solution.py:354
  11.8 2.6 %collective-permute-start.1 = (bf16[272,128]{1,0:T(8,128)(2,1)S(1)}, bf16[272,128]{1,0:T(8,128)(2,1)S(1)}, u32[]{:S(2)}, u32[]{:S(2)}) collective-permute-start(bf16[272,128]{1,0:T(8,128)(2,1)S(1)} %get-tuple-element.96), channel_id=1, source_target_pairs={{0,2},{1,3},{2,0},{3,1},{4,6},{5,7},{6,4},{7,5},{8,10},{9,11},{10,... | collective-permute-start | bytes 208904 | tf_op jit(solution)/shard_map/ppermute | solution.py:324
  14.5 1.8 collective-permute-start.3
  16.3 2.6 %collective-permute-start.5 = (bf16[272,128]{1,0:T(8,128)(2,1)S(1)}, bf16[272,128]{1,0:T(8,128)(2,1)S(1)}, u32[]{:S(2)}, u32[]{:S(2)}) collective-permute-start(bf16[272,128]{1,0:T(8,128)(2,1)S(1)} %get-tuple-element.100), channel_id=1, source_target_pairs={{0,6},{1,7},{2,4},{3,5},{4,2},{5,3},{6,0},{7,1},{8,14},{9,15},{10,... | collective-permute-start | bytes 208904 | tf_op jit(solution)/shard_map/ppermute | solution.py:324
  19.2 2.6 %collective-permute-start.7 = (bf16[272,128]{1,0:T(8,128)(2,1)S(1)}, bf16[272,128]{1,0:T(8,128)(2,1)S(1)}, u32[]{:S(2)}, u32[]{:S(2)}) collective-permute-start(bf16[272,128]{1,0:T(8,128)(2,1)S(1)} %get-tuple-element.102), channel_id=1, source_target_pairs={{0,8},{1,9},{2,10},{3,11},{4,12},{5,13},{6,14},{7,15},{8,0},{9,1},... | collective-permute-start | bytes 208904 | tf_op jit(solution)/shard_map/ppermute | solution.py:324
  22.8 2.4 %collective-permute-start.9 = (bf16[272,128]{1,0:T(8,128)(2,1)S(1)}, bf16[272,128]{1,0:T(8,128)(2,1)S(1)}, u32[]{:S(2)}, u32[]{:S(2)}) collective-permute-start(bf16[272,128]{1,0:T(8,128)(2,1)S(1)} %get-tuple-element.104), channel_id=1, source_target_pairs={{0,10},{1,11},{2,8},{3,9},{4,14},{5,15},{6,12},{7,13},{8,2},{9,3},... | collective-permute-start | bytes 208904 | tf_op jit(solution)/shard_map/ppermute | solution.py:324
  26.1 2.8 %collective-permute-start.11 = (bf16[272,128]{1,0:T(8,128)(2,1)S(1)}, bf16[272,128]{1,0:T(8,128)(2,1)S(1)}, u32[]{:S(2)}, u32[]{:S(2)}) collective-permute-start(bf16[272,128]{1,0:T(8,128)(2,1)S(1)} %get-tuple-element.106), channel_id=1, source_target_pairs={{0,12},{1,13},{2,14},{3,15},{4,8},{5,9},{6,10},{7,11},{8,4},{9,5},... | collective-permute-start | bytes 208904 | tf_op jit(solution)/shard_map/ppermute | solution.py:324
  28.9 4.2 %collective-permute-start.12 = (bf16[272,128]{1,0:T(8,128)(2,1)S(1)}, bf16[272,128]{1,0:T(8,128)(2,1)S(1)}, u32[]{:S(2)}, u32[]{:S(2)}) collective-permute-start(bf16[272,128]{1,0:T(8,128)(2,1)S(1)} %get-tuple-element.107), channel_id=1, source_target_pairs={{0,13},{1,12},{2,15},{3,14},{4,9},{5,8},{6,11},{7,10},{8,5},{9,4},... | collective-permute-start | bytes 208904 | tf_op jit(solution)/shard_map/ppermute | solution.py:324
  34.3 3.3 %collective-permute-start.13 = (bf16[272,128]{1,0:T(8,128)(2,1)S(1)}, bf16[272,128]{1,0:T(8,128)(2,1)S(1)}, u32[]{:S(2)}, u32[]{:S(2)}) collective-permute-start(bf16[272,128]{1,0:T(8,128)(2,1)S(1)} %get-tuple-element.108), channel_id=1, source_target_pairs={{0,14},{1,15},{2,12},{3,13},{4,10},{5,11},{6,8},{7,9},{8,6},{9,7},... | collective-permute-start | bytes 208904 | tf_op jit(solution)/shard_map/ppermute | solution.py:324
  37.8 2.4 %collective-permute-start.14 = (bf16[272,128]{1,0:T(8,128)(2,1)S(1)}, bf16[272,128]{1,0:T(8,128)(2,1)S(1)}, u32[]{:S(2)}, u32[]{:S(2)}) collective-permute-start(bf16[272,128]{1,0:T(8,128)(2,1)S(1)} %get-tuple-element.109), channel_id=1, source_target_pairs={{0,15},{1,14},{2,13},{3,12},{4,11},{5,10},{6,9},{7,8},{8,7},{9,6},... | collective-permute-start | bytes 208904 | tf_op jit(solution)/shard_map/ppermute | solution.py:324
  41.4 3.5 %collective-permute-done.14.refs_15_ = bf16[272,128]{1,0:T(8,128)(2,1)S(1)} collective-permute-done((bf16[272,128]{1,0:T(8,128)(2,1)S(1)}, bf16[272,128]{1,0:T(8,128)(2,1)S(1)}, u32[]{:S(2)}, u32[]{:S(2)}) %collective-permute-start.14) | collective-permute-done | bytes 69664 | tf_op jit(solution)/shard_map/ppermute | solution.py:324
  45.0 2.7 %cells_first.1 = (f32[64,8192]{1,0:T(8,128)S(1)}, f32[64,128]{1,0:T(8,128)S(1)}, bf16[272,128]{1,0:T(8,128)(2,1)S(1)}, bf16[272,128]{1,0:T(8,128)(2,1)S(1)}, bf1...) custom-call(bf16[272,128]{1,0:T(8,128)(2,1)S(1)} %get-tuple-element., ...), custom_call_target="tpu_custom_call" | custom-call | bytes 6291456 | tf_op jit(solution)/shard_map/cells_first/pallas_call | solution.py:367
  49.6 4.3 %collective-permute-start.18 = (bf16[272,128]{1,0:T(8,128)(2,1)S(1)}, bf16[272,128]{1,0:T(8,128)(2,1)S(1)}, u32[]{:S(2)}, u32[]{:S(2)}) collective-permute-start(bf16[272,128]{1,0:T(8,128)(2,1)S(1)} %get-tuple-element.117), channel_id=1, source_target_pairs={{0,4},{1,5},{2,6},{3,7},{4,0},{5,1},{6,2},{7,3},{8,12},{9,13},{10,... | collective-permute-start | bytes 208904 | tf_op jit(solution)/shard_map/ppermute | solution.py:324
  54.0 1.6 collective-permute-start.20
  56.4 2.8 %collective-permute-start.22 = (bf16[272,128]{1,0:T(8,128)(2,1)S(1)}, bf16[272,128]{1,0:T(8,128)(2,1)S(1)}, u32[]{:S(2)}, u32[]{:S(2)}) collective-permute-start(bf16[272,128]{1,0:T(8,128)(2,1)S(1)} %get-tuple-element.121), channel_id=1, source_target_pairs={{0,8},{1,9},{2,10},{3,11},{4,12},{5,13},{6,14},{7,15},{8,0},{9,1},... | collective-permute-start | bytes 208904 | tf_op jit(solution)/shard_map/ppermute | solution.py:324
  59.3 2.5 %collective-permute-start.24 = (bf16[272,128]{1,0:T(8,128)(2,1)S(1)}, bf16[272,128]{1,0:T(8,128)(2,1)S(1)}, u32[]{:S(2)}, u32[]{:S(2)}) collective-permute-start(bf16[272,128]{1,0:T(8,128)(2,1)S(1)} %get-tuple-element.123), channel_id=1, source_target_pairs={{0,10},{1,11},{2,8},{3,9},{4,14},{5,15},{6,12},{7,13},{8,2},{9,3},... | collective-permute-start | bytes 208904 | tf_op jit(solution)/shard_map/ppermute | solution.py:324
  63.0 1.9 collective-permute-start.26
  64.9 2.0 collective-permute-start.27
  66.9 6.3 %collective-permute-done.23.refs_9_ = bf16[272,128]{1,0:T(8,128)(2,1)S(1)} collective-permute-done((bf16[272,128]{1,0:T(8,128)(2,1)S(1)}, bf16[272,128]{1,0:T(8,128)(2,1)S(1)}, u32[]{:S(2)}, u32[]{:S(2)}) %collective-permute-start.23) | collective-permute-done | bytes 69664 | tf_op jit(solution)/shard_map/ppermute | solution.py:324
  73.2 1.9 collective-permute-start.28
  75.1 2.7 %collective-permute-start.29 = (bf16[272,128]{1,0:T(8,128)(2,1)S(1)}, bf16[272,128]{1,0:T(8,128)(2,1)S(1)}, u32[]{:S(2)}, u32[]{:S(2)}) collective-permute-start(bf16[272,128]{1,0:T(8,128)(2,1)S(1)} %get-tuple-element.128), channel_id=1, source_target_pairs={{0,15},{1,14},{2,13},{3,12},{4,11},{5,10},{6,9},{7,8},{8,7},{9,6},... | collective-permute-start | bytes 208904 | tf_op jit(solution)/shard_map/ppermute | solution.py:324
  77.7 2.8 %collective-permute-done.28.refs_14_ = bf16[272,128]{1,0:T(8,128)(2,1)S(1)} collective-permute-done((bf16[272,128]{1,0:T(8,128)(2,1)S(1)}, bf16[272,128]{1,0:T(8,128)(2,1)S(1)}, u32[]{:S(2)}, u32[]{:S(2)}) %collective-permute-start.28) | collective-permute-done | bytes 69664 | tf_op jit(solution)/shard_map/ppermute | solution.py:324
  82.0 5.9 %pairs.2 = (bf16[272,128]{1,0:T(8,128)(2,1)S(1)}, bf16[272,128]{1,0:T(8,128)(2,1)S(1)}, bf16[272,128]{1,0:T(8,128)(2,1)S(1)}, bf16[272,128]{1,0:T(8,128)(2,1)S(1...) custom-call(s32[128]{0:T(128)S(1)} %get-tuple-element.112.target_ref, ...), custom_call_target="tpu_custom_call" | custom-call | flops 1073741824 | bytes 8388608 | tf_op jit(solution)/shard_map/pairs/pallas_call | solution.py:384
  88.0 1.8 collective-permute-start.31
  89.9 3.5 %collective-permute-start.33 = (bf16[272,128]{1,0:T(8,128)(2,1)S(1)}, bf16[272,128]{1,0:T(8,128)(2,1)S(1)}, u32[]{:S(2)}, u32[]{:S(2)}) collective-permute-start(bf16[272,128]{1,0:T(8,128)(2,1)S(1)} %get-tuple-element.133), channel_id=1, source_target_pairs={{0,4},{1,5},{2,6},{3,7},{4,0},{5,1},{6,2},{7,3},{8,12},{9,13},{10,... | collective-permute-start | bytes 208904 | tf_op jit(solution)/shard_map/ppermute | solution.py:324
  93.4 2.8 %collective-permute-start.35 = (bf16[272,128]{1,0:T(8,128)(2,1)S(1)}, bf16[272,128]{1,0:T(8,128)(2,1)S(1)}, u32[]{:S(2)}, u32[]{:S(2)}) collective-permute-start(bf16[272,128]{1,0:T(8,128)(2,1)S(1)} %get-tuple-element.135), channel_id=1, source_target_pairs={{0,6},{1,7},{2,4},{3,5},{4,2},{5,3},{6,0},{7,1},{8,14},{9,15},{10,... | collective-permute-start | bytes 208904 | tf_op jit(solution)/shard_map/ppermute | solution.py:324
  96.4 2.3 %collective-permute-start.37 = (bf16[272,128]{1,0:T(8,128)(2,1)S(1)}, bf16[272,128]{1,0:T(8,128)(2,1)S(1)}, u32[]{:S(2)}, u32[]{:S(2)}) collective-permute-start(bf16[272,128]{1,0:T(8,128)(2,1)S(1)} %get-tuple-element.137), channel_id=1, source_target_pairs={{0,8},{1,9},{2,10},{3,11},{4,12},{5,13},{6,14},{7,15},{8,0},{9,1},... | collective-permute-start | bytes 208904 | tf_op jit(solution)/shard_map/ppermute | solution.py:324
  100.0 1.6 collective-permute-start.39
  104.4 6.8 %collective-permute-start.42 = (bf16[272,128]{1,0:T(8,128)(2,1)S(1)}, bf16[272,128]{1,0:T(8,128)(2,1)S(1)}, u32[]{:S(2)}, u32[]{:S(2)}) collective-permute-start(bf16[272,128]{1,0:T(8,128)(2,1)S(1)} %get-tuple-element.142), channel_id=1, source_target_pairs={{0,13},{1,12},{2,15},{3,14},{4,9},{5,8},{6,11},{7,10},{8,5},{9,4},... | collective-permute-start | bytes 208904 | tf_op jit(solution)/shard_map/ppermute | solution.py:324
  111.9 3.2 %collective-permute-start.43 = (bf16[272,128]{1,0:T(8,128)(2,1)S(1)}, bf16[272,128]{1,0:T(8,128)(2,1)S(1)}, u32[]{:S(2)}, u32[]{:S(2)}) collective-permute-start(bf16[272,128]{1,0:T(8,128)(2,1)S(1)} %get-tuple-element.143), channel_id=1, source_target_pairs={{0,14},{1,15},{2,12},{3,13},{4,10},{5,11},{6,8},{7,9},{8,6},{9,7},... | collective-permute-start | bytes 208904 | tf_op jit(solution)/shard_map/ppermute | solution.py:324
  116.1 2.9 %collective-permute-done.43.refs_15_ = bf16[272,128]{1,0:T(8,128)(2,1)S(1)} collective-permute-done((bf16[272,128]{1,0:T(8,128)(2,1)S(1)}, bf16[272,128]{1,0:T(8,128)(2,1)S(1)}, u32[]{:S(2)}, u32[]{:S(2)}) %collective-permute-start.43) | collective-permute-done | bytes 69664 | tf_op jit(solution)/shard_map/ppermute | solution.py:324
  119.0 3.2 %collective-permute-done.44.refs_16_ = bf16[272,128]{1,0:T(8,128)(2,1)S(1)} collective-permute-done((bf16[272,128]{1,0:T(8,128)(2,1)S(1)}, bf16[272,128]{1,0:T(8,128)(2,1)S(1)}, u32[]{:S(2)}, u32[]{:S(2)}) %collective-permute-start.44) | collective-permute-done | bytes 69664 | tf_op jit(solution)/shard_map/ppermute | solution.py:324
  122.2 2.3 %cells.1 = (f32[64,8192]{1,0:T(8,128)S(1)}, f32[64,128]{1,0:T(8,128)S(1)}, bf16[272,128]{1,0:T(8,128)(2,1)S(1)}, bf16[272,128]{1,0:T(8,128)(2,1)S(1)}, bf16[272,...) custom-call(s32[16,128]{1,0:T(8,128)S(1)} %get-tuple-element.111.ref, ...), custom_call_target="tpu_custom_call" | custom-call | bytes 8388608 | tf_op jit(solution)/shard_map/cells/pallas_call | solution.py:398
  126.4 3.2 %collective-permute-start.48 = (bf16[272,128]{1,0:T(8,128)(2,1)S(1)}, bf16[272,128]{1,0:T(8,128)(2,1)S(1)}, u32[]{:S(2)}, u32[]{:S(2)}) collective-permute-start(bf16[272,128]{1,0:T(8,128)(2,1)S(1)} %get-tuple-element.152), channel_id=1, source_target_pairs={{0,4},{1,5},{2,6},{3,7},{4,0},{5,1},{6,2},{7,3},{8,12},{9,13},{10,... | collective-permute-start | bytes 208904 | tf_op jit(solution)/shard_map/ppermute | solution.py:324
  129.7 2.4 %collective-permute-start.50 = (bf16[272,128]{1,0:T(8,128)(2,1)S(1)}, bf16[272,128]{1,0:T(8,128)(2,1)S(1)}, u32[]{:S(2)}, u32[]{:S(2)}) collective-permute-start(bf16[272,128]{1,0:T(8,128)(2,1)S(1)} %get-tuple-element.154), channel_id=1, source_target_pairs={{0,6},{1,7},{2,4},{3,5},{4,2},{5,3},{6,0},{7,1},{8,14},{9,15},{10,... | collective-permute-start | bytes 208904 | tf_op jit(solution)/shard_map/ppermute | solution.py:324
  132.2 2.6 %collective-permute-start.52 = (bf16[272,128]{1,0:T(8,128)(2,1)S(1)}, bf16[272,128]{1,0:T(8,128)(2,1)S(1)}, u32[]{:S(2)}, u32[]{:S(2)}) collective-permute-start(bf16[272,128]{1,0:T(8,128)(2,1)S(1)} %get-tuple-element.156), channel_id=1, source_target_pairs={{0,8},{1,9},{2,10},{3,11},{4,12},{5,13},{6,14},{7,15},{8,0},{9,1},... | collective-permute-start | bytes 208904 | tf_op jit(solution)/shard_map/ppermute | solution.py:324
  135.9 1.8 collective-permute-start.54
  139.0 2.0 collective-permute-start.56
  141.0 2.1 collective-permute-start.57
  143.0 5.8 %collective-permute-done.53.refs_9_ = bf16[272,128]{1,0:T(8,128)(2,1)S(1)} collective-permute-done((bf16[272,128]{1,0:T(8,128)(2,1)S(1)}, bf16[272,128]{1,0:T(8,128)(2,1)S(1)}, u32[]{:S(2)}, u32[]{:S(2)}) %collective-permute-start.53) | collective-permute-done | bytes 69664 | tf_op jit(solution)/shard_map/ppermute | solution.py:324
  148.8 2.2 %collective-permute-start.58 = (bf16[272,128]{1,0:T(8,128)(2,1)S(1)}, bf16[272,128]{1,0:T(8,128)(2,1)S(1)}, u32[]{:S(2)}, u32[]{:S(2)}) collective-permute-start(bf16[272,128]{1,0:T(8,128)(2,1)S(1)} %get-tuple-element.162), channel_id=1, source_target_pairs={{0,14},{1,15},{2,12},{3,13},{4,10},{5,11},{6,8},{7,9},{8,6},{9,7},... | collective-permute-start | bytes 208904 | tf_op jit(solution)/shard_map/ppermute | solution.py:324
  151.1 2.0 collective-permute-start.59
  153.1 2.8 %collective-permute-done.58.refs_14_ = bf16[272,128]{1,0:T(8,128)(2,1)S(1)} collective-permute-done((bf16[272,128]{1,0:T(8,128)(2,1)S(1)}, bf16[272,128]{1,0:T(8,128)(2,1)S(1)}, u32[]{:S(2)}, u32[]{:S(2)}) %collective-permute-start.58) | collective-permute-done | bytes 69664 | tf_op jit(solution)/shard_map/ppermute | solution.py:324
  155.9 2.4 %collective-permute-done.59.refs_15_ = bf16[272,128]{1,0:T(8,128)(2,1)S(1)} collective-permute-done((bf16[272,128]{1,0:T(8,128)(2,1)S(1)}, bf16[272,128]{1,0:T(8,128)(2,1)S(1)}, u32[]{:S(2)}, u32[]{:S(2)}) %collective-permute-start.59) | collective-permute-done | bytes 69664 | tf_op jit(solution)/shard_map/ppermute | solution.py:324
  158.3 6.4 %pairs.3 = (bf16[272,128]{1,0:T(8,128)(2,1)S(1)}, bf16[272,128]{1,0:T(8,128)(2,1)S(1)}, bf16[272,128]{1,0:T(8,128)(2,1)S(1)}, bf16[272,128]{1,0:T(8,128)(2,1)S(1...) custom-call(s32[128]{0:T(128)S(1)} %get-tuple-element.112.target_ref, ...), custom_call_target="tpu_custom_call" | custom-call | flops 1073741824 | bytes 8388608 | tf_op jit(solution)/shard_map/pairs/pallas_call | solution.py:384
  166.6 3.4 %collective-permute-start.63 = (bf16[272,128]{1,0:T(8,128)(2,1)S(1)}, bf16[272,128]{1,0:T(8,128)(2,1)S(1)}, u32[]{:S(2)}, u32[]{:S(2)}) collective-permute-start(bf16[272,128]{1,0:T(8,128)(2,1)S(1)} %get-tuple-element.169), channel_id=1, source_target_pairs={{0,4},{1,5},{2,6},{3,7},{4,0},{5,1},{6,2},{7,3},{8,12},{9,13},{10,... | collective-permute-start | bytes 208904 | tf_op jit(solution)/shard_map/ppermute | solution.py:324
  170.0 2.3 %collective-permute-start.65 = (bf16[272,128]{1,0:T(8,128)(2,1)S(1)}, bf16[272,128]{1,0:T(8,128)(2,1)S(1)}, u32[]{:S(2)}, u32[]{:S(2)}) collective-permute-start(bf16[272,128]{1,0:T(8,128)(2,1)S(1)} %get-tuple-element.171), channel_id=1, source_target_pairs={{0,6},{1,7},{2,4},{3,5},{4,2},{5,3},{6,0},{7,1},{8,14},{9,15},{10,... | collective-permute-start | bytes 208904 | tf_op jit(solution)/shard_map/ppermute | solution.py:324
  172.5 2.3 %collective-permute-start.67 = (bf16[272,128]{1,0:T(8,128)(2,1)S(1)}, bf16[272,128]{1,0:T(8,128)(2,1)S(1)}, u32[]{:S(2)}, u32[]{:S(2)}) collective-permute-start(bf16[272,128]{1,0:T(8,128)(2,1)S(1)} %get-tuple-element.173), channel_id=1, source_target_pairs={{0,8},{1,9},{2,10},{3,11},{4,12},{5,13},{6,14},{7,15},{8,0},{9,1},... | collective-permute-start | bytes 208904 | tf_op jit(solution)/shard_map/ppermute | solution.py:324
  176.1 1.9 collective-permute-start.69
  179.3 1.8 collective-permute-start.71
  181.1 2.1 collective-permute-start.72
  183.2 5.6 %collective-permute-done.68.refs_10_ = bf16[272,128]{1,0:T(8,128)(2,1)S(1)} collective-permute-done((bf16[272,128]{1,0:T(8,128)(2,1)S(1)}, bf16[272,128]{1,0:T(8,128)(2,1)S(1)}, u32[]{:S(2)}, u32[]{:S(2)}) %collective-permute-start.68) | collective-permute-done | bytes 69664 | tf_op jit(solution)/shard_map/ppermute | solution.py:324
  188.8 2.5 %collective-permute-start.73 = (bf16[272,128]{1,0:T(8,128)(2,1)S(1)}, bf16[272,128]{1,0:T(8,128)(2,1)S(1)}, u32[]{:S(2)}, u32[]{:S(2)}) collective-permute-start(bf16[272,128]{1,0:T(8,128)(2,1)S(1)} %get-tuple-element.179), channel_id=1, source_target_pairs={{0,14},{1,15},{2,12},{3,13},{4,10},{5,11},{6,8},{7,9},{8,6},{9,7},... | collective-permute-start | bytes 208904 | tf_op jit(solution)/shard_map/ppermute | solution.py:324
  191.3 1.7 collective-permute-start.74
  193.0 2.8 %collective-permute-done.73.refs_15_ = bf16[272,128]{1,0:T(8,128)(2,1)S(1)} collective-permute-done((bf16[272,128]{1,0:T(8,128)(2,1)S(1)}, bf16[272,128]{1,0:T(8,128)(2,1)S(1)}, u32[]{:S(2)}, u32[]{:S(2)}) %collective-permute-start.73) | collective-permute-done | bytes 69664 | tf_op jit(solution)/shard_map/ppermute | solution.py:324
  195.9 2.7 %collective-permute-done.74.refs_16_ = bf16[272,128]{1,0:T(8,128)(2,1)S(1)} collective-permute-done((bf16[272,128]{1,0:T(8,128)(2,1)S(1)}, bf16[272,128]{1,0:T(8,128)(2,1)S(1)}, u32[]{:S(2)}, u32[]{:S(2)}) %collective-permute-start.74) | collective-permute-done | bytes 69664 | tf_op jit(solution)/shard_map/ppermute | solution.py:324
  198.5 2.7 %cells_last.1 = (f32[64,8192]{1,0:T(8,128)S(1)}, f32[64,128]{1,0:T(8,128)S(1)}, f32[16,16,128]{2,1,0:T(8,128)}) custom-call(s32[16,128]{1,0:T(8,128)S(1)} %get-tuple-element.111.refs_0_, bf16[272,128]{1,0:T(8,128)(2,1)S(1)} %get-tuple-element.165.refs_1_, bf16[272,128]{1,0:T(8,128)(2,1)S(1)} %collective-permute-done.60.refs_2_, ...), custom_call_target="tpu_custom_call" | custom-call | bytes 8388608 | tf_op jit(solution)/shard_map/cells_last/pallas_call | solution.py:398
  202.5 5.5 %all-to-all-start = ((f32[16,16,128]{2,1,0:T(8,128)}), f32[16,16,128]{2,1,0:T(8,128)S(1)}, u32[]{:S(2)}, u32[]{:S(2)}) async-start(f32[16,16,128]{2,1,0:T(8,128)} %get-tuple-element.184), calls=%async_computation | async-start | bytes 262144 | tf_op jit(solution)/shard_map/all_to_all | solution.py:409
  208.0 1.6 copy-done.3
  209.6 2.1 estimate.1
  211.7 4.3 %all-to-all-done.tails_ref = f32[16,16,128]{2,1,0:T(8,128)S(1)} async-done(((f32[16,16,128]{2,1,0:T(8,128)}), f32[16,16,128]{2,1,0:T(8,128)S(1)}, u32[]{:S(2)}, u32[]{:S(2)}) %all-to-all-start) | async-done | bytes 131104 | tf_op jit(solution)/shard_map/all_to_all | solution.py:409
  215.9 1.6 copy-done.5
  217.5 1.9 model.1
  (116 shorter events, 30.0 us)
Async XLA Ops:
  11.8 7.1 %collective-permute-start.1 = (bf16[272,128]{1,0:T(8,128)(2,1)S(1)}, bf16[272,128]{1,0:T(8,128)(2,1)S(1)}, u32[]{:S(2)}, u32[]{:S(2)}) collective-permute-start(bf16[272,128]{1,0:T(8,128)(2,1)S(1)} %get-tuple-element.96), channel_id=1, source_target_pairs={{0,2},{1,3},{2,0},{3,1},{4,6},{5,7},{6,4},{7,5},{8,10},{9,11},{10,... | collective-permute-start | bytes 208904 | tf_op jit(solution)/shard_map/ppermute | solution.py:324
  14.5 7.3 %collective-permute-start.3 = (bf16[272,128]{1,0:T(8,128)(2,1)S(1)}, bf16[272,128]{1,0:T(8,128)(2,1)S(1)}, u32[]{:S(2)}, u32[]{:S(2)}) collective-permute-start(bf16[272,128]{1,0:T(8,128)(2,1)S(1)} %get-tuple-element.98), channel_id=1, source_target_pairs={{0,4},{1,5},{2,6},{3,7},{4,0},{5,1},{6,2},{7,3},{8,12},{9,13},{10,... | collective-permute-start | bytes 208904 | tf_op jit(solution)/shard_map/ppermute | solution.py:324
  16.3 9.0 %collective-permute-start.5 = (bf16[272,128]{1,0:T(8,128)(2,1)S(1)}, bf16[272,128]{1,0:T(8,128)(2,1)S(1)}, u32[]{:S(2)}, u32[]{:S(2)}) collective-permute-start(bf16[272,128]{1,0:T(8,128)(2,1)S(1)} %get-tuple-element.100), channel_id=1, source_target_pairs={{0,6},{1,7},{2,4},{3,5},{4,2},{5,3},{6,0},{7,1},{8,14},{9,15},{10,... | collective-permute-start | bytes 208904 | tf_op jit(solution)/shard_map/ppermute | solution.py:324
  18.9 7.1 %collective-permute-start.6 = (bf16[272,128]{1,0:T(8,128)(2,1)S(1)}, bf16[272,128]{1,0:T(8,128)(2,1)S(1)}, u32[]{:S(2)}, u32[]{:S(2)}) collective-permute-start(bf16[272,128]{1,0:T(8,128)(2,1)S(1)} %get-tuple-element.101), channel_id=1, source_target_pairs={{0,7},{1,6},{2,5},{3,4},{4,3},{5,2},{6,1},{7,0},{8,15},{9,14},{10,... | collective-permute-start | bytes 208904 | tf_op jit(solution)/shard_map/ppermute | solution.py:324
  19.2 9.7 %collective-permute-start.7 = (bf16[272,128]{1,0:T(8,128)(2,1)S(1)}, bf16[272,128]{1,0:T(8,128)(2,1)S(1)}, u32[]{:S(2)}, u32[]{:S(2)}) collective-permute-start(bf16[272,128]{1,0:T(8,128)(2,1)S(1)} %get-tuple-element.102), channel_id=1, source_target_pairs={{0,8},{1,9},{2,10},{3,11},{4,12},{5,13},{6,14},{7,15},{8,0},{9,1},... | collective-permute-start | bytes 208904 | tf_op jit(solution)/shard_map/ppermute | solution.py:324
  21.8 12.5 %collective-permute-start.8 = (bf16[272,128]{1,0:T(8,128)(2,1)S(1)}, bf16[272,128]{1,0:T(8,128)(2,1)S(1)}, u32[]{:S(2)}, u32[]{:S(2)}) collective-permute-start(bf16[272,128]{1,0:T(8,128)(2,1)S(1)} %get-tuple-element.103), channel_id=1, source_target_pairs={{0,9},{1,8},{2,11},{3,10},{4,13},{5,12},{6,15},{7,14},{8,1},{9,0},... | collective-permute-start | bytes 208904 | tf_op jit(solution)/shard_map/ppermute | solution.py:324
  22.8 15.0 %collective-permute-start.9 = (bf16[272,128]{1,0:T(8,128)(2,1)S(1)}, bf16[272,128]{1,0:T(8,128)(2,1)S(1)}, u32[]{:S(2)}, u32[]{:S(2)}) collective-permute-start(bf16[272,128]{1,0:T(8,128)(2,1)S(1)} %get-tuple-element.104), channel_id=1, source_target_pairs={{0,10},{1,11},{2,8},{3,9},{4,14},{5,15},{6,12},{7,13},{8,2},{9,3},... | collective-permute-start | bytes 208904 | tf_op jit(solution)/shard_map/ppermute | solution.py:324
  25.2 15.0 %collective-permute-start.10 = (bf16[272,128]{1,0:T(8,128)(2,1)S(1)}, bf16[272,128]{1,0:T(8,128)(2,1)S(1)}, u32[]{:S(2)}, u32[]{:S(2)}) collective-permute-start(bf16[272,128]{1,0:T(8,128)(2,1)S(1)} %get-tuple-element.105), channel_id=1, source_target_pairs={{0,11},{1,10},{2,9},{3,8},{4,15},{5,14},{6,13},{7,12},{8,3},{9,2},... | collective-permute-start | bytes 208904 | tf_op jit(solution)/shard_map/ppermute | solution.py:324
  26.1 14.1 %collective-permute-start.11 = (bf16[272,128]{1,0:T(8,128)(2,1)S(1)}, bf16[272,128]{1,0:T(8,128)(2,1)S(1)}, u32[]{:S(2)}, u32[]{:S(2)}) collective-permute-start(bf16[272,128]{1,0:T(8,128)(2,1)S(1)} %get-tuple-element.106), channel_id=1, source_target_pairs={{0,12},{1,13},{2,14},{3,15},{4,8},{5,9},{6,10},{7,11},{8,4},{9,5},... | collective-permute-start | bytes 208904 | tf_op jit(solution)/shard_map/ppermute | solution.py:324
  28.9 11.3 %collective-permute-start.12 = (bf16[272,128]{1,0:T(8,128)(2,1)S(1)}, bf16[272,128]{1,0:T(8,128)(2,1)S(1)}, u32[]{:S(2)}, u32[]{:S(2)}) collective-permute-start(bf16[272,128]{1,0:T(8,128)(2,1)S(1)} %get-tuple-element.107), channel_id=1, source_target_pairs={{0,13},{1,12},{2,15},{3,14},{4,9},{5,8},{6,11},{7,10},{8,5},{9,4},... | collective-permute-start | bytes 208904 | tf_op jit(solution)/shard_map/ppermute | solution.py:324
  34.3 7.1 %collective-permute-start.13 = (bf16[272,128]{1,0:T(8,128)(2,1)S(1)}, bf16[272,128]{1,0:T(8,128)(2,1)S(1)}, u32[]{:S(2)}, u32[]{:S(2)}) collective-permute-start(bf16[272,128]{1,0:T(8,128)(2,1)S(1)} %get-tuple-element.108), channel_id=1, source_target_pairs={{0,14},{1,15},{2,12},{3,13},{4,10},{5,11},{6,8},{7,9},{8,6},{9,7},... | collective-permute-start | bytes 208904 | tf_op jit(solution)/shard_map/ppermute | solution.py:324
  37.8 7.1 %collective-permute-start.14 = (bf16[272,128]{1,0:T(8,128)(2,1)S(1)}, bf16[272,128]{1,0:T(8,128)(2,1)S(1)}, u32[]{:S(2)}, u32[]{:S(2)}) collective-permute-start(bf16[272,128]{1,0:T(8,128)(2,1)S(1)} %get-tuple-element.109), channel_id=1, source_target_pairs={{0,15},{1,14},{2,13},{3,12},{4,11},{5,10},{6,9},{7,8},{8,7},{9,6},... | collective-permute-start | bytes 208904 | tf_op jit(solution)/shard_map/ppermute | solution.py:324
  47.8 7.9 %collective-permute-start.16 = (bf16[272,128]{1,0:T(8,128)(2,1)S(1)}, bf16[272,128]{1,0:T(8,128)(2,1)S(1)}, u32[]{:S(2)}, u32[]{:S(2)}) collective-permute-start(bf16[272,128]{1,0:T(8,128)(2,1)S(1)} %get-tuple-element.115), channel_id=1, source_target_pairs={{0,2},{1,3},{2,0},{3,1},{4,6},{5,7},{6,4},{7,5},{8,10},{9,11},{10,... | collective-permute-start | bytes 208904 | tf_op jit(solution)/shard_map/ppermute | solution.py:324
  48.4 8.0 %collective-permute-start.17 = (bf16[272,128]{1,0:T(8,128)(2,1)S(1)}, bf16[272,128]{1,0:T(8,128)(2,1)S(1)}, u32[]{:S(2)}, u32[]{:S(2)}) collective-permute-start(bf16[272,128]{1,0:T(8,128)(2,1)S(1)} %get-tuple-element.116), channel_id=1, source_target_pairs={{0,3},{1,2},{2,1},{3,0},{4,7},{5,6},{6,5},{7,4},{8,11},{9,10},{10,... | collective-permute-start | bytes 208904 | tf_op jit(solution)/shard_map/ppermute | solution.py:324
  49.6 9.6 %collective-permute-start.18 = (bf16[272,128]{1,0:T(8,128)(2,1)S(1)}, bf16[272,128]{1,0:T(8,128)(2,1)S(1)}, u32[]{:S(2)}, u32[]{:S(2)}) collective-permute-start(bf16[272,128]{1,0:T(8,128)(2,1)S(1)} %get-tuple-element.117), channel_id=1, source_target_pairs={{0,4},{1,5},{2,6},{3,7},{4,0},{5,1},{6,2},{7,3},{8,12},{9,13},{10,... | collective-permute-start | bytes 208904 | tf_op jit(solution)/shard_map/ppermute | solution.py:324
  54.0 7.8 %collective-permute-start.20 = (bf16[272,128]{1,0:T(8,128)(2,1)S(1)}, bf16[272,128]{1,0:T(8,128)(2,1)S(1)}, u32[]{:S(2)}, u32[]{:S(2)}) collective-permute-start(bf16[272,128]{1,0:T(8,128)(2,1)S(1)} %get-tuple-element.119), channel_id=1, source_target_pairs={{0,6},{1,7},{2,4},{3,5},{4,2},{5,3},{6,0},{7,1},{8,14},{9,15},{10,... | collective-permute-start | bytes 208904 | tf_op jit(solution)/shard_map/ppermute | solution.py:324
  55.7 7.4 %collective-permute-start.21 = (bf16[272,128]{1,0:T(8,128)(2,1)S(1)}, bf16[272,128]{1,0:T(8,128)(2,1)S(1)}, u32[]{:S(2)}, u32[]{:S(2)}) collective-permute-start(bf16[272,128]{1,0:T(8,128)(2,1)S(1)} %get-tuple-element.120), channel_id=1, source_target_pairs={{0,7},{1,6},{2,5},{3,4},{4,3},{5,2},{6,1},{7,0},{8,15},{9,14},{10,... | collective-permute-start | bytes 208904 | tf_op jit(solution)/shard_map/ppermute | solution.py:324
  56.4 8.5 %collective-permute-start.22 = (bf16[272,128]{1,0:T(8,128)(2,1)S(1)}, bf16[272,128]{1,0:T(8,128)(2,1)S(1)}, u32[]{:S(2)}, u32[]{:S(2)}) collective-permute-start(bf16[272,128]{1,0:T(8,128)(2,1)S(1)} %get-tuple-element.121), channel_id=1, source_target_pairs={{0,8},{1,9},{2,10},{3,11},{4,12},{5,13},{6,14},{7,15},{8,0},{9,1},... | collective-permute-start | bytes 208904 | tf_op jit(solution)/shard_map/ppermute | solution.py:324
  59.2 14.0 %collective-permute-start.23 = (bf16[272,128]{1,0:T(8,128)(2,1)S(1)}, bf16[272,128]{1,0:T(8,128)(2,1)S(1)}, u32[]{:S(2)}, u32[]{:S(2)}) collective-permute-start(bf16[272,128]{1,0:T(8,128)(2,1)S(1)} %get-tuple-element.122), channel_id=1, source_target_pairs={{0,9},{1,8},{2,11},{3,10},{4,13},{5,12},{6,15},{7,14},{8,1},{9,0},... | collective-permute-start | bytes 208904 | tf_op jit(solution)/shard_map/ppermute | solution.py:324
  59.3 15.7 %collective-permute-start.24 = (bf16[272,128]{1,0:T(8,128)(2,1)S(1)}, bf16[272,128]{1,0:T(8,128)(2,1)S(1)}, u32[]{:S(2)}, u32[]{:S(2)}) collective-permute-start(bf16[272,128]{1,0:T(8,128)(2,1)S(1)} %get-tuple-element.123), channel_id=1, source_target_pairs={{0,10},{1,11},{2,8},{3,9},{4,14},{5,15},{6,12},{7,13},{8,2},{9,3},... | collective-permute-start | bytes 208904 | tf_op jit(solution)/shard_map/ppermute | solution.py:324
  61.8 15.9 %collective-permute-start.25 = (bf16[272,128]{1,0:T(8,128)(2,1)S(1)}, bf16[272,128]{1,0:T(8,128)(2,1)S(1)}, u32[]{:S(2)}, u32[]{:S(2)}) collective-permute-start(bf16[272,128]{1,0:T(8,128)(2,1)S(1)} %get-tuple-element.124), channel_id=1, source_target_pairs={{0,11},{1,10},{2,9},{3,8},{4,15},{5,14},{6,13},{7,12},{8,3},{9,2},... | collective-permute-start | bytes 208904 | tf_op jit(solution)/shard_map/ppermute | solution.py:324
  63.0 14.7 %collective-permute-start.26 = (bf16[272,128]{1,0:T(8,128)(2,1)S(1)}, bf16[272,128]{1,0:T(8,128)(2,1)S(1)}, u32[]{:S(2)}, u32[]{:S(2)}) collective-permute-start(bf16[272,128]{1,0:T(8,128)(2,1)S(1)} %get-tuple-element.125), channel_id=1, source_target_pairs={{0,12},{1,13},{2,14},{3,15},{4,8},{5,9},{6,10},{7,11},{8,4},{9,5},... | collective-permute-start | bytes 208904 | tf_op jit(solution)/shard_map/ppermute | solution.py:324
  64.9 12.8 %collective-permute-start.27 = (bf16[272,128]{1,0:T(8,128)(2,1)S(1)}, bf16[272,128]{1,0:T(8,128)(2,1)S(1)}, u32[]{:S(2)}, u32[]{:S(2)}) collective-permute-start(bf16[272,128]{1,0:T(8,128)(2,1)S(1)} %get-tuple-element.126), channel_id=1, source_target_pairs={{0,13},{1,12},{2,15},{3,14},{4,9},{5,8},{6,11},{7,10},{8,5},{9,4},... | collective-permute-start | bytes 208904 | tf_op jit(solution)/shard_map/ppermute | solution.py:324
  73.2 7.4 %collective-permute-start.28 = (bf16[272,128]{1,0:T(8,128)(2,1)S(1)}, bf16[272,128]{1,0:T(8,128)(2,1)S(1)}, u32[]{:S(2)}, u32[]{:S(2)}) collective-permute-start(bf16[272,128]{1,0:T(8,128)(2,1)S(1)} %get-tuple-element.127), channel_id=1, source_target_pairs={{0,14},{1,15},{2,12},{3,13},{4,10},{5,11},{6,8},{7,9},{8,6},{9,7},... | collective-permute-start | bytes 208904 | tf_op jit(solution)/shard_map/ppermute | solution.py:324
  75.1 7.0 %collective-permute-start.29 = (bf16[272,128]{1,0:T(8,128)(2,1)S(1)}, bf16[272,128]{1,0:T(8,128)(2,1)S(1)}, u32[]{:S(2)}, u32[]{:S(2)}) collective-permute-start(bf16[272,128]{1,0:T(8,128)(2,1)S(1)} %get-tuple-element.128), channel_id=1, source_target_pairs={{0,15},{1,14},{2,13},{3,12},{4,11},{5,10},{6,9},{7,8},{8,7},{9,6},... | collective-permute-start | bytes 208904 | tf_op jit(solution)/shard_map/ppermute | solution.py:324
  88.0 8.1 %collective-permute-start.31 = (bf16[272,128]{1,0:T(8,128)(2,1)S(1)}, bf16[272,128]{1,0:T(8,128)(2,1)S(1)}, u32[]{:S(2)}, u32[]{:S(2)}) collective-permute-start(bf16[272,128]{1,0:T(8,128)(2,1)S(1)} %get-tuple-element.131), channel_id=1, source_target_pairs={{0,2},{1,3},{2,0},{3,1},{4,6},{5,7},{6,4},{7,5},{8,10},{9,11},{10,... | collective-permute-start | bytes 208904 | tf_op jit(solution)/shard_map/ppermute | solution.py:324
  89.8 6.6 %collective-permute-start.32 = (bf16[272,128]{1,0:T(8,128)(2,1)S(1)}, bf16[272,128]{1,0:T(8,128)(2,1)S(1)}, u32[]{:S(2)}, u32[]{:S(2)}) collective-permute-start(bf16[272,128]{1,0:T(8,128)(2,1)S(1)} %get-tuple-element.132), channel_id=1, source_target_pairs={{0,3},{1,2},{2,1},{3,0},{4,7},{5,6},{6,5},{7,4},{8,11},{9,10},{10,... | collective-permute-start | bytes 208904 | tf_op jit(solution)/shard_map/ppermute | solution.py:324
  89.9 8.8 %collective-permute-start.33 = (bf16[272,128]{1,0:T(8,128)(2,1)S(1)}, bf16[272,128]{1,0:T(8,128)(2,1)S(1)}, u32[]{:S(2)}, u32[]{:S(2)}) collective-permute-start(bf16[272,128]{1,0:T(8,128)(2,1)S(1)} %get-tuple-element.133), channel_id=1, source_target_pairs={{0,4},{1,5},{2,6},{3,7},{4,0},{5,1},{6,2},{7,3},{8,12},{9,13},{10,... | collective-permute-start | bytes 208904 | tf_op jit(solution)/shard_map/ppermute | solution.py:324
  93.4 6.7 %collective-permute-start.34 = (bf16[272,128]{1,0:T(8,128)(2,1)S(1)}, bf16[272,128]{1,0:T(8,128)(2,1)S(1)}, u32[]{:S(2)}, u32[]{:S(2)}) collective-permute-start(bf16[272,128]{1,0:T(8,128)(2,1)S(1)} %get-tuple-element.134), channel_id=1, source_target_pairs={{0,5},{1,4},{2,7},{3,6},{4,1},{5,0},{6,3},{7,2},{8,13},{9,12},{10,... | collective-permute-start | bytes 208904 | tf_op jit(solution)/shard_map/ppermute | solution.py:324
  93.4 8.2 %collective-permute-start.35 = (bf16[272,128]{1,0:T(8,128)(2,1)S(1)}, bf16[272,128]{1,0:T(8,128)(2,1)S(1)}, u32[]{:S(2)}, u32[]{:S(2)}) collective-permute-start(bf16[272,128]{1,0:T(8,128)(2,1)S(1)} %get-tuple-element.135), channel_id=1, source_target_pairs={{0,6},{1,7},{2,4},{3,5},{4,2},{5,3},{6,0},{7,1},{8,14},{9,15},{10,... | collective-permute-start | bytes 208904 | tf_op jit(solution)/shard_map/ppermute | solution.py:324
  96.2 7.4 %collective-permute-start.36 = (bf16[272,128]{1,0:T(8,128)(2,1)S(1)}, bf16[272,128]{1,0:T(8,128)(2,1)S(1)}, u32[]{:S(2)}, u32[]{:S(2)}) collective-permute-start(bf16[272,128]{1,0:T(8,128)(2,1)S(1)} %get-tuple-element.136), channel_id=1, source_target_pairs={{0,7},{1,6},{2,5},{3,4},{4,3},{5,2},{6,1},{7,0},{8,15},{9,14},{10,... | collective-permute-start | bytes 208904 | tf_op jit(solution)/shard_map/ppermute | solution.py:324
  96.4 8.0 %collective-permute-start.37 = (bf16[272,128]{1,0:T(8,128)(2,1)S(1)}, bf16[272,128]{1,0:T(8,128)(2,1)S(1)}, u32[]{:S(2)}, u32[]{:S(2)}) collective-permute-start(bf16[272,128]{1,0:T(8,128)(2,1)S(1)} %get-tuple-element.137), channel_id=1, source_target_pairs={{0,8},{1,9},{2,10},{3,11},{4,12},{5,13},{6,14},{7,15},{8,0},{9,1},... | collective-permute-start | bytes 208904 | tf_op jit(solution)/shard_map/ppermute | solution.py:324
  98.7 13.2 %collective-permute-start.38 = (bf16[272,128]{1,0:T(8,128)(2,1)S(1)}, bf16[272,128]{1,0:T(8,128)(2,1)S(1)}, u32[]{:S(2)}, u32[]{:S(2)}) collective-permute-start(bf16[272,128]{1,0:T(8,128)(2,1)S(1)} %get-tuple-element.138), channel_id=1, source_target_pairs={{0,9},{1,8},{2,11},{3,10},{4,13},{5,12},{6,15},{7,14},{8,1},{9,0},... | collective-permute-start | bytes 208904 | tf_op jit(solution)/shard_map/ppermute | solution.py:324
  100.0 15.2 %collective-permute-start.39 = (bf16[272,128]{1,0:T(8,128)(2,1)S(1)}, bf16[272,128]{1,0:T(8,128)(2,1)S(1)}, u32[]{:S(2)}, u32[]{:S(2)}) collective-permute-start(bf16[272,128]{1,0:T(8,128)(2,1)S(1)} %get-tuple-element.139), channel_id=1, source_target_pairs={{0,10},{1,11},{2,8},{3,9},{4,14},{5,15},{6,12},{7,13},{8,2},{9,3},... | collective-permute-start | bytes 208904 | tf_op jit(solution)/shard_map/ppermute | solution.py:324
  101.6 14.5 %collective-permute-start.40 = (bf16[272,128]{1,0:T(8,128)(2,1)S(1)}, bf16[272,128]{1,0:T(8,128)(2,1)S(1)}, u32[]{:S(2)}, u32[]{:S(2)}) collective-permute-start(bf16[272,128]{1,0:T(8,128)(2,1)S(1)} %get-tuple-element.140), channel_id=1, source_target_pairs={{0,11},{1,10},{2,9},{3,8},{4,15},{5,14},{6,13},{7,12},{8,3},{9,2},... | collective-permute-start | bytes 208904 | tf_op jit(solution)/shard_map/ppermute | solution.py:324
  103.6 12.5 %collective-permute-start.41 = (bf16[272,128]{1,0:T(8,128)(2,1)S(1)}, bf16[272,128]{1,0:T(8,128)(2,1)S(1)}, u32[]{:S(2)}, u32[]{:S(2)}) collective-permute-start(bf16[272,128]{1,0:T(8,128)(2,1)S(1)} %get-tuple-element.141), channel_id=1, source_target_pairs={{0,12},{1,13},{2,14},{3,15},{4,8},{5,9},{6,10},{7,11},{8,4},{9,5},... | collective-permute-start | bytes 208904 | tf_op jit(solution)/shard_map/ppermute | solution.py:324
  104.4 11.7 %collective-permute-start.42 = (bf16[272,128]{1,0:T(8,128)(2,1)S(1)}, bf16[272,128]{1,0:T(8,128)(2,1)S(1)}, u32[]{:S(2)}, u32[]{:S(2)}) collective-permute-start(bf16[272,128]{1,0:T(8,128)(2,1)S(1)} %get-tuple-element.142), channel_id=1, source_target_pairs={{0,13},{1,12},{2,15},{3,14},{4,9},{5,8},{6,11},{7,10},{8,5},{9,4},... | collective-permute-start | bytes 208904 | tf_op jit(solution)/shard_map/ppermute | solution.py:324
  111.9 7.1 %collective-permute-start.43 = (bf16[272,128]{1,0:T(8,128)(2,1)S(1)}, bf16[272,128]{1,0:T(8,128)(2,1)S(1)}, u32[]{:S(2)}, u32[]{:S(2)}) collective-permute-start(bf16[272,128]{1,0:T(8,128)(2,1)S(1)} %get-tuple-element.143), channel_id=1, source_target_pairs={{0,14},{1,15},{2,12},{3,13},{4,10},{5,11},{6,8},{7,9},{8,6},{9,7},... | collective-permute-start | bytes 208904 | tf_op jit(solution)/shard_map/ppermute | solution.py:324
  115.2 7.0 %collective-permute-start.44 = (bf16[272,128]{1,0:T(8,128)(2,1)S(1)}, bf16[272,128]{1,0:T(8,128)(2,1)S(1)}, u32[]{:S(2)}, u32[]{:S(2)}) collective-permute-start(bf16[272,128]{1,0:T(8,128)(2,1)S(1)} %get-tuple-element.144), channel_id=1, source_target_pairs={{0,15},{1,14},{2,13},{3,12},{4,11},{5,10},{6,9},{7,8},{8,7},{9,6},... | collective-permute-start | bytes 208904 | tf_op jit(solution)/shard_map/ppermute | solution.py:324
  124.6 7.5 %collective-permute-start.46 = (bf16[272,128]{1,0:T(8,128)(2,1)S(1)}, bf16[272,128]{1,0:T(8,128)(2,1)S(1)}, u32[]{:S(2)}, u32[]{:S(2)}) collective-permute-start(bf16[272,128]{1,0:T(8,128)(2,1)S(1)} %get-tuple-element.150), channel_id=1, source_target_pairs={{0,2},{1,3},{2,0},{3,1},{4,6},{5,7},{6,4},{7,5},{8,10},{9,11},{10,... | collective-permute-start | bytes 208904 | tf_op jit(solution)/shard_map/ppermute | solution.py:324
  126.4 8.4 %collective-permute-start.48 = (bf16[272,128]{1,0:T(8,128)(2,1)S(1)}, bf16[272,128]{1,0:T(8,128)(2,1)S(1)}, u32[]{:S(2)}, u32[]{:S(2)}) collective-permute-start(bf16[272,128]{1,0:T(8,128)(2,1)S(1)} %get-tuple-element.152), channel_id=1, source_target_pairs={{0,4},{1,5},{2,6},{3,7},{4,0},{5,1},{6,2},{7,3},{8,12},{9,13},{10,... | collective-permute-start | bytes 208904 | tf_op jit(solution)/shard_map/ppermute | solution.py:324
  129.7 8.1 %collective-permute-start.50 = (bf16[272,128]{1,0:T(8,128)(2,1)S(1)}, bf16[272,128]{1,0:T(8,128)(2,1)S(1)}, u32[]{:S(2)}, u32[]{:S(2)}) collective-permute-start(bf16[272,128]{1,0:T(8,128)(2,1)S(1)} %get-tuple-element.154), channel_id=1, source_target_pairs={{0,6},{1,7},{2,4},{3,5},{4,2},{5,3},{6,0},{7,1},{8,14},{9,15},{10,... | collective-permute-start | bytes 208904 | tf_op jit(solution)/shard_map/ppermute | solution.py:324
  132.1 6.9 %collective-permute-start.51 = (bf16[272,128]{1,0:T(8,128)(2,1)S(1)}, bf16[272,128]{1,0:T(8,128)(2,1)S(1)}, u32[]{:S(2)}, u32[]{:S(2)}) collective-permute-start(bf16[272,128]{1,0:T(8,128)(2,1)S(1)} %get-tuple-element.155), channel_id=1, source_target_pairs={{0,7},{1,6},{2,5},{3,4},{4,3},{5,2},{6,1},{7,0},{8,15},{9,14},{10,... | collective-permute-start | bytes 208904 | tf_op jit(solution)/shard_map/ppermute | solution.py:324
  132.2 8.8 %collective-permute-start.52 = (bf16[272,128]{1,0:T(8,128)(2,1)S(1)}, bf16[272,128]{1,0:T(8,128)(2,1)S(1)}, u32[]{:S(2)}, u32[]{:S(2)}) collective-permute-start(bf16[272,128]{1,0:T(8,128)(2,1)S(1)} %get-tuple-element.156), channel_id=1, source_target_pairs={{0,8},{1,9},{2,10},{3,11},{4,12},{5,13},{6,14},{7,15},{8,0},{9,1},... | collective-permute-start | bytes 208904 | tf_op jit(solution)/shard_map/ppermute | solution.py:324
  134.8 14.0 %collective-permute-start.53 = (bf16[272,128]{1,0:T(8,128)(2,1)S(1)}, bf16[272,128]{1,0:T(8,128)(2,1)S(1)}, u32[]{:S(2)}, u32[]{:S(2)}) collective-permute-start(bf16[272,128]{1,0:T(8,128)(2,1)S(1)} %get-tuple-element.157), channel_id=1, source_target_pairs={{0,9},{1,8},{2,11},{3,10},{4,13},{5,12},{6,15},{7,14},{8,1},{9,0},... | collective-permute-start | bytes 208904 | tf_op jit(solution)/shard_map/ppermute | solution.py:324
  135.9 15.1 %collective-permute-start.54 = (bf16[272,128]{1,0:T(8,128)(2,1)S(1)}, bf16[272,128]{1,0:T(8,128)(2,1)S(1)}, u32[]{:S(2)}, u32[]{:S(2)}) collective-permute-start(bf16[272,128]{1,0:T(8,128)(2,1)S(1)} %get-tuple-element.158), channel_id=1, source_target_pairs={{0,10},{1,11},{2,8},{3,9},{4,14},{5,15},{6,12},{7,13},{8,2},{9,3},... | collective-permute-start | bytes 208904 | tf_op jit(solution)/shard_map/ppermute | solution.py:324
  137.8 15.3 %collective-permute-start.55 = (bf16[272,128]{1,0:T(8,128)(2,1)S(1)}, bf16[272,128]{1,0:T(8,128)(2,1)S(1)}, u32[]{:S(2)}, u32[]{:S(2)}) collective-permute-start(bf16[272,128]{1,0:T(8,128)(2,1)S(1)} %get-tuple-element.159), channel_id=1, source_target_pairs={{0,11},{1,10},{2,9},{3,8},{4,15},{5,14},{6,13},{7,12},{8,3},{9,2},... | collective-permute-start | bytes 208904 | tf_op jit(solution)/shard_map/ppermute | solution.py:324
  139.0 14.1 %collective-permute-start.56 = (bf16[272,128]{1,0:T(8,128)(2,1)S(1)}, bf16[272,128]{1,0:T(8,128)(2,1)S(1)}, u32[]{:S(2)}, u32[]{:S(2)}) collective-permute-start(bf16[272,128]{1,0:T(8,128)(2,1)S(1)} %get-tuple-element.160), channel_id=1, source_target_pairs={{0,12},{1,13},{2,14},{3,15},{4,8},{5,9},{6,10},{7,11},{8,4},{9,5},... | collective-permute-start | bytes 208904 | tf_op jit(solution)/shard_map/ppermute | solution.py:324
  141.0 12.1 %collective-permute-start.57 = (bf16[272,128]{1,0:T(8,128)(2,1)S(1)}, bf16[272,128]{1,0:T(8,128)(2,1)S(1)}, u32[]{:S(2)}, u32[]{:S(2)}) collective-permute-start(bf16[272,128]{1,0:T(8,128)(2,1)S(1)} %get-tuple-element.161), channel_id=1, source_target_pairs={{0,13},{1,12},{2,15},{3,14},{4,9},{5,8},{6,11},{7,10},{8,5},{9,4},... | collective-permute-start | bytes 208904 | tf_op jit(solution)/shard_map/ppermute | solution.py:324
  148.8 7.1 %collective-permute-start.58 = (bf16[272,128]{1,0:T(8,128)(2,1)S(1)}, bf16[272,128]{1,0:T(8,128)(2,1)S(1)}, u32[]{:S(2)}, u32[]{:S(2)}) collective-permute-start(bf16[272,128]{1,0:T(8,128)(2,1)S(1)} %get-tuple-element.162), channel_id=1, source_target_pairs={{0,14},{1,15},{2,12},{3,13},{4,10},{5,11},{6,8},{7,9},{8,6},{9,7},... | collective-permute-start | bytes 208904 | tf_op jit(solution)/shard_map/ppermute | solution.py:324
  151.1 7.2 %collective-permute-start.59 = (bf16[272,128]{1,0:T(8,128)(2,1)S(1)}, bf16[272,128]{1,0:T(8,128)(2,1)S(1)}, u32[]{:S(2)}, u32[]{:S(2)}) collective-permute-start(bf16[272,128]{1,0:T(8,128)(2,1)S(1)} %get-tuple-element.163), channel_id=1, source_target_pairs={{0,15},{1,14},{2,13},{3,12},{4,11},{5,10},{6,9},{7,8},{8,7},{9,6},... | collective-permute-start | bytes 208904 | tf_op jit(solution)/shard_map/ppermute | solution.py:324
  164.8 7.5 %collective-permute-start.61 = (bf16[272,128]{1,0:T(8,128)(2,1)S(1)}, bf16[272,128]{1,0:T(8,128)(2,1)S(1)}, u32[]{:S(2)}, u32[]{:S(2)}) collective-permute-start(bf16[272,128]{1,0:T(8,128)(2,1)S(1)} %get-tuple-element.167), channel_id=1, source_target_pairs={{0,2},{1,3},{2,0},{3,1},{4,6},{5,7},{6,4},{7,5},{8,10},{9,11},{10,... | collective-permute-start | bytes 208904 | tf_op jit(solution)/shard_map/ppermute | solution.py:324
  166.6 8.2 %collective-permute-start.63 = (bf16[272,128]{1,0:T(8,128)(2,1)S(1)}, bf16[272,128]{1,0:T(8,128)(2,1)S(1)}, u32[]{:S(2)}, u32[]{:S(2)}) collective-permute-start(bf16[272,128]{1,0:T(8,128)(2,1)S(1)} %get-tuple-element.169), channel_id=1, source_target_pairs={{0,4},{1,5},{2,6},{3,7},{4,0},{5,1},{6,2},{7,3},{8,12},{9,13},{10,... | collective-permute-start | bytes 208904 | tf_op jit(solution)/shard_map/ppermute | solution.py:324
  170.0 8.1 %collective-permute-start.65 = (bf16[272,128]{1,0:T(8,128)(2,1)S(1)}, bf16[272,128]{1,0:T(8,128)(2,1)S(1)}, u32[]{:S(2)}, u32[]{:S(2)}) collective-permute-start(bf16[272,128]{1,0:T(8,128)(2,1)S(1)} %get-tuple-element.171), channel_id=1, source_target_pairs={{0,6},{1,7},{2,4},{3,5},{4,2},{5,3},{6,0},{7,1},{8,14},{9,15},{10,... | collective-permute-start | bytes 208904 | tf_op jit(solution)/shard_map/ppermute | solution.py:324
  172.3 7.0 %collective-permute-start.66 = (bf16[272,128]{1,0:T(8,128)(2,1)S(1)}, bf16[272,128]{1,0:T(8,128)(2,1)S(1)}, u32[]{:S(2)}, u32[]{:S(2)}) collective-permute-start(bf16[272,128]{1,0:T(8,128)(2,1)S(1)} %get-tuple-element.172), channel_id=1, source_target_pairs={{0,7},{1,6},{2,5},{3,4},{4,3},{5,2},{6,1},{7,0},{8,15},{9,14},{10,... | collective-permute-start | bytes 208904 | tf_op jit(solution)/shard_map/ppermute | solution.py:324
  172.5 8.6 %collective-permute-start.67 = (bf16[272,128]{1,0:T(8,128)(2,1)S(1)}, bf16[272,128]{1,0:T(8,128)(2,1)S(1)}, u32[]{:S(2)}, u32[]{:S(2)}) collective-permute-start(bf16[272,128]{1,0:T(8,128)(2,1)S(1)} %get-tuple-element.173), channel_id=1, source_target_pairs={{0,8},{1,9},{2,10},{3,11},{4,12},{5,13},{6,14},{7,15},{8,0},{9,1},... | collective-permute-start | bytes 208904 | tf_op jit(solution)/shard_map/ppermute | solution.py:324
  174.8 14.0 %collective-permute-start.68 = (bf16[272,128]{1,0:T(8,128)(2,1)S(1)}, bf16[272,128]{1,0:T(8,128)(2,1)S(1)}, u32[]{:S(2)}, u32[]{:S(2)}) collective-permute-start(bf16[272,128]{1,0:T(8,128)(2,1)S(1)} %get-tuple-element.174), channel_id=1, source_target_pairs={{0,9},{1,8},{2,11},{3,10},{4,13},{5,12},{6,15},{7,14},{8,1},{9,0},... | collective-permute-start | bytes 208904 | tf_op jit(solution)/shard_map/ppermute | solution.py:324
  176.1 15.2 %collective-permute-start.69 = (bf16[272,128]{1,0:T(8,128)(2,1)S(1)}, bf16[272,128]{1,0:T(8,128)(2,1)S(1)}, u32[]{:S(2)}, u32[]{:S(2)}) collective-permute-start(bf16[272,128]{1,0:T(8,128)(2,1)S(1)} %get-tuple-element.175), channel_id=1, source_target_pairs={{0,10},{1,11},{2,8},{3,9},{4,14},{5,15},{6,12},{7,13},{8,2},{9,3},... | collective-permute-start | bytes 208904 | tf_op jit(solution)/shard_map/ppermute | solution.py:324
  178.0 15.0 %collective-permute-start.70 = (bf16[272,128]{1,0:T(8,128)(2,1)S(1)}, bf16[272,128]{1,0:T(8,128)(2,1)S(1)}, u32[]{:S(2)}, u32[]{:S(2)}) collective-permute-start(bf16[272,128]{1,0:T(8,128)(2,1)S(1)} %get-tuple-element.176), channel_id=1, source_target_pairs={{0,11},{1,10},{2,9},{3,8},{4,15},{5,14},{6,13},{7,12},{8,3},{9,2},... | collective-permute-start | bytes 208904 | tf_op jit(solution)/shard_map/ppermute | solution.py:324
  179.3 13.7 %collective-permute-start.71 = (bf16[272,128]{1,0:T(8,128)(2,1)S(1)}, bf16[272,128]{1,0:T(8,128)(2,1)S(1)}, u32[]{:S(2)}, u32[]{:S(2)}) collective-permute-start(bf16[272,128]{1,0:T(8,128)(2,1)S(1)} %get-tuple-element.177), channel_id=1, source_target_pairs={{0,12},{1,13},{2,14},{3,15},{4,8},{5,9},{6,10},{7,11},{8,4},{9,5},... | collective-permute-start | bytes 208904 | tf_op jit(solution)/shard_map/ppermute | solution.py:324
  181.1 11.9 %collective-permute-start.72 = (bf16[272,128]{1,0:T(8,128)(2,1)S(1)}, bf16[272,128]{1,0:T(8,128)(2,1)S(1)}, u32[]{:S(2)}, u32[]{:S(2)}) collective-permute-start(bf16[272,128]{1,0:T(8,128)(2,1)S(1)} %get-tuple-element.178), channel_id=1, source_target_pairs={{0,13},{1,12},{2,15},{3,14},{4,9},{5,8},{6,11},{7,10},{8,5},{9,4},... | collective-permute-start | bytes 208904 | tf_op jit(solution)/shard_map/ppermute | solution.py:324
  188.8 7.1 %collective-permute-start.73 = (bf16[272,128]{1,0:T(8,128)(2,1)S(1)}, bf16[272,128]{1,0:T(8,128)(2,1)S(1)}, u32[]{:S(2)}, u32[]{:S(2)}) collective-permute-start(bf16[272,128]{1,0:T(8,128)(2,1)S(1)} %get-tuple-element.179), channel_id=1, source_target_pairs={{0,14},{1,15},{2,12},{3,13},{4,10},{5,11},{6,8},{7,9},{8,6},{9,7},... | collective-permute-start | bytes 208904 | tf_op jit(solution)/shard_map/ppermute | solution.py:324
  191.3 7.3 %collective-permute-start.74 = (bf16[272,128]{1,0:T(8,128)(2,1)S(1)}, bf16[272,128]{1,0:T(8,128)(2,1)S(1)}, u32[]{:S(2)}, u32[]{:S(2)}) collective-permute-start(bf16[272,128]{1,0:T(8,128)(2,1)S(1)} %get-tuple-element.180), channel_id=1, source_target_pairs={{0,15},{1,14},{2,13},{3,12},{4,11},{5,10},{6,9},{7,8},{8,7},{9,6},... | collective-permute-start | bytes 208904 | tf_op jit(solution)/shard_map/ppermute | solution.py:324
  202.5 13.4 %all-to-all-start = ((f32[16,16,128]{2,1,0:T(8,128)}), f32[16,16,128]{2,1,0:T(8,128)S(1)}, u32[]{:S(2)}, u32[]{:S(2)}) async-start(f32[16,16,128]{2,1,0:T(8,128)} %get-tuple-element.184), calls=%async_computation | async-start | bytes 262144 | tf_op jit(solution)/shard_map/all_to_all | solution.py:409
  (22 other events, 306.5 us)

commit v4 on v3

--- a/solution.py
+++ b/solution.py
@@ -131,7 +131,7 @@
         count = counts_ref[pair]
         for slot in range(slot_count):
             cell = cells_ref[pair, slot]
-            owner = (cell // owned) ^ me_ref[0]
+            owner = (peers - ((cell // owned) ^ me_ref[0])) % peers
             local = cell % owned
             used = used_ref[owner]
             rank = used
@@ -321,8 +321,8 @@
 def exchange(values):
     peers = len(values)
     return [values[0]] + [
-        lax.ppermute(values[step], "pair", [(i, i ^ step) for i in range(peers)])
-        for step in range(1, peers)
+        lax.ppermute(values[i], "pair", [(one, one ^ (peers - i)) for one in range(peers)])
+        for i in range(1, peers)
     ]
 
 

time: 220 us -> 218 us (level)
  starting transfers between devices: 128 us -> 117 us
  waiting for transfers between devices: 51.9 us -> 60.9 us
    ppermute x75, starting transfers between devices: 122 us -> 113 us  [exchange(): lax.ppermute(values[i], 'pair', [(one, one ^ peers - i) for one in range(...]
    ppermute x75, waiting for transfers between devices: 47.7 us -> 56.6 us  [exchange(): lax.ppermute(values[i], 'pair', [(one, one ^ peers - i) for one in range(...]
  transfers between devices with their start and end apart: 76 -> 76, of which waited for: 20 -> 42; matrix products, arithmetic and copies ran while one was open for 0% -> 0% of each run, Pallas kernels for 1% -> 1%
where the time goes in v4:
time: 218 us
  starting transfers between devices  117 us (54%)
  waiting for transfers between devices  60.9 us (28%)
  Pallas kernels  30.4 us (14%)
  local copies, waits for them, and re-layouts  8.96 us (4%)
    ppermute x75, starting transfers between devices, exchange(): lax.ppermute(values[i], 'pair', [(one, one ^ peers - i) for one in range(...  113 us
    ppermute x75, waiting for transfers between devices, exchange(): lax.ppermute(values[i], 'pair', [(one, one ^ peers - i) for one in range(...  56.6 us
    pallas_call x2, Pallas kernels, on_device(): call(functools.partial(pair_kernel, rows, peers), 'pairs', [SMEM] + ins +...  12.3 us
    unnamed x20, local copies, waits for them, and re-layouts  8.96 us
    pallas_call x1, Pallas kernels, on_device(): call(kernel, 'start', [SMEM, SMEM, SMEM, VMEM, VMEM], messages + [((slots...  6.46 us
    pallas_call x2, Pallas kernels, on_device(): call(functools.partial(cell_kernel, False, last, peers), 'cells_last' if...  4.94 us
  transfers between devices with their start and end apart: 76, of which 42 were waited for; matrix products, arithmetic and copies ran while one was open for 0% of the time, Pallas kernels for 1%

profile of v4, /device:TPU:0, one launch (start us, length us, event | category | flops | bytes accessed | tf_op | source)
XLA Modules:
  0.0 217.9 jit_solution(9988630637150041869)
XLA Ops:
  0.6 2.2 %copy-done = bf16[8,16,128,128]{3,2,1,0:T(8,128)(2,1)S(1)} copy-done((bf16[8,16,128,128]{3,2,1,0:T(8,128)(2,1)S(1)}, bf16[8,16,128,128]{3,2,1,0:T(8,128)(2,1)}, u32[]{:S(2)}) %copy-start) | copy-done | bytes 4194328
  5.1 6.5 %start.1 = (bf16[272,128]{1,0:T(8,128)(2,1)S(1)}, bf16[272,128]{1,0:T(8,128)(2,1)S(1)}, bf16[272,128]{1,0:T(8,128)(2,1)S(1)}, bf16[272,128]{1,0:T(8,128)(2,1)S(1...) custom-call(s32[1]{0:T(128)} %bitcast.refs_0_, ...), custom_call_target="tpu_custom_call" | custom-call | flops 536870912 | bytes 6291456 | tf_op jit(solution)/shard_map/start/pallas_call | solution.py:354
  11.6 5.5 %collective-permute-start = (bf16[272,128]{1,0:T(8,128)(2,1)S(1)}, bf16[272,128]{1,0:T(8,128)(2,1)S(1)}, u32[]{:S(2)}, u32[]{:S(2)}) collective-permute-start(bf16[272,128]{1,0:T(8,128)(2,1)S(1)} %get-tuple-element.95), channel_id=1, source_target_pairs={{0,15},{1,14},{2,13},{3,12},{4,11},{5,10},{6,9},{7,8},{8,7},{9,6},... | collective-permute-start | bytes 208904 | tf_op jit(solution)/shard_map/ppermute | solution.py:324
  17.7 3.2 %collective-permute-start.2 = (bf16[272,128]{1,0:T(8,128)(2,1)S(1)}, bf16[272,128]{1,0:T(8,128)(2,1)S(1)}, u32[]{:S(2)}, u32[]{:S(2)}) collective-permute-start(bf16[272,128]{1,0:T(8,128)(2,1)S(1)} %get-tuple-element.97), channel_id=1, source_target_pairs={{0,13},{1,12},{2,15},{3,14},{4,9},{5,8},{6,11},{7,10},{8,5},{9,4},... | collective-permute-start | bytes 208904 | tf_op jit(solution)/shard_map/ppermute | solution.py:324
  21.2 3.6 %collective-permute-start.5 = (bf16[272,128]{1,0:T(8,128)(2,1)S(1)}, bf16[272,128]{1,0:T(8,128)(2,1)S(1)}, u32[]{:S(2)}, u32[]{:S(2)}) collective-permute-start(bf16[272,128]{1,0:T(8,128)(2,1)S(1)} %get-tuple-element.100), channel_id=1, source_target_pairs={{0,10},{1,11},{2,8},{3,9},{4,14},{5,15},{6,12},{7,13},{8,2},{9,3},... | collective-permute-start | bytes 208904 | tf_op jit(solution)/shard_map/ppermute | solution.py:324
  25.2 9.4 %collective-permute-start.7 = (bf16[272,128]{1,0:T(8,128)(2,1)S(1)}, bf16[272,128]{1,0:T(8,128)(2,1)S(1)}, u32[]{:S(2)}, u32[]{:S(2)}) collective-permute-start(bf16[272,128]{1,0:T(8,128)(2,1)S(1)} %get-tuple-element.102), channel_id=1, source_target_pairs={{0,8},{1,9},{2,10},{3,11},{4,12},{5,13},{6,14},{7,15},{8,0},{9,1},... | collective-permute-start | bytes 208904 | tf_op jit(solution)/shard_map/ppermute | solution.py:324
  34.6 2.6 %collective-permute-done.4.refs_5_ = bf16[272,128]{1,0:T(8,128)(2,1)S(1)} collective-permute-done((bf16[272,128]{1,0:T(8,128)(2,1)S(1)}, bf16[272,128]{1,0:T(8,128)(2,1)S(1)}, u32[]{:S(2)}, u32[]{:S(2)}) %collective-permute-start.4) | collective-permute-done | bytes 69664 | tf_op jit(solution)/shard_map/ppermute | solution.py:324
  37.2 1.9 collective-permute-done.5.refs_6_
  40.5 1.5 collective-permute-done.7.refs_8_
  42.0 1.4 collective-permute-done.8.refs_9_
  45.5 1.8 collective-permute-done.11.refs_12_
  48.0 2.7 %cells_first.1 = (f32[64,8192]{1,0:T(8,128)S(1)}, f32[64,128]{1,0:T(8,128)S(1)}, bf16[272,128]{1,0:T(8,128)(2,1)S(1)}, bf16[272,128]{1,0:T(8,128)(2,1)S(1)}, bf1...) custom-call(bf16[272,128]{1,0:T(8,128)(2,1)S(1)} %get-tuple-element., ...), custom_call_target="tpu_custom_call" | custom-call | bytes 6291456 | tf_op jit(solution)/shard_map/cells_first/pallas_call | solution.py:367
  50.7 1.9 collective-permute-start.15
  52.6 2.1 collective-permute-start.16
  54.7 2.6 %collective-permute-start.17 = (bf16[272,128]{1,0:T(8,128)(2,1)S(1)}, bf16[272,128]{1,0:T(8,128)(2,1)S(1)}, u32[]{:S(2)}, u32[]{:S(2)}) collective-permute-start(bf16[272,128]{1,0:T(8,128)(2,1)S(1)} %get-tuple-element.116), channel_id=1, source_target_pairs={{0,13},{1,12},{2,15},{3,14},{4,9},{5,8},{6,11},{7,10},{8,5},{9,4},... | collective-permute-start | bytes 208904 | tf_op jit(solution)/shard_map/ppermute | solution.py:324
  57.3 1.4 collective-permute-start.18
  58.8 3.0 %collective-permute-start.20 = (bf16[272,128]{1,0:T(8,128)(2,1)S(1)}, bf16[272,128]{1,0:T(8,128)(2,1)S(1)}, u32[]{:S(2)}, u32[]{:S(2)}) collective-permute-start(bf16[272,128]{1,0:T(8,128)(2,1)S(1)} %get-tuple-element.119), channel_id=1, source_target_pairs={{0,10},{1,11},{2,8},{3,9},{4,14},{5,15},{6,12},{7,13},{8,2},{9,3},... | collective-permute-start | bytes 208904 | tf_op jit(solution)/shard_map/ppermute | solution.py:324
  61.8 4.2 %collective-permute-start.21 = (bf16[272,128]{1,0:T(8,128)(2,1)S(1)}, bf16[272,128]{1,0:T(8,128)(2,1)S(1)}, u32[]{:S(2)}, u32[]{:S(2)}) collective-permute-start(bf16[272,128]{1,0:T(8,128)(2,1)S(1)} %get-tuple-element.120), channel_id=1, source_target_pairs={{0,9},{1,8},{2,11},{3,10},{4,13},{5,12},{6,15},{7,14},{8,1},{9,0},... | collective-permute-start | bytes 208904 | tf_op jit(solution)/shard_map/ppermute | solution.py:324
  66.0 3.1 %collective-permute-start.22 = (bf16[272,128]{1,0:T(8,128)(2,1)S(1)}, bf16[272,128]{1,0:T(8,128)(2,1)S(1)}, u32[]{:S(2)}, u32[]{:S(2)}) collective-permute-start(bf16[272,128]{1,0:T(8,128)(2,1)S(1)} %get-tuple-element.121), channel_id=1, source_target_pairs={{0,8},{1,9},{2,10},{3,11},{4,12},{5,13},{6,14},{7,15},{8,0},{9,1},... | collective-permute-start | bytes 208904 | tf_op jit(solution)/shard_map/ppermute | solution.py:324
  69.2 1.9 collective-permute-start.23
  72.3 3.6 %collective-permute-done.20.refs_6_ = bf16[272,128]{1,0:T(8,128)(2,1)S(1)} collective-permute-done((bf16[272,128]{1,0:T(8,128)(2,1)S(1)}, bf16[272,128]{1,0:T(8,128)(2,1)S(1)}, u32[]{:S(2)}, u32[]{:S(2)}) %collective-permute-start.20) | collective-permute-done | bytes 69664 | tf_op jit(solution)/shard_map/ppermute | solution.py:324
  78.8 1.4 collective-permute-start.28
  81.7 1.8 collective-permute-done.26.refs_12_
  84.3 5.9 %pairs.2 = (bf16[272,128]{1,0:T(8,128)(2,1)S(1)}, bf16[272,128]{1,0:T(8,128)(2,1)S(1)}, bf16[272,128]{1,0:T(8,128)(2,1)S(1)}, bf16[272,128]{1,0:T(8,128)(2,1)S(1...) custom-call(s32[128]{0:T(128)S(1)} %get-tuple-element.112.target_ref, ...), custom_call_target="tpu_custom_call" | custom-call | flops 1073741824 | bytes 8388608 | tf_op jit(solution)/shard_map/pairs/pallas_call | solution.py:384
  90.2 2.4 %collective-permute-start.30 = (bf16[272,128]{1,0:T(8,128)(2,1)S(1)}, bf16[272,128]{1,0:T(8,128)(2,1)S(1)}, u32[]{:S(2)}, u32[]{:S(2)}) collective-permute-start(bf16[272,128]{1,0:T(8,128)(2,1)S(1)} %get-tuple-element.130), channel_id=1, source_target_pairs={{0,15},{1,14},{2,13},{3,12},{4,11},{5,10},{6,9},{7,8},{8,7},{9,6},... | collective-permute-start | bytes 208904 | tf_op jit(solution)/shard_map/ppermute | solution.py:324
  92.6 1.9 collective-permute-start.31
  94.6 1.7 collective-permute-start.32
  96.3 2.0 collective-permute-start.33
  98.3 3.4 %collective-permute-start.35 = (bf16[272,128]{1,0:T(8,128)(2,1)S(1)}, bf16[272,128]{1,0:T(8,128)(2,1)S(1)}, u32[]{:S(2)}, u32[]{:S(2)}) collective-permute-start(bf16[272,128]{1,0:T(8,128)(2,1)S(1)} %get-tuple-element.135), channel_id=1, source_target_pairs={{0,10},{1,11},{2,8},{3,9},{4,14},{5,15},{6,12},{7,13},{8,2},{9,3},... | collective-permute-start | bytes 208904 | tf_op jit(solution)/shard_map/ppermute | solution.py:324
  101.7 7.5 %collective-permute-start.37 = (bf16[272,128]{1,0:T(8,128)(2,1)S(1)}, bf16[272,128]{1,0:T(8,128)(2,1)S(1)}, u32[]{:S(2)}, u32[]{:S(2)}) collective-permute-start(bf16[272,128]{1,0:T(8,128)(2,1)S(1)} %get-tuple-element.137), channel_id=1, source_target_pairs={{0,8},{1,9},{2,10},{3,11},{4,12},{5,13},{6,14},{7,15},{8,0},{9,1},... | collective-permute-start | bytes 208904 | tf_op jit(solution)/shard_map/ppermute | solution.py:324
  109.2 1.5 collective-permute-start.38
  112.0 3.4 %collective-permute-done.35.refs_7_ = bf16[272,128]{1,0:T(8,128)(2,1)S(1)} collective-permute-done((bf16[272,128]{1,0:T(8,128)(2,1)S(1)}, bf16[272,128]{1,0:T(8,128)(2,1)S(1)}, u32[]{:S(2)}, u32[]{:S(2)}) %collective-permute-start.35) | collective-permute-done | bytes 69664 | tf_op jit(solution)/shard_map/ppermute | solution.py:324
  120.2 1.4 collective-permute-done.41.refs_13_
  121.5 1.5 collective-permute-done.43.refs_15_
  123.0 2.3 %cells.1 = (f32[64,8192]{1,0:T(8,128)S(1)}, f32[64,128]{1,0:T(8,128)S(1)}, bf16[272,128]{1,0:T(8,128)(2,1)S(1)}, bf16[272,128]{1,0:T(8,128)(2,1)S(1)}, bf16[272,...) custom-call(s32[16,128]{1,0:T(8,128)S(1)} %get-tuple-element.111.ref, ...), custom_call_target="tpu_custom_call" | custom-call | bytes 8388608 | tf_op jit(solution)/shard_map/cells/pallas_call | solution.py:398
  125.3 2.0 collective-permute-start.45
  127.3 2.3 %collective-permute-start.46 = (bf16[272,128]{1,0:T(8,128)(2,1)S(1)}, bf16[272,128]{1,0:T(8,128)(2,1)S(1)}, u32[]{:S(2)}, u32[]{:S(2)}) collective-permute-start(bf16[272,128]{1,0:T(8,128)(2,1)S(1)} %get-tuple-element.150), channel_id=1, source_target_pairs={{0,14},{1,15},{2,12},{3,13},{4,10},{5,11},{6,8},{7,9},{8,6},{9,7},... | collective-permute-start | bytes 208904 | tf_op jit(solution)/shard_map/ppermute | solution.py:324
  129.7 2.2 collective-permute-start.47
  131.8 1.5 collective-permute-start.48
  133.4 3.4 %collective-permute-start.50 = (bf16[272,128]{1,0:T(8,128)(2,1)S(1)}, bf16[272,128]{1,0:T(8,128)(2,1)S(1)}, u32[]{:S(2)}, u32[]{:S(2)}) collective-permute-start(bf16[272,128]{1,0:T(8,128)(2,1)S(1)} %get-tuple-element.154), channel_id=1, source_target_pairs={{0,10},{1,11},{2,8},{3,9},{4,14},{5,15},{6,12},{7,13},{8,2},{9,3},... | collective-permute-start | bytes 208904 | tf_op jit(solution)/shard_map/ppermute | solution.py:324
  136.8 2.0 collective-permute-start.51
  138.7 6.1 %collective-permute-start.52 = (bf16[272,128]{1,0:T(8,128)(2,1)S(1)}, bf16[272,128]{1,0:T(8,128)(2,1)S(1)}, u32[]{:S(2)}, u32[]{:S(2)}) collective-permute-start(bf16[272,128]{1,0:T(8,128)(2,1)S(1)} %get-tuple-element.156), channel_id=1, source_target_pairs={{0,8},{1,9},{2,10},{3,11},{4,12},{5,13},{6,14},{7,15},{8,0},{9,1},... | collective-permute-start | bytes 208904 | tf_op jit(solution)/shard_map/ppermute | solution.py:324
  144.9 3.3 %collective-permute-done.49.refs_5_ = bf16[272,128]{1,0:T(8,128)(2,1)S(1)} collective-permute-done((bf16[272,128]{1,0:T(8,128)(2,1)S(1)}, bf16[272,128]{1,0:T(8,128)(2,1)S(1)}, u32[]{:S(2)}, u32[]{:S(2)}) %collective-permute-start.49) | collective-permute-done | bytes 69664 | tf_op jit(solution)/shard_map/ppermute | solution.py:324
  148.2 2.1 collective-permute-done.50.refs_6_
  151.7 1.5 collective-permute-done.52.refs_8_
  156.0 1.5 collective-permute-done.56.refs_12_
  157.5 1.6 collective-permute-done.58.refs_14_
  159.1 6.4 %pairs.3 = (bf16[272,128]{1,0:T(8,128)(2,1)S(1)}, bf16[272,128]{1,0:T(8,128)(2,1)S(1)}, bf16[272,128]{1,0:T(8,128)(2,1)S(1)}, bf16[272,128]{1,0:T(8,128)(2,1)S(1...) custom-call(s32[128]{0:T(128)S(1)} %get-tuple-element.112.target_ref, ...), custom_call_target="tpu_custom_call" | custom-call | flops 1073741824 | bytes 8388608 | tf_op jit(solution)/shard_map/pairs/pallas_call | solution.py:384
  165.6 1.7 collective-permute-start.60
  167.3 2.3 %collective-permute-start.61 = (bf16[272,128]{1,0:T(8,128)(2,1)S(1)}, bf16[272,128]{1,0:T(8,128)(2,1)S(1)}, u32[]{:S(2)}, u32[]{:S(2)}) collective-permute-start(bf16[272,128]{1,0:T(8,128)(2,1)S(1)} %get-tuple-element.167), channel_id=1, source_target_pairs={{0,14},{1,15},{2,12},{3,13},{4,10},{5,11},{6,8},{7,9},{8,6},{9,7},... | collective-permute-start | bytes 208904 | tf_op jit(solution)/shard_map/ppermute | solution.py:324
  169.6 2.1 collective-permute-start.62
  171.7 1.9 collective-permute-start.63
  173.6 3.1 %collective-permute-start.65 = (bf16[272,128]{1,0:T(8,128)(2,1)S(1)}, bf16[272,128]{1,0:T(8,128)(2,1)S(1)}, u32[]{:S(2)}, u32[]{:S(2)}) collective-permute-start(bf16[272,128]{1,0:T(8,128)(2,1)S(1)} %get-tuple-element.171), channel_id=1, source_target_pairs={{0,10},{1,11},{2,8},{3,9},{4,14},{5,15},{6,12},{7,13},{8,2},{9,3},... | collective-permute-start | bytes 208904 | tf_op jit(solution)/shard_map/ppermute | solution.py:324
  176.7 5.7 %collective-permute-start.67 = (bf16[272,128]{1,0:T(8,128)(2,1)S(1)}, bf16[272,128]{1,0:T(8,128)(2,1)S(1)}, u32[]{:S(2)}, u32[]{:S(2)}) collective-permute-start(bf16[272,128]{1,0:T(8,128)(2,1)S(1)} %get-tuple-element.173), channel_id=1, source_target_pairs={{0,8},{1,9},{2,10},{3,11},{4,12},{5,13},{6,14},{7,15},{8,0},{9,1},... | collective-permute-start | bytes 208904 | tf_op jit(solution)/shard_map/ppermute | solution.py:324
  182.4 3.3 %collective-permute-start.68 = (bf16[272,128]{1,0:T(8,128)(2,1)S(1)}, bf16[272,128]{1,0:T(8,128)(2,1)S(1)}, u32[]{:S(2)}, u32[]{:S(2)}) collective-permute-start(bf16[272,128]{1,0:T(8,128)(2,1)S(1)} %get-tuple-element.174), channel_id=1, source_target_pairs={{0,7},{1,6},{2,5},{3,4},{4,3},{5,2},{6,1},{7,0},{8,15},{9,14},{10,... | collective-permute-start | bytes 208904 | tf_op jit(solution)/shard_map/ppermute | solution.py:324
  186.9 3.7 %collective-permute-done.65.refs_7_ = bf16[272,128]{1,0:T(8,128)(2,1)S(1)} collective-permute-done((bf16[272,128]{1,0:T(8,128)(2,1)S(1)}, bf16[272,128]{1,0:T(8,128)(2,1)S(1)}, u32[]{:S(2)}, u32[]{:S(2)}) %collective-permute-start.65) | collective-permute-done | bytes 69664 | tf_op jit(solution)/shard_map/ppermute | solution.py:324
  195.5 1.8 collective-permute-done.71.refs_13_
  198.3 2.7 %cells_last.1 = (f32[64,8192]{1,0:T(8,128)S(1)}, f32[64,128]{1,0:T(8,128)S(1)}, f32[16,16,128]{2,1,0:T(8,128)}) custom-call(s32[16,128]{1,0:T(8,128)S(1)} %get-tuple-element.111.refs_0_, bf16[272,128]{1,0:T(8,128)(2,1)S(1)} %get-tuple-element.165.refs_1_, bf16[272,128]{1,0:T(8,128)(2,1)S(1)} %collective-permute-done.60.refs_2_, ...), custom_call_target="tpu_custom_call" | custom-call | bytes 8388608 | tf_op jit(solution)/shard_map/cells_last/pallas_call | solution.py:398
  202.2 4.2 %all-to-all-start = ((f32[16,16,128]{2,1,0:T(8,128)}), f32[16,16,128]{2,1,0:T(8,128)S(1)}, u32[]{:S(2)}, u32[]{:S(2)}) async-start(f32[16,16,128]{2,1,0:T(8,128)} %get-tuple-element.184), calls=%async_computation | async-start | bytes 262144 | tf_op jit(solution)/shard_map/all_to_all | solution.py:409
  206.5 1.6 copy-done.3
  208.1 2.1 estimate.1
  210.1 4.3 %all-to-all-done.tails_ref = f32[16,16,128]{2,1,0:T(8,128)S(1)} async-done(((f32[16,16,128]{2,1,0:T(8,128)}), f32[16,16,128]{2,1,0:T(8,128)S(1)}, u32[]{:S(2)}, u32[]{:S(2)}) %all-to-all-start) | async-done | bytes 131104 | tf_op jit(solution)/shard_map/all_to_all | solution.py:409
  214.4 1.6 copy-done.5
  216.0 1.9 model.1
  (116 shorter events, 33.0 us)
Async XLA Ops:
  11.6 9.6 %collective-permute-start = (bf16[272,128]{1,0:T(8,128)(2,1)S(1)}, bf16[272,128]{1,0:T(8,128)(2,1)S(1)}, u32[]{:S(2)}, u32[]{:S(2)}) collective-permute-start(bf16[272,128]{1,0:T(8,128)(2,1)S(1)} %get-tuple-element.95), channel_id=1, source_target_pairs={{0,15},{1,14},{2,13},{3,12},{4,11},{5,10},{6,9},{7,8},{8,7},{9,6},... | collective-permute-start | bytes 208904 | tf_op jit(solution)/shard_map/ppermute | solution.py:324
  17.1 7.8 %collective-permute-start.1 = (bf16[272,128]{1,0:T(8,128)(2,1)S(1)}, bf16[272,128]{1,0:T(8,128)(2,1)S(1)}, u32[]{:S(2)}, u32[]{:S(2)}) collective-permute-start(bf16[272,128]{1,0:T(8,128)(2,1)S(1)} %get-tuple-element.96), channel_id=1, source_target_pairs={{0,14},{1,15},{2,12},{3,13},{4,10},{5,11},{6,8},{7,9},{8,6},{9,7},... | collective-permute-start | bytes 208904 | tf_op jit(solution)/shard_map/ppermute | solution.py:324
  17.7 7.5 %collective-permute-start.2 = (bf16[272,128]{1,0:T(8,128)(2,1)S(1)}, bf16[272,128]{1,0:T(8,128)(2,1)S(1)}, u32[]{:S(2)}, u32[]{:S(2)}) collective-permute-start(bf16[272,128]{1,0:T(8,128)(2,1)S(1)} %get-tuple-element.97), channel_id=1, source_target_pairs={{0,13},{1,12},{2,15},{3,14},{4,9},{5,8},{6,11},{7,10},{8,5},{9,4},... | collective-permute-start | bytes 208904 | tf_op jit(solution)/shard_map/ppermute | solution.py:324
  20.9 13.7 %collective-permute-start.3 = (bf16[272,128]{1,0:T(8,128)(2,1)S(1)}, bf16[272,128]{1,0:T(8,128)(2,1)S(1)}, u32[]{:S(2)}, u32[]{:S(2)}) collective-permute-start(bf16[272,128]{1,0:T(8,128)(2,1)S(1)} %get-tuple-element.98), channel_id=1, source_target_pairs={{0,12},{1,13},{2,14},{3,15},{4,8},{5,9},{6,10},{7,11},{8,4},{9,5},... | collective-permute-start | bytes 208904 | tf_op jit(solution)/shard_map/ppermute | solution.py:324
  21.2 16.0 %collective-permute-start.4 = (bf16[272,128]{1,0:T(8,128)(2,1)S(1)}, bf16[272,128]{1,0:T(8,128)(2,1)S(1)}, u32[]{:S(2)}, u32[]{:S(2)}) collective-permute-start(bf16[272,128]{1,0:T(8,128)(2,1)S(1)} %get-tuple-element.99), channel_id=1, source_target_pairs={{0,11},{1,10},{2,9},{3,8},{4,15},{5,14},{6,13},{7,12},{8,3},{9,2},... | collective-permute-start | bytes 208904 | tf_op jit(solution)/shard_map/ppermute | solution.py:324
  21.2 17.9 %collective-permute-start.5 = (bf16[272,128]{1,0:T(8,128)(2,1)S(1)}, bf16[272,128]{1,0:T(8,128)(2,1)S(1)}, u32[]{:S(2)}, u32[]{:S(2)}) collective-permute-start(bf16[272,128]{1,0:T(8,128)(2,1)S(1)} %get-tuple-element.100), channel_id=1, source_target_pairs={{0,10},{1,11},{2,8},{3,9},{4,14},{5,15},{6,12},{7,13},{8,2},{9,3},... | collective-permute-start | bytes 208904 | tf_op jit(solution)/shard_map/ppermute | solution.py:324
  25.0 15.6 %collective-permute-start.6 = (bf16[272,128]{1,0:T(8,128)(2,1)S(1)}, bf16[272,128]{1,0:T(8,128)(2,1)S(1)}, u32[]{:S(2)}, u32[]{:S(2)}) collective-permute-start(bf16[272,128]{1,0:T(8,128)(2,1)S(1)} %get-tuple-element.101), channel_id=1, source_target_pairs={{0,9},{1,8},{2,11},{3,10},{4,13},{5,12},{6,15},{7,14},{8,1},{9,0},... | collective-permute-start | bytes 208904 | tf_op jit(solution)/shard_map/ppermute | solution.py:324
  25.2 16.8 %collective-permute-start.7 = (bf16[272,128]{1,0:T(8,128)(2,1)S(1)}, bf16[272,128]{1,0:T(8,128)(2,1)S(1)}, u32[]{:S(2)}, u32[]{:S(2)}) collective-permute-start(bf16[272,128]{1,0:T(8,128)(2,1)S(1)} %get-tuple-element.102), channel_id=1, source_target_pairs={{0,8},{1,9},{2,10},{3,11},{4,12},{5,13},{6,14},{7,15},{8,0},{9,1},... | collective-permute-start | bytes 208904 | tf_op jit(solution)/shard_map/ppermute | solution.py:324
  34.6 8.8 %collective-permute-start.8 = (bf16[272,128]{1,0:T(8,128)(2,1)S(1)}, bf16[272,128]{1,0:T(8,128)(2,1)S(1)}, u32[]{:S(2)}, u32[]{:S(2)}) collective-permute-start(bf16[272,128]{1,0:T(8,128)(2,1)S(1)} %get-tuple-element.103), channel_id=1, source_target_pairs={{0,7},{1,6},{2,5},{3,4},{4,3},{5,2},{6,1},{7,0},{8,15},{9,14},{10,... | collective-permute-start | bytes 208904 | tf_op jit(solution)/shard_map/ppermute | solution.py:324
  37.2 7.6 %collective-permute-start.9 = (bf16[272,128]{1,0:T(8,128)(2,1)S(1)}, bf16[272,128]{1,0:T(8,128)(2,1)S(1)}, u32[]{:S(2)}, u32[]{:S(2)}) collective-permute-start(bf16[272,128]{1,0:T(8,128)(2,1)S(1)} %get-tuple-element.104), channel_id=1, source_target_pairs={{0,6},{1,7},{2,4},{3,5},{4,2},{5,3},{6,0},{7,1},{8,14},{9,15},{10,... | collective-permute-start | bytes 208904 | tf_op jit(solution)/shard_map/ppermute | solution.py:324
  39.2 6.3 %collective-permute-start.10 = (bf16[272,128]{1,0:T(8,128)(2,1)S(1)}, bf16[272,128]{1,0:T(8,128)(2,1)S(1)}, u32[]{:S(2)}, u32[]{:S(2)}) collective-permute-start(bf16[272,128]{1,0:T(8,128)(2,1)S(1)} %get-tuple-element.105), channel_id=1, source_target_pairs={{0,5},{1,4},{2,7},{3,6},{4,1},{5,0},{6,3},{7,2},{8,13},{9,12},{10,... | collective-permute-start | bytes 208904 | tf_op jit(solution)/shard_map/ppermute | solution.py:324
  40.5 6.8 %collective-permute-start.11 = (bf16[272,128]{1,0:T(8,128)(2,1)S(1)}, bf16[272,128]{1,0:T(8,128)(2,1)S(1)}, u32[]{:S(2)}, u32[]{:S(2)}) collective-permute-start(bf16[272,128]{1,0:T(8,128)(2,1)S(1)} %get-tuple-element.106), channel_id=1, source_target_pairs={{0,4},{1,5},{2,6},{3,7},{4,0},{5,1},{6,2},{7,3},{8,12},{9,13},{10,... | collective-permute-start | bytes 208904 | tf_op jit(solution)/shard_map/ppermute | solution.py:324
  42.0 5.3 %collective-permute-start.12 = (bf16[272,128]{1,0:T(8,128)(2,1)S(1)}, bf16[272,128]{1,0:T(8,128)(2,1)S(1)}, u32[]{:S(2)}, u32[]{:S(2)}) collective-permute-start(bf16[272,128]{1,0:T(8,128)(2,1)S(1)} %get-tuple-element.107), channel_id=1, source_target_pairs={{0,3},{1,2},{2,1},{3,0},{4,7},{5,6},{6,5},{7,4},{8,11},{9,10},{10,... | collective-permute-start | bytes 208904 | tf_op jit(solution)/shard_map/ppermute | solution.py:324
  50.7 8.1 %collective-permute-start.15 = (bf16[272,128]{1,0:T(8,128)(2,1)S(1)}, bf16[272,128]{1,0:T(8,128)(2,1)S(1)}, u32[]{:S(2)}, u32[]{:S(2)}) collective-permute-start(bf16[272,128]{1,0:T(8,128)(2,1)S(1)} %get-tuple-element.114), channel_id=1, source_target_pairs={{0,15},{1,14},{2,13},{3,12},{4,11},{5,10},{6,9},{7,8},{8,7},{9,6},... | collective-permute-start | bytes 208904 | tf_op jit(solution)/shard_map/ppermute | solution.py:324
  52.6 9.2 %collective-permute-start.16 = (bf16[272,128]{1,0:T(8,128)(2,1)S(1)}, bf16[272,128]{1,0:T(8,128)(2,1)S(1)}, u32[]{:S(2)}, u32[]{:S(2)}) collective-permute-start(bf16[272,128]{1,0:T(8,128)(2,1)S(1)} %get-tuple-element.115), channel_id=1, source_target_pairs={{0,14},{1,15},{2,12},{3,13},{4,10},{5,11},{6,8},{7,9},{8,6},{9,7},... | collective-permute-start | bytes 208904 | tf_op jit(solution)/shard_map/ppermute | solution.py:324
  54.7 11.3 %collective-permute-start.17 = (bf16[272,128]{1,0:T(8,128)(2,1)S(1)}, bf16[272,128]{1,0:T(8,128)(2,1)S(1)}, u32[]{:S(2)}, u32[]{:S(2)}) collective-permute-start(bf16[272,128]{1,0:T(8,128)(2,1)S(1)} %get-tuple-element.116), channel_id=1, source_target_pairs={{0,13},{1,12},{2,15},{3,14},{4,9},{5,8},{6,11},{7,10},{8,5},{9,4},... | collective-permute-start | bytes 208904 | tf_op jit(solution)/shard_map/ppermute | solution.py:324
  57.3 11.8 %collective-permute-start.18 = (bf16[272,128]{1,0:T(8,128)(2,1)S(1)}, bf16[272,128]{1,0:T(8,128)(2,1)S(1)}, u32[]{:S(2)}, u32[]{:S(2)}) collective-permute-start(bf16[272,128]{1,0:T(8,128)(2,1)S(1)} %get-tuple-element.117), channel_id=1, source_target_pairs={{0,12},{1,13},{2,14},{3,15},{4,8},{5,9},{6,10},{7,11},{8,4},{9,5},... | collective-permute-start | bytes 208904 | tf_op jit(solution)/shard_map/ppermute | solution.py:324
  58.8 13.5 %collective-permute-start.19 = (bf16[272,128]{1,0:T(8,128)(2,1)S(1)}, bf16[272,128]{1,0:T(8,128)(2,1)S(1)}, u32[]{:S(2)}, u32[]{:S(2)}) collective-permute-start(bf16[272,128]{1,0:T(8,128)(2,1)S(1)} %get-tuple-element.118), channel_id=1, source_target_pairs={{0,11},{1,10},{2,9},{3,8},{4,15},{5,14},{6,13},{7,12},{8,3},{9,2},... | collective-permute-start | bytes 208904 | tf_op jit(solution)/shard_map/ppermute | solution.py:324
  58.8 17.1 %collective-permute-start.20 = (bf16[272,128]{1,0:T(8,128)(2,1)S(1)}, bf16[272,128]{1,0:T(8,128)(2,1)S(1)}, u32[]{:S(2)}, u32[]{:S(2)}) collective-permute-start(bf16[272,128]{1,0:T(8,128)(2,1)S(1)} %get-tuple-element.119), channel_id=1, source_target_pairs={{0,10},{1,11},{2,8},{3,9},{4,14},{5,15},{6,12},{7,13},{8,2},{9,3},... | collective-permute-start | bytes 208904 | tf_op jit(solution)/shard_map/ppermute | solution.py:324
  61.8 15.0 %collective-permute-start.21 = (bf16[272,128]{1,0:T(8,128)(2,1)S(1)}, bf16[272,128]{1,0:T(8,128)(2,1)S(1)}, u32[]{:S(2)}, u32[]{:S(2)}) collective-permute-start(bf16[272,128]{1,0:T(8,128)(2,1)S(1)} %get-tuple-element.120), channel_id=1, source_target_pairs={{0,9},{1,8},{2,11},{3,10},{4,13},{5,12},{6,15},{7,14},{8,1},{9,0},... | collective-permute-start | bytes 208904 | tf_op jit(solution)/shard_map/ppermute | solution.py:324
  66.0 12.3 %collective-permute-start.22 = (bf16[272,128]{1,0:T(8,128)(2,1)S(1)}, bf16[272,128]{1,0:T(8,128)(2,1)S(1)}, u32[]{:S(2)}, u32[]{:S(2)}) collective-permute-start(bf16[272,128]{1,0:T(8,128)(2,1)S(1)} %get-tuple-element.121), channel_id=1, source_target_pairs={{0,8},{1,9},{2,10},{3,11},{4,12},{5,13},{6,14},{7,15},{8,0},{9,1},... | collective-permute-start | bytes 208904 | tf_op jit(solution)/shard_map/ppermute | solution.py:324
  69.2 9.6 %collective-permute-start.23 = (bf16[272,128]{1,0:T(8,128)(2,1)S(1)}, bf16[272,128]{1,0:T(8,128)(2,1)S(1)}, u32[]{:S(2)}, u32[]{:S(2)}) collective-permute-start(bf16[272,128]{1,0:T(8,128)(2,1)S(1)} %get-tuple-element.122), channel_id=1, source_target_pairs={{0,7},{1,6},{2,5},{3,4},{4,3},{5,2},{6,1},{7,0},{8,15},{9,14},{10,... | collective-permute-start | bytes 208904 | tf_op jit(solution)/shard_map/ppermute | solution.py:324
  72.2 8.6 %collective-permute-start.24 = (bf16[272,128]{1,0:T(8,128)(2,1)S(1)}, bf16[272,128]{1,0:T(8,128)(2,1)S(1)}, u32[]{:S(2)}, u32[]{:S(2)}) collective-permute-start(bf16[272,128]{1,0:T(8,128)(2,1)S(1)} %get-tuple-element.123), channel_id=1, source_target_pairs={{0,6},{1,7},{2,4},{3,5},{4,2},{5,3},{6,0},{7,1},{8,14},{9,15},{10,... | collective-permute-start | bytes 208904 | tf_op jit(solution)/shard_map/ppermute | solution.py:324
  75.9 5.8 %collective-permute-start.25 = (bf16[272,128]{1,0:T(8,128)(2,1)S(1)}, bf16[272,128]{1,0:T(8,128)(2,1)S(1)}, u32[]{:S(2)}, u32[]{:S(2)}) collective-permute-start(bf16[272,128]{1,0:T(8,128)(2,1)S(1)} %get-tuple-element.124), channel_id=1, source_target_pairs={{0,5},{1,4},{2,7},{3,6},{4,1},{5,0},{6,3},{7,2},{8,13},{9,12},{10,... | collective-permute-start | bytes 208904 | tf_op jit(solution)/shard_map/ppermute | solution.py:324
  76.8 6.7 %collective-permute-start.26 = (bf16[272,128]{1,0:T(8,128)(2,1)S(1)}, bf16[272,128]{1,0:T(8,128)(2,1)S(1)}, u32[]{:S(2)}, u32[]{:S(2)}) collective-permute-start(bf16[272,128]{1,0:T(8,128)(2,1)S(1)} %get-tuple-element.125), channel_id=1, source_target_pairs={{0,4},{1,5},{2,6},{3,7},{4,0},{5,1},{6,2},{7,3},{8,12},{9,13},{10,... | collective-permute-start | bytes 208904 | tf_op jit(solution)/shard_map/ppermute | solution.py:324
  78.3 5.2 %collective-permute-start.27 = (bf16[272,128]{1,0:T(8,128)(2,1)S(1)}, bf16[272,128]{1,0:T(8,128)(2,1)S(1)}, u32[]{:S(2)}, u32[]{:S(2)}) collective-permute-start(bf16[272,128]{1,0:T(8,128)(2,1)S(1)} %get-tuple-element.126), channel_id=1, source_target_pairs={{0,3},{1,2},{2,1},{3,0},{4,7},{5,6},{6,5},{7,4},{8,11},{9,10},{10,... | collective-permute-start | bytes 208904 | tf_op jit(solution)/shard_map/ppermute | solution.py:324
  78.8 5.5 %collective-permute-start.28 = (bf16[272,128]{1,0:T(8,128)(2,1)S(1)}, bf16[272,128]{1,0:T(8,128)(2,1)S(1)}, u32[]{:S(2)}, u32[]{:S(2)}) collective-permute-start(bf16[272,128]{1,0:T(8,128)(2,1)S(1)} %get-tuple-element.127), channel_id=1, source_target_pairs={{0,2},{1,3},{2,0},{3,1},{4,6},{5,7},{6,4},{7,5},{8,10},{9,11},{10,... | collective-permute-start | bytes 208904 | tf_op jit(solution)/shard_map/ppermute | solution.py:324
  90.2 8.1 %collective-permute-start.30 = (bf16[272,128]{1,0:T(8,128)(2,1)S(1)}, bf16[272,128]{1,0:T(8,128)(2,1)S(1)}, u32[]{:S(2)}, u32[]{:S(2)}) collective-permute-start(bf16[272,128]{1,0:T(8,128)(2,1)S(1)} %get-tuple-element.130), channel_id=1, source_target_pairs={{0,15},{1,14},{2,13},{3,12},{4,11},{5,10},{6,9},{7,8},{8,7},{9,6},... | collective-permute-start | bytes 208904 | tf_op jit(solution)/shard_map/ppermute | solution.py:324
  92.6 9.0 %collective-permute-start.31 = (bf16[272,128]{1,0:T(8,128)(2,1)S(1)}, bf16[272,128]{1,0:T(8,128)(2,1)S(1)}, u32[]{:S(2)}, u32[]{:S(2)}) collective-permute-start(bf16[272,128]{1,0:T(8,128)(2,1)S(1)} %get-tuple-element.131), channel_id=1, source_target_pairs={{0,14},{1,15},{2,12},{3,13},{4,10},{5,11},{6,8},{7,9},{8,6},{9,7},... | collective-permute-start | bytes 208904 | tf_op jit(solution)/shard_map/ppermute | solution.py:324
  94.6 7.1 %collective-permute-start.32 = (bf16[272,128]{1,0:T(8,128)(2,1)S(1)}, bf16[272,128]{1,0:T(8,128)(2,1)S(1)}, u32[]{:S(2)}, u32[]{:S(2)}) collective-permute-start(bf16[272,128]{1,0:T(8,128)(2,1)S(1)} %get-tuple-element.132), channel_id=1, source_target_pairs={{0,13},{1,12},{2,15},{3,14},{4,9},{5,8},{6,11},{7,10},{8,5},{9,4},... | collective-permute-start | bytes 208904 | tf_op jit(solution)/shard_map/ppermute | solution.py:324
  96.3 12.9 %collective-permute-start.33 = (bf16[272,128]{1,0:T(8,128)(2,1)S(1)}, bf16[272,128]{1,0:T(8,128)(2,1)S(1)}, u32[]{:S(2)}, u32[]{:S(2)}) collective-permute-start(bf16[272,128]{1,0:T(8,128)(2,1)S(1)} %get-tuple-element.133), channel_id=1, source_target_pairs={{0,12},{1,13},{2,14},{3,15},{4,8},{5,9},{6,10},{7,11},{8,4},{9,5},... | collective-permute-start | bytes 208904 | tf_op jit(solution)/shard_map/ppermute | solution.py:324
  98.3 13.6 %collective-permute-start.34 = (bf16[272,128]{1,0:T(8,128)(2,1)S(1)}, bf16[272,128]{1,0:T(8,128)(2,1)S(1)}, u32[]{:S(2)}, u32[]{:S(2)}) collective-permute-start(bf16[272,128]{1,0:T(8,128)(2,1)S(1)} %get-tuple-element.134), channel_id=1, source_target_pairs={{0,11},{1,10},{2,9},{3,8},{4,15},{5,14},{6,13},{7,12},{8,3},{9,2},... | collective-permute-start | bytes 208904 | tf_op jit(solution)/shard_map/ppermute | solution.py:324
  98.3 17.0 %collective-permute-start.35 = (bf16[272,128]{1,0:T(8,128)(2,1)S(1)}, bf16[272,128]{1,0:T(8,128)(2,1)S(1)}, u32[]{:S(2)}, u32[]{:S(2)}) collective-permute-start(bf16[272,128]{1,0:T(8,128)(2,1)S(1)} %get-tuple-element.135), channel_id=1, source_target_pairs={{0,10},{1,11},{2,8},{3,9},{4,14},{5,15},{6,12},{7,13},{8,2},{9,3},... | collective-permute-start | bytes 208904 | tf_op jit(solution)/shard_map/ppermute | solution.py:324
  101.7 13.8 %collective-permute-start.36 = (bf16[272,128]{1,0:T(8,128)(2,1)S(1)}, bf16[272,128]{1,0:T(8,128)(2,1)S(1)}, u32[]{:S(2)}, u32[]{:S(2)}) collective-permute-start(bf16[272,128]{1,0:T(8,128)(2,1)S(1)} %get-tuple-element.136), channel_id=1, source_target_pairs={{0,9},{1,8},{2,11},{3,10},{4,13},{5,12},{6,15},{7,14},{8,1},{9,0},... | collective-permute-start | bytes 208904 | tf_op jit(solution)/shard_map/ppermute | solution.py:324
  101.7 15.4 %collective-permute-start.37 = (bf16[272,128]{1,0:T(8,128)(2,1)S(1)}, bf16[272,128]{1,0:T(8,128)(2,1)S(1)}, u32[]{:S(2)}, u32[]{:S(2)}) collective-permute-start(bf16[272,128]{1,0:T(8,128)(2,1)S(1)} %get-tuple-element.137), channel_id=1, source_target_pairs={{0,8},{1,9},{2,10},{3,11},{4,12},{5,13},{6,14},{7,15},{8,0},{9,1},... | collective-permute-start | bytes 208904 | tf_op jit(solution)/shard_map/ppermute | solution.py:324
  109.2 9.0 %collective-permute-start.38 = (bf16[272,128]{1,0:T(8,128)(2,1)S(1)}, bf16[272,128]{1,0:T(8,128)(2,1)S(1)}, u32[]{:S(2)}, u32[]{:S(2)}) collective-permute-start(bf16[272,128]{1,0:T(8,128)(2,1)S(1)} %get-tuple-element.138), channel_id=1, source_target_pairs={{0,7},{1,6},{2,5},{3,4},{4,3},{5,2},{6,1},{7,0},{8,15},{9,14},{10,... | collective-permute-start | bytes 208904 | tf_op jit(solution)/shard_map/ppermute | solution.py:324
  111.8 8.3 %collective-permute-start.39 = (bf16[272,128]{1,0:T(8,128)(2,1)S(1)}, bf16[272,128]{1,0:T(8,128)(2,1)S(1)}, u32[]{:S(2)}, u32[]{:S(2)}) collective-permute-start(bf16[272,128]{1,0:T(8,128)(2,1)S(1)} %get-tuple-element.139), channel_id=1, source_target_pairs={{0,6},{1,7},{2,4},{3,5},{4,2},{5,3},{6,0},{7,1},{8,14},{9,15},{10,... | collective-permute-start | bytes 208904 | tf_op jit(solution)/shard_map/ppermute | solution.py:324
  115.5 6.1 %collective-permute-start.41 = (bf16[272,128]{1,0:T(8,128)(2,1)S(1)}, bf16[272,128]{1,0:T(8,128)(2,1)S(1)}, u32[]{:S(2)}, u32[]{:S(2)}) collective-permute-start(bf16[272,128]{1,0:T(8,128)(2,1)S(1)} %get-tuple-element.141), channel_id=1, source_target_pairs={{0,4},{1,5},{2,6},{3,7},{4,0},{5,1},{6,2},{7,3},{8,12},{9,13},{10,... | collective-permute-start | bytes 208904 | tf_op jit(solution)/shard_map/ppermute | solution.py:324
  125.3 8.1 %collective-permute-start.45 = (bf16[272,128]{1,0:T(8,128)(2,1)S(1)}, bf16[272,128]{1,0:T(8,128)(2,1)S(1)}, u32[]{:S(2)}, u32[]{:S(2)}) collective-permute-start(bf16[272,128]{1,0:T(8,128)(2,1)S(1)} %get-tuple-element.149), channel_id=1, source_target_pairs={{0,15},{1,14},{2,13},{3,12},{4,11},{5,10},{6,9},{7,8},{8,7},{9,6},... | collective-permute-start | bytes 208904 | tf_op jit(solution)/shard_map/ppermute | solution.py:324
  127.3 9.4 %collective-permute-start.46 = (bf16[272,128]{1,0:T(8,128)(2,1)S(1)}, bf16[272,128]{1,0:T(8,128)(2,1)S(1)}, u32[]{:S(2)}, u32[]{:S(2)}) collective-permute-start(bf16[272,128]{1,0:T(8,128)(2,1)S(1)} %get-tuple-element.150), channel_id=1, source_target_pairs={{0,14},{1,15},{2,12},{3,13},{4,10},{5,11},{6,8},{7,9},{8,6},{9,7},... | collective-permute-start | bytes 208904 | tf_op jit(solution)/shard_map/ppermute | solution.py:324
  129.7 9.1 %collective-permute-start.47 = (bf16[272,128]{1,0:T(8,128)(2,1)S(1)}, bf16[272,128]{1,0:T(8,128)(2,1)S(1)}, u32[]{:S(2)}, u32[]{:S(2)}) collective-permute-start(bf16[272,128]{1,0:T(8,128)(2,1)S(1)} %get-tuple-element.151), channel_id=1, source_target_pairs={{0,13},{1,12},{2,15},{3,14},{4,9},{5,8},{6,11},{7,10},{8,5},{9,4},... | collective-permute-start | bytes 208904 | tf_op jit(solution)/shard_map/ppermute | solution.py:324
  131.8 13.0 %collective-permute-start.48 = (bf16[272,128]{1,0:T(8,128)(2,1)S(1)}, bf16[272,128]{1,0:T(8,128)(2,1)S(1)}, u32[]{:S(2)}, u32[]{:S(2)}) collective-permute-start(bf16[272,128]{1,0:T(8,128)(2,1)S(1)} %get-tuple-element.152), channel_id=1, source_target_pairs={{0,12},{1,13},{2,14},{3,15},{4,8},{5,9},{6,10},{7,11},{8,4},{9,5},... | collective-permute-start | bytes 208904 | tf_op jit(solution)/shard_map/ppermute | solution.py:324
  133.4 14.8 %collective-permute-start.49 = (bf16[272,128]{1,0:T(8,128)(2,1)S(1)}, bf16[272,128]{1,0:T(8,128)(2,1)S(1)}, u32[]{:S(2)}, u32[]{:S(2)}) collective-permute-start(bf16[272,128]{1,0:T(8,128)(2,1)S(1)} %get-tuple-element.153), channel_id=1, source_target_pairs={{0,11},{1,10},{2,9},{3,8},{4,15},{5,14},{6,13},{7,12},{8,3},{9,2},... | collective-permute-start | bytes 208904 | tf_op jit(solution)/shard_map/ppermute | solution.py:324
  133.4 17.0 %collective-permute-start.50 = (bf16[272,128]{1,0:T(8,128)(2,1)S(1)}, bf16[272,128]{1,0:T(8,128)(2,1)S(1)}, u32[]{:S(2)}, u32[]{:S(2)}) collective-permute-start(bf16[272,128]{1,0:T(8,128)(2,1)S(1)} %get-tuple-element.154), channel_id=1, source_target_pairs={{0,10},{1,11},{2,8},{3,9},{4,14},{5,15},{6,12},{7,13},{8,2},{9,3},... | collective-permute-start | bytes 208904 | tf_op jit(solution)/shard_map/ppermute | solution.py:324
  136.8 14.9 %collective-permute-start.51 = (bf16[272,128]{1,0:T(8,128)(2,1)S(1)}, bf16[272,128]{1,0:T(8,128)(2,1)S(1)}, u32[]{:S(2)}, u32[]{:S(2)}) collective-permute-start(bf16[272,128]{1,0:T(8,128)(2,1)S(1)} %get-tuple-element.155), channel_id=1, source_target_pairs={{0,9},{1,8},{2,11},{3,10},{4,13},{5,12},{6,15},{7,14},{8,1},{9,0},... | collective-permute-start | bytes 208904 | tf_op jit(solution)/shard_map/ppermute | solution.py:324
  138.7 14.4 %collective-permute-start.52 = (bf16[272,128]{1,0:T(8,128)(2,1)S(1)}, bf16[272,128]{1,0:T(8,128)(2,1)S(1)}, u32[]{:S(2)}, u32[]{:S(2)}) collective-permute-start(bf16[272,128]{1,0:T(8,128)(2,1)S(1)} %get-tuple-element.156), channel_id=1, source_target_pairs={{0,8},{1,9},{2,10},{3,11},{4,12},{5,13},{6,14},{7,15},{8,0},{9,1},... | collective-permute-start | bytes 208904 | tf_op jit(solution)/shard_map/ppermute | solution.py:324
  144.9 9.6 %collective-permute-start.53 = (bf16[272,128]{1,0:T(8,128)(2,1)S(1)}, bf16[272,128]{1,0:T(8,128)(2,1)S(1)}, u32[]{:S(2)}, u32[]{:S(2)}) collective-permute-start(bf16[272,128]{1,0:T(8,128)(2,1)S(1)} %get-tuple-element.157), channel_id=1, source_target_pairs={{0,7},{1,6},{2,5},{3,4},{4,3},{5,2},{6,1},{7,0},{8,15},{9,14},{10,... | collective-permute-start | bytes 208904 | tf_op jit(solution)/shard_map/ppermute | solution.py:324
  148.2 7.7 %collective-permute-start.54 = (bf16[272,128]{1,0:T(8,128)(2,1)S(1)}, bf16[272,128]{1,0:T(8,128)(2,1)S(1)}, u32[]{:S(2)}, u32[]{:S(2)}) collective-permute-start(bf16[272,128]{1,0:T(8,128)(2,1)S(1)} %get-tuple-element.158), channel_id=1, source_target_pairs={{0,6},{1,7},{2,4},{3,5},{4,2},{5,3},{6,0},{7,1},{8,14},{9,15},{10,... | collective-permute-start | bytes 208904 | tf_op jit(solution)/shard_map/ppermute | solution.py:324
  150.3 5.7 %collective-permute-start.55 = (bf16[272,128]{1,0:T(8,128)(2,1)S(1)}, bf16[272,128]{1,0:T(8,128)(2,1)S(1)}, u32[]{:S(2)}, u32[]{:S(2)}) collective-permute-start(bf16[272,128]{1,0:T(8,128)(2,1)S(1)} %get-tuple-element.159), channel_id=1, source_target_pairs={{0,5},{1,4},{2,7},{3,6},{4,1},{5,0},{6,3},{7,2},{8,13},{9,12},{10,... | collective-permute-start | bytes 208904 | tf_op jit(solution)/shard_map/ppermute | solution.py:324
  151.7 5.9 %collective-permute-start.56 = (bf16[272,128]{1,0:T(8,128)(2,1)S(1)}, bf16[272,128]{1,0:T(8,128)(2,1)S(1)}, u32[]{:S(2)}, u32[]{:S(2)}) collective-permute-start(bf16[272,128]{1,0:T(8,128)(2,1)S(1)} %get-tuple-element.160), channel_id=1, source_target_pairs={{0,4},{1,5},{2,6},{3,7},{4,0},{5,1},{6,2},{7,3},{8,12},{9,13},{10,... | collective-permute-start | bytes 208904 | tf_op jit(solution)/shard_map/ppermute | solution.py:324
  165.6 8.0 %collective-permute-start.60 = (bf16[272,128]{1,0:T(8,128)(2,1)S(1)}, bf16[272,128]{1,0:T(8,128)(2,1)S(1)}, u32[]{:S(2)}, u32[]{:S(2)}) collective-permute-start(bf16[272,128]{1,0:T(8,128)(2,1)S(1)} %get-tuple-element.166), channel_id=1, source_target_pairs={{0,15},{1,14},{2,13},{3,12},{4,11},{5,10},{6,9},{7,8},{8,7},{9,6},... | collective-permute-start | bytes 208904 | tf_op jit(solution)/shard_map/ppermute | solution.py:324
  167.3 9.4 %collective-permute-start.61 = (bf16[272,128]{1,0:T(8,128)(2,1)S(1)}, bf16[272,128]{1,0:T(8,128)(2,1)S(1)}, u32[]{:S(2)}, u32[]{:S(2)}) collective-permute-start(bf16[272,128]{1,0:T(8,128)(2,1)S(1)} %get-tuple-element.167), channel_id=1, source_target_pairs={{0,14},{1,15},{2,12},{3,13},{4,10},{5,11},{6,8},{7,9},{8,6},{9,7},... | collective-permute-start | bytes 208904 | tf_op jit(solution)/shard_map/ppermute | solution.py:324
  169.6 7.1 %collective-permute-start.62 = (bf16[272,128]{1,0:T(8,128)(2,1)S(1)}, bf16[272,128]{1,0:T(8,128)(2,1)S(1)}, u32[]{:S(2)}, u32[]{:S(2)}) collective-permute-start(bf16[272,128]{1,0:T(8,128)(2,1)S(1)} %get-tuple-element.168), channel_id=1, source_target_pairs={{0,13},{1,12},{2,15},{3,14},{4,9},{5,8},{6,11},{7,10},{8,5},{9,4},... | collective-permute-start | bytes 208904 | tf_op jit(solution)/shard_map/ppermute | solution.py:324
  171.7 10.7 %collective-permute-start.63 = (bf16[272,128]{1,0:T(8,128)(2,1)S(1)}, bf16[272,128]{1,0:T(8,128)(2,1)S(1)}, u32[]{:S(2)}, u32[]{:S(2)}) collective-permute-start(bf16[272,128]{1,0:T(8,128)(2,1)S(1)} %get-tuple-element.169), channel_id=1, source_target_pairs={{0,12},{1,13},{2,14},{3,15},{4,8},{5,9},{6,10},{7,11},{8,4},{9,5},... | collective-permute-start | bytes 208904 | tf_op jit(solution)/shard_map/ppermute | solution.py:324
  173.5 13.3 %collective-permute-start.64 = (bf16[272,128]{1,0:T(8,128)(2,1)S(1)}, bf16[272,128]{1,0:T(8,128)(2,1)S(1)}, u32[]{:S(2)}, u32[]{:S(2)}) collective-permute-start(bf16[272,128]{1,0:T(8,128)(2,1)S(1)} %get-tuple-element.170), channel_id=1, source_target_pairs={{0,11},{1,10},{2,9},{3,8},{4,15},{5,14},{6,13},{7,12},{8,3},{9,2},... | collective-permute-start | bytes 208904 | tf_op jit(solution)/shard_map/ppermute | solution.py:324
  173.6 17.0 %collective-permute-start.65 = (bf16[272,128]{1,0:T(8,128)(2,1)S(1)}, bf16[272,128]{1,0:T(8,128)(2,1)S(1)}, u32[]{:S(2)}, u32[]{:S(2)}) collective-permute-start(bf16[272,128]{1,0:T(8,128)(2,1)S(1)} %get-tuple-element.171), channel_id=1, source_target_pairs={{0,10},{1,11},{2,8},{3,9},{4,14},{5,15},{6,12},{7,13},{8,2},{9,3},... | collective-permute-start | bytes 208904 | tf_op jit(solution)/shard_map/ppermute | solution.py:324
  176.7 13.9 %collective-permute-start.66 = (bf16[272,128]{1,0:T(8,128)(2,1)S(1)}, bf16[272,128]{1,0:T(8,128)(2,1)S(1)}, u32[]{:S(2)}, u32[]{:S(2)}) collective-permute-start(bf16[272,128]{1,0:T(8,128)(2,1)S(1)} %get-tuple-element.172), channel_id=1, source_target_pairs={{0,9},{1,8},{2,11},{3,10},{4,13},{5,12},{6,15},{7,14},{8,1},{9,0},... | collective-permute-start | bytes 208904 | tf_op jit(solution)/shard_map/ppermute | solution.py:324
  176.7 15.6 %collective-permute-start.67 = (bf16[272,128]{1,0:T(8,128)(2,1)S(1)}, bf16[272,128]{1,0:T(8,128)(2,1)S(1)}, u32[]{:S(2)}, u32[]{:S(2)}) collective-permute-start(bf16[272,128]{1,0:T(8,128)(2,1)S(1)} %get-tuple-element.173), channel_id=1, source_target_pairs={{0,8},{1,9},{2,10},{3,11},{4,12},{5,13},{6,14},{7,15},{8,0},{9,1},... | collective-permute-start | bytes 208904 | tf_op jit(solution)/shard_map/ppermute | solution.py:324
  182.4 10.8 %collective-permute-start.68 = (bf16[272,128]{1,0:T(8,128)(2,1)S(1)}, bf16[272,128]{1,0:T(8,128)(2,1)S(1)}, u32[]{:S(2)}, u32[]{:S(2)}) collective-permute-start(bf16[272,128]{1,0:T(8,128)(2,1)S(1)} %get-tuple-element.174), channel_id=1, source_target_pairs={{0,7},{1,6},{2,5},{3,4},{4,3},{5,2},{6,1},{7,0},{8,15},{9,14},{10,... | collective-permute-start | bytes 208904 | tf_op jit(solution)/shard_map/ppermute | solution.py:324
  186.9 7.9 %collective-permute-start.69 = (bf16[272,128]{1,0:T(8,128)(2,1)S(1)}, bf16[272,128]{1,0:T(8,128)(2,1)S(1)}, u32[]{:S(2)}, u32[]{:S(2)}) collective-permute-start(bf16[272,128]{1,0:T(8,128)(2,1)S(1)} %get-tuple-element.175), channel_id=1, source_target_pairs={{0,6},{1,7},{2,4},{3,5},{4,2},{5,3},{6,0},{7,1},{8,14},{9,15},{10,... | collective-permute-start | bytes 208904 | tf_op jit(solution)/shard_map/ppermute | solution.py:324
  190.6 6.7 %collective-permute-start.71 = (bf16[272,128]{1,0:T(8,128)(2,1)S(1)}, bf16[272,128]{1,0:T(8,128)(2,1)S(1)}, u32[]{:S(2)}, u32[]{:S(2)}) collective-permute-start(bf16[272,128]{1,0:T(8,128)(2,1)S(1)} %get-tuple-element.177), channel_id=1, source_target_pairs={{0,4},{1,5},{2,6},{3,7},{4,0},{5,1},{6,2},{7,3},{8,12},{9,13},{10,... | collective-permute-start | bytes 208904 | tf_op jit(solution)/shard_map/ppermute | solution.py:324
  192.3 5.0 %collective-permute-start.72 = (bf16[272,128]{1,0:T(8,128)(2,1)S(1)}, bf16[272,128]{1,0:T(8,128)(2,1)S(1)}, u32[]{:S(2)}, u32[]{:S(2)}) collective-permute-start(bf16[272,128]{1,0:T(8,128)(2,1)S(1)} %get-tuple-element.178), channel_id=1, source_target_pairs={{0,3},{1,2},{2,1},{3,0},{4,7},{5,6},{6,5},{7,4},{8,11},{9,10},{10,... | collective-permute-start | bytes 208904 | tf_op jit(solution)/shard_map/ppermute | solution.py:324
  193.2 5.0 %collective-permute-start.73 = (bf16[272,128]{1,0:T(8,128)(2,1)S(1)}, bf16[272,128]{1,0:T(8,128)(2,1)S(1)}, u32[]{:S(2)}, u32[]{:S(2)}) collective-permute-start(bf16[272,128]{1,0:T(8,128)(2,1)S(1)} %get-tuple-element.179), channel_id=1, source_target_pairs={{0,2},{1,3},{2,0},{3,1},{4,6},{5,7},{6,4},{7,5},{8,10},{9,11},{10,... | collective-permute-start | bytes 208904 | tf_op jit(solution)/shard_map/ppermute | solution.py:324
  202.2 12.1 %all-to-all-start = ((f32[16,16,128]{2,1,0:T(8,128)}), f32[16,16,128]{2,1,0:T(8,128)S(1)}, u32[]{:S(2)}, u32[]{:S(2)}) async-start(f32[16,16,128]{2,1,0:T(8,128)} %get-tuple-element.184), calls=%async_computation | async-start | bytes 262144 | tf_op jit(solution)/shard_map/all_to_all | solution.py:409
  (22 other events, 289.3 us)

commit v5 on v1

--- a/solution.py
+++ b/solution.py
@@ -17,6 +17,8 @@
 BF16 = jnp.bfloat16
 VMEM = pltpu.VMEM
 SMEM = pltpu.SMEM
+HBM = pltpu.HBM
+CHUNKS = 8
 
 
 def diagonal(cols):
@@ -24,14 +26,14 @@
     return lax.broadcasted_iota(jnp.int32, shape, 0) == lax.broadcasted_iota(jnp.int32, shape, 1)
 
 
-def squares_tail(squares):
+def squares_tail(squares, rows=TAIL):
     cols = squares.shape[0]
     total = jnp.sum(squares, axis=1, keepdims=True)
     row = jnp.sum(jnp.where(diagonal(cols), total, 0.0), axis=0, keepdims=True)
     high = row.astype(BF16).astype(F32)
     middle = (row - high).astype(BF16).astype(F32)
     low = row - high - middle
-    place = lax.broadcasted_iota(jnp.int32, (TAIL, BS), 0)
+    place = lax.broadcasted_iota(jnp.int32, (rows, BS), 0)
     return jnp.where(
         place == 0, high, jnp.where(place == 1, middle, jnp.where(place == 2, low, 0.0))
     )
@@ -49,7 +51,7 @@
     return pl.ds(pl.multiple_of(block * BS, BS), BS)
 
 
-def transposed(data_ref, rays_ref, target_ref, total_ref, message_ref):
+def transposed(data_ref, rays_ref, ready, target_ref, total_ref, message_ref):
     pair_count, slot_count = rays_ref.shape[:2]
     cols = data_ref.shape[0]
     peers = message_ref.shape[0]
@@ -62,16 +64,21 @@
     lax.fori_loop(0, spots, clear, 0, unroll=8)
 
     def one_pair(pair, carry):
-        data = data_ref[:, lanes(pair)].astype(BF16)
+        ready(pair)
+        data = data_ref[:, lanes(pair)]
+        high = data.astype(BF16)
+        low = (data - high.astype(F32)).astype(BF16)
+        pieces = jnp.concatenate([high, low], axis=0)
         for slot in range(0, slot_count, 2):
             rays = jnp.concatenate([rays_ref[pair, slot], rays_ref[pair, slot + 1]], axis=1)
-            part = jnp.dot(data, rays, preferred_element_type=F32)
+            part = jnp.dot(pieces, rays, preferred_element_type=F32)
+            part = part[:cols] + part[cols:]
             for half in range(2):
                 spot = target_ref[pair * slot_count + slot + half]
                 total_ref[spot] += part[:, half * BS : (half + 1) * BS]
         return carry
 
-    lax.fori_loop(0, pair_count, one_pair, 0)
+    lax.fori_loop(0, pair_count, one_pair, 0, unroll=2)
 
     def pack(peer, carry):
         for rank in range(BCAP):
@@ -84,12 +91,30 @@
 
 
 def start_kernel(
-    cells_ref, counts_ref, times_ref, rays_ref, message_ref, target_ref, total_ref, table_ref, used_ref
+    cells_hbm, counts_hbm, times_hbm, rays_hbm, message_ref, target_ref,
+    total_ref, table_ref, used_ref, cells_ref, counts_ref, times_ref, rays_ref, sems, ray_sems,
 ):
     pair_count, slot_count = rays_ref.shape[:2]
     peers = message_ref.shape[0]
     cols = times_ref.shape[0]
     owned = CELL_DEV // BS
+    copies = [
+        pltpu.make_async_copy(source, dest, sems.at[index])
+        for index, (source, dest) in enumerate(
+            [(cells_hbm, cells_ref), (counts_hbm, counts_ref), (times_hbm, times_ref)]
+        )
+    ]
+    for copy in copies:
+        copy.start()
+
+    def ray_copy(pair):
+        return pltpu.make_async_copy(rays_hbm.at[pair], rays_ref.at[pair], ray_sems.at[pair])
+
+    def fetch(pair, carry):
+        ray_copy(pair).start()
+        return carry
+
+    lax.fori_loop(0, pair_count, fetch, 0)
 
     def clear(peer, carry):
         used_ref[peer] = 0
@@ -98,6 +123,8 @@
         return carry
 
     lax.fori_loop(0, peers, clear, 0)
+    copies[0].wait()
+    copies[1].wait()
 
     def one_pair(pair, carry):
         count = counts_ref[pair]
@@ -117,7 +144,10 @@
         return carry
 
     lax.fori_loop(0, pair_count, one_pair, 0)
-    transposed(times_ref, rays_ref, target_ref, total_ref, message_ref)
+    copies[2].wait()
+    transposed(
+        times_ref, rays_ref, lambda pair: ray_copy(pair).wait(), target_ref, total_ref, message_ref
+    )
     squares = jnp.zeros((cols, BS), F32)
     for pair in range(pair_count):
         part = times_ref[:, pair * BS : (pair + 1) * BS]
@@ -138,38 +168,34 @@
 
 
 def pair_kernel(
-    target_ref, fetched_ref, data_ref, beta_ref, rays_ref,
+    target_ref, source_ref, fetched_ref, data_ref, rays_ref,
     message_ref, raw_ref, alpha_ref, total_ref,
 ):
     pair_count, slot_count = rays_ref.shape[:2]
     peers = message_ref.shape[0]
     cols = data_ref.shape[0]
-    spots = peers * BCAP
     alpha = norm_of_tails(fetched_ref, cols)
     alpha_ref[...] = alpha
     model_scale = 1.0 / alpha
-    data_scale = alpha / beta_ref[...]
 
     def one_pair(pair, squares):
         chosen = []
         for slot in range(slot_count):
-            spot = target_ref[pair * slot_count + slot]
-            live = spot < spots
-            spot = jnp.where(live, spot, 0)
-            rows = pl.ds(pl.multiple_of((spot % BCAP) * cols, cols), cols)
-            block = fetched_ref[spot // BCAP, rows, :]
-            chosen.append(jnp.where(live, block, jnp.zeros_like(block)))
+            index = pair * slot_count + slot
+            rows = pl.ds(pl.multiple_of(source_ref[1, index], cols), cols)
+            block = fetched_ref[source_ref[0, index], rows, :]
+            chosen.append(jnp.where(source_ref[2, index] != 0, block, jnp.zeros_like(block)))
         rays = jnp.concatenate([rays_ref[pair, slot] for slot in range(slot_count)], axis=1)
         product = lax.dot_general(
-            jnp.concatenate(chosen, axis=1), rays, (((1,), (1,)), ((), ())),
+            rays, jnp.concatenate(chosen, axis=1), (((1,), (1,)), ((), ())),
             preferred_element_type=F32,
         )
-        raw = product * model_scale - data_ref[:, lanes(pair)] * data_scale
+        raw = product.T * model_scale - data_ref[:, lanes(pair)] * alpha
         raw_ref[:, lanes(pair)] = raw
         return squares + raw * raw
 
-    squares = lax.fori_loop(0, pair_count, one_pair, jnp.zeros((cols, BS), F32))
-    transposed(raw_ref, rays_ref, target_ref, total_ref, message_ref)
+    squares = lax.fori_loop(0, pair_count, one_pair, jnp.zeros((cols, BS), F32), unroll=2)
+    transposed(raw_ref, rays_ref, lambda pair: None, target_ref, total_ref, message_ref)
     tail = squares_tail(squares).astype(BF16)
     message_ref[:, BCAP * cols :, :] = jnp.broadcast_to(tail[None], (peers, TAIL, BS))
 
@@ -177,8 +203,10 @@
 def cell_kernel(first, last, *refs):
     if first:
         arrived_ref, raw_ref, beta_ref, out_ref, asked_ref, table_ref, sem = refs
+    elif last:
+        asked_ref, arrived_ref, model_ref, raw_hbm, beta_ref, out_ref, raw_ref, sems = refs
     else:
-        asked_ref, arrived_ref, model_ref, alpha_ref, raw_ref, beta_ref, out_ref = refs
+        asked_ref, arrived_ref, model_ref, raw_ref, beta_ref, out_ref = refs
     peers = arrived_ref.shape[0]
     cols, cells = raw_ref.shape
     if first:
@@ -199,30 +227,41 @@
 
     lax.fori_loop(0, peers, add, 0, unroll=2)
     scale = 1.0 / beta
-    if not first:
-        model_scale = beta / alpha_ref[...]
 
     def settle(block, squares):
         raw = raw_ref[:, lanes(block)] * scale
         if not first:
-            raw = raw - model_ref[:, lanes(block)] * model_scale
+            raw = raw - model_ref[:, lanes(block)] * beta
         raw_ref[:, lanes(block)] = raw
         return squares + raw * raw
 
-    squares = lax.fori_loop(0, cells // BS, settle, jnp.zeros((cols, BS), F32), unroll=4)
-    tail = squares_tail(squares)
-    if last:
-        out_ref[...] = jnp.broadcast_to(tail[None], out_ref.shape).astype(out_ref.dtype)
+    squares = jnp.zeros((cols, BS), F32)
+    blocks = cells // BS
+    if not last:
+        squares = lax.fori_loop(0, blocks, settle, squares, unroll=4)
+        tail = squares_tail(squares)
+        out_ref[:, BCAP * cols :, :] = jnp.broadcast_to(tail[None], (peers, TAIL, BS)).astype(BF16)
+
+        def reply(peer, carry):
+            for rank in range(BCAP):
+                block = raw_ref[:, lanes(asked_ref[peer, rank])]
+                out_ref[peer, rank * cols : (rank + 1) * cols, :] = block.astype(BF16)
+            return carry
+
+        lax.fori_loop(0, peers, reply, 0, unroll=2)
         return
-    out_ref[:, BCAP * cols :, :] = jnp.broadcast_to(tail[None], (peers, TAIL, BS)).astype(BF16)
-
-    def reply(peer, carry):
-        for rank in range(BCAP):
-            block = raw_ref[:, lanes(asked_ref[peer, rank])]
-            out_ref[peer, rank * cols : (rank + 1) * cols, :] = block.astype(BF16)
-        return carry
-
-    lax.fori_loop(0, peers, reply, 0, unroll=2)
+    copies = []
+    for chunk in range(CHUNKS):
+        each = blocks // CHUNKS
+        squares = lax.fori_loop(chunk * each, (chunk + 1) * each, settle, squares, unroll=4)
+        where = slice(chunk * each * BS, (chunk + 1) * each * BS)
+        copies.append(
+            pltpu.make_async_copy(raw_ref.at[:, where], raw_hbm.at[:, where], sems.at[chunk])
+        )
+        copies[-1].start()
+    out_ref[...] = jnp.broadcast_to(squares_tail(squares, out_ref.shape[1])[None], out_ref.shape)
+    for copy in copies:
+        copy.wait()
 
 
 def estimate_kernel(*refs):
@@ -233,7 +272,7 @@
     cols, cells = estimate_ref.shape
     phi_bar = betas[0][...]
     rho_bar = alphas[0][...]
-    trace = [1.0 / alphas[0][...]]
+    trace = [jnp.ones((cols, BS), F32)]
     weight = [jnp.zeros((cols, BS), F32)] * ITERS
     for step in range(ITERS):
         beta = betas[step + 1][...]
@@ -249,7 +288,7 @@
             theta = sine * alpha
             rho_bar = -cosine * alpha
             phi_bar = sine * phi_bar
-            trace = [-(theta / rho) * value for value in trace] + [1.0 / alpha]
+            trace = [-(theta / rho) * value for value in trace] + [jnp.ones((cols, BS), F32)]
 
     def one_block(block, carry):
         where = lanes(block)
@@ -262,21 +301,37 @@
     lax.fori_loop(0, cells // BS, one_block, 0, unroll=4)
 
 
-def model_kernel(tails_ref, raw_ref, model_ref):
+def model_kernel(tails_ref, raw_hbm, model_hbm, raw_ref, in_sems, out_sems):
     cols, cells = raw_ref.shape
+    blocks = cells // BS // CHUNKS
+    ins, outs = [], []
+    for chunk in range(CHUNKS):
+        where = slice(chunk * blocks * BS, (chunk + 1) * blocks * BS)
+        ins.append(
+            pltpu.make_async_copy(raw_hbm.at[:, where], raw_ref.at[:, where], in_sems.at[chunk])
+        )
+        outs.append(
+            pltpu.make_async_copy(raw_ref.at[:, where], model_hbm.at[:, where], out_sems.at[chunk])
+        )
+        ins[-1].start()
     summed = jnp.sum(tails_ref[...], axis=0)
     row = summed[0:1] + summed[1:2] + summed[2:3]
     column = jnp.sum(jnp.where(diagonal(cols), row, 0.0), axis=1, keepdims=True)
     scale = jnp.broadcast_to(1.0 / jnp.sqrt(column + EPS), (cols, BS))
 
     def one_block(block, carry):
-        model_ref[:, lanes(block)] = raw_ref[:, lanes(block)] * scale
-        return carry
-
-    lax.fori_loop(0, cells // BS, one_block, 0, unroll=4)
-
-
-def call(kernel, name, in_spaces, outs, scratch=(), flops=0, moved=0):
+        raw_ref[:, lanes(block)] *= scale
+        return carry
+
+    for chunk in range(CHUNKS):
+        ins[chunk].wait()
+        lax.fori_loop(chunk * blocks, (chunk + 1) * blocks, one_block, 0, unroll=4)
+        outs[chunk].start()
+    for copy in outs:
+        copy.wait()
+
+
+def call(kernel, name, in_spaces, outs, scratch=(), flops=0, moved=0, limit=16 << 20):
     return pl.pallas_call(
         kernel,
         name=name,
@@ -284,7 +339,7 @@
         out_specs=[pl.BlockSpec(memory_space=space) for _, _, space in outs],
         out_shape=[jax.ShapeDtypeStruct(shape, dtype) for shape, dtype, _ in outs],
         scratch_shapes=list(scratch),
-        compiler_params=pltpu.CompilerParams(vmem_limit_bytes=24 * 1024 * 1024),
+        compiler_params=pltpu.CompilerParams(vmem_limit_bytes=limit),
         cost_estimate=pl.CostEstimate(flops=flops, bytes_accessed=moved, transcendentals=0),
     )
 
@@ -307,43 +362,58 @@
         return lax.all_to_all(values, "pair", split_axis=0, concat_axis=0, tiled=True)
 
     outgoing, target = call(
-        start_kernel, "start", [SMEM, SMEM, VMEM, VMEM],
+        start_kernel, "start", [HBM, HBM, HBM, HBM],
         [message, ((slots,), jnp.int32, SMEM)],
-        [totals, SMEM((spots,), jnp.int32), SMEM((peers,), jnp.int32)],
-        flops, 6 << 20,
+        [
+            totals, SMEM((spots,), jnp.int32), SMEM((peers,), jnp.int32),
+            SMEM(block_cells.shape, jnp.int32), SMEM(block_counts.shape, jnp.int32),
+            VMEM(times.shape, F32), VMEM(ray_blocks.shape, BF16),
+            pltpu.SemaphoreType.DMA((3,)), pltpu.SemaphoreType.DMA((pair_count,)),
+        ],
+        flops, 6 << 20, 60 << 20,
     )(block_cells, block_counts, times, ray_blocks)
     arrived = exchange(outgoing)
+    within = jnp.minimum(target, spots - 1)
+    source = jnp.stack(
+        [within // BCAP, within % BCAP * cols, (target < spots).astype(jnp.int32)]
+    )
     raw, beta, reply, asked = call(
         functools.partial(cell_kernel, True, False), "cells_first", [VMEM],
         [model, tile, message, ((peers, BS), jnp.int32, SMEM)],
         [VMEM((peers, BS), jnp.int32), pltpu.SemaphoreType.DMA],
         0, 6 << 20,
     )(arrived)
-    models, betas, alphas = [raw], [beta], []
+    models, betas, alphas = [], [beta], []
     current = times
     for step in range(ITERS):
         fetched = exchange(reply)
-        outgoing, current, alpha = call(
-            pair_kernel, "pairs", [SMEM, VMEM, VMEM, VMEM, VMEM],
+        current = current / betas[-1][:, :1]
+        outgoing, data_raw, alpha = call(
+            pair_kernel, "pairs", [SMEM, SMEM, VMEM, VMEM, VMEM],
             [message, data, tile], [totals], 2 * flops, 8 << 20,
-        )(target, fetched, current, betas[-1], ray_blocks)
+        )(target, source, fetched, current, ray_blocks)
+        current = data_raw
         alphas.append(alpha)
         arrived = exchange(outgoing)
+        models.append(raw / alpha[:, :1])
         last = step + 1 == ITERS
-        out = ((peers, TAIL, BS), F32, VMEM) if last else message
         raw, beta, reply = call(
             functools.partial(cell_kernel, False, last), "cells_last" if last else "cells",
-            [SMEM, VMEM, VMEM, VMEM], [model, tile, out], (), 0, 8 << 20,
-        )(asked, arrived, models[-1], alpha)
+            [SMEM, VMEM, VMEM],
+            [((cols, CELL_DEV), F32, HBM), tile, ((peers, 8, BS), F32, VMEM)]
+            if last else [model, tile, message],
+            [VMEM((cols, CELL_DEV), F32), pltpu.SemaphoreType.DMA((CHUNKS,))] if last else (),
+            0, 8 << 20,
+        )(asked, arrived, models[-1])
         betas.append(beta)
-        models.append(raw)
     tails = exchange(reply)
     (estimate,) = call(
         estimate_kernel, "estimate", [VMEM] * (3 * ITERS + 1), [model], (), 0, 6 << 20
-    )(*betas, *alphas, *models[:ITERS])
-    (model_vec,) = call(model_kernel, "model", [VMEM, VMEM], [model], (), 0, 4 << 20)(
-        tails, models[-1]
-    )
+    )(*betas, *alphas, *models)
+    (model_vec,) = call(
+        model_kernel, "model", [VMEM, HBM], [((cols, CELL_DEV), F32, HBM)],
+        [VMEM((cols, CELL_DEV), F32)] + [pltpu.SemaphoreType.DMA((CHUNKS,))] * 2, 0, 4 << 20,
+    )(tails, raw)
     return (estimate.T, model_vec.T)
 
 

time: 209 us -> 216 us (1.033)
  blocking collectives: 161 us -> 35.9 us
  waiting for transfers between devices: 4.22 us -> 92.6 us
  starting transfers between devices: 3.51 us -> 32.5 us
  local copies, waits for them, and re-layouts: 8.99 us -> 17.8 us
  other arithmetic: 0 us -> 6.13 us
    all_to_all x5 -> x1, blocking collectives: 161 us -> 35.9 us  [exchange(): lax.all_to_all(values, 'pair', split_axis=0, concat_axis=0, tiled=True)]
    all_to_all x1 -> x5, waiting for transfers between devices: 4.22 us -> 92.6 us  [exchange(): lax.all_to_all(values, 'pair', split_axis=0, concat_axis=0, tiled=True)]
    all_to_all x1 -> x5, starting transfers between devices: 3.51 us -> 32.5 us  [exchange(): lax.all_to_all(values, 'pair', split_axis=0, concat_axis=0, tiled=True)]
    unnamed x18 -> x36, local copies, waits for them, and re-layouts: 8.99 us -> 17.4 us
    div x0 -> x4, other arithmetic: none -> 6.1 us  [the longest x2 4.96 us: on_device(): models.append(raw / alpha[:, :1])]
  transfers between devices with their start and end apart: 1 -> 5, of which waited for: 1 -> 5; matrix products, arithmetic and copies ran while one was open for 0% -> 3% of each run, Pallas kernels for 1% -> 1%
where the time goes in v5:
time: 216 us; the launch traced here: 215 us
  waiting for transfers between devices  92.6 us (43%)
  blocking collectives  35.9 us (17%)
  starting transfers between devices  32.5 us (15%)
  Pallas kernels  29.6 us (14%)
  local copies, waits for them, and re-layouts  17.8 us (8%)
  other arithmetic  6.13 us (3%)
    all_to_all x5, waiting for transfers between devices, exchange(): lax.all_to_all(values, 'pair', split_axis=0, concat_axis=0, tiled=True)  92.6 us
    all_to_all x1, blocking collectives, exchange(): lax.all_to_all(values, 'pair', split_axis=0, concat_axis=0, tiled=True)  35.9 us
    all_to_all x5, starting transfers between devices, exchange(): lax.all_to_all(values, 'pair', split_axis=0, concat_axis=0, tiled=True)  32.5 us
    unnamed x36, local copies, waits for them, and re-layouts  17.4 us
    pallas_call x2, Pallas kernels, on_device(): call(pair_kernel, 'pairs', [SMEM, SMEM, VMEM, VMEM, VMEM], [message, data...  10.3 us
    pallas_call x1, Pallas kernels, on_device(): call(start_kernel, 'start', [HBM, HBM, HBM, HBM], [message, ((slots,), jn...  6.91 us
    pallas_call x2, Pallas kernels, on_device(): call(functools.partial(cell_kernel, False, last), 'cells_last' if last el...  5.32 us
    div x2, other arithmetic, on_device(): models.append(raw / alpha[:, :1])  4.96 us
  transfers between devices with their start and end apart: 5, of which 5 were waited for; matrix products, arithmetic and copies ran while one was open for 3% of the time, Pallas kernels for 1%

profile of v5, /device:TPU:0, one launch (start us, length us, event | category | flops | bytes accessed | tf_op | source)
XLA Modules:
  0.0 215.3 jit_solution(2533173399427903548)
XLA Ops:
  0.6 6.9 %start.1 = (bf16[16,272,128]{2,1,0:T(8,128)(2,1)}, s32[128]{0:T(128)}) custom-call(s32[8,16]{1,0:T(8,128)} %cells_hbm.1, s32[8]{0:T(128)} %counts_hbm.1, f32[64,1024]{1,0:T(8,128)} %bitcast.12, bf16[8,16,128,128]{3,2,1,0:T(8,128)(2,1)} %rays_ref.3), custom_call_target="tpu_custom_call" | custom-call | flops 268435456 | bytes 6291456 | tf_op jit(solution)/shard_map/start/pallas_call | solution.py:364
  7.5 35.9 %all_to_all.30.refs_0_ = bf16[16,272,128]{2,1,0:T(8,128)(2,1)S(1)} all-to-all(bf16[16,272,128]{2,1,0:T(8,128)(2,1)} %get-tuple-element.19), channel_id=1, replica_groups=mesh['groups'=2,'pair'=16] {'pair'}, dimensions={0} | all-to-all | bytes 2228224 | tf_op jit(solution)/shard_map/all_to_all | solution.py:362
  43.5 0.0 copy-start.16
  43.5 0.0 copy-start.17
  43.5 3.2 %cells_first.1 = (f32[64,8192]{1,0:T(8,128)S(1)}, f32[64,128]{1,0:T(8,128)S(1)}, bf16[16,272,128]{2,1,0:T(8,128)(2,1)}, s32[16,128]{1,0:T(8,128)S(1)}) custom-call(bf16[16,272,128]{2,1,0:T(8,128)(2,1)S(1)} %all_to_all.30.refs_0_), custom_call_target="tpu_custom_call" | custom-call | bytes 6291456 | tf_op jit(solution)/shard_map/cells_first/pallas_call | solution.py:380
  46.7 0.0 copy-start.4
  46.7 1.3 copy-done.4
  48.0 3.7 %all-to-all-start.1 = ((bf16[16,272,128]{2,1,0:T(8,128)(2,1)}), bf16[16,272,128]{2,1,0:T(8,128)(2,1)S(1)}, u32[]{:S(2)}, u32[]{:S(2)}) async-start(bf16[16,272,128]{2,1,0:T(8,128)(2,1)} %get-tuple-element.23), calls=%async_computation.1 | async-start | bytes 2228224 | tf_op jit(solution)/shard_map/all_to_all | solution.py:362
  51.7 0.0 copy-done.16
  51.8 0.1 slice_reduce_fusion.3
  51.9 0.0 copy-done.17
  51.9 0.1 broadcast_divide_fusion.3.data_ref
  52.0 23.7 %all-to-all-done.1.fetched_ref = bf16[16,272,128]{2,1,0:T(8,128)(2,1)S(1)} async-done(((bf16[16,272,128]{2,1,0:T(8,128)(2,1)}), bf16[16,272,128]{2,1,0:T(8,128)(2,1)S(1)}, u32[]{:S(2)}, u32[]{:S(2)}) %all-to-all-start.1) | async-done | bytes 1114144 | tf_op jit(solution)/shard_map/all_to_all | solution.py:362
  75.7 0.0 copy-start
  75.7 2.2 %copy-done = bf16[8,16,128,128]{3,2,1,0:T(8,128)(2,1)S(1)} copy-done((bf16[8,16,128,128]{3,2,1,0:T(8,128)(2,1)S(1)}, bf16[8,16,128,128]{3,2,1,0:T(8,128)(2,1)}, u32[]{:S(2)}) %copy-start) | copy-done | bytes 4194328
  77.9 4.8 %pairs.2 = (bf16[16,272,128]{2,1,0:T(8,128)(2,1)S(1)}, f32[64,1024]{1,0:T(8,128)S(1)}, f32[64,128]{1,0:T(8,128)S(1)}) custom-call(s32[128]{0:T(128)S(1)} %copy-done.16, s32[3,128]{1,0:T(4,128)S(1)} %pad_add_fusion.source_ref, bf16[16,272,128]{2,1,0:T(8,128)(2,1)S(1)} %all-to-all-done.1.fetched_ref, f32[64,1024]{1,0:T(8,128)S(1)} %broadcast_divide_fusion.3.data_ref, ...), custom_call_target="tpu_custom_call" | custom-call | flops 536870912 | bytes 8388608 | tf_op jit(solution)/shard_map/pairs/pallas_call | solution.py:391
  82.7 0.0 copy-start.9
  82.7 1.0 copy-done.9
  83.7 0.0 copy-start.11
  83.7 0.7 copy-done.11
  84.4 7.1 %all-to-all-start.2 = ((bf16[16,272,128]{2,1,0:T(8,128)(2,1)}), bf16[16,272,128]{2,1,0:T(8,128)(2,1)S(1)}, u32[]{:S(2)}, u32[]{:S(2)}) async-start(bf16[16,272,128]{2,1,0:T(8,128)(2,1)} %copy-done.9), calls=%async_computation.2 | async-start | bytes 2228224 | tf_op jit(solution)/shard_map/all_to_all | solution.py:362
  91.5 0.1 slice_reduce_fusion.2
  91.6 1.8 broadcast_divide_fusion.1.refs_2_.refs_5_
  93.4 22.1 %all-to-all-done.2.refs_1_ = bf16[16,272,128]{2,1,0:T(8,128)(2,1)S(1)} async-done(((bf16[16,272,128]{2,1,0:T(8,128)(2,1)}), bf16[16,272,128]{2,1,0:T(8,128)(2,1)S(1)}, u32[]{:S(2)}, u32[]{:S(2)}) %all-to-all-start.2) | async-done | bytes 1114144 | tf_op jit(solution)/shard_map/all_to_all | solution.py:362
  115.5 2.4 %cells.1 = (f32[64,8192]{1,0:T(8,128)S(1)}, f32[64,128]{1,0:T(8,128)S(1)}, bf16[16,272,128]{2,1,0:T(8,128)(2,1)S(1)}) custom-call(s32[16,128]{1,0:T(8,128)S(1)} %get-tuple-element.21.refs_0_, bf16[16,272,128]{2,1,0:T(8,128)(2,1)S(1)} %all-to-all-done.2.refs_1_, f32[64,8192]{1,0:T(8,128)S(1)} %broadcast_divide_fusion.1.refs_2_.refs_5_), custom_call_target="tpu_custom_call" | custom-call | bytes 8388608 | tf_op jit(solution)/shard_map/cells/pallas_call | solution.py:400
  117.9 0.0 copy-start.5
  118.0 1.3 copy-done.5
  119.3 0.0 copy-start.10
  119.3 1.0 copy-done.10
  120.3 0.0 copy-start.12
  120.3 7.2 %all-to-all-start.3 = ((bf16[16,272,128]{2,1,0:T(8,128)(2,1)}), bf16[16,272,128]{2,1,0:T(8,128)(2,1)S(1)}, u32[]{:S(2)}, u32[]{:S(2)}) async-start(bf16[16,272,128]{2,1,0:T(8,128)(2,1)} %copy-done.10), calls=%async_computation.3 | async-start | bytes 2228224 | tf_op jit(solution)/shard_map/all_to_all | solution.py:362
  127.5 0.1 slice_reduce_fusion.1
  127.6 0.0 copy-done.12
  127.6 1.0 broadcast_divide_fusion.2.data_ref
  128.6 22.9 %all-to-all-done.3.fetched_ref = bf16[16,272,128]{2,1,0:T(8,128)(2,1)S(1)} async-done(((bf16[16,272,128]{2,1,0:T(8,128)(2,1)}), bf16[16,272,128]{2,1,0:T(8,128)(2,1)S(1)}, u32[]{:S(2)}, u32[]{:S(2)}) %all-to-all-start.3) | async-done | bytes 1114144 | tf_op jit(solution)/shard_map/all_to_all | solution.py:362
  151.5 0.0 copy-start.1
  151.5 2.2 %copy-done.1 = bf16[8,16,128,128]{3,2,1,0:T(8,128)(2,1)S(1)} copy-done((bf16[8,16,128,128]{3,2,1,0:T(8,128)(2,1)S(1)}, bf16[8,16,128,128]{3,2,1,0:T(8,128)(2,1)}, u32[]{:S(2)}) %copy-start.1) | copy-done | bytes 4194328
  153.7 5.4 %pairs.3 = (bf16[16,272,128]{2,1,0:T(8,128)(2,1)S(1)}, f32[64,1024]{1,0:T(8,128)}, f32[64,128]{1,0:T(8,128)S(1)}) custom-call(s32[128]{0:T(128)S(1)} %copy-done.16, s32[3,128]{1,0:T(4,128)S(1)} %pad_add_fusion.source_ref, bf16[16,272,128]{2,1,0:T(8,128)(2,1)S(1)} %all-to-all-done.3.fetched_ref, f32[64,1024]{1,0:T(8,128)S(1)} %broadcast_divide_fusion.2.data_ref, ...), custom_call_target="tpu_custom_call" | custom-call | flops 536870912 | bytes 8388608 | tf_op jit(solution)/shard_map/pairs/pallas_call | solution.py:391
  159.1 0.0 copy-start.8
  159.1 1.0 copy-done.8
  160.1 0.0 copy-start.14
  160.1 0.6 copy-done.14
  160.7 0.0 copy-start.15
  160.7 7.3 %all-to-all-start.4 = ((bf16[16,272,128]{2,1,0:T(8,128)(2,1)}), bf16[16,272,128]{2,1,0:T(8,128)(2,1)S(1)}, u32[]{:S(2)}, u32[]{:S(2)}) async-start(bf16[16,272,128]{2,1,0:T(8,128)(2,1)} %copy-done.8), calls=%async_computation.4 | async-start | bytes 2228224 | tf_op jit(solution)/shard_map/all_to_all | solution.py:362
  168.0 0.0 copy-done.15
  168.0 0.1 slice_reduce_fusion
  168.1 3.2 %broadcast_divide_fusion.refs_2_.refs_6_ = f32[64,8192]{1,0:T(8,128)} fusion(f32[64,8192]{1,0:T(8,128)} %copy-done.5, f32[64]{0:T(128)S(1)} %slice_reduce_fusion), kind=kLoop, calls=%fused_computation | loop fusion | flops 524288 | bytes 4194560 | tf_op jit(solution)/shard_map/div | solution.py:398
  171.3 20.8 %all-to-all-done.4.refs_1_ = bf16[16,272,128]{2,1,0:T(8,128)(2,1)S(1)} async-done(((bf16[16,272,128]{2,1,0:T(8,128)(2,1)}), bf16[16,272,128]{2,1,0:T(8,128)(2,1)S(1)}, u32[]{:S(2)}, u32[]{:S(2)}) %all-to-all-start.4) | async-done | bytes 1114144 | tf_op jit(solution)/shard_map/all_to_all | solution.py:362
  192.0 0.0 copy-start.2
  192.0 1.6 copy-done.2
  193.6 0.0 copy-start.13
  193.6 2.9 %cells_last.1 = (f32[64,8192]{1,0:T(8,128)S(1)}, f32[64,128]{1,0:T(8,128)S(1)}, f32[16,8,128]{2,1,0:T(8,128)}) custom-call(s32[16,128]{1,0:T(8,128)S(1)} %get-tuple-element.21.refs_0_, bf16[16,272,128]{2,1,0:T(8,128)(2,1)S(1)} %all-to-all-done.4.refs_1_, f32[64,8192]{1,0:T(8,128)S(1)} %copy-done.2), custom_call_target="tpu_custom_call" | custom-call | bytes 8388608 | tf_op jit(solution)/shard_map/cells_last/pallas_call | solution.py:400
  196.6 0.0 copy-start.6
  196.6 1.3 copy-done.6
  197.9 7.2 %all-to-all-start.5 = ((f32[16,8,128]{2,1,0:T(8,128)}), f32[16,8,128]{2,1,0:T(8,128)S(1)}, u32[]{:S(2)}, u32[]{:S(2)}) async-start(f32[16,8,128]{2,1,0:T(8,128)} %get-tuple-element.34), calls=%async_computation.5 | async-start | bytes 131072 | tf_op jit(solution)/shard_map/all_to_all | solution.py:362
  205.1 0.0 copy-done.13
  205.1 0.0 copy-start.3
  205.1 1.6 copy-done.3
  206.7 2.1 estimate.1
  208.8 3.2 %all-to-all-done.5.tails_ref = f32[16,8,128]{2,1,0:T(8,128)S(1)} async-done(((f32[16,8,128]{2,1,0:T(8,128)}), f32[16,8,128]{2,1,0:T(8,128)S(1)}, u32[]{:S(2)}, u32[]{:S(2)}) %all-to-all-start.5) | async-done | bytes 65568 | tf_op jit(solution)/shard_map/all_to_all | solution.py:362
  212.0 0.0 copy-start.7
  212.0 1.6 copy-done.7
  213.6 1.8 model.1
  (4 shorter events, 0.0 us)
Async XLA Ops:
  43.5 8.3 %copy-start.16 = (s32[128]{0:T(128)S(1)}, s32[128]{0:T(128)}, u32[]{:S(2)}) copy-start(s32[128]{0:T(128)} %get-tuple-element.22.target_ref) | copy-start | bytes 1540
  43.5 8.4 %copy-start.17 = (f32[1024,64]{0,1:T(8,128)S(1)}, f32[1024,64]{0,1:T(8,128)}, u32[]{:S(2)}) copy-start(f32[1024,64]{0,1:T(8,128)} %param.7) | copy-start | bytes 786436
  46.7 1.3 copy-start.4
  48.0 27.7 %all-to-all-start.1 = ((bf16[16,272,128]{2,1,0:T(8,128)(2,1)}), bf16[16,272,128]{2,1,0:T(8,128)(2,1)S(1)}, u32[]{:S(2)}, u32[]{:S(2)}) async-start(bf16[16,272,128]{2,1,0:T(8,128)(2,1)} %get-tuple-element.23), calls=%async_computation.1 | async-start | bytes 2228224 | tf_op jit(solution)/shard_map/all_to_all | solution.py:362
  75.7 2.2 %copy-start = (bf16[8,16,128,128]{3,2,1,0:T(8,128)(2,1)S(1)}, bf16[8,16,128,128]{3,2,1,0:T(8,128)(2,1)}, u32[]{:S(2)}) copy-start(bf16[8,16,128,128]{3,2,1,0:T(8,128)(2,1)} %rays_ref.3) | copy-start | bytes 12582916
  82.7 1.0 copy-start.9
  83.7 0.7 copy-start.11
  84.4 31.1 %all-to-all-start.2 = ((bf16[16,272,128]{2,1,0:T(8,128)(2,1)}), bf16[16,272,128]{2,1,0:T(8,128)(2,1)S(1)}, u32[]{:S(2)}, u32[]{:S(2)}) async-start(bf16[16,272,128]{2,1,0:T(8,128)(2,1)} %copy-done.9), calls=%async_computation.2 | async-start | bytes 2228224 | tf_op jit(solution)/shard_map/all_to_all | solution.py:362
  117.9 1.3 copy-start.5
  119.3 1.0 copy-start.10
  120.3 7.3 %copy-start.12 = (f32[64,128]{1,0:T(8,128)}, f32[64,128]{1,0:T(8,128)S(1)}, u32[]{:S(2)}) copy-start(f32[64,128]{1,0:T(8,128)S(1)} %get-tuple-element.27.refs_1_) | copy-start | bytes 98308
  120.3 31.2 %all-to-all-start.3 = ((bf16[16,272,128]{2,1,0:T(8,128)(2,1)}), bf16[16,272,128]{2,1,0:T(8,128)(2,1)S(1)}, u32[]{:S(2)}, u32[]{:S(2)}) async-start(bf16[16,272,128]{2,1,0:T(8,128)(2,1)} %copy-done.10), calls=%async_computation.3 | async-start | bytes 2228224 | tf_op jit(solution)/shard_map/all_to_all | solution.py:362
  151.5 2.2 %copy-start.1 = (bf16[8,16,128,128]{3,2,1,0:T(8,128)(2,1)S(1)}, bf16[8,16,128,128]{3,2,1,0:T(8,128)(2,1)}, u32[]{:S(2)}) copy-start(bf16[8,16,128,128]{3,2,1,0:T(8,128)(2,1)} %rays_ref.3) | copy-start | bytes 12582916
  159.1 1.0 copy-start.8
  160.1 0.6 copy-start.14
  160.7 7.3 %copy-start.15 = (f32[64,128]{1,0:T(8,128)S(1)}, f32[64,128]{1,0:T(8,128)}, u32[]{:S(2)}) copy-start(f32[64,128]{1,0:T(8,128)} %copy-done.14) | copy-start | bytes 98308
  160.7 31.3 %all-to-all-start.4 = ((bf16[16,272,128]{2,1,0:T(8,128)(2,1)}), bf16[16,272,128]{2,1,0:T(8,128)(2,1)S(1)}, u32[]{:S(2)}, u32[]{:S(2)}) async-start(bf16[16,272,128]{2,1,0:T(8,128)(2,1)} %copy-done.8), calls=%async_computation.4 | async-start | bytes 2228224 | tf_op jit(solution)/shard_map/all_to_all | solution.py:362
  192.0 1.6 copy-start.2
  193.6 11.5 %copy-start.13 = (f32[64,128]{1,0:T(8,128)S(1)}, f32[64,128]{1,0:T(8,128)}, u32[]{:S(2)}) copy-start(f32[64,128]{1,0:T(8,128)} %copy-done.12) | copy-start | bytes 98308
  196.6 1.3 copy-start.6
  197.9 14.1 %all-to-all-start.5 = ((f32[16,8,128]{2,1,0:T(8,128)}), f32[16,8,128]{2,1,0:T(8,128)S(1)}, u32[]{:S(2)}, u32[]{:S(2)}) async-start(f32[16,8,128]{2,1,0:T(8,128)} %get-tuple-element.34), calls=%async_computation.5 | async-start | bytes 131072 | tf_op jit(solution)/shard_map/all_to_all | solution.py:362
  205.1 1.6 copy-start.3
  212.0 1.6 copy-start.7

commit v6 on v5

v6 whole, which is shorter than its diff:
```python
import functools

import jax
import jax.numpy as jnp
from jax import lax
from jax.experimental import pallas as pl
from jax.experimental.pallas import tpu as pltpu
from jax.sharding import PartitionSpec as P

CELL_DEV = 8192
BCAP = 4
BS = 128
TAIL = 8
ITERS = 2
EPS = 1e-12
F32 = jnp.float32
BF16 = jnp.bfloat16
VMEM = pltpu.VMEM
SMEM = pltpu.SMEM
HBM = pltpu.HBM
CHUNKS = 8


def diagonal(cols):
    shape = (cols, BS)
    return lax.broadcasted_iota(jnp.int32, shape, 0) == lax.broadcasted_iota(jnp.int32, shape, 1)


def squares_tail(squares):
    cols = squares.shape[0]
    total = jnp.sum(squares, axis=1, keepdims=True)
    row = jnp.sum(jnp.where(diagonal(cols), total, 0.0), axis=0, keepdims=True)
    high = row.astype(BF16).astype(F32)
    middle = (row - high).astype(BF16).astype(F32)
    low = row - high - middle
    place = lax.broadcasted_iota(jnp.int32, (TAIL, BS), 0)
    return jnp.where(
        place == 0, high, jnp.where(place == 1, middle, jnp.where(place == 2, low, 0.0))
    )


def norm_of_tails(message_ref, cols):
    tails = message_ref[:, BCAP * cols :, :].astype(F32)
    summed = jnp.sum(tails, axis=0)
    row = summed[0:1] + summed[1:2] + summed[2:3]
    column = jnp.sum(jnp.where(diagonal(cols), row, 0.0), axis=1, keepdims=True)
    return jnp.broadcast_to(jnp.sqrt(column + EPS), (cols, BS))


def lanes(block):
    return pl.ds(pl.multiple_of(block * BS, BS), BS)


def transposed(data_ref, rays_ref, before, target_ref, total_ref, message_ref):
    pair_count, slot_count = rays_ref.shape[:2]
    cols = data_ref.shape[0]
    peers = message_ref.shape[0]
    spots = peers * BCAP

    def clear(index, carry):
        total_ref[index] = jnp.zeros((cols, BS), F32)
        return carry

    lax.fori_loop(0, spots, clear, 0, unroll=8)

    def one_pair(pair, carry):
        before(pair)
        data = data_ref[:, lanes(pair)]
        high = data.astype(BF16)
        low = (data - high.astype(F32)).astype(BF16)
        pieces = jnp.concatenate([high, low], axis=0)
        for slot in range(0, slot_count, 2):
            rays = jnp.concatenate([rays_ref[pair, slot], rays_ref[pair, slot + 1]], axis=1)
            part = jnp.dot(pieces, rays, preferred_element_type=F32)
            part = part[:cols] + part[cols:]
            for half in range(2):
                spot = target_ref[pair * slot_count + slot + half]
                total_ref[spot] += part[:, half * BS : (half + 1) * BS]
        return carry

    lax.fori_loop(0, pair_count, one_pair, 0, unroll=2)

    def pack(peer, carry):
        for rank in range(BCAP):
            message_ref[peer, rank * cols : (rank + 1) * cols, :] = total_ref[
                peer * BCAP + rank
            ].astype(BF16)
        return carry

    lax.fori_loop(0, peers, pack, 0, unroll=2)


def start_kernel(
    cells_hbm, counts_hbm, times_hbm, rays_hbm, message_ref, target_ref,
    total_ref, table_ref, used_ref, cells_ref, counts_ref, times_ref, rays_ref, sems, ray_sems,
):
    pair_count, slot_count = rays_ref.shape[:2]
    peers = message_ref.shape[0]
    cols = times_ref.shape[0]
    owned = CELL_DEV // BS
    copies = [
        pltpu.make_async_copy(source, dest, sems.at[index])
        for index, (source, dest) in enumerate(
            [(cells_hbm, cells_ref), (counts_hbm, counts_ref), (times_hbm, times_ref)]
        )
    ]
    for copy in copies:
        copy.start()

    def ray_copy(pair):
        return pltpu.make_async_copy(rays_hbm.at[pair], rays_ref.at[pair], ray_sems.at[pair])

    def fetch(pair, carry):
        ray_copy(pair).start()
        return carry

    lax.fori_loop(0, pair_count, fetch, 0)

    def clear(peer, carry):
        used_ref[peer] = 0
        for rank in range(BCAP):
            table_ref[peer * BCAP + rank] = 0
        return carry

    lax.fori_loop(0, peers, clear, 0)
    for copy in copies:
        copy.wait()

    def find_places(pair):
        count = counts_ref[pair]
        for slot in range(slot_count):
            cell = cells_ref[pair, slot]
            owner = cell // owned
            local = cell % owned
            used = used_ref[owner]
            rank = used
            for other in range(BCAP - 1, -1, -1):
                same = (table_ref[owner * BCAP + other] == local) & (other < used)
                rank = jnp.where(same, other, rank)
            spot = owner * BCAP + rank
            table_ref[spot] = local
            used_ref[owner] = jnp.maximum(used, rank + 1)
            target_ref[pair * slot_count + slot] = jnp.where(slot < count, spot, peers * BCAP)

    def before(pair):
        find_places(pair)
        ray_copy(pair).wait()

    transposed(times_ref, rays_ref, before, target_ref, total_ref, message_ref)
    squares = jnp.zeros((cols, BS), F32)
    for pair in range(pair_count):
        part = times_ref[:, pair * BS : (pair + 1) * BS]
        squares += part * part
    tail = squares_tail(squares)
    place = lax.broadcasted_iota(jnp.int32, (TAIL, BS), 0)
    lane = lax.broadcasted_iota(jnp.int32, (TAIL, BS), 1)

    def ask(peer, carry):
        rows = tail
        for rank in range(BCAP):
            asked = table_ref[peer * BCAP + rank].astype(F32)
            rows = jnp.where((place == 3) & (lane == rank), asked, rows)
        message_ref[peer, BCAP * cols :, :] = rows.astype(BF16)
        return carry

    lax.fori_loop(0, peers, ask, 0)


def pair_kernel(
    target_ref, fetched_ref, data_ref, beta_ref, rays_ref,
    message_ref, raw_ref, alpha_ref, total_ref,
):
    pair_count, slot_count = rays_ref.shape[:2]
    peers = message_ref.shape[0]
    cols = data_ref.shape[0]
    spots = peers * BCAP
    alpha = norm_of_tails(fetched_ref, cols)
    alpha_ref[...] = alpha
    beta = beta_ref[...]
    model_scale = 1.0 / (alpha * beta)
    data_scale = alpha / beta

    def one_pair(pair, squares):
        chosen = []
        for slot in range(slot_count):
            spot = target_ref[pair * slot_count + slot]
            live = spot < spots
            spot = jnp.where(live, spot, 0)
            rows = pl.ds(pl.multiple_of((spot % BCAP) * cols, cols), cols)
            block = fetched_ref[spot // BCAP, rows, :]
            chosen.append(jnp.where(live, block, jnp.zeros_like(block)))
        rays = jnp.concatenate([rays_ref[pair, slot] for slot in range(slot_count)], axis=1)
        product = lax.dot_general(
            rays, jnp.concatenate(chosen, axis=1), (((1,), (1,)), ((), ())),
            preferred_element_type=F32,
        )
        raw = product.T * model_scale - data_ref[:, lanes(pair)] * data_scale
        raw_ref[:, lanes(pair)] = raw
        return squares + raw * raw

    squares = lax.fori_loop(0, pair_count, one_pair, jnp.zeros((cols, BS), F32), unroll=2)
    transposed(raw_ref, rays_ref, lambda pair: None, target_ref, total_ref, message_ref)
    tail = squares_tail(squares).astype(BF16)
    message_ref[:, BCAP * cols :, :] = jnp.broadcast_to(tail[None], (peers, TAIL, BS))


def gathered(arrived_ref, asked_ref, model_ref):
    peers = arrived_ref.shape[0]
    cols = model_ref.shape[0]

    def add(peer, carry):
        for rank in range(BCAP):
            where = lanes(asked_ref[peer, rank])
            block = arrived_ref[peer, rank * cols : (rank + 1) * cols, :]
            model_ref[:, where] += block.astype(F32)
        return carry

    lax.fori_loop(0, peers, add, 0, unroll=2)


def reply(squares, scale, asked_ref, model_ref, out_ref):
    peers = out_ref.shape[0]
    cols = model_ref.shape[0]
    tail = squares_tail(squares * scale * scale).astype(BF16)
    out_ref[:, BCAP * cols :, :] = jnp.broadcast_to(tail[None], (peers, TAIL, BS))

    def one_peer(peer, carry):
        for rank in range(BCAP):
            block = model_ref[:, lanes(asked_ref[peer, rank])]
            out_ref[peer, rank * cols : (rank + 1) * cols, :] = block.astype(BF16)
        return carry

    lax.fori_loop(0, peers, one_peer, 0, unroll=2)


def squares_of(model_ref):
    cols, cells = model_ref.shape

    def one_block(block, squares):
        values = model_ref[:, lanes(block)]
        return squares + values * values

    return lax.fori_loop(0, cells // BS, one_block, jnp.zeros((cols, BS), F32), unroll=8)


def first_cell_kernel(arrived_ref, model_ref, beta_ref, out_ref, asked_ref, table_ref, sem):
    cols, cells = model_ref.shape
    table_ref[...] = arrived_ref[:, BCAP * cols :, :].astype(F32)[:, 3, :].astype(jnp.int32)
    copy = pltpu.make_async_copy(table_ref, asked_ref, sem)
    copy.start()
    beta = norm_of_tails(arrived_ref, cols)
    beta_ref[...] = beta
    model_ref[...] = jnp.zeros((cols, cells), F32)
    copy.wait()
    gathered(arrived_ref, asked_ref, model_ref)
    reply(squares_of(model_ref), 1.0 / beta, asked_ref, model_ref, out_ref)


def start_from(before_ref, scale, model_ref):
    def one_block(block, carry):
        model_ref[:, lanes(block)] = before_ref[:, lanes(block)] * -scale
        return carry

    lax.fori_loop(0, model_ref.shape[1] // BS, one_block, 0, unroll=8)


def cell_kernel(
    asked_ref, arrived_ref, before_ref, alpha_ref, beta_before_ref, model_ref, beta_ref, out_ref
):
    beta = norm_of_tails(arrived_ref, model_ref.shape[0])
    beta_ref[...] = beta
    start_from(before_ref, beta * beta / (alpha_ref[...] * beta_before_ref[...]), model_ref)
    gathered(arrived_ref, asked_ref, model_ref)
    reply(squares_of(model_ref), 1.0 / beta, asked_ref, model_ref, out_ref)


def last_cell_kernel(asked_ref, arrived_ref, *refs):
    models = refs[:ITERS]
    alphas = [ref[...] for ref in refs[ITERS : 2 * ITERS]]
    betas = [ref[...] for ref in refs[2 * ITERS : 3 * ITERS]]
    model_ref, beta_ref, out_ref, estimate_hbm, estimate_ref, sems = refs[3 * ITERS :]
    cols, cells = model_ref.shape
    beta = norm_of_tails(arrived_ref, cols)
    beta_ref[...] = beta
    weights = estimate_weights(betas + [beta], alphas)
    scale = beta * beta / (alphas[-1] * betas[-1])
    blocks = cells // BS // CHUNKS

    def one_block(block, carry):
        where = lanes(block)
        values = models[-1][:, where]
        model_ref[:, where] = values * -scale
        total = values * weights[-1]
        for i in range(ITERS - 1):
            total += weights[i] * models[i][:, where]
        estimate_ref[:, where] = total
        return carry

    copies = []
    for chunk in range(CHUNKS):
        lax.fori_loop(chunk * blocks, (chunk + 1) * blocks, one_block, 0, unroll=4)
        where = slice(chunk * blocks * BS, (chunk + 1) * blocks * BS)
        copies.append(
            pltpu.make_async_copy(
                estimate_ref.at[:, where], estimate_hbm.at[:, where], sems.at[chunk]
            )
        )
        copies[-1].start()
    gathered(arrived_ref, asked_ref, model_ref)
    scale = 1.0 / beta
    tail = squares_tail(squares_of(model_ref) * scale * scale)
    out_ref[...] = jnp.broadcast_to(tail[None], out_ref.shape)
    for copy in copies:
        copy.wait()


def estimate_weights(betas, alphas):
    phi_bar = betas[0]
    rho_bar = alphas[0]
    trace = [1.0 / (alphas[0] * betas[0])]
    weight = [jnp.zeros_like(phi_bar)] * ITERS
    for step in range(ITERS):
        beta = betas[step + 1]
        rho = jnp.sqrt(rho_bar * rho_bar + beta * beta)
        cosine = rho_bar / rho
        sine = beta / rho
        gain = cosine * phi_bar / rho
        weight = [
            weight[i] + gain * trace[i] if i < len(trace) else weight[i] for i in range(ITERS)
        ]
        if step + 1 < ITERS:
            alpha = alphas[step + 1]
            theta = sine * alpha
            rho_bar = -cosine * alpha
            phi_bar = sine * phi_bar
            trace = [-(theta / rho) * value for value in trace] + [1.0 / (alpha * beta)]
    return weight


def model_kernel(tails_ref, beta_ref, model_ref, out_hbm, out_ref, sems):
    cols, cells = model_ref.shape
    blocks = cells // BS // CHUNKS
    summed = jnp.sum(tails_ref[...], axis=0)
    row = summed[0:1] + summed[1:2] + summed[2:3]
    column = jnp.sum(jnp.where(diagonal(cols), row, 0.0), axis=1, keepdims=True)
    alpha = jnp.broadcast_to(jnp.sqrt(column + EPS), (cols, BS))
    scale = 1.0 / (alpha * beta_ref[...])

    def one_block(block, carry):
        out_ref[:, lanes(block)] = model_ref[:, lanes(block)] * scale
        return carry

    copies = []
    for chunk in range(CHUNKS):
        lax.fori_loop(chunk * blocks, (chunk + 1) * blocks, one_block, 0, unroll=4)
        where = slice(chunk * blocks * BS, (chunk + 1) * blocks * BS)
        copies.append(
            pltpu.make_async_copy(out_ref.at[:, where], out_hbm.at[:, where], sems.at[chunk])
        )
        copies[-1].start()
    for copy in copies:
        copy.wait()


def call(kernel, name, in_spaces, outs, scratch=(), flops=0, moved=0, limit=16 << 20):
    return pl.pallas_call(
        kernel,
        name=name,
        in_specs=[pl.BlockSpec(memory_space=space) for space in in_spaces],
        out_specs=[pl.BlockSpec(memory_space=space) for _, _, space in outs],
        out_shape=[jax.ShapeDtypeStruct(shape, dtype) for shape, dtype, _ in outs],
        scratch_shapes=list(scratch),
        compiler_params=pltpu.CompilerParams(vmem_limit_bytes=limit),
        cost_estimate=pl.CostEstimate(flops=flops, bytes_accessed=moved, transcendentals=0),
    )


def on_device(ray_blocks, block_cells, block_counts, travel_times):
    pair_count, slot_count = ray_blocks.shape[:2]
    slots = pair_count * slot_count
    peers = lax.axis_size("pair")
    spots = peers * BCAP
    times = travel_times.T
    cols, pairs = times.shape
    message = ((peers, BCAP * cols + TAIL, BS), BF16, VMEM)
    tile = ((cols, BS), F32, VMEM)
    data = ((cols, pairs), F32, VMEM)
    whole = ((cols, CELL_DEV), F32, VMEM)
    totals = VMEM((spots + 1, cols, BS), F32)
    flops = 2 * slots * BS * BS * cols

    def exchange(values):
        return lax.all_to_all(values, "pair", split_axis=0, concat_axis=0, tiled=True)

    outgoing, target = call(
        start_kernel, "start", [HBM, HBM, HBM, HBM],
        [message, ((slots,), jnp.int32, SMEM)],
        [
            totals, SMEM((spots,), jnp.int32), SMEM((peers,), jnp.int32),
            SMEM(block_cells.shape, jnp.int32), SMEM(block_counts.shape, jnp.int32),
            VMEM(times.shape, F32), VMEM(ray_blocks.shape, BF16),
            pltpu.SemaphoreType.DMA((3,)), pltpu.SemaphoreType.DMA((pair_count,)),
        ],
        flops, 6 << 20, 60 << 20,
    )(block_cells, block_counts, times, ray_blocks)
    arrived = exchange(outgoing)
    model, beta, reply_, asked = call(
        first_cell_kernel, "cells_first", [VMEM],
        [whole, tile, message, ((peers, BS), jnp.int32, SMEM)],
        [VMEM((peers, BS), jnp.int32), pltpu.SemaphoreType.DMA],
        0, 6 << 20,
    )(arrived)
    models, betas, alphas = [model], [beta], []
    current = times
    for step in range(ITERS):
        fetched = exchange(reply_)
        outgoing, current, alpha = call(
            pair_kernel, "pairs", [SMEM, VMEM, VMEM, VMEM, VMEM],
            [message, data, tile], [totals], 2 * flops, 8 << 20,
        )(target, fetched, current, betas[-1], ray_blocks)
        alphas.append(alpha)
        arrived = exchange(outgoing)
        if step + 1 < ITERS:
            model, beta, reply_ = call(
                cell_kernel, "cells", [SMEM] + [VMEM] * 4, [whole, tile, message], (), 0, 8 << 20
            )(asked, arrived, models[-1], alpha, betas[-1])
            models.append(model)
            betas.append(beta)
    scratch = [VMEM(whole[0], F32), pltpu.SemaphoreType.DMA((CHUNKS,))]
    model, beta, tails, estimate = call(
        last_cell_kernel, "cells_last", [SMEM] + [VMEM] * (3 * ITERS + 1),
        [whole, tile, ((peers, TAIL, BS), F32, VMEM), (whole[0], F32, HBM)], scratch, 0, 10 << 20,
    )(asked, arrived, *models, *alphas, *betas)
    (model_vec,) = call(
        model_kernel, "model", [VMEM, VMEM, VMEM], [(whole[0], F32, HBM)], scratch, 0, 4 << 20
    )(exchange(tails), beta, model)
    return (estimate.T, model_vec.T)


def solution(mesh):
    return jax.shard_map(
        on_device,
        mesh=mesh,
        in_specs=(
            P(("groups", "pair"), None, None, None),
            P(("groups", "pair"), None),
            P(("groups", "pair")),
            P(("groups", "pair"), None),
        ),
        out_specs=(P(("groups", "pair"), None), P(("groups", "pair"), None)),
        check_vma=False,
    )
```

time: 216 us -> 195 us (0.903)
  blocking collectives: 35.9 us -> 168 us
  waiting for transfers between devices: 92.6 us -> 0 us
  starting transfers between devices: 32.5 us -> 0 us
  local copies, waits for them, and re-layouts: 17.8 us -> 0.02 us
  other arithmetic: 6.13 us -> 0 us
  Pallas kernels: 29.6 us -> 25.9 us
    all_to_all x1 -> x6, blocking collectives: 35.9 us -> 168 us  [exchange(): lax.all_to_all(values, 'pair', split_axis=0, concat_axis=0, tiled=True)]
    all_to_all x5 -> x0, waiting for transfers between devices: 92.6 us -> none  [exchange(): lax.all_to_all(values, 'pair', split_axis=0, concat_axis=0, tiled=True)]
    all_to_all x5 -> x0, starting transfers between devices: 32.5 us -> none  [exchange(): lax.all_to_all(values, 'pair', split_axis=0, concat_axis=0, tiled=True)]
    unnamed x36 -> x6, local copies, waits for them, and re-layouts: 17.4 us -> 0.02 us
    div x4 -> x0, other arithmetic: 6.1 us -> none  [the longest x2 4.96 us: on_device(): models.append(raw / alpha[:, :1])]
    pallas_call x7 -> x6, Pallas kernels: 22.7 us -> 19.7 us  [the longest x2 10.3 us: on_device(): call(pair_kernel, 'pairs', [SMEM, VMEM, VMEM, VMEM, VMEM], [message, data...]
  transfers between devices with their start and end apart: 5 -> 0, of which waited for: 5 -> 0; matrix products, arithmetic and copies ran while one was open for 3% -> 0% of each run, Pallas kernels for 1% -> 0%
where the time goes in v6:
time: 195 us
  blocking collectives  168 us (86%)
  Pallas kernels  25.9 us (13%)
    all_to_all x6, blocking collectives, exchange(): lax.all_to_all(values, 'pair', split_axis=0, concat_axis=0, tiled=True)  168 us
    pallas_call x2, Pallas kernels, on_device(): call(pair_kernel, 'pairs', [SMEM, VMEM, VMEM, VMEM, VMEM], [message, data...  10.3 us
    pallas_call x1, Pallas kernels, on_device(): call(start_kernel, 'start', [HBM, HBM, HBM, HBM], [message, ((slots,), jn...  6.19 us

profile of v6, /device:TPU:0, one launch (start us, length us, event | category | flops | bytes accessed | tf_op | source)
XLA Modules:
  0.0 194.9 jit_solution(4040891322814175512)
XLA Ops:
  0.6 6.2 %start.1 = (bf16[16,264,128]{2,1,0:T(8,128)(2,1)}, s32[128]{0:T(128)}) custom-call(s32[8,16]{1,0:T(8,128)} %cells_hbm.1, s32[8]{0:T(128)} %counts_hbm.1, f32[64,1024]{1,0:T(8,128)} %bitcast.3, bf16[8,16,128,128]{3,2,1,0:T(8,128)(2,1)} %rays_ref.3), custom_call_target="tpu_custom_call" | custom-call | flops 268435456 | bytes 6291456 | tf_op jit(solution)/shard_map/start/pallas_call | solution.py:395
  6.8 0.0 copy-start
  6.8 35.6 %all_to_all.30.arrived_ref = bf16[16,264,128]{2,1,0:T(8,128)(2,1)S(1)} all-to-all(bf16[16,264,128]{2,1,0:T(8,128)(2,1)} %get-tuple-element.20), channel_id=1, replica_groups=mesh['groups'=2,'pair'=16] {'pair'}, dimensions={0} | all-to-all | bytes 2162688 | tf_op jit(solution)/shard_map/all_to_all | solution.py:393
  42.5 2.7 %cells_first.1 = (f32[64,8192]{1,0:T(8,128)S(1)}, f32[64,128]{1,0:T(8,128)S(1)}, bf16[16,264,128]{2,1,0:T(8,128)(2,1)S(1)}, s32[16,128]{1,0:T(8,128)S(1)}) custom-call(bf16[16,264,128]{2,1,0:T(8,128)(2,1)S(1)} %all_to_all.30.arrived_ref), custom_call_target="tpu_custom_call" | custom-call | bytes 6291456 | tf_op jit(solution)/shard_map/cells_first/pallas_call | solution.py:407
  45.2 0.0 copy-start.1
  45.2 0.0 copy-start.2
  45.2 30.9 %all_to_all.31.fetched_ref = bf16[16,264,128]{2,1,0:T(8,128)(2,1)S(1)} all-to-all(bf16[16,264,128]{2,1,0:T(8,128)(2,1)S(1)} %get-tuple-element.23), channel_id=1, replica_groups=mesh['groups'=2,'pair'=16] {'pair'}, dimensions={0} | all-to-all | bytes 2162688 | tf_op jit(solution)/shard_map/all_to_all | solution.py:393
  76.1 0.0 copy-done
  76.1 0.0 copy-done.1
  76.1 0.0 copy-done.2
  76.1 4.9 %pairs.2 = (bf16[16,264,128]{2,1,0:T(8,128)(2,1)S(1)}, f32[64,1024]{1,0:T(8,128)S(1)}, f32[64,128]{1,0:T(8,128)S(1)}) custom-call(s32[128]{0:T(128)S(1)} %copy-done.2, bf16[16,264,128]{2,1,0:T(8,128)(2,1)S(1)} %all_to_all.31.fetched_ref, f32[64,1024]{1,0:T(8,128)S(1)} %bitcast.4, f32[64,128]{1,0:T(8,128)S(1)} %get-tuple-element.24.beta_ref.beta_before_ref.refs_4_, ...), custom_call_target="tpu_custom_call" | custom-call | flops 536870912 | bytes 8388608 | tf_op jit(solution)/shard_map/pairs/pallas_call | solution.py:417
  81.0 30.7 %all_to_all.32.arrived_ref = bf16[16,264,128]{2,1,0:T(8,128)(2,1)S(1)} all-to-all(bf16[16,264,128]{2,1,0:T(8,128)(2,1)S(1)} %get-tuple-element.25), channel_id=1, replica_groups=mesh['groups'=2,'pair'=16] {'pair'}, dimensions={0} | all-to-all | bytes 2162688 | tf_op jit(solution)/shard_map/all_to_all | solution.py:393
  111.7 2.4 %cells.1 = (f32[64,8192]{1,0:T(8,128)S(1)}, f32[64,128]{1,0:T(8,128)S(1)}, bf16[16,264,128]{2,1,0:T(8,128)(2,1)S(1)}) custom-call(s32[16,128]{1,0:T(8,128)S(1)} %get-tuple-element.21.asked_ref, bf16[16,264,128]{2,1,0:T(8,128)(2,1)S(1)} %all_to_all.32.arrived_ref, f32[64,8192]{1,0:T(8,128)S(1)} %get-tuple-element.26.before_ref.refs_0_, ...), custom_call_target="tpu_custom_call" | custom-call | bytes 8388608 | tf_op jit(solution)/shard_map/cells/pallas_call | solution.py:424
  114.1 30.7 %all_to_all.33.fetched_ref = bf16[16,264,128]{2,1,0:T(8,128)(2,1)S(1)} all-to-all(bf16[16,264,128]{2,1,0:T(8,128)(2,1)S(1)} %get-tuple-element.28), channel_id=1, replica_groups=mesh['groups'=2,'pair'=16] {'pair'}, dimensions={0} | all-to-all | bytes 2162688 | tf_op jit(solution)/shard_map/all_to_all | solution.py:393
  144.9 5.5 %pairs.3 = (bf16[16,264,128]{2,1,0:T(8,128)(2,1)S(1)}, f32[64,1024]{1,0:T(8,128)}, f32[64,128]{1,0:T(8,128)S(1)}) custom-call(s32[128]{0:T(128)S(1)} %copy-done.2, bf16[16,264,128]{2,1,0:T(8,128)(2,1)S(1)} %all_to_all.33.fetched_ref, f32[64,1024]{1,0:T(8,128)S(1)} %get-tuple-element.29.data_ref, f32[64,128]{1,0:T(8,128)S(1)} %get-tuple-element.30.beta_ref.refs_5_, ...), custom_call_target="tpu_custom_call" | custom-call | flops 536870912 | bytes 8388608 | tf_op jit(solution)/shard_map/pairs/pallas_call | solution.py:417
  150.3 30.7 %all_to_all.34.arrived_ref = bf16[16,264,128]{2,1,0:T(8,128)(2,1)S(1)} all-to-all(bf16[16,264,128]{2,1,0:T(8,128)(2,1)S(1)} %get-tuple-element.31), channel_id=1, replica_groups=mesh['groups'=2,'pair'=16] {'pair'}, dimensions={0} | all-to-all | bytes 2162688 | tf_op jit(solution)/shard_map/all_to_all | solution.py:393
  181.0 2.7 %cells_last.1 = (f32[64,8192]{1,0:T(8,128)S(1)}, f32[64,128]{1,0:T(8,128)S(1)}, f32[16,8,128]{2,1,0:T(8,128)S(1)}, f32[64,8192]{1,0:T(8,128)}) custom-call(s32[16,128]{1,0:T(8,128)S(1)} %get-tuple-element.21.asked_ref, bf16[16,264,128]{2,1,0:T(8,128)(2,1)S(1)} %all_to_all.34.arrived_ref, f32[64,8192]{1,0:T(8,128)S(1)} %get-tuple-element.26.before_ref.refs_0_, ...), custom_call_target="tpu_custom_call" | custom-call | bytes 10485760 | tf_op jit(solution)/shard_map/cells_last/pallas_call | solution.py:430
  183.7 9.6 %all_to_all.35.tails_ref = f32[16,8,128]{2,1,0:T(8,128)S(1)} all-to-all(f32[16,8,128]{2,1,0:T(8,128)S(1)} %get-tuple-element.35), channel_id=1, replica_groups=mesh['groups'=2,'pair'=16] {'pair'}, dimensions={0} | all-to-all | bytes 131072 | tf_op jit(solution)/shard_map/all_to_all | solution.py:393
  193.4 1.5 model.1
Async XLA Ops:
  6.8 69.3 %copy-start = (bf16[8,16,128,128]{3,2,1,0:T(8,128)(2,1)S(1)}, bf16[8,16,128,128]{3,2,1,0:T(8,128)(2,1)}, u32[]{:S(2)}) copy-start(bf16[8,16,128,128]{3,2,1,0:T(8,128)(2,1)} %rays_ref.3) | copy-start | bytes 12582916
  45.2 30.9 %copy-start.1 = (f32[1024,64]{0,1:T(8,128)S(1)}, f32[1024,64]{0,1:T(8,128)}, u32[]{:S(2)}) copy-start(f32[1024,64]{0,1:T(8,128)} %param.7) | copy-start | bytes 786436
  45.2 30.9 %copy-start.2 = (s32[128]{0:T(128)S(1)}, s32[128]{0:T(128)}, u32[]{:S(2)}) copy-start(s32[128]{0:T(128)} %get-tuple-element.22.target_ref) | copy-start | bytes 1540

commit v7 on v6

--- a/solution.py
+++ b/solution.py
@@ -131,6 +131,7 @@
         for slot in range(slot_count):
             cell = cells_ref[pair, slot]
             owner = cell // owned
+            owner = owner * 2 - jnp.where(owner < peers // 2, 0, peers - 1)
             local = cell % owned
             used = used_ref[owner]
             rank = used
@@ -389,8 +390,12 @@
     totals = VMEM((spots + 1, cols, BS), F32)
     flops = 2 * slots * BS * BS * cols
 
+    order = [peer // 2 + peer % 2 * (peers // 2) for peer in range(peers)]
+
     def exchange(values):
-        return lax.all_to_all(values, "pair", split_axis=0, concat_axis=0, tiled=True)
+        return lax.all_to_all(
+            values, "pair", split_axis=0, concat_axis=0, axis_index_groups=[order], tiled=True
+        )
 
     outgoing, target = call(
         start_kernel, "start", [HBM, HBM, HBM, HBM],

time: 195 us -> 195 us (level)
  no operation moved by 1% of the time
where the time goes in v7:
time: 195 us
  blocking collectives  168 us (86%)
  Pallas kernels  26.1 us (13%)
    all_to_all x6, blocking collectives, exchange(): lax.all_to_all(values, 'pair', split_axis=0, concat_axis=0, axis_index_gr...  168 us
    pallas_call x2, Pallas kernels, on_device(): call(pair_kernel, 'pairs', [SMEM, VMEM, VMEM, VMEM, VMEM], [message, data...  10.4 us
    pallas_call x1, Pallas kernels, on_device(): call(start_kernel, 'start', [HBM, HBM, HBM, HBM], [message, ((slots,), jn...  6.38 us

profile of v7, /device:TPU:0, one launch (start us, length us, event | category | flops | bytes accessed | tf_op | source)
XLA Modules:
  0.0 194.9 jit_solution(2027525579236228099)
XLA Ops:
  0.6 6.4 %start.1 = (bf16[16,264,128]{2,1,0:T(8,128)(2,1)}, s32[128]{0:T(128)}) custom-call(s32[8,16]{1,0:T(8,128)} %cells_hbm.1, s32[8]{0:T(128)} %counts_hbm.1, f32[64,1024]{1,0:T(8,128)} %bitcast.3, bf16[8,16,128,128]{3,2,1,0:T(8,128)(2,1)} %rays_ref.3), custom_call_target="tpu_custom_call" | custom-call | flops 268435456 | bytes 6291456 | tf_op jit(solution)/shard_map/start/pallas_call | solution.py:400
  7.0 0.0 copy-start
  7.0 35.7 %all_to_all.30.arrived_ref = bf16[16,264,128]{2,1,0:T(8,128)(2,1)S(1)} all-to-all(bf16[16,264,128]{2,1,0:T(8,128)(2,1)} %get-tuple-element.20), channel_id=1, replica_groups={{0,8,1,9,2,10,3,11,4,12,5,13,6,14,7,15},{16,24,17,25,18,26,19,27,20,28,..., dimensions={0} | all-to-all | bytes 2162688 | tf_op jit(solution)/shard_map/all_to_all | solution.py:396
  42.7 2.7 %cells_first.1 = (f32[64,8192]{1,0:T(8,128)S(1)}, f32[64,128]{1,0:T(8,128)S(1)}, bf16[16,264,128]{2,1,0:T(8,128)(2,1)S(1)}, s32[16,128]{1,0:T(8,128)S(1)}) custom-call(bf16[16,264,128]{2,1,0:T(8,128)(2,1)S(1)} %all_to_all.30.arrived_ref), custom_call_target="tpu_custom_call" | custom-call | bytes 6291456 | tf_op jit(solution)/shard_map/cells_first/pallas_call | solution.py:412
  45.5 0.0 copy-start.1
  45.5 0.0 copy-start.2
  45.5 30.9 %all_to_all.31.fetched_ref = bf16[16,264,128]{2,1,0:T(8,128)(2,1)S(1)} all-to-all(bf16[16,264,128]{2,1,0:T(8,128)(2,1)S(1)} %get-tuple-element.23), channel_id=1, replica_groups={{0,8,1,9,2,10,3,11,4,12,5,13,6,14,7,15},{16,24,17,25,18,26,19,27,20,28,..., dimensions={0} | all-to-all | bytes 2162688 | tf_op jit(solution)/shard_map/all_to_all | solution.py:396
  76.4 0.0 copy-done
  76.4 0.0 copy-done.1
  76.4 0.0 copy-done.2
  76.4 4.9 %pairs.2 = (bf16[16,264,128]{2,1,0:T(8,128)(2,1)S(1)}, f32[64,1024]{1,0:T(8,128)S(1)}, f32[64,128]{1,0:T(8,128)S(1)}) custom-call(s32[128]{0:T(128)S(1)} %copy-done.2, bf16[16,264,128]{2,1,0:T(8,128)(2,1)S(1)} %all_to_all.31.fetched_ref, f32[64,1024]{1,0:T(8,128)S(1)} %bitcast.4, f32[64,128]{1,0:T(8,128)S(1)} %get-tuple-element.24.beta_ref.beta_before_ref.refs_4_, ...), custom_call_target="tpu_custom_call" | custom-call | flops 536870912 | bytes 8388608 | tf_op jit(solution)/shard_map/pairs/pallas_call | solution.py:422
  81.2 30.7 %all_to_all.32.arrived_ref = bf16[16,264,128]{2,1,0:T(8,128)(2,1)S(1)} all-to-all(bf16[16,264,128]{2,1,0:T(8,128)(2,1)S(1)} %get-tuple-element.25), channel_id=1, replica_groups={{0,8,1,9,2,10,3,11,4,12,5,13,6,14,7,15},{16,24,17,25,18,26,19,27,20,28,..., dimensions={0} | all-to-all | bytes 2162688 | tf_op jit(solution)/shard_map/all_to_all | solution.py:396
  112.0 2.4 %cells.1 = (f32[64,8192]{1,0:T(8,128)S(1)}, f32[64,128]{1,0:T(8,128)S(1)}, bf16[16,264,128]{2,1,0:T(8,128)(2,1)S(1)}) custom-call(s32[16,128]{1,0:T(8,128)S(1)} %get-tuple-element.21.asked_ref, bf16[16,264,128]{2,1,0:T(8,128)(2,1)S(1)} %all_to_all.32.arrived_ref, f32[64,8192]{1,0:T(8,128)S(1)} %get-tuple-element.26.before_ref.refs_0_, ...), custom_call_target="tpu_custom_call" | custom-call | bytes 8388608 | tf_op jit(solution)/shard_map/cells/pallas_call | solution.py:429
  114.4 30.7 %all_to_all.33.fetched_ref = bf16[16,264,128]{2,1,0:T(8,128)(2,1)S(1)} all-to-all(bf16[16,264,128]{2,1,0:T(8,128)(2,1)S(1)} %get-tuple-element.28), channel_id=1, replica_groups={{0,8,1,9,2,10,3,11,4,12,5,13,6,14,7,15},{16,24,17,25,18,26,19,27,20,28,..., dimensions={0} | all-to-all | bytes 2162688 | tf_op jit(solution)/shard_map/all_to_all | solution.py:396
  145.1 5.5 %pairs.3 = (bf16[16,264,128]{2,1,0:T(8,128)(2,1)S(1)}, f32[64,1024]{1,0:T(8,128)}, f32[64,128]{1,0:T(8,128)S(1)}) custom-call(s32[128]{0:T(128)S(1)} %copy-done.2, bf16[16,264,128]{2,1,0:T(8,128)(2,1)S(1)} %all_to_all.33.fetched_ref, f32[64,1024]{1,0:T(8,128)S(1)} %get-tuple-element.29.data_ref, f32[64,128]{1,0:T(8,128)S(1)} %get-tuple-element.30.beta_ref.refs_5_, ...), custom_call_target="tpu_custom_call" | custom-call | flops 536870912 | bytes 8388608 | tf_op jit(solution)/shard_map/pairs/pallas_call | solution.py:422
  150.6 30.7 %all_to_all.34.arrived_ref = bf16[16,264,128]{2,1,0:T(8,128)(2,1)S(1)} all-to-all(bf16[16,264,128]{2,1,0:T(8,128)(2,1)S(1)} %get-tuple-element.31), channel_id=1, replica_groups={{0,8,1,9,2,10,3,11,4,12,5,13,6,14,7,15},{16,24,17,25,18,26,19,27,20,28,..., dimensions={0} | all-to-all | bytes 2162688 | tf_op jit(solution)/shard_map/all_to_all | solution.py:396
  181.3 2.7 %cells_last.1 = (f32[64,8192]{1,0:T(8,128)S(1)}, f32[64,128]{1,0:T(8,128)S(1)}, f32[16,8,128]{2,1,0:T(8,128)S(1)}, f32[64,8192]{1,0:T(8,128)}) custom-call(s32[16,128]{1,0:T(8,128)S(1)} %get-tuple-element.21.asked_ref, bf16[16,264,128]{2,1,0:T(8,128)(2,1)S(1)} %all_to_all.34.arrived_ref, f32[64,8192]{1,0:T(8,128)S(1)} %get-tuple-element.26.before_ref.refs_0_, ...), custom_call_target="tpu_custom_call" | custom-call | bytes 10485760 | tf_op jit(solution)/shard_map/cells_last/pallas_call | solution.py:435
  184.0 9.3 %all_to_all.35.tails_ref = f32[16,8,128]{2,1,0:T(8,128)S(1)} all-to-all(f32[16,8,128]{2,1,0:T(8,128)S(1)} %get-tuple-element.35), channel_id=1, replica_groups={{0,8,1,9,2,10,3,11,4,12,5,13,6,14,7,15},{16,24,17,25,18,26,19,27,20,28,..., dimensions={0} | all-to-all | bytes 131072 | tf_op jit(solution)/shard_map/all_to_all | solution.py:396
  193.3 1.5 model.1
Async XLA Ops:
  7.0 69.3 %copy-start = (bf16[8,16,128,128]{3,2,1,0:T(8,128)(2,1)S(1)}, bf16[8,16,128,128]{3,2,1,0:T(8,128)(2,1)}, u32[]{:S(2)}) copy-start(bf16[8,16,128,128]{3,2,1,0:T(8,128)(2,1)} %rays_ref.3) | copy-start | bytes 12582916
  45.5 30.9 %copy-start.1 = (f32[1024,64]{0,1:T(8,128)S(1)}, f32[1024,64]{0,1:T(8,128)}, u32[]{:S(2)}) copy-start(f32[1024,64]{0,1:T(8,128)} %param.7) | copy-start | bytes 786436
  45.5 30.9 %copy-start.2 = (s32[128]{0:T(128)S(1)}, s32[128]{0:T(128)}, u32[]{:S(2)}) copy-start(s32[128]{0:T(128)} %get-tuple-element.22.target_ref) | copy-start | bytes 1540

commit v8 on v6

--- a/solution.py
+++ b/solution.py
@@ -78,7 +78,7 @@
                 total_ref[spot] += part[:, half * BS : (half + 1) * BS]
         return carry
 
-    lax.fori_loop(0, pair_count, one_pair, 0, unroll=2)
+    lax.fori_loop(0, pair_count, one_pair, 0, unroll=4)
 
     def pack(peer, carry):
         for rank in range(BCAP):
@@ -168,7 +168,7 @@
 
 def pair_kernel(
     target_ref, fetched_ref, data_ref, beta_ref, rays_ref,
-    message_ref, raw_ref, alpha_ref, total_ref,
+    message_ref, alpha_ref, raw_ref, total_ref,
 ):
     pair_count, slot_count = rays_ref.shape[:2]
     peers = message_ref.shape[0]
@@ -198,7 +198,7 @@
         raw_ref[:, lanes(pair)] = raw
         return squares + raw * raw
 
-    squares = lax.fori_loop(0, pair_count, one_pair, jnp.zeros((cols, BS), F32), unroll=2)
+    squares = lax.fori_loop(0, pair_count, one_pair, jnp.zeros((cols, BS), F32), unroll=4)
     transposed(raw_ref, rays_ref, lambda pair: None, target_ref, total_ref, message_ref)
     tail = squares_tail(squares).astype(BF16)
     message_ref[:, BCAP * cols :, :] = jnp.broadcast_to(tail[None], (peers, TAIL, BS))
@@ -414,13 +414,16 @@
     current = times
     for step in range(ITERS):
         fetched = exchange(reply_)
-        outgoing, current, alpha = call(
-            pair_kernel, "pairs", [SMEM, VMEM, VMEM, VMEM, VMEM],
-            [message, data, tile], [totals], 2 * flops, 8 << 20,
+        last = step + 1 == ITERS
+        outgoing, alpha, *raw = call(
+            pair_kernel, "pairs_last" if last else "pairs", [SMEM, VMEM, VMEM, VMEM, VMEM],
+            [message, tile] + [data] * (not last), [VMEM(data[0], F32)] * last + [totals],
+            2 * flops, 8 << 20,
         )(target, fetched, current, betas[-1], ray_blocks)
+        current = raw[0] if raw else None
         alphas.append(alpha)
         arrived = exchange(outgoing)
-        if step + 1 < ITERS:
+        if not last:
             model, beta, reply_ = call(
                 cell_kernel, "cells", [SMEM] + [VMEM] * 4, [whole, tile, message], (), 0, 8 << 20
             )(asked, arrived, models[-1], alpha, betas[-1])

time: 195 us -> 193 us (0.990)
  Pallas kernels: 25.9 us -> 23.3 us
    pallas_call x2, Pallas kernels: 10.3 us -> 8.14 us  [on_device(): call(pair_kernel, 'pairs_last' if last else 'pairs', [SMEM, VMEM, VMEM, V...]
where the time goes in v8:
time: 193 us; the launch traced here: 192 us
  blocking collectives  168 us (87%)
  Pallas kernels  23.3 us (12%)
    all_to_all x6, blocking collectives, exchange(): lax.all_to_all(values, 'pair', split_axis=0, concat_axis=0, tiled=True)  168 us
    pallas_call x2, Pallas kernels, on_device(): call(pair_kernel, 'pairs_last' if last else 'pairs', [SMEM, VMEM, VMEM, V...  8.14 us
    pallas_call x1, Pallas kernels, on_device(): call(start_kernel, 'start', [HBM, HBM, HBM, HBM], [message, ((slots,), jn...  5.72 us

profile of v8, /device:TPU:0, one launch (start us, length us, event | category | flops | bytes accessed | tf_op | source)
XLA Modules:
  0.0 192.4 jit_solution(16529142573900590679)
XLA Ops:
  0.6 5.7 %start.1 = (bf16[16,264,128]{2,1,0:T(8,128)(2,1)}, s32[128]{0:T(128)}) custom-call(s32[8,16]{1,0:T(8,128)} %cells_hbm.1, s32[8]{0:T(128)} %counts_hbm.1, f32[64,1024]{1,0:T(8,128)} %bitcast.3, bf16[8,16,128,128]{3,2,1,0:T(8,128)(2,1)} %rays_ref.3), custom_call_target="tpu_custom_call" | custom-call | flops 268435456 | bytes 6291456 | tf_op jit(solution)/shard_map/start/pallas_call | solution.py:395
  6.4 0.0 copy-start
  6.4 35.7 %all_to_all.30.arrived_ref = bf16[16,264,128]{2,1,0:T(8,128)(2,1)S(1)} all-to-all(bf16[16,264,128]{2,1,0:T(8,128)(2,1)} %get-tuple-element.20), channel_id=1, replica_groups=mesh['groups'=2,'pair'=16] {'pair'}, dimensions={0} | all-to-all | bytes 2162688 | tf_op jit(solution)/shard_map/all_to_all | solution.py:393
  42.0 2.7 %cells_first.1 = (f32[64,8192]{1,0:T(8,128)S(1)}, f32[64,128]{1,0:T(8,128)S(1)}, bf16[16,264,128]{2,1,0:T(8,128)(2,1)S(1)}, s32[16,128]{1,0:T(8,128)S(1)}) custom-call(bf16[16,264,128]{2,1,0:T(8,128)(2,1)S(1)} %all_to_all.30.arrived_ref), custom_call_target="tpu_custom_call" | custom-call | bytes 6291456 | tf_op jit(solution)/shard_map/cells_first/pallas_call | solution.py:407
  44.8 0.0 copy-start.1
  44.8 0.0 copy-start.2
  44.8 30.9 %all_to_all.31.fetched_ref = bf16[16,264,128]{2,1,0:T(8,128)(2,1)S(1)} all-to-all(bf16[16,264,128]{2,1,0:T(8,128)(2,1)S(1)} %get-tuple-element.23), channel_id=1, replica_groups=mesh['groups'=2,'pair'=16] {'pair'}, dimensions={0} | all-to-all | bytes 2162688 | tf_op jit(solution)/shard_map/all_to_all | solution.py:393
  75.6 0.0 copy-done
  75.7 0.0 copy-done.1
  75.7 0.0 copy-done.2
  75.7 4.1 %pairs.1 = (bf16[16,264,128]{2,1,0:T(8,128)(2,1)S(1)}, f32[64,128]{1,0:T(8,128)S(1)}, f32[64,1024]{1,0:T(8,128)S(1)}) custom-call(s32[128]{0:T(128)S(1)} %copy-done.2, bf16[16,264,128]{2,1,0:T(8,128)(2,1)S(1)} %all_to_all.31.fetched_ref, f32[64,1024]{1,0:T(8,128)S(1)} %bitcast.4, f32[64,128]{1,0:T(8,128)S(1)} %get-tuple-element.24.beta_ref.beta_before_ref.refs_4_, ...), custom_call_target="tpu_custom_call" | custom-call | flops 536870912 | bytes 8388608 | tf_op jit(solution)/shard_map/pairs/pallas_call | solution.py:418
  79.7 30.8 %all_to_all.32.arrived_ref = bf16[16,264,128]{2,1,0:T(8,128)(2,1)S(1)} all-to-all(bf16[16,264,128]{2,1,0:T(8,128)(2,1)S(1)} %get-tuple-element.25), channel_id=1, replica_groups=mesh['groups'=2,'pair'=16] {'pair'}, dimensions={0} | all-to-all | bytes 2162688 | tf_op jit(solution)/shard_map/all_to_all | solution.py:393
  110.5 2.4 %cells.1 = (f32[64,8192]{1,0:T(8,128)S(1)}, f32[64,128]{1,0:T(8,128)S(1)}, bf16[16,264,128]{2,1,0:T(8,128)(2,1)S(1)}) custom-call(s32[16,128]{1,0:T(8,128)S(1)} %get-tuple-element.21.asked_ref, bf16[16,264,128]{2,1,0:T(8,128)(2,1)S(1)} %all_to_all.32.arrived_ref, f32[64,8192]{1,0:T(8,128)S(1)} %get-tuple-element.26.before_ref.refs_0_, ...), custom_call_target="tpu_custom_call" | custom-call | bytes 8388608 | tf_op jit(solution)/shard_map/cells/pallas_call | solution.py:427
  112.9 30.7 %all_to_all.33.fetched_ref = bf16[16,264,128]{2,1,0:T(8,128)(2,1)S(1)} all-to-all(bf16[16,264,128]{2,1,0:T(8,128)(2,1)S(1)} %get-tuple-element.28), channel_id=1, replica_groups=mesh['groups'=2,'pair'=16] {'pair'}, dimensions={0} | all-to-all | bytes 2162688 | tf_op jit(solution)/shard_map/all_to_all | solution.py:393
  143.6 4.1 %pairs_last.1 = (bf16[16,264,128]{2,1,0:T(8,128)(2,1)S(1)}, f32[64,128]{1,0:T(8,128)S(1)}) custom-call(s32[128]{0:T(128)S(1)} %copy-done.2, bf16[16,264,128]{2,1,0:T(8,128)(2,1)S(1)} %all_to_all.33.fetched_ref, f32[64,1024]{1,0:T(8,128)S(1)} %get-tuple-element.29.data_ref, f32[64,128]{1,0:T(8,128)S(1)} %get-tuple-element.30.beta_ref.refs_5_, ...), custom_call_target="tpu_custom_call" | custom-call | flops 536870912 | bytes 8388608 | tf_op jit(solution)/shard_map/pairs_last/pallas_call | solution.py:418
  147.7 30.7 %all_to_all.34.arrived_ref = bf16[16,264,128]{2,1,0:T(8,128)(2,1)S(1)} all-to-all(bf16[16,264,128]{2,1,0:T(8,128)(2,1)S(1)} %get-tuple-element.31), channel_id=1, replica_groups=mesh['groups'=2,'pair'=16] {'pair'}, dimensions={0} | all-to-all | bytes 2162688 | tf_op jit(solution)/shard_map/all_to_all | solution.py:393
  178.5 2.7 %cells_last.1 = (f32[64,8192]{1,0:T(8,128)S(1)}, f32[64,128]{1,0:T(8,128)S(1)}, f32[16,8,128]{2,1,0:T(8,128)S(1)}, f32[64,8192]{1,0:T(8,128)}) custom-call(s32[16,128]{1,0:T(8,128)S(1)} %get-tuple-element.21.asked_ref, bf16[16,264,128]{2,1,0:T(8,128)(2,1)S(1)} %all_to_all.34.arrived_ref, f32[64,8192]{1,0:T(8,128)S(1)} %get-tuple-element.26.before_ref.refs_0_, ...), custom_call_target="tpu_custom_call" | custom-call | bytes 10485760 | tf_op jit(solution)/shard_map/cells_last/pallas_call | solution.py:433
  181.2 9.6 %all_to_all.35.tails_ref = f32[16,8,128]{2,1,0:T(8,128)S(1)} all-to-all(f32[16,8,128]{2,1,0:T(8,128)S(1)} %get-tuple-element.35), channel_id=1, replica_groups=mesh['groups'=2,'pair'=16] {'pair'}, dimensions={0} | all-to-all | bytes 131072 | tf_op jit(solution)/shard_map/all_to_all | solution.py:393
  190.8 1.5 model.1
Async XLA Ops:
  6.4 69.3 %copy-start = (bf16[8,16,128,128]{3,2,1,0:T(8,128)(2,1)S(1)}, bf16[8,16,128,128]{3,2,1,0:T(8,128)(2,1)}, u32[]{:S(2)}) copy-start(bf16[8,16,128,128]{3,2,1,0:T(8,128)(2,1)} %rays_ref.3) | copy-start | bytes 12582916
  44.8 30.9 %copy-start.1 = (f32[1024,64]{0,1:T(8,128)S(1)}, f32[1024,64]{0,1:T(8,128)}, u32[]{:S(2)}) copy-start(f32[1024,64]{0,1:T(8,128)} %param.7) | copy-start | bytes 786436
  44.8 30.9 %copy-start.2 = (s32[128]{0:T(128)S(1)}, s32[128]{0:T(128)}, u32[]{:S(2)}) copy-start(s32[128]{0:T(128)} %get-tuple-element.22.target_ref) | copy-start | bytes 1540

commit v9 on v8

--- a/solution.py
+++ b/solution.py
@@ -78,7 +78,7 @@
                 total_ref[spot] += part[:, half * BS : (half + 1) * BS]
         return carry
 
-    lax.fori_loop(0, pair_count, one_pair, 0, unroll=4)
+    lax.fori_loop(0, pair_count, one_pair, 0, unroll=True)
 
     def pack(peer, carry):
         for rank in range(BCAP):
@@ -87,7 +87,7 @@
             ].astype(BF16)
         return carry
 
-    lax.fori_loop(0, peers, pack, 0, unroll=2)
+    lax.fori_loop(0, peers, pack, 0, unroll=True)
 
 
 def start_kernel(
@@ -198,7 +198,7 @@
         raw_ref[:, lanes(pair)] = raw
         return squares + raw * raw
 
-    squares = lax.fori_loop(0, pair_count, one_pair, jnp.zeros((cols, BS), F32), unroll=4)
+    squares = lax.fori_loop(0, pair_count, one_pair, jnp.zeros((cols, BS), F32), unroll=True)
     transposed(raw_ref, rays_ref, lambda pair: None, target_ref, total_ref, message_ref)
     tail = squares_tail(squares).astype(BF16)
     message_ref[:, BCAP * cols :, :] = jnp.broadcast_to(tail[None], (peers, TAIL, BS))
@@ -215,7 +215,7 @@
             model_ref[:, where] += block.astype(F32)
         return carry
 
-    lax.fori_loop(0, peers, add, 0, unroll=2)
+    lax.fori_loop(0, peers, add, 0, unroll=True)
 
 
 def reply(squares, scale, asked_ref, model_ref, out_ref):
@@ -230,7 +230,7 @@
             out_ref[peer, rank * cols : (rank + 1) * cols, :] = block.astype(BF16)
         return carry
 
-    lax.fori_loop(0, peers, one_peer, 0, unroll=2)
+    lax.fori_loop(0, peers, one_peer, 0, unroll=True)
 
 
 def squares_of(model_ref):

time: 193 us -> 191 us (0.990)
  no operation moved by 1% of the time
where the time goes in v9:
time: 191 us
  blocking collectives  168 us (88%)
  Pallas kernels  21.5 us (11%)
    all_to_all x6, blocking collectives, exchange(): lax.all_to_all(values, 'pair', split_axis=0, concat_axis=0, tiled=True)  168 us
    pallas_call x2, Pallas kernels, on_device(): call(pair_kernel, 'pairs_last' if last else 'pairs', [SMEM, VMEM, VMEM, V...  6.88 us
    pallas_call x1, Pallas kernels, on_device(): call(start_kernel, 'start', [HBM, HBM, HBM, HBM], [message, ((slots,), jn...  5.64 us

profile of v9, /device:TPU:0, one launch (start us, length us, event | category | flops | bytes accessed | tf_op | source)
XLA Modules:
  0.0 190.6 jit_solution(14463725425941059523)
XLA Ops:
  0.6 5.6 %start.1 = (bf16[16,264,128]{2,1,0:T(8,128)(2,1)}, s32[128]{0:T(128)}) custom-call(s32[8,16]{1,0:T(8,128)} %cells_hbm.1, s32[8]{0:T(128)} %counts_hbm.1, f32[64,1024]{1,0:T(8,128)} %bitcast.3, bf16[8,16,128,128]{3,2,1,0:T(8,128)(2,1)} %rays_ref.3), custom_call_target="tpu_custom_call" | custom-call | flops 268435456 | bytes 6291456 | tf_op jit(solution)/shard_map/start/pallas_call | solution.py:395
  6.3 0.0 copy-start
  6.3 35.6 %all_to_all.30.arrived_ref = bf16[16,264,128]{2,1,0:T(8,128)(2,1)S(1)} all-to-all(bf16[16,264,128]{2,1,0:T(8,128)(2,1)} %get-tuple-element.20), channel_id=1, replica_groups=mesh['groups'=2,'pair'=16] {'pair'}, dimensions={0} | all-to-all | bytes 2162688 | tf_op jit(solution)/shard_map/all_to_all | solution.py:393
  41.9 2.6 %cells_first.1 = (f32[64,8192]{1,0:T(8,128)S(1)}, f32[64,128]{1,0:T(8,128)S(1)}, bf16[16,264,128]{2,1,0:T(8,128)(2,1)S(1)}, s32[16,128]{1,0:T(8,128)S(1)}) custom-call(bf16[16,264,128]{2,1,0:T(8,128)(2,1)S(1)} %all_to_all.30.arrived_ref), custom_call_target="tpu_custom_call" | custom-call | bytes 6291456 | tf_op jit(solution)/shard_map/cells_first/pallas_call | solution.py:407
  44.5 0.0 copy-start.1
  44.5 0.0 copy-start.2
  44.5 30.9 %all_to_all.31.fetched_ref = bf16[16,264,128]{2,1,0:T(8,128)(2,1)S(1)} all-to-all(bf16[16,264,128]{2,1,0:T(8,128)(2,1)S(1)} %get-tuple-element.23), channel_id=1, replica_groups=mesh['groups'=2,'pair'=16] {'pair'}, dimensions={0} | all-to-all | bytes 2162688 | tf_op jit(solution)/shard_map/all_to_all | solution.py:393
  75.4 0.0 copy-done
  75.4 0.0 copy-done.1
  75.4 0.0 copy-done.2
  75.4 3.4 %pairs.1 = (bf16[16,264,128]{2,1,0:T(8,128)(2,1)S(1)}, f32[64,128]{1,0:T(8,128)S(1)}, f32[64,1024]{1,0:T(8,128)S(1)}) custom-call(s32[128]{0:T(128)S(1)} %copy-done.2, bf16[16,264,128]{2,1,0:T(8,128)(2,1)S(1)} %all_to_all.31.fetched_ref, f32[64,1024]{1,0:T(8,128)S(1)} %bitcast.4, f32[64,128]{1,0:T(8,128)S(1)} %get-tuple-element.24.beta_ref.beta_before_ref.refs_4_, ...), custom_call_target="tpu_custom_call" | custom-call | flops 536870912 | bytes 8388608 | tf_op jit(solution)/shard_map/pairs/pallas_call | solution.py:418
  78.9 30.7 %all_to_all.32.arrived_ref = bf16[16,264,128]{2,1,0:T(8,128)(2,1)S(1)} all-to-all(bf16[16,264,128]{2,1,0:T(8,128)(2,1)S(1)} %get-tuple-element.25), channel_id=1, replica_groups=mesh['groups'=2,'pair'=16] {'pair'}, dimensions={0} | all-to-all | bytes 2162688 | tf_op jit(solution)/shard_map/all_to_all | solution.py:393
  109.6 2.2 %cells.1 = (f32[64,8192]{1,0:T(8,128)S(1)}, f32[64,128]{1,0:T(8,128)S(1)}, bf16[16,264,128]{2,1,0:T(8,128)(2,1)S(1)}) custom-call(s32[16,128]{1,0:T(8,128)S(1)} %get-tuple-element.21.asked_ref, bf16[16,264,128]{2,1,0:T(8,128)(2,1)S(1)} %all_to_all.32.arrived_ref, f32[64,8192]{1,0:T(8,128)S(1)} %get-tuple-element.26.before_ref.refs_0_, ...), custom_call_target="tpu_custom_call" | custom-call | bytes 8388608 | tf_op jit(solution)/shard_map/cells/pallas_call | solution.py:427
  111.8 30.7 %all_to_all.33.fetched_ref = bf16[16,264,128]{2,1,0:T(8,128)(2,1)S(1)} all-to-all(bf16[16,264,128]{2,1,0:T(8,128)(2,1)S(1)} %get-tuple-element.28), channel_id=1, replica_groups=mesh['groups'=2,'pair'=16] {'pair'}, dimensions={0} | all-to-all | bytes 2162688 | tf_op jit(solution)/shard_map/all_to_all | solution.py:393
  142.6 3.4 %pairs_last.1 = (bf16[16,264,128]{2,1,0:T(8,128)(2,1)S(1)}, f32[64,128]{1,0:T(8,128)S(1)}) custom-call(s32[128]{0:T(128)S(1)} %copy-done.2, bf16[16,264,128]{2,1,0:T(8,128)(2,1)S(1)} %all_to_all.33.fetched_ref, f32[64,1024]{1,0:T(8,128)S(1)} %get-tuple-element.29.data_ref, f32[64,128]{1,0:T(8,128)S(1)} %get-tuple-element.30.beta_ref.refs_5_, ...), custom_call_target="tpu_custom_call" | custom-call | flops 536870912 | bytes 8388608 | tf_op jit(solution)/shard_map/pairs_last/pallas_call | solution.py:418
  146.0 30.7 %all_to_all.34.arrived_ref = bf16[16,264,128]{2,1,0:T(8,128)(2,1)S(1)} all-to-all(bf16[16,264,128]{2,1,0:T(8,128)(2,1)S(1)} %get-tuple-element.31), channel_id=1, replica_groups=mesh['groups'=2,'pair'=16] {'pair'}, dimensions={0} | all-to-all | bytes 2162688 | tf_op jit(solution)/shard_map/all_to_all | solution.py:393
  176.7 2.6 %cells_last.1 = (f32[64,8192]{1,0:T(8,128)S(1)}, f32[64,128]{1,0:T(8,128)S(1)}, f32[16,8,128]{2,1,0:T(8,128)S(1)}, f32[64,8192]{1,0:T(8,128)}) custom-call(s32[16,128]{1,0:T(8,128)S(1)} %get-tuple-element.21.asked_ref, bf16[16,264,128]{2,1,0:T(8,128)(2,1)S(1)} %all_to_all.34.arrived_ref, f32[64,8192]{1,0:T(8,128)S(1)} %get-tuple-element.26.before_ref.refs_0_, ...), custom_call_target="tpu_custom_call" | custom-call | bytes 10485760 | tf_op jit(solution)/shard_map/cells_last/pallas_call | solution.py:433
  179.4 9.7 %all_to_all.35.tails_ref = f32[16,8,128]{2,1,0:T(8,128)S(1)} all-to-all(f32[16,8,128]{2,1,0:T(8,128)S(1)} %get-tuple-element.35), channel_id=1, replica_groups=mesh['groups'=2,'pair'=16] {'pair'}, dimensions={0} | all-to-all | bytes 131072 | tf_op jit(solution)/shard_map/all_to_all | solution.py:393
  189.1 1.5 model.1
Async XLA Ops:
  6.3 69.1 %copy-start = (bf16[8,16,128,128]{3,2,1,0:T(8,128)(2,1)S(1)}, bf16[8,16,128,128]{3,2,1,0:T(8,128)(2,1)}, u32[]{:S(2)}) copy-start(bf16[8,16,128,128]{3,2,1,0:T(8,128)(2,1)} %rays_ref.3) | copy-start | bytes 12582916
  44.5 30.9 %copy-start.1 = (f32[1024,64]{0,1:T(8,128)S(1)}, f32[1024,64]{0,1:T(8,128)}, u32[]{:S(2)}) copy-start(f32[1024,64]{0,1:T(8,128)} %param.7) | copy-start | bytes 786436
  44.5 30.9 %copy-start.2 = (s32[128]{0:T(128)S(1)}, s32[128]{0:T(128)}, u32[]{:S(2)}) copy-start(s32[128]{0:T(128)} %get-tuple-element.22.target_ref) | copy-start | bytes 1540

commit v10 on v9

--- a/solution.py
+++ b/solution.py
@@ -39,9 +39,8 @@
     )
 
 
-def norm_of_tails(message_ref, cols):
-    tails = message_ref[:, BCAP * cols :, :].astype(F32)
-    summed = jnp.sum(tails, axis=0)
+def norm_of_tails(message_refs, cols):
+    summed = sum(message_ref[BCAP * cols :, :].astype(F32) for message_ref in message_refs)
     row = summed[0:1] + summed[1:2] + summed[2:3]
     column = jnp.sum(jnp.where(diagonal(cols), row, 0.0), axis=1, keepdims=True)
     return jnp.broadcast_to(jnp.sqrt(column + EPS), (cols, BS))
@@ -51,11 +50,10 @@
     return pl.ds(pl.multiple_of(block * BS, BS), BS)
 
 
-def transposed(data_ref, rays_ref, before, target_ref, total_ref, message_ref):
+def transposed(data_ref, rays_ref, before, target_ref, total_ref, message_refs):
     pair_count, slot_count = rays_ref.shape[:2]
     cols = data_ref.shape[0]
-    peers = message_ref.shape[0]
-    spots = peers * BCAP
+    spots = len(message_refs) * BCAP
 
     def clear(index, carry):
         total_ref[index] = jnp.zeros((cols, BS), F32)
@@ -80,22 +78,18 @@
 
     lax.fori_loop(0, pair_count, one_pair, 0, unroll=True)
 
-    def pack(peer, carry):
+    for peer, message_ref in enumerate(message_refs):
         for rank in range(BCAP):
-            message_ref[peer, rank * cols : (rank + 1) * cols, :] = total_ref[
+            message_ref[rank * cols : (rank + 1) * cols, :] = total_ref[
                 peer * BCAP + rank
             ].astype(BF16)
-        return carry
-
-    lax.fori_loop(0, peers, pack, 0, unroll=True)
-
-
-def start_kernel(
-    cells_hbm, counts_hbm, times_hbm, rays_hbm, message_ref, target_ref,
-    total_ref, table_ref, used_ref, cells_ref, counts_ref, times_ref, rays_ref, sems, ray_sems,
-):
+
+
+def start_kernel(peers, me_ref, cells_hbm, counts_hbm, times_hbm, rays_hbm, *refs):
+    message_refs = refs[:peers]
+    target_ref, total_ref, table_ref, used_ref, cells_ref, counts_ref = refs[peers : peers + 6]
+    times_ref, rays_ref, sems, ray_sems = refs[peers + 6 :]
     pair_count, slot_count = rays_ref.shape[:2]
-    peers = message_ref.shape[0]
     cols = times_ref.shape[0]
     owned = CELL_DEV // BS
     copies = [
@@ -130,7 +124,8 @@
         count = counts_ref[pair]
         for slot in range(slot_count):
             cell = cells_ref[pair, slot]
-            owner = cell // owned
+            apart = (cell // owned) ^ me_ref[0]
+            owner = apart * 2 - jnp.where(apart < peers // 2, 0, peers - 1)
             local = cell % owned
             used = used_ref[owner]
             rank = used
@@ -146,7 +141,7 @@
         find_places(pair)
         ray_copy(pair).wait()
 
-    transposed(times_ref, rays_ref, before, target_ref, total_ref, message_ref)
+    transposed(times_ref, rays_ref, before, target_ref, total_ref, message_refs)
     squares = jnp.zeros((cols, BS), F32)
     for pair in range(pair_count):
         part = times_ref[:, pair * BS : (pair + 1) * BS]
@@ -155,26 +150,25 @@
     place = lax.broadcasted_iota(jnp.int32, (TAIL, BS), 0)
     lane = lax.broadcasted_iota(jnp.int32, (TAIL, BS), 1)
 
-    def ask(peer, carry):
+    for peer, message_ref in enumerate(message_refs):
         rows = tail
         for rank in range(BCAP):
             asked = table_ref[peer * BCAP + rank].astype(F32)
             rows = jnp.where((place == 3) & (lane == rank), asked, rows)
-        message_ref[peer, BCAP * cols :, :] = rows.astype(BF16)
-        return carry
-
-    lax.fori_loop(0, peers, ask, 0)
-
-
-def pair_kernel(
-    target_ref, fetched_ref, data_ref, beta_ref, rays_ref,
-    message_ref, alpha_ref, raw_ref, total_ref,
-):
+        message_ref[BCAP * cols :, :] = rows.astype(BF16)
+
+
+def pair_kernel(peers, target_ref, *refs):
+    fetched_refs = refs[:peers]
+    data_ref, beta_ref, rays_ref = refs[peers : peers + 3]
+    message_refs = refs[peers + 3 : 2 * peers + 3]
+    alpha_ref, raw_ref, total_ref, fetched_ref = refs[2 * peers + 3 :]
     pair_count, slot_count = rays_ref.shape[:2]
-    peers = message_ref.shape[0]
     cols = data_ref.shape[0]
     spots = peers * BCAP
-    alpha = norm_of_tails(fetched_ref, cols)
+    for peer in range(peers):
+        fetched_ref[peer] = fetched_refs[peer][: BCAP * cols, :]
+    alpha = norm_of_tails(fetched_refs, cols)
     alpha_ref[...] = alpha
     beta = beta_ref[...]
     model_scale = 1.0 / (alpha * beta)
@@ -199,38 +193,28 @@
         return squares + raw * raw
 
     squares = lax.fori_loop(0, pair_count, one_pair, jnp.zeros((cols, BS), F32), unroll=True)
-    transposed(raw_ref, rays_ref, lambda pair: None, target_ref, total_ref, message_ref)
+    transposed(raw_ref, rays_ref, lambda pair: None, target_ref, total_ref, message_refs)
     tail = squares_tail(squares).astype(BF16)
-    message_ref[:, BCAP * cols :, :] = jnp.broadcast_to(tail[None], (peers, TAIL, BS))
-
-
-def gathered(arrived_ref, asked_ref, model_ref):
-    peers = arrived_ref.shape[0]
+    for message_ref in message_refs:
+        message_ref[BCAP * cols :, :] = tail
+
+
+def gathered(arrived_refs, asked_ref, model_ref):
     cols = model_ref.shape[0]
-
-    def add(peer, carry):
+    for peer, arrived_ref in enumerate(arrived_refs):
         for rank in range(BCAP):
             where = lanes(asked_ref[peer, rank])
-            block = arrived_ref[peer, rank * cols : (rank + 1) * cols, :]
-            model_ref[:, where] += block.astype(F32)
-        return carry
-
-    lax.fori_loop(0, peers, add, 0, unroll=True)
-
-
-def reply(squares, scale, asked_ref, model_ref, out_ref):
-    peers = out_ref.shape[0]
+            model_ref[:, where] += arrived_ref[rank * cols : (rank + 1) * cols, :].astype(F32)
+
+
+def reply(squares, scale, asked_ref, model_ref, out_refs):
     cols = model_ref.shape[0]
     tail = squares_tail(squares * scale * scale).astype(BF16)
-    out_ref[:, BCAP * cols :, :] = jnp.broadcast_to(tail[None], (peers, TAIL, BS))
-
-    def one_peer(peer, carry):
+    for peer, out_ref in enumerate(out_refs):
+        out_ref[BCAP * cols :, :] = tail
         for rank in range(BCAP):
             block = model_ref[:, lanes(asked_ref[peer, rank])]
-            out_ref[peer, rank * cols : (rank + 1) * cols, :] = block.astype(BF16)
-        return carry
-
-    lax.fori_loop(0, peers, one_peer, 0, unroll=True)
+            out_ref[rank * cols : (rank + 1) * cols, :] = block.astype(BF16)
 
 
 def squares_of(model_ref):
@@ -243,17 +227,22 @@
     return lax.fori_loop(0, cells // BS, one_block, jnp.zeros((cols, BS), F32), unroll=8)
 
 
-def first_cell_kernel(arrived_ref, model_ref, beta_ref, out_ref, asked_ref, table_ref, sem):
+def first_cell_kernel(peers, *refs):
+    arrived_refs, out_refs = refs[:peers], refs[peers + 2 : 2 * peers + 2]
+    model_ref, beta_ref = refs[peers : peers + 2]
+    asked_ref, table_ref, sem = refs[2 * peers + 2 :]
     cols, cells = model_ref.shape
-    table_ref[...] = arrived_ref[:, BCAP * cols :, :].astype(F32)[:, 3, :].astype(jnp.int32)
+    for peer in range(peers):
+        tail = arrived_refs[peer][BCAP * cols :, :].astype(F32)
+        table_ref[peer : peer + 1, :] = tail[3:4].astype(jnp.int32)
     copy = pltpu.make_async_copy(table_ref, asked_ref, sem)
     copy.start()
-    beta = norm_of_tails(arrived_ref, cols)
+    beta = norm_of_tails(arrived_refs, cols)
     beta_ref[...] = beta
     model_ref[...] = jnp.zeros((cols, cells), F32)
     copy.wait()
-    gathered(arrived_ref, asked_ref, model_ref)
-    reply(squares_of(model_ref), 1.0 / beta, asked_ref, model_ref, out_ref)
+    gathered(arrived_refs, asked_ref, model_ref)
+    reply(squares_of(model_ref), 1.0 / beta, asked_ref, model_ref, out_refs)
 
 
 def start_from(before_ref, scale, model_ref):
@@ -264,23 +253,24 @@
     lax.fori_loop(0, model_ref.shape[1] // BS, one_block, 0, unroll=8)
 
 
-def cell_kernel(
-    asked_ref, arrived_ref, before_ref, alpha_ref, beta_before_ref, model_ref, beta_ref, out_ref
-):
-    beta = norm_of_tails(arrived_ref, model_ref.shape[0])
+def cell_kernel(peers, asked_ref, *refs):
+    arrived_refs, out_refs = refs[:peers], refs[peers + 5 :]
+    before_ref, alpha_ref, beta_before_ref, model_ref, beta_ref = refs[peers : peers + 5]
+    beta = norm_of_tails(arrived_refs, model_ref.shape[0])
     beta_ref[...] = beta
     start_from(before_ref, beta * beta / (alpha_ref[...] * beta_before_ref[...]), model_ref)
-    gathered(arrived_ref, asked_ref, model_ref)
-    reply(squares_of(model_ref), 1.0 / beta, asked_ref, model_ref, out_ref)
-
-
-def last_cell_kernel(asked_ref, arrived_ref, *refs):
+    gathered(arrived_refs, asked_ref, model_ref)
+    reply(squares_of(model_ref), 1.0 / beta, asked_ref, model_ref, out_refs)
+
+
+def last_cell_kernel(peers, asked_ref, *refs):
+    arrived_refs, refs = refs[:peers], refs[peers:]
     models = refs[:ITERS]
     alphas = [ref[...] for ref in refs[ITERS : 2 * ITERS]]
     betas = [ref[...] for ref in refs[2 * ITERS : 3 * ITERS]]
     model_ref, beta_ref, out_ref, estimate_hbm, estimate_ref, sems = refs[3 * ITERS :]
     cols, cells = model_ref.shape
-    beta = norm_of_tails(arrived_ref, cols)
+    beta = norm_of_tails(arrived_refs, cols)
     beta_ref[...] = beta
     weights = estimate_weights(betas + [beta], alphas)
     scale = beta * beta / (alphas[-1] * betas[-1])
@@ -306,7 +296,7 @@
             )
         )
         copies[-1].start()
-    gathered(arrived_ref, asked_ref, model_ref)
+    gathered(arrived_refs, asked_ref, model_ref)
     scale = 1.0 / beta
     tail = squares_tail(squares_of(model_ref) * scale * scale)
     out_ref[...] = jnp.broadcast_to(tail[None], out_ref.shape)
@@ -382,7 +372,9 @@
     spots = peers * BCAP
     times = travel_times.T
     cols, pairs = times.shape
-    message = ((peers, BCAP * cols + TAIL, BS), BF16, VMEM)
+    messages = [((BCAP * cols + TAIL, BS), BF16, VMEM)] * peers
+    ins = [VMEM] * peers
+    gathered_blocks = VMEM((peers, BCAP * cols, BS), BF16)
     tile = ((cols, BS), F32, VMEM)
     data = ((cols, pairs), F32, VMEM)
     whole = ((cols, CELL_DEV), F32, VMEM)
@@ -390,11 +382,17 @@
     flops = 2 * slots * BS * BS * cols
 
     def exchange(values):
-        return lax.all_to_all(values, "pair", split_axis=0, concat_axis=0, tiled=True)
-
-    outgoing, target = call(
-        start_kernel, "start", [HBM, HBM, HBM, HBM],
-        [message, ((slots,), jnp.int32, SMEM)],
+        half = peers // 2
+        steps = [i // 2 + i % 2 * half for i in range(peers)]
+        return [values[0]] + [
+            lax.ppermute(value, "pair", [(one, one ^ step) for one in range(peers)])
+            for value, step in zip(values[1:], steps[1:])
+        ]
+
+    me = lax.axis_index("pair").astype(jnp.int32).reshape(1)
+    *outgoing, target = call(
+        functools.partial(start_kernel, peers), "start", [SMEM, HBM, HBM, HBM, HBM],
+        messages + [((slots,), jnp.int32, SMEM)],
         [
             totals, SMEM((spots,), jnp.int32), SMEM((peers,), jnp.int32),
             SMEM(block_cells.shape, jnp.int32), SMEM(block_counts.shape, jnp.int32),
@@ -402,41 +400,44 @@
             pltpu.SemaphoreType.DMA((3,)), pltpu.SemaphoreType.DMA((pair_count,)),
         ],
         flops, 6 << 20, 60 << 20,
-    )(block_cells, block_counts, times, ray_blocks)
+    )(me, block_cells, block_counts, times, ray_blocks)
     arrived = exchange(outgoing)
-    model, beta, reply_, asked = call(
-        first_cell_kernel, "cells_first", [VMEM],
-        [whole, tile, message, ((peers, BS), jnp.int32, SMEM)],
+    model, beta, *replies, asked = call(
+        functools.partial(first_cell_kernel, peers), "cells_first", ins,
+        [whole, tile] + messages + [((peers, BS), jnp.int32, SMEM)],
         [VMEM((peers, BS), jnp.int32), pltpu.SemaphoreType.DMA],
         0, 6 << 20,
-    )(arrived)
+    )(*arrived)
     models, betas, alphas = [model], [beta], []
     current = times
     for step in range(ITERS):
-        fetched = exchange(reply_)
+        fetched = exchange(replies)
         last = step + 1 == ITERS
-        outgoing, alpha, *raw = call(
-            pair_kernel, "pairs_last" if last else "pairs", [SMEM, VMEM, VMEM, VMEM, VMEM],
-            [message, tile] + [data] * (not last), [VMEM(data[0], F32)] * last + [totals],
-            2 * flops, 8 << 20,
-        )(target, fetched, current, betas[-1], ray_blocks)
-        current = raw[0] if raw else None
-        alphas.append(alpha)
-        arrived = exchange(outgoing)
+        made = call(
+            functools.partial(pair_kernel, peers), "pairs_last" if last else "pairs",
+            [SMEM] + ins + [VMEM, VMEM, VMEM], messages + [tile] + [data] * (not last),
+            [VMEM(data[0], F32)] * last + [totals, gathered_blocks], 2 * flops, 8 << 20,
+        )(target, *fetched, current, betas[-1], ray_blocks)
+        alphas.append(made[peers])
+        current = made[-1]
+        arrived = exchange(made[:peers])
         if not last:
-            model, beta, reply_ = call(
-                cell_kernel, "cells", [SMEM] + [VMEM] * 4, [whole, tile, message], (), 0, 8 << 20
-            )(asked, arrived, models[-1], alpha, betas[-1])
+            model, beta, *replies = call(
+                functools.partial(cell_kernel, peers), "cells", [SMEM] + ins + [VMEM] * 3,
+                [whole, tile] + messages, (), 0, 8 << 20,
+            )(asked, *arrived, models[-1], alphas[-1], betas[-1])
             models.append(model)
             betas.append(beta)
     scratch = [VMEM(whole[0], F32), pltpu.SemaphoreType.DMA((CHUNKS,))]
     model, beta, tails, estimate = call(
-        last_cell_kernel, "cells_last", [SMEM] + [VMEM] * (3 * ITERS + 1),
+        functools.partial(last_cell_kernel, peers), "cells_last",
+        [SMEM] + ins + [VMEM] * (3 * ITERS),
         [whole, tile, ((peers, TAIL, BS), F32, VMEM), (whole[0], F32, HBM)], scratch, 0, 10 << 20,
-    )(asked, arrived, *models, *alphas, *betas)
+    )(asked, *arrived, *models, *alphas, *betas)
+    tails = lax.all_to_all(tails, "pair", split_axis=0, concat_axis=0, tiled=True)
     (model_vec,) = call(
         model_kernel, "model", [VMEM, VMEM, VMEM], [(whole[0], F32, HBM)], scratch, 0, 4 << 20
-    )(exchange(tails), beta, model)
+    )(tails, beta, model)
     return (estimate.T, model_vec.T)
 
 

time: 191 us -> 179 us (0.937)
  blocking collectives: 168 us -> 10.6 us
  starting transfers between devices: 0 us -> 98.5 us
  waiting for transfers between devices: 0 us -> 43.3 us
  local copies, waits for them, and re-layouts: 0.02 us -> 3.68 us
    all_to_all x6 -> x1, blocking collectives: 168 us -> 10.6 us  [on_device(): lax.all_to_all(tails, 'pair', split_axis=0, concat_axis=0, tiled=True)]
    ppermute x0 -> x75, starting transfers between devices: none -> 98.5 us  [exchange(): lax.ppermute(value, 'pair', [(one, one ^ step) for one in range(peers)])]
    ppermute x0 -> x75, waiting for transfers between devices: none -> 43.3 us  [exchange(): lax.ppermute(value, 'pair', [(one, one ^ step) for one in range(peers)])]
    unnamed x6 -> x12, local copies, waits for them, and re-layouts: 0.02 us -> 3.68 us
  transfers between devices with their start and end apart: 0 -> 75, of which waited for: 0 -> 28; matrix products, arithmetic and copies ran while one was open for 0% -> 0% of each run, Pallas kernels for 0% -> 0%
where the time goes in v10:
time: 179 us
  starting transfers between devices  98.5 us (55%)
  waiting for transfers between devices  43.3 us (24%)
  Pallas kernels  21.6 us (12%)
  blocking collectives  10.6 us (6%)
  local copies, waits for them, and re-layouts  3.68 us (2%)
    ppermute x75, starting transfers between devices, exchange(): lax.ppermute(value, 'pair', [(one, one ^ step) for one in range(peers)])  98.5 us
    ppermute x75, waiting for transfers between devices, exchange(): lax.ppermute(value, 'pair', [(one, one ^ step) for one in range(peers)])  43.3 us
    all_to_all x1, blocking collectives, on_device(): lax.all_to_all(tails, 'pair', split_axis=0, concat_axis=0, tiled=True)  10.6 us
    pallas_call x2, Pallas kernels, on_device(): call(functools.partial(pair_kernel, peers), 'pairs_last' if last else 'pa...  6.92 us
    pallas_call x1, Pallas kernels, on_device(): call(functools.partial(start_kernel, peers), 'start', [SMEM, HBM, HBM, HB...  5.67 us
    unnamed x12, local copies, waits for them, and re-layouts  3.68 us
  transfers between devices with their start and end apart: 75, of which 28 were waited for; matrix products, arithmetic and copies ran while one was open for 0% of the time, Pallas kernels for 0%

profile of v10, /device:TPU:0, one launch (start us, length us, event | category | flops | bytes accessed | tf_op | source)
XLA Modules:
  0.0 178.6 jit_solution(5043833214288695971)
XLA Ops:
  0.6 5.7 %start.1 = (bf16[264,128]{1,0:T(8,128)(2,1)}, bf16[264,128]{1,0:T(8,128)(2,1)}, bf16[264,128]{1,0:T(8,128)(2,1)}, bf16[264,128]{1,0:T(8,128)(2,1)}, bf16[264,128...) custom-call(s32[1]{0:T(128)} %bitcast.me_ref, ...), custom_call_target="tpu_custom_call" | custom-call | flops 268435456 | bytes 6291456 | tf_op jit(solution)/shard_map/start/pallas_call | solution.py:393
  6.3 4.1 %collective-permute-start = (bf16[264,128]{1,0:T(8,128)(2,1)}, bf16[264,128]{1,0:T(8,128)(2,1)S(1)}, u32[]{:S(2)}, u32[]{:S(2)}) collective-permute-start(bf16[264,128]{1,0:T(8,128)(2,1)} %get-tuple-element.96), channel_id=1, source_target_pairs={{0,8},{1,9},{2,10},{3,11},{4,12},{5,13},{6,14},{7,15},{8,0},{9,1},... | collective-permute-start | bytes 202760 | tf_op jit(solution)/shard_map/ppermute | solution.py:388
  10.7 1.9 %collective-permute-start.3 = (bf16[264,128]{1,0:T(8,128)(2,1)}, bf16[264,128]{1,0:T(8,128)(2,1)S(1)}, u32[]{:S(2)}, u32[]{:S(2)}) collective-permute-start(bf16[264,128]{1,0:T(8,128)(2,1)} %get-tuple-element.99), channel_id=1, source_target_pairs={{0,2},{1,3},{2,0},{3,1},{4,6},{5,7},{6,4},{7,5},{8,10},{9,11},{10,... | collective-permute-start | bytes 202760 | tf_op jit(solution)/shard_map/ppermute | solution.py:388
  12.5 2.4 %collective-permute-start.4 = (bf16[264,128]{1,0:T(8,128)(2,1)}, bf16[264,128]{1,0:T(8,128)(2,1)S(1)}, u32[]{:S(2)}, u32[]{:S(2)}) collective-permute-start(bf16[264,128]{1,0:T(8,128)(2,1)} %get-tuple-element.100), channel_id=1, source_target_pairs={{0,10},{1,11},{2,8},{3,9},{4,14},{5,15},{6,12},{7,13},{8,2},{9,3},... | collective-permute-start | bytes 202760 | tf_op jit(solution)/shard_map/ppermute | solution.py:388
  15.6 2.0 %collective-permute-start.6 = (bf16[264,128]{1,0:T(8,128)(2,1)}, bf16[264,128]{1,0:T(8,128)(2,1)S(1)}, u32[]{:S(2)}, u32[]{:S(2)}) collective-permute-start(bf16[264,128]{1,0:T(8,128)(2,1)} %get-tuple-element.102), channel_id=1, source_target_pairs={{0,11},{1,10},{2,9},{3,8},{4,15},{5,14},{6,13},{7,12},{8,3},{9,2},... | collective-permute-start | bytes 202760 | tf_op jit(solution)/shard_map/ppermute | solution.py:388
  17.6 4.4 %collective-permute-start.7 = (bf16[264,128]{1,0:T(8,128)(2,1)}, bf16[264,128]{1,0:T(8,128)(2,1)S(1)}, u32[]{:S(2)}, u32[]{:S(2)}) collective-permute-start(bf16[264,128]{1,0:T(8,128)(2,1)} %get-tuple-element.103), channel_id=1, source_target_pairs={{0,4},{1,5},{2,6},{3,7},{4,0},{5,1},{6,2},{7,3},{8,12},{9,13},{10,... | collective-permute-start | bytes 202760 | tf_op jit(solution)/shard_map/ppermute | solution.py:388
  22.4 4.4 %collective-permute-start.10 = (bf16[264,128]{1,0:T(8,128)(2,1)}, bf16[264,128]{1,0:T(8,128)(2,1)S(1)}, u32[]{:S(2)}, u32[]{:S(2)}) collective-permute-start(bf16[264,128]{1,0:T(8,128)(2,1)} %get-tuple-element.106), channel_id=1, source_target_pairs={{0,13},{1,12},{2,15},{3,14},{4,9},{5,8},{6,11},{7,10},{8,5},{9,4},... | collective-permute-start | bytes 202760 | tf_op jit(solution)/shard_map/ppermute | solution.py:388
  27.6 1.9 %collective-permute-start.12 = (bf16[264,128]{1,0:T(8,128)(2,1)}, bf16[264,128]{1,0:T(8,128)(2,1)S(1)}, u32[]{:S(2)}, u32[]{:S(2)}) collective-permute-start(bf16[264,128]{1,0:T(8,128)(2,1)} %get-tuple-element.108), channel_id=1, source_target_pairs={{0,14},{1,15},{2,12},{3,13},{4,10},{5,11},{6,8},{7,9},{8,6},{9,7},... | collective-permute-start | bytes 202760 | tf_op jit(solution)/shard_map/ppermute | solution.py:388
  29.7 3.5 %collective-permute-start.14 = (bf16[264,128]{1,0:T(8,128)(2,1)}, bf16[264,128]{1,0:T(8,128)(2,1)S(1)}, u32[]{:S(2)}, u32[]{:S(2)}) collective-permute-start(bf16[264,128]{1,0:T(8,128)(2,1)} %get-tuple-element.110), channel_id=1, source_target_pairs={{0,15},{1,14},{2,13},{3,12},{4,11},{5,10},{6,9},{7,8},{8,7},{9,6},... | collective-permute-start | bytes 202760 | tf_op jit(solution)/shard_map/ppermute | solution.py:388
  33.2 1.8 %collective-permute-done.12.refs_13_ = bf16[264,128]{1,0:T(8,128)(2,1)S(1)} collective-permute-done((bf16[264,128]{1,0:T(8,128)(2,1)}, bf16[264,128]{1,0:T(8,128)(2,1)S(1)}, u32[]{:S(2)}, u32[]{:S(2)}) %collective-permute-start.12) | collective-permute-done | bytes 67616 | tf_op jit(solution)/shard_map/ppermute | solution.py:388
  35.9 1.5 collective-permute-done.14.refs_15_
  38.2 2.5 %cells_first.1 = (f32[64,8192]{1,0:T(8,128)S(1)}, f32[64,128]{1,0:T(8,128)S(1)}, bf16[264,128]{1,0:T(8,128)(2,1)S(1)}, bf16[264,128]{1,0:T(8,128)(2,1)S(1)}, bf1...) custom-call(bf16[264,128]{1,0:T(8,128)(2,1)S(1)} %copy-done.3, ...), custom_call_target="tpu_custom_call" | custom-call | bytes 6291456 | tf_op jit(solution)/shard_map/cells_first/pallas_call | solution.py:405
  41.1 1.2 collective-permute-start.16
  42.3 1.5 collective-permute-start.17
  44.1 2.1 %collective-permute-start.19 = (bf16[264,128]{1,0:T(8,128)(2,1)S(1)}, bf16[264,128]{1,0:T(8,128)(2,1)S(1)}, u32[]{:S(2)}, u32[]{:S(2)}) collective-permute-start(bf16[264,128]{1,0:T(8,128)(2,1)S(1)} %get-tuple-element.118), channel_id=1, source_target_pairs={{0,10},{1,11},{2,8},{3,9},{4,14},{5,15},{6,12},{7,13},{8,2},{9,3},... | collective-permute-start | bytes 202760 | tf_op jit(solution)/shard_map/ppermute | solution.py:388
  46.3 4.3 %collective-permute-done.15.refs_1_ = bf16[264,128]{1,0:T(8,128)(2,1)S(1)} collective-permute-done((bf16[264,128]{1,0:T(8,128)(2,1)S(1)}, bf16[264,128]{1,0:T(8,128)(2,1)S(1)}, u32[]{:S(2)}, u32[]{:S(2)}) %collective-permute-start.15) | collective-permute-done | bytes 67616 | tf_op jit(solution)/shard_map/ppermute | solution.py:388
  51.4 1.2 collective-permute-start.22
  52.6 3.6 %collective-permute-start.23 = (bf16[264,128]{1,0:T(8,128)(2,1)S(1)}, bf16[264,128]{1,0:T(8,128)(2,1)S(1)}, u32[]{:S(2)}, u32[]{:S(2)}) collective-permute-start(bf16[264,128]{1,0:T(8,128)(2,1)S(1)} %get-tuple-element.122), channel_id=1, source_target_pairs={{0,12},{1,13},{2,14},{3,15},{4,8},{5,9},{6,10},{7,11},{8,4},{9,5},... | collective-permute-start | bytes 202760 | tf_op jit(solution)/shard_map/ppermute | solution.py:388
  56.6 2.5 %collective-permute-start.26 = (bf16[264,128]{1,0:T(8,128)(2,1)S(1)}, bf16[264,128]{1,0:T(8,128)(2,1)S(1)}, u32[]{:S(2)}, u32[]{:S(2)}) collective-permute-start(bf16[264,128]{1,0:T(8,128)(2,1)S(1)} %get-tuple-element.125), channel_id=1, source_target_pairs={{0,6},{1,7},{2,4},{3,5},{4,2},{5,3},{6,0},{7,1},{8,14},{9,15},{10,... | collective-permute-start | bytes 202760 | tf_op jit(solution)/shard_map/ppermute | solution.py:388
  59.2 2.6 %collective-permute-start.27 = (bf16[264,128]{1,0:T(8,128)(2,1)S(1)}, bf16[264,128]{1,0:T(8,128)(2,1)S(1)}, u32[]{:S(2)}, u32[]{:S(2)}) collective-permute-start(bf16[264,128]{1,0:T(8,128)(2,1)S(1)} %get-tuple-element.126), channel_id=1, source_target_pairs={{0,14},{1,15},{2,12},{3,13},{4,10},{5,11},{6,8},{7,9},{8,6},{9,7},... | collective-permute-start | bytes 202760 | tf_op jit(solution)/shard_map/ppermute | solution.py:388
  61.8 1.3 collective-permute-start.29
  63.1 3.1 %collective-permute-done.27.refs_13_ = bf16[264,128]{1,0:T(8,128)(2,1)S(1)} collective-permute-done((bf16[264,128]{1,0:T(8,128)(2,1)S(1)}, bf16[264,128]{1,0:T(8,128)(2,1)S(1)}, u32[]{:S(2)}, u32[]{:S(2)}) %collective-permute-start.27) | collective-permute-done | bytes 67616 | tf_op jit(solution)/shard_map/ppermute | solution.py:388
  66.9 2.0 %collective-permute-done.29.refs_15_ = bf16[264,128]{1,0:T(8,128)(2,1)S(1)} collective-permute-done((bf16[264,128]{1,0:T(8,128)(2,1)S(1)}, bf16[264,128]{1,0:T(8,128)(2,1)S(1)}, u32[]{:S(2)}, u32[]{:S(2)}) %collective-permute-start.29) | collective-permute-done | bytes 67616 | tf_op jit(solution)/shard_map/ppermute | solution.py:388
  68.9 2.2 %copy-done = bf16[8,16,128,128]{3,2,1,0:T(8,128)(2,1)S(1)} copy-done((bf16[8,16,128,128]{3,2,1,0:T(8,128)(2,1)S(1)}, bf16[8,16,128,128]{3,2,1,0:T(8,128)(2,1)}, u32[]{:S(2)}) %copy-start) | copy-done | bytes 4194328
  71.7 3.4 %pairs.1 = (bf16[264,128]{1,0:T(8,128)(2,1)S(1)}, bf16[264,128]{1,0:T(8,128)(2,1)S(1)}, bf16[264,128]{1,0:T(8,128)(2,1)S(1)}, bf16[264,128]{1,0:T(8,128)(2,1)S(1...) custom-call(s32[128]{0:T(128)S(1)} %copy-done.4, ...), custom_call_target="tpu_custom_call" | custom-call | flops 536870912 | bytes 8388608 | tf_op jit(solution)/shard_map/pairs/pallas_call | solution.py:416
  76.4 1.8 %collective-permute-start.32 = (bf16[264,128]{1,0:T(8,128)(2,1)S(1)}, bf16[264,128]{1,0:T(8,128)(2,1)S(1)}, u32[]{:S(2)}, u32[]{:S(2)}) collective-permute-start(bf16[264,128]{1,0:T(8,128)(2,1)S(1)} %get-tuple-element.133), channel_id=1, source_target_pairs={{0,9},{1,8},{2,11},{3,10},{4,13},{5,12},{6,15},{7,14},{8,1},{9,0},... | collective-permute-start | bytes 202760 | tf_op jit(solution)/shard_map/ppermute | solution.py:388
  78.2 1.3 collective-permute-start.33
  80.4 2.5 %collective-permute-done.30.refs_1_ = bf16[264,128]{1,0:T(8,128)(2,1)S(1)} collective-permute-done((bf16[264,128]{1,0:T(8,128)(2,1)S(1)}, bf16[264,128]{1,0:T(8,128)(2,1)S(1)}, u32[]{:S(2)}, u32[]{:S(2)}) %collective-permute-start.30) | collective-permute-done | bytes 67616 | tf_op jit(solution)/shard_map/ppermute | solution.py:388
  83.8 1.7 collective-permute-done.32.refs_3_
  85.5 1.3 collective-permute-start.37
  86.8 1.7 collective-permute-start.38
  89.1 1.8 %collective-permute-start.40 = (bf16[264,128]{1,0:T(8,128)(2,1)S(1)}, bf16[264,128]{1,0:T(8,128)(2,1)S(1)}, u32[]{:S(2)}, u32[]{:S(2)}) collective-permute-start(bf16[264,128]{1,0:T(8,128)(2,1)S(1)} %get-tuple-element.141), channel_id=1, source_target_pairs={{0,13},{1,12},{2,15},{3,14},{4,9},{5,8},{6,11},{7,10},{8,5},{9,4},... | collective-permute-start | bytes 202760 | tf_op jit(solution)/shard_map/ppermute | solution.py:388
  90.9 2.8 %collective-permute-start.41 = (bf16[264,128]{1,0:T(8,128)(2,1)S(1)}, bf16[264,128]{1,0:T(8,128)(2,1)S(1)}, u32[]{:S(2)}, u32[]{:S(2)}) collective-permute-start(bf16[264,128]{1,0:T(8,128)(2,1)S(1)} %get-tuple-element.142), channel_id=1, source_target_pairs={{0,6},{1,7},{2,4},{3,5},{4,2},{5,3},{6,0},{7,1},{8,14},{9,15},{10,... | collective-permute-start | bytes 202760 | tf_op jit(solution)/shard_map/ppermute | solution.py:388
  93.7 1.2 collective-permute-start.42
  95.4 2.0 %collective-permute-start.44 = (bf16[264,128]{1,0:T(8,128)(2,1)S(1)}, bf16[264,128]{1,0:T(8,128)(2,1)S(1)}, u32[]{:S(2)}, u32[]{:S(2)}) collective-permute-start(bf16[264,128]{1,0:T(8,128)(2,1)S(1)} %get-tuple-element.145), channel_id=1, source_target_pairs={{0,15},{1,14},{2,13},{3,12},{4,11},{5,10},{6,9},{7,8},{8,7},{9,6},... | collective-permute-start | bytes 202760 | tf_op jit(solution)/shard_map/ppermute | solution.py:388
  98.2 2.8 %collective-permute-done.42.refs_13_ = bf16[264,128]{1,0:T(8,128)(2,1)S(1)} collective-permute-done((bf16[264,128]{1,0:T(8,128)(2,1)S(1)}, bf16[264,128]{1,0:T(8,128)(2,1)S(1)}, u32[]{:S(2)}, u32[]{:S(2)}) %collective-permute-start.42) | collective-permute-done | bytes 67616 | tf_op jit(solution)/shard_map/ppermute | solution.py:388
  102.5 2.4 %cells.1 = (f32[64,8192]{1,0:T(8,128)S(1)}, f32[64,128]{1,0:T(8,128)S(1)}, bf16[264,128]{1,0:T(8,128)(2,1)S(1)}, bf16[264,128]{1,0:T(8,128)(2,1)S(1)}, bf16[264,...) custom-call(s32[16,128]{1,0:T(8,128)S(1)} %get-tuple-element.111.ask, ...), custom_call_target="tpu_custom_call" | custom-call | bytes 8388608 | tf_op jit(solution)/shard_map/cells/pallas_call | solution.py:425
  105.0 1.8 %collective-permute-start.46 = (bf16[264,128]{1,0:T(8,128)(2,1)S(1)}, bf16[264,128]{1,0:T(8,128)(2,1)S(1)}, u32[]{:S(2)}, u32[]{:S(2)}) collective-permute-start(bf16[264,128]{1,0:T(8,128)(2,1)S(1)} %get-tuple-element.150), channel_id=1, source_target_pairs={{0,1},{1,0},{2,3},{3,2},{4,5},{5,4},{6,7},{7,6},{8,9},{9,8},{10,11... | collective-permute-start | bytes 202760 | tf_op jit(solution)/shard_map/ppermute | solution.py:388
  106.9 1.2 collective-permute-start.47
  108.1 1.2 collective-permute-start.48
  109.3 1.6 collective-permute-start.49
  110.9 2.6 %collective-permute-done.45.refs_1_ = bf16[264,128]{1,0:T(8,128)(2,1)S(1)} collective-permute-done((bf16[264,128]{1,0:T(8,128)(2,1)S(1)}, bf16[264,128]{1,0:T(8,128)(2,1)S(1)}, u32[]{:S(2)}, u32[]{:S(2)}) %collective-permute-start.45) | collective-permute-done | bytes 67616 | tf_op jit(solution)/shard_map/ppermute | solution.py:388
  115.1 1.8 %collective-permute-start.52 = (bf16[264,128]{1,0:T(8,128)(2,1)S(1)}, bf16[264,128]{1,0:T(8,128)(2,1)S(1)}, u32[]{:S(2)}, u32[]{:S(2)}) collective-permute-start(bf16[264,128]{1,0:T(8,128)(2,1)S(1)} %get-tuple-element.156), channel_id=1, source_target_pairs={{0,4},{1,5},{2,6},{3,7},{4,0},{5,1},{6,2},{7,3},{8,12},{9,13},{10,... | collective-permute-start | bytes 202760 | tf_op jit(solution)/shard_map/ppermute | solution.py:388
  116.9 2.2 %collective-permute-start.53 = (bf16[264,128]{1,0:T(8,128)(2,1)S(1)}, bf16[264,128]{1,0:T(8,128)(2,1)S(1)}, u32[]{:S(2)}, u32[]{:S(2)}) collective-permute-start(bf16[264,128]{1,0:T(8,128)(2,1)S(1)} %get-tuple-element.157), channel_id=1, source_target_pairs={{0,12},{1,13},{2,14},{3,15},{4,8},{5,9},{6,10},{7,11},{8,4},{9,5},... | collective-permute-start | bytes 202760 | tf_op jit(solution)/shard_map/ppermute | solution.py:388
  119.1 1.6 collective-permute-start.55
  120.8 2.8 %collective-permute-start.56 = (bf16[264,128]{1,0:T(8,128)(2,1)S(1)}, bf16[264,128]{1,0:T(8,128)(2,1)S(1)}, u32[]{:S(2)}, u32[]{:S(2)}) collective-permute-start(bf16[264,128]{1,0:T(8,128)(2,1)S(1)} %get-tuple-element.160), channel_id=1, source_target_pairs={{0,6},{1,7},{2,4},{3,5},{4,2},{5,3},{6,0},{7,1},{8,14},{9,15},{10,... | collective-permute-start | bytes 202760 | tf_op jit(solution)/shard_map/ppermute | solution.py:388
  125.3 2.1 %collective-permute-start.59 = (bf16[264,128]{1,0:T(8,128)(2,1)S(1)}, bf16[264,128]{1,0:T(8,128)(2,1)S(1)}, u32[]{:S(2)}, u32[]{:S(2)}) collective-permute-start(bf16[264,128]{1,0:T(8,128)(2,1)S(1)} %get-tuple-element.163), channel_id=1, source_target_pairs={{0,15},{1,14},{2,13},{3,12},{4,11},{5,10},{6,9},{7,8},{8,7},{9,6},... | collective-permute-start | bytes 202760 | tf_op jit(solution)/shard_map/ppermute | solution.py:388
  127.5 3.3 %collective-permute-done.57.refs_13_ = bf16[264,128]{1,0:T(8,128)(2,1)S(1)} collective-permute-done((bf16[264,128]{1,0:T(8,128)(2,1)S(1)}, bf16[264,128]{1,0:T(8,128)(2,1)S(1)}, u32[]{:S(2)}, u32[]{:S(2)}) %collective-permute-start.57) | collective-permute-done | bytes 67616 | tf_op jit(solution)/shard_map/ppermute | solution.py:388
  130.9 1.5 collective-permute-done.59.refs_15_
  132.4 3.5 %pairs_last.1 = (bf16[264,128]{1,0:T(8,128)(2,1)S(1)}, bf16[264,128]{1,0:T(8,128)(2,1)S(1)}, bf16[264,128]{1,0:T(8,128)(2,1)S(1)}, bf16[264,128]{1,0:T(8,128)(2,...) custom-call(s32[128]{0:T(128)S(1)} %copy-done.5, ...), custom_call_target="tpu_custom_call" | custom-call | flops 536870912 | bytes 8388608 | tf_op jit(solution)/shard_map/pairs_last/pallas_call | solution.py:416
  136.0 1.8 %collective-permute-start.61 = (bf16[264,128]{1,0:T(8,128)(2,1)S(1)}, bf16[264,128]{1,0:T(8,128)(2,1)S(1)}, u32[]{:S(2)}, u32[]{:S(2)}) collective-permute-start(bf16[264,128]{1,0:T(8,128)(2,1)S(1)} %get-tuple-element.168), channel_id=1, source_target_pairs={{0,1},{1,0},{2,3},{3,2},{4,5},{5,4},{6,7},{7,6},{8,9},{9,8},{10,11... | collective-permute-start | bytes 202760 | tf_op jit(solution)/shard_map/ppermute | solution.py:388
  139.0 1.4 collective-permute-start.63
  140.5 1.4 collective-permute-start.64
  141.9 3.6 %collective-permute-done.60.refs_1_ = bf16[264,128]{1,0:T(8,128)(2,1)S(1)} collective-permute-done((bf16[264,128]{1,0:T(8,128)(2,1)S(1)}, bf16[264,128]{1,0:T(8,128)(2,1)S(1)}, u32[]{:S(2)}, u32[]{:S(2)}) %collective-permute-start.60) | collective-permute-done | bytes 67616 | tf_op jit(solution)/shard_map/ppermute | solution.py:388
  146.5 1.4 collective-permute-start.67
  147.9 3.2 %collective-permute-start.68 = (bf16[264,128]{1,0:T(8,128)(2,1)S(1)}, bf16[264,128]{1,0:T(8,128)(2,1)S(1)}, u32[]{:S(2)}, u32[]{:S(2)}) collective-permute-start(bf16[264,128]{1,0:T(8,128)(2,1)S(1)} %get-tuple-element.175), channel_id=1, source_target_pairs={{0,12},{1,13},{2,14},{3,15},{4,8},{5,9},{6,10},{7,11},{8,4},{9,5},... | collective-permute-start | bytes 202760 | tf_op jit(solution)/shard_map/ppermute | solution.py:388
  151.8 2.3 %collective-permute-start.71 = (bf16[264,128]{1,0:T(8,128)(2,1)S(1)}, bf16[264,128]{1,0:T(8,128)(2,1)S(1)}, u32[]{:S(2)}, u32[]{:S(2)}) collective-permute-start(bf16[264,128]{1,0:T(8,128)(2,1)S(1)} %get-tuple-element.178), channel_id=1, source_target_pairs={{0,6},{1,7},{2,4},{3,5},{4,2},{5,3},{6,0},{7,1},{8,14},{9,15},{10,... | collective-permute-start | bytes 202760 | tf_op jit(solution)/shard_map/ppermute | solution.py:388
  154.1 2.5 %collective-permute-start.72 = (bf16[264,128]{1,0:T(8,128)(2,1)S(1)}, bf16[264,128]{1,0:T(8,128)(2,1)S(1)}, u32[]{:S(2)}, u32[]{:S(2)}) collective-permute-start(bf16[264,128]{1,0:T(8,128)(2,1)S(1)} %get-tuple-element.179), channel_id=1, source_target_pairs={{0,14},{1,15},{2,12},{3,13},{4,10},{5,11},{6,8},{7,9},{8,6},{9,7},... | collective-permute-start | bytes 202760 | tf_op jit(solution)/shard_map/ppermute | solution.py:388
  156.6 1.6 collective-permute-start.74
  159.2 2.3 %collective-permute-done.72.refs_13_ = bf16[264,128]{1,0:T(8,128)(2,1)S(1)} collective-permute-done((bf16[264,128]{1,0:T(8,128)(2,1)S(1)}, bf16[264,128]{1,0:T(8,128)(2,1)S(1)}, u32[]{:S(2)}, u32[]{:S(2)}) %collective-permute-start.72) | collective-permute-done | bytes 67616 | tf_op jit(solution)/shard_map/ppermute | solution.py:388
  162.1 1.6 collective-permute-done.74.refs_15_
  163.7 2.6 %cells_last.1 = (f32[64,8192]{1,0:T(8,128)S(1)}, f32[64,128]{1,0:T(8,128)S(1)}, f32[16,8,128]{2,1,0:T(8,128)S(1)}, f32[64,8192]{1,0:T(8,128)}) custom-call(s32[16,128]{1,0:T(8,128)S(1)} %get-tuple-element.111.asked_ref, bf16[264,128]{1,0:T(8,128)(2,1)S(1)} %get-tuple-element.166.refs_0_, bf16[264,128]{1,0:T(8,128)(2,1)S(1)} %collective-permute-done.60.refs_1_, ...), custom_call_target="tpu_custom_call" | custom-call | bytes 10485760 | tf_op jit(solution)/shard_map/cells_last/pallas_call | solution.py:432
  166.3 10.6 %all_to_all.5.tails_ref = f32[16,8,128]{2,1,0:T(8,128)S(1)} all-to-all(f32[16,8,128]{2,1,0:T(8,128)S(1)} %get-tuple-element.185), channel_id=1, replica_groups=mesh['groups'=2,'pair'=16] {'pair'}, dimensions={0} | all-to-all | bytes 131072 | tf_op jit(solution)/shard_map/all_to_all | solution.py:437
  176.9 1.5 model.1
  (106 shorter events, 22.1 us)
Async XLA Ops:
  6.3 8.6 %collective-permute-start = (bf16[264,128]{1,0:T(8,128)(2,1)}, bf16[264,128]{1,0:T(8,128)(2,1)S(1)}, u32[]{:S(2)}, u32[]{:S(2)}) collective-permute-start(bf16[264,128]{1,0:T(8,128)(2,1)} %get-tuple-element.96), channel_id=1, source_target_pairs={{0,8},{1,9},{2,10},{3,11},{4,12},{5,13},{6,14},{7,15},{8,0},{9,1},... | collective-permute-start | bytes 202760 | tf_op jit(solution)/shard_map/ppermute | solution.py:388
  10.5 7.1 %collective-permute-start.2 = (bf16[264,128]{1,0:T(8,128)(2,1)}, bf16[264,128]{1,0:T(8,128)(2,1)S(1)}, u32[]{:S(2)}, u32[]{:S(2)}) collective-permute-start(bf16[264,128]{1,0:T(8,128)(2,1)} %get-tuple-element.98), channel_id=1, source_target_pairs={{0,9},{1,8},{2,11},{3,10},{4,13},{5,12},{6,15},{7,14},{8,1},{9,0},... | collective-permute-start | bytes 202760 | tf_op jit(solution)/shard_map/ppermute | solution.py:388
  10.7 11.3 %collective-permute-start.3 = (bf16[264,128]{1,0:T(8,128)(2,1)}, bf16[264,128]{1,0:T(8,128)(2,1)S(1)}, u32[]{:S(2)}, u32[]{:S(2)}) collective-permute-start(bf16[264,128]{1,0:T(8,128)(2,1)} %get-tuple-element.99), channel_id=1, source_target_pairs={{0,2},{1,3},{2,0},{3,1},{4,6},{5,7},{6,4},{7,5},{8,10},{9,11},{10,... | collective-permute-start | bytes 202760 | tf_op jit(solution)/shard_map/ppermute | solution.py:388
  12.5 9.4 %collective-permute-start.4 = (bf16[264,128]{1,0:T(8,128)(2,1)}, bf16[264,128]{1,0:T(8,128)(2,1)S(1)}, u32[]{:S(2)}, u32[]{:S(2)}) collective-permute-start(bf16[264,128]{1,0:T(8,128)(2,1)} %get-tuple-element.100), channel_id=1, source_target_pairs={{0,10},{1,11},{2,8},{3,9},{4,14},{5,15},{6,12},{7,13},{8,2},{9,3},... | collective-permute-start | bytes 202760 | tf_op jit(solution)/shard_map/ppermute | solution.py:388
  15.0 7.4 %collective-permute-start.5 = (bf16[264,128]{1,0:T(8,128)(2,1)}, bf16[264,128]{1,0:T(8,128)(2,1)S(1)}, u32[]{:S(2)}, u32[]{:S(2)}) collective-permute-start(bf16[264,128]{1,0:T(8,128)(2,1)} %get-tuple-element.101), channel_id=1, source_target_pairs={{0,3},{1,2},{2,1},{3,0},{4,7},{5,6},{6,5},{7,4},{8,11},{9,10},{10,... | collective-permute-start | bytes 202760 | tf_op jit(solution)/shard_map/ppermute | solution.py:388
  15.6 11.2 %collective-permute-start.6 = (bf16[264,128]{1,0:T(8,128)(2,1)}, bf16[264,128]{1,0:T(8,128)(2,1)S(1)}, u32[]{:S(2)}, u32[]{:S(2)}) collective-permute-start(bf16[264,128]{1,0:T(8,128)(2,1)} %get-tuple-element.102), channel_id=1, source_target_pairs={{0,11},{1,10},{2,9},{3,8},{4,15},{5,14},{6,13},{7,12},{8,3},{9,2},... | collective-permute-start | bytes 202760 | tf_op jit(solution)/shard_map/ppermute | solution.py:388
  17.6 10.0 %collective-permute-start.7 = (bf16[264,128]{1,0:T(8,128)(2,1)}, bf16[264,128]{1,0:T(8,128)(2,1)S(1)}, u32[]{:S(2)}, u32[]{:S(2)}) collective-permute-start(bf16[264,128]{1,0:T(8,128)(2,1)} %get-tuple-element.103), channel_id=1, source_target_pairs={{0,4},{1,5},{2,6},{3,7},{4,0},{5,1},{6,2},{7,3},{8,12},{9,13},{10,... | collective-permute-start | bytes 202760 | tf_op jit(solution)/shard_map/ppermute | solution.py:388
  22.0 7.6 %collective-permute-start.8 = (bf16[264,128]{1,0:T(8,128)(2,1)}, bf16[264,128]{1,0:T(8,128)(2,1)S(1)}, u32[]{:S(2)}, u32[]{:S(2)}) collective-permute-start(bf16[264,128]{1,0:T(8,128)(2,1)} %get-tuple-element.104), channel_id=1, source_target_pairs={{0,12},{1,13},{2,14},{3,15},{4,8},{5,9},{6,10},{7,11},{8,4},{9,5},... | collective-permute-start | bytes 202760 | tf_op jit(solution)/shard_map/ppermute | solution.py:388
  22.0 7.7 %collective-permute-start.9 = (bf16[264,128]{1,0:T(8,128)(2,1)}, bf16[264,128]{1,0:T(8,128)(2,1)S(1)}, u32[]{:S(2)}, u32[]{:S(2)}) collective-permute-start(bf16[264,128]{1,0:T(8,128)(2,1)} %get-tuple-element.105), channel_id=1, source_target_pairs={{0,5},{1,4},{2,7},{3,6},{4,1},{5,0},{6,3},{7,2},{8,13},{9,12},{10,... | collective-permute-start | bytes 202760 | tf_op jit(solution)/shard_map/ppermute | solution.py:388
  22.4 10.9 %collective-permute-start.10 = (bf16[264,128]{1,0:T(8,128)(2,1)}, bf16[264,128]{1,0:T(8,128)(2,1)S(1)}, u32[]{:S(2)}, u32[]{:S(2)}) collective-permute-start(bf16[264,128]{1,0:T(8,128)(2,1)} %get-tuple-element.106), channel_id=1, source_target_pairs={{0,13},{1,12},{2,15},{3,14},{4,9},{5,8},{6,11},{7,10},{8,5},{9,4},... | collective-permute-start | bytes 202760 | tf_op jit(solution)/shard_map/ppermute | solution.py:388
  26.7 6.5 %collective-permute-start.11 = (bf16[264,128]{1,0:T(8,128)(2,1)}, bf16[264,128]{1,0:T(8,128)(2,1)S(1)}, u32[]{:S(2)}, u32[]{:S(2)}) collective-permute-start(bf16[264,128]{1,0:T(8,128)(2,1)} %get-tuple-element.107), channel_id=1, source_target_pairs={{0,6},{1,7},{2,4},{3,5},{4,2},{5,3},{6,0},{7,1},{8,14},{9,15},{10,... | collective-permute-start | bytes 202760 | tf_op jit(solution)/shard_map/ppermute | solution.py:388
  27.6 7.4 %collective-permute-start.12 = (bf16[264,128]{1,0:T(8,128)(2,1)}, bf16[264,128]{1,0:T(8,128)(2,1)S(1)}, u32[]{:S(2)}, u32[]{:S(2)}) collective-permute-start(bf16[264,128]{1,0:T(8,128)(2,1)} %get-tuple-element.108), channel_id=1, source_target_pairs={{0,14},{1,15},{2,12},{3,13},{4,10},{5,11},{6,8},{7,9},{8,6},{9,7},... | collective-permute-start | bytes 202760 | tf_op jit(solution)/shard_map/ppermute | solution.py:388
  29.5 6.3 %collective-permute-start.13 = (bf16[264,128]{1,0:T(8,128)(2,1)}, bf16[264,128]{1,0:T(8,128)(2,1)S(1)}, u32[]{:S(2)}, u32[]{:S(2)}) collective-permute-start(bf16[264,128]{1,0:T(8,128)(2,1)} %get-tuple-element.109), channel_id=1, source_target_pairs={{0,7},{1,6},{2,5},{3,4},{4,3},{5,2},{6,1},{7,0},{8,15},{9,14},{10,... | collective-permute-start | bytes 202760 | tf_op jit(solution)/shard_map/ppermute | solution.py:388
  29.7 7.6 %collective-permute-start.14 = (bf16[264,128]{1,0:T(8,128)(2,1)}, bf16[264,128]{1,0:T(8,128)(2,1)S(1)}, u32[]{:S(2)}, u32[]{:S(2)}) collective-permute-start(bf16[264,128]{1,0:T(8,128)(2,1)} %get-tuple-element.110), channel_id=1, source_target_pairs={{0,15},{1,14},{2,13},{3,12},{4,11},{5,10},{6,9},{7,8},{8,7},{9,6},... | collective-permute-start | bytes 202760 | tf_op jit(solution)/shard_map/ppermute | solution.py:388
  40.7 9.9 %collective-permute-start.15 = (bf16[264,128]{1,0:T(8,128)(2,1)S(1)}, bf16[264,128]{1,0:T(8,128)(2,1)S(1)}, u32[]{:S(2)}, u32[]{:S(2)}) collective-permute-start(bf16[264,128]{1,0:T(8,128)(2,1)S(1)} %get-tuple-element.114), channel_id=1, source_target_pairs={{0,8},{1,9},{2,10},{3,11},{4,12},{5,13},{6,14},{7,15},{8,0},{9,1},... | collective-permute-start | bytes 202760 | tf_op jit(solution)/shard_map/ppermute | solution.py:388
  41.1 9.5 %collective-permute-start.16 = (bf16[264,128]{1,0:T(8,128)(2,1)S(1)}, bf16[264,128]{1,0:T(8,128)(2,1)S(1)}, u32[]{:S(2)}, u32[]{:S(2)}) collective-permute-start(bf16[264,128]{1,0:T(8,128)(2,1)S(1)} %get-tuple-element.115), channel_id=1, source_target_pairs={{0,1},{1,0},{2,3},{3,2},{4,5},{5,4},{6,7},{7,6},{8,9},{9,8},{10,11... | collective-permute-start | bytes 202760 | tf_op jit(solution)/shard_map/ppermute | solution.py:388
  42.3 9.1 %collective-permute-start.17 = (bf16[264,128]{1,0:T(8,128)(2,1)S(1)}, bf16[264,128]{1,0:T(8,128)(2,1)S(1)}, u32[]{:S(2)}, u32[]{:S(2)}) collective-permute-start(bf16[264,128]{1,0:T(8,128)(2,1)S(1)} %get-tuple-element.116), channel_id=1, source_target_pairs={{0,9},{1,8},{2,11},{3,10},{4,13},{5,12},{6,15},{7,14},{8,1},{9,0},... | collective-permute-start | bytes 202760 | tf_op jit(solution)/shard_map/ppermute | solution.py:388
  43.8 8.8 %collective-permute-start.18 = (bf16[264,128]{1,0:T(8,128)(2,1)S(1)}, bf16[264,128]{1,0:T(8,128)(2,1)S(1)}, u32[]{:S(2)}, u32[]{:S(2)}) collective-permute-start(bf16[264,128]{1,0:T(8,128)(2,1)S(1)} %get-tuple-element.117), channel_id=1, source_target_pairs={{0,2},{1,3},{2,0},{3,1},{4,6},{5,7},{6,4},{7,5},{8,10},{9,11},{10,... | collective-permute-start | bytes 202760 | tf_op jit(solution)/shard_map/ppermute | solution.py:388
  44.1 12.1 %collective-permute-start.19 = (bf16[264,128]{1,0:T(8,128)(2,1)S(1)}, bf16[264,128]{1,0:T(8,128)(2,1)S(1)}, u32[]{:S(2)}, u32[]{:S(2)}) collective-permute-start(bf16[264,128]{1,0:T(8,128)(2,1)S(1)} %get-tuple-element.118), channel_id=1, source_target_pairs={{0,10},{1,11},{2,8},{3,9},{4,14},{5,15},{6,12},{7,13},{8,2},{9,3},... | collective-permute-start | bytes 202760 | tf_op jit(solution)/shard_map/ppermute | solution.py:388
  51.4 7.8 %collective-permute-start.22 = (bf16[264,128]{1,0:T(8,128)(2,1)S(1)}, bf16[264,128]{1,0:T(8,128)(2,1)S(1)}, u32[]{:S(2)}, u32[]{:S(2)}) collective-permute-start(bf16[264,128]{1,0:T(8,128)(2,1)S(1)} %get-tuple-element.121), channel_id=1, source_target_pairs={{0,4},{1,5},{2,6},{3,7},{4,0},{5,1},{6,2},{7,3},{8,12},{9,13},{10,... | collective-permute-start | bytes 202760 | tf_op jit(solution)/shard_map/ppermute | solution.py:388
  52.6 9.1 %collective-permute-start.23 = (bf16[264,128]{1,0:T(8,128)(2,1)S(1)}, bf16[264,128]{1,0:T(8,128)(2,1)S(1)}, u32[]{:S(2)}, u32[]{:S(2)}) collective-permute-start(bf16[264,128]{1,0:T(8,128)(2,1)S(1)} %get-tuple-element.122), channel_id=1, source_target_pairs={{0,12},{1,13},{2,14},{3,15},{4,8},{5,9},{6,10},{7,11},{8,4},{9,5},... | collective-permute-start | bytes 202760 | tf_op jit(solution)/shard_map/ppermute | solution.py:388
  56.2 6.9 %collective-permute-start.25 = (bf16[264,128]{1,0:T(8,128)(2,1)S(1)}, bf16[264,128]{1,0:T(8,128)(2,1)S(1)}, u32[]{:S(2)}, u32[]{:S(2)}) collective-permute-start(bf16[264,128]{1,0:T(8,128)(2,1)S(1)} %get-tuple-element.124), channel_id=1, source_target_pairs={{0,13},{1,12},{2,15},{3,14},{4,9},{5,8},{6,11},{7,10},{8,5},{9,4},... | collective-permute-start | bytes 202760 | tf_op jit(solution)/shard_map/ppermute | solution.py:388
  56.6 6.5 %collective-permute-start.26 = (bf16[264,128]{1,0:T(8,128)(2,1)S(1)}, bf16[264,128]{1,0:T(8,128)(2,1)S(1)}, u32[]{:S(2)}, u32[]{:S(2)}) collective-permute-start(bf16[264,128]{1,0:T(8,128)(2,1)S(1)} %get-tuple-element.125), channel_id=1, source_target_pairs={{0,6},{1,7},{2,4},{3,5},{4,2},{5,3},{6,0},{7,1},{8,14},{9,15},{10,... | collective-permute-start | bytes 202760 | tf_op jit(solution)/shard_map/ppermute | solution.py:388
  59.2 7.1 %collective-permute-start.27 = (bf16[264,128]{1,0:T(8,128)(2,1)S(1)}, bf16[264,128]{1,0:T(8,128)(2,1)S(1)}, u32[]{:S(2)}, u32[]{:S(2)}) collective-permute-start(bf16[264,128]{1,0:T(8,128)(2,1)S(1)} %get-tuple-element.126), channel_id=1, source_target_pairs={{0,14},{1,15},{2,12},{3,13},{4,10},{5,11},{6,8},{7,9},{8,6},{9,7},... | collective-permute-start | bytes 202760 | tf_op jit(solution)/shard_map/ppermute | solution.py:388
  61.8 7.1 %collective-permute-start.29 = (bf16[264,128]{1,0:T(8,128)(2,1)S(1)}, bf16[264,128]{1,0:T(8,128)(2,1)S(1)}, u32[]{:S(2)}, u32[]{:S(2)}) collective-permute-start(bf16[264,128]{1,0:T(8,128)(2,1)S(1)} %get-tuple-element.128), channel_id=1, source_target_pairs={{0,15},{1,14},{2,13},{3,12},{4,11},{5,10},{6,9},{7,8},{8,7},{9,6},... | collective-permute-start | bytes 202760 | tf_op jit(solution)/shard_map/ppermute | solution.py:388
  75.1 7.8 %collective-permute-start.30 = (bf16[264,128]{1,0:T(8,128)(2,1)S(1)}, bf16[264,128]{1,0:T(8,128)(2,1)S(1)}, u32[]{:S(2)}, u32[]{:S(2)}) collective-permute-start(bf16[264,128]{1,0:T(8,128)(2,1)S(1)} %get-tuple-element.131), channel_id=1, source_target_pairs={{0,8},{1,9},{2,10},{3,11},{4,12},{5,13},{6,14},{7,15},{8,0},{9,1},... | collective-permute-start | bytes 202760 | tf_op jit(solution)/shard_map/ppermute | solution.py:388
  75.2 8.4 %collective-permute-start.31 = (bf16[264,128]{1,0:T(8,128)(2,1)S(1)}, bf16[264,128]{1,0:T(8,128)(2,1)S(1)}, u32[]{:S(2)}, u32[]{:S(2)}) collective-permute-start(bf16[264,128]{1,0:T(8,128)(2,1)S(1)} %get-tuple-element.132), channel_id=1, source_target_pairs={{0,1},{1,0},{2,3},{3,2},{4,5},{5,4},{6,7},{7,6},{8,9},{9,8},{10,11... | collective-permute-start | bytes 202760 | tf_op jit(solution)/shard_map/ppermute | solution.py:388
  76.4 9.1 %collective-permute-start.32 = (bf16[264,128]{1,0:T(8,128)(2,1)S(1)}, bf16[264,128]{1,0:T(8,128)(2,1)S(1)}, u32[]{:S(2)}, u32[]{:S(2)}) collective-permute-start(bf16[264,128]{1,0:T(8,128)(2,1)S(1)} %get-tuple-element.133), channel_id=1, source_target_pairs={{0,9},{1,8},{2,11},{3,10},{4,13},{5,12},{6,15},{7,14},{8,1},{9,0},... | collective-permute-start | bytes 202760 | tf_op jit(solution)/shard_map/ppermute | solution.py:388
  78.2 8.6 %collective-permute-start.33 = (bf16[264,128]{1,0:T(8,128)(2,1)S(1)}, bf16[264,128]{1,0:T(8,128)(2,1)S(1)}, u32[]{:S(2)}, u32[]{:S(2)}) collective-permute-start(bf16[264,128]{1,0:T(8,128)(2,1)S(1)} %get-tuple-element.134), channel_id=1, source_target_pairs={{0,2},{1,3},{2,0},{3,1},{4,6},{5,7},{6,4},{7,5},{8,10},{9,11},{10,... | collective-permute-start | bytes 202760 | tf_op jit(solution)/shard_map/ppermute | solution.py:388
  79.5 9.1 %collective-permute-start.34 = (bf16[264,128]{1,0:T(8,128)(2,1)S(1)}, bf16[264,128]{1,0:T(8,128)(2,1)S(1)}, u32[]{:S(2)}, u32[]{:S(2)}) collective-permute-start(bf16[264,128]{1,0:T(8,128)(2,1)S(1)} %get-tuple-element.135), channel_id=1, source_target_pairs={{0,10},{1,11},{2,8},{3,9},{4,14},{5,15},{6,12},{7,13},{8,2},{9,3},... | collective-permute-start | bytes 202760 | tf_op jit(solution)/shard_map/ppermute | solution.py:388
  83.7 7.2 %collective-permute-start.36 = (bf16[264,128]{1,0:T(8,128)(2,1)S(1)}, bf16[264,128]{1,0:T(8,128)(2,1)S(1)}, u32[]{:S(2)}, u32[]{:S(2)}) collective-permute-start(bf16[264,128]{1,0:T(8,128)(2,1)S(1)} %get-tuple-element.137), channel_id=1, source_target_pairs={{0,11},{1,10},{2,9},{3,8},{4,15},{5,14},{6,13},{7,12},{8,3},{9,2},... | collective-permute-start | bytes 202760 | tf_op jit(solution)/shard_map/ppermute | solution.py:388
  85.5 8.1 %collective-permute-start.37 = (bf16[264,128]{1,0:T(8,128)(2,1)S(1)}, bf16[264,128]{1,0:T(8,128)(2,1)S(1)}, u32[]{:S(2)}, u32[]{:S(2)}) collective-permute-start(bf16[264,128]{1,0:T(8,128)(2,1)S(1)} %get-tuple-element.138), channel_id=1, source_target_pairs={{0,4},{1,5},{2,6},{3,7},{4,0},{5,1},{6,2},{7,3},{8,12},{9,13},{10,... | collective-permute-start | bytes 202760 | tf_op jit(solution)/shard_map/ppermute | solution.py:388
  86.8 8.1 %collective-permute-start.38 = (bf16[264,128]{1,0:T(8,128)(2,1)S(1)}, bf16[264,128]{1,0:T(8,128)(2,1)S(1)}, u32[]{:S(2)}, u32[]{:S(2)}) collective-permute-start(bf16[264,128]{1,0:T(8,128)(2,1)S(1)} %get-tuple-element.139), channel_id=1, source_target_pairs={{0,12},{1,13},{2,14},{3,15},{4,8},{5,9},{6,10},{7,11},{8,4},{9,5},... | collective-permute-start | bytes 202760 | tf_op jit(solution)/shard_map/ppermute | solution.py:388
  88.7 6.7 %collective-permute-start.39 = (bf16[264,128]{1,0:T(8,128)(2,1)S(1)}, bf16[264,128]{1,0:T(8,128)(2,1)S(1)}, u32[]{:S(2)}, u32[]{:S(2)}) collective-permute-start(bf16[264,128]{1,0:T(8,128)(2,1)S(1)} %get-tuple-element.140), channel_id=1, source_target_pairs={{0,5},{1,4},{2,7},{3,6},{4,1},{5,0},{6,3},{7,2},{8,13},{9,12},{10,... | collective-permute-start | bytes 202760 | tf_op jit(solution)/shard_map/ppermute | solution.py:388
  89.1 8.3 %collective-permute-start.40 = (bf16[264,128]{1,0:T(8,128)(2,1)S(1)}, bf16[264,128]{1,0:T(8,128)(2,1)S(1)}, u32[]{:S(2)}, u32[]{:S(2)}) collective-permute-start(bf16[264,128]{1,0:T(8,128)(2,1)S(1)} %get-tuple-element.141), channel_id=1, source_target_pairs={{0,13},{1,12},{2,15},{3,14},{4,9},{5,8},{6,11},{7,10},{8,5},{9,4},... | collective-permute-start | bytes 202760 | tf_op jit(solution)/shard_map/ppermute | solution.py:388
  90.9 7.3 %collective-permute-start.41 = (bf16[264,128]{1,0:T(8,128)(2,1)S(1)}, bf16[264,128]{1,0:T(8,128)(2,1)S(1)}, u32[]{:S(2)}, u32[]{:S(2)}) collective-permute-start(bf16[264,128]{1,0:T(8,128)(2,1)S(1)} %get-tuple-element.142), channel_id=1, source_target_pairs={{0,6},{1,7},{2,4},{3,5},{4,2},{5,3},{6,0},{7,1},{8,14},{9,15},{10,... | collective-permute-start | bytes 202760 | tf_op jit(solution)/shard_map/ppermute | solution.py:388
  93.7 7.3 %collective-permute-start.42 = (bf16[264,128]{1,0:T(8,128)(2,1)S(1)}, bf16[264,128]{1,0:T(8,128)(2,1)S(1)}, u32[]{:S(2)}, u32[]{:S(2)}) collective-permute-start(bf16[264,128]{1,0:T(8,128)(2,1)S(1)} %get-tuple-element.143), channel_id=1, source_target_pairs={{0,14},{1,15},{2,12},{3,13},{4,10},{5,11},{6,8},{7,9},{8,6},{9,7},... | collective-permute-start | bytes 202760 | tf_op jit(solution)/shard_map/ppermute | solution.py:388
  94.9 6.5 %collective-permute-start.43 = (bf16[264,128]{1,0:T(8,128)(2,1)S(1)}, bf16[264,128]{1,0:T(8,128)(2,1)S(1)}, u32[]{:S(2)}, u32[]{:S(2)}) collective-permute-start(bf16[264,128]{1,0:T(8,128)(2,1)S(1)} %get-tuple-element.144), channel_id=1, source_target_pairs={{0,7},{1,6},{2,5},{3,4},{4,3},{5,2},{6,1},{7,0},{8,15},{9,14},{10,... | collective-permute-start | bytes 202760 | tf_op jit(solution)/shard_map/ppermute | solution.py:388
  95.4 7.1 %collective-permute-start.44 = (bf16[264,128]{1,0:T(8,128)(2,1)S(1)}, bf16[264,128]{1,0:T(8,128)(2,1)S(1)}, u32[]{:S(2)}, u32[]{:S(2)}) collective-permute-start(bf16[264,128]{1,0:T(8,128)(2,1)S(1)} %get-tuple-element.145), channel_id=1, source_target_pairs={{0,15},{1,14},{2,13},{3,12},{4,11},{5,10},{6,9},{7,8},{8,7},{9,6},... | collective-permute-start | bytes 202760 | tf_op jit(solution)/shard_map/ppermute | solution.py:388
  104.9 8.5 %collective-permute-start.45 = (bf16[264,128]{1,0:T(8,128)(2,1)S(1)}, bf16[264,128]{1,0:T(8,128)(2,1)S(1)}, u32[]{:S(2)}, u32[]{:S(2)}) collective-permute-start(bf16[264,128]{1,0:T(8,128)(2,1)S(1)} %get-tuple-element.149), channel_id=1, source_target_pairs={{0,8},{1,9},{2,10},{3,11},{4,12},{5,13},{6,14},{7,15},{8,0},{9,1},... | collective-permute-start | bytes 202760 | tf_op jit(solution)/shard_map/ppermute | solution.py:388
  105.0 8.5 %collective-permute-start.46 = (bf16[264,128]{1,0:T(8,128)(2,1)S(1)}, bf16[264,128]{1,0:T(8,128)(2,1)S(1)}, u32[]{:S(2)}, u32[]{:S(2)}) collective-permute-start(bf16[264,128]{1,0:T(8,128)(2,1)S(1)} %get-tuple-element.150), channel_id=1, source_target_pairs={{0,1},{1,0},{2,3},{3,2},{4,5},{5,4},{6,7},{7,6},{8,9},{9,8},{10,11... | collective-permute-start | bytes 202760 | tf_op jit(solution)/shard_map/ppermute | solution.py:388
  106.9 8.2 %collective-permute-start.47 = (bf16[264,128]{1,0:T(8,128)(2,1)S(1)}, bf16[264,128]{1,0:T(8,128)(2,1)S(1)}, u32[]{:S(2)}, u32[]{:S(2)}) collective-permute-start(bf16[264,128]{1,0:T(8,128)(2,1)S(1)} %get-tuple-element.151), channel_id=1, source_target_pairs={{0,9},{1,8},{2,11},{3,10},{4,13},{5,12},{6,15},{7,14},{8,1},{9,0},... | collective-permute-start | bytes 202760 | tf_op jit(solution)/shard_map/ppermute | solution.py:388
  108.1 8.8 %collective-permute-start.48 = (bf16[264,128]{1,0:T(8,128)(2,1)S(1)}, bf16[264,128]{1,0:T(8,128)(2,1)S(1)}, u32[]{:S(2)}, u32[]{:S(2)}) collective-permute-start(bf16[264,128]{1,0:T(8,128)(2,1)S(1)} %get-tuple-element.152), channel_id=1, source_target_pairs={{0,2},{1,3},{2,0},{3,1},{4,6},{5,7},{6,4},{7,5},{8,10},{9,11},{10,... | collective-permute-start | bytes 202760 | tf_op jit(solution)/shard_map/ppermute | solution.py:388
  109.3 9.8 %collective-permute-start.49 = (bf16[264,128]{1,0:T(8,128)(2,1)S(1)}, bf16[264,128]{1,0:T(8,128)(2,1)S(1)}, u32[]{:S(2)}, u32[]{:S(2)}) collective-permute-start(bf16[264,128]{1,0:T(8,128)(2,1)S(1)} %get-tuple-element.153), channel_id=1, source_target_pairs={{0,10},{1,11},{2,8},{3,9},{4,14},{5,15},{6,12},{7,13},{8,2},{9,3},... | collective-permute-start | bytes 202760 | tf_op jit(solution)/shard_map/ppermute | solution.py:388
  113.5 7.3 %collective-permute-start.51 = (bf16[264,128]{1,0:T(8,128)(2,1)S(1)}, bf16[264,128]{1,0:T(8,128)(2,1)S(1)}, u32[]{:S(2)}, u32[]{:S(2)}) collective-permute-start(bf16[264,128]{1,0:T(8,128)(2,1)S(1)} %get-tuple-element.155), channel_id=1, source_target_pairs={{0,11},{1,10},{2,9},{3,8},{4,15},{5,14},{6,13},{7,12},{8,3},{9,2},... | collective-permute-start | bytes 202760 | tf_op jit(solution)/shard_map/ppermute | solution.py:388
  115.1 8.5 %collective-permute-start.52 = (bf16[264,128]{1,0:T(8,128)(2,1)S(1)}, bf16[264,128]{1,0:T(8,128)(2,1)S(1)}, u32[]{:S(2)}, u32[]{:S(2)}) collective-permute-start(bf16[264,128]{1,0:T(8,128)(2,1)S(1)} %get-tuple-element.156), channel_id=1, source_target_pairs={{0,4},{1,5},{2,6},{3,7},{4,0},{5,1},{6,2},{7,3},{8,12},{9,13},{10,... | collective-permute-start | bytes 202760 | tf_op jit(solution)/shard_map/ppermute | solution.py:388
  116.9 7.8 %collective-permute-start.53 = (bf16[264,128]{1,0:T(8,128)(2,1)S(1)}, bf16[264,128]{1,0:T(8,128)(2,1)S(1)}, u32[]{:S(2)}, u32[]{:S(2)}) collective-permute-start(bf16[264,128]{1,0:T(8,128)(2,1)S(1)} %get-tuple-element.157), channel_id=1, source_target_pairs={{0,12},{1,13},{2,14},{3,15},{4,8},{5,9},{6,10},{7,11},{8,4},{9,5},... | collective-permute-start | bytes 202760 | tf_op jit(solution)/shard_map/ppermute | solution.py:388
  119.1 8.2 %collective-permute-start.55 = (bf16[264,128]{1,0:T(8,128)(2,1)S(1)}, bf16[264,128]{1,0:T(8,128)(2,1)S(1)}, u32[]{:S(2)}, u32[]{:S(2)}) collective-permute-start(bf16[264,128]{1,0:T(8,128)(2,1)S(1)} %get-tuple-element.159), channel_id=1, source_target_pairs={{0,13},{1,12},{2,15},{3,14},{4,9},{5,8},{6,11},{7,10},{8,5},{9,4},... | collective-permute-start | bytes 202760 | tf_op jit(solution)/shard_map/ppermute | solution.py:388
  120.8 6.8 %collective-permute-start.56 = (bf16[264,128]{1,0:T(8,128)(2,1)S(1)}, bf16[264,128]{1,0:T(8,128)(2,1)S(1)}, u32[]{:S(2)}, u32[]{:S(2)}) collective-permute-start(bf16[264,128]{1,0:T(8,128)(2,1)S(1)} %get-tuple-element.160), channel_id=1, source_target_pairs={{0,6},{1,7},{2,4},{3,5},{4,2},{5,3},{6,0},{7,1},{8,14},{9,15},{10,... | collective-permute-start | bytes 202760 | tf_op jit(solution)/shard_map/ppermute | solution.py:388
  123.6 7.3 %collective-permute-start.57 = (bf16[264,128]{1,0:T(8,128)(2,1)S(1)}, bf16[264,128]{1,0:T(8,128)(2,1)S(1)}, u32[]{:S(2)}, u32[]{:S(2)}) collective-permute-start(bf16[264,128]{1,0:T(8,128)(2,1)S(1)} %get-tuple-element.161), channel_id=1, source_target_pairs={{0,14},{1,15},{2,12},{3,13},{4,10},{5,11},{6,8},{7,9},{8,6},{9,7},... | collective-permute-start | bytes 202760 | tf_op jit(solution)/shard_map/ppermute | solution.py:388
  124.7 6.3 %collective-permute-start.58 = (bf16[264,128]{1,0:T(8,128)(2,1)S(1)}, bf16[264,128]{1,0:T(8,128)(2,1)S(1)}, u32[]{:S(2)}, u32[]{:S(2)}) collective-permute-start(bf16[264,128]{1,0:T(8,128)(2,1)S(1)} %get-tuple-element.162), channel_id=1, source_target_pairs={{0,7},{1,6},{2,5},{3,4},{4,3},{5,2},{6,1},{7,0},{8,15},{9,14},{10,... | collective-permute-start | bytes 202760 | tf_op jit(solution)/shard_map/ppermute | solution.py:388
  125.3 7.1 %collective-permute-start.59 = (bf16[264,128]{1,0:T(8,128)(2,1)S(1)}, bf16[264,128]{1,0:T(8,128)(2,1)S(1)}, u32[]{:S(2)}, u32[]{:S(2)}) collective-permute-start(bf16[264,128]{1,0:T(8,128)(2,1)S(1)} %get-tuple-element.163), channel_id=1, source_target_pairs={{0,15},{1,14},{2,13},{3,12},{4,11},{5,10},{6,9},{7,8},{8,7},{9,6},... | collective-permute-start | bytes 202760 | tf_op jit(solution)/shard_map/ppermute | solution.py:388
  135.9 9.5 %collective-permute-start.60 = (bf16[264,128]{1,0:T(8,128)(2,1)S(1)}, bf16[264,128]{1,0:T(8,128)(2,1)S(1)}, u32[]{:S(2)}, u32[]{:S(2)}) collective-permute-start(bf16[264,128]{1,0:T(8,128)(2,1)S(1)} %get-tuple-element.167), channel_id=1, source_target_pairs={{0,8},{1,9},{2,10},{3,11},{4,12},{5,13},{6,14},{7,15},{8,0},{9,1},... | collective-permute-start | bytes 202760 | tf_op jit(solution)/shard_map/ppermute | solution.py:388
  136.0 9.5 %collective-permute-start.61 = (bf16[264,128]{1,0:T(8,128)(2,1)S(1)}, bf16[264,128]{1,0:T(8,128)(2,1)S(1)}, u32[]{:S(2)}, u32[]{:S(2)}) collective-permute-start(bf16[264,128]{1,0:T(8,128)(2,1)S(1)} %get-tuple-element.168), channel_id=1, source_target_pairs={{0,1},{1,0},{2,3},{3,2},{4,5},{5,4},{6,7},{7,6},{8,9},{9,8},{10,11... | collective-permute-start | bytes 202760 | tf_op jit(solution)/shard_map/ppermute | solution.py:388
  137.9 8.7 %collective-permute-start.62 = (bf16[264,128]{1,0:T(8,128)(2,1)S(1)}, bf16[264,128]{1,0:T(8,128)(2,1)S(1)}, u32[]{:S(2)}, u32[]{:S(2)}) collective-permute-start(bf16[264,128]{1,0:T(8,128)(2,1)S(1)} %get-tuple-element.169), channel_id=1, source_target_pairs={{0,9},{1,8},{2,11},{3,10},{4,13},{5,12},{6,15},{7,14},{8,1},{9,0},... | collective-permute-start | bytes 202760 | tf_op jit(solution)/shard_map/ppermute | solution.py:388
  139.0 8.9 %collective-permute-start.63 = (bf16[264,128]{1,0:T(8,128)(2,1)S(1)}, bf16[264,128]{1,0:T(8,128)(2,1)S(1)}, u32[]{:S(2)}, u32[]{:S(2)}) collective-permute-start(bf16[264,128]{1,0:T(8,128)(2,1)S(1)} %get-tuple-element.170), channel_id=1, source_target_pairs={{0,2},{1,3},{2,0},{3,1},{4,6},{5,7},{6,4},{7,5},{8,10},{9,11},{10,... | collective-permute-start | bytes 202760 | tf_op jit(solution)/shard_map/ppermute | solution.py:388
  140.5 10.6 %collective-permute-start.64 = (bf16[264,128]{1,0:T(8,128)(2,1)S(1)}, bf16[264,128]{1,0:T(8,128)(2,1)S(1)}, u32[]{:S(2)}, u32[]{:S(2)}) collective-permute-start(bf16[264,128]{1,0:T(8,128)(2,1)S(1)} %get-tuple-element.171), channel_id=1, source_target_pairs={{0,10},{1,11},{2,8},{3,9},{4,14},{5,15},{6,12},{7,13},{8,2},{9,3},... | collective-permute-start | bytes 202760 | tf_op jit(solution)/shard_map/ppermute | solution.py:388
  145.5 6.3 %collective-permute-start.66 = (bf16[264,128]{1,0:T(8,128)(2,1)S(1)}, bf16[264,128]{1,0:T(8,128)(2,1)S(1)}, u32[]{:S(2)}, u32[]{:S(2)}) collective-permute-start(bf16[264,128]{1,0:T(8,128)(2,1)S(1)} %get-tuple-element.173), channel_id=1, source_target_pairs={{0,11},{1,10},{2,9},{3,8},{4,15},{5,14},{6,13},{7,12},{8,3},{9,2},... | collective-permute-start | bytes 202760 | tf_op jit(solution)/shard_map/ppermute | solution.py:388
  146.5 7.6 %collective-permute-start.67 = (bf16[264,128]{1,0:T(8,128)(2,1)S(1)}, bf16[264,128]{1,0:T(8,128)(2,1)S(1)}, u32[]{:S(2)}, u32[]{:S(2)}) collective-permute-start(bf16[264,128]{1,0:T(8,128)(2,1)S(1)} %get-tuple-element.174), channel_id=1, source_target_pairs={{0,4},{1,5},{2,6},{3,7},{4,0},{5,1},{6,2},{7,3},{8,12},{9,13},{10,... | collective-permute-start | bytes 202760 | tf_op jit(solution)/shard_map/ppermute | solution.py:388
  147.9 8.7 %collective-permute-start.68 = (bf16[264,128]{1,0:T(8,128)(2,1)S(1)}, bf16[264,128]{1,0:T(8,128)(2,1)S(1)}, u32[]{:S(2)}, u32[]{:S(2)}) collective-permute-start(bf16[264,128]{1,0:T(8,128)(2,1)S(1)} %get-tuple-element.175), channel_id=1, source_target_pairs={{0,12},{1,13},{2,14},{3,15},{4,8},{5,9},{6,10},{7,11},{8,4},{9,5},... | collective-permute-start | bytes 202760 | tf_op jit(solution)/shard_map/ppermute | solution.py:388
  151.1 7.2 %collective-permute-start.70 = (bf16[264,128]{1,0:T(8,128)(2,1)S(1)}, bf16[264,128]{1,0:T(8,128)(2,1)S(1)}, u32[]{:S(2)}, u32[]{:S(2)}) collective-permute-start(bf16[264,128]{1,0:T(8,128)(2,1)S(1)} %get-tuple-element.177), channel_id=1, source_target_pairs={{0,13},{1,12},{2,15},{3,14},{4,9},{5,8},{6,11},{7,10},{8,5},{9,4},... | collective-permute-start | bytes 202760 | tf_op jit(solution)/shard_map/ppermute | solution.py:388
  151.8 7.4 %collective-permute-start.71 = (bf16[264,128]{1,0:T(8,128)(2,1)S(1)}, bf16[264,128]{1,0:T(8,128)(2,1)S(1)}, u32[]{:S(2)}, u32[]{:S(2)}) collective-permute-start(bf16[264,128]{1,0:T(8,128)(2,1)S(1)} %get-tuple-element.178), channel_id=1, source_target_pairs={{0,6},{1,7},{2,4},{3,5},{4,2},{5,3},{6,0},{7,1},{8,14},{9,15},{10,... | collective-permute-start | bytes 202760 | tf_op jit(solution)/shard_map/ppermute | solution.py:388
  154.1 7.3 %collective-permute-start.72 = (bf16[264,128]{1,0:T(8,128)(2,1)S(1)}, bf16[264,128]{1,0:T(8,128)(2,1)S(1)}, u32[]{:S(2)}, u32[]{:S(2)}) collective-permute-start(bf16[264,128]{1,0:T(8,128)(2,1)S(1)} %get-tuple-element.179), channel_id=1, source_target_pairs={{0,14},{1,15},{2,12},{3,13},{4,10},{5,11},{6,8},{7,9},{8,6},{9,7},... | collective-permute-start | bytes 202760 | tf_op jit(solution)/shard_map/ppermute | solution.py:388
  156.6 7.0 %collective-permute-start.74 = (bf16[264,128]{1,0:T(8,128)(2,1)S(1)}, bf16[264,128]{1,0:T(8,128)(2,1)S(1)}, u32[]{:S(2)}, u32[]{:S(2)}) collective-permute-start(bf16[264,128]{1,0:T(8,128)(2,1)S(1)} %get-tuple-element.181), channel_id=1, source_target_pairs={{0,15},{1,14},{2,13},{3,12},{4,11},{5,10},{6,9},{7,8},{8,7},{9,6},... | collective-permute-start | bytes 202760 | tf_op jit(solution)/shard_map/ppermute | solution.py:388
  (17 other events, 252.2 us)

commit v11 on v10

--- a/solution.py
+++ b/solution.py
@@ -156,6 +156,18 @@
             asked = table_ref[peer * BCAP + rank].astype(F32)
             rows = jnp.where((place == 3) & (lane == rank), asked, rows)
         message_ref[BCAP * cols :, :] = rows.astype(BF16)
+
+
+def keep_kernel(after_ref, target_hbm, rays_hbm, target_ref, rays_ref, sems):
+    del after_ref
+    copies = [
+        pltpu.make_async_copy(target_hbm, target_ref, sems.at[0]),
+        pltpu.make_async_copy(rays_hbm, rays_ref, sems.at[1]),
+    ]
+    for copy in copies:
+        copy.start()
+    for copy in copies:
+        copy.wait()
 
 
 def pair_kernel(peers, target_ref, *refs):
@@ -412,6 +424,12 @@
     current = times
     for step in range(ITERS):
         fetched = exchange(replies)
+        if step == 0:
+            target, ray_blocks = call(
+                keep_kernel, "keep", [VMEM, HBM, HBM],
+                [((slots,), jnp.int32, SMEM), (ray_blocks.shape, BF16, VMEM)],
+                [pltpu.SemaphoreType.DMA((2,))], 0, 8 << 20, 48 << 20,
+            )(beta, target, ray_blocks)
         last = step + 1 == ITERS
         made = call(
             functools.partial(pair_kernel, peers), "pairs_last" if last else "pairs",

time: 179 us -> 176 us (0.983)
  waiting for transfers between devices: 43.3 us -> 39.6 us
  Pallas kernels: 21.6 us -> 24.6 us
  local copies, waits for them, and re-layouts: 3.68 us -> 1.52 us
    ppermute x75, waiting for transfers between devices: 43.3 us -> 39.6 us  [exchange(): lax.ppermute(value, 'pair', [(one, one ^ step) for one in range(peers)])]
    pallas_call x0 -> x1, Pallas kernels: none -> 2.84 us  [on_device(): call(keep_kernel, 'keep', [VMEM, HBM, HBM], [((slots,), jnp.int32, SMEM),...]
    unnamed x12 -> x6, local copies, waits for them, and re-layouts: 3.68 us -> 1.52 us
  transfers between devices with their start and end apart: 75 -> 75, of which waited for: 28 -> 26; matrix products, arithmetic and copies ran while one was open for 0% -> 0% of each run, Pallas kernels for 0% -> 2%
where the time goes in v11:
time: 176 us
  starting transfers between devices  99.2 us (56%)
  waiting for transfers between devices  39.6 us (22%)
  Pallas kernels  24.6 us (14%)
  blocking collectives  10.1 us (6%)
    ppermute x75, starting transfers between devices, exchange(): lax.ppermute(value, 'pair', [(one, one ^ step) for one in range(peers)])  99.2 us
    ppermute x75, waiting for transfers between devices, exchange(): lax.ppermute(value, 'pair', [(one, one ^ step) for one in range(peers)])  39.6 us
    all_to_all x1, blocking collectives, on_device(): lax.all_to_all(tails, 'pair', split_axis=0, concat_axis=0, tiled=True)  10.1 us
    pallas_call x2, Pallas kernels, on_device(): call(functools.partial(pair_kernel, peers), 'pairs_last' if last else 'pa...  7.05 us
    pallas_call x1, Pallas kernels, on_device(): call(functools.partial(start_kernel, peers), 'start', [SMEM, HBM, HBM, HB...  5.72 us
  transfers between devices with their start and end apart: 75, of which 26 were waited for; matrix products, arithmetic and copies ran while one was open for 0% of the time, Pallas kernels for 2%

profile of v11, /device:TPU:0, one launch (start us, length us, event | category | flops | bytes accessed | tf_op | source)
XLA Modules:
  0.0 176.0 jit_solution(5866877139049597599)
XLA Ops:
  0.6 5.7 %start.1 = (bf16[264,128]{1,0:T(8,128)(2,1)}, bf16[264,128]{1,0:T(8,128)(2,1)}, bf16[264,128]{1,0:T(8,128)(2,1)}, bf16[264,128]{1,0:T(8,128)(2,1)}, bf16[264,128...) custom-call(s32[1]{0:T(128)} %bitcast.me_ref, ...), custom_call_target="tpu_custom_call" | custom-call | flops 268435456 | bytes 6291456 | tf_op jit(solution)/shard_map/start/pallas_call | solution.py:405
  6.4 4.1 %collective-permute-start = (bf16[264,128]{1,0:T(8,128)(2,1)}, bf16[264,128]{1,0:T(8,128)(2,1)S(1)}, u32[]{:S(2)}, u32[]{:S(2)}) collective-permute-start(bf16[264,128]{1,0:T(8,128)(2,1)} %get-tuple-element.98), channel_id=1, source_target_pairs={{0,8},{1,9},{2,10},{3,11},{4,12},{5,13},{6,14},{7,15},{8,0},{9,1},... | collective-permute-start | bytes 202760 | tf_op jit(solution)/shard_map/ppermute | solution.py:400
  10.7 1.7 collective-permute-start.3
  12.4 2.6 %collective-permute-start.4 = (bf16[264,128]{1,0:T(8,128)(2,1)}, bf16[264,128]{1,0:T(8,128)(2,1)S(1)}, u32[]{:S(2)}, u32[]{:S(2)}) collective-permute-start(bf16[264,128]{1,0:T(8,128)(2,1)} %get-tuple-element.102), channel_id=1, source_target_pairs={{0,10},{1,11},{2,8},{3,9},{4,14},{5,15},{6,12},{7,13},{8,2},{9,3},... | collective-permute-start | bytes 202760 | tf_op jit(solution)/shard_map/ppermute | solution.py:400
  15.6 2.1 %collective-permute-start.6 = (bf16[264,128]{1,0:T(8,128)(2,1)}, bf16[264,128]{1,0:T(8,128)(2,1)S(1)}, u32[]{:S(2)}, u32[]{:S(2)}) collective-permute-start(bf16[264,128]{1,0:T(8,128)(2,1)} %get-tuple-element.104), channel_id=1, source_target_pairs={{0,11},{1,10},{2,9},{3,8},{4,15},{5,14},{6,13},{7,12},{8,3},{9,2},... | collective-permute-start | bytes 202760 | tf_op jit(solution)/shard_map/ppermute | solution.py:400
  17.6 4.4 %collective-permute-start.7 = (bf16[264,128]{1,0:T(8,128)(2,1)}, bf16[264,128]{1,0:T(8,128)(2,1)S(1)}, u32[]{:S(2)}, u32[]{:S(2)}) collective-permute-start(bf16[264,128]{1,0:T(8,128)(2,1)} %get-tuple-element.105), channel_id=1, source_target_pairs={{0,4},{1,5},{2,6},{3,7},{4,0},{5,1},{6,2},{7,3},{8,12},{9,13},{10,... | collective-permute-start | bytes 202760 | tf_op jit(solution)/shard_map/ppermute | solution.py:400
  22.4 4.4 %collective-permute-start.10 = (bf16[264,128]{1,0:T(8,128)(2,1)}, bf16[264,128]{1,0:T(8,128)(2,1)S(1)}, u32[]{:S(2)}, u32[]{:S(2)}) collective-permute-start(bf16[264,128]{1,0:T(8,128)(2,1)} %get-tuple-element.108), channel_id=1, source_target_pairs={{0,13},{1,12},{2,15},{3,14},{4,9},{5,8},{6,11},{7,10},{8,5},{9,4},... | collective-permute-start | bytes 202760 | tf_op jit(solution)/shard_map/ppermute | solution.py:400
  27.6 1.9 %collective-permute-start.12 = (bf16[264,128]{1,0:T(8,128)(2,1)}, bf16[264,128]{1,0:T(8,128)(2,1)S(1)}, u32[]{:S(2)}, u32[]{:S(2)}) collective-permute-start(bf16[264,128]{1,0:T(8,128)(2,1)} %get-tuple-element.110), channel_id=1, source_target_pairs={{0,14},{1,15},{2,12},{3,13},{4,10},{5,11},{6,8},{7,9},{8,6},{9,7},... | collective-permute-start | bytes 202760 | tf_op jit(solution)/shard_map/ppermute | solution.py:400
  29.9 3.4 %collective-permute-start.14 = (bf16[264,128]{1,0:T(8,128)(2,1)}, bf16[264,128]{1,0:T(8,128)(2,1)S(1)}, u32[]{:S(2)}, u32[]{:S(2)}) collective-permute-start(bf16[264,128]{1,0:T(8,128)(2,1)} %get-tuple-element.112), channel_id=1, source_target_pairs={{0,15},{1,14},{2,13},{3,12},{4,11},{5,10},{6,9},{7,8},{8,7},{9,6},... | collective-permute-start | bytes 202760 | tf_op jit(solution)/shard_map/ppermute | solution.py:400
  33.3 1.7 collective-permute-done.12.refs_13_
  35.8 1.7 collective-permute-done.14.refs_15_
  38.4 2.5 %cells_first.1 = (f32[64,8192]{1,0:T(8,128)S(1)}, f32[64,128]{1,0:T(8,128)S(1)}, bf16[264,128]{1,0:T(8,128)(2,1)S(1)}, bf16[264,128]{1,0:T(8,128)(2,1)S(1)}, bf1...) custom-call(bf16[264,128]{1,0:T(8,128)(2,1)S(1)} %copy-done.1, ...), custom_call_target="tpu_custom_call" | custom-call | bytes 6291456 | tf_op jit(solution)/shard_map/cells_first/pallas_call | solution.py:417
  41.1 1.2 collective-permute-start.16
  42.2 1.8 %collective-permute-start.17 = (bf16[264,128]{1,0:T(8,128)(2,1)S(1)}, bf16[264,128]{1,0:T(8,128)(2,1)S(1)}, u32[]{:S(2)}, u32[]{:S(2)}) collective-permute-start(bf16[264,128]{1,0:T(8,128)(2,1)S(1)} %get-tuple-element.120), channel_id=1, source_target_pairs={{0,9},{1,8},{2,11},{3,10},{4,13},{5,12},{6,15},{7,14},{8,1},{9,0},... | collective-permute-start | bytes 202760 | tf_op jit(solution)/shard_map/ppermute | solution.py:400
  44.1 2.1 %collective-permute-start.19 = (bf16[264,128]{1,0:T(8,128)(2,1)S(1)}, bf16[264,128]{1,0:T(8,128)(2,1)S(1)}, u32[]{:S(2)}, u32[]{:S(2)}) collective-permute-start(bf16[264,128]{1,0:T(8,128)(2,1)S(1)} %get-tuple-element.122), channel_id=1, source_target_pairs={{0,10},{1,11},{2,8},{3,9},{4,14},{5,15},{6,12},{7,13},{8,2},{9,3},... | collective-permute-start | bytes 202760 | tf_op jit(solution)/shard_map/ppermute | solution.py:400
  46.2 4.3 %collective-permute-done.15.refs_1_ = bf16[264,128]{1,0:T(8,128)(2,1)S(1)} collective-permute-done((bf16[264,128]{1,0:T(8,128)(2,1)S(1)}, bf16[264,128]{1,0:T(8,128)(2,1)S(1)}, u32[]{:S(2)}, u32[]{:S(2)}) %collective-permute-start.15) | collective-permute-done | bytes 67616 | tf_op jit(solution)/shard_map/ppermute | solution.py:400
  52.7 3.4 %collective-permute-start.23 = (bf16[264,128]{1,0:T(8,128)(2,1)S(1)}, bf16[264,128]{1,0:T(8,128)(2,1)S(1)}, u32[]{:S(2)}, u32[]{:S(2)}) collective-permute-start(bf16[264,128]{1,0:T(8,128)(2,1)S(1)} %get-tuple-element.126), channel_id=1, source_target_pairs={{0,12},{1,13},{2,14},{3,15},{4,8},{5,9},{6,10},{7,11},{8,4},{9,5},... | collective-permute-start | bytes 202760 | tf_op jit(solution)/shard_map/ppermute | solution.py:400
  56.6 2.5 %collective-permute-start.26 = (bf16[264,128]{1,0:T(8,128)(2,1)S(1)}, bf16[264,128]{1,0:T(8,128)(2,1)S(1)}, u32[]{:S(2)}, u32[]{:S(2)}) collective-permute-start(bf16[264,128]{1,0:T(8,128)(2,1)S(1)} %get-tuple-element.129), channel_id=1, source_target_pairs={{0,6},{1,7},{2,4},{3,5},{4,2},{5,3},{6,0},{7,1},{8,14},{9,15},{10,... | collective-permute-start | bytes 202760 | tf_op jit(solution)/shard_map/ppermute | solution.py:400
  59.1 2.6 %collective-permute-start.27 = (bf16[264,128]{1,0:T(8,128)(2,1)S(1)}, bf16[264,128]{1,0:T(8,128)(2,1)S(1)}, u32[]{:S(2)}, u32[]{:S(2)}) collective-permute-start(bf16[264,128]{1,0:T(8,128)(2,1)S(1)} %get-tuple-element.130), channel_id=1, source_target_pairs={{0,14},{1,15},{2,12},{3,13},{4,10},{5,11},{6,8},{7,9},{8,6},{9,7},... | collective-permute-start | bytes 202760 | tf_op jit(solution)/shard_map/ppermute | solution.py:400
  61.7 1.4 collective-permute-start.29
  63.7 2.8 %keep.1 = (s32[128]{0:T(128)S(1)}, bf16[8,16,128,128]{3,2,1,0:T(8,128)(2,1)S(1)}) custom-call(f32[64,128]{1,0:T(8,128)S(1)} %get-tuple-element.114.after_ref.refs_17_.refs_18_.refs_20_, s32[128]{0:T(128)S(1)} %copy-done.2, bf16[8,16,128,128]{3,2,1,0:T(8,128)(2,1)} %rays_hbm.3), custom_call_target="tpu_custom_call" | custom-call | bytes 8388608 | tf_op jit(solution)/shard_map/keep/pallas_call | solution.py:428
  67.0 1.8 %collective-permute-done.29.refs_15_ = bf16[264,128]{1,0:T(8,128)(2,1)S(1)} collective-permute-done((bf16[264,128]{1,0:T(8,128)(2,1)S(1)}, bf16[264,128]{1,0:T(8,128)(2,1)S(1)}, u32[]{:S(2)}, u32[]{:S(2)}) %collective-permute-start.29) | collective-permute-done | bytes 67616 | tf_op jit(solution)/shard_map/ppermute | solution.py:400
  68.8 3.5 %pairs.1 = (bf16[264,128]{1,0:T(8,128)(2,1)S(1)}, bf16[264,128]{1,0:T(8,128)(2,1)S(1)}, bf16[264,128]{1,0:T(8,128)(2,1)S(1)}, bf16[264,128]{1,0:T(8,128)(2,1)S(1...) custom-call(s32[128]{0:T(128)S(1)} %get-tuple-element.116.target_ref, ...), custom_call_target="tpu_custom_call" | custom-call | flops 536870912 | bytes 8388608 | tf_op jit(solution)/shard_map/pairs/pallas_call | solution.py:434
  73.7 1.7 collective-permute-start.32
  75.4 1.4 collective-permute-start.33
  77.7 4.0 %collective-permute-done.30.refs_1_ = bf16[264,128]{1,0:T(8,128)(2,1)S(1)} collective-permute-done((bf16[264,128]{1,0:T(8,128)(2,1)S(1)}, bf16[264,128]{1,0:T(8,128)(2,1)S(1)}, u32[]{:S(2)}, u32[]{:S(2)}) %collective-permute-start.30) | collective-permute-done | bytes 67616 | tf_op jit(solution)/shard_map/ppermute | solution.py:400
  82.6 3.5 %collective-permute-start.37 = (bf16[264,128]{1,0:T(8,128)(2,1)S(1)}, bf16[264,128]{1,0:T(8,128)(2,1)S(1)}, u32[]{:S(2)}, u32[]{:S(2)}) collective-permute-start(bf16[264,128]{1,0:T(8,128)(2,1)S(1)} %get-tuple-element.142), channel_id=1, source_target_pairs={{0,4},{1,5},{2,6},{3,7},{4,0},{5,1},{6,2},{7,3},{8,12},{9,13},{10,... | collective-permute-start | bytes 202760 | tf_op jit(solution)/shard_map/ppermute | solution.py:400
  86.0 1.3 collective-permute-start.38
  87.3 1.4 collective-permute-start.40
  89.1 1.3 collective-permute-start.41
  90.4 2.5 %collective-permute-start.42 = (bf16[264,128]{1,0:T(8,128)(2,1)S(1)}, bf16[264,128]{1,0:T(8,128)(2,1)S(1)}, u32[]{:S(2)}, u32[]{:S(2)}) collective-permute-start(bf16[264,128]{1,0:T(8,128)(2,1)S(1)} %get-tuple-element.147), channel_id=1, source_target_pairs={{0,14},{1,15},{2,12},{3,13},{4,10},{5,11},{6,8},{7,9},{8,6},{9,7},... | collective-permute-start | bytes 202760 | tf_op jit(solution)/shard_map/ppermute | solution.py:400
  93.6 2.0 %collective-permute-start.44 = (bf16[264,128]{1,0:T(8,128)(2,1)S(1)}, bf16[264,128]{1,0:T(8,128)(2,1)S(1)}, u32[]{:S(2)}, u32[]{:S(2)}) collective-permute-start(bf16[264,128]{1,0:T(8,128)(2,1)S(1)} %get-tuple-element.149), channel_id=1, source_target_pairs={{0,15},{1,14},{2,13},{3,12},{4,11},{5,10},{6,9},{7,8},{8,7},{9,6},... | collective-permute-start | bytes 202760 | tf_op jit(solution)/shard_map/ppermute | solution.py:400
  95.9 2.1 %collective-permute-done.42.refs_13_ = bf16[264,128]{1,0:T(8,128)(2,1)S(1)} collective-permute-done((bf16[264,128]{1,0:T(8,128)(2,1)S(1)}, bf16[264,128]{1,0:T(8,128)(2,1)S(1)}, u32[]{:S(2)}, u32[]{:S(2)}) %collective-permute-start.42) | collective-permute-done | bytes 67616 | tf_op jit(solution)/shard_map/ppermute | solution.py:400
  98.7 1.7 collective-permute-done.44.refs_15_
  100.4 2.4 %cells.1 = (f32[64,8192]{1,0:T(8,128)S(1)}, f32[64,128]{1,0:T(8,128)S(1)}, bf16[264,128]{1,0:T(8,128)(2,1)S(1)}, bf16[264,128]{1,0:T(8,128)(2,1)S(1)}, bf16[264,...) custom-call(s32[16,128]{1,0:T(8,128)S(1)} %get-tuple-element.113.ask, ...), custom_call_target="tpu_custom_call" | custom-call | bytes 8388608 | tf_op jit(solution)/shard_map/cells/pallas_call | solution.py:443
  102.9 1.1 collective-permute-start.46
  104.0 1.9 %collective-permute-start.47 = (bf16[264,128]{1,0:T(8,128)(2,1)S(1)}, bf16[264,128]{1,0:T(8,128)(2,1)S(1)}, u32[]{:S(2)}, u32[]{:S(2)}) collective-permute-start(bf16[264,128]{1,0:T(8,128)(2,1)S(1)} %get-tuple-element.155), channel_id=1, source_target_pairs={{0,9},{1,8},{2,11},{3,10},{4,13},{5,12},{6,15},{7,14},{8,1},{9,0},... | collective-permute-start | bytes 202760 | tf_op jit(solution)/shard_map/ppermute | solution.py:400
  106.5 1.5 collective-permute-start.49
  108.0 2.9 %collective-permute-done.45.refs_1_ = bf16[264,128]{1,0:T(8,128)(2,1)S(1)} collective-permute-done((bf16[264,128]{1,0:T(8,128)(2,1)S(1)}, bf16[264,128]{1,0:T(8,128)(2,1)S(1)}, u32[]{:S(2)}, u32[]{:S(2)}) %collective-permute-start.45) | collective-permute-done | bytes 67616 | tf_op jit(solution)/shard_map/ppermute | solution.py:400
  111.9 2.6 %collective-permute-start.52 = (bf16[264,128]{1,0:T(8,128)(2,1)S(1)}, bf16[264,128]{1,0:T(8,128)(2,1)S(1)}, u32[]{:S(2)}, u32[]{:S(2)}) collective-permute-start(bf16[264,128]{1,0:T(8,128)(2,1)S(1)} %get-tuple-element.160), channel_id=1, source_target_pairs={{0,4},{1,5},{2,6},{3,7},{4,0},{5,1},{6,2},{7,3},{8,12},{9,13},{10,... | collective-permute-start | bytes 202760 | tf_op jit(solution)/shard_map/ppermute | solution.py:400
  114.5 2.0 %collective-permute-start.53 = (bf16[264,128]{1,0:T(8,128)(2,1)S(1)}, bf16[264,128]{1,0:T(8,128)(2,1)S(1)}, u32[]{:S(2)}, u32[]{:S(2)}) collective-permute-start(bf16[264,128]{1,0:T(8,128)(2,1)S(1)} %get-tuple-element.161), channel_id=1, source_target_pairs={{0,12},{1,13},{2,14},{3,15},{4,8},{5,9},{6,10},{7,11},{8,4},{9,5},... | collective-permute-start | bytes 202760 | tf_op jit(solution)/shard_map/ppermute | solution.py:400
  117.8 2.0 %collective-permute-start.56 = (bf16[264,128]{1,0:T(8,128)(2,1)S(1)}, bf16[264,128]{1,0:T(8,128)(2,1)S(1)}, u32[]{:S(2)}, u32[]{:S(2)}) collective-permute-start(bf16[264,128]{1,0:T(8,128)(2,1)S(1)} %get-tuple-element.164), channel_id=1, source_target_pairs={{0,6},{1,7},{2,4},{3,5},{4,2},{5,3},{6,0},{7,1},{8,14},{9,15},{10,... | collective-permute-start | bytes 202760 | tf_op jit(solution)/shard_map/ppermute | solution.py:400
  119.8 2.9 %collective-permute-start.57 = (bf16[264,128]{1,0:T(8,128)(2,1)S(1)}, bf16[264,128]{1,0:T(8,128)(2,1)S(1)}, u32[]{:S(2)}, u32[]{:S(2)}) collective-permute-start(bf16[264,128]{1,0:T(8,128)(2,1)S(1)} %get-tuple-element.165), channel_id=1, source_target_pairs={{0,14},{1,15},{2,12},{3,13},{4,10},{5,11},{6,8},{7,9},{8,6},{9,7},... | collective-permute-start | bytes 202760 | tf_op jit(solution)/shard_map/ppermute | solution.py:400
  123.1 1.8 %collective-permute-start.59 = (bf16[264,128]{1,0:T(8,128)(2,1)S(1)}, bf16[264,128]{1,0:T(8,128)(2,1)S(1)}, u32[]{:S(2)}, u32[]{:S(2)}) collective-permute-start(bf16[264,128]{1,0:T(8,128)(2,1)S(1)} %get-tuple-element.167), channel_id=1, source_target_pairs={{0,15},{1,14},{2,13},{3,12},{4,11},{5,10},{6,9},{7,8},{8,7},{9,6},... | collective-permute-start | bytes 202760 | tf_op jit(solution)/shard_map/ppermute | solution.py:400
  125.3 2.3 %collective-permute-done.57.refs_13_ = bf16[264,128]{1,0:T(8,128)(2,1)S(1)} collective-permute-done((bf16[264,128]{1,0:T(8,128)(2,1)S(1)}, bf16[264,128]{1,0:T(8,128)(2,1)S(1)}, u32[]{:S(2)}, u32[]{:S(2)}) %collective-permute-start.57) | collective-permute-done | bytes 67616 | tf_op jit(solution)/shard_map/ppermute | solution.py:400
  128.5 1.6 collective-permute-done.59.refs_15_
  130.1 3.5 %pairs_last.1 = (bf16[264,128]{1,0:T(8,128)(2,1)S(1)}, bf16[264,128]{1,0:T(8,128)(2,1)S(1)}, bf16[264,128]{1,0:T(8,128)(2,1)S(1)}, bf16[264,128]{1,0:T(8,128)(2,...) custom-call(s32[128]{0:T(128)S(1)} %get-tuple-element.116.target_ref, ...), custom_call_target="tpu_custom_call" | custom-call | flops 536870912 | bytes 8388608 | tf_op jit(solution)/shard_map/pairs_last/pallas_call | solution.py:434
  133.7 1.7 collective-permute-start.60
  135.4 1.4 collective-permute-start.62
  136.8 1.3 collective-permute-start.63
  138.0 1.8 %collective-permute-start.64 = (bf16[264,128]{1,0:T(8,128)(2,1)S(1)}, bf16[264,128]{1,0:T(8,128)(2,1)S(1)}, u32[]{:S(2)}, u32[]{:S(2)}) collective-permute-start(bf16[264,128]{1,0:T(8,128)(2,1)S(1)} %get-tuple-element.175), channel_id=1, source_target_pairs={{0,10},{1,11},{2,8},{3,9},{4,14},{5,15},{6,12},{7,13},{8,2},{9,3},... | collective-permute-start | bytes 202760 | tf_op jit(solution)/shard_map/ppermute | solution.py:400
  139.9 1.6 collective-permute-done.60.refs_1_
  142.4 1.5 collective-permute-done.62.refs_3_
  143.8 1.7 collective-permute-start.67
  145.5 1.5 collective-permute-start.68
  147.1 2.3 %collective-permute-start.70 = (bf16[264,128]{1,0:T(8,128)(2,1)S(1)}, bf16[264,128]{1,0:T(8,128)(2,1)S(1)}, u32[]{:S(2)}, u32[]{:S(2)}) collective-permute-start(bf16[264,128]{1,0:T(8,128)(2,1)S(1)} %get-tuple-element.181), channel_id=1, source_target_pairs={{0,13},{1,12},{2,15},{3,14},{4,9},{5,8},{6,11},{7,10},{8,5},{9,4},... | collective-permute-start | bytes 202760 | tf_op jit(solution)/shard_map/ppermute | solution.py:400
  149.4 2.8 %collective-permute-start.71 = (bf16[264,128]{1,0:T(8,128)(2,1)S(1)}, bf16[264,128]{1,0:T(8,128)(2,1)S(1)}, u32[]{:S(2)}, u32[]{:S(2)}) collective-permute-start(bf16[264,128]{1,0:T(8,128)(2,1)S(1)} %get-tuple-element.182), channel_id=1, source_target_pairs={{0,6},{1,7},{2,4},{3,5},{4,2},{5,3},{6,0},{7,1},{8,14},{9,15},{10,... | collective-permute-start | bytes 202760 | tf_op jit(solution)/shard_map/ppermute | solution.py:400
  152.6 1.7 collective-permute-start.73
  154.3 1.5 collective-permute-start.74
  156.3 3.1 %collective-permute-done.72.refs_13_ = bf16[264,128]{1,0:T(8,128)(2,1)S(1)} collective-permute-done((bf16[264,128]{1,0:T(8,128)(2,1)S(1)}, bf16[264,128]{1,0:T(8,128)(2,1)S(1)}, u32[]{:S(2)}, u32[]{:S(2)}) %collective-permute-start.72) | collective-permute-done | bytes 67616 | tf_op jit(solution)/shard_map/ppermute | solution.py:400
  159.4 2.2 %collective-permute-done.74.refs_15_ = bf16[264,128]{1,0:T(8,128)(2,1)S(1)} collective-permute-done((bf16[264,128]{1,0:T(8,128)(2,1)S(1)}, bf16[264,128]{1,0:T(8,128)(2,1)S(1)}, u32[]{:S(2)}, u32[]{:S(2)}) %collective-permute-start.74) | collective-permute-done | bytes 67616 | tf_op jit(solution)/shard_map/ppermute | solution.py:400
  161.6 2.6 %cells_last.1 = (f32[64,8192]{1,0:T(8,128)S(1)}, f32[64,128]{1,0:T(8,128)S(1)}, f32[16,8,128]{2,1,0:T(8,128)S(1)}, f32[64,8192]{1,0:T(8,128)}) custom-call(s32[16,128]{1,0:T(8,128)S(1)} %get-tuple-element.113.asked_ref, bf16[264,128]{1,0:T(8,128)(2,1)S(1)} %get-tuple-element.170.refs_0_, bf16[264,128]{1,0:T(8,128)(2,1)S(1)} %collective-permute-done.60.refs_1_, ...), custom_call_target="tpu_custom_call" | custom-call | bytes 10485760 | tf_op jit(solution)/shard_map/cells_last/pallas_call | solution.py:450
  164.2 10.1 %all_to_all.5.tails_ref = f32[16,8,128]{2,1,0:T(8,128)S(1)} all-to-all(f32[16,8,128]{2,1,0:T(8,128)S(1)} %get-tuple-element.189), channel_id=1, replica_groups=mesh['groups'=2,'pair'=16] {'pair'}, dimensions={0} | all-to-all | bytes 131072 | tf_op jit(solution)/shard_map/all_to_all | solution.py:455
  174.3 1.5 model.1
  (101 shorter events, 19.7 us)
Async XLA Ops:
  6.4 8.7 %collective-permute-start = (bf16[264,128]{1,0:T(8,128)(2,1)}, bf16[264,128]{1,0:T(8,128)(2,1)S(1)}, u32[]{:S(2)}, u32[]{:S(2)}) collective-permute-start(bf16[264,128]{1,0:T(8,128)(2,1)} %get-tuple-element.98), channel_id=1, source_target_pairs={{0,8},{1,9},{2,10},{3,11},{4,12},{5,13},{6,14},{7,15},{8,0},{9,1},... | collective-permute-start | bytes 202760 | tf_op jit(solution)/shard_map/ppermute | solution.py:400
  10.5 7.1 %collective-permute-start.2 = (bf16[264,128]{1,0:T(8,128)(2,1)}, bf16[264,128]{1,0:T(8,128)(2,1)S(1)}, u32[]{:S(2)}, u32[]{:S(2)}) collective-permute-start(bf16[264,128]{1,0:T(8,128)(2,1)} %get-tuple-element.100), channel_id=1, source_target_pairs={{0,9},{1,8},{2,11},{3,10},{4,13},{5,12},{6,15},{7,14},{8,1},{9,0},... | collective-permute-start | bytes 202760 | tf_op jit(solution)/shard_map/ppermute | solution.py:400
  10.7 11.3 %collective-permute-start.3 = (bf16[264,128]{1,0:T(8,128)(2,1)}, bf16[264,128]{1,0:T(8,128)(2,1)S(1)}, u32[]{:S(2)}, u32[]{:S(2)}) collective-permute-start(bf16[264,128]{1,0:T(8,128)(2,1)} %get-tuple-element.101), channel_id=1, source_target_pairs={{0,2},{1,3},{2,0},{3,1},{4,6},{5,7},{6,4},{7,5},{8,10},{9,11},{10,... | collective-permute-start | bytes 202760 | tf_op jit(solution)/shard_map/ppermute | solution.py:400
  12.4 9.6 %collective-permute-start.4 = (bf16[264,128]{1,0:T(8,128)(2,1)}, bf16[264,128]{1,0:T(8,128)(2,1)S(1)}, u32[]{:S(2)}, u32[]{:S(2)}) collective-permute-start(bf16[264,128]{1,0:T(8,128)(2,1)} %get-tuple-element.102), channel_id=1, source_target_pairs={{0,10},{1,11},{2,8},{3,9},{4,14},{5,15},{6,12},{7,13},{8,2},{9,3},... | collective-permute-start | bytes 202760 | tf_op jit(solution)/shard_map/ppermute | solution.py:400
  15.0 7.4 %collective-permute-start.5 = (bf16[264,128]{1,0:T(8,128)(2,1)}, bf16[264,128]{1,0:T(8,128)(2,1)S(1)}, u32[]{:S(2)}, u32[]{:S(2)}) collective-permute-start(bf16[264,128]{1,0:T(8,128)(2,1)} %get-tuple-element.103), channel_id=1, source_target_pairs={{0,3},{1,2},{2,1},{3,0},{4,7},{5,6},{6,5},{7,4},{8,11},{9,10},{10,... | collective-permute-start | bytes 202760 | tf_op jit(solution)/shard_map/ppermute | solution.py:400
  15.6 11.2 %collective-permute-start.6 = (bf16[264,128]{1,0:T(8,128)(2,1)}, bf16[264,128]{1,0:T(8,128)(2,1)S(1)}, u32[]{:S(2)}, u32[]{:S(2)}) collective-permute-start(bf16[264,128]{1,0:T(8,128)(2,1)} %get-tuple-element.104), channel_id=1, source_target_pairs={{0,11},{1,10},{2,9},{3,8},{4,15},{5,14},{6,13},{7,12},{8,3},{9,2},... | collective-permute-start | bytes 202760 | tf_op jit(solution)/shard_map/ppermute | solution.py:400
  17.6 10.0 %collective-permute-start.7 = (bf16[264,128]{1,0:T(8,128)(2,1)}, bf16[264,128]{1,0:T(8,128)(2,1)S(1)}, u32[]{:S(2)}, u32[]{:S(2)}) collective-permute-start(bf16[264,128]{1,0:T(8,128)(2,1)} %get-tuple-element.105), channel_id=1, source_target_pairs={{0,4},{1,5},{2,6},{3,7},{4,0},{5,1},{6,2},{7,3},{8,12},{9,13},{10,... | collective-permute-start | bytes 202760 | tf_op jit(solution)/shard_map/ppermute | solution.py:400
  22.0 7.5 %collective-permute-start.8 = (bf16[264,128]{1,0:T(8,128)(2,1)}, bf16[264,128]{1,0:T(8,128)(2,1)S(1)}, u32[]{:S(2)}, u32[]{:S(2)}) collective-permute-start(bf16[264,128]{1,0:T(8,128)(2,1)} %get-tuple-element.106), channel_id=1, source_target_pairs={{0,12},{1,13},{2,14},{3,15},{4,8},{5,9},{6,10},{7,11},{8,4},{9,5},... | collective-permute-start | bytes 202760 | tf_op jit(solution)/shard_map/ppermute | solution.py:400
  22.0 7.8 %collective-permute-start.9 = (bf16[264,128]{1,0:T(8,128)(2,1)}, bf16[264,128]{1,0:T(8,128)(2,1)S(1)}, u32[]{:S(2)}, u32[]{:S(2)}) collective-permute-start(bf16[264,128]{1,0:T(8,128)(2,1)} %get-tuple-element.107), channel_id=1, source_target_pairs={{0,5},{1,4},{2,7},{3,6},{4,1},{5,0},{6,3},{7,2},{8,13},{9,12},{10,... | collective-permute-start | bytes 202760 | tf_op jit(solution)/shard_map/ppermute | solution.py:400
  22.4 10.9 %collective-permute-start.10 = (bf16[264,128]{1,0:T(8,128)(2,1)}, bf16[264,128]{1,0:T(8,128)(2,1)S(1)}, u32[]{:S(2)}, u32[]{:S(2)}) collective-permute-start(bf16[264,128]{1,0:T(8,128)(2,1)} %get-tuple-element.108), channel_id=1, source_target_pairs={{0,13},{1,12},{2,15},{3,14},{4,9},{5,8},{6,11},{7,10},{8,5},{9,4},... | collective-permute-start | bytes 202760 | tf_op jit(solution)/shard_map/ppermute | solution.py:400
  26.8 6.5 %collective-permute-start.11 = (bf16[264,128]{1,0:T(8,128)(2,1)}, bf16[264,128]{1,0:T(8,128)(2,1)S(1)}, u32[]{:S(2)}, u32[]{:S(2)}) collective-permute-start(bf16[264,128]{1,0:T(8,128)(2,1)} %get-tuple-element.109), channel_id=1, source_target_pairs={{0,6},{1,7},{2,4},{3,5},{4,2},{5,3},{6,0},{7,1},{8,14},{9,15},{10,... | collective-permute-start | bytes 202760 | tf_op jit(solution)/shard_map/ppermute | solution.py:400
  27.6 7.3 %collective-permute-start.12 = (bf16[264,128]{1,0:T(8,128)(2,1)}, bf16[264,128]{1,0:T(8,128)(2,1)S(1)}, u32[]{:S(2)}, u32[]{:S(2)}) collective-permute-start(bf16[264,128]{1,0:T(8,128)(2,1)} %get-tuple-element.110), channel_id=1, source_target_pairs={{0,14},{1,15},{2,12},{3,13},{4,10},{5,11},{6,8},{7,9},{8,6},{9,7},... | collective-permute-start | bytes 202760 | tf_op jit(solution)/shard_map/ppermute | solution.py:400
  29.5 6.3 %collective-permute-start.13 = (bf16[264,128]{1,0:T(8,128)(2,1)}, bf16[264,128]{1,0:T(8,128)(2,1)S(1)}, u32[]{:S(2)}, u32[]{:S(2)}) collective-permute-start(bf16[264,128]{1,0:T(8,128)(2,1)} %get-tuple-element.111), channel_id=1, source_target_pairs={{0,7},{1,6},{2,5},{3,4},{4,3},{5,2},{6,1},{7,0},{8,15},{9,14},{10,... | collective-permute-start | bytes 202760 | tf_op jit(solution)/shard_map/ppermute | solution.py:400
  29.9 7.7 %collective-permute-start.14 = (bf16[264,128]{1,0:T(8,128)(2,1)}, bf16[264,128]{1,0:T(8,128)(2,1)S(1)}, u32[]{:S(2)}, u32[]{:S(2)}) collective-permute-start(bf16[264,128]{1,0:T(8,128)(2,1)} %get-tuple-element.112), channel_id=1, source_target_pairs={{0,15},{1,14},{2,13},{3,12},{4,11},{5,10},{6,9},{7,8},{8,7},{9,6},... | collective-permute-start | bytes 202760 | tf_op jit(solution)/shard_map/ppermute | solution.py:400
  40.9 9.6 %collective-permute-start.15 = (bf16[264,128]{1,0:T(8,128)(2,1)S(1)}, bf16[264,128]{1,0:T(8,128)(2,1)S(1)}, u32[]{:S(2)}, u32[]{:S(2)}) collective-permute-start(bf16[264,128]{1,0:T(8,128)(2,1)S(1)} %get-tuple-element.118), channel_id=1, source_target_pairs={{0,8},{1,9},{2,10},{3,11},{4,12},{5,13},{6,14},{7,15},{8,0},{9,1},... | collective-permute-start | bytes 202760 | tf_op jit(solution)/shard_map/ppermute | solution.py:400
  41.1 9.4 %collective-permute-start.16 = (bf16[264,128]{1,0:T(8,128)(2,1)S(1)}, bf16[264,128]{1,0:T(8,128)(2,1)S(1)}, u32[]{:S(2)}, u32[]{:S(2)}) collective-permute-start(bf16[264,128]{1,0:T(8,128)(2,1)S(1)} %get-tuple-element.119), channel_id=1, source_target_pairs={{0,1},{1,0},{2,3},{3,2},{4,5},{5,4},{6,7},{7,6},{8,9},{9,8},{10,11... | collective-permute-start | bytes 202760 | tf_op jit(solution)/shard_map/ppermute | solution.py:400
  42.2 9.4 %collective-permute-start.17 = (bf16[264,128]{1,0:T(8,128)(2,1)S(1)}, bf16[264,128]{1,0:T(8,128)(2,1)S(1)}, u32[]{:S(2)}, u32[]{:S(2)}) collective-permute-start(bf16[264,128]{1,0:T(8,128)(2,1)S(1)} %get-tuple-element.120), channel_id=1, source_target_pairs={{0,9},{1,8},{2,11},{3,10},{4,13},{5,12},{6,15},{7,14},{8,1},{9,0},... | collective-permute-start | bytes 202760 | tf_op jit(solution)/shard_map/ppermute | solution.py:400
  44.0 8.6 %collective-permute-start.18 = (bf16[264,128]{1,0:T(8,128)(2,1)S(1)}, bf16[264,128]{1,0:T(8,128)(2,1)S(1)}, u32[]{:S(2)}, u32[]{:S(2)}) collective-permute-start(bf16[264,128]{1,0:T(8,128)(2,1)S(1)} %get-tuple-element.121), channel_id=1, source_target_pairs={{0,2},{1,3},{2,0},{3,1},{4,6},{5,7},{6,4},{7,5},{8,10},{9,11},{10,... | collective-permute-start | bytes 202760 | tf_op jit(solution)/shard_map/ppermute | solution.py:400
  44.1 12.0 %collective-permute-start.19 = (bf16[264,128]{1,0:T(8,128)(2,1)S(1)}, bf16[264,128]{1,0:T(8,128)(2,1)S(1)}, u32[]{:S(2)}, u32[]{:S(2)}) collective-permute-start(bf16[264,128]{1,0:T(8,128)(2,1)S(1)} %get-tuple-element.122), channel_id=1, source_target_pairs={{0,10},{1,11},{2,8},{3,9},{4,14},{5,15},{6,12},{7,13},{8,2},{9,3},... | collective-permute-start | bytes 202760 | tf_op jit(solution)/shard_map/ppermute | solution.py:400
  51.7 7.5 %collective-permute-start.22 = (bf16[264,128]{1,0:T(8,128)(2,1)S(1)}, bf16[264,128]{1,0:T(8,128)(2,1)S(1)}, u32[]{:S(2)}, u32[]{:S(2)}) collective-permute-start(bf16[264,128]{1,0:T(8,128)(2,1)S(1)} %get-tuple-element.125), channel_id=1, source_target_pairs={{0,4},{1,5},{2,6},{3,7},{4,0},{5,1},{6,2},{7,3},{8,12},{9,13},{10,... | collective-permute-start | bytes 202760 | tf_op jit(solution)/shard_map/ppermute | solution.py:400
  52.7 9.0 %collective-permute-start.23 = (bf16[264,128]{1,0:T(8,128)(2,1)S(1)}, bf16[264,128]{1,0:T(8,128)(2,1)S(1)}, u32[]{:S(2)}, u32[]{:S(2)}) collective-permute-start(bf16[264,128]{1,0:T(8,128)(2,1)S(1)} %get-tuple-element.126), channel_id=1, source_target_pairs={{0,12},{1,13},{2,14},{3,15},{4,8},{5,9},{6,10},{7,11},{8,4},{9,5},... | collective-permute-start | bytes 202760 | tf_op jit(solution)/shard_map/ppermute | solution.py:400
  56.1 10.5 %collective-permute-start.25 = (bf16[264,128]{1,0:T(8,128)(2,1)S(1)}, bf16[264,128]{1,0:T(8,128)(2,1)S(1)}, u32[]{:S(2)}, u32[]{:S(2)}) collective-permute-start(bf16[264,128]{1,0:T(8,128)(2,1)S(1)} %get-tuple-element.128), channel_id=1, source_target_pairs={{0,13},{1,12},{2,15},{3,14},{4,9},{5,8},{6,11},{7,10},{8,5},{9,4},... | collective-permute-start | bytes 202760 | tf_op jit(solution)/shard_map/ppermute | solution.py:400
  56.6 10.0 %collective-permute-start.26 = (bf16[264,128]{1,0:T(8,128)(2,1)S(1)}, bf16[264,128]{1,0:T(8,128)(2,1)S(1)}, u32[]{:S(2)}, u32[]{:S(2)}) collective-permute-start(bf16[264,128]{1,0:T(8,128)(2,1)S(1)} %get-tuple-element.129), channel_id=1, source_target_pairs={{0,6},{1,7},{2,4},{3,5},{4,2},{5,3},{6,0},{7,1},{8,14},{9,15},{10,... | collective-permute-start | bytes 202760 | tf_op jit(solution)/shard_map/ppermute | solution.py:400
  59.1 7.5 %collective-permute-start.27 = (bf16[264,128]{1,0:T(8,128)(2,1)S(1)}, bf16[264,128]{1,0:T(8,128)(2,1)S(1)}, u32[]{:S(2)}, u32[]{:S(2)}) collective-permute-start(bf16[264,128]{1,0:T(8,128)(2,1)S(1)} %get-tuple-element.130), channel_id=1, source_target_pairs={{0,14},{1,15},{2,12},{3,13},{4,10},{5,11},{6,8},{7,9},{8,6},{9,7},... | collective-permute-start | bytes 202760 | tf_op jit(solution)/shard_map/ppermute | solution.py:400
  61.7 7.1 %collective-permute-start.29 = (bf16[264,128]{1,0:T(8,128)(2,1)S(1)}, bf16[264,128]{1,0:T(8,128)(2,1)S(1)}, u32[]{:S(2)}, u32[]{:S(2)}) collective-permute-start(bf16[264,128]{1,0:T(8,128)(2,1)S(1)} %get-tuple-element.132), channel_id=1, source_target_pairs={{0,15},{1,14},{2,13},{3,12},{4,11},{5,10},{6,9},{7,8},{8,7},{9,6},... | collective-permute-start | bytes 202760 | tf_op jit(solution)/shard_map/ppermute | solution.py:400
  72.3 9.4 %collective-permute-start.30 = (bf16[264,128]{1,0:T(8,128)(2,1)S(1)}, bf16[264,128]{1,0:T(8,128)(2,1)S(1)}, u32[]{:S(2)}, u32[]{:S(2)}) collective-permute-start(bf16[264,128]{1,0:T(8,128)(2,1)S(1)} %get-tuple-element.135), channel_id=1, source_target_pairs={{0,8},{1,9},{2,10},{3,11},{4,12},{5,13},{6,14},{7,15},{8,0},{9,1},... | collective-permute-start | bytes 202760 | tf_op jit(solution)/shard_map/ppermute | solution.py:400
  73.0 8.7 %collective-permute-start.31 = (bf16[264,128]{1,0:T(8,128)(2,1)S(1)}, bf16[264,128]{1,0:T(8,128)(2,1)S(1)}, u32[]{:S(2)}, u32[]{:S(2)}) collective-permute-start(bf16[264,128]{1,0:T(8,128)(2,1)S(1)} %get-tuple-element.136), channel_id=1, source_target_pairs={{0,1},{1,0},{2,3},{3,2},{4,5},{5,4},{6,7},{7,6},{8,9},{9,8},{10,11... | collective-permute-start | bytes 202760 | tf_op jit(solution)/shard_map/ppermute | solution.py:400
  73.7 8.8 %collective-permute-start.32 = (bf16[264,128]{1,0:T(8,128)(2,1)S(1)}, bf16[264,128]{1,0:T(8,128)(2,1)S(1)}, u32[]{:S(2)}, u32[]{:S(2)}) collective-permute-start(bf16[264,128]{1,0:T(8,128)(2,1)S(1)} %get-tuple-element.137), channel_id=1, source_target_pairs={{0,9},{1,8},{2,11},{3,10},{4,13},{5,12},{6,15},{7,14},{8,1},{9,0},... | collective-permute-start | bytes 202760 | tf_op jit(solution)/shard_map/ppermute | solution.py:400
  75.4 10.6 %collective-permute-start.33 = (bf16[264,128]{1,0:T(8,128)(2,1)S(1)}, bf16[264,128]{1,0:T(8,128)(2,1)S(1)}, u32[]{:S(2)}, u32[]{:S(2)}) collective-permute-start(bf16[264,128]{1,0:T(8,128)(2,1)S(1)} %get-tuple-element.138), channel_id=1, source_target_pairs={{0,2},{1,3},{2,0},{3,1},{4,6},{5,7},{6,4},{7,5},{8,10},{9,11},{10,... | collective-permute-start | bytes 202760 | tf_op jit(solution)/shard_map/ppermute | solution.py:400
  76.8 10.5 %collective-permute-start.34 = (bf16[264,128]{1,0:T(8,128)(2,1)S(1)}, bf16[264,128]{1,0:T(8,128)(2,1)S(1)}, u32[]{:S(2)}, u32[]{:S(2)}) collective-permute-start(bf16[264,128]{1,0:T(8,128)(2,1)S(1)} %get-tuple-element.139), channel_id=1, source_target_pairs={{0,10},{1,11},{2,8},{3,9},{4,14},{5,15},{6,12},{7,13},{8,2},{9,3},... | collective-permute-start | bytes 202760 | tf_op jit(solution)/shard_map/ppermute | solution.py:400
  81.7 7.3 %collective-permute-start.36 = (bf16[264,128]{1,0:T(8,128)(2,1)S(1)}, bf16[264,128]{1,0:T(8,128)(2,1)S(1)}, u32[]{:S(2)}, u32[]{:S(2)}) collective-permute-start(bf16[264,128]{1,0:T(8,128)(2,1)S(1)} %get-tuple-element.141), channel_id=1, source_target_pairs={{0,11},{1,10},{2,9},{3,8},{4,15},{5,14},{6,13},{7,12},{8,3},{9,2},... | collective-permute-start | bytes 202760 | tf_op jit(solution)/shard_map/ppermute | solution.py:400
  82.6 7.8 %collective-permute-start.37 = (bf16[264,128]{1,0:T(8,128)(2,1)S(1)}, bf16[264,128]{1,0:T(8,128)(2,1)S(1)}, u32[]{:S(2)}, u32[]{:S(2)}) collective-permute-start(bf16[264,128]{1,0:T(8,128)(2,1)S(1)} %get-tuple-element.142), channel_id=1, source_target_pairs={{0,4},{1,5},{2,6},{3,7},{4,0},{5,1},{6,2},{7,3},{8,12},{9,13},{10,... | collective-permute-start | bytes 202760 | tf_op jit(solution)/shard_map/ppermute | solution.py:400
  86.0 6.9 %collective-permute-start.38 = (bf16[264,128]{1,0:T(8,128)(2,1)S(1)}, bf16[264,128]{1,0:T(8,128)(2,1)S(1)}, u32[]{:S(2)}, u32[]{:S(2)}) collective-permute-start(bf16[264,128]{1,0:T(8,128)(2,1)S(1)} %get-tuple-element.143), channel_id=1, source_target_pairs={{0,12},{1,13},{2,14},{3,15},{4,8},{5,9},{6,10},{7,11},{8,4},{9,5},... | collective-permute-start | bytes 202760 | tf_op jit(solution)/shard_map/ppermute | solution.py:400
  87.3 6.3 %collective-permute-start.39 = (bf16[264,128]{1,0:T(8,128)(2,1)S(1)}, bf16[264,128]{1,0:T(8,128)(2,1)S(1)}, u32[]{:S(2)}, u32[]{:S(2)}) collective-permute-start(bf16[264,128]{1,0:T(8,128)(2,1)S(1)} %get-tuple-element.144), channel_id=1, source_target_pairs={{0,5},{1,4},{2,7},{3,6},{4,1},{5,0},{6,3},{7,2},{8,13},{9,12},{10,... | collective-permute-start | bytes 202760 | tf_op jit(solution)/shard_map/ppermute | solution.py:400
  87.3 8.2 %collective-permute-start.40 = (bf16[264,128]{1,0:T(8,128)(2,1)S(1)}, bf16[264,128]{1,0:T(8,128)(2,1)S(1)}, u32[]{:S(2)}, u32[]{:S(2)}) collective-permute-start(bf16[264,128]{1,0:T(8,128)(2,1)S(1)} %get-tuple-element.145), channel_id=1, source_target_pairs={{0,13},{1,12},{2,15},{3,14},{4,9},{5,8},{6,11},{7,10},{8,5},{9,4},... | collective-permute-start | bytes 202760 | tf_op jit(solution)/shard_map/ppermute | solution.py:400
  89.1 6.8 %collective-permute-start.41 = (bf16[264,128]{1,0:T(8,128)(2,1)S(1)}, bf16[264,128]{1,0:T(8,128)(2,1)S(1)}, u32[]{:S(2)}, u32[]{:S(2)}) collective-permute-start(bf16[264,128]{1,0:T(8,128)(2,1)S(1)} %get-tuple-element.146), channel_id=1, source_target_pairs={{0,6},{1,7},{2,4},{3,5},{4,2},{5,3},{6,0},{7,1},{8,14},{9,15},{10,... | collective-permute-start | bytes 202760 | tf_op jit(solution)/shard_map/ppermute | solution.py:400
  90.4 7.6 %collective-permute-start.42 = (bf16[264,128]{1,0:T(8,128)(2,1)S(1)}, bf16[264,128]{1,0:T(8,128)(2,1)S(1)}, u32[]{:S(2)}, u32[]{:S(2)}) collective-permute-start(bf16[264,128]{1,0:T(8,128)(2,1)S(1)} %get-tuple-element.147), channel_id=1, source_target_pairs={{0,14},{1,15},{2,12},{3,13},{4,10},{5,11},{6,8},{7,9},{8,6},{9,7},... | collective-permute-start | bytes 202760 | tf_op jit(solution)/shard_map/ppermute | solution.py:400
  93.6 6.8 %collective-permute-start.44 = (bf16[264,128]{1,0:T(8,128)(2,1)S(1)}, bf16[264,128]{1,0:T(8,128)(2,1)S(1)}, u32[]{:S(2)}, u32[]{:S(2)}) collective-permute-start(bf16[264,128]{1,0:T(8,128)(2,1)S(1)} %get-tuple-element.149), channel_id=1, source_target_pairs={{0,15},{1,14},{2,13},{3,12},{4,11},{5,10},{6,9},{7,8},{8,7},{9,6},... | collective-permute-start | bytes 202760 | tf_op jit(solution)/shard_map/ppermute | solution.py:400
  102.8 8.1 %collective-permute-start.45 = (bf16[264,128]{1,0:T(8,128)(2,1)S(1)}, bf16[264,128]{1,0:T(8,128)(2,1)S(1)}, u32[]{:S(2)}, u32[]{:S(2)}) collective-permute-start(bf16[264,128]{1,0:T(8,128)(2,1)S(1)} %get-tuple-element.153), channel_id=1, source_target_pairs={{0,8},{1,9},{2,10},{3,11},{4,12},{5,13},{6,14},{7,15},{8,0},{9,1},... | collective-permute-start | bytes 202760 | tf_op jit(solution)/shard_map/ppermute | solution.py:400
  102.9 8.1 %collective-permute-start.46 = (bf16[264,128]{1,0:T(8,128)(2,1)S(1)}, bf16[264,128]{1,0:T(8,128)(2,1)S(1)}, u32[]{:S(2)}, u32[]{:S(2)}) collective-permute-start(bf16[264,128]{1,0:T(8,128)(2,1)S(1)} %get-tuple-element.154), channel_id=1, source_target_pairs={{0,1},{1,0},{2,3},{3,2},{4,5},{5,4},{6,7},{7,6},{8,9},{9,8},{10,11... | collective-permute-start | bytes 202760 | tf_op jit(solution)/shard_map/ppermute | solution.py:400
  104.0 7.9 %collective-permute-start.47 = (bf16[264,128]{1,0:T(8,128)(2,1)S(1)}, bf16[264,128]{1,0:T(8,128)(2,1)S(1)}, u32[]{:S(2)}, u32[]{:S(2)}) collective-permute-start(bf16[264,128]{1,0:T(8,128)(2,1)S(1)} %get-tuple-element.155), channel_id=1, source_target_pairs={{0,9},{1,8},{2,11},{3,10},{4,13},{5,12},{6,15},{7,14},{8,1},{9,0},... | collective-permute-start | bytes 202760 | tf_op jit(solution)/shard_map/ppermute | solution.py:400
  105.9 8.6 %collective-permute-start.48 = (bf16[264,128]{1,0:T(8,128)(2,1)S(1)}, bf16[264,128]{1,0:T(8,128)(2,1)S(1)}, u32[]{:S(2)}, u32[]{:S(2)}) collective-permute-start(bf16[264,128]{1,0:T(8,128)(2,1)S(1)} %get-tuple-element.156), channel_id=1, source_target_pairs={{0,2},{1,3},{2,0},{3,1},{4,6},{5,7},{6,4},{7,5},{8,10},{9,11},{10,... | collective-permute-start | bytes 202760 | tf_op jit(solution)/shard_map/ppermute | solution.py:400
  106.5 10.6 %collective-permute-start.49 = (bf16[264,128]{1,0:T(8,128)(2,1)S(1)}, bf16[264,128]{1,0:T(8,128)(2,1)S(1)}, u32[]{:S(2)}, u32[]{:S(2)}) collective-permute-start(bf16[264,128]{1,0:T(8,128)(2,1)S(1)} %get-tuple-element.157), channel_id=1, source_target_pairs={{0,10},{1,11},{2,8},{3,9},{4,14},{5,15},{6,12},{7,13},{8,2},{9,3},... | collective-permute-start | bytes 202760 | tf_op jit(solution)/shard_map/ppermute | solution.py:400
  110.9 6.2 %collective-permute-start.50 = (bf16[264,128]{1,0:T(8,128)(2,1)S(1)}, bf16[264,128]{1,0:T(8,128)(2,1)S(1)}, u32[]{:S(2)}, u32[]{:S(2)}) collective-permute-start(bf16[264,128]{1,0:T(8,128)(2,1)S(1)} %get-tuple-element.158), channel_id=1, source_target_pairs={{0,3},{1,2},{2,1},{3,0},{4,7},{5,6},{6,5},{7,4},{8,11},{9,10},{10,... | collective-permute-start | bytes 202760 | tf_op jit(solution)/shard_map/ppermute | solution.py:400
  110.9 6.9 %collective-permute-start.51 = (bf16[264,128]{1,0:T(8,128)(2,1)S(1)}, bf16[264,128]{1,0:T(8,128)(2,1)S(1)}, u32[]{:S(2)}, u32[]{:S(2)}) collective-permute-start(bf16[264,128]{1,0:T(8,128)(2,1)S(1)} %get-tuple-element.159), channel_id=1, source_target_pairs={{0,11},{1,10},{2,9},{3,8},{4,15},{5,14},{6,13},{7,12},{8,3},{9,2},... | collective-permute-start | bytes 202760 | tf_op jit(solution)/shard_map/ppermute | solution.py:400
  111.9 7.9 %collective-permute-start.52 = (bf16[264,128]{1,0:T(8,128)(2,1)S(1)}, bf16[264,128]{1,0:T(8,128)(2,1)S(1)}, u32[]{:S(2)}, u32[]{:S(2)}) collective-permute-start(bf16[264,128]{1,0:T(8,128)(2,1)S(1)} %get-tuple-element.160), channel_id=1, source_target_pairs={{0,4},{1,5},{2,6},{3,7},{4,0},{5,1},{6,2},{7,3},{8,12},{9,13},{10,... | collective-permute-start | bytes 202760 | tf_op jit(solution)/shard_map/ppermute | solution.py:400
  114.5 8.2 %collective-permute-start.53 = (bf16[264,128]{1,0:T(8,128)(2,1)S(1)}, bf16[264,128]{1,0:T(8,128)(2,1)S(1)}, u32[]{:S(2)}, u32[]{:S(2)}) collective-permute-start(bf16[264,128]{1,0:T(8,128)(2,1)S(1)} %get-tuple-element.161), channel_id=1, source_target_pairs={{0,12},{1,13},{2,14},{3,15},{4,8},{5,9},{6,10},{7,11},{8,4},{9,5},... | collective-permute-start | bytes 202760 | tf_op jit(solution)/shard_map/ppermute | solution.py:400
  117.1 7.8 %collective-permute-start.55 = (bf16[264,128]{1,0:T(8,128)(2,1)S(1)}, bf16[264,128]{1,0:T(8,128)(2,1)S(1)}, u32[]{:S(2)}, u32[]{:S(2)}) collective-permute-start(bf16[264,128]{1,0:T(8,128)(2,1)S(1)} %get-tuple-element.163), channel_id=1, source_target_pairs={{0,13},{1,12},{2,15},{3,14},{4,9},{5,8},{6,11},{7,10},{8,5},{9,4},... | collective-permute-start | bytes 202760 | tf_op jit(solution)/shard_map/ppermute | solution.py:400
  117.8 7.4 %collective-permute-start.56 = (bf16[264,128]{1,0:T(8,128)(2,1)S(1)}, bf16[264,128]{1,0:T(8,128)(2,1)S(1)}, u32[]{:S(2)}, u32[]{:S(2)}) collective-permute-start(bf16[264,128]{1,0:T(8,128)(2,1)S(1)} %get-tuple-element.164), channel_id=1, source_target_pairs={{0,6},{1,7},{2,4},{3,5},{4,2},{5,3},{6,0},{7,1},{8,14},{9,15},{10,... | collective-permute-start | bytes 202760 | tf_op jit(solution)/shard_map/ppermute | solution.py:400
  119.8 7.7 %collective-permute-start.57 = (bf16[264,128]{1,0:T(8,128)(2,1)S(1)}, bf16[264,128]{1,0:T(8,128)(2,1)S(1)}, u32[]{:S(2)}, u32[]{:S(2)}) collective-permute-start(bf16[264,128]{1,0:T(8,128)(2,1)S(1)} %get-tuple-element.165), channel_id=1, source_target_pairs={{0,14},{1,15},{2,12},{3,13},{4,10},{5,11},{6,8},{7,9},{8,6},{9,7},... | collective-permute-start | bytes 202760 | tf_op jit(solution)/shard_map/ppermute | solution.py:400
  123.1 7.0 %collective-permute-start.59 = (bf16[264,128]{1,0:T(8,128)(2,1)S(1)}, bf16[264,128]{1,0:T(8,128)(2,1)S(1)}, u32[]{:S(2)}, u32[]{:S(2)}) collective-permute-start(bf16[264,128]{1,0:T(8,128)(2,1)S(1)} %get-tuple-element.167), channel_id=1, source_target_pairs={{0,15},{1,14},{2,13},{3,12},{4,11},{5,10},{6,9},{7,8},{8,7},{9,6},... | collective-permute-start | bytes 202760 | tf_op jit(solution)/shard_map/ppermute | solution.py:400
  133.7 7.8 %collective-permute-start.60 = (bf16[264,128]{1,0:T(8,128)(2,1)S(1)}, bf16[264,128]{1,0:T(8,128)(2,1)S(1)}, u32[]{:S(2)}, u32[]{:S(2)}) collective-permute-start(bf16[264,128]{1,0:T(8,128)(2,1)S(1)} %get-tuple-element.171), channel_id=1, source_target_pairs={{0,8},{1,9},{2,10},{3,11},{4,12},{5,13},{6,14},{7,15},{8,0},{9,1},... | collective-permute-start | bytes 202760 | tf_op jit(solution)/shard_map/ppermute | solution.py:400
  135.4 8.5 %collective-permute-start.62 = (bf16[264,128]{1,0:T(8,128)(2,1)S(1)}, bf16[264,128]{1,0:T(8,128)(2,1)S(1)}, u32[]{:S(2)}, u32[]{:S(2)}) collective-permute-start(bf16[264,128]{1,0:T(8,128)(2,1)S(1)} %get-tuple-element.173), channel_id=1, source_target_pairs={{0,9},{1,8},{2,11},{3,10},{4,13},{5,12},{6,15},{7,14},{8,1},{9,0},... | collective-permute-start | bytes 202760 | tf_op jit(solution)/shard_map/ppermute | solution.py:400
  136.8 8.7 %collective-permute-start.63 = (bf16[264,128]{1,0:T(8,128)(2,1)S(1)}, bf16[264,128]{1,0:T(8,128)(2,1)S(1)}, u32[]{:S(2)}, u32[]{:S(2)}) collective-permute-start(bf16[264,128]{1,0:T(8,128)(2,1)S(1)} %get-tuple-element.174), channel_id=1, source_target_pairs={{0,2},{1,3},{2,0},{3,1},{4,6},{5,7},{6,4},{7,5},{8,10},{9,11},{10,... | collective-permute-start | bytes 202760 | tf_op jit(solution)/shard_map/ppermute | solution.py:400
  138.0 9.0 %collective-permute-start.64 = (bf16[264,128]{1,0:T(8,128)(2,1)S(1)}, bf16[264,128]{1,0:T(8,128)(2,1)S(1)}, u32[]{:S(2)}, u32[]{:S(2)}) collective-permute-start(bf16[264,128]{1,0:T(8,128)(2,1)S(1)} %get-tuple-element.175), channel_id=1, source_target_pairs={{0,10},{1,11},{2,8},{3,9},{4,14},{5,15},{6,12},{7,13},{8,2},{9,3},... | collective-permute-start | bytes 202760 | tf_op jit(solution)/shard_map/ppermute | solution.py:400
  141.5 7.9 %collective-permute-start.66 = (bf16[264,128]{1,0:T(8,128)(2,1)S(1)}, bf16[264,128]{1,0:T(8,128)(2,1)S(1)}, u32[]{:S(2)}, u32[]{:S(2)}) collective-permute-start(bf16[264,128]{1,0:T(8,128)(2,1)S(1)} %get-tuple-element.177), channel_id=1, source_target_pairs={{0,11},{1,10},{2,9},{3,8},{4,15},{5,14},{6,13},{7,12},{8,3},{9,2},... | collective-permute-start | bytes 202760 | tf_op jit(solution)/shard_map/ppermute | solution.py:400
  143.8 8.4 %collective-permute-start.67 = (bf16[264,128]{1,0:T(8,128)(2,1)S(1)}, bf16[264,128]{1,0:T(8,128)(2,1)S(1)}, u32[]{:S(2)}, u32[]{:S(2)}) collective-permute-start(bf16[264,128]{1,0:T(8,128)(2,1)S(1)} %get-tuple-element.178), channel_id=1, source_target_pairs={{0,4},{1,5},{2,6},{3,7},{4,0},{5,1},{6,2},{7,3},{8,12},{9,13},{10,... | collective-permute-start | bytes 202760 | tf_op jit(solution)/shard_map/ppermute | solution.py:400
  145.5 7.1 %collective-permute-start.68 = (bf16[264,128]{1,0:T(8,128)(2,1)S(1)}, bf16[264,128]{1,0:T(8,128)(2,1)S(1)}, u32[]{:S(2)}, u32[]{:S(2)}) collective-permute-start(bf16[264,128]{1,0:T(8,128)(2,1)S(1)} %get-tuple-element.179), channel_id=1, source_target_pairs={{0,12},{1,13},{2,14},{3,15},{4,8},{5,9},{6,10},{7,11},{8,4},{9,5},... | collective-permute-start | bytes 202760 | tf_op jit(solution)/shard_map/ppermute | solution.py:400
  147.1 7.3 %collective-permute-start.69 = (bf16[264,128]{1,0:T(8,128)(2,1)S(1)}, bf16[264,128]{1,0:T(8,128)(2,1)S(1)}, u32[]{:S(2)}, u32[]{:S(2)}) collective-permute-start(bf16[264,128]{1,0:T(8,128)(2,1)S(1)} %get-tuple-element.180), channel_id=1, source_target_pairs={{0,5},{1,4},{2,7},{3,6},{4,1},{5,0},{6,3},{7,2},{8,13},{9,12},{10,... | collective-permute-start | bytes 202760 | tf_op jit(solution)/shard_map/ppermute | solution.py:400
  147.1 8.8 %collective-permute-start.70 = (bf16[264,128]{1,0:T(8,128)(2,1)S(1)}, bf16[264,128]{1,0:T(8,128)(2,1)S(1)}, u32[]{:S(2)}, u32[]{:S(2)}) collective-permute-start(bf16[264,128]{1,0:T(8,128)(2,1)S(1)} %get-tuple-element.181), channel_id=1, source_target_pairs={{0,13},{1,12},{2,15},{3,14},{4,9},{5,8},{6,11},{7,10},{8,5},{9,4},... | collective-permute-start | bytes 202760 | tf_op jit(solution)/shard_map/ppermute | solution.py:400
  149.4 6.9 %collective-permute-start.71 = (bf16[264,128]{1,0:T(8,128)(2,1)S(1)}, bf16[264,128]{1,0:T(8,128)(2,1)S(1)}, u32[]{:S(2)}, u32[]{:S(2)}) collective-permute-start(bf16[264,128]{1,0:T(8,128)(2,1)S(1)} %get-tuple-element.182), channel_id=1, source_target_pairs={{0,6},{1,7},{2,4},{3,5},{4,2},{5,3},{6,0},{7,1},{8,14},{9,15},{10,... | collective-permute-start | bytes 202760 | tf_op jit(solution)/shard_map/ppermute | solution.py:400
  152.2 7.2 %collective-permute-start.72 = (bf16[264,128]{1,0:T(8,128)(2,1)S(1)}, bf16[264,128]{1,0:T(8,128)(2,1)S(1)}, u32[]{:S(2)}, u32[]{:S(2)}) collective-permute-start(bf16[264,128]{1,0:T(8,128)(2,1)S(1)} %get-tuple-element.183), channel_id=1, source_target_pairs={{0,14},{1,15},{2,12},{3,13},{4,10},{5,11},{6,8},{7,9},{8,6},{9,7},... | collective-permute-start | bytes 202760 | tf_op jit(solution)/shard_map/ppermute | solution.py:400
  152.6 6.8 %collective-permute-start.73 = (bf16[264,128]{1,0:T(8,128)(2,1)S(1)}, bf16[264,128]{1,0:T(8,128)(2,1)S(1)}, u32[]{:S(2)}, u32[]{:S(2)}) collective-permute-start(bf16[264,128]{1,0:T(8,128)(2,1)S(1)} %get-tuple-element.184), channel_id=1, source_target_pairs={{0,7},{1,6},{2,5},{3,4},{4,3},{5,2},{6,1},{7,0},{8,15},{9,14},{10,... | collective-permute-start | bytes 202760 | tf_op jit(solution)/shard_map/ppermute | solution.py:400
  154.3 7.3 %collective-permute-start.74 = (bf16[264,128]{1,0:T(8,128)(2,1)S(1)}, bf16[264,128]{1,0:T(8,128)(2,1)S(1)}, u32[]{:S(2)}, u32[]{:S(2)}) collective-permute-start(bf16[264,128]{1,0:T(8,128)(2,1)S(1)} %get-tuple-element.185), channel_id=1, source_target_pairs={{0,15},{1,14},{2,13},{3,12},{4,11},{5,10},{6,9},{7,8},{8,7},{9,6},... | collective-permute-start | bytes 202760 | tf_op jit(solution)/shard_map/ppermute | solution.py:400
  (14 other events, 69.0 us)

commit v12 on v10

--- a/solution.py
+++ b/solution.py
@@ -156,6 +156,19 @@
             asked = table_ref[peer * BCAP + rank].astype(F32)
             rows = jnp.where((place == 3) & (lane == rank), asked, rows)
         message_ref[BCAP * cols :, :] = rows.astype(BF16)
+
+
+def keep_kernel(target_hbm, own_hbm, rays_hbm, target_ref, own_ref, rays_ref, sems):
+    copies = [
+        pltpu.make_async_copy(source, dest, sems.at[index])
+        for index, (source, dest) in enumerate(
+            [(target_hbm, target_ref), (own_hbm, own_ref), (rays_hbm, rays_ref)]
+        )
+    ]
+    for copy in copies:
+        copy.start()
+    for copy in copies:
+        copy.wait()
 
 
 def pair_kernel(peers, target_ref, *refs):
@@ -264,24 +277,31 @@
 
 
 def last_cell_kernel(peers, asked_ref, *refs):
-    arrived_refs, refs = refs[:peers], refs[peers:]
+    arrived_refs = refs[:peers]
+    before_ref, alpha_ref, beta_before_ref, model_ref, beta_ref, out_ref = refs[peers:]
+    beta = norm_of_tails(arrived_refs, model_ref.shape[0])
+    beta_ref[...] = beta
+    start_from(before_ref, beta * beta / (alpha_ref[...] * beta_before_ref[...]), model_ref)
+    gathered(arrived_refs, asked_ref, model_ref)
+    squares = squares_of(model_ref) / (beta * beta)
+    total = jnp.sum(squares, axis=1, keepdims=True)
+    row = jnp.sum(jnp.where(diagonal(total.shape[0]), total, 0.0), axis=0, keepdims=True)
+    out_ref[...] = jnp.broadcast_to(row, out_ref.shape)
+
+
+def estimate_kernel(*refs):
     models = refs[:ITERS]
     alphas = [ref[...] for ref in refs[ITERS : 2 * ITERS]]
-    betas = [ref[...] for ref in refs[2 * ITERS : 3 * ITERS]]
-    model_ref, beta_ref, out_ref, estimate_hbm, estimate_ref, sems = refs[3 * ITERS :]
-    cols, cells = model_ref.shape
-    beta = norm_of_tails(arrived_refs, cols)
-    beta_ref[...] = beta
-    weights = estimate_weights(betas + [beta], alphas)
-    scale = beta * beta / (alphas[-1] * betas[-1])
+    betas = [ref[...] for ref in refs[2 * ITERS : 3 * ITERS + 1]]
+    estimate_hbm, estimate_ref, sems = refs[3 * ITERS + 1 :]
+    cells = estimate_ref.shape[1]
+    weights = estimate_weights(betas, alphas)
     blocks = cells // BS // CHUNKS
 
     def one_block(block, carry):
         where = lanes(block)
-        values = models[-1][:, where]
-        model_ref[:, where] = values * -scale
-        total = values * weights[-1]
-        for i in range(ITERS - 1):
+        total = weights[0] * models[0][:, where]
+        for i in range(1, ITERS):
             total += weights[i] * models[i][:, where]
         estimate_ref[:, where] = total
         return carry
@@ -296,10 +316,6 @@
             )
         )
         copies[-1].start()
-    gathered(arrived_refs, asked_ref, model_ref)
-    scale = 1.0 / beta
-    tail = squares_tail(squares_of(model_ref) * scale * scale)
-    out_ref[...] = jnp.broadcast_to(tail[None], out_ref.shape)
     for copy in copies:
         copy.wait()
 
@@ -327,11 +343,11 @@
     return weight
 
 
-def model_kernel(tails_ref, beta_ref, model_ref, out_hbm, out_ref, sems):
+def model_kernel(*refs):
+    *share_refs, beta_ref, model_ref, out_hbm, out_ref, sems = refs
     cols, cells = model_ref.shape
     blocks = cells // BS // CHUNKS
-    summed = jnp.sum(tails_ref[...], axis=0)
-    row = summed[0:1] + summed[1:2] + summed[2:3]
+    row = sum(ref[...] for ref in share_refs)[0:1]
     column = jnp.sum(jnp.where(diagonal(cols), row, 0.0), axis=1, keepdims=True)
     alpha = jnp.broadcast_to(jnp.sqrt(column + EPS), (cols, BS))
     scale = 1.0 / (alpha * beta_ref[...])
@@ -402,6 +418,11 @@
         flops, 6 << 20, 60 << 20,
     )(me, block_cells, block_counts, times, ray_blocks)
     arrived = exchange(outgoing)
+    target, arrived[0], ray_blocks = call(
+        keep_kernel, "keep", [HBM, HBM, HBM],
+        [((slots,), jnp.int32, SMEM), messages[0], (ray_blocks.shape, BF16, VMEM)],
+        [pltpu.SemaphoreType.DMA((3,))], 0, 8 << 20, 48 << 20,
+    )(target, arrived[0], ray_blocks)
     model, beta, *replies, asked = call(
         functools.partial(first_cell_kernel, peers), "cells_first", ins,
         [whole, tile] + messages + [((peers, BS), jnp.int32, SMEM)],
@@ -428,16 +449,29 @@
             )(asked, *arrived, models[-1], alphas[-1], betas[-1])
             models.append(model)
             betas.append(beta)
+    model, beta, share = call(
+        functools.partial(last_cell_kernel, peers), "cells_last", [SMEM] + ins + [VMEM] * 3,
+        [whole, tile, ((8, BS), F32, VMEM)], (), 0, 8 << 20,
+    )(asked, *arrived, models[-1], alphas[-1], betas[-1])
+    betas.append(beta)
+    reach, shares = peers, [share]
+    while reach > 1:
+        share = sum(shares[1:], shares[0])
+        low = max(reach // 4, 1)
+        shares = [share] + [
+            lax.ppermute(share, "pair", [(one, one ^ step) for one in range(peers)])
+            for step in range(low, reach, low)
+        ]
+        reach = low
     scratch = [VMEM(whole[0], F32), pltpu.SemaphoreType.DMA((CHUNKS,))]
-    model, beta, tails, estimate = call(
-        functools.partial(last_cell_kernel, peers), "cells_last",
-        [SMEM] + ins + [VMEM] * (3 * ITERS),
-        [whole, tile, ((peers, TAIL, BS), F32, VMEM), (whole[0], F32, HBM)], scratch, 0, 10 << 20,
-    )(asked, *arrived, *models, *alphas, *betas)
-    tails = lax.all_to_all(tails, "pair", split_axis=0, concat_axis=0, tiled=True)
+    (estimate,) = call(
+        estimate_kernel, "estimate", [VMEM] * (3 * ITERS + 1), [(whole[0], F32, HBM)], scratch,
+        0, 6 << 20,
+    )(*models, *alphas, *betas)
     (model_vec,) = call(
-        model_kernel, "model", [VMEM, VMEM, VMEM], [(whole[0], F32, HBM)], scratch, 0, 4 << 20
-    )(tails, beta, model)
+        model_kernel, "model", [VMEM] * (len(shares) + 2), [(whole[0], F32, HBM)], scratch,
+        0, 4 << 20,
+    )(*shares, beta, model)
     return (estimate.T, model_vec.T)
 
 

time: 179 us -> 174 us (0.972)
  blocking collectives: 10.6 us -> 0 us
  starting transfers between devices: 98.5 us -> 104 us
  Pallas kernels: 21.6 us -> 25.5 us
  local copies, waits for them, and re-layouts: 3.68 us -> 1.48 us
    all_to_all x1 -> x0, blocking collectives: 10.6 us -> none  [on_device(): lax.all_to_all(tails, 'pair', split_axis=0, concat_axis=0, tiled=True)]
    ppermute x0 -> x6, starting transfers between devices: none -> 6.37 us  [on_device(): lax.ppermute(share, 'pair', [(one, one ^ step) for one in range(peers)])]
    pallas_call x1 -> x3, Pallas kernels: 1.54 us -> 5.97 us  [the longest x1 2.9 us: on_device(): call(keep_kernel, 'keep', [HBM, HBM, HBM], [((slots,), jnp.int32, SMEM),...]
    ppermute x75, waiting for transfers between devices: 43.3 us -> 39.7 us  [exchange(): lax.ppermute(value, 'pair', [(one, one ^ step) for one in range(peers)])]
    unnamed x12 -> x6, local copies, waits for them, and re-layouts: 3.68 us -> 1.48 us
    ppermute x0 -> x6, waiting for transfers between devices: none -> 2.08 us  [on_device(): lax.ppermute(share, 'pair', [(one, one ^ step) for one in range(peers)])]
  transfers between devices with their start and end apart: 75 -> 81, of which waited for: 28 -> 32; matrix products, arithmetic and copies ran while one was open for 0% -> 0% of each run, Pallas kernels for 0% -> 3%
where the time goes in v12:
time: 174 us; the launch traced here: 173 us
  starting transfers between devices  104 us (60%)
  waiting for transfers between devices  41.8 us (24%)
  Pallas kernels  25.5 us (15%)
    ppermute x75, starting transfers between devices, exchange(): lax.ppermute(value, 'pair', [(one, one ^ step) for one in range(peers)])  97.3 us
    ppermute x75, waiting for transfers between devices, exchange(): lax.ppermute(value, 'pair', [(one, one ^ step) for one in range(peers)])  39.7 us
    pallas_call x2, Pallas kernels, on_device(): call(functools.partial(pair_kernel, peers), 'pairs_last' if last else 'pa...  6.9 us
    ppermute x6, starting transfers between devices, on_device(): lax.ppermute(share, 'pair', [(one, one ^ step) for one in range(peers)])  6.37 us
    pallas_call x1, Pallas kernels, on_device(): call(functools.partial(start_kernel, peers), 'start', [SMEM, HBM, HBM, HB...  5.73 us
  transfers between devices with their start and end apart: 81, of which 32 were waited for; matrix products, arithmetic and copies ran while one was open for 0% of the time, Pallas kernels for 3%

profile of v12, /device:TPU:0, one launch (start us, length us, event | category | flops | bytes accessed | tf_op | source)
XLA Modules:
  0.0 173.4 jit_solution(9374203651138937680)
XLA Ops:
  0.6 5.7 %start.1 = (bf16[264,128]{1,0:T(8,128)(2,1)}, bf16[264,128]{1,0:T(8,128)(2,1)}, bf16[264,128]{1,0:T(8,128)(2,1)}, bf16[264,128]{1,0:T(8,128)(2,1)}, bf16[264,128...) custom-call(s32[1]{0:T(128)} %bitcast.me_ref, ...), custom_call_target="tpu_custom_call" | custom-call | flops 268435456 | bytes 6291456 | tf_op jit(solution)/shard_map/start/pallas_call | solution.py:409
  6.4 4.1 %collective-permute-start = (bf16[264,128]{1,0:T(8,128)(2,1)}, bf16[264,128]{1,0:T(8,128)(2,1)S(1)}, u32[]{:S(2)}, u32[]{:S(2)}) collective-permute-start(bf16[264,128]{1,0:T(8,128)(2,1)} %get-tuple-element.100), channel_id=1, source_target_pairs={{0,8},{1,9},{2,10},{3,11},{4,12},{5,13},{6,14},{7,15},{8,0},{9,1},... | collective-permute-start | bytes 202760 | tf_op jit(solution)/shard_map/ppermute | solution.py:404
  10.7 1.6 collective-permute-start.3
  12.3 2.7 %collective-permute-start.4 = (bf16[264,128]{1,0:T(8,128)(2,1)}, bf16[264,128]{1,0:T(8,128)(2,1)S(1)}, u32[]{:S(2)}, u32[]{:S(2)}) collective-permute-start(bf16[264,128]{1,0:T(8,128)(2,1)} %get-tuple-element.104), channel_id=1, source_target_pairs={{0,10},{1,11},{2,8},{3,9},{4,14},{5,15},{6,12},{7,13},{8,2},{9,3},... | collective-permute-start | bytes 202760 | tf_op jit(solution)/shard_map/ppermute | solution.py:404
  15.5 2.1 %collective-permute-start.6 = (bf16[264,128]{1,0:T(8,128)(2,1)}, bf16[264,128]{1,0:T(8,128)(2,1)S(1)}, u32[]{:S(2)}, u32[]{:S(2)}) collective-permute-start(bf16[264,128]{1,0:T(8,128)(2,1)} %get-tuple-element.106), channel_id=1, source_target_pairs={{0,11},{1,10},{2,9},{3,8},{4,15},{5,14},{6,13},{7,12},{8,3},{9,2},... | collective-permute-start | bytes 202760 | tf_op jit(solution)/shard_map/ppermute | solution.py:404
  17.6 4.4 %collective-permute-start.7 = (bf16[264,128]{1,0:T(8,128)(2,1)}, bf16[264,128]{1,0:T(8,128)(2,1)S(1)}, u32[]{:S(2)}, u32[]{:S(2)}) collective-permute-start(bf16[264,128]{1,0:T(8,128)(2,1)} %get-tuple-element.107), channel_id=1, source_target_pairs={{0,4},{1,5},{2,6},{3,7},{4,0},{5,1},{6,2},{7,3},{8,12},{9,13},{10,... | collective-permute-start | bytes 202760 | tf_op jit(solution)/shard_map/ppermute | solution.py:404
  22.4 4.4 %collective-permute-start.10 = (bf16[264,128]{1,0:T(8,128)(2,1)}, bf16[264,128]{1,0:T(8,128)(2,1)S(1)}, u32[]{:S(2)}, u32[]{:S(2)}) collective-permute-start(bf16[264,128]{1,0:T(8,128)(2,1)} %get-tuple-element.110), channel_id=1, source_target_pairs={{0,13},{1,12},{2,15},{3,14},{4,9},{5,8},{6,11},{7,10},{8,5},{9,4},... | collective-permute-start | bytes 202760 | tf_op jit(solution)/shard_map/ppermute | solution.py:404
  27.6 1.9 %collective-permute-start.12 = (bf16[264,128]{1,0:T(8,128)(2,1)}, bf16[264,128]{1,0:T(8,128)(2,1)S(1)}, u32[]{:S(2)}, u32[]{:S(2)}) collective-permute-start(bf16[264,128]{1,0:T(8,128)(2,1)} %get-tuple-element.112), channel_id=1, source_target_pairs={{0,14},{1,15},{2,12},{3,13},{4,10},{5,11},{6,8},{7,9},{8,6},{9,7},... | collective-permute-start | bytes 202760 | tf_op jit(solution)/shard_map/ppermute | solution.py:404
  29.8 3.5 %collective-permute-start.14 = (bf16[264,128]{1,0:T(8,128)(2,1)}, bf16[264,128]{1,0:T(8,128)(2,1)S(1)}, u32[]{:S(2)}, u32[]{:S(2)}) collective-permute-start(bf16[264,128]{1,0:T(8,128)(2,1)} %get-tuple-element.114), channel_id=1, source_target_pairs={{0,15},{1,14},{2,13},{3,12},{4,11},{5,10},{6,9},{7,8},{8,7},{9,6},... | collective-permute-start | bytes 202760 | tf_op jit(solution)/shard_map/ppermute | solution.py:404
  34.7 2.9 %keep.1 = (s32[128]{0:T(128)S(1)}, bf16[264,128]{1,0:T(8,128)(2,1)S(1)}, bf16[8,16,128,128]{3,2,1,0:T(8,128)(2,1)S(1)}) custom-call(s32[128]{0:T(128)S(1)} %copy-done.2, bf16[264,128]{1,0:T(8,128)(2,1)S(1)} %copy-done.1, bf16[8,16,128,128]{3,2,1,0:T(8,128)(2,1)} %rays_hbm.3), custom_call_target="tpu_custom_call" | custom-call | bytes 8388608 | tf_op jit(solution)/shard_map/keep/pallas_call | solution.py:421
  37.7 2.5 %cells_first.1 = (f32[64,8192]{1,0:T(8,128)S(1)}, f32[64,128]{1,0:T(8,128)S(1)}, bf16[264,128]{1,0:T(8,128)(2,1)S(1)}, bf16[264,128]{1,0:T(8,128)(2,1)S(1)}, bf1...) custom-call(bf16[264,128]{1,0:T(8,128)(2,1)S(1)} %get-tuple-element., ...), custom_call_target="tpu_custom_call" | custom-call | bytes 6291456 | tf_op jit(solution)/shard_map/cells_first/pallas_call | solution.py:426
  41.4 2.0 %collective-permute-start.17 = (bf16[264,128]{1,0:T(8,128)(2,1)S(1)}, bf16[264,128]{1,0:T(8,128)(2,1)S(1)}, u32[]{:S(2)}, u32[]{:S(2)}) collective-permute-start(bf16[264,128]{1,0:T(8,128)(2,1)S(1)} %get-tuple-element.121), channel_id=1, source_target_pairs={{0,9},{1,8},{2,11},{3,10},{4,13},{5,12},{6,15},{7,14},{8,1},{9,0},... | collective-permute-start | bytes 202760 | tf_op jit(solution)/shard_map/ppermute | solution.py:404
  43.3 2.0 %collective-permute-start.19 = (bf16[264,128]{1,0:T(8,128)(2,1)S(1)}, bf16[264,128]{1,0:T(8,128)(2,1)S(1)}, u32[]{:S(2)}, u32[]{:S(2)}) collective-permute-start(bf16[264,128]{1,0:T(8,128)(2,1)S(1)} %get-tuple-element.123), channel_id=1, source_target_pairs={{0,10},{1,11},{2,8},{3,9},{4,14},{5,15},{6,12},{7,13},{8,2},{9,3},... | collective-permute-start | bytes 202760 | tf_op jit(solution)/shard_map/ppermute | solution.py:404
  45.3 3.7 %collective-permute-done.15.refs_1_ = bf16[264,128]{1,0:T(8,128)(2,1)S(1)} collective-permute-done((bf16[264,128]{1,0:T(8,128)(2,1)S(1)}, bf16[264,128]{1,0:T(8,128)(2,1)S(1)}, u32[]{:S(2)}, u32[]{:S(2)}) %collective-permute-start.15) | collective-permute-done | bytes 67616 | tf_op jit(solution)/shard_map/ppermute | solution.py:404
  49.8 1.4 collective-permute-done.17.refs_3_
  51.1 2.6 %collective-permute-start.22 = (bf16[264,128]{1,0:T(8,128)(2,1)S(1)}, bf16[264,128]{1,0:T(8,128)(2,1)S(1)}, u32[]{:S(2)}, u32[]{:S(2)}) collective-permute-start(bf16[264,128]{1,0:T(8,128)(2,1)S(1)} %get-tuple-element.126), channel_id=1, source_target_pairs={{0,4},{1,5},{2,6},{3,7},{4,0},{5,1},{6,2},{7,3},{8,12},{9,13},{10,... | collective-permute-start | bytes 202760 | tf_op jit(solution)/shard_map/ppermute | solution.py:404
  54.6 1.8 %collective-permute-start.25 = (bf16[264,128]{1,0:T(8,128)(2,1)S(1)}, bf16[264,128]{1,0:T(8,128)(2,1)S(1)}, u32[]{:S(2)}, u32[]{:S(2)}) collective-permute-start(bf16[264,128]{1,0:T(8,128)(2,1)S(1)} %get-tuple-element.129), channel_id=1, source_target_pairs={{0,13},{1,12},{2,15},{3,14},{4,9},{5,8},{6,11},{7,10},{8,5},{9,4},... | collective-permute-start | bytes 202760 | tf_op jit(solution)/shard_map/ppermute | solution.py:404
  56.6 1.7 collective-permute-start.26
  58.3 1.9 %collective-permute-start.27 = (bf16[264,128]{1,0:T(8,128)(2,1)S(1)}, bf16[264,128]{1,0:T(8,128)(2,1)S(1)}, u32[]{:S(2)}, u32[]{:S(2)}) collective-permute-start(bf16[264,128]{1,0:T(8,128)(2,1)S(1)} %get-tuple-element.131), channel_id=1, source_target_pairs={{0,14},{1,15},{2,12},{3,13},{4,10},{5,11},{6,8},{7,9},{8,6},{9,7},... | collective-permute-start | bytes 202760 | tf_op jit(solution)/shard_map/ppermute | solution.py:404
  60.5 2.6 %collective-permute-start.29 = (bf16[264,128]{1,0:T(8,128)(2,1)S(1)}, bf16[264,128]{1,0:T(8,128)(2,1)S(1)}, u32[]{:S(2)}, u32[]{:S(2)}) collective-permute-start(bf16[264,128]{1,0:T(8,128)(2,1)S(1)} %get-tuple-element.133), channel_id=1, source_target_pairs={{0,15},{1,14},{2,13},{3,12},{4,11},{5,10},{6,9},{7,8},{8,7},{9,6},... | collective-permute-start | bytes 202760 | tf_op jit(solution)/shard_map/ppermute | solution.py:404
  63.1 2.7 %collective-permute-done.27.refs_13_ = bf16[264,128]{1,0:T(8,128)(2,1)S(1)} collective-permute-done((bf16[264,128]{1,0:T(8,128)(2,1)S(1)}, bf16[264,128]{1,0:T(8,128)(2,1)S(1)}, u32[]{:S(2)}, u32[]{:S(2)}) %collective-permute-start.27) | collective-permute-done | bytes 67616 | tf_op jit(solution)/shard_map/ppermute | solution.py:404
  66.4 1.4 collective-permute-done.29.refs_15_
  67.8 3.5 %pairs.1 = (bf16[264,128]{1,0:T(8,128)(2,1)S(1)}, bf16[264,128]{1,0:T(8,128)(2,1)S(1)}, bf16[264,128]{1,0:T(8,128)(2,1)S(1)}, bf16[264,128]{1,0:T(8,128)(2,1)S(1...) custom-call(s32[128]{0:T(128)S(1)} %get-tuple-element.117.target_ref, ...), custom_call_target="tpu_custom_call" | custom-call | flops 536870912 | bytes 8388608 | tf_op jit(solution)/shard_map/pairs/pallas_call | solution.py:437
  71.6 1.5 collective-permute-start.31
  73.1 1.3 collective-permute-start.32
  74.4 1.5 collective-permute-start.33
  77.1 3.6 %collective-permute-done.30.refs_1_ = bf16[264,128]{1,0:T(8,128)(2,1)S(1)} collective-permute-done((bf16[264,128]{1,0:T(8,128)(2,1)S(1)}, bf16[264,128]{1,0:T(8,128)(2,1)S(1)}, u32[]{:S(2)}, u32[]{:S(2)}) %collective-permute-start.30) | collective-permute-done | bytes 67616 | tf_op jit(solution)/shard_map/ppermute | solution.py:404
  81.3 1.9 %collective-permute-start.37 = (bf16[264,128]{1,0:T(8,128)(2,1)S(1)}, bf16[264,128]{1,0:T(8,128)(2,1)S(1)}, u32[]{:S(2)}, u32[]{:S(2)}) collective-permute-start(bf16[264,128]{1,0:T(8,128)(2,1)S(1)} %get-tuple-element.144), channel_id=1, source_target_pairs={{0,4},{1,5},{2,6},{3,7},{4,0},{5,1},{6,2},{7,3},{8,12},{9,13},{10,... | collective-permute-start | bytes 202760 | tf_op jit(solution)/shard_map/ppermute | solution.py:404
  83.1 3.1 %collective-permute-start.38 = (bf16[264,128]{1,0:T(8,128)(2,1)S(1)}, bf16[264,128]{1,0:T(8,128)(2,1)S(1)}, u32[]{:S(2)}, u32[]{:S(2)}) collective-permute-start(bf16[264,128]{1,0:T(8,128)(2,1)S(1)} %get-tuple-element.145), channel_id=1, source_target_pairs={{0,12},{1,13},{2,14},{3,15},{4,8},{5,9},{6,10},{7,11},{8,4},{9,5},... | collective-permute-start | bytes 202760 | tf_op jit(solution)/shard_map/ppermute | solution.py:404
  87.0 1.5 collective-permute-start.41
  88.5 3.5 %collective-permute-start.42 = (bf16[264,128]{1,0:T(8,128)(2,1)S(1)}, bf16[264,128]{1,0:T(8,128)(2,1)S(1)}, u32[]{:S(2)}, u32[]{:S(2)}) collective-permute-start(bf16[264,128]{1,0:T(8,128)(2,1)S(1)} %get-tuple-element.149), channel_id=1, source_target_pairs={{0,14},{1,15},{2,12},{3,13},{4,10},{5,11},{6,8},{7,9},{8,6},{9,7},... | collective-permute-start | bytes 202760 | tf_op jit(solution)/shard_map/ppermute | solution.py:404
  93.5 2.1 %collective-permute-done.41.refs_12_ = bf16[264,128]{1,0:T(8,128)(2,1)S(1)} collective-permute-done((bf16[264,128]{1,0:T(8,128)(2,1)S(1)}, bf16[264,128]{1,0:T(8,128)(2,1)S(1)}, u32[]{:S(2)}, u32[]{:S(2)}) %collective-permute-start.41) | collective-permute-done | bytes 67616 | tf_op jit(solution)/shard_map/ppermute | solution.py:404
  96.2 1.3 collective-permute-done.43.refs_14_
  97.5 1.7 collective-permute-done.44.refs_15_
  99.3 2.4 %cells.1 = (f32[64,8192]{1,0:T(8,128)S(1)}, f32[64,128]{1,0:T(8,128)S(1)}, bf16[264,128]{1,0:T(8,128)(2,1)S(1)}, bf16[264,128]{1,0:T(8,128)(2,1)S(1)}, bf16[264,...) custom-call(s32[16,128]{1,0:T(8,128)S(1)} %get-tuple-element.116.ask, ...), custom_call_target="tpu_custom_call" | custom-call | bytes 8388608 | tf_op jit(solution)/shard_map/cells/pallas_call | solution.py:446
  101.7 1.3 collective-permute-start.45
  103.0 1.8 %collective-permute-start.47 = (bf16[264,128]{1,0:T(8,128)(2,1)S(1)}, bf16[264,128]{1,0:T(8,128)(2,1)S(1)}, u32[]{:S(2)}, u32[]{:S(2)}) collective-permute-start(bf16[264,128]{1,0:T(8,128)(2,1)S(1)} %get-tuple-element.157), channel_id=1, source_target_pairs={{0,9},{1,8},{2,11},{3,10},{4,13},{5,12},{6,15},{7,14},{8,1},{9,0},... | collective-permute-start | bytes 202760 | tf_op jit(solution)/shard_map/ppermute | solution.py:404
  104.8 1.6 collective-permute-start.48
  107.5 2.1 %collective-permute-done.45.refs_1_ = bf16[264,128]{1,0:T(8,128)(2,1)S(1)} collective-permute-done((bf16[264,128]{1,0:T(8,128)(2,1)S(1)}, bf16[264,128]{1,0:T(8,128)(2,1)S(1)}, u32[]{:S(2)}, u32[]{:S(2)}) %collective-permute-start.45) | collective-permute-done | bytes 67616 | tf_op jit(solution)/shard_map/ppermute | solution.py:404
  110.4 1.6 collective-permute-done.47.refs_3_
  112.0 2.4 %collective-permute-start.52 = (bf16[264,128]{1,0:T(8,128)(2,1)S(1)}, bf16[264,128]{1,0:T(8,128)(2,1)S(1)}, u32[]{:S(2)}, u32[]{:S(2)}) collective-permute-start(bf16[264,128]{1,0:T(8,128)(2,1)S(1)} %get-tuple-element.162), channel_id=1, source_target_pairs={{0,4},{1,5},{2,6},{3,7},{4,0},{5,1},{6,2},{7,3},{8,12},{9,13},{10,... | collective-permute-start | bytes 202760 | tf_op jit(solution)/shard_map/ppermute | solution.py:404
  115.5 1.7 collective-permute-start.55
  117.1 1.9 %collective-permute-start.56 = (bf16[264,128]{1,0:T(8,128)(2,1)S(1)}, bf16[264,128]{1,0:T(8,128)(2,1)S(1)}, u32[]{:S(2)}, u32[]{:S(2)}) collective-permute-start(bf16[264,128]{1,0:T(8,128)(2,1)S(1)} %get-tuple-element.166), channel_id=1, source_target_pairs={{0,6},{1,7},{2,4},{3,5},{4,2},{5,3},{6,0},{7,1},{8,14},{9,15},{10,... | collective-permute-start | bytes 202760 | tf_op jit(solution)/shard_map/ppermute | solution.py:404
  119.0 1.7 %collective-permute-start.57 = (bf16[264,128]{1,0:T(8,128)(2,1)S(1)}, bf16[264,128]{1,0:T(8,128)(2,1)S(1)}, u32[]{:S(2)}, u32[]{:S(2)}) collective-permute-start(bf16[264,128]{1,0:T(8,128)(2,1)S(1)} %get-tuple-element.167), channel_id=1, source_target_pairs={{0,14},{1,15},{2,12},{3,13},{4,10},{5,11},{6,8},{7,9},{8,6},{9,7},... | collective-permute-start | bytes 202760 | tf_op jit(solution)/shard_map/ppermute | solution.py:404
  121.3 2.3 %collective-permute-start.59 = (bf16[264,128]{1,0:T(8,128)(2,1)S(1)}, bf16[264,128]{1,0:T(8,128)(2,1)S(1)}, u32[]{:S(2)}, u32[]{:S(2)}) collective-permute-start(bf16[264,128]{1,0:T(8,128)(2,1)S(1)} %get-tuple-element.169), channel_id=1, source_target_pairs={{0,15},{1,14},{2,13},{3,12},{4,11},{5,10},{6,9},{7,8},{8,7},{9,6},... | collective-permute-start | bytes 202760 | tf_op jit(solution)/shard_map/ppermute | solution.py:404
  124.1 2.2 %collective-permute-done.57.refs_13_ = bf16[264,128]{1,0:T(8,128)(2,1)S(1)} collective-permute-done((bf16[264,128]{1,0:T(8,128)(2,1)S(1)}, bf16[264,128]{1,0:T(8,128)(2,1)S(1)}, u32[]{:S(2)}, u32[]{:S(2)}) %collective-permute-start.57) | collective-permute-done | bytes 67616 | tf_op jit(solution)/shard_map/ppermute | solution.py:404
  128.1 3.5 %pairs_last.1 = (bf16[264,128]{1,0:T(8,128)(2,1)S(1)}, bf16[264,128]{1,0:T(8,128)(2,1)S(1)}, bf16[264,128]{1,0:T(8,128)(2,1)S(1)}, bf16[264,128]{1,0:T(8,128)(2,...) custom-call(s32[128]{0:T(128)S(1)} %get-tuple-element.117.target_ref, ...), custom_call_target="tpu_custom_call" | custom-call | flops 536870912 | bytes 8388608 | tf_op jit(solution)/shard_map/pairs_last/pallas_call | solution.py:437
  132.3 1.4 collective-permute-start.61
  134.7 1.5 collective-permute-start.63
  136.2 1.4 collective-permute-start.64
  138.8 1.5 collective-permute-start.66
  140.3 1.9 %collective-permute-done.62.refs_3_ = bf16[264,128]{1,0:T(8,128)(2,1)S(1)} collective-permute-done((bf16[264,128]{1,0:T(8,128)(2,1)S(1)}, bf16[264,128]{1,0:T(8,128)(2,1)S(1)}, u32[]{:S(2)}, u32[]{:S(2)}) %collective-permute-start.62) | collective-permute-done | bytes 67616 | tf_op jit(solution)/shard_map/ppermute | solution.py:404
  142.2 1.8 %collective-permute-start.67 = (bf16[264,128]{1,0:T(8,128)(2,1)S(1)}, bf16[264,128]{1,0:T(8,128)(2,1)S(1)}, u32[]{:S(2)}, u32[]{:S(2)}) collective-permute-start(bf16[264,128]{1,0:T(8,128)(2,1)S(1)} %get-tuple-element.181), channel_id=1, source_target_pairs={{0,4},{1,5},{2,6},{3,7},{4,0},{5,1},{6,2},{7,3},{8,12},{9,13},{10,... | collective-permute-start | bytes 202760 | tf_op jit(solution)/shard_map/ppermute | solution.py:404
  144.4 2.7 %collective-permute-done.64.refs_5_ = bf16[264,128]{1,0:T(8,128)(2,1)S(1)} collective-permute-done((bf16[264,128]{1,0:T(8,128)(2,1)S(1)}, bf16[264,128]{1,0:T(8,128)(2,1)S(1)}, u32[]{:S(2)}, u32[]{:S(2)}) %collective-permute-start.64) | collective-permute-done | bytes 67616 | tf_op jit(solution)/shard_map/ppermute | solution.py:404
  149.2 3.4 %collective-permute-start.72 = (bf16[264,128]{1,0:T(8,128)(2,1)S(1)}, bf16[264,128]{1,0:T(8,128)(2,1)S(1)}, u32[]{:S(2)}, u32[]{:S(2)}) collective-permute-start(bf16[264,128]{1,0:T(8,128)(2,1)S(1)} %get-tuple-element.186), channel_id=1, source_target_pairs={{0,14},{1,15},{2,12},{3,13},{4,10},{5,11},{6,8},{7,9},{8,6},{9,7},... | collective-permute-start | bytes 202760 | tf_op jit(solution)/shard_map/ppermute | solution.py:404
  152.7 2.0 %collective-permute-start.74 = (bf16[264,128]{1,0:T(8,128)(2,1)S(1)}, bf16[264,128]{1,0:T(8,128)(2,1)S(1)}, u32[]{:S(2)}, u32[]{:S(2)}) collective-permute-start(bf16[264,128]{1,0:T(8,128)(2,1)S(1)} %get-tuple-element.188), channel_id=1, source_target_pairs={{0,15},{1,14},{2,13},{3,12},{4,11},{5,10},{6,9},{7,8},{8,7},{9,6},... | collective-permute-start | bytes 202760 | tf_op jit(solution)/shard_map/ppermute | solution.py:404
  155.3 1.9 %collective-permute-done.72.refs_13_ = bf16[264,128]{1,0:T(8,128)(2,1)S(1)} collective-permute-done((bf16[264,128]{1,0:T(8,128)(2,1)S(1)}, bf16[264,128]{1,0:T(8,128)(2,1)S(1)}, u32[]{:S(2)}, u32[]{:S(2)}) %collective-permute-start.72) | collective-permute-done | bytes 67616 | tf_op jit(solution)/shard_map/ppermute | solution.py:404
  158.3 1.4 collective-permute-done.74.refs_15_
  159.7 2.0 %cells_last.1 = (f32[64,8192]{1,0:T(8,128)S(1)}, f32[64,128]{1,0:T(8,128)S(1)}, f32[8,128]{1,0:T(8,128)S(1)}) custom-call(s32[16,128]{1,0:T(8,128)S(1)} %get-tuple-element.116.asked_ref, bf16[264,128]{1,0:T(8,128)(2,1)S(1)} %get-tuple-element.173.refs_0_, bf16[264,128]{1,0:T(8,128)(2,1)S(1)} %collective-permute-done.60.refs_1_, ...), custom_call_target="tpu_custom_call" | custom-call | bytes 8388608 | tf_op jit(solution)/shard_map/cells_last/pallas_call | solution.py:452
  161.7 1.8 %collective-permute-start.77 = (f32[8,128]{1,0:T(8,128)S(1)}, f32[8,128]{1,0:T(8,128)S(1)}, u32[]{:S(2)}, u32[]{:S(2)}) collective-permute-start(f32[8,128]{1,0:T(8,128)S(1)} %get-tuple-element.190), channel_id=1, source_target_pairs={{0,12},{1,13},{2,14},{3,15},{4,8},{5,9},{6,10},{7,11},{8,4},{9,5},... | collective-permute-start | bytes 12296 | tf_op jit(solution)/shard_map/ppermute | solution.py:462
  163.5 2.7 %collective-permute-start.75 = (f32[8,128]{1,0:T(8,128)S(1)}, f32[8,128]{1,0:T(8,128)S(1)}, u32[]{:S(2)}, u32[]{:S(2)}) collective-permute-start(f32[8,128]{1,0:T(8,128)S(1)} %get-tuple-element.190), channel_id=1, source_target_pairs={{0,4},{1,5},{2,6},{3,7},{4,0},{5,1},{6,2},{7,3},{8,12},{9,13},{10,... | collective-permute-start | bytes 12296 | tf_op jit(solution)/shard_map/ppermute | solution.py:462
  168.1 1.5 collective-permute-start.79
  169.9 1.5 estimate.1
  171.8 1.5 model.1
  (114 shorter events, 28.2 us)
Async XLA Ops:
  6.4 8.6 %collective-permute-start = (bf16[264,128]{1,0:T(8,128)(2,1)}, bf16[264,128]{1,0:T(8,128)(2,1)S(1)}, u32[]{:S(2)}, u32[]{:S(2)}) collective-permute-start(bf16[264,128]{1,0:T(8,128)(2,1)} %get-tuple-element.100), channel_id=1, source_target_pairs={{0,8},{1,9},{2,10},{3,11},{4,12},{5,13},{6,14},{7,15},{8,0},{9,1},... | collective-permute-start | bytes 202760 | tf_op jit(solution)/shard_map/ppermute | solution.py:404
  10.5 7.1 %collective-permute-start.2 = (bf16[264,128]{1,0:T(8,128)(2,1)}, bf16[264,128]{1,0:T(8,128)(2,1)S(1)}, u32[]{:S(2)}, u32[]{:S(2)}) collective-permute-start(bf16[264,128]{1,0:T(8,128)(2,1)} %get-tuple-element.102), channel_id=1, source_target_pairs={{0,9},{1,8},{2,11},{3,10},{4,13},{5,12},{6,15},{7,14},{8,1},{9,0},... | collective-permute-start | bytes 202760 | tf_op jit(solution)/shard_map/ppermute | solution.py:404
  10.7 11.3 %collective-permute-start.3 = (bf16[264,128]{1,0:T(8,128)(2,1)}, bf16[264,128]{1,0:T(8,128)(2,1)S(1)}, u32[]{:S(2)}, u32[]{:S(2)}) collective-permute-start(bf16[264,128]{1,0:T(8,128)(2,1)} %get-tuple-element.103), channel_id=1, source_target_pairs={{0,2},{1,3},{2,0},{3,1},{4,6},{5,7},{6,4},{7,5},{8,10},{9,11},{10,... | collective-permute-start | bytes 202760 | tf_op jit(solution)/shard_map/ppermute | solution.py:404
  12.3 9.6 %collective-permute-start.4 = (bf16[264,128]{1,0:T(8,128)(2,1)}, bf16[264,128]{1,0:T(8,128)(2,1)S(1)}, u32[]{:S(2)}, u32[]{:S(2)}) collective-permute-start(bf16[264,128]{1,0:T(8,128)(2,1)} %get-tuple-element.104), channel_id=1, source_target_pairs={{0,10},{1,11},{2,8},{3,9},{4,14},{5,15},{6,12},{7,13},{8,2},{9,3},... | collective-permute-start | bytes 202760 | tf_op jit(solution)/shard_map/ppermute | solution.py:404
  15.0 7.4 %collective-permute-start.5 = (bf16[264,128]{1,0:T(8,128)(2,1)}, bf16[264,128]{1,0:T(8,128)(2,1)S(1)}, u32[]{:S(2)}, u32[]{:S(2)}) collective-permute-start(bf16[264,128]{1,0:T(8,128)(2,1)} %get-tuple-element.105), channel_id=1, source_target_pairs={{0,3},{1,2},{2,1},{3,0},{4,7},{5,6},{6,5},{7,4},{8,11},{9,10},{10,... | collective-permute-start | bytes 202760 | tf_op jit(solution)/shard_map/ppermute | solution.py:404
  15.5 11.2 %collective-permute-start.6 = (bf16[264,128]{1,0:T(8,128)(2,1)}, bf16[264,128]{1,0:T(8,128)(2,1)S(1)}, u32[]{:S(2)}, u32[]{:S(2)}) collective-permute-start(bf16[264,128]{1,0:T(8,128)(2,1)} %get-tuple-element.106), channel_id=1, source_target_pairs={{0,11},{1,10},{2,9},{3,8},{4,15},{5,14},{6,13},{7,12},{8,3},{9,2},... | collective-permute-start | bytes 202760 | tf_op jit(solution)/shard_map/ppermute | solution.py:404
  17.6 10.0 %collective-permute-start.7 = (bf16[264,128]{1,0:T(8,128)(2,1)}, bf16[264,128]{1,0:T(8,128)(2,1)S(1)}, u32[]{:S(2)}, u32[]{:S(2)}) collective-permute-start(bf16[264,128]{1,0:T(8,128)(2,1)} %get-tuple-element.107), channel_id=1, source_target_pairs={{0,4},{1,5},{2,6},{3,7},{4,0},{5,1},{6,2},{7,3},{8,12},{9,13},{10,... | collective-permute-start | bytes 202760 | tf_op jit(solution)/shard_map/ppermute | solution.py:404
  22.0 7.5 %collective-permute-start.8 = (bf16[264,128]{1,0:T(8,128)(2,1)}, bf16[264,128]{1,0:T(8,128)(2,1)S(1)}, u32[]{:S(2)}, u32[]{:S(2)}) collective-permute-start(bf16[264,128]{1,0:T(8,128)(2,1)} %get-tuple-element.108), channel_id=1, source_target_pairs={{0,12},{1,13},{2,14},{3,15},{4,8},{5,9},{6,10},{7,11},{8,4},{9,5},... | collective-permute-start | bytes 202760 | tf_op jit(solution)/shard_map/ppermute | solution.py:404
  22.0 7.8 %collective-permute-start.9 = (bf16[264,128]{1,0:T(8,128)(2,1)}, bf16[264,128]{1,0:T(8,128)(2,1)S(1)}, u32[]{:S(2)}, u32[]{:S(2)}) collective-permute-start(bf16[264,128]{1,0:T(8,128)(2,1)} %get-tuple-element.109), channel_id=1, source_target_pairs={{0,5},{1,4},{2,7},{3,6},{4,1},{5,0},{6,3},{7,2},{8,13},{9,12},{10,... | collective-permute-start | bytes 202760 | tf_op jit(solution)/shard_map/ppermute | solution.py:404
  22.4 15.2 %collective-permute-start.10 = (bf16[264,128]{1,0:T(8,128)(2,1)}, bf16[264,128]{1,0:T(8,128)(2,1)S(1)}, u32[]{:S(2)}, u32[]{:S(2)}) collective-permute-start(bf16[264,128]{1,0:T(8,128)(2,1)} %get-tuple-element.110), channel_id=1, source_target_pairs={{0,13},{1,12},{2,15},{3,14},{4,9},{5,8},{6,11},{7,10},{8,5},{9,4},... | collective-permute-start | bytes 202760 | tf_op jit(solution)/shard_map/ppermute | solution.py:404
  26.8 10.9 %collective-permute-start.11 = (bf16[264,128]{1,0:T(8,128)(2,1)}, bf16[264,128]{1,0:T(8,128)(2,1)S(1)}, u32[]{:S(2)}, u32[]{:S(2)}) collective-permute-start(bf16[264,128]{1,0:T(8,128)(2,1)} %get-tuple-element.111), channel_id=1, source_target_pairs={{0,6},{1,7},{2,4},{3,5},{4,2},{5,3},{6,0},{7,1},{8,14},{9,15},{10,... | collective-permute-start | bytes 202760 | tf_op jit(solution)/shard_map/ppermute | solution.py:404
  27.6 10.1 %collective-permute-start.12 = (bf16[264,128]{1,0:T(8,128)(2,1)}, bf16[264,128]{1,0:T(8,128)(2,1)S(1)}, u32[]{:S(2)}, u32[]{:S(2)}) collective-permute-start(bf16[264,128]{1,0:T(8,128)(2,1)} %get-tuple-element.112), channel_id=1, source_target_pairs={{0,14},{1,15},{2,12},{3,13},{4,10},{5,11},{6,8},{7,9},{8,6},{9,7},... | collective-permute-start | bytes 202760 | tf_op jit(solution)/shard_map/ppermute | solution.py:404
  29.5 8.2 %collective-permute-start.13 = (bf16[264,128]{1,0:T(8,128)(2,1)}, bf16[264,128]{1,0:T(8,128)(2,1)S(1)}, u32[]{:S(2)}, u32[]{:S(2)}) collective-permute-start(bf16[264,128]{1,0:T(8,128)(2,1)} %get-tuple-element.113), channel_id=1, source_target_pairs={{0,7},{1,6},{2,5},{3,4},{4,3},{5,2},{6,1},{7,0},{8,15},{9,14},{10,... | collective-permute-start | bytes 202760 | tf_op jit(solution)/shard_map/ppermute | solution.py:404
  29.8 7.9 %collective-permute-start.14 = (bf16[264,128]{1,0:T(8,128)(2,1)}, bf16[264,128]{1,0:T(8,128)(2,1)S(1)}, u32[]{:S(2)}, u32[]{:S(2)}) collective-permute-start(bf16[264,128]{1,0:T(8,128)(2,1)} %get-tuple-element.114), channel_id=1, source_target_pairs={{0,15},{1,14},{2,13},{3,12},{4,11},{5,10},{6,9},{7,8},{8,7},{9,6},... | collective-permute-start | bytes 202760 | tf_op jit(solution)/shard_map/ppermute | solution.py:404
  40.2 8.8 %collective-permute-start.15 = (bf16[264,128]{1,0:T(8,128)(2,1)S(1)}, bf16[264,128]{1,0:T(8,128)(2,1)S(1)}, u32[]{:S(2)}, u32[]{:S(2)}) collective-permute-start(bf16[264,128]{1,0:T(8,128)(2,1)S(1)} %get-tuple-element.119), channel_id=1, source_target_pairs={{0,8},{1,9},{2,10},{3,11},{4,12},{5,13},{6,14},{7,15},{8,0},{9,1},... | collective-permute-start | bytes 202760 | tf_op jit(solution)/shard_map/ppermute | solution.py:404
  40.7 8.4 %collective-permute-start.16 = (bf16[264,128]{1,0:T(8,128)(2,1)S(1)}, bf16[264,128]{1,0:T(8,128)(2,1)S(1)}, u32[]{:S(2)}, u32[]{:S(2)}) collective-permute-start(bf16[264,128]{1,0:T(8,128)(2,1)S(1)} %get-tuple-element.120), channel_id=1, source_target_pairs={{0,1},{1,0},{2,3},{3,2},{4,5},{5,4},{6,7},{7,6},{8,9},{9,8},{10,11... | collective-permute-start | bytes 202760 | tf_op jit(solution)/shard_map/ppermute | solution.py:404
  41.4 9.8 %collective-permute-start.17 = (bf16[264,128]{1,0:T(8,128)(2,1)S(1)}, bf16[264,128]{1,0:T(8,128)(2,1)S(1)}, u32[]{:S(2)}, u32[]{:S(2)}) collective-permute-start(bf16[264,128]{1,0:T(8,128)(2,1)S(1)} %get-tuple-element.121), channel_id=1, source_target_pairs={{0,9},{1,8},{2,11},{3,10},{4,13},{5,12},{6,15},{7,14},{8,1},{9,0},... | collective-permute-start | bytes 202760 | tf_op jit(solution)/shard_map/ppermute | solution.py:404
  43.3 10.4 %collective-permute-start.18 = (bf16[264,128]{1,0:T(8,128)(2,1)S(1)}, bf16[264,128]{1,0:T(8,128)(2,1)S(1)}, u32[]{:S(2)}, u32[]{:S(2)}) collective-permute-start(bf16[264,128]{1,0:T(8,128)(2,1)S(1)} %get-tuple-element.122), channel_id=1, source_target_pairs={{0,2},{1,3},{2,0},{3,1},{4,6},{5,7},{6,4},{7,5},{8,10},{9,11},{10,... | collective-permute-start | bytes 202760 | tf_op jit(solution)/shard_map/ppermute | solution.py:404
  43.3 11.3 %collective-permute-start.19 = (bf16[264,128]{1,0:T(8,128)(2,1)S(1)}, bf16[264,128]{1,0:T(8,128)(2,1)S(1)}, u32[]{:S(2)}, u32[]{:S(2)}) collective-permute-start(bf16[264,128]{1,0:T(8,128)(2,1)S(1)} %get-tuple-element.123), channel_id=1, source_target_pairs={{0,10},{1,11},{2,8},{3,9},{4,14},{5,15},{6,12},{7,13},{8,2},{9,3},... | collective-permute-start | bytes 202760 | tf_op jit(solution)/shard_map/ppermute | solution.py:404
  49.0 7.6 %collective-permute-start.21 = (bf16[264,128]{1,0:T(8,128)(2,1)S(1)}, bf16[264,128]{1,0:T(8,128)(2,1)S(1)}, u32[]{:S(2)}, u32[]{:S(2)}) collective-permute-start(bf16[264,128]{1,0:T(8,128)(2,1)S(1)} %get-tuple-element.125), channel_id=1, source_target_pairs={{0,11},{1,10},{2,9},{3,8},{4,15},{5,14},{6,13},{7,12},{8,3},{9,2},... | collective-permute-start | bytes 202760 | tf_op jit(solution)/shard_map/ppermute | solution.py:404
  51.1 7.2 %collective-permute-start.22 = (bf16[264,128]{1,0:T(8,128)(2,1)S(1)}, bf16[264,128]{1,0:T(8,128)(2,1)S(1)}, u32[]{:S(2)}, u32[]{:S(2)}) collective-permute-start(bf16[264,128]{1,0:T(8,128)(2,1)S(1)} %get-tuple-element.126), channel_id=1, source_target_pairs={{0,4},{1,5},{2,6},{3,7},{4,0},{5,1},{6,2},{7,3},{8,12},{9,13},{10,... | collective-permute-start | bytes 202760 | tf_op jit(solution)/shard_map/ppermute | solution.py:404
  53.7 6.6 %collective-permute-start.23 = (bf16[264,128]{1,0:T(8,128)(2,1)S(1)}, bf16[264,128]{1,0:T(8,128)(2,1)S(1)}, u32[]{:S(2)}, u32[]{:S(2)}) collective-permute-start(bf16[264,128]{1,0:T(8,128)(2,1)S(1)} %get-tuple-element.127), channel_id=1, source_target_pairs={{0,12},{1,13},{2,14},{3,15},{4,8},{5,9},{6,10},{7,11},{8,4},{9,5},... | collective-permute-start | bytes 202760 | tf_op jit(solution)/shard_map/ppermute | solution.py:404
  54.6 8.5 %collective-permute-start.25 = (bf16[264,128]{1,0:T(8,128)(2,1)S(1)}, bf16[264,128]{1,0:T(8,128)(2,1)S(1)}, u32[]{:S(2)}, u32[]{:S(2)}) collective-permute-start(bf16[264,128]{1,0:T(8,128)(2,1)S(1)} %get-tuple-element.129), channel_id=1, source_target_pairs={{0,13},{1,12},{2,15},{3,14},{4,9},{5,8},{6,11},{7,10},{8,5},{9,4},... | collective-permute-start | bytes 202760 | tf_op jit(solution)/shard_map/ppermute | solution.py:404
  56.6 6.5 %collective-permute-start.26 = (bf16[264,128]{1,0:T(8,128)(2,1)S(1)}, bf16[264,128]{1,0:T(8,128)(2,1)S(1)}, u32[]{:S(2)}, u32[]{:S(2)}) collective-permute-start(bf16[264,128]{1,0:T(8,128)(2,1)S(1)} %get-tuple-element.130), channel_id=1, source_target_pairs={{0,6},{1,7},{2,4},{3,5},{4,2},{5,3},{6,0},{7,1},{8,14},{9,15},{10,... | collective-permute-start | bytes 202760 | tf_op jit(solution)/shard_map/ppermute | solution.py:404
  58.3 7.4 %collective-permute-start.27 = (bf16[264,128]{1,0:T(8,128)(2,1)S(1)}, bf16[264,128]{1,0:T(8,128)(2,1)S(1)}, u32[]{:S(2)}, u32[]{:S(2)}) collective-permute-start(bf16[264,128]{1,0:T(8,128)(2,1)S(1)} %get-tuple-element.131), channel_id=1, source_target_pairs={{0,14},{1,15},{2,12},{3,13},{4,10},{5,11},{6,8},{7,9},{8,6},{9,7},... | collective-permute-start | bytes 202760 | tf_op jit(solution)/shard_map/ppermute | solution.py:404
  60.5 7.3 %collective-permute-start.29 = (bf16[264,128]{1,0:T(8,128)(2,1)S(1)}, bf16[264,128]{1,0:T(8,128)(2,1)S(1)}, u32[]{:S(2)}, u32[]{:S(2)}) collective-permute-start(bf16[264,128]{1,0:T(8,128)(2,1)S(1)} %get-tuple-element.133), channel_id=1, source_target_pairs={{0,15},{1,14},{2,13},{3,12},{4,11},{5,10},{6,9},{7,8},{8,7},{9,6},... | collective-permute-start | bytes 202760 | tf_op jit(solution)/shard_map/ppermute | solution.py:404
  71.3 9.4 %collective-permute-start.30 = (bf16[264,128]{1,0:T(8,128)(2,1)S(1)}, bf16[264,128]{1,0:T(8,128)(2,1)S(1)}, u32[]{:S(2)}, u32[]{:S(2)}) collective-permute-start(bf16[264,128]{1,0:T(8,128)(2,1)S(1)} %get-tuple-element.137), channel_id=1, source_target_pairs={{0,8},{1,9},{2,10},{3,11},{4,12},{5,13},{6,14},{7,15},{8,0},{9,1},... | collective-permute-start | bytes 202760 | tf_op jit(solution)/shard_map/ppermute | solution.py:404
  71.6 9.1 %collective-permute-start.31 = (bf16[264,128]{1,0:T(8,128)(2,1)S(1)}, bf16[264,128]{1,0:T(8,128)(2,1)S(1)}, u32[]{:S(2)}, u32[]{:S(2)}) collective-permute-start(bf16[264,128]{1,0:T(8,128)(2,1)S(1)} %get-tuple-element.138), channel_id=1, source_target_pairs={{0,1},{1,0},{2,3},{3,2},{4,5},{5,4},{6,7},{7,6},{8,9},{9,8},{10,11... | collective-permute-start | bytes 202760 | tf_op jit(solution)/shard_map/ppermute | solution.py:404
  73.1 8.2 %collective-permute-start.32 = (bf16[264,128]{1,0:T(8,128)(2,1)S(1)}, bf16[264,128]{1,0:T(8,128)(2,1)S(1)}, u32[]{:S(2)}, u32[]{:S(2)}) collective-permute-start(bf16[264,128]{1,0:T(8,128)(2,1)S(1)} %get-tuple-element.139), channel_id=1, source_target_pairs={{0,9},{1,8},{2,11},{3,10},{4,13},{5,12},{6,15},{7,14},{8,1},{9,0},... | collective-permute-start | bytes 202760 | tf_op jit(solution)/shard_map/ppermute | solution.py:404
  74.4 8.7 %collective-permute-start.33 = (bf16[264,128]{1,0:T(8,128)(2,1)S(1)}, bf16[264,128]{1,0:T(8,128)(2,1)S(1)}, u32[]{:S(2)}, u32[]{:S(2)}) collective-permute-start(bf16[264,128]{1,0:T(8,128)(2,1)S(1)} %get-tuple-element.140), channel_id=1, source_target_pairs={{0,2},{1,3},{2,0},{3,1},{4,6},{5,7},{6,4},{7,5},{8,10},{9,11},{10,... | collective-permute-start | bytes 202760 | tf_op jit(solution)/shard_map/ppermute | solution.py:404
  75.9 10.6 %collective-permute-start.34 = (bf16[264,128]{1,0:T(8,128)(2,1)S(1)}, bf16[264,128]{1,0:T(8,128)(2,1)S(1)}, u32[]{:S(2)}, u32[]{:S(2)}) collective-permute-start(bf16[264,128]{1,0:T(8,128)(2,1)S(1)} %get-tuple-element.141), channel_id=1, source_target_pairs={{0,10},{1,11},{2,8},{3,9},{4,14},{5,15},{6,12},{7,13},{8,2},{9,3},... | collective-permute-start | bytes 202760 | tf_op jit(solution)/shard_map/ppermute | solution.py:404
  80.7 6.3 %collective-permute-start.36 = (bf16[264,128]{1,0:T(8,128)(2,1)S(1)}, bf16[264,128]{1,0:T(8,128)(2,1)S(1)}, u32[]{:S(2)}, u32[]{:S(2)}) collective-permute-start(bf16[264,128]{1,0:T(8,128)(2,1)S(1)} %get-tuple-element.143), channel_id=1, source_target_pairs={{0,11},{1,10},{2,9},{3,8},{4,15},{5,14},{6,13},{7,12},{8,3},{9,2},... | collective-permute-start | bytes 202760 | tf_op jit(solution)/shard_map/ppermute | solution.py:404
  81.3 7.3 %collective-permute-start.37 = (bf16[264,128]{1,0:T(8,128)(2,1)S(1)}, bf16[264,128]{1,0:T(8,128)(2,1)S(1)}, u32[]{:S(2)}, u32[]{:S(2)}) collective-permute-start(bf16[264,128]{1,0:T(8,128)(2,1)S(1)} %get-tuple-element.144), channel_id=1, source_target_pairs={{0,4},{1,5},{2,6},{3,7},{4,0},{5,1},{6,2},{7,3},{8,12},{9,13},{10,... | collective-permute-start | bytes 202760 | tf_op jit(solution)/shard_map/ppermute | solution.py:404
  83.1 8.9 %collective-permute-start.38 = (bf16[264,128]{1,0:T(8,128)(2,1)S(1)}, bf16[264,128]{1,0:T(8,128)(2,1)S(1)}, u32[]{:S(2)}, u32[]{:S(2)}) collective-permute-start(bf16[264,128]{1,0:T(8,128)(2,1)S(1)} %get-tuple-element.145), channel_id=1, source_target_pairs={{0,12},{1,13},{2,14},{3,15},{4,8},{5,9},{6,10},{7,11},{8,4},{9,5},... | collective-permute-start | bytes 202760 | tf_op jit(solution)/shard_map/ppermute | solution.py:404
  86.5 7.0 %collective-permute-start.40 = (bf16[264,128]{1,0:T(8,128)(2,1)S(1)}, bf16[264,128]{1,0:T(8,128)(2,1)S(1)}, u32[]{:S(2)}, u32[]{:S(2)}) collective-permute-start(bf16[264,128]{1,0:T(8,128)(2,1)S(1)} %get-tuple-element.147), channel_id=1, source_target_pairs={{0,13},{1,12},{2,15},{3,14},{4,9},{5,8},{6,11},{7,10},{8,5},{9,4},... | collective-permute-start | bytes 202760 | tf_op jit(solution)/shard_map/ppermute | solution.py:404
  87.0 8.5 %collective-permute-start.41 = (bf16[264,128]{1,0:T(8,128)(2,1)S(1)}, bf16[264,128]{1,0:T(8,128)(2,1)S(1)}, u32[]{:S(2)}, u32[]{:S(2)}) collective-permute-start(bf16[264,128]{1,0:T(8,128)(2,1)S(1)} %get-tuple-element.148), channel_id=1, source_target_pairs={{0,6},{1,7},{2,4},{3,5},{4,2},{5,3},{6,0},{7,1},{8,14},{9,15},{10,... | collective-permute-start | bytes 202760 | tf_op jit(solution)/shard_map/ppermute | solution.py:404
  88.5 7.7 %collective-permute-start.42 = (bf16[264,128]{1,0:T(8,128)(2,1)S(1)}, bf16[264,128]{1,0:T(8,128)(2,1)S(1)}, u32[]{:S(2)}, u32[]{:S(2)}) collective-permute-start(bf16[264,128]{1,0:T(8,128)(2,1)S(1)} %get-tuple-element.149), channel_id=1, source_target_pairs={{0,14},{1,15},{2,12},{3,13},{4,10},{5,11},{6,8},{7,9},{8,6},{9,7},... | collective-permute-start | bytes 202760 | tf_op jit(solution)/shard_map/ppermute | solution.py:404
  92.4 6.9 %collective-permute-start.44 = (bf16[264,128]{1,0:T(8,128)(2,1)S(1)}, bf16[264,128]{1,0:T(8,128)(2,1)S(1)}, u32[]{:S(2)}, u32[]{:S(2)}) collective-permute-start(bf16[264,128]{1,0:T(8,128)(2,1)S(1)} %get-tuple-element.151), channel_id=1, source_target_pairs={{0,15},{1,14},{2,13},{3,12},{4,11},{5,10},{6,9},{7,8},{8,7},{9,6},... | collective-permute-start | bytes 202760 | tf_op jit(solution)/shard_map/ppermute | solution.py:404
  101.7 7.9 %collective-permute-start.45 = (bf16[264,128]{1,0:T(8,128)(2,1)S(1)}, bf16[264,128]{1,0:T(8,128)(2,1)S(1)}, u32[]{:S(2)}, u32[]{:S(2)}) collective-permute-start(bf16[264,128]{1,0:T(8,128)(2,1)S(1)} %get-tuple-element.155), channel_id=1, source_target_pairs={{0,8},{1,9},{2,10},{3,11},{4,12},{5,13},{6,14},{7,15},{8,0},{9,1},... | collective-permute-start | bytes 202760 | tf_op jit(solution)/shard_map/ppermute | solution.py:404
  103.0 6.6 %collective-permute-start.46 = (bf16[264,128]{1,0:T(8,128)(2,1)S(1)}, bf16[264,128]{1,0:T(8,128)(2,1)S(1)}, u32[]{:S(2)}, u32[]{:S(2)}) collective-permute-start(bf16[264,128]{1,0:T(8,128)(2,1)S(1)} %get-tuple-element.156), channel_id=1, source_target_pairs={{0,1},{1,0},{2,3},{3,2},{4,5},{5,4},{6,7},{7,6},{8,9},{9,8},{10,11... | collective-permute-start | bytes 202760 | tf_op jit(solution)/shard_map/ppermute | solution.py:404
  103.0 9.0 %collective-permute-start.47 = (bf16[264,128]{1,0:T(8,128)(2,1)S(1)}, bf16[264,128]{1,0:T(8,128)(2,1)S(1)}, u32[]{:S(2)}, u32[]{:S(2)}) collective-permute-start(bf16[264,128]{1,0:T(8,128)(2,1)S(1)} %get-tuple-element.157), channel_id=1, source_target_pairs={{0,9},{1,8},{2,11},{3,10},{4,13},{5,12},{6,15},{7,14},{8,1},{9,0},... | collective-permute-start | bytes 202760 | tf_op jit(solution)/shard_map/ppermute | solution.py:404
  104.8 9.6 %collective-permute-start.48 = (bf16[264,128]{1,0:T(8,128)(2,1)S(1)}, bf16[264,128]{1,0:T(8,128)(2,1)S(1)}, u32[]{:S(2)}, u32[]{:S(2)}) collective-permute-start(bf16[264,128]{1,0:T(8,128)(2,1)S(1)} %get-tuple-element.158), channel_id=1, source_target_pairs={{0,2},{1,3},{2,0},{3,1},{4,6},{5,7},{6,4},{7,5},{8,10},{9,11},{10,... | collective-permute-start | bytes 202760 | tf_op jit(solution)/shard_map/ppermute | solution.py:404
  106.4 8.8 %collective-permute-start.49 = (bf16[264,128]{1,0:T(8,128)(2,1)S(1)}, bf16[264,128]{1,0:T(8,128)(2,1)S(1)}, u32[]{:S(2)}, u32[]{:S(2)}) collective-permute-start(bf16[264,128]{1,0:T(8,128)(2,1)S(1)} %get-tuple-element.159), channel_id=1, source_target_pairs={{0,10},{1,11},{2,8},{3,9},{4,14},{5,15},{6,12},{7,13},{8,2},{9,3},... | collective-permute-start | bytes 202760 | tf_op jit(solution)/shard_map/ppermute | solution.py:404
  109.6 7.5 %collective-permute-start.51 = (bf16[264,128]{1,0:T(8,128)(2,1)S(1)}, bf16[264,128]{1,0:T(8,128)(2,1)S(1)}, u32[]{:S(2)}, u32[]{:S(2)}) collective-permute-start(bf16[264,128]{1,0:T(8,128)(2,1)S(1)} %get-tuple-element.161), channel_id=1, source_target_pairs={{0,11},{1,10},{2,9},{3,8},{4,15},{5,14},{6,13},{7,12},{8,3},{9,2},... | collective-permute-start | bytes 202760 | tf_op jit(solution)/shard_map/ppermute | solution.py:404
  112.0 7.0 %collective-permute-start.52 = (bf16[264,128]{1,0:T(8,128)(2,1)S(1)}, bf16[264,128]{1,0:T(8,128)(2,1)S(1)}, u32[]{:S(2)}, u32[]{:S(2)}) collective-permute-start(bf16[264,128]{1,0:T(8,128)(2,1)S(1)} %get-tuple-element.162), channel_id=1, source_target_pairs={{0,4},{1,5},{2,6},{3,7},{4,0},{5,1},{6,2},{7,3},{8,12},{9,13},{10,... | collective-permute-start | bytes 202760 | tf_op jit(solution)/shard_map/ppermute | solution.py:404
  114.4 6.6 %collective-permute-start.53 = (bf16[264,128]{1,0:T(8,128)(2,1)S(1)}, bf16[264,128]{1,0:T(8,128)(2,1)S(1)}, u32[]{:S(2)}, u32[]{:S(2)}) collective-permute-start(bf16[264,128]{1,0:T(8,128)(2,1)S(1)} %get-tuple-element.163), channel_id=1, source_target_pairs={{0,12},{1,13},{2,14},{3,15},{4,8},{5,9},{6,10},{7,11},{8,4},{9,5},... | collective-permute-start | bytes 202760 | tf_op jit(solution)/shard_map/ppermute | solution.py:404
  115.2 6.1 %collective-permute-start.54 = (bf16[264,128]{1,0:T(8,128)(2,1)S(1)}, bf16[264,128]{1,0:T(8,128)(2,1)S(1)}, u32[]{:S(2)}, u32[]{:S(2)}) collective-permute-start(bf16[264,128]{1,0:T(8,128)(2,1)S(1)} %get-tuple-element.164), channel_id=1, source_target_pairs={{0,5},{1,4},{2,7},{3,6},{4,1},{5,0},{6,3},{7,2},{8,13},{9,12},{10,... | collective-permute-start | bytes 202760 | tf_op jit(solution)/shard_map/ppermute | solution.py:404
  115.5 8.2 %collective-permute-start.55 = (bf16[264,128]{1,0:T(8,128)(2,1)S(1)}, bf16[264,128]{1,0:T(8,128)(2,1)S(1)}, u32[]{:S(2)}, u32[]{:S(2)}) collective-permute-start(bf16[264,128]{1,0:T(8,128)(2,1)S(1)} %get-tuple-element.165), channel_id=1, source_target_pairs={{0,13},{1,12},{2,15},{3,14},{4,9},{5,8},{6,11},{7,10},{8,5},{9,4},... | collective-permute-start | bytes 202760 | tf_op jit(solution)/shard_map/ppermute | solution.py:404
  117.1 6.9 %collective-permute-start.56 = (bf16[264,128]{1,0:T(8,128)(2,1)S(1)}, bf16[264,128]{1,0:T(8,128)(2,1)S(1)}, u32[]{:S(2)}, u32[]{:S(2)}) collective-permute-start(bf16[264,128]{1,0:T(8,128)(2,1)S(1)} %get-tuple-element.166), channel_id=1, source_target_pairs={{0,6},{1,7},{2,4},{3,5},{4,2},{5,3},{6,0},{7,1},{8,14},{9,15},{10,... | collective-permute-start | bytes 202760 | tf_op jit(solution)/shard_map/ppermute | solution.py:404
  119.0 7.3 %collective-permute-start.57 = (bf16[264,128]{1,0:T(8,128)(2,1)S(1)}, bf16[264,128]{1,0:T(8,128)(2,1)S(1)}, u32[]{:S(2)}, u32[]{:S(2)}) collective-permute-start(bf16[264,128]{1,0:T(8,128)(2,1)S(1)} %get-tuple-element.167), channel_id=1, source_target_pairs={{0,14},{1,15},{2,12},{3,13},{4,10},{5,11},{6,8},{7,9},{8,6},{9,7},... | collective-permute-start | bytes 202760 | tf_op jit(solution)/shard_map/ppermute | solution.py:404
  121.3 6.9 %collective-permute-start.59 = (bf16[264,128]{1,0:T(8,128)(2,1)S(1)}, bf16[264,128]{1,0:T(8,128)(2,1)S(1)}, u32[]{:S(2)}, u32[]{:S(2)}) collective-permute-start(bf16[264,128]{1,0:T(8,128)(2,1)S(1)} %get-tuple-element.169), channel_id=1, source_target_pairs={{0,15},{1,14},{2,13},{3,12},{4,11},{5,10},{6,9},{7,8},{8,7},{9,6},... | collective-permute-start | bytes 202760 | tf_op jit(solution)/shard_map/ppermute | solution.py:404
  131.6 7.2 %collective-permute-start.60 = (bf16[264,128]{1,0:T(8,128)(2,1)S(1)}, bf16[264,128]{1,0:T(8,128)(2,1)S(1)}, u32[]{:S(2)}, u32[]{:S(2)}) collective-permute-start(bf16[264,128]{1,0:T(8,128)(2,1)S(1)} %get-tuple-element.174), channel_id=1, source_target_pairs={{0,8},{1,9},{2,10},{3,11},{4,12},{5,13},{6,14},{7,15},{8,0},{9,1},... | collective-permute-start | bytes 202760 | tf_op jit(solution)/shard_map/ppermute | solution.py:404
  132.3 6.5 %collective-permute-start.61 = (bf16[264,128]{1,0:T(8,128)(2,1)S(1)}, bf16[264,128]{1,0:T(8,128)(2,1)S(1)}, u32[]{:S(2)}, u32[]{:S(2)}) collective-permute-start(bf16[264,128]{1,0:T(8,128)(2,1)S(1)} %get-tuple-element.175), channel_id=1, source_target_pairs={{0,1},{1,0},{2,3},{3,2},{4,5},{5,4},{6,7},{7,6},{8,9},{9,8},{10,11... | collective-permute-start | bytes 202760 | tf_op jit(solution)/shard_map/ppermute | solution.py:404
  133.6 8.6 %collective-permute-start.62 = (bf16[264,128]{1,0:T(8,128)(2,1)S(1)}, bf16[264,128]{1,0:T(8,128)(2,1)S(1)}, u32[]{:S(2)}, u32[]{:S(2)}) collective-permute-start(bf16[264,128]{1,0:T(8,128)(2,1)S(1)} %get-tuple-element.176), channel_id=1, source_target_pairs={{0,9},{1,8},{2,11},{3,10},{4,13},{5,12},{6,15},{7,14},{8,1},{9,0},... | collective-permute-start | bytes 202760 | tf_op jit(solution)/shard_map/ppermute | solution.py:404
  134.7 9.3 %collective-permute-start.63 = (bf16[264,128]{1,0:T(8,128)(2,1)S(1)}, bf16[264,128]{1,0:T(8,128)(2,1)S(1)}, u32[]{:S(2)}, u32[]{:S(2)}) collective-permute-start(bf16[264,128]{1,0:T(8,128)(2,1)S(1)} %get-tuple-element.177), channel_id=1, source_target_pairs={{0,2},{1,3},{2,0},{3,1},{4,6},{5,7},{6,4},{7,5},{8,10},{9,11},{10,... | collective-permute-start | bytes 202760 | tf_op jit(solution)/shard_map/ppermute | solution.py:404
  136.2 10.9 %collective-permute-start.64 = (bf16[264,128]{1,0:T(8,128)(2,1)S(1)}, bf16[264,128]{1,0:T(8,128)(2,1)S(1)}, u32[]{:S(2)}, u32[]{:S(2)}) collective-permute-start(bf16[264,128]{1,0:T(8,128)(2,1)S(1)} %get-tuple-element.178), channel_id=1, source_target_pairs={{0,10},{1,11},{2,8},{3,9},{4,14},{5,15},{6,12},{7,13},{8,2},{9,3},... | collective-permute-start | bytes 202760 | tf_op jit(solution)/shard_map/ppermute | solution.py:404
  138.8 8.3 %collective-permute-start.65 = (bf16[264,128]{1,0:T(8,128)(2,1)S(1)}, bf16[264,128]{1,0:T(8,128)(2,1)S(1)}, u32[]{:S(2)}, u32[]{:S(2)}) collective-permute-start(bf16[264,128]{1,0:T(8,128)(2,1)S(1)} %get-tuple-element.179), channel_id=1, source_target_pairs={{0,3},{1,2},{2,1},{3,0},{4,7},{5,6},{6,5},{7,4},{8,11},{9,10},{10,... | collective-permute-start | bytes 202760 | tf_op jit(solution)/shard_map/ppermute | solution.py:404
  138.8 9.3 %collective-permute-start.66 = (bf16[264,128]{1,0:T(8,128)(2,1)S(1)}, bf16[264,128]{1,0:T(8,128)(2,1)S(1)}, u32[]{:S(2)}, u32[]{:S(2)}) collective-permute-start(bf16[264,128]{1,0:T(8,128)(2,1)S(1)} %get-tuple-element.180), channel_id=1, source_target_pairs={{0,11},{1,10},{2,9},{3,8},{4,15},{5,14},{6,13},{7,12},{8,3},{9,2},... | collective-permute-start | bytes 202760 | tf_op jit(solution)/shard_map/ppermute | solution.py:404
  142.2 7.1 %collective-permute-start.67 = (bf16[264,128]{1,0:T(8,128)(2,1)S(1)}, bf16[264,128]{1,0:T(8,128)(2,1)S(1)}, u32[]{:S(2)}, u32[]{:S(2)}) collective-permute-start(bf16[264,128]{1,0:T(8,128)(2,1)S(1)} %get-tuple-element.181), channel_id=1, source_target_pairs={{0,4},{1,5},{2,6},{3,7},{4,0},{5,1},{6,2},{7,3},{8,12},{9,13},{10,... | collective-permute-start | bytes 202760 | tf_op jit(solution)/shard_map/ppermute | solution.py:404
  144.0 8.7 %collective-permute-start.68 = (bf16[264,128]{1,0:T(8,128)(2,1)S(1)}, bf16[264,128]{1,0:T(8,128)(2,1)S(1)}, u32[]{:S(2)}, u32[]{:S(2)}) collective-permute-start(bf16[264,128]{1,0:T(8,128)(2,1)S(1)} %get-tuple-element.182), channel_id=1, source_target_pairs={{0,12},{1,13},{2,14},{3,15},{4,8},{5,9},{6,10},{7,11},{8,4},{9,5},... | collective-permute-start | bytes 202760 | tf_op jit(solution)/shard_map/ppermute | solution.py:404
  147.1 7.6 %collective-permute-start.70 = (bf16[264,128]{1,0:T(8,128)(2,1)S(1)}, bf16[264,128]{1,0:T(8,128)(2,1)S(1)}, u32[]{:S(2)}, u32[]{:S(2)}) collective-permute-start(bf16[264,128]{1,0:T(8,128)(2,1)S(1)} %get-tuple-element.184), channel_id=1, source_target_pairs={{0,13},{1,12},{2,15},{3,14},{4,9},{5,8},{6,11},{7,10},{8,5},{9,4},... | collective-permute-start | bytes 202760 | tf_op jit(solution)/shard_map/ppermute | solution.py:404
  148.1 7.2 %collective-permute-start.71 = (bf16[264,128]{1,0:T(8,128)(2,1)S(1)}, bf16[264,128]{1,0:T(8,128)(2,1)S(1)}, u32[]{:S(2)}, u32[]{:S(2)}) collective-permute-start(bf16[264,128]{1,0:T(8,128)(2,1)S(1)} %get-tuple-element.185), channel_id=1, source_target_pairs={{0,6},{1,7},{2,4},{3,5},{4,2},{5,3},{6,0},{7,1},{8,14},{9,15},{10,... | collective-permute-start | bytes 202760 | tf_op jit(solution)/shard_map/ppermute | solution.py:404
  149.2 7.9 %collective-permute-start.72 = (bf16[264,128]{1,0:T(8,128)(2,1)S(1)}, bf16[264,128]{1,0:T(8,128)(2,1)S(1)}, u32[]{:S(2)}, u32[]{:S(2)}) collective-permute-start(bf16[264,128]{1,0:T(8,128)(2,1)S(1)} %get-tuple-element.186), channel_id=1, source_target_pairs={{0,14},{1,15},{2,12},{3,13},{4,10},{5,11},{6,8},{7,9},{8,6},{9,7},... | collective-permute-start | bytes 202760 | tf_op jit(solution)/shard_map/ppermute | solution.py:404
  152.7 7.0 %collective-permute-start.74 = (bf16[264,128]{1,0:T(8,128)(2,1)S(1)}, bf16[264,128]{1,0:T(8,128)(2,1)S(1)}, u32[]{:S(2)}, u32[]{:S(2)}) collective-permute-start(bf16[264,128]{1,0:T(8,128)(2,1)S(1)} %get-tuple-element.188), channel_id=1, source_target_pairs={{0,15},{1,14},{2,13},{3,12},{4,11},{5,10},{6,9},{7,8},{8,7},{9,6},... | collective-permute-start | bytes 202760 | tf_op jit(solution)/shard_map/ppermute | solution.py:404
  (20 other events, 121.5 us)

commit v13 on v12

--- a/solution.py
+++ b/solution.py
@@ -21,6 +21,30 @@
 CHUNKS = 8
 
 
+def steps_of(peers):
+    tailed = tailed_of(peers)
+    rest = [step for step in range(1, peers) if step not in tailed]
+    near = [step for step in rest if step < peers // 2]
+    far = [step for step in rest if step >= peers // 2]
+    turns = [step for both in zip(far, near) for step in both]
+    return [0] + tailed + turns + far[len(near) :] + near[len(far) :]
+
+
+def tailed_of(peers):
+    return [peers // 2, peers // 4, peers // 2 + peers // 4]
+
+
+def later(values, rows):
+    cut = len(values) * 2 // 3
+    return [*values[:cut], *rows, *values[cut:]]
+
+
+def parted(refs, peers):
+    cut = peers * 2 // 3
+    rest = peers - cut
+    return [*refs[:cut], *refs[len(refs) - rest :]], refs[cut : len(refs) - rest]
+
+
 def diagonal(cols):
     shape = (cols, BS)
     return lax.broadcasted_iota(jnp.int32, shape, 0) == lax.broadcasted_iota(jnp.int32, shape, 1)
@@ -39,8 +63,8 @@
     )
 
 
-def norm_of_tails(message_refs, cols):
-    summed = sum(message_ref[BCAP * cols :, :].astype(F32) for message_ref in message_refs)
+def norm_of(tails, cols):
+    summed = sum(tails)
     row = summed[0:1] + summed[1:2] + summed[2:3]
     column = jnp.sum(jnp.where(diagonal(cols), row, 0.0), axis=1, keepdims=True)
     return jnp.broadcast_to(jnp.sqrt(column + EPS), (cols, BS))
@@ -88,7 +112,9 @@
 def start_kernel(peers, me_ref, cells_hbm, counts_hbm, times_hbm, rays_hbm, *refs):
     message_refs = refs[:peers]
     target_ref, total_ref, table_ref, used_ref, cells_ref, counts_ref = refs[peers : peers + 6]
-    times_ref, rays_ref, sems, ray_sems = refs[peers + 6 :]
+    times_ref, rays_ref, place_ref, sems, ray_sems = refs[peers + 6 :]
+    for index, step in enumerate(steps_of(peers)):
+        place_ref[me_ref[0] ^ step] = index
     pair_count, slot_count = rays_ref.shape[:2]
     cols = times_ref.shape[0]
     owned = CELL_DEV // BS
@@ -124,8 +150,7 @@
         count = counts_ref[pair]
         for slot in range(slot_count):
             cell = cells_ref[pair, slot]
-            apart = (cell // owned) ^ me_ref[0]
-            owner = apart * 2 - jnp.where(apart < peers // 2, 0, peers - 1)
+            owner = place_ref[cell // owned]
             local = cell % owned
             used = used_ref[owner]
             rank = used
@@ -171,17 +196,18 @@
         copy.wait()
 
 
-def pair_kernel(peers, target_ref, *refs):
-    fetched_refs = refs[:peers]
-    data_ref, beta_ref, rays_ref = refs[peers : peers + 3]
-    message_refs = refs[peers + 3 : 2 * peers + 3]
-    alpha_ref, raw_ref, total_ref, fetched_ref = refs[2 * peers + 3 :]
+def pair_kernel(peers, rows, target_ref, *refs):
+    fetched_refs, row_refs = parted(refs[: peers + rows], peers)
+    refs = refs[peers + rows :]
+    data_ref, beta_ref, rays_ref = refs[:3]
+    message_refs = refs[3 : peers + 3]
+    alpha_ref, share_ref, raw_ref, total_ref, fetched_ref = refs[peers + 3 :]
     pair_count, slot_count = rays_ref.shape[:2]
     cols = data_ref.shape[0]
     spots = peers * BCAP
     for peer in range(peers):
         fetched_ref[peer] = fetched_refs[peer][: BCAP * cols, :]
-    alpha = norm_of_tails(fetched_refs, cols)
+    alpha = norm_of([ref[...] for ref in row_refs], cols)
     alpha_ref[...] = alpha
     beta = beta_ref[...]
     model_scale = 1.0 / (alpha * beta)
@@ -207,9 +233,14 @@
 
     squares = lax.fori_loop(0, pair_count, one_pair, jnp.zeros((cols, BS), F32), unroll=True)
     transposed(raw_ref, rays_ref, lambda pair: None, target_ref, total_ref, message_refs)
-    tail = squares_tail(squares).astype(BF16)
+    write_tails(squares_tail(squares), message_refs, share_ref, cols)
+
+
+def write_tails(tail, message_refs, share_ref, cols):
+    share_ref[...] = tail
     for message_ref in message_refs:
-        message_ref[BCAP * cols :, :] = tail
+        if message_ref.shape[0] > BCAP * cols:
+            message_ref[BCAP * cols :, :] = tail.astype(BF16)
 
 
 def gathered(arrived_refs, asked_ref, model_ref):
@@ -220,11 +251,10 @@
             model_ref[:, where] += arrived_ref[rank * cols : (rank + 1) * cols, :].astype(F32)
 
 
-def reply(squares, scale, asked_ref, model_ref, out_refs):
+def reply(squares, scale, asked_ref, model_ref, out_refs, share_ref):
     cols = model_ref.shape[0]
-    tail = squares_tail(squares * scale * scale).astype(BF16)
+    write_tails(squares_tail(squares * scale * scale), out_refs, share_ref, cols)
     for peer, out_ref in enumerate(out_refs):
-        out_ref[BCAP * cols :, :] = tail
         for rank in range(BCAP):
             block = model_ref[:, lanes(asked_ref[peer, rank])]
             out_ref[rank * cols : (rank + 1) * cols, :] = block.astype(BF16)
@@ -241,21 +271,21 @@
 
 
 def first_cell_kernel(peers, *refs):
-    arrived_refs, out_refs = refs[:peers], refs[peers + 2 : 2 * peers + 2]
-    model_ref, beta_ref = refs[peers : peers + 2]
-    asked_ref, table_ref, sem = refs[2 * peers + 2 :]
+    arrived_refs, out_refs = refs[:peers], refs[peers + 3 : 2 * peers + 3]
+    model_ref, beta_ref, share_ref = refs[peers : peers + 3]
+    asked_ref, table_ref, sem = refs[2 * peers + 3 :]
     cols, cells = model_ref.shape
     for peer in range(peers):
         tail = arrived_refs[peer][BCAP * cols :, :].astype(F32)
         table_ref[peer : peer + 1, :] = tail[3:4].astype(jnp.int32)
     copy = pltpu.make_async_copy(table_ref, asked_ref, sem)
     copy.start()
-    beta = norm_of_tails(arrived_refs, cols)
+    beta = norm_of([ref[BCAP * cols :, :].astype(F32) for ref in arrived_refs], cols)
     beta_ref[...] = beta
     model_ref[...] = jnp.zeros((cols, cells), F32)
     copy.wait()
     gathered(arrived_refs, asked_ref, model_ref)
-    reply(squares_of(model_ref), 1.0 / beta, asked_ref, model_ref, out_refs)
+    reply(squares_of(model_ref), 1.0 / beta, asked_ref, model_ref, out_refs, share_ref)
 
 
 def start_from(before_ref, scale, model_ref):
@@ -266,27 +296,16 @@
     lax.fori_loop(0, model_ref.shape[1] // BS, one_block, 0, unroll=8)
 
 
-def cell_kernel(peers, asked_ref, *refs):
-    arrived_refs, out_refs = refs[:peers], refs[peers + 5 :]
-    before_ref, alpha_ref, beta_before_ref, model_ref, beta_ref = refs[peers : peers + 5]
-    beta = norm_of_tails(arrived_refs, model_ref.shape[0])
+def cell_kernel(peers, rows, asked_ref, *refs):
+    arrived_refs, row_refs = parted(refs[: peers + rows], peers)
+    before_ref, alpha_ref, beta_before_ref, model_ref, beta_ref, share_ref, *out_refs = refs[
+        peers + rows :
+    ]
+    beta = norm_of([ref[...] for ref in row_refs], model_ref.shape[0])
     beta_ref[...] = beta
     start_from(before_ref, beta * beta / (alpha_ref[...] * beta_before_ref[...]), model_ref)
     gathered(arrived_refs, asked_ref, model_ref)
-    reply(squares_of(model_ref), 1.0 / beta, asked_ref, model_ref, out_refs)
-
-
-def last_cell_kernel(peers, asked_ref, *refs):
-    arrived_refs = refs[:peers]
-    before_ref, alpha_ref, beta_before_ref, model_ref, beta_ref, out_ref = refs[peers:]
-    beta = norm_of_tails(arrived_refs, model_ref.shape[0])
-    beta_ref[...] = beta
-    start_from(before_ref, beta * beta / (alpha_ref[...] * beta_before_ref[...]), model_ref)
-    gathered(arrived_refs, asked_ref, model_ref)
-    squares = squares_of(model_ref) / (beta * beta)
-    total = jnp.sum(squares, axis=1, keepdims=True)
-    row = jnp.sum(jnp.where(diagonal(total.shape[0]), total, 0.0), axis=0, keepdims=True)
-    out_ref[...] = jnp.broadcast_to(row, out_ref.shape)
+    reply(squares_of(model_ref), 1.0 / beta, asked_ref, model_ref, out_refs, share_ref)
 
 
 def estimate_kernel(*refs):
@@ -347,10 +366,7 @@
     *share_refs, beta_ref, model_ref, out_hbm, out_ref, sems = refs
     cols, cells = model_ref.shape
     blocks = cells // BS // CHUNKS
-    row = sum(ref[...] for ref in share_refs)[0:1]
-    column = jnp.sum(jnp.where(diagonal(cols), row, 0.0), axis=1, keepdims=True)
-    alpha = jnp.broadcast_to(jnp.sqrt(column + EPS), (cols, BS))
-    scale = 1.0 / (alpha * beta_ref[...])
+    scale = 1.0 / (norm_of([ref[...] for ref in share_refs], cols) * beta_ref[...])
 
     def one_block(block, carry):
         out_ref[:, lanes(block)] = model_ref[:, lanes(block)] * scale
@@ -388,8 +404,12 @@
     spots = peers * BCAP
     times = travel_times.T
     cols, pairs = times.shape
-    messages = [((BCAP * cols + TAIL, BS), BF16, VMEM)] * peers
-    ins = [VMEM] * peers
+    steps = steps_of(peers)
+    messages = [
+        ((BCAP * cols + TAIL * (step in tailed_of(peers)), BS), BF16, VMEM) for step in steps
+    ]
+    first_messages = [((BCAP * cols + TAIL, BS), BF16, VMEM)] * peers
+    row = ((TAIL, BS), F32, VMEM)
     gathered_blocks = VMEM((peers, BCAP * cols, BS), BF16)
     tile = ((cols, BS), F32, VMEM)
     data = ((cols, pairs), F32, VMEM)
@@ -397,22 +417,24 @@
     totals = VMEM((spots + 1, cols, BS), F32)
     flops = 2 * slots * BS * BS * cols
 
+    def send(value, step):
+        return lax.ppermute(value, "pair", [(one, one ^ step) for one in range(peers)])
+
     def exchange(values):
-        half = peers // 2
-        steps = [i // 2 + i % 2 * half for i in range(peers)]
-        return [values[0]] + [
-            lax.ppermute(value, "pair", [(one, one ^ step) for one in range(peers)])
-            for value, step in zip(values[1:], steps[1:])
-        ]
+        return [values[0]] + [send(value, step) for value, step in zip(values[1:], steps[1:])]
+
+    def completed(share, arrived):
+        share = sum((arrived[i][BCAP * cols :, :].astype(F32) for i in range(1, 4)), share)
+        return [share] + [send(share, step) for step in range(1, peers // 4)]
 
     me = lax.axis_index("pair").astype(jnp.int32).reshape(1)
     *outgoing, target = call(
         functools.partial(start_kernel, peers), "start", [SMEM, HBM, HBM, HBM, HBM],
-        messages + [((slots,), jnp.int32, SMEM)],
+        first_messages + [((slots,), jnp.int32, SMEM)],
         [
             totals, SMEM((spots,), jnp.int32), SMEM((peers,), jnp.int32),
             SMEM(block_cells.shape, jnp.int32), SMEM(block_counts.shape, jnp.int32),
-            VMEM(times.shape, F32), VMEM(ray_blocks.shape, BF16),
+            VMEM(times.shape, F32), VMEM(ray_blocks.shape, BF16), SMEM((peers,), jnp.int32),
             pltpu.SemaphoreType.DMA((3,)), pltpu.SemaphoreType.DMA((pair_count,)),
         ],
         flops, 6 << 20, 60 << 20,
@@ -420,12 +442,12 @@
     arrived = exchange(outgoing)
     target, arrived[0], ray_blocks = call(
         keep_kernel, "keep", [HBM, HBM, HBM],
-        [((slots,), jnp.int32, SMEM), messages[0], (ray_blocks.shape, BF16, VMEM)],
+        [((slots,), jnp.int32, SMEM), first_messages[0], (ray_blocks.shape, BF16, VMEM)],
         [pltpu.SemaphoreType.DMA((3,))], 0, 8 << 20, 48 << 20,
     )(target, arrived[0], ray_blocks)
-    model, beta, *replies, asked = call(
-        functools.partial(first_cell_kernel, peers), "cells_first", ins,
-        [whole, tile] + messages + [((peers, BS), jnp.int32, SMEM)],
+    model, beta, share, *replies, asked = call(
+        functools.partial(first_cell_kernel, peers), "cells_first", [VMEM] * peers,
+        [whole, tile, row] + messages + [((peers, BS), jnp.int32, SMEM)],
         [VMEM((peers, BS), jnp.int32), pltpu.SemaphoreType.DMA],
         0, 6 << 20,
     )(*arrived)
@@ -433,45 +455,36 @@
     current = times
     for step in range(ITERS):
         fetched = exchange(replies)
+        rows = completed(share, fetched)
+        ins = [VMEM] * (peers + len(rows))
         last = step + 1 == ITERS
         made = call(
-            functools.partial(pair_kernel, peers), "pairs_last" if last else "pairs",
-            [SMEM] + ins + [VMEM, VMEM, VMEM], messages + [tile] + [data] * (not last),
+            functools.partial(pair_kernel, peers, len(rows)), "pairs_last" if last else "pairs",
+            [SMEM] + ins + [VMEM, VMEM, VMEM], messages + [tile, row] + [data] * (not last),
             [VMEM(data[0], F32)] * last + [totals, gathered_blocks], 2 * flops, 8 << 20,
-        )(target, *fetched, current, betas[-1], ray_blocks)
+        )(target, *later(fetched, rows), current, betas[-1], ray_blocks)
         alphas.append(made[peers])
         current = made[-1]
         arrived = exchange(made[:peers])
-        if not last:
-            model, beta, *replies = call(
-                functools.partial(cell_kernel, peers), "cells", [SMEM] + ins + [VMEM] * 3,
-                [whole, tile] + messages, (), 0, 8 << 20,
-            )(asked, *arrived, models[-1], alphas[-1], betas[-1])
-            models.append(model)
-            betas.append(beta)
-    model, beta, share = call(
-        functools.partial(last_cell_kernel, peers), "cells_last", [SMEM] + ins + [VMEM] * 3,
-        [whole, tile, ((8, BS), F32, VMEM)], (), 0, 8 << 20,
-    )(asked, *arrived, models[-1], alphas[-1], betas[-1])
-    betas.append(beta)
-    reach, shares = peers, [share]
-    while reach > 1:
-        share = sum(shares[1:], shares[0])
-        low = max(reach // 4, 1)
-        shares = [share] + [
-            lax.ppermute(share, "pair", [(one, one ^ step) for one in range(peers)])
-            for step in range(low, reach, low)
-        ]
-        reach = low
+        rows = completed(made[peers + 1], arrived)
+        model, beta, share, *replies = call(
+            functools.partial(cell_kernel, peers, len(rows)), "cells_last" if last else "cells",
+            [SMEM] + ins + [VMEM] * 3, [whole, tile, row] + messages * (not last), (), 0, 8 << 20,
+        )(asked, *later(arrived, rows), models[-1], alphas[-1], betas[-1])
+        models.append(model)
+        betas.append(beta)
+    for low, reach in ((peers // 4, peers), (1, peers // 4)):
+        rows = [share] + [send(share, step) for step in range(low, reach, low)]
+        share = sum(rows[1:], rows[0])
     scratch = [VMEM(whole[0], F32), pltpu.SemaphoreType.DMA((CHUNKS,))]
     (estimate,) = call(
         estimate_kernel, "estimate", [VMEM] * (3 * ITERS + 1), [(whole[0], F32, HBM)], scratch,
         0, 6 << 20,
-    )(*models, *alphas, *betas)
+    )(*models[:ITERS], *alphas, *betas)
     (model_vec,) = call(
-        model_kernel, "model", [VMEM] * (len(shares) + 2), [(whole[0], F32, HBM)], scratch,
+        model_kernel, "model", [VMEM] * (len(rows) + 2), [(whole[0], F32, HBM)], scratch,
         0, 4 << 20,
-    )(*shares, beta, model)
+    )(*rows, beta, model)
     return (estimate.T, model_vec.T)
 
 

time: 174 us -> 194 us (1.11)
  starting transfers between devices: 104 us -> 122 us
  waiting for transfers between devices: 41.8 us -> 44.6 us
    ppermute x81 -> x93, starting transfers between devices: 104 us -> 122 us  [send(): lax.ppermute(value, 'pair', [(one, one ^ step) for one in range(peers)])]
    ppermute x81 -> x93, waiting for transfers between devices: 41.8 us -> 44.6 us  [send(): lax.ppermute(value, 'pair', [(one, one ^ step) for one in range(peers)])]
  transfers between devices with their start and end apart: 81 -> 93, of which waited for: 32 -> 33; matrix products, arithmetic and copies ran while one was open for 0% -> 0% of each run, Pallas kernels for 3% -> 2%
where the time goes in v13:
time: 194 us
  starting transfers between devices  122 us (63%)
  waiting for transfers between devices  44.6 us (23%)
  Pallas kernels  25.2 us (13%)
    ppermute x93, starting transfers between devices, send(): lax.ppermute(value, 'pair', [(one, one ^ step) for one in range(peers)])  122 us
    ppermute x93, waiting for transfers between devices, send(): lax.ppermute(value, 'pair', [(one, one ^ step) for one in range(peers)])  44.6 us
    pallas_call x2, Pallas kernels, on_device(): call(functools.partial(pair_kernel, peers, len(rows)), 'pairs_last' if la...  6.94 us
    pallas_call x1, Pallas kernels, on_device(): call(functools.partial(start_kernel, peers), 'start', [SMEM, HBM, HBM, HB...  5.44 us
    pallas_call x2, Pallas kernels, on_device(): call(functools.partial(cell_kernel, peers, len(rows)), 'cells_last' if la...  4.37 us
  transfers between devices with their start and end apart: 93, of which 33 were waited for; matrix products, arithmetic and copies ran while one was open for 0% of the time, Pallas kernels for 2%

profile of v13, /device:TPU:0, one launch (start us, length us, event | category | flops | bytes accessed | tf_op | source)
XLA Modules:
  0.0 194.3 jit_solution(8836614056085748977)
XLA Ops:
  0.6 5.4 %start.1 = (bf16[264,128]{1,0:T(8,128)(2,1)}, bf16[264,128]{1,0:T(8,128)(2,1)}, bf16[264,128]{1,0:T(8,128)(2,1)}, bf16[264,128]{1,0:T(8,128)(2,1)}, bf16[264,128...) custom-call(s32[1]{0:T(128)} %bitcast.me_ref, ...), custom_call_target="tpu_custom_call" | custom-call | flops 268435456 | bytes 6291456 | tf_op jit(solution)/shard_map/start/pallas_call | solution.py:431
  6.1 4.1 %collective-permute-start = (bf16[264,128]{1,0:T(8,128)(2,1)}, bf16[264,128]{1,0:T(8,128)(2,1)S(1)}, u32[]{:S(2)}, u32[]{:S(2)}) collective-permute-start(bf16[264,128]{1,0:T(8,128)(2,1)} %get-tuple-element.104), channel_id=1, source_target_pairs={{0,8},{1,9},{2,10},{3,11},{4,12},{5,13},{6,14},{7,15},{8,0},{9,1},... | collective-permute-start | bytes 202760 | tf_op jit(solution)/shard_map/ppermute | solution.py:421
  10.2 1.5 collective-permute-start.1
  12.2 1.6 collective-permute-start.4
  13.8 3.2 %collective-permute-start.5 = (bf16[264,128]{1,0:T(8,128)(2,1)}, bf16[264,128]{1,0:T(8,128)(2,1)S(1)}, u32[]{:S(2)}, u32[]{:S(2)}) collective-permute-start(bf16[264,128]{1,0:T(8,128)(2,1)} %get-tuple-element.109), channel_id=1, source_target_pairs={{0,10},{1,11},{2,8},{3,9},{4,14},{5,15},{6,12},{7,13},{8,2},{9,3},... | collective-permute-start | bytes 202760 | tf_op jit(solution)/shard_map/ppermute | solution.py:421
  18.0 4.6 %collective-permute-start.7 = (bf16[264,128]{1,0:T(8,128)(2,1)}, bf16[264,128]{1,0:T(8,128)(2,1)S(1)}, u32[]{:S(2)}, u32[]{:S(2)}) collective-permute-start(bf16[264,128]{1,0:T(8,128)(2,1)} %get-tuple-element.111), channel_id=1, source_target_pairs={{0,11},{1,10},{2,9},{3,8},{4,15},{5,14},{6,13},{7,12},{8,3},{9,2},... | collective-permute-start | bytes 202760 | tf_op jit(solution)/shard_map/ppermute | solution.py:421
  22.6 1.4 collective-permute-start.8
  24.0 2.6 %collective-permute-start.9 = (bf16[264,128]{1,0:T(8,128)(2,1)}, bf16[264,128]{1,0:T(8,128)(2,1)S(1)}, u32[]{:S(2)}, u32[]{:S(2)}) collective-permute-start(bf16[264,128]{1,0:T(8,128)(2,1)} %get-tuple-element.113), channel_id=1, source_target_pairs={{0,13},{1,12},{2,15},{3,14},{4,9},{5,8},{6,11},{7,10},{8,5},{9,4},... | collective-permute-start | bytes 202760 | tf_op jit(solution)/shard_map/ppermute | solution.py:421
  26.7 4.4 %collective-permute-start.11 = (bf16[264,128]{1,0:T(8,128)(2,1)}, bf16[264,128]{1,0:T(8,128)(2,1)S(1)}, u32[]{:S(2)}, u32[]{:S(2)}) collective-permute-start(bf16[264,128]{1,0:T(8,128)(2,1)} %get-tuple-element.115), channel_id=1, source_target_pairs={{0,14},{1,15},{2,12},{3,13},{4,10},{5,11},{6,8},{7,9},{8,6},{9,7},... | collective-permute-start | bytes 202760 | tf_op jit(solution)/shard_map/ppermute | solution.py:421
  34.7 2.9 %keep.1 = (s32[128]{0:T(128)S(1)}, bf16[264,128]{1,0:T(8,128)(2,1)S(1)}, bf16[8,16,128,128]{3,2,1,0:T(8,128)(2,1)S(1)}) custom-call(s32[128]{0:T(128)S(1)} %copy-done.2, bf16[264,128]{1,0:T(8,128)(2,1)S(1)} %copy-done.1, bf16[8,16,128,128]{3,2,1,0:T(8,128)(2,1)} %rays_hbm.3), custom_call_target="tpu_custom_call" | custom-call | bytes 8388608 | tf_op jit(solution)/shard_map/keep/pallas_call | solution.py:443
  38.4 2.5 %cells_first.1 = (f32[64,8192]{1,0:T(8,128)S(1)}, f32[64,128]{1,0:T(8,128)S(1)}, f32[8,128]{1,0:T(8,128)S(1)}, bf16[256,128]{1,0:T(8,128)(2,1)S(1)}, bf16[264,12...) custom-call(bf16[264,128]{1,0:T(8,128)(2,1)S(1)} %get-tuple-element., ...), custom_call_target="tpu_custom_call" | custom-call | bytes 6291456 | tf_op jit(solution)/shard_map/cells_first/pallas_call | solution.py:448
  40.9 2.0 %collective-permute-start.18 = (bf16[256,128]{1,0:T(8,128)(2,1)S(1)}, bf16[256,128]{1,0:T(8,128)(2,1)S(1)}, u32[]{:S(2)}, u32[]{:S(2)}) collective-permute-start(bf16[256,128]{1,0:T(8,128)(2,1)S(1)} %get-tuple-element.126), channel_id=1, source_target_pairs={{0,9},{1,8},{2,11},{3,10},{4,13},{5,12},{6,15},{7,14},{8,1},{9,0},... | collective-permute-start | bytes 196616 | tf_op jit(solution)/shard_map/ppermute | solution.py:421
  43.3 1.5 collective-permute-start.20
  45.7 2.5 %collective-permute-start.22 = (bf16[256,128]{1,0:T(8,128)(2,1)S(1)}, bf16[256,128]{1,0:T(8,128)(2,1)S(1)}, u32[]{:S(2)}, u32[]{:S(2)}) collective-permute-start(bf16[256,128]{1,0:T(8,128)(2,1)S(1)} %get-tuple-element.130), channel_id=1, source_target_pairs={{0,11},{1,10},{2,9},{3,8},{4,15},{5,14},{6,13},{7,12},{8,3},{9,2},... | collective-permute-start | bytes 196616 | tf_op jit(solution)/shard_map/ppermute | solution.py:421
  48.6 4.1 %collective-permute-start.16 = (bf16[264,128]{1,0:T(8,128)(2,1)S(1)}, bf16[264,128]{1,0:T(8,128)(2,1)S(1)}, u32[]{:S(2)}, u32[]{:S(2)}) collective-permute-start(bf16[264,128]{1,0:T(8,128)(2,1)S(1)} %get-tuple-element.124), channel_id=1, source_target_pairs={{0,4},{1,5},{2,6},{3,7},{4,0},{5,1},{6,2},{7,3},{8,12},{9,13},{10,... | collective-permute-start | bytes 202760 | tf_op jit(solution)/shard_map/ppermute | solution.py:421
  53.0 3.6 %collective-permute-start.17 = (bf16[264,128]{1,0:T(8,128)(2,1)S(1)}, bf16[264,128]{1,0:T(8,128)(2,1)S(1)}, u32[]{:S(2)}, u32[]{:S(2)}) collective-permute-start(bf16[264,128]{1,0:T(8,128)(2,1)S(1)} %get-tuple-element.125), channel_id=1, source_target_pairs={{0,12},{1,13},{2,14},{3,15},{4,8},{5,9},{6,10},{7,11},{8,4},{9,5},... | collective-permute-start | bytes 202760 | tf_op jit(solution)/shard_map/ppermute | solution.py:421
  56.6 1.2 collective-permute-start.27
  57.8 3.1 %collective-permute-done.23.refs_9_ = bf16[256,128]{1,0:T(8,128)(2,1)S(1)} collective-permute-done((bf16[256,128]{1,0:T(8,128)(2,1)S(1)}, bf16[256,128]{1,0:T(8,128)(2,1)S(1)}, u32[]{:S(2)}, u32[]{:S(2)}) %collective-permute-start.23) | collective-permute-done | bytes 65568 | tf_op jit(solution)/shard_map/ppermute | solution.py:421
  60.9 1.3 collective-permute-done.27.refs_14_
  62.2 2.6 %collective-permute-start.29 = (bf16[256,128]{1,0:T(8,128)(2,1)S(1)}, bf16[256,128]{1,0:T(8,128)(2,1)S(1)}, u32[]{:S(2)}, u32[]{:S(2)}) collective-permute-start(bf16[256,128]{1,0:T(8,128)(2,1)S(1)} %get-tuple-element.135), channel_id=1, source_target_pairs={{0,14},{1,15},{2,12},{3,13},{4,10},{5,11},{6,8},{7,9},{8,6},{9,7},... | collective-permute-start | bytes 196616 | tf_op jit(solution)/shard_map/ppermute | solution.py:421
  65.5 2.1 %collective-permute-start.31 = (bf16[256,128]{1,0:T(8,128)(2,1)S(1)}, bf16[256,128]{1,0:T(8,128)(2,1)S(1)}, u32[]{:S(2)}, u32[]{:S(2)}) collective-permute-start(bf16[256,128]{1,0:T(8,128)(2,1)S(1)} %get-tuple-element.137), channel_id=1, source_target_pairs={{0,15},{1,14},{2,13},{3,12},{4,11},{5,10},{6,9},{7,8},{8,7},{9,6},... | collective-permute-start | bytes 196616 | tf_op jit(solution)/shard_map/ppermute | solution.py:421
  68.7 1.7 collective-permute-start.26
  71.2 1.6 collective-permute-done.31.refs_18_
  74.0 3.5 %pairs.1 = (bf16[256,128]{1,0:T(8,128)(2,1)S(1)}, bf16[264,128]{1,0:T(8,128)(2,1)S(1)}, bf16[264,128]{1,0:T(8,128)(2,1)S(1)}, bf16[264,128]{1,0:T(8,128)(2,1)S(1...) custom-call(s32[128]{0:T(128)S(1)} %get-tuple-element.121.target_ref, ...), custom_call_target="tpu_custom_call" | custom-call | flops 536870912 | bytes 8388608 | tf_op jit(solution)/shard_map/pairs/pallas_call | solution.py:461
  79.1 2.3 %collective-permute-start.38 = (bf16[256,128]{1,0:T(8,128)(2,1)S(1)}, bf16[256,128]{1,0:T(8,128)(2,1)S(1)}, u32[]{:S(2)}, u32[]{:S(2)}) collective-permute-start(bf16[256,128]{1,0:T(8,128)(2,1)S(1)} %get-tuple-element.147), channel_id=1, source_target_pairs={{0,10},{1,11},{2,8},{3,9},{4,14},{5,15},{6,12},{7,13},{8,2},{9,3},... | collective-permute-start | bytes 196616 | tf_op jit(solution)/shard_map/ppermute | solution.py:421
  82.1 1.3 collective-permute-start.40
  83.4 2.3 %collective-permute-done.36.refs_4_ = bf16[256,128]{1,0:T(8,128)(2,1)S(1)} collective-permute-done((bf16[256,128]{1,0:T(8,128)(2,1)S(1)}, bf16[256,128]{1,0:T(8,128)(2,1)S(1)}, u32[]{:S(2)}, u32[]{:S(2)}) %collective-permute-start.36) | collective-permute-done | bytes 65568 | tf_op jit(solution)/shard_map/ppermute | solution.py:421
  86.3 2.5 %collective-permute-done.38.refs_6_ = bf16[256,128]{1,0:T(8,128)(2,1)S(1)} collective-permute-done((bf16[256,128]{1,0:T(8,128)(2,1)S(1)}, bf16[256,128]{1,0:T(8,128)(2,1)S(1)}, u32[]{:S(2)}, u32[]{:S(2)}) %collective-permute-start.38) | collective-permute-done | bytes 65568 | tf_op jit(solution)/shard_map/ppermute | solution.py:421
  88.8 3.8 %collective-permute-start.35 = (bf16[264,128]{1,0:T(8,128)(2,1)S(1)}, bf16[264,128]{1,0:T(8,128)(2,1)S(1)}, u32[]{:S(2)}, u32[]{:S(2)}) collective-permute-start(bf16[264,128]{1,0:T(8,128)(2,1)S(1)} %get-tuple-element.144), channel_id=1, source_target_pairs={{0,12},{1,13},{2,14},{3,15},{4,8},{5,9},{6,10},{7,11},{8,4},{9,5},... | collective-permute-start | bytes 202760 | tf_op jit(solution)/shard_map/ppermute | solution.py:421
  92.5 2.5 %collective-permute-start.45 = (bf16[256,128]{1,0:T(8,128)(2,1)S(1)}, bf16[256,128]{1,0:T(8,128)(2,1)S(1)}, u32[]{:S(2)}, u32[]{:S(2)}) collective-permute-start(bf16[256,128]{1,0:T(8,128)(2,1)S(1)} %get-tuple-element.152), channel_id=1, source_target_pairs={{0,13},{1,12},{2,15},{3,14},{4,9},{5,8},{6,11},{7,10},{8,5},{9,4},... | collective-permute-start | bytes 196616 | tf_op jit(solution)/shard_map/ppermute | solution.py:421
  96.2 2.3 %collective-permute-done.45.refs_14_ = bf16[256,128]{1,0:T(8,128)(2,1)S(1)} collective-permute-done((bf16[256,128]{1,0:T(8,128)(2,1)S(1)}, bf16[256,128]{1,0:T(8,128)(2,1)S(1)}, u32[]{:S(2)}, u32[]{:S(2)}) %collective-permute-start.45) | collective-permute-done | bytes 65568 | tf_op jit(solution)/shard_map/ppermute | solution.py:421
  98.6 2.5 %collective-permute-start.47 = (bf16[256,128]{1,0:T(8,128)(2,1)S(1)}, bf16[256,128]{1,0:T(8,128)(2,1)S(1)}, u32[]{:S(2)}, u32[]{:S(2)}) collective-permute-start(bf16[256,128]{1,0:T(8,128)(2,1)S(1)} %get-tuple-element.154), channel_id=1, source_target_pairs={{0,14},{1,15},{2,12},{3,13},{4,10},{5,11},{6,8},{7,9},{8,6},{9,7},... | collective-permute-start | bytes 196616 | tf_op jit(solution)/shard_map/ppermute | solution.py:421
  101.1 1.3 collective-permute-start.49
  102.4 2.7 %collective-permute-start.50 = (bf16[256,128]{1,0:T(8,128)(2,1)S(1)}, bf16[256,128]{1,0:T(8,128)(2,1)S(1)}, u32[]{:S(2)}, u32[]{:S(2)}) collective-permute-start(bf16[256,128]{1,0:T(8,128)(2,1)S(1)} %get-tuple-element.157), channel_id=1, source_target_pairs={{0,7},{1,6},{2,5},{3,4},{4,3},{5,2},{6,1},{7,0},{8,15},{9,14},{10,... | collective-permute-start | bytes 196616 | tf_op jit(solution)/shard_map/ppermute | solution.py:421
  109.5 2.4 %cells.1 = (f32[64,8192]{1,0:T(8,128)S(1)}, f32[64,128]{1,0:T(8,128)S(1)}, f32[8,128]{1,0:T(8,128)S(1)}, bf16[256,128]{1,0:T(8,128)(2,1)S(1)}, bf16[264,128]{1,0...) custom-call(s32[16,128]{1,0:T(8,128)S(1)} %get-tuple-element.120.ask, ...), custom_call_target="tpu_custom_call" | custom-call | bytes 8388608 | tf_op jit(solution)/shard_map/cells/pallas_call | solution.py:470
  113.5 2.1 %collective-permute-start.56 = (bf16[256,128]{1,0:T(8,128)(2,1)S(1)}, bf16[256,128]{1,0:T(8,128)(2,1)S(1)}, u32[]{:S(2)}, u32[]{:S(2)}) collective-permute-start(bf16[256,128]{1,0:T(8,128)(2,1)S(1)} %get-tuple-element.166), channel_id=1, source_target_pairs={{0,10},{1,11},{2,8},{3,9},{4,14},{5,15},{6,12},{7,13},{8,2},{9,3},... | collective-permute-start | bytes 196616 | tf_op jit(solution)/shard_map/ppermute | solution.py:421
  116.4 1.4 collective-permute-start.58
  117.8 1.4 collective-permute-start.51
  119.2 3.3 %collective-permute-start.52 = (bf16[264,128]{1,0:T(8,128)(2,1)S(1)}, bf16[264,128]{1,0:T(8,128)(2,1)S(1)}, u32[]{:S(2)}, u32[]{:S(2)}) collective-permute-start(bf16[264,128]{1,0:T(8,128)(2,1)S(1)} %get-tuple-element.162), channel_id=1, source_target_pairs={{0,4},{1,5},{2,6},{3,7},{4,0},{5,1},{6,2},{7,3},{8,12},{9,13},{10,... | collective-permute-start | bytes 202760 | tf_op jit(solution)/shard_map/ppermute | solution.py:421
  122.5 2.8 %collective-permute-done.56.refs_6_ = bf16[256,128]{1,0:T(8,128)(2,1)S(1)} collective-permute-done((bf16[256,128]{1,0:T(8,128)(2,1)S(1)}, bf16[256,128]{1,0:T(8,128)(2,1)S(1)}, u32[]{:S(2)}, u32[]{:S(2)}) %collective-permute-start.56) | collective-permute-done | bytes 65568 | tf_op jit(solution)/shard_map/ppermute | solution.py:421
  125.3 1.7 collective-permute-start.53
  128.0 3.2 %collective-permute-done.59.refs_9_ = bf16[256,128]{1,0:T(8,128)(2,1)S(1)} collective-permute-done((bf16[256,128]{1,0:T(8,128)(2,1)S(1)}, bf16[256,128]{1,0:T(8,128)(2,1)S(1)}, u32[]{:S(2)}, u32[]{:S(2)}) %collective-permute-start.59) | collective-permute-done | bytes 65568 | tf_op jit(solution)/shard_map/ppermute | solution.py:421
  131.3 1.3 collective-permute-done.63.refs_14_
  132.6 1.6 collective-permute-start.65
  134.2 3.7 %collective-permute-start.67 = (bf16[256,128]{1,0:T(8,128)(2,1)S(1)}, bf16[256,128]{1,0:T(8,128)(2,1)S(1)}, u32[]{:S(2)}, u32[]{:S(2)}) collective-permute-start(bf16[256,128]{1,0:T(8,128)(2,1)S(1)} %get-tuple-element.175), channel_id=1, source_target_pairs={{0,15},{1,14},{2,13},{3,12},{4,11},{5,10},{6,9},{7,8},{8,7},{9,6},... | collective-permute-start | bytes 196616 | tf_op jit(solution)/shard_map/ppermute | solution.py:421
  139.1 1.6 collective-permute-start.62
  142.6 1.9 collective-permute-done.68.refs_19_
  144.5 3.5 %pairs_last.1 = (bf16[256,128]{1,0:T(8,128)(2,1)S(1)}, bf16[264,128]{1,0:T(8,128)(2,1)S(1)}, bf16[264,128]{1,0:T(8,128)(2,1)S(1)}, bf16[264,128]{1,0:T(8,128)(2,...) custom-call(s32[128]{0:T(128)S(1)} %get-tuple-element.121.target_ref, ...), custom_call_target="tpu_custom_call" | custom-call | flops 536870912 | bytes 8388608 | tf_op jit(solution)/shard_map/pairs_last/pallas_call | solution.py:461
  149.7 2.1 %collective-permute-start.74 = (bf16[256,128]{1,0:T(8,128)(2,1)S(1)}, bf16[256,128]{1,0:T(8,128)(2,1)S(1)}, u32[]{:S(2)}, u32[]{:S(2)}) collective-permute-start(bf16[256,128]{1,0:T(8,128)(2,1)S(1)} %get-tuple-element.186), channel_id=1, source_target_pairs={{0,10},{1,11},{2,8},{3,9},{4,14},{5,15},{6,12},{7,13},{8,2},{9,3},... | collective-permute-start | bytes 196616 | tf_op jit(solution)/shard_map/ppermute | solution.py:421
  153.8 2.2 %collective-permute-done.72.refs_4_ = bf16[256,128]{1,0:T(8,128)(2,1)S(1)} collective-permute-done((bf16[256,128]{1,0:T(8,128)(2,1)S(1)}, bf16[256,128]{1,0:T(8,128)(2,1)S(1)}, u32[]{:S(2)}, u32[]{:S(2)}) %collective-permute-start.72) | collective-permute-done | bytes 65568 | tf_op jit(solution)/shard_map/ppermute | solution.py:421
  156.0 1.7 collective-permute-start.70
  157.6 3.2 %collective-permute-done.74.refs_6_ = bf16[256,128]{1,0:T(8,128)(2,1)S(1)} collective-permute-done((bf16[256,128]{1,0:T(8,128)(2,1)S(1)}, bf16[256,128]{1,0:T(8,128)(2,1)S(1)}, u32[]{:S(2)}, u32[]{:S(2)}) %collective-permute-start.74) | collective-permute-done | bytes 65568 | tf_op jit(solution)/shard_map/ppermute | solution.py:421
  162.3 3.0 %collective-permute-start.81 = (bf16[256,128]{1,0:T(8,128)(2,1)S(1)}, bf16[256,128]{1,0:T(8,128)(2,1)S(1)}, u32[]{:S(2)}, u32[]{:S(2)}) collective-permute-start(bf16[256,128]{1,0:T(8,128)(2,1)S(1)} %get-tuple-element.191), channel_id=1, source_target_pairs={{0,13},{1,12},{2,15},{3,14},{4,9},{5,8},{6,11},{7,10},{8,5},{9,4},... | collective-permute-start | bytes 196616 | tf_op jit(solution)/shard_map/ppermute | solution.py:421
  165.4 2.5 %collective-permute-done.81.refs_14_ = bf16[256,128]{1,0:T(8,128)(2,1)S(1)} collective-permute-done((bf16[256,128]{1,0:T(8,128)(2,1)S(1)}, bf16[256,128]{1,0:T(8,128)(2,1)S(1)}, u32[]{:S(2)}, u32[]{:S(2)}) %collective-permute-start.81) | collective-permute-done | bytes 65568 | tf_op jit(solution)/shard_map/ppermute | solution.py:421
  167.9 2.8 %collective-permute-start.83 = (bf16[256,128]{1,0:T(8,128)(2,1)S(1)}, bf16[256,128]{1,0:T(8,128)(2,1)S(1)}, u32[]{:S(2)}, u32[]{:S(2)}) collective-permute-start(bf16[256,128]{1,0:T(8,128)(2,1)S(1)} %get-tuple-element.193), channel_id=1, source_target_pairs={{0,14},{1,15},{2,12},{3,13},{4,10},{5,11},{6,8},{7,9},{8,6},{9,7},... | collective-permute-start | bytes 196616 | tf_op jit(solution)/shard_map/ppermute | solution.py:421
  170.7 3.5 %collective-permute-start.85 = (bf16[256,128]{1,0:T(8,128)(2,1)S(1)}, bf16[256,128]{1,0:T(8,128)(2,1)S(1)}, u32[]{:S(2)}, u32[]{:S(2)}) collective-permute-start(bf16[256,128]{1,0:T(8,128)(2,1)S(1)} %get-tuple-element.195), channel_id=1, source_target_pairs={{0,15},{1,14},{2,13},{3,12},{4,11},{5,10},{6,9},{7,8},{8,7},{9,6},... | collective-permute-start | bytes 196616 | tf_op jit(solution)/shard_map/ppermute | solution.py:421
  175.5 2.2 %collective-permute-start.79 = (f32[8,128]{1,0:T(8,128)S(1)}, f32[8,128]{1,0:T(8,128)S(1)}, u32[]{:S(2)}, u32[]{:S(2)}) collective-permute-start(f32[8,128]{1,0:T(8,128)S(1)} %convert_add_fusion.refs_10_), channel_id=1, source_target_pairs={{0,2},{1,3},{2,0},{3,1},{4,6},{5,7},{6,4},{7,5},{8,10},{9,11},{10,... | collective-permute-start | bytes 12296 | tf_op jit(solution)/shard_map/ppermute | solution.py:421
  178.7 1.4 collective-permute-done.86.refs_19_
  180.2 2.0 %cells_last.1 = (f32[64,8192]{1,0:T(8,128)S(1)}, f32[64,128]{1,0:T(8,128)S(1)}, f32[8,128]{1,0:T(8,128)S(1)}) custom-call(s32[16,128]{1,0:T(8,128)S(1)} %get-tuple-element.120.asked_ref, bf16[256,128]{1,0:T(8,128)(2,1)S(1)} %get-tuple-element.180.refs_0_, bf16[264,128]{1,0:T(8,128)(2,1)S(1)} %collective-permute-done.69.refs_1_, ...), custom_call_target="tpu_custom_call" | custom-call | bytes 8388608 | tf_op jit(solution)/shard_map/cells_last/pallas_call | solution.py:470
  182.2 2.2 %collective-permute-start.89 = (f32[8,128]{1,0:T(8,128)S(1)}, f32[8,128]{1,0:T(8,128)S(1)}, u32[]{:S(2)}, u32[]{:S(2)}) collective-permute-start(f32[8,128]{1,0:T(8,128)S(1)} %get-tuple-element.198), channel_id=1, source_target_pairs={{0,12},{1,13},{2,14},{3,15},{4,8},{5,9},{6,10},{7,11},{8,4},{9,5},... | collective-permute-start | bytes 12296 | tf_op jit(solution)/shard_map/ppermute | solution.py:421
  185.1 1.5 collective-permute-start.87
  187.7 1.2 collective-permute-done.88
  190.8 1.5 estimate.1
  192.6 1.5 model.1
  (142 shorter events, 38.4 us)
Async XLA Ops:
  6.1 7.7 %collective-permute-start = (bf16[264,128]{1,0:T(8,128)(2,1)}, bf16[264,128]{1,0:T(8,128)(2,1)S(1)}, u32[]{:S(2)}, u32[]{:S(2)}) collective-permute-start(bf16[264,128]{1,0:T(8,128)(2,1)} %get-tuple-element.104), channel_id=1, source_target_pairs={{0,8},{1,9},{2,10},{3,11},{4,12},{5,13},{6,14},{7,15},{8,0},{9,1},... | collective-permute-start | bytes 202760 | tf_op jit(solution)/shard_map/ppermute | solution.py:421
  10.2 6.8 %collective-permute-start.1 = (bf16[264,128]{1,0:T(8,128)(2,1)}, bf16[264,128]{1,0:T(8,128)(2,1)S(1)}, u32[]{:S(2)}, u32[]{:S(2)}) collective-permute-start(bf16[264,128]{1,0:T(8,128)(2,1)} %get-tuple-element.105), channel_id=1, source_target_pairs={{0,4},{1,5},{2,6},{3,7},{4,0},{5,1},{6,2},{7,3},{8,12},{9,13},{10,... | collective-permute-start | bytes 202760 | tf_op jit(solution)/shard_map/ppermute | solution.py:421
  11.7 6.3 %collective-permute-start.2 = (bf16[264,128]{1,0:T(8,128)(2,1)}, bf16[264,128]{1,0:T(8,128)(2,1)S(1)}, u32[]{:S(2)}, u32[]{:S(2)}) collective-permute-start(bf16[264,128]{1,0:T(8,128)(2,1)} %get-tuple-element.106), channel_id=1, source_target_pairs={{0,12},{1,13},{2,14},{3,15},{4,8},{5,9},{6,10},{7,11},{8,4},{9,5},... | collective-permute-start | bytes 202760 | tf_op jit(solution)/shard_map/ppermute | solution.py:421
  11.7 10.9 %collective-permute-start.3 = (bf16[264,128]{1,0:T(8,128)(2,1)}, bf16[264,128]{1,0:T(8,128)(2,1)S(1)}, u32[]{:S(2)}, u32[]{:S(2)}) collective-permute-start(bf16[264,128]{1,0:T(8,128)(2,1)} %get-tuple-element.107), channel_id=1, source_target_pairs={{0,9},{1,8},{2,11},{3,10},{4,13},{5,12},{6,15},{7,14},{8,1},{9,0},... | collective-permute-start | bytes 202760 | tf_op jit(solution)/shard_map/ppermute | solution.py:421
  12.2 11.8 %collective-permute-start.4 = (bf16[264,128]{1,0:T(8,128)(2,1)}, bf16[264,128]{1,0:T(8,128)(2,1)S(1)}, u32[]{:S(2)}, u32[]{:S(2)}) collective-permute-start(bf16[264,128]{1,0:T(8,128)(2,1)} %get-tuple-element.108), channel_id=1, source_target_pairs={{0,1},{1,0},{2,3},{3,2},{4,5},{5,4},{6,7},{7,6},{8,9},{9,8},{10,11... | collective-permute-start | bytes 202760 | tf_op jit(solution)/shard_map/ppermute | solution.py:421
  13.8 12.9 %collective-permute-start.5 = (bf16[264,128]{1,0:T(8,128)(2,1)}, bf16[264,128]{1,0:T(8,128)(2,1)S(1)}, u32[]{:S(2)}, u32[]{:S(2)}) collective-permute-start(bf16[264,128]{1,0:T(8,128)(2,1)} %get-tuple-element.109), channel_id=1, source_target_pairs={{0,10},{1,11},{2,8},{3,9},{4,14},{5,15},{6,12},{7,13},{8,2},{9,3},... | collective-permute-start | bytes 202760 | tf_op jit(solution)/shard_map/ppermute | solution.py:421
  17.0 9.6 %collective-permute-start.6 = (bf16[264,128]{1,0:T(8,128)(2,1)}, bf16[264,128]{1,0:T(8,128)(2,1)S(1)}, u32[]{:S(2)}, u32[]{:S(2)}) collective-permute-start(bf16[264,128]{1,0:T(8,128)(2,1)} %get-tuple-element.110), channel_id=1, source_target_pairs={{0,2},{1,3},{2,0},{3,1},{4,6},{5,7},{6,4},{7,5},{8,10},{9,11},{10,... | collective-permute-start | bytes 202760 | tf_op jit(solution)/shard_map/ppermute | solution.py:421
  18.0 13.0 %collective-permute-start.7 = (bf16[264,128]{1,0:T(8,128)(2,1)}, bf16[264,128]{1,0:T(8,128)(2,1)S(1)}, u32[]{:S(2)}, u32[]{:S(2)}) collective-permute-start(bf16[264,128]{1,0:T(8,128)(2,1)} %get-tuple-element.111), channel_id=1, source_target_pairs={{0,11},{1,10},{2,9},{3,8},{4,15},{5,14},{6,13},{7,12},{8,3},{9,2},... | collective-permute-start | bytes 202760 | tf_op jit(solution)/shard_map/ppermute | solution.py:421
  22.6 8.4 %collective-permute-start.8 = (bf16[264,128]{1,0:T(8,128)(2,1)}, bf16[264,128]{1,0:T(8,128)(2,1)S(1)}, u32[]{:S(2)}, u32[]{:S(2)}) collective-permute-start(bf16[264,128]{1,0:T(8,128)(2,1)} %get-tuple-element.112), channel_id=1, source_target_pairs={{0,3},{1,2},{2,1},{3,0},{4,7},{5,6},{6,5},{7,4},{8,11},{9,10},{10,... | collective-permute-start | bytes 202760 | tf_op jit(solution)/shard_map/ppermute | solution.py:421
  24.0 8.1 %collective-permute-start.9 = (bf16[264,128]{1,0:T(8,128)(2,1)}, bf16[264,128]{1,0:T(8,128)(2,1)S(1)}, u32[]{:S(2)}, u32[]{:S(2)}) collective-permute-start(bf16[264,128]{1,0:T(8,128)(2,1)} %get-tuple-element.113), channel_id=1, source_target_pairs={{0,13},{1,12},{2,15},{3,14},{4,9},{5,8},{6,11},{7,10},{8,5},{9,4},... | collective-permute-start | bytes 202760 | tf_op jit(solution)/shard_map/ppermute | solution.py:421
  26.7 10.9 %collective-permute-start.10 = (bf16[264,128]{1,0:T(8,128)(2,1)}, bf16[264,128]{1,0:T(8,128)(2,1)S(1)}, u32[]{:S(2)}, u32[]{:S(2)}) collective-permute-start(bf16[264,128]{1,0:T(8,128)(2,1)} %get-tuple-element.114), channel_id=1, source_target_pairs={{0,5},{1,4},{2,7},{3,6},{4,1},{5,0},{6,3},{7,2},{8,13},{9,12},{10,... | collective-permute-start | bytes 202760 | tf_op jit(solution)/shard_map/ppermute | solution.py:421
  26.7 10.9 %collective-permute-start.11 = (bf16[264,128]{1,0:T(8,128)(2,1)}, bf16[264,128]{1,0:T(8,128)(2,1)S(1)}, u32[]{:S(2)}, u32[]{:S(2)}) collective-permute-start(bf16[264,128]{1,0:T(8,128)(2,1)} %get-tuple-element.115), channel_id=1, source_target_pairs={{0,14},{1,15},{2,12},{3,13},{4,10},{5,11},{6,8},{7,9},{8,6},{9,7},... | collective-permute-start | bytes 202760 | tf_op jit(solution)/shard_map/ppermute | solution.py:421
  31.0 6.6 %collective-permute-start.12 = (bf16[264,128]{1,0:T(8,128)(2,1)}, bf16[264,128]{1,0:T(8,128)(2,1)S(1)}, u32[]{:S(2)}, u32[]{:S(2)}) collective-permute-start(bf16[264,128]{1,0:T(8,128)(2,1)} %get-tuple-element.116), channel_id=1, source_target_pairs={{0,6},{1,7},{2,4},{3,5},{4,2},{5,3},{6,0},{7,1},{8,14},{9,15},{10,... | collective-permute-start | bytes 202760 | tf_op jit(solution)/shard_map/ppermute | solution.py:421
  31.1 7.2 %collective-permute-start.13 = (bf16[264,128]{1,0:T(8,128)(2,1)}, bf16[264,128]{1,0:T(8,128)(2,1)S(1)}, u32[]{:S(2)}, u32[]{:S(2)}) collective-permute-start(bf16[264,128]{1,0:T(8,128)(2,1)} %get-tuple-element.117), channel_id=1, source_target_pairs={{0,15},{1,14},{2,13},{3,12},{4,11},{5,10},{6,9},{7,8},{8,7},{9,6},... | collective-permute-start | bytes 202760 | tf_op jit(solution)/shard_map/ppermute | solution.py:421
  32.2 6.3 %collective-permute-start.14 = (bf16[264,128]{1,0:T(8,128)(2,1)}, bf16[264,128]{1,0:T(8,128)(2,1)S(1)}, u32[]{:S(2)}, u32[]{:S(2)}) collective-permute-start(bf16[264,128]{1,0:T(8,128)(2,1)} %get-tuple-element.118), channel_id=1, source_target_pairs={{0,7},{1,6},{2,5},{3,4},{4,3},{5,2},{6,1},{7,0},{8,15},{9,14},{10,... | collective-permute-start | bytes 202760 | tf_op jit(solution)/shard_map/ppermute | solution.py:421
  40.9 7.3 %collective-permute-start.18 = (bf16[256,128]{1,0:T(8,128)(2,1)S(1)}, bf16[256,128]{1,0:T(8,128)(2,1)S(1)}, u32[]{:S(2)}, u32[]{:S(2)}) collective-permute-start(bf16[256,128]{1,0:T(8,128)(2,1)S(1)} %get-tuple-element.126), channel_id=1, source_target_pairs={{0,9},{1,8},{2,11},{3,10},{4,13},{5,12},{6,15},{7,14},{8,1},{9,0},... | collective-permute-start | bytes 196616 | tf_op jit(solution)/shard_map/ppermute | solution.py:421
  43.3 9.7 %collective-permute-start.20 = (bf16[256,128]{1,0:T(8,128)(2,1)S(1)}, bf16[256,128]{1,0:T(8,128)(2,1)S(1)}, u32[]{:S(2)}, u32[]{:S(2)}) collective-permute-start(bf16[256,128]{1,0:T(8,128)(2,1)S(1)} %get-tuple-element.128), channel_id=1, source_target_pairs={{0,10},{1,11},{2,8},{3,9},{4,14},{5,15},{6,12},{7,13},{8,2},{9,3},... | collective-permute-start | bytes 196616 | tf_op jit(solution)/shard_map/ppermute | solution.py:421
  44.7 11.9 %collective-permute-start.21 = (bf16[256,128]{1,0:T(8,128)(2,1)S(1)}, bf16[256,128]{1,0:T(8,128)(2,1)S(1)}, u32[]{:S(2)}, u32[]{:S(2)}) collective-permute-start(bf16[256,128]{1,0:T(8,128)(2,1)S(1)} %get-tuple-element.129), channel_id=1, source_target_pairs={{0,2},{1,3},{2,0},{3,1},{4,6},{5,7},{6,4},{7,5},{8,10},{9,11},{10,... | collective-permute-start | bytes 196616 | tf_op jit(solution)/shard_map/ppermute | solution.py:421
  45.7 10.9 %collective-permute-start.22 = (bf16[256,128]{1,0:T(8,128)(2,1)S(1)}, bf16[256,128]{1,0:T(8,128)(2,1)S(1)}, u32[]{:S(2)}, u32[]{:S(2)}) collective-permute-start(bf16[256,128]{1,0:T(8,128)(2,1)S(1)} %get-tuple-element.130), channel_id=1, source_target_pairs={{0,11},{1,10},{2,9},{3,8},{4,15},{5,14},{6,13},{7,12},{8,3},{9,2},... | collective-permute-start | bytes 196616 | tf_op jit(solution)/shard_map/ppermute | solution.py:421
  48.2 16.5 %collective-permute-start.15 = (bf16[264,128]{1,0:T(8,128)(2,1)S(1)}, bf16[264,128]{1,0:T(8,128)(2,1)S(1)}, u32[]{:S(2)}, u32[]{:S(2)}) collective-permute-start(bf16[264,128]{1,0:T(8,128)(2,1)S(1)} %get-tuple-element.123), channel_id=1, source_target_pairs={{0,8},{1,9},{2,10},{3,11},{4,12},{5,13},{6,14},{7,15},{8,0},{9,1},... | collective-permute-start | bytes 202760 | tf_op jit(solution)/shard_map/ppermute | solution.py:421
  48.6 16.9 %collective-permute-start.16 = (bf16[264,128]{1,0:T(8,128)(2,1)S(1)}, bf16[264,128]{1,0:T(8,128)(2,1)S(1)}, u32[]{:S(2)}, u32[]{:S(2)}) collective-permute-start(bf16[264,128]{1,0:T(8,128)(2,1)S(1)} %get-tuple-element.124), channel_id=1, source_target_pairs={{0,4},{1,5},{2,6},{3,7},{4,0},{5,1},{6,2},{7,3},{8,12},{9,13},{10,... | collective-permute-start | bytes 202760 | tf_op jit(solution)/shard_map/ppermute | solution.py:421
  53.0 14.6 %collective-permute-start.17 = (bf16[264,128]{1,0:T(8,128)(2,1)S(1)}, bf16[264,128]{1,0:T(8,128)(2,1)S(1)}, u32[]{:S(2)}, u32[]{:S(2)}) collective-permute-start(bf16[264,128]{1,0:T(8,128)(2,1)S(1)} %get-tuple-element.125), channel_id=1, source_target_pairs={{0,12},{1,13},{2,14},{3,15},{4,8},{5,9},{6,10},{7,11},{8,4},{9,5},... | collective-permute-start | bytes 202760 | tf_op jit(solution)/shard_map/ppermute | solution.py:421
  60.9 7.8 %collective-permute-start.28 = (bf16[256,128]{1,0:T(8,128)(2,1)S(1)}, bf16[256,128]{1,0:T(8,128)(2,1)S(1)}, u32[]{:S(2)}, u32[]{:S(2)}) collective-permute-start(bf16[256,128]{1,0:T(8,128)(2,1)S(1)} %get-tuple-element.134), channel_id=1, source_target_pairs={{0,5},{1,4},{2,7},{3,6},{4,1},{5,0},{6,3},{7,2},{8,13},{9,12},{10,... | collective-permute-start | bytes 196616 | tf_op jit(solution)/shard_map/ppermute | solution.py:421
  62.2 8.2 %collective-permute-start.29 = (bf16[256,128]{1,0:T(8,128)(2,1)S(1)}, bf16[256,128]{1,0:T(8,128)(2,1)S(1)}, u32[]{:S(2)}, u32[]{:S(2)}) collective-permute-start(bf16[256,128]{1,0:T(8,128)(2,1)S(1)} %get-tuple-element.135), channel_id=1, source_target_pairs={{0,14},{1,15},{2,12},{3,13},{4,10},{5,11},{6,8},{7,9},{8,6},{9,7},... | collective-permute-start | bytes 196616 | tf_op jit(solution)/shard_map/ppermute | solution.py:421
  64.7 6.4 %collective-permute-start.30 = (bf16[256,128]{1,0:T(8,128)(2,1)S(1)}, bf16[256,128]{1,0:T(8,128)(2,1)S(1)}, u32[]{:S(2)}, u32[]{:S(2)}) collective-permute-start(bf16[256,128]{1,0:T(8,128)(2,1)S(1)} %get-tuple-element.136), channel_id=1, source_target_pairs={{0,6},{1,7},{2,4},{3,5},{4,2},{5,3},{6,0},{7,1},{8,14},{9,15},{10,... | collective-permute-start | bytes 196616 | tf_op jit(solution)/shard_map/ppermute | solution.py:421
  65.5 7.3 %collective-permute-start.31 = (bf16[256,128]{1,0:T(8,128)(2,1)S(1)}, bf16[256,128]{1,0:T(8,128)(2,1)S(1)}, u32[]{:S(2)}, u32[]{:S(2)}) collective-permute-start(bf16[256,128]{1,0:T(8,128)(2,1)S(1)} %get-tuple-element.137), channel_id=1, source_target_pairs={{0,15},{1,14},{2,13},{3,12},{4,11},{5,10},{6,9},{7,8},{8,7},{9,6},... | collective-permute-start | bytes 196616 | tf_op jit(solution)/shard_map/ppermute | solution.py:421
  67.6 6.3 %collective-permute-start.32 = (bf16[256,128]{1,0:T(8,128)(2,1)S(1)}, bf16[256,128]{1,0:T(8,128)(2,1)S(1)}, u32[]{:S(2)}, u32[]{:S(2)}) collective-permute-start(bf16[256,128]{1,0:T(8,128)(2,1)S(1)} %get-tuple-element.138), channel_id=1, source_target_pairs={{0,7},{1,6},{2,5},{3,4},{4,3},{5,2},{6,1},{7,0},{8,15},{9,14},{10,... | collective-permute-start | bytes 196616 | tf_op jit(solution)/shard_map/ppermute | solution.py:421
  77.5 8.1 %collective-permute-start.36 = (bf16[256,128]{1,0:T(8,128)(2,1)S(1)}, bf16[256,128]{1,0:T(8,128)(2,1)S(1)}, u32[]{:S(2)}, u32[]{:S(2)}) collective-permute-start(bf16[256,128]{1,0:T(8,128)(2,1)S(1)} %get-tuple-element.145), channel_id=1, source_target_pairs={{0,9},{1,8},{2,11},{3,10},{4,13},{5,12},{6,15},{7,14},{8,1},{9,0},... | collective-permute-start | bytes 196616 | tf_op jit(solution)/shard_map/ppermute | solution.py:421
  78.7 7.0 %collective-permute-start.37 = (bf16[256,128]{1,0:T(8,128)(2,1)S(1)}, bf16[256,128]{1,0:T(8,128)(2,1)S(1)}, u32[]{:S(2)}, u32[]{:S(2)}) collective-permute-start(bf16[256,128]{1,0:T(8,128)(2,1)S(1)} %get-tuple-element.146), channel_id=1, source_target_pairs={{0,1},{1,0},{2,3},{3,2},{4,5},{5,4},{6,7},{7,6},{8,9},{9,8},{10,11... | collective-permute-start | bytes 196616 | tf_op jit(solution)/shard_map/ppermute | solution.py:421
  79.1 9.7 %collective-permute-start.38 = (bf16[256,128]{1,0:T(8,128)(2,1)S(1)}, bf16[256,128]{1,0:T(8,128)(2,1)S(1)}, u32[]{:S(2)}, u32[]{:S(2)}) collective-permute-start(bf16[256,128]{1,0:T(8,128)(2,1)S(1)} %get-tuple-element.147), channel_id=1, source_target_pairs={{0,10},{1,11},{2,8},{3,9},{4,14},{5,15},{6,12},{7,13},{8,2},{9,3},... | collective-permute-start | bytes 196616 | tf_op jit(solution)/shard_map/ppermute | solution.py:421
  81.4 11.1 %collective-permute-start.39 = (bf16[256,128]{1,0:T(8,128)(2,1)S(1)}, bf16[256,128]{1,0:T(8,128)(2,1)S(1)}, u32[]{:S(2)}, u32[]{:S(2)}) collective-permute-start(bf16[256,128]{1,0:T(8,128)(2,1)S(1)} %get-tuple-element.148), channel_id=1, source_target_pairs={{0,2},{1,3},{2,0},{3,1},{4,6},{5,7},{6,4},{7,5},{8,10},{9,11},{10,... | collective-permute-start | bytes 196616 | tf_op jit(solution)/shard_map/ppermute | solution.py:421
  82.1 10.4 %collective-permute-start.40 = (bf16[256,128]{1,0:T(8,128)(2,1)S(1)}, bf16[256,128]{1,0:T(8,128)(2,1)S(1)}, u32[]{:S(2)}, u32[]{:S(2)}) collective-permute-start(bf16[256,128]{1,0:T(8,128)(2,1)S(1)} %get-tuple-element.149), channel_id=1, source_target_pairs={{0,11},{1,10},{2,9},{3,8},{4,15},{5,14},{6,13},{7,12},{8,3},{9,2},... | collective-permute-start | bytes 196616 | tf_op jit(solution)/shard_map/ppermute | solution.py:421
  85.7 15.4 %collective-permute-start.33 = (bf16[264,128]{1,0:T(8,128)(2,1)S(1)}, bf16[264,128]{1,0:T(8,128)(2,1)S(1)}, u32[]{:S(2)}, u32[]{:S(2)}) collective-permute-start(bf16[264,128]{1,0:T(8,128)(2,1)S(1)} %get-tuple-element.142), channel_id=1, source_target_pairs={{0,8},{1,9},{2,10},{3,11},{4,12},{5,13},{6,14},{7,15},{8,0},{9,1},... | collective-permute-start | bytes 202760 | tf_op jit(solution)/shard_map/ppermute | solution.py:421
  85.7 15.4 %collective-permute-start.34 = (bf16[264,128]{1,0:T(8,128)(2,1)S(1)}, bf16[264,128]{1,0:T(8,128)(2,1)S(1)}, u32[]{:S(2)}, u32[]{:S(2)}) collective-permute-start(bf16[264,128]{1,0:T(8,128)(2,1)S(1)} %get-tuple-element.143), channel_id=1, source_target_pairs={{0,4},{1,5},{2,6},{3,7},{4,0},{5,1},{6,2},{7,3},{8,12},{9,13},{10,... | collective-permute-start | bytes 202760 | tf_op jit(solution)/shard_map/ppermute | solution.py:421
  88.8 13.6 %collective-permute-start.35 = (bf16[264,128]{1,0:T(8,128)(2,1)S(1)}, bf16[264,128]{1,0:T(8,128)(2,1)S(1)}, u32[]{:S(2)}, u32[]{:S(2)}) collective-permute-start(bf16[264,128]{1,0:T(8,128)(2,1)S(1)} %get-tuple-element.144), channel_id=1, source_target_pairs={{0,12},{1,13},{2,14},{3,15},{4,8},{5,9},{6,10},{7,11},{8,4},{9,5},... | collective-permute-start | bytes 202760 | tf_op jit(solution)/shard_map/ppermute | solution.py:421
  92.5 6.0 %collective-permute-start.45 = (bf16[256,128]{1,0:T(8,128)(2,1)S(1)}, bf16[256,128]{1,0:T(8,128)(2,1)S(1)}, u32[]{:S(2)}, u32[]{:S(2)}) collective-permute-start(bf16[256,128]{1,0:T(8,128)(2,1)S(1)} %get-tuple-element.152), channel_id=1, source_target_pairs={{0,13},{1,12},{2,15},{3,14},{4,9},{5,8},{6,11},{7,10},{8,5},{9,4},... | collective-permute-start | bytes 196616 | tf_op jit(solution)/shard_map/ppermute | solution.py:421
  96.2 8.8 %collective-permute-start.46 = (bf16[256,128]{1,0:T(8,128)(2,1)S(1)}, bf16[256,128]{1,0:T(8,128)(2,1)S(1)}, u32[]{:S(2)}, u32[]{:S(2)}) collective-permute-start(bf16[256,128]{1,0:T(8,128)(2,1)S(1)} %get-tuple-element.153), channel_id=1, source_target_pairs={{0,5},{1,4},{2,7},{3,6},{4,1},{5,0},{6,3},{7,2},{8,13},{9,12},{10,... | collective-permute-start | bytes 196616 | tf_op jit(solution)/shard_map/ppermute | solution.py:421
  98.6 7.2 %collective-permute-start.47 = (bf16[256,128]{1,0:T(8,128)(2,1)S(1)}, bf16[256,128]{1,0:T(8,128)(2,1)S(1)}, u32[]{:S(2)}, u32[]{:S(2)}) collective-permute-start(bf16[256,128]{1,0:T(8,128)(2,1)S(1)} %get-tuple-element.154), channel_id=1, source_target_pairs={{0,14},{1,15},{2,12},{3,13},{4,10},{5,11},{6,8},{7,9},{8,6},{9,7},... | collective-permute-start | bytes 196616 | tf_op jit(solution)/shard_map/ppermute | solution.py:421
  101.1 7.1 %collective-permute-start.49 = (bf16[256,128]{1,0:T(8,128)(2,1)S(1)}, bf16[256,128]{1,0:T(8,128)(2,1)S(1)}, u32[]{:S(2)}, u32[]{:S(2)}) collective-permute-start(bf16[256,128]{1,0:T(8,128)(2,1)S(1)} %get-tuple-element.156), channel_id=1, source_target_pairs={{0,15},{1,14},{2,13},{3,12},{4,11},{5,10},{6,9},{7,8},{8,7},{9,6},... | collective-permute-start | bytes 196616 | tf_op jit(solution)/shard_map/ppermute | solution.py:421
  102.4 6.7 %collective-permute-start.50 = (bf16[256,128]{1,0:T(8,128)(2,1)S(1)}, bf16[256,128]{1,0:T(8,128)(2,1)S(1)}, u32[]{:S(2)}, u32[]{:S(2)}) collective-permute-start(bf16[256,128]{1,0:T(8,128)(2,1)S(1)} %get-tuple-element.157), channel_id=1, source_target_pairs={{0,7},{1,6},{2,5},{3,4},{4,3},{5,2},{6,1},{7,0},{8,15},{9,14},{10,... | collective-permute-start | bytes 196616 | tf_op jit(solution)/shard_map/ppermute | solution.py:421
  112.4 6.8 %collective-permute-start.55 = (bf16[256,128]{1,0:T(8,128)(2,1)S(1)}, bf16[256,128]{1,0:T(8,128)(2,1)S(1)}, u32[]{:S(2)}, u32[]{:S(2)}) collective-permute-start(bf16[256,128]{1,0:T(8,128)(2,1)S(1)} %get-tuple-element.165), channel_id=1, source_target_pairs={{0,1},{1,0},{2,3},{3,2},{4,5},{5,4},{6,7},{7,6},{8,9},{9,8},{10,11... | collective-permute-start | bytes 196616 | tf_op jit(solution)/shard_map/ppermute | solution.py:421
  113.5 11.8 %collective-permute-start.56 = (bf16[256,128]{1,0:T(8,128)(2,1)S(1)}, bf16[256,128]{1,0:T(8,128)(2,1)S(1)}, u32[]{:S(2)}, u32[]{:S(2)}) collective-permute-start(bf16[256,128]{1,0:T(8,128)(2,1)S(1)} %get-tuple-element.166), channel_id=1, source_target_pairs={{0,10},{1,11},{2,8},{3,9},{4,14},{5,15},{6,12},{7,13},{8,2},{9,3},... | collective-permute-start | bytes 196616 | tf_op jit(solution)/shard_map/ppermute | solution.py:421
  115.6 11.4 %collective-permute-start.57 = (bf16[256,128]{1,0:T(8,128)(2,1)S(1)}, bf16[256,128]{1,0:T(8,128)(2,1)S(1)}, u32[]{:S(2)}, u32[]{:S(2)}) collective-permute-start(bf16[256,128]{1,0:T(8,128)(2,1)S(1)} %get-tuple-element.167), channel_id=1, source_target_pairs={{0,2},{1,3},{2,0},{3,1},{4,6},{5,7},{6,4},{7,5},{8,10},{9,11},{10,... | collective-permute-start | bytes 196616 | tf_op jit(solution)/shard_map/ppermute | solution.py:421
  116.4 10.7 %collective-permute-start.58 = (bf16[256,128]{1,0:T(8,128)(2,1)S(1)}, bf16[256,128]{1,0:T(8,128)(2,1)S(1)}, u32[]{:S(2)}, u32[]{:S(2)}) collective-permute-start(bf16[256,128]{1,0:T(8,128)(2,1)S(1)} %get-tuple-element.168), channel_id=1, source_target_pairs={{0,11},{1,10},{2,9},{3,8},{4,15},{5,14},{6,13},{7,12},{8,3},{9,2},... | collective-permute-start | bytes 196616 | tf_op jit(solution)/shard_map/ppermute | solution.py:421
  117.8 16.4 %collective-permute-start.51 = (bf16[264,128]{1,0:T(8,128)(2,1)S(1)}, bf16[264,128]{1,0:T(8,128)(2,1)S(1)}, u32[]{:S(2)}, u32[]{:S(2)}) collective-permute-start(bf16[264,128]{1,0:T(8,128)(2,1)S(1)} %get-tuple-element.161), channel_id=1, source_target_pairs={{0,8},{1,9},{2,10},{3,11},{4,12},{5,13},{6,14},{7,15},{8,0},{9,1},... | collective-permute-start | bytes 202760 | tf_op jit(solution)/shard_map/ppermute | solution.py:421
  119.2 15.1 %collective-permute-start.52 = (bf16[264,128]{1,0:T(8,128)(2,1)S(1)}, bf16[264,128]{1,0:T(8,128)(2,1)S(1)}, u32[]{:S(2)}, u32[]{:S(2)}) collective-permute-start(bf16[264,128]{1,0:T(8,128)(2,1)S(1)} %get-tuple-element.162), channel_id=1, source_target_pairs={{0,4},{1,5},{2,6},{3,7},{4,0},{5,1},{6,2},{7,3},{8,12},{9,13},{10,... | collective-permute-start | bytes 202760 | tf_op jit(solution)/shard_map/ppermute | solution.py:421
  125.3 12.6 %collective-permute-start.53 = (bf16[264,128]{1,0:T(8,128)(2,1)S(1)}, bf16[264,128]{1,0:T(8,128)(2,1)S(1)}, u32[]{:S(2)}, u32[]{:S(2)}) collective-permute-start(bf16[264,128]{1,0:T(8,128)(2,1)S(1)} %get-tuple-element.163), channel_id=1, source_target_pairs={{0,12},{1,13},{2,14},{3,15},{4,8},{5,9},{6,10},{7,11},{8,4},{9,5},... | collective-permute-start | bytes 202760 | tf_op jit(solution)/shard_map/ppermute | solution.py:421
  131.3 7.8 %collective-permute-start.64 = (bf16[256,128]{1,0:T(8,128)(2,1)S(1)}, bf16[256,128]{1,0:T(8,128)(2,1)S(1)}, u32[]{:S(2)}, u32[]{:S(2)}) collective-permute-start(bf16[256,128]{1,0:T(8,128)(2,1)S(1)} %get-tuple-element.172), channel_id=1, source_target_pairs={{0,5},{1,4},{2,7},{3,6},{4,1},{5,0},{6,3},{7,2},{8,13},{9,12},{10,... | collective-permute-start | bytes 196616 | tf_op jit(solution)/shard_map/ppermute | solution.py:421
  132.6 8.1 %collective-permute-start.65 = (bf16[256,128]{1,0:T(8,128)(2,1)S(1)}, bf16[256,128]{1,0:T(8,128)(2,1)S(1)}, u32[]{:S(2)}, u32[]{:S(2)}) collective-permute-start(bf16[256,128]{1,0:T(8,128)(2,1)S(1)} %get-tuple-element.173), channel_id=1, source_target_pairs={{0,14},{1,15},{2,12},{3,13},{4,10},{5,11},{6,8},{7,9},{8,6},{9,7},... | collective-permute-start | bytes 196616 | tf_op jit(solution)/shard_map/ppermute | solution.py:421
  134.2 7.2 %collective-permute-start.66 = (bf16[256,128]{1,0:T(8,128)(2,1)S(1)}, bf16[256,128]{1,0:T(8,128)(2,1)S(1)}, u32[]{:S(2)}, u32[]{:S(2)}) collective-permute-start(bf16[256,128]{1,0:T(8,128)(2,1)S(1)} %get-tuple-element.174), channel_id=1, source_target_pairs={{0,6},{1,7},{2,4},{3,5},{4,2},{5,3},{6,0},{7,1},{8,14},{9,15},{10,... | collective-permute-start | bytes 196616 | tf_op jit(solution)/shard_map/ppermute | solution.py:421
  134.2 8.4 %collective-permute-start.67 = (bf16[256,128]{1,0:T(8,128)(2,1)S(1)}, bf16[256,128]{1,0:T(8,128)(2,1)S(1)}, u32[]{:S(2)}, u32[]{:S(2)}) collective-permute-start(bf16[256,128]{1,0:T(8,128)(2,1)S(1)} %get-tuple-element.175), channel_id=1, source_target_pairs={{0,15},{1,14},{2,13},{3,12},{4,11},{5,10},{6,9},{7,8},{8,7},{9,6},... | collective-permute-start | bytes 196616 | tf_op jit(solution)/shard_map/ppermute | solution.py:421
  137.9 6.5 %collective-permute-start.68 = (bf16[256,128]{1,0:T(8,128)(2,1)S(1)}, bf16[256,128]{1,0:T(8,128)(2,1)S(1)}, u32[]{:S(2)}, u32[]{:S(2)}) collective-permute-start(bf16[256,128]{1,0:T(8,128)(2,1)S(1)} %get-tuple-element.176), channel_id=1, source_target_pairs={{0,7},{1,6},{2,5},{3,4},{4,3},{5,2},{6,1},{7,0},{8,15},{9,14},{10,... | collective-permute-start | bytes 196616 | tf_op jit(solution)/shard_map/ppermute | solution.py:421
  148.0 7.9 %collective-permute-start.72 = (bf16[256,128]{1,0:T(8,128)(2,1)S(1)}, bf16[256,128]{1,0:T(8,128)(2,1)S(1)}, u32[]{:S(2)}, u32[]{:S(2)}) collective-permute-start(bf16[256,128]{1,0:T(8,128)(2,1)S(1)} %get-tuple-element.184), channel_id=1, source_target_pairs={{0,9},{1,8},{2,11},{3,10},{4,13},{5,12},{6,15},{7,14},{8,1},{9,0},... | collective-permute-start | bytes 196616 | tf_op jit(solution)/shard_map/ppermute | solution.py:421
  148.8 7.2 %collective-permute-start.73 = (bf16[256,128]{1,0:T(8,128)(2,1)S(1)}, bf16[256,128]{1,0:T(8,128)(2,1)S(1)}, u32[]{:S(2)}, u32[]{:S(2)}) collective-permute-start(bf16[256,128]{1,0:T(8,128)(2,1)S(1)} %get-tuple-element.185), channel_id=1, source_target_pairs={{0,1},{1,0},{2,3},{3,2},{4,5},{5,4},{6,7},{7,6},{8,9},{9,8},{10,11... | collective-permute-start | bytes 196616 | tf_op jit(solution)/shard_map/ppermute | solution.py:421
  149.7 11.2 %collective-permute-start.74 = (bf16[256,128]{1,0:T(8,128)(2,1)S(1)}, bf16[256,128]{1,0:T(8,128)(2,1)S(1)}, u32[]{:S(2)}, u32[]{:S(2)}) collective-permute-start(bf16[256,128]{1,0:T(8,128)(2,1)S(1)} %get-tuple-element.186), channel_id=1, source_target_pairs={{0,10},{1,11},{2,8},{3,9},{4,14},{5,15},{6,12},{7,13},{8,2},{9,3},... | collective-permute-start | bytes 196616 | tf_op jit(solution)/shard_map/ppermute | solution.py:421
  151.7 9.7 %collective-permute-start.75 = (bf16[256,128]{1,0:T(8,128)(2,1)S(1)}, bf16[256,128]{1,0:T(8,128)(2,1)S(1)}, u32[]{:S(2)}, u32[]{:S(2)}) collective-permute-start(bf16[256,128]{1,0:T(8,128)(2,1)S(1)} %get-tuple-element.187), channel_id=1, source_target_pairs={{0,2},{1,3},{2,0},{3,1},{4,6},{5,7},{6,4},{7,5},{8,10},{9,11},{10,... | collective-permute-start | bytes 196616 | tf_op jit(solution)/shard_map/ppermute | solution.py:421
  152.6 9.7 %collective-permute-start.76 = (bf16[256,128]{1,0:T(8,128)(2,1)S(1)}, bf16[256,128]{1,0:T(8,128)(2,1)S(1)}, u32[]{:S(2)}, u32[]{:S(2)}) collective-permute-start(bf16[256,128]{1,0:T(8,128)(2,1)S(1)} %get-tuple-element.188), channel_id=1, source_target_pairs={{0,11},{1,10},{2,9},{3,8},{4,15},{5,14},{6,13},{7,12},{8,3},{9,2},... | collective-permute-start | bytes 196616 | tf_op jit(solution)/shard_map/ppermute | solution.py:421
  156.0 14.7 %collective-permute-start.69 = (bf16[264,128]{1,0:T(8,128)(2,1)S(1)}, bf16[264,128]{1,0:T(8,128)(2,1)S(1)}, u32[]{:S(2)}, u32[]{:S(2)}) collective-permute-start(bf16[264,128]{1,0:T(8,128)(2,1)S(1)} %get-tuple-element.181), channel_id=1, source_target_pairs={{0,8},{1,9},{2,10},{3,11},{4,12},{5,13},{6,14},{7,15},{8,0},{9,1},... | collective-permute-start | bytes 202760 | tf_op jit(solution)/shard_map/ppermute | solution.py:421
  156.0 14.7 %collective-permute-start.70 = (bf16[264,128]{1,0:T(8,128)(2,1)S(1)}, bf16[264,128]{1,0:T(8,128)(2,1)S(1)}, u32[]{:S(2)}, u32[]{:S(2)}) collective-permute-start(bf16[264,128]{1,0:T(8,128)(2,1)S(1)} %get-tuple-element.182), channel_id=1, source_target_pairs={{0,4},{1,5},{2,6},{3,7},{4,0},{5,1},{6,2},{7,3},{8,12},{9,13},{10,... | collective-permute-start | bytes 202760 | tf_op jit(solution)/shard_map/ppermute | solution.py:421
  160.9 13.3 %collective-permute-start.71 = (bf16[264,128]{1,0:T(8,128)(2,1)S(1)}, bf16[264,128]{1,0:T(8,128)(2,1)S(1)}, u32[]{:S(2)}, u32[]{:S(2)}) collective-permute-start(bf16[264,128]{1,0:T(8,128)(2,1)S(1)} %get-tuple-element.183), channel_id=1, source_target_pairs={{0,12},{1,13},{2,14},{3,15},{4,8},{5,9},{6,10},{7,11},{8,4},{9,5},... | collective-permute-start | bytes 202760 | tf_op jit(solution)/shard_map/ppermute | solution.py:421
  165.4 9.0 %collective-permute-start.82 = (bf16[256,128]{1,0:T(8,128)(2,1)S(1)}, bf16[256,128]{1,0:T(8,128)(2,1)S(1)}, u32[]{:S(2)}, u32[]{:S(2)}) collective-permute-start(bf16[256,128]{1,0:T(8,128)(2,1)S(1)} %get-tuple-element.192), channel_id=1, source_target_pairs={{0,5},{1,4},{2,7},{3,6},{4,1},{5,0},{6,3},{7,2},{8,13},{9,12},{10,... | collective-permute-start | bytes 196616 | tf_op jit(solution)/shard_map/ppermute | solution.py:421
  167.9 7.6 %collective-permute-start.83 = (bf16[256,128]{1,0:T(8,128)(2,1)S(1)}, bf16[256,128]{1,0:T(8,128)(2,1)S(1)}, u32[]{:S(2)}, u32[]{:S(2)}) collective-permute-start(bf16[256,128]{1,0:T(8,128)(2,1)S(1)} %get-tuple-element.193), channel_id=1, source_target_pairs={{0,14},{1,15},{2,12},{3,13},{4,10},{5,11},{6,8},{7,9},{8,6},{9,7},... | collective-permute-start | bytes 196616 | tf_op jit(solution)/shard_map/ppermute | solution.py:421
  170.6 8.0 %collective-permute-start.84 = (bf16[256,128]{1,0:T(8,128)(2,1)S(1)}, bf16[256,128]{1,0:T(8,128)(2,1)S(1)}, u32[]{:S(2)}, u32[]{:S(2)}) collective-permute-start(bf16[256,128]{1,0:T(8,128)(2,1)S(1)} %get-tuple-element.194), channel_id=1, source_target_pairs={{0,6},{1,7},{2,4},{3,5},{4,2},{5,3},{6,0},{7,1},{8,14},{9,15},{10,... | collective-permute-start | bytes 196616 | tf_op jit(solution)/shard_map/ppermute | solution.py:421
  170.7 8.0 %collective-permute-start.85 = (bf16[256,128]{1,0:T(8,128)(2,1)S(1)}, bf16[256,128]{1,0:T(8,128)(2,1)S(1)}, u32[]{:S(2)}, u32[]{:S(2)}) collective-permute-start(bf16[256,128]{1,0:T(8,128)(2,1)S(1)} %get-tuple-element.195), channel_id=1, source_target_pairs={{0,15},{1,14},{2,13},{3,12},{4,11},{5,10},{6,9},{7,8},{8,7},{9,6},... | collective-permute-start | bytes 196616 | tf_op jit(solution)/shard_map/ppermute | solution.py:421
  (32 other events, 166.9 us)

commit v14 on v12

--- a/solution.py
+++ b/solution.py
@@ -19,6 +19,15 @@
 SMEM = pltpu.SMEM
 HBM = pltpu.HBM
 CHUNKS = 8
+
+
+def steps_of(peers):
+    near, far = list(range(1, peers // 2)), list(range(peers // 2, peers))
+    steps = [0]
+    while far:
+        steps += far[:2] + near[:1]
+        far, near = far[2:], near[1:]
+    return steps + near
 
 
 def diagonal(cols):
@@ -88,7 +97,9 @@
 def start_kernel(peers, me_ref, cells_hbm, counts_hbm, times_hbm, rays_hbm, *refs):
     message_refs = refs[:peers]
     target_ref, total_ref, table_ref, used_ref, cells_ref, counts_ref = refs[peers : peers + 6]
-    times_ref, rays_ref, sems, ray_sems = refs[peers + 6 :]
+    times_ref, rays_ref, place_ref, sems, ray_sems = refs[peers + 6 :]
+    for index, step in enumerate(steps_of(peers)):
+        place_ref[me_ref[0] ^ step] = index
     pair_count, slot_count = rays_ref.shape[:2]
     cols = times_ref.shape[0]
     owned = CELL_DEV // BS
@@ -124,8 +135,7 @@
         count = counts_ref[pair]
         for slot in range(slot_count):
             cell = cells_ref[pair, slot]
-            apart = (cell // owned) ^ me_ref[0]
-            owner = apart * 2 - jnp.where(apart < peers // 2, 0, peers - 1)
+            owner = place_ref[cell // owned]
             local = cell % owned
             used = used_ref[owner]
             rank = used
@@ -397,9 +407,9 @@
     totals = VMEM((spots + 1, cols, BS), F32)
     flops = 2 * slots * BS * BS * cols
 
+    steps = steps_of(peers)
+
     def exchange(values):
-        half = peers // 2
-        steps = [i // 2 + i % 2 * half for i in range(peers)]
         return [values[0]] + [
             lax.ppermute(value, "pair", [(one, one ^ step) for one in range(peers)])
             for value, step in zip(values[1:], steps[1:])
@@ -412,7 +422,7 @@
         [
             totals, SMEM((spots,), jnp.int32), SMEM((peers,), jnp.int32),
             SMEM(block_cells.shape, jnp.int32), SMEM(block_counts.shape, jnp.int32),
-            VMEM(times.shape, F32), VMEM(ray_blocks.shape, BF16),
+            VMEM(times.shape, F32), VMEM(ray_blocks.shape, BF16), SMEM((peers,), jnp.int32),
             pltpu.SemaphoreType.DMA((3,)), pltpu.SemaphoreType.DMA((pair_count,)),
         ],
         flops, 6 << 20, 60 << 20,

time: 174 us -> 192 us (1.10)
  waiting for transfers between devices: 41.8 us -> 57 us
  starting transfers between devices: 104 us -> 107 us
    ppermute x75, waiting for transfers between devices: 39.7 us -> 54.6 us  [exchange(): lax.ppermute(value, 'pair', [(one, one ^ step) for one in range(peers)])]
    ppermute x75, starting transfers between devices: 97.3 us -> 101 us  [exchange(): lax.ppermute(value, 'pair', [(one, one ^ step) for one in range(peers)])]
  transfers between devices with their start and end apart: 81 -> 81, of which waited for: 32 -> 35; matrix products, arithmetic and copies ran while one was open for 0% -> 0% of each run, Pallas kernels for 3% -> 2%
where the time goes in v14:
time: 192 us
  starting transfers between devices  107 us (56%)
  waiting for transfers between devices  57 us (30%)
  Pallas kernels  25.1 us (13%)
    ppermute x75, starting transfers between devices, exchange(): lax.ppermute(value, 'pair', [(one, one ^ step) for one in range(peers)])  101 us
    ppermute x75, waiting for transfers between devices, exchange(): lax.ppermute(value, 'pair', [(one, one ^ step) for one in range(peers)])  54.6 us
    pallas_call x2, Pallas kernels, on_device(): call(functools.partial(pair_kernel, peers), 'pairs_last' if last else 'pa...  6.88 us
    ppermute x6, starting transfers between devices, on_device(): lax.ppermute(share, 'pair', [(one, one ^ step) for one in range(peers)])  6.37 us
    pallas_call x1, Pallas kernels, on_device(): call(functools.partial(start_kernel, peers), 'start', [SMEM, HBM, HBM, HB...  5.37 us
  transfers between devices with their start and end apart: 81, of which 35 were waited for; matrix products, arithmetic and copies ran while one was open for 0% of the time, Pallas kernels for 2%

profile of v14, /device:TPU:0, one launch (start us, length us, event | category | flops | bytes accessed | tf_op | source)
XLA Modules:
  0.0 191.9 jit_solution(3447580640363298661)
XLA Ops:
  0.6 5.4 %start.1 = (bf16[264,128]{1,0:T(8,128)(2,1)}, bf16[264,128]{1,0:T(8,128)(2,1)}, bf16[264,128]{1,0:T(8,128)(2,1)}, bf16[264,128]{1,0:T(8,128)(2,1)}, bf16[264,128...) custom-call(s32[1]{0:T(128)} %bitcast.me_ref, ...), custom_call_target="tpu_custom_call" | custom-call | flops 268435456 | bytes 6291456 | tf_op jit(solution)/shard_map/start/pallas_call | solution.py:419
  6.0 4.1 %collective-permute-start = (bf16[264,128]{1,0:T(8,128)(2,1)}, bf16[264,128]{1,0:T(8,128)(2,1)S(1)}, u32[]{:S(2)}, u32[]{:S(2)}) collective-permute-start(bf16[264,128]{1,0:T(8,128)(2,1)} %get-tuple-element.100), channel_id=1, source_target_pairs={{0,8},{1,9},{2,10},{3,11},{4,12},{5,13},{6,14},{7,15},{8,0},{9,1},... | collective-permute-start | bytes 202760 | tf_op jit(solution)/shard_map/ppermute | solution.py:414
  10.3 3.8 %collective-permute-start.3 = (bf16[264,128]{1,0:T(8,128)(2,1)}, bf16[264,128]{1,0:T(8,128)(2,1)S(1)}, u32[]{:S(2)}, u32[]{:S(2)}) collective-permute-start(bf16[264,128]{1,0:T(8,128)(2,1)} %get-tuple-element.103), channel_id=1, source_target_pairs={{0,10},{1,11},{2,8},{3,9},{4,14},{5,15},{6,12},{7,13},{8,2},{9,3},... | collective-permute-start | bytes 202760 | tf_op jit(solution)/shard_map/ppermute | solution.py:414
  14.1 1.7 collective-permute-start.5
  15.8 2.8 %collective-permute-done.1.refs_2_ = bf16[264,128]{1,0:T(8,128)(2,1)S(1)} collective-permute-done((bf16[264,128]{1,0:T(8,128)(2,1)}, bf16[264,128]{1,0:T(8,128)(2,1)S(1)}, u32[]{:S(2)}, u32[]{:S(2)}) %collective-permute-start.1) | collective-permute-done | bytes 67616 | tf_op jit(solution)/shard_map/ppermute | solution.py:414
  18.6 4.9 %collective-permute-start.6 = (bf16[264,128]{1,0:T(8,128)(2,1)}, bf16[264,128]{1,0:T(8,128)(2,1)S(1)}, u32[]{:S(2)}, u32[]{:S(2)}) collective-permute-start(bf16[264,128]{1,0:T(8,128)(2,1)} %get-tuple-element.106), channel_id=1, source_target_pairs={{0,12},{1,13},{2,14},{3,15},{4,8},{5,9},{6,10},{7,11},{8,4},{9,5},... | collective-permute-start | bytes 202760 | tf_op jit(solution)/shard_map/ppermute | solution.py:414
  24.5 4.1 %collective-permute-start.9 = (bf16[264,128]{1,0:T(8,128)(2,1)}, bf16[264,128]{1,0:T(8,128)(2,1)S(1)}, u32[]{:S(2)}, u32[]{:S(2)}) collective-permute-start(bf16[264,128]{1,0:T(8,128)(2,1)} %get-tuple-element.109), channel_id=1, source_target_pairs={{0,14},{1,15},{2,12},{3,13},{4,10},{5,11},{6,8},{7,9},{8,6},{9,7},... | collective-permute-start | bytes 202760 | tf_op jit(solution)/shard_map/ppermute | solution.py:414
  30.7 1.4 collective-permute-start.13
  32.1 1.2 collective-permute-start.14
  34.8 2.9 %keep.1 = (s32[128]{0:T(128)S(1)}, bf16[264,128]{1,0:T(8,128)(2,1)S(1)}, bf16[8,16,128,128]{3,2,1,0:T(8,128)(2,1)S(1)}) custom-call(s32[128]{0:T(128)S(1)} %copy-done.2, bf16[264,128]{1,0:T(8,128)(2,1)S(1)} %copy-done.1, bf16[8,16,128,128]{3,2,1,0:T(8,128)(2,1)} %rays_hbm.3), custom_call_target="tpu_custom_call" | custom-call | bytes 8388608 | tf_op jit(solution)/shard_map/keep/pallas_call | solution.py:431
  38.2 1.5 collective-permute-done.14.refs_15_
  39.7 2.5 %cells_first.1 = (f32[64,8192]{1,0:T(8,128)S(1)}, f32[64,128]{1,0:T(8,128)S(1)}, bf16[264,128]{1,0:T(8,128)(2,1)S(1)}, bf16[264,128]{1,0:T(8,128)(2,1)S(1)}, bf1...) custom-call(bf16[264,128]{1,0:T(8,128)(2,1)S(1)} %get-tuple-element., ...), custom_call_target="tpu_custom_call" | custom-call | bytes 6291456 | tf_op jit(solution)/shard_map/cells_first/pallas_call | solution.py:436
  42.1 2.0 %collective-permute-start.15 = (bf16[264,128]{1,0:T(8,128)(2,1)S(1)}, bf16[264,128]{1,0:T(8,128)(2,1)S(1)}, u32[]{:S(2)}, u32[]{:S(2)}) collective-permute-start(bf16[264,128]{1,0:T(8,128)(2,1)S(1)} %get-tuple-element.119), channel_id=1, source_target_pairs={{0,8},{1,9},{2,10},{3,11},{4,12},{5,13},{6,14},{7,15},{8,0},{9,1},... | collective-permute-start | bytes 202760 | tf_op jit(solution)/shard_map/ppermute | solution.py:414
  45.2 2.8 %collective-permute-start.18 = (bf16[264,128]{1,0:T(8,128)(2,1)S(1)}, bf16[264,128]{1,0:T(8,128)(2,1)S(1)}, u32[]{:S(2)}, u32[]{:S(2)}) collective-permute-start(bf16[264,128]{1,0:T(8,128)(2,1)S(1)} %get-tuple-element.122), channel_id=1, source_target_pairs={{0,10},{1,11},{2,8},{3,9},{4,14},{5,15},{6,12},{7,13},{8,2},{9,3},... | collective-permute-start | bytes 202760 | tf_op jit(solution)/shard_map/ppermute | solution.py:414
  49.6 3.0 %collective-permute-done.16.refs_2_ = bf16[264,128]{1,0:T(8,128)(2,1)S(1)} collective-permute-done((bf16[264,128]{1,0:T(8,128)(2,1)S(1)}, bf16[264,128]{1,0:T(8,128)(2,1)S(1)}, u32[]{:S(2)}, u32[]{:S(2)}) %collective-permute-start.16) | collective-permute-done | bytes 67616 | tf_op jit(solution)/shard_map/ppermute | solution.py:414
  52.6 4.8 %collective-permute-start.21 = (bf16[264,128]{1,0:T(8,128)(2,1)S(1)}, bf16[264,128]{1,0:T(8,128)(2,1)S(1)}, u32[]{:S(2)}, u32[]{:S(2)}) collective-permute-start(bf16[264,128]{1,0:T(8,128)(2,1)S(1)} %get-tuple-element.125), channel_id=1, source_target_pairs={{0,12},{1,13},{2,14},{3,15},{4,8},{5,9},{6,10},{7,11},{8,4},{9,5},... | collective-permute-start | bytes 202760 | tf_op jit(solution)/shard_map/ppermute | solution.py:414
  58.4 4.0 %collective-permute-start.24 = (bf16[264,128]{1,0:T(8,128)(2,1)S(1)}, bf16[264,128]{1,0:T(8,128)(2,1)S(1)}, u32[]{:S(2)}, u32[]{:S(2)}) collective-permute-start(bf16[264,128]{1,0:T(8,128)(2,1)S(1)} %get-tuple-element.128), channel_id=1, source_target_pairs={{0,14},{1,15},{2,12},{3,13},{4,10},{5,11},{6,8},{7,9},{8,6},{9,7},... | collective-permute-start | bytes 202760 | tf_op jit(solution)/shard_map/ppermute | solution.py:414
  64.6 1.5 collective-permute-start.28
  66.1 1.2 collective-permute-start.29
  67.3 2.3 %collective-permute-done.25.refs_11_ = bf16[264,128]{1,0:T(8,128)(2,1)S(1)} collective-permute-done((bf16[264,128]{1,0:T(8,128)(2,1)S(1)}, bf16[264,128]{1,0:T(8,128)(2,1)S(1)}, u32[]{:S(2)}, u32[]{:S(2)}) %collective-permute-start.25) | collective-permute-done | bytes 67616 | tf_op jit(solution)/shard_map/ppermute | solution.py:414
  69.6 3.5 %collective-permute-done.28.refs_14_ = bf16[264,128]{1,0:T(8,128)(2,1)S(1)} collective-permute-done((bf16[264,128]{1,0:T(8,128)(2,1)S(1)}, bf16[264,128]{1,0:T(8,128)(2,1)S(1)}, u32[]{:S(2)}, u32[]{:S(2)}) %collective-permute-start.28) | collective-permute-done | bytes 67616 | tf_op jit(solution)/shard_map/ppermute | solution.py:414
  73.2 3.4 %pairs.1 = (bf16[264,128]{1,0:T(8,128)(2,1)S(1)}, bf16[264,128]{1,0:T(8,128)(2,1)S(1)}, bf16[264,128]{1,0:T(8,128)(2,1)S(1)}, bf16[264,128]{1,0:T(8,128)(2,1)S(1...) custom-call(s32[128]{0:T(128)S(1)} %get-tuple-element.117.target_ref, ...), custom_call_target="tpu_custom_call" | custom-call | flops 536870912 | bytes 8388608 | tf_op jit(solution)/shard_map/pairs/pallas_call | solution.py:447
  76.6 2.5 %collective-permute-start.30 = (bf16[264,128]{1,0:T(8,128)(2,1)S(1)}, bf16[264,128]{1,0:T(8,128)(2,1)S(1)}, u32[]{:S(2)}, u32[]{:S(2)}) collective-permute-start(bf16[264,128]{1,0:T(8,128)(2,1)S(1)} %get-tuple-element.137), channel_id=1, source_target_pairs={{0,8},{1,9},{2,10},{3,11},{4,12},{5,13},{6,14},{7,15},{8,0},{9,1},... | collective-permute-start | bytes 202760 | tf_op jit(solution)/shard_map/ppermute | solution.py:414
  79.8 3.2 %collective-permute-start.33 = (bf16[264,128]{1,0:T(8,128)(2,1)S(1)}, bf16[264,128]{1,0:T(8,128)(2,1)S(1)}, u32[]{:S(2)}, u32[]{:S(2)}) collective-permute-start(bf16[264,128]{1,0:T(8,128)(2,1)S(1)} %get-tuple-element.140), channel_id=1, source_target_pairs={{0,10},{1,11},{2,8},{3,9},{4,14},{5,15},{6,12},{7,13},{8,2},{9,3},... | collective-permute-start | bytes 202760 | tf_op jit(solution)/shard_map/ppermute | solution.py:414
  84.3 5.0 %collective-permute-done.31.refs_2_ = bf16[264,128]{1,0:T(8,128)(2,1)S(1)} collective-permute-done((bf16[264,128]{1,0:T(8,128)(2,1)S(1)}, bf16[264,128]{1,0:T(8,128)(2,1)S(1)}, u32[]{:S(2)}, u32[]{:S(2)}) %collective-permute-start.31) | collective-permute-done | bytes 67616 | tf_op jit(solution)/shard_map/ppermute | solution.py:414
  89.3 2.7 %collective-permute-start.36 = (bf16[264,128]{1,0:T(8,128)(2,1)S(1)}, bf16[264,128]{1,0:T(8,128)(2,1)S(1)}, u32[]{:S(2)}, u32[]{:S(2)}) collective-permute-start(bf16[264,128]{1,0:T(8,128)(2,1)S(1)} %get-tuple-element.143), channel_id=1, source_target_pairs={{0,12},{1,13},{2,14},{3,15},{4,8},{5,9},{6,10},{7,11},{8,4},{9,5},... | collective-permute-start | bytes 202760 | tf_op jit(solution)/shard_map/ppermute | solution.py:414
  92.8 4.2 %collective-permute-start.39 = (bf16[264,128]{1,0:T(8,128)(2,1)S(1)}, bf16[264,128]{1,0:T(8,128)(2,1)S(1)}, u32[]{:S(2)}, u32[]{:S(2)}) collective-permute-start(bf16[264,128]{1,0:T(8,128)(2,1)S(1)} %get-tuple-element.146), channel_id=1, source_target_pairs={{0,14},{1,15},{2,12},{3,13},{4,10},{5,11},{6,8},{7,9},{8,6},{9,7},... | collective-permute-start | bytes 202760 | tf_op jit(solution)/shard_map/ppermute | solution.py:414
  99.1 1.8 collective-permute-start.43
  101.9 2.3 %collective-permute-done.40.refs_11_ = bf16[264,128]{1,0:T(8,128)(2,1)S(1)} collective-permute-done((bf16[264,128]{1,0:T(8,128)(2,1)S(1)}, bf16[264,128]{1,0:T(8,128)(2,1)S(1)}, u32[]{:S(2)}, u32[]{:S(2)}) %collective-permute-start.40) | collective-permute-done | bytes 67616 | tf_op jit(solution)/shard_map/ppermute | solution.py:414
  104.3 3.5 %collective-permute-done.43.refs_14_ = bf16[264,128]{1,0:T(8,128)(2,1)S(1)} collective-permute-done((bf16[264,128]{1,0:T(8,128)(2,1)S(1)}, bf16[264,128]{1,0:T(8,128)(2,1)S(1)}, u32[]{:S(2)}, u32[]{:S(2)}) %collective-permute-start.43) | collective-permute-done | bytes 67616 | tf_op jit(solution)/shard_map/ppermute | solution.py:414
  108.8 2.4 %cells.1 = (f32[64,8192]{1,0:T(8,128)S(1)}, f32[64,128]{1,0:T(8,128)S(1)}, bf16[264,128]{1,0:T(8,128)(2,1)S(1)}, bf16[264,128]{1,0:T(8,128)(2,1)S(1)}, bf16[264,...) custom-call(s32[16,128]{1,0:T(8,128)S(1)} %get-tuple-element.116.ask, ...), custom_call_target="tpu_custom_call" | custom-call | bytes 8388608 | tf_op jit(solution)/shard_map/cells/pallas_call | solution.py:456
  111.2 1.6 collective-permute-start.45
  114.3 2.1 %collective-permute-start.48 = (bf16[264,128]{1,0:T(8,128)(2,1)S(1)}, bf16[264,128]{1,0:T(8,128)(2,1)S(1)}, u32[]{:S(2)}, u32[]{:S(2)}) collective-permute-start(bf16[264,128]{1,0:T(8,128)(2,1)S(1)} %get-tuple-element.158), channel_id=1, source_target_pairs={{0,10},{1,11},{2,8},{3,9},{4,14},{5,15},{6,12},{7,13},{8,2},{9,3},... | collective-permute-start | bytes 202760 | tf_op jit(solution)/shard_map/ppermute | solution.py:414
  117.4 3.3 %collective-permute-done.45.refs_1_ = bf16[264,128]{1,0:T(8,128)(2,1)S(1)} collective-permute-done((bf16[264,128]{1,0:T(8,128)(2,1)S(1)}, bf16[264,128]{1,0:T(8,128)(2,1)S(1)}, u32[]{:S(2)}, u32[]{:S(2)}) %collective-permute-start.45) | collective-permute-done | bytes 67616 | tf_op jit(solution)/shard_map/ppermute | solution.py:414
  120.7 2.5 %collective-permute-done.46.refs_2_ = bf16[264,128]{1,0:T(8,128)(2,1)S(1)} collective-permute-done((bf16[264,128]{1,0:T(8,128)(2,1)S(1)}, bf16[264,128]{1,0:T(8,128)(2,1)S(1)}, u32[]{:S(2)}, u32[]{:S(2)}) %collective-permute-start.46) | collective-permute-done | bytes 67616 | tf_op jit(solution)/shard_map/ppermute | solution.py:414
  123.2 2.4 %collective-permute-start.51 = (bf16[264,128]{1,0:T(8,128)(2,1)S(1)}, bf16[264,128]{1,0:T(8,128)(2,1)S(1)}, u32[]{:S(2)}, u32[]{:S(2)}) collective-permute-start(bf16[264,128]{1,0:T(8,128)(2,1)S(1)} %get-tuple-element.161), channel_id=1, source_target_pairs={{0,12},{1,13},{2,14},{3,15},{4,8},{5,9},{6,10},{7,11},{8,4},{9,5},... | collective-permute-start | bytes 202760 | tf_op jit(solution)/shard_map/ppermute | solution.py:414
  125.6 1.2 collective-permute-start.52
  127.2 3.4 %collective-permute-start.54 = (bf16[264,128]{1,0:T(8,128)(2,1)S(1)}, bf16[264,128]{1,0:T(8,128)(2,1)S(1)}, u32[]{:S(2)}, u32[]{:S(2)}) collective-permute-start(bf16[264,128]{1,0:T(8,128)(2,1)S(1)} %get-tuple-element.164), channel_id=1, source_target_pairs={{0,14},{1,15},{2,12},{3,13},{4,10},{5,11},{6,8},{7,9},{8,6},{9,7},... | collective-permute-start | bytes 202760 | tf_op jit(solution)/shard_map/ppermute | solution.py:414
  131.9 1.5 collective-permute-start.57
  133.4 1.4 collective-permute-start.58
  134.8 1.2 collective-permute-start.59
  136.0 1.8 collective-permute-done.55.refs_11_
  138.8 3.0 %collective-permute-done.58.refs_14_ = bf16[264,128]{1,0:T(8,128)(2,1)S(1)} collective-permute-done((bf16[264,128]{1,0:T(8,128)(2,1)S(1)}, bf16[264,128]{1,0:T(8,128)(2,1)S(1)}, u32[]{:S(2)}, u32[]{:S(2)}) %collective-permute-start.58) | collective-permute-done | bytes 67616 | tf_op jit(solution)/shard_map/ppermute | solution.py:414
  142.7 3.4 %pairs_last.1 = (bf16[264,128]{1,0:T(8,128)(2,1)S(1)}, bf16[264,128]{1,0:T(8,128)(2,1)S(1)}, bf16[264,128]{1,0:T(8,128)(2,1)S(1)}, bf16[264,128]{1,0:T(8,128)(2,...) custom-call(s32[128]{0:T(128)S(1)} %get-tuple-element.117.target_ref, ...), custom_call_target="tpu_custom_call" | custom-call | flops 536870912 | bytes 8388608 | tf_op jit(solution)/shard_map/pairs_last/pallas_call | solution.py:447
  146.1 1.3 collective-permute-start.60
  147.5 1.1 collective-permute-start.61
  149.2 1.8 collective-permute-start.63
  151.1 1.3 collective-permute-start.64
  152.4 3.3 %collective-permute-done.60.refs_1_ = bf16[264,128]{1,0:T(8,128)(2,1)S(1)} collective-permute-done((bf16[264,128]{1,0:T(8,128)(2,1)S(1)}, bf16[264,128]{1,0:T(8,128)(2,1)S(1)}, u32[]{:S(2)}, u32[]{:S(2)}) %collective-permute-start.60) | collective-permute-done | bytes 67616 | tf_op jit(solution)/shard_map/ppermute | solution.py:414
  156.1 2.2 %collective-permute-done.61.refs_2_ = bf16[264,128]{1,0:T(8,128)(2,1)S(1)} collective-permute-done((bf16[264,128]{1,0:T(8,128)(2,1)S(1)}, bf16[264,128]{1,0:T(8,128)(2,1)S(1)}, u32[]{:S(2)}, u32[]{:S(2)}) %collective-permute-start.61) | collective-permute-done | bytes 67616 | tf_op jit(solution)/shard_map/ppermute | solution.py:414
  158.3 2.0 %collective-permute-start.66 = (bf16[264,128]{1,0:T(8,128)(2,1)S(1)}, bf16[264,128]{1,0:T(8,128)(2,1)S(1)}, u32[]{:S(2)}, u32[]{:S(2)}) collective-permute-start(bf16[264,128]{1,0:T(8,128)(2,1)S(1)} %get-tuple-element.180), channel_id=1, source_target_pairs={{0,12},{1,13},{2,14},{3,15},{4,8},{5,9},{6,10},{7,11},{8,4},{9,5},... | collective-permute-start | bytes 202760 | tf_op jit(solution)/shard_map/ppermute | solution.py:414
  160.3 1.5 collective-permute-start.67
  162.3 3.0 %collective-permute-start.69 = (bf16[264,128]{1,0:T(8,128)(2,1)S(1)}, bf16[264,128]{1,0:T(8,128)(2,1)S(1)}, u32[]{:S(2)}, u32[]{:S(2)}) collective-permute-start(bf16[264,128]{1,0:T(8,128)(2,1)S(1)} %get-tuple-element.183), channel_id=1, source_target_pairs={{0,14},{1,15},{2,12},{3,13},{4,10},{5,11},{6,8},{7,9},{8,6},{9,7},... | collective-permute-start | bytes 202760 | tf_op jit(solution)/shard_map/ppermute | solution.py:414
  166.4 2.1 %collective-permute-start.72 = (bf16[264,128]{1,0:T(8,128)(2,1)S(1)}, bf16[264,128]{1,0:T(8,128)(2,1)S(1)}, u32[]{:S(2)}, u32[]{:S(2)}) collective-permute-start(bf16[264,128]{1,0:T(8,128)(2,1)S(1)} %get-tuple-element.186), channel_id=1, source_target_pairs={{0,5},{1,4},{2,7},{3,6},{4,1},{5,0},{6,3},{7,2},{8,13},{9,12},{10,... | collective-permute-start | bytes 202760 | tf_op jit(solution)/shard_map/ppermute | solution.py:414
  168.5 1.4 collective-permute-start.73
  169.9 1.2 collective-permute-start.74
  171.1 1.5 collective-permute-done.70.refs_11_
  173.8 3.0 %collective-permute-done.73.refs_14_ = bf16[264,128]{1,0:T(8,128)(2,1)S(1)} collective-permute-done((bf16[264,128]{1,0:T(8,128)(2,1)S(1)}, bf16[264,128]{1,0:T(8,128)(2,1)S(1)}, u32[]{:S(2)}, u32[]{:S(2)}) %collective-permute-start.73) | collective-permute-done | bytes 67616 | tf_op jit(solution)/shard_map/ppermute | solution.py:414
  177.8 2.0 %cells_last.1 = (f32[64,8192]{1,0:T(8,128)S(1)}, f32[64,128]{1,0:T(8,128)S(1)}, f32[8,128]{1,0:T(8,128)S(1)}) custom-call(s32[16,128]{1,0:T(8,128)S(1)} %get-tuple-element.116.asked_ref, bf16[264,128]{1,0:T(8,128)(2,1)S(1)} %get-tuple-element.173.refs_0_, bf16[264,128]{1,0:T(8,128)(2,1)S(1)} %collective-permute-done.60.refs_1_, ...), custom_call_target="tpu_custom_call" | custom-call | bytes 8388608 | tf_op jit(solution)/shard_map/cells_last/pallas_call | solution.py:462
  179.8 2.1 %collective-permute-start.77 = (f32[8,128]{1,0:T(8,128)S(1)}, f32[8,128]{1,0:T(8,128)S(1)}, u32[]{:S(2)}, u32[]{:S(2)}) collective-permute-start(f32[8,128]{1,0:T(8,128)S(1)} %get-tuple-element.190), channel_id=1, source_target_pairs={{0,12},{1,13},{2,14},{3,15},{4,8},{5,9},{6,10},{7,11},{8,4},{9,5},... | collective-permute-start | bytes 12296 | tf_op jit(solution)/shard_map/ppermute | solution.py:472
  181.9 2.4 %collective-permute-start.75 = (f32[8,128]{1,0:T(8,128)S(1)}, f32[8,128]{1,0:T(8,128)S(1)}, u32[]{:S(2)}, u32[]{:S(2)}) collective-permute-start(f32[8,128]{1,0:T(8,128)S(1)} %get-tuple-element.190), channel_id=1, source_target_pairs={{0,4},{1,5},{2,6},{3,7},{4,0},{5,1},{6,2},{7,3},{8,12},{9,13},{10,... | collective-permute-start | bytes 12296 | tf_op jit(solution)/shard_map/ppermute | solution.py:472
  187.2 1.1 collective-permute-start.78
  188.3 1.5 estimate.1
  190.2 1.5 model.1
  (114 shorter events, 32.3 us)
Async XLA Ops:
  6.0 8.1 %collective-permute-start = (bf16[264,128]{1,0:T(8,128)(2,1)}, bf16[264,128]{1,0:T(8,128)(2,1)S(1)}, u32[]{:S(2)}, u32[]{:S(2)}) collective-permute-start(bf16[264,128]{1,0:T(8,128)(2,1)} %get-tuple-element.100), channel_id=1, source_target_pairs={{0,8},{1,9},{2,10},{3,11},{4,12},{5,13},{6,14},{7,15},{8,0},{9,1},... | collective-permute-start | bytes 202760 | tf_op jit(solution)/shard_map/ppermute | solution.py:414
  10.1 8.5 %collective-permute-start.1 = (bf16[264,128]{1,0:T(8,128)(2,1)}, bf16[264,128]{1,0:T(8,128)(2,1)S(1)}, u32[]{:S(2)}, u32[]{:S(2)}) collective-permute-start(bf16[264,128]{1,0:T(8,128)(2,1)} %get-tuple-element.101), channel_id=1, source_target_pairs={{0,9},{1,8},{2,11},{3,10},{4,13},{5,12},{6,15},{7,14},{8,1},{9,0},... | collective-permute-start | bytes 202760 | tf_op jit(solution)/shard_map/ppermute | solution.py:414
  10.1 13.4 %collective-permute-start.2 = (bf16[264,128]{1,0:T(8,128)(2,1)}, bf16[264,128]{1,0:T(8,128)(2,1)S(1)}, u32[]{:S(2)}, u32[]{:S(2)}) collective-permute-start(bf16[264,128]{1,0:T(8,128)(2,1)} %get-tuple-element.102), channel_id=1, source_target_pairs={{0,1},{1,0},{2,3},{3,2},{4,5},{5,4},{6,7},{7,6},{8,9},{9,8},{10,11... | collective-permute-start | bytes 202760 | tf_op jit(solution)/shard_map/ppermute | solution.py:414
  10.3 13.2 %collective-permute-start.3 = (bf16[264,128]{1,0:T(8,128)(2,1)}, bf16[264,128]{1,0:T(8,128)(2,1)S(1)}, u32[]{:S(2)}, u32[]{:S(2)}) collective-permute-start(bf16[264,128]{1,0:T(8,128)(2,1)} %get-tuple-element.103), channel_id=1, source_target_pairs={{0,10},{1,11},{2,8},{3,9},{4,14},{5,15},{6,12},{7,13},{8,2},{9,3},... | collective-permute-start | bytes 202760 | tf_op jit(solution)/shard_map/ppermute | solution.py:414
  14.1 10.3 %collective-permute-start.4 = (bf16[264,128]{1,0:T(8,128)(2,1)}, bf16[264,128]{1,0:T(8,128)(2,1)S(1)}, u32[]{:S(2)}, u32[]{:S(2)}) collective-permute-start(bf16[264,128]{1,0:T(8,128)(2,1)} %get-tuple-element.104), channel_id=1, source_target_pairs={{0,11},{1,10},{2,9},{3,8},{4,15},{5,14},{6,13},{7,12},{8,3},{9,2},... | collective-permute-start | bytes 202760 | tf_op jit(solution)/shard_map/ppermute | solution.py:414
  14.1 14.4 %collective-permute-start.5 = (bf16[264,128]{1,0:T(8,128)(2,1)}, bf16[264,128]{1,0:T(8,128)(2,1)S(1)}, u32[]{:S(2)}, u32[]{:S(2)}) collective-permute-start(bf16[264,128]{1,0:T(8,128)(2,1)} %get-tuple-element.105), channel_id=1, source_target_pairs={{0,2},{1,3},{2,0},{3,1},{4,6},{5,7},{6,4},{7,5},{8,10},{9,11},{10,... | collective-permute-start | bytes 202760 | tf_op jit(solution)/shard_map/ppermute | solution.py:414
  18.6 10.2 %collective-permute-start.6 = (bf16[264,128]{1,0:T(8,128)(2,1)}, bf16[264,128]{1,0:T(8,128)(2,1)S(1)}, u32[]{:S(2)}, u32[]{:S(2)}) collective-permute-start(bf16[264,128]{1,0:T(8,128)(2,1)} %get-tuple-element.106), channel_id=1, source_target_pairs={{0,12},{1,13},{2,14},{3,15},{4,8},{5,9},{6,10},{7,11},{8,4},{9,5},... | collective-permute-start | bytes 202760 | tf_op jit(solution)/shard_map/ppermute | solution.py:414
  23.5 7.2 %collective-permute-start.8 = (bf16[264,128]{1,0:T(8,128)(2,1)}, bf16[264,128]{1,0:T(8,128)(2,1)S(1)}, u32[]{:S(2)}, u32[]{:S(2)}) collective-permute-start(bf16[264,128]{1,0:T(8,128)(2,1)} %get-tuple-element.108), channel_id=1, source_target_pairs={{0,3},{1,2},{2,1},{3,0},{4,7},{5,6},{6,5},{7,4},{8,11},{9,10},{10,... | collective-permute-start | bytes 202760 | tf_op jit(solution)/shard_map/ppermute | solution.py:414
  24.5 7.6 %collective-permute-start.9 = (bf16[264,128]{1,0:T(8,128)(2,1)}, bf16[264,128]{1,0:T(8,128)(2,1)S(1)}, u32[]{:S(2)}, u32[]{:S(2)}) collective-permute-start(bf16[264,128]{1,0:T(8,128)(2,1)} %get-tuple-element.109), channel_id=1, source_target_pairs={{0,14},{1,15},{2,12},{3,13},{4,10},{5,11},{6,8},{7,9},{8,6},{9,7},... | collective-permute-start | bytes 202760 | tf_op jit(solution)/shard_map/ppermute | solution.py:414
  28.5 9.2 %collective-permute-start.10 = (bf16[264,128]{1,0:T(8,128)(2,1)}, bf16[264,128]{1,0:T(8,128)(2,1)S(1)}, u32[]{:S(2)}, u32[]{:S(2)}) collective-permute-start(bf16[264,128]{1,0:T(8,128)(2,1)} %get-tuple-element.110), channel_id=1, source_target_pairs={{0,15},{1,14},{2,13},{3,12},{4,11},{5,10},{6,9},{7,8},{8,7},{9,6},... | collective-permute-start | bytes 202760 | tf_op jit(solution)/shard_map/ppermute | solution.py:414
  28.9 8.8 %collective-permute-start.11 = (bf16[264,128]{1,0:T(8,128)(2,1)}, bf16[264,128]{1,0:T(8,128)(2,1)S(1)}, u32[]{:S(2)}, u32[]{:S(2)}) collective-permute-start(bf16[264,128]{1,0:T(8,128)(2,1)} %get-tuple-element.111), channel_id=1, source_target_pairs={{0,4},{1,5},{2,6},{3,7},{4,0},{5,1},{6,2},{7,3},{8,12},{9,13},{10,... | collective-permute-start | bytes 202760 | tf_op jit(solution)/shard_map/ppermute | solution.py:414
  29.7 8.0 %collective-permute-start.12 = (bf16[264,128]{1,0:T(8,128)(2,1)}, bf16[264,128]{1,0:T(8,128)(2,1)S(1)}, u32[]{:S(2)}, u32[]{:S(2)}) collective-permute-start(bf16[264,128]{1,0:T(8,128)(2,1)} %get-tuple-element.112), channel_id=1, source_target_pairs={{0,5},{1,4},{2,7},{3,6},{4,1},{5,0},{6,3},{7,2},{8,13},{9,12},{10,... | collective-permute-start | bytes 202760 | tf_op jit(solution)/shard_map/ppermute | solution.py:414
  30.7 7.5 %collective-permute-start.13 = (bf16[264,128]{1,0:T(8,128)(2,1)}, bf16[264,128]{1,0:T(8,128)(2,1)S(1)}, u32[]{:S(2)}, u32[]{:S(2)}) collective-permute-start(bf16[264,128]{1,0:T(8,128)(2,1)} %get-tuple-element.113), channel_id=1, source_target_pairs={{0,6},{1,7},{2,4},{3,5},{4,2},{5,3},{6,0},{7,1},{8,14},{9,15},{10,... | collective-permute-start | bytes 202760 | tf_op jit(solution)/shard_map/ppermute | solution.py:414
  32.1 7.6 %collective-permute-start.14 = (bf16[264,128]{1,0:T(8,128)(2,1)}, bf16[264,128]{1,0:T(8,128)(2,1)S(1)}, u32[]{:S(2)}, u32[]{:S(2)}) collective-permute-start(bf16[264,128]{1,0:T(8,128)(2,1)} %get-tuple-element.114), channel_id=1, source_target_pairs={{0,7},{1,6},{2,5},{3,4},{4,3},{5,2},{6,1},{7,0},{8,15},{9,14},{10,... | collective-permute-start | bytes 202760 | tf_op jit(solution)/shard_map/ppermute | solution.py:414
  42.1 7.0 %collective-permute-start.15 = (bf16[264,128]{1,0:T(8,128)(2,1)S(1)}, bf16[264,128]{1,0:T(8,128)(2,1)S(1)}, u32[]{:S(2)}, u32[]{:S(2)}) collective-permute-start(bf16[264,128]{1,0:T(8,128)(2,1)S(1)} %get-tuple-element.119), channel_id=1, source_target_pairs={{0,8},{1,9},{2,10},{3,11},{4,12},{5,13},{6,14},{7,15},{8,0},{9,1},... | collective-permute-start | bytes 202760 | tf_op jit(solution)/shard_map/ppermute | solution.py:414
  44.2 8.4 %collective-permute-start.16 = (bf16[264,128]{1,0:T(8,128)(2,1)S(1)}, bf16[264,128]{1,0:T(8,128)(2,1)S(1)}, u32[]{:S(2)}, u32[]{:S(2)}) collective-permute-start(bf16[264,128]{1,0:T(8,128)(2,1)S(1)} %get-tuple-element.120), channel_id=1, source_target_pairs={{0,9},{1,8},{2,11},{3,10},{4,13},{5,12},{6,15},{7,14},{8,1},{9,0},... | collective-permute-start | bytes 202760 | tf_op jit(solution)/shard_map/ppermute | solution.py:414
  44.5 12.9 %collective-permute-start.17 = (bf16[264,128]{1,0:T(8,128)(2,1)S(1)}, bf16[264,128]{1,0:T(8,128)(2,1)S(1)}, u32[]{:S(2)}, u32[]{:S(2)}) collective-permute-start(bf16[264,128]{1,0:T(8,128)(2,1)S(1)} %get-tuple-element.121), channel_id=1, source_target_pairs={{0,1},{1,0},{2,3},{3,2},{4,5},{5,4},{6,7},{7,6},{8,9},{9,8},{10,11... | collective-permute-start | bytes 202760 | tf_op jit(solution)/shard_map/ppermute | solution.py:414
  45.2 12.9 %collective-permute-start.18 = (bf16[264,128]{1,0:T(8,128)(2,1)S(1)}, bf16[264,128]{1,0:T(8,128)(2,1)S(1)}, u32[]{:S(2)}, u32[]{:S(2)}) collective-permute-start(bf16[264,128]{1,0:T(8,128)(2,1)S(1)} %get-tuple-element.122), channel_id=1, source_target_pairs={{0,10},{1,11},{2,8},{3,9},{4,14},{5,15},{6,12},{7,13},{8,2},{9,3},... | collective-permute-start | bytes 202760 | tf_op jit(solution)/shard_map/ppermute | solution.py:414
  48.1 10.3 %collective-permute-start.19 = (bf16[264,128]{1,0:T(8,128)(2,1)S(1)}, bf16[264,128]{1,0:T(8,128)(2,1)S(1)}, u32[]{:S(2)}, u32[]{:S(2)}) collective-permute-start(bf16[264,128]{1,0:T(8,128)(2,1)S(1)} %get-tuple-element.123), channel_id=1, source_target_pairs={{0,11},{1,10},{2,9},{3,8},{4,15},{5,14},{6,13},{7,12},{8,3},{9,2},... | collective-permute-start | bytes 202760 | tf_op jit(solution)/shard_map/ppermute | solution.py:414
  49.1 13.4 %collective-permute-start.20 = (bf16[264,128]{1,0:T(8,128)(2,1)S(1)}, bf16[264,128]{1,0:T(8,128)(2,1)S(1)}, u32[]{:S(2)}, u32[]{:S(2)}) collective-permute-start(bf16[264,128]{1,0:T(8,128)(2,1)S(1)} %get-tuple-element.124), channel_id=1, source_target_pairs={{0,2},{1,3},{2,0},{3,1},{4,6},{5,7},{6,4},{7,5},{8,10},{9,11},{10,... | collective-permute-start | bytes 202760 | tf_op jit(solution)/shard_map/ppermute | solution.py:414
  52.6 10.3 %collective-permute-start.21 = (bf16[264,128]{1,0:T(8,128)(2,1)S(1)}, bf16[264,128]{1,0:T(8,128)(2,1)S(1)}, u32[]{:S(2)}, u32[]{:S(2)}) collective-permute-start(bf16[264,128]{1,0:T(8,128)(2,1)S(1)} %get-tuple-element.125), channel_id=1, source_target_pairs={{0,12},{1,13},{2,14},{3,15},{4,8},{5,9},{6,10},{7,11},{8,4},{9,5},... | collective-permute-start | bytes 202760 | tf_op jit(solution)/shard_map/ppermute | solution.py:414
  58.4 7.7 %collective-permute-start.24 = (bf16[264,128]{1,0:T(8,128)(2,1)S(1)}, bf16[264,128]{1,0:T(8,128)(2,1)S(1)}, u32[]{:S(2)}, u32[]{:S(2)}) collective-permute-start(bf16[264,128]{1,0:T(8,128)(2,1)S(1)} %get-tuple-element.128), channel_id=1, source_target_pairs={{0,14},{1,15},{2,12},{3,13},{4,10},{5,11},{6,8},{7,9},{8,6},{9,7},... | collective-permute-start | bytes 202760 | tf_op jit(solution)/shard_map/ppermute | solution.py:414
  62.5 7.1 %collective-permute-start.25 = (bf16[264,128]{1,0:T(8,128)(2,1)S(1)}, bf16[264,128]{1,0:T(8,128)(2,1)S(1)}, u32[]{:S(2)}, u32[]{:S(2)}) collective-permute-start(bf16[264,128]{1,0:T(8,128)(2,1)S(1)} %get-tuple-element.129), channel_id=1, source_target_pairs={{0,15},{1,14},{2,13},{3,12},{4,11},{5,10},{6,9},{7,8},{8,7},{9,6},... | collective-permute-start | bytes 202760 | tf_op jit(solution)/shard_map/ppermute | solution.py:414
  62.9 6.7 %collective-permute-start.26 = (bf16[264,128]{1,0:T(8,128)(2,1)S(1)}, bf16[264,128]{1,0:T(8,128)(2,1)S(1)}, u32[]{:S(2)}, u32[]{:S(2)}) collective-permute-start(bf16[264,128]{1,0:T(8,128)(2,1)S(1)} %get-tuple-element.130), channel_id=1, source_target_pairs={{0,4},{1,5},{2,6},{3,7},{4,0},{5,1},{6,2},{7,3},{8,12},{9,13},{10,... | collective-permute-start | bytes 202760 | tf_op jit(solution)/shard_map/ppermute | solution.py:414
  64.6 8.5 %collective-permute-start.28 = (bf16[264,128]{1,0:T(8,128)(2,1)S(1)}, bf16[264,128]{1,0:T(8,128)(2,1)S(1)}, u32[]{:S(2)}, u32[]{:S(2)}) collective-permute-start(bf16[264,128]{1,0:T(8,128)(2,1)S(1)} %get-tuple-element.132), channel_id=1, source_target_pairs={{0,6},{1,7},{2,4},{3,5},{4,2},{5,3},{6,0},{7,1},{8,14},{9,15},{10,... | collective-permute-start | bytes 202760 | tf_op jit(solution)/shard_map/ppermute | solution.py:414
  66.1 7.1 %collective-permute-start.29 = (bf16[264,128]{1,0:T(8,128)(2,1)S(1)}, bf16[264,128]{1,0:T(8,128)(2,1)S(1)}, u32[]{:S(2)}, u32[]{:S(2)}) collective-permute-start(bf16[264,128]{1,0:T(8,128)(2,1)S(1)} %get-tuple-element.133), channel_id=1, source_target_pairs={{0,7},{1,6},{2,5},{3,4},{4,3},{5,2},{6,1},{7,0},{8,15},{9,14},{10,... | collective-permute-start | bytes 202760 | tf_op jit(solution)/shard_map/ppermute | solution.py:414
  76.6 7.1 %collective-permute-start.30 = (bf16[264,128]{1,0:T(8,128)(2,1)S(1)}, bf16[264,128]{1,0:T(8,128)(2,1)S(1)}, u32[]{:S(2)}, u32[]{:S(2)}) collective-permute-start(bf16[264,128]{1,0:T(8,128)(2,1)S(1)} %get-tuple-element.137), channel_id=1, source_target_pairs={{0,8},{1,9},{2,10},{3,11},{4,12},{5,13},{6,14},{7,15},{8,0},{9,1},... | collective-permute-start | bytes 202760 | tf_op jit(solution)/shard_map/ppermute | solution.py:414
  79.1 10.2 %collective-permute-start.31 = (bf16[264,128]{1,0:T(8,128)(2,1)S(1)}, bf16[264,128]{1,0:T(8,128)(2,1)S(1)}, u32[]{:S(2)}, u32[]{:S(2)}) collective-permute-start(bf16[264,128]{1,0:T(8,128)(2,1)S(1)} %get-tuple-element.138), channel_id=1, source_target_pairs={{0,9},{1,8},{2,11},{3,10},{4,13},{5,12},{6,15},{7,14},{8,1},{9,0},... | collective-permute-start | bytes 202760 | tf_op jit(solution)/shard_map/ppermute | solution.py:414
  79.5 12.5 %collective-permute-start.32 = (bf16[264,128]{1,0:T(8,128)(2,1)S(1)}, bf16[264,128]{1,0:T(8,128)(2,1)S(1)}, u32[]{:S(2)}, u32[]{:S(2)}) collective-permute-start(bf16[264,128]{1,0:T(8,128)(2,1)S(1)} %get-tuple-element.139), channel_id=1, source_target_pairs={{0,1},{1,0},{2,3},{3,2},{4,5},{5,4},{6,7},{7,6},{8,9},{9,8},{10,11... | collective-permute-start | bytes 202760 | tf_op jit(solution)/shard_map/ppermute | solution.py:414
  79.8 13.1 %collective-permute-start.33 = (bf16[264,128]{1,0:T(8,128)(2,1)S(1)}, bf16[264,128]{1,0:T(8,128)(2,1)S(1)}, u32[]{:S(2)}, u32[]{:S(2)}) collective-permute-start(bf16[264,128]{1,0:T(8,128)(2,1)S(1)} %get-tuple-element.140), channel_id=1, source_target_pairs={{0,10},{1,11},{2,8},{3,9},{4,14},{5,15},{6,12},{7,13},{8,2},{9,3},... | collective-permute-start | bytes 202760 | tf_op jit(solution)/shard_map/ppermute | solution.py:414
  82.9 9.9 %collective-permute-start.34 = (bf16[264,128]{1,0:T(8,128)(2,1)S(1)}, bf16[264,128]{1,0:T(8,128)(2,1)S(1)}, u32[]{:S(2)}, u32[]{:S(2)}) collective-permute-start(bf16[264,128]{1,0:T(8,128)(2,1)S(1)} %get-tuple-element.141), channel_id=1, source_target_pairs={{0,11},{1,10},{2,9},{3,8},{4,15},{5,14},{6,13},{7,12},{8,3},{9,2},... | collective-permute-start | bytes 202760 | tf_op jit(solution)/shard_map/ppermute | solution.py:414
  83.8 13.3 %collective-permute-start.35 = (bf16[264,128]{1,0:T(8,128)(2,1)S(1)}, bf16[264,128]{1,0:T(8,128)(2,1)S(1)}, u32[]{:S(2)}, u32[]{:S(2)}) collective-permute-start(bf16[264,128]{1,0:T(8,128)(2,1)S(1)} %get-tuple-element.142), channel_id=1, source_target_pairs={{0,2},{1,3},{2,0},{3,1},{4,6},{5,7},{6,4},{7,5},{8,10},{9,11},{10,... | collective-permute-start | bytes 202760 | tf_op jit(solution)/shard_map/ppermute | solution.py:414
  89.3 8.1 %collective-permute-start.36 = (bf16[264,128]{1,0:T(8,128)(2,1)S(1)}, bf16[264,128]{1,0:T(8,128)(2,1)S(1)}, u32[]{:S(2)}, u32[]{:S(2)}) collective-permute-start(bf16[264,128]{1,0:T(8,128)(2,1)S(1)} %get-tuple-element.143), channel_id=1, source_target_pairs={{0,12},{1,13},{2,14},{3,15},{4,8},{5,9},{6,10},{7,11},{8,4},{9,5},... | collective-permute-start | bytes 202760 | tf_op jit(solution)/shard_map/ppermute | solution.py:414
  92.8 8.1 %collective-permute-start.39 = (bf16[264,128]{1,0:T(8,128)(2,1)S(1)}, bf16[264,128]{1,0:T(8,128)(2,1)S(1)}, u32[]{:S(2)}, u32[]{:S(2)}) collective-permute-start(bf16[264,128]{1,0:T(8,128)(2,1)S(1)} %get-tuple-element.146), channel_id=1, source_target_pairs={{0,14},{1,15},{2,12},{3,13},{4,10},{5,11},{6,8},{7,9},{8,6},{9,7},... | collective-permute-start | bytes 202760 | tf_op jit(solution)/shard_map/ppermute | solution.py:414
  97.0 7.2 %collective-permute-start.40 = (bf16[264,128]{1,0:T(8,128)(2,1)S(1)}, bf16[264,128]{1,0:T(8,128)(2,1)S(1)}, u32[]{:S(2)}, u32[]{:S(2)}) collective-permute-start(bf16[264,128]{1,0:T(8,128)(2,1)S(1)} %get-tuple-element.147), channel_id=1, source_target_pairs={{0,15},{1,14},{2,13},{3,12},{4,11},{5,10},{6,9},{7,8},{8,7},{9,6},... | collective-permute-start | bytes 202760 | tf_op jit(solution)/shard_map/ppermute | solution.py:414
  97.4 6.8 %collective-permute-start.41 = (bf16[264,128]{1,0:T(8,128)(2,1)S(1)}, bf16[264,128]{1,0:T(8,128)(2,1)S(1)}, u32[]{:S(2)}, u32[]{:S(2)}) collective-permute-start(bf16[264,128]{1,0:T(8,128)(2,1)S(1)} %get-tuple-element.148), channel_id=1, source_target_pairs={{0,4},{1,5},{2,6},{3,7},{4,0},{5,1},{6,2},{7,3},{8,12},{9,13},{10,... | collective-permute-start | bytes 202760 | tf_op jit(solution)/shard_map/ppermute | solution.py:414
  99.1 8.7 %collective-permute-start.43 = (bf16[264,128]{1,0:T(8,128)(2,1)S(1)}, bf16[264,128]{1,0:T(8,128)(2,1)S(1)}, u32[]{:S(2)}, u32[]{:S(2)}) collective-permute-start(bf16[264,128]{1,0:T(8,128)(2,1)S(1)} %get-tuple-element.150), channel_id=1, source_target_pairs={{0,6},{1,7},{2,4},{3,5},{4,2},{5,3},{6,0},{7,1},{8,14},{9,15},{10,... | collective-permute-start | bytes 202760 | tf_op jit(solution)/shard_map/ppermute | solution.py:414
  100.9 7.9 %collective-permute-start.44 = (bf16[264,128]{1,0:T(8,128)(2,1)S(1)}, bf16[264,128]{1,0:T(8,128)(2,1)S(1)}, u32[]{:S(2)}, u32[]{:S(2)}) collective-permute-start(bf16[264,128]{1,0:T(8,128)(2,1)S(1)} %get-tuple-element.151), channel_id=1, source_target_pairs={{0,7},{1,6},{2,5},{3,4},{4,3},{5,2},{6,1},{7,0},{8,15},{9,14},{10,... | collective-permute-start | bytes 202760 | tf_op jit(solution)/shard_map/ppermute | solution.py:414
  111.2 9.5 %collective-permute-start.45 = (bf16[264,128]{1,0:T(8,128)(2,1)S(1)}, bf16[264,128]{1,0:T(8,128)(2,1)S(1)}, u32[]{:S(2)}, u32[]{:S(2)}) collective-permute-start(bf16[264,128]{1,0:T(8,128)(2,1)S(1)} %get-tuple-element.155), channel_id=1, source_target_pairs={{0,8},{1,9},{2,10},{3,11},{4,12},{5,13},{6,14},{7,15},{8,0},{9,1},... | collective-permute-start | bytes 202760 | tf_op jit(solution)/shard_map/ppermute | solution.py:414
  112.8 10.5 %collective-permute-start.46 = (bf16[264,128]{1,0:T(8,128)(2,1)S(1)}, bf16[264,128]{1,0:T(8,128)(2,1)S(1)}, u32[]{:S(2)}, u32[]{:S(2)}) collective-permute-start(bf16[264,128]{1,0:T(8,128)(2,1)S(1)} %get-tuple-element.156), channel_id=1, source_target_pairs={{0,9},{1,8},{2,11},{3,10},{4,13},{5,12},{6,15},{7,14},{8,1},{9,0},... | collective-permute-start | bytes 202760 | tf_op jit(solution)/shard_map/ppermute | solution.py:414
  113.6 12.0 %collective-permute-start.47 = (bf16[264,128]{1,0:T(8,128)(2,1)S(1)}, bf16[264,128]{1,0:T(8,128)(2,1)S(1)}, u32[]{:S(2)}, u32[]{:S(2)}) collective-permute-start(bf16[264,128]{1,0:T(8,128)(2,1)S(1)} %get-tuple-element.157), channel_id=1, source_target_pairs={{0,1},{1,0},{2,3},{3,2},{4,5},{5,4},{6,7},{7,6},{8,9},{9,8},{10,11... | collective-permute-start | bytes 202760 | tf_op jit(solution)/shard_map/ppermute | solution.py:414
  114.3 12.6 %collective-permute-start.48 = (bf16[264,128]{1,0:T(8,128)(2,1)S(1)}, bf16[264,128]{1,0:T(8,128)(2,1)S(1)}, u32[]{:S(2)}, u32[]{:S(2)}) collective-permute-start(bf16[264,128]{1,0:T(8,128)(2,1)S(1)} %get-tuple-element.158), channel_id=1, source_target_pairs={{0,10},{1,11},{2,8},{3,9},{4,14},{5,15},{6,12},{7,13},{8,2},{9,3},... | collective-permute-start | bytes 202760 | tf_op jit(solution)/shard_map/ppermute | solution.py:414
  116.4 10.8 %collective-permute-start.49 = (bf16[264,128]{1,0:T(8,128)(2,1)S(1)}, bf16[264,128]{1,0:T(8,128)(2,1)S(1)}, u32[]{:S(2)}, u32[]{:S(2)}) collective-permute-start(bf16[264,128]{1,0:T(8,128)(2,1)S(1)} %get-tuple-element.159), channel_id=1, source_target_pairs={{0,11},{1,10},{2,9},{3,8},{4,15},{5,14},{6,13},{7,12},{8,3},{9,2},... | collective-permute-start | bytes 202760 | tf_op jit(solution)/shard_map/ppermute | solution.py:414
  120.7 10.0 %collective-permute-start.50 = (bf16[264,128]{1,0:T(8,128)(2,1)S(1)}, bf16[264,128]{1,0:T(8,128)(2,1)S(1)}, u32[]{:S(2)}, u32[]{:S(2)}) collective-permute-start(bf16[264,128]{1,0:T(8,128)(2,1)S(1)} %get-tuple-element.160), channel_id=1, source_target_pairs={{0,2},{1,3},{2,0},{3,1},{4,6},{5,7},{6,4},{7,5},{8,10},{9,11},{10,... | collective-permute-start | bytes 202760 | tf_op jit(solution)/shard_map/ppermute | solution.py:414
  123.2 8.1 %collective-permute-start.51 = (bf16[264,128]{1,0:T(8,128)(2,1)S(1)}, bf16[264,128]{1,0:T(8,128)(2,1)S(1)}, u32[]{:S(2)}, u32[]{:S(2)}) collective-permute-start(bf16[264,128]{1,0:T(8,128)(2,1)S(1)} %get-tuple-element.161), channel_id=1, source_target_pairs={{0,12},{1,13},{2,14},{3,15},{4,8},{5,9},{6,10},{7,11},{8,4},{9,5},... | collective-permute-start | bytes 202760 | tf_op jit(solution)/shard_map/ppermute | solution.py:414
  126.9 6.6 %collective-permute-start.53 = (bf16[264,128]{1,0:T(8,128)(2,1)S(1)}, bf16[264,128]{1,0:T(8,128)(2,1)S(1)}, u32[]{:S(2)}, u32[]{:S(2)}) collective-permute-start(bf16[264,128]{1,0:T(8,128)(2,1)S(1)} %get-tuple-element.163), channel_id=1, source_target_pairs={{0,3},{1,2},{2,1},{3,0},{4,7},{5,6},{6,5},{7,4},{8,11},{9,10},{10,... | collective-permute-start | bytes 202760 | tf_op jit(solution)/shard_map/ppermute | solution.py:414
  127.2 7.6 %collective-permute-start.54 = (bf16[264,128]{1,0:T(8,128)(2,1)S(1)}, bf16[264,128]{1,0:T(8,128)(2,1)S(1)}, u32[]{:S(2)}, u32[]{:S(2)}) collective-permute-start(bf16[264,128]{1,0:T(8,128)(2,1)S(1)} %get-tuple-element.164), channel_id=1, source_target_pairs={{0,14},{1,15},{2,12},{3,13},{4,10},{5,11},{6,8},{7,9},{8,6},{9,7},... | collective-permute-start | bytes 202760 | tf_op jit(solution)/shard_map/ppermute | solution.py:414
  130.7 7.1 %collective-permute-start.55 = (bf16[264,128]{1,0:T(8,128)(2,1)S(1)}, bf16[264,128]{1,0:T(8,128)(2,1)S(1)}, u32[]{:S(2)}, u32[]{:S(2)}) collective-permute-start(bf16[264,128]{1,0:T(8,128)(2,1)S(1)} %get-tuple-element.165), channel_id=1, source_target_pairs={{0,15},{1,14},{2,13},{3,12},{4,11},{5,10},{6,9},{7,8},{8,7},{9,6},... | collective-permute-start | bytes 202760 | tf_op jit(solution)/shard_map/ppermute | solution.py:414
  131.9 6.9 %collective-permute-start.57 = (bf16[264,128]{1,0:T(8,128)(2,1)S(1)}, bf16[264,128]{1,0:T(8,128)(2,1)S(1)}, u32[]{:S(2)}, u32[]{:S(2)}) collective-permute-start(bf16[264,128]{1,0:T(8,128)(2,1)S(1)} %get-tuple-element.167), channel_id=1, source_target_pairs={{0,5},{1,4},{2,7},{3,6},{4,1},{5,0},{6,3},{7,2},{8,13},{9,12},{10,... | collective-permute-start | bytes 202760 | tf_op jit(solution)/shard_map/ppermute | solution.py:414
  133.4 8.3 %collective-permute-start.58 = (bf16[264,128]{1,0:T(8,128)(2,1)S(1)}, bf16[264,128]{1,0:T(8,128)(2,1)S(1)}, u32[]{:S(2)}, u32[]{:S(2)}) collective-permute-start(bf16[264,128]{1,0:T(8,128)(2,1)S(1)} %get-tuple-element.168), channel_id=1, source_target_pairs={{0,6},{1,7},{2,4},{3,5},{4,2},{5,3},{6,0},{7,1},{8,14},{9,15},{10,... | collective-permute-start | bytes 202760 | tf_op jit(solution)/shard_map/ppermute | solution.py:414
  134.8 7.9 %collective-permute-start.59 = (bf16[264,128]{1,0:T(8,128)(2,1)S(1)}, bf16[264,128]{1,0:T(8,128)(2,1)S(1)}, u32[]{:S(2)}, u32[]{:S(2)}) collective-permute-start(bf16[264,128]{1,0:T(8,128)(2,1)S(1)} %get-tuple-element.169), channel_id=1, source_target_pairs={{0,7},{1,6},{2,5},{3,4},{4,3},{5,2},{6,1},{7,0},{8,15},{9,14},{10,... | collective-permute-start | bytes 202760 | tf_op jit(solution)/shard_map/ppermute | solution.py:414
  146.1 9.5 %collective-permute-start.60 = (bf16[264,128]{1,0:T(8,128)(2,1)S(1)}, bf16[264,128]{1,0:T(8,128)(2,1)S(1)}, u32[]{:S(2)}, u32[]{:S(2)}) collective-permute-start(bf16[264,128]{1,0:T(8,128)(2,1)S(1)} %get-tuple-element.174), channel_id=1, source_target_pairs={{0,8},{1,9},{2,10},{3,11},{4,12},{5,13},{6,14},{7,15},{8,0},{9,1},... | collective-permute-start | bytes 202760 | tf_op jit(solution)/shard_map/ppermute | solution.py:414
  147.5 10.8 %collective-permute-start.61 = (bf16[264,128]{1,0:T(8,128)(2,1)S(1)}, bf16[264,128]{1,0:T(8,128)(2,1)S(1)}, u32[]{:S(2)}, u32[]{:S(2)}) collective-permute-start(bf16[264,128]{1,0:T(8,128)(2,1)S(1)} %get-tuple-element.175), channel_id=1, source_target_pairs={{0,9},{1,8},{2,11},{3,10},{4,13},{5,12},{6,15},{7,14},{8,1},{9,0},... | collective-permute-start | bytes 202760 | tf_op jit(solution)/shard_map/ppermute | solution.py:414
  148.6 11.7 %collective-permute-start.62 = (bf16[264,128]{1,0:T(8,128)(2,1)S(1)}, bf16[264,128]{1,0:T(8,128)(2,1)S(1)}, u32[]{:S(2)}, u32[]{:S(2)}) collective-permute-start(bf16[264,128]{1,0:T(8,128)(2,1)S(1)} %get-tuple-element.176), channel_id=1, source_target_pairs={{0,1},{1,0},{2,3},{3,2},{4,5},{5,4},{6,7},{7,6},{8,9},{9,8},{10,11... | collective-permute-start | bytes 202760 | tf_op jit(solution)/shard_map/ppermute | solution.py:414
  149.2 12.6 %collective-permute-start.63 = (bf16[264,128]{1,0:T(8,128)(2,1)S(1)}, bf16[264,128]{1,0:T(8,128)(2,1)S(1)}, u32[]{:S(2)}, u32[]{:S(2)}) collective-permute-start(bf16[264,128]{1,0:T(8,128)(2,1)S(1)} %get-tuple-element.177), channel_id=1, source_target_pairs={{0,10},{1,11},{2,8},{3,9},{4,14},{5,15},{6,12},{7,13},{8,2},{9,3},... | collective-permute-start | bytes 202760 | tf_op jit(solution)/shard_map/ppermute | solution.py:414
  151.1 11.2 %collective-permute-start.64 = (bf16[264,128]{1,0:T(8,128)(2,1)S(1)}, bf16[264,128]{1,0:T(8,128)(2,1)S(1)}, u32[]{:S(2)}, u32[]{:S(2)}) collective-permute-start(bf16[264,128]{1,0:T(8,128)(2,1)S(1)} %get-tuple-element.178), channel_id=1, source_target_pairs={{0,11},{1,10},{2,9},{3,8},{4,15},{5,14},{6,13},{7,12},{8,3},{9,2},... | collective-permute-start | bytes 202760 | tf_op jit(solution)/shard_map/ppermute | solution.py:414
  155.7 9.6 %collective-permute-start.65 = (bf16[264,128]{1,0:T(8,128)(2,1)S(1)}, bf16[264,128]{1,0:T(8,128)(2,1)S(1)}, u32[]{:S(2)}, u32[]{:S(2)}) collective-permute-start(bf16[264,128]{1,0:T(8,128)(2,1)S(1)} %get-tuple-element.179), channel_id=1, source_target_pairs={{0,2},{1,3},{2,0},{3,1},{4,6},{5,7},{6,4},{7,5},{8,10},{9,11},{10,... | collective-permute-start | bytes 202760 | tf_op jit(solution)/shard_map/ppermute | solution.py:414
  158.3 8.1 %collective-permute-start.66 = (bf16[264,128]{1,0:T(8,128)(2,1)S(1)}, bf16[264,128]{1,0:T(8,128)(2,1)S(1)}, u32[]{:S(2)}, u32[]{:S(2)}) collective-permute-start(bf16[264,128]{1,0:T(8,128)(2,1)S(1)} %get-tuple-element.180), channel_id=1, source_target_pairs={{0,12},{1,13},{2,14},{3,15},{4,8},{5,9},{6,10},{7,11},{8,4},{9,5},... | collective-permute-start | bytes 202760 | tf_op jit(solution)/shard_map/ppermute | solution.py:414
  161.8 6.7 %collective-permute-start.68 = (bf16[264,128]{1,0:T(8,128)(2,1)S(1)}, bf16[264,128]{1,0:T(8,128)(2,1)S(1)}, u32[]{:S(2)}, u32[]{:S(2)}) collective-permute-start(bf16[264,128]{1,0:T(8,128)(2,1)S(1)} %get-tuple-element.182), channel_id=1, source_target_pairs={{0,3},{1,2},{2,1},{3,0},{4,7},{5,6},{6,5},{7,4},{8,11},{9,10},{10,... | collective-permute-start | bytes 202760 | tf_op jit(solution)/shard_map/ppermute | solution.py:414
  162.3 7.6 %collective-permute-start.69 = (bf16[264,128]{1,0:T(8,128)(2,1)S(1)}, bf16[264,128]{1,0:T(8,128)(2,1)S(1)}, u32[]{:S(2)}, u32[]{:S(2)}) collective-permute-start(bf16[264,128]{1,0:T(8,128)(2,1)S(1)} %get-tuple-element.183), channel_id=1, source_target_pairs={{0,14},{1,15},{2,12},{3,13},{4,10},{5,11},{6,8},{7,9},{8,6},{9,7},... | collective-permute-start | bytes 202760 | tf_op jit(solution)/shard_map/ppermute | solution.py:414
  165.3 7.2 %collective-permute-start.70 = (bf16[264,128]{1,0:T(8,128)(2,1)S(1)}, bf16[264,128]{1,0:T(8,128)(2,1)S(1)}, u32[]{:S(2)}, u32[]{:S(2)}) collective-permute-start(bf16[264,128]{1,0:T(8,128)(2,1)S(1)} %get-tuple-element.184), channel_id=1, source_target_pairs={{0,15},{1,14},{2,13},{3,12},{4,11},{5,10},{6,9},{7,8},{8,7},{9,6},... | collective-permute-start | bytes 202760 | tf_op jit(solution)/shard_map/ppermute | solution.py:414
  166.4 7.4 %collective-permute-start.72 = (bf16[264,128]{1,0:T(8,128)(2,1)S(1)}, bf16[264,128]{1,0:T(8,128)(2,1)S(1)}, u32[]{:S(2)}, u32[]{:S(2)}) collective-permute-start(bf16[264,128]{1,0:T(8,128)(2,1)S(1)} %get-tuple-element.186), channel_id=1, source_target_pairs={{0,5},{1,4},{2,7},{3,6},{4,1},{5,0},{6,3},{7,2},{8,13},{9,12},{10,... | collective-permute-start | bytes 202760 | tf_op jit(solution)/shard_map/ppermute | solution.py:414
  168.5 8.3 %collective-permute-start.73 = (bf16[264,128]{1,0:T(8,128)(2,1)S(1)}, bf16[264,128]{1,0:T(8,128)(2,1)S(1)}, u32[]{:S(2)}, u32[]{:S(2)}) collective-permute-start(bf16[264,128]{1,0:T(8,128)(2,1)S(1)} %get-tuple-element.187), channel_id=1, source_target_pairs={{0,6},{1,7},{2,4},{3,5},{4,2},{5,3},{6,0},{7,1},{8,14},{9,15},{10,... | collective-permute-start | bytes 202760 | tf_op jit(solution)/shard_map/ppermute | solution.py:414
  169.9 7.9 %collective-permute-start.74 = (bf16[264,128]{1,0:T(8,128)(2,1)S(1)}, bf16[264,128]{1,0:T(8,128)(2,1)S(1)}, u32[]{:S(2)}, u32[]{:S(2)}) collective-permute-start(bf16[264,128]{1,0:T(8,128)(2,1)S(1)} %get-tuple-element.188), channel_id=1, source_target_pairs={{0,7},{1,6},{2,5},{3,4},{4,3},{5,2},{6,1},{7,0},{8,15},{9,14},{10,... | collective-permute-start | bytes 202760 | tf_op jit(solution)/shard_map/ppermute | solution.py:414
  (20 other events, 133.2 us)

commit v15 on v12

--- a/solution.py
+++ b/solution.py
@@ -212,12 +212,37 @@
         message_ref[BCAP * cols :, :] = tail
 
 
-def gathered(arrived_refs, asked_ref, model_ref):
+def gathered(arrived_refs, first, asked_ref, model_ref):
     cols = model_ref.shape[0]
-    for peer, arrived_ref in enumerate(arrived_refs):
+    for peer, arrived_ref in enumerate(arrived_refs, first):
         for rank in range(BCAP):
             where = lanes(asked_ref[peer, rank])
             model_ref[:, where] += arrived_ref[rank * cols : (rank + 1) * cols, :].astype(F32)
+
+
+def read_asked(arrived_refs, table_ref, asked_ref, sem):
+    for peer, arrived_ref in enumerate(arrived_refs):
+        tail = arrived_ref[arrived_ref.shape[0] - TAIL :, :].astype(F32)
+        table_ref[peer : peer + 1, :] = tail[3:4].astype(jnp.int32)
+    copy = pltpu.make_async_copy(table_ref, asked_ref, sem)
+    copy.start()
+    return copy
+
+
+def early_kernel(early, *refs):
+    model_ref = refs[-1]
+    asked_ref, *arrived_refs = refs[: early + 1]
+    model_ref[...] = jnp.zeros(model_ref.shape, F32)
+    gathered(arrived_refs, 0, asked_ref, model_ref)
+
+
+def first_early_kernel(early, *refs):
+    arrived_refs = refs[:early]
+    model_ref, asked_ref, table_ref, sem = refs[early:]
+    copy = read_asked(arrived_refs, table_ref, asked_ref, sem)
+    model_ref[...] = jnp.zeros(model_ref.shape, F32)
+    copy.wait()
+    gathered(arrived_refs, 0, asked_ref, model_ref)
 
 
 def reply(squares, scale, asked_ref, model_ref, out_refs):
@@ -240,49 +265,49 @@
     return lax.fori_loop(0, cells // BS, one_block, jnp.zeros((cols, BS), F32), unroll=8)
 
 
-def first_cell_kernel(peers, *refs):
-    arrived_refs, out_refs = refs[:peers], refs[peers + 2 : 2 * peers + 2]
-    model_ref, beta_ref = refs[peers : peers + 2]
-    asked_ref, table_ref, sem = refs[2 * peers + 2 :]
-    cols, cells = model_ref.shape
-    for peer in range(peers):
-        tail = arrived_refs[peer][BCAP * cols :, :].astype(F32)
-        table_ref[peer : peer + 1, :] = tail[3:4].astype(jnp.int32)
-    copy = pltpu.make_async_copy(table_ref, asked_ref, sem)
-    copy.start()
-    beta = norm_of_tails(arrived_refs, cols)
-    beta_ref[...] = beta
-    model_ref[...] = jnp.zeros((cols, cells), F32)
-    copy.wait()
-    gathered(arrived_refs, asked_ref, model_ref)
-    reply(squares_of(model_ref), 1.0 / beta, asked_ref, model_ref, out_refs)
-
-
-def start_from(before_ref, scale, model_ref):
-    def one_block(block, carry):
-        model_ref[:, lanes(block)] = before_ref[:, lanes(block)] * -scale
-        return carry
-
-    lax.fori_loop(0, model_ref.shape[1] // BS, one_block, 0, unroll=8)
-
-
-def cell_kernel(peers, asked_ref, *refs):
-    arrived_refs, out_refs = refs[:peers], refs[peers + 5 :]
-    before_ref, alpha_ref, beta_before_ref, model_ref, beta_ref = refs[peers : peers + 5]
+def first_cell_kernel(peers, early, *refs):
+    arrived_refs, sum_ref, refs = refs[:peers], refs[peers], refs[peers + 1 :]
+    model_ref, beta_ref, *out_refs = refs[: peers + 2]
+    asked_ref, table_ref, sem = refs[peers + 2 :]
+    copy = read_asked(arrived_refs, table_ref, asked_ref, sem)
     beta = norm_of_tails(arrived_refs, model_ref.shape[0])
     beta_ref[...] = beta
-    start_from(before_ref, beta * beta / (alpha_ref[...] * beta_before_ref[...]), model_ref)
-    gathered(arrived_refs, asked_ref, model_ref)
+    model_ref[...] = sum_ref[...]
+    copy.wait()
+    gathered(arrived_refs[early:], early, asked_ref, model_ref)
     reply(squares_of(model_ref), 1.0 / beta, asked_ref, model_ref, out_refs)
 
 
-def last_cell_kernel(peers, asked_ref, *refs):
-    arrived_refs = refs[:peers]
-    before_ref, alpha_ref, beta_before_ref, model_ref, beta_ref, out_ref = refs[peers:]
+def start_from(sum_ref, before_ref, scale, model_ref):
+    def one_block(block, carry):
+        where = lanes(block)
+        model_ref[:, where] = sum_ref[:, where] - before_ref[:, where] * scale
+        return carry
+
+    lax.fori_loop(0, model_ref.shape[1] // BS, one_block, 0, unroll=8)
+
+
+def cell_kernel(peers, early, asked_ref, *refs):
+    arrived_refs, out_refs = refs[:peers], refs[peers + 6 :]
+    sum_ref, before_ref, alpha_ref, beta_before_ref, model_ref, beta_ref = refs[
+        peers : peers + 6
+    ]
     beta = norm_of_tails(arrived_refs, model_ref.shape[0])
     beta_ref[...] = beta
-    start_from(before_ref, beta * beta / (alpha_ref[...] * beta_before_ref[...]), model_ref)
-    gathered(arrived_refs, asked_ref, model_ref)
+    scale = beta * beta / (alpha_ref[...] * beta_before_ref[...])
+    start_from(sum_ref, before_ref, scale, model_ref)
+    gathered(arrived_refs[early:], early, asked_ref, model_ref)
+    reply(squares_of(model_ref), 1.0 / beta, asked_ref, model_ref, out_refs)
+
+
+def last_cell_kernel(peers, early, asked_ref, *refs):
+    arrived_refs = refs[:peers]
+    sum_ref, before_ref, alpha_ref, beta_before_ref, model_ref, beta_ref, out_ref = refs[peers:]
+    beta = norm_of_tails(arrived_refs, model_ref.shape[0])
+    beta_ref[...] = beta
+    scale = beta * beta / (alpha_ref[...] * beta_before_ref[...])
+    start_from(sum_ref, before_ref, scale, model_ref)
+    gathered(arrived_refs[early:], early, asked_ref, model_ref)
     squares = squares_of(model_ref) / (beta * beta)
     total = jnp.sum(squares, axis=1, keepdims=True)
     row = jnp.sum(jnp.where(diagonal(total.shape[0]), total, 0.0), axis=0, keepdims=True)
@@ -423,12 +448,18 @@
         [((slots,), jnp.int32, SMEM), messages[0], (ray_blocks.shape, BF16, VMEM)],
         [pltpu.SemaphoreType.DMA((3,))], 0, 8 << 20, 48 << 20,
     )(target, arrived[0], ray_blocks)
+    early = max(peers - 5, 1)
+    (summed,) = call(
+        functools.partial(first_early_kernel, early), "early_first", [VMEM] * early, [whole],
+        [SMEM((early, BS), jnp.int32), VMEM((early, BS), jnp.int32), pltpu.SemaphoreType.DMA],
+        0, 4 << 20,
+    )(*arrived[:early])
     model, beta, *replies, asked = call(
-        functools.partial(first_cell_kernel, peers), "cells_first", ins,
+        functools.partial(first_cell_kernel, peers, early), "cells_first", ins + [VMEM],
         [whole, tile] + messages + [((peers, BS), jnp.int32, SMEM)],
         [VMEM((peers, BS), jnp.int32), pltpu.SemaphoreType.DMA],
         0, 6 << 20,
-    )(*arrived)
+    )(*arrived, summed)
     models, betas, alphas = [model], [beta], []
     current = times
     for step in range(ITERS):
@@ -442,32 +473,38 @@
         alphas.append(made[peers])
         current = made[-1]
         arrived = exchange(made[:peers])
+        (summed,) = call(
+            functools.partial(early_kernel, early), "early", [SMEM] + [VMEM] * early, [whole],
+            (), 0, 4 << 20,
+        )(asked, *arrived[:early])
         if not last:
             model, beta, *replies = call(
-                functools.partial(cell_kernel, peers), "cells", [SMEM] + ins + [VMEM] * 3,
+                functools.partial(cell_kernel, peers, early), "cells", [SMEM] + ins + [VMEM] * 4,
                 [whole, tile] + messages, (), 0, 8 << 20,
-            )(asked, *arrived, models[-1], alphas[-1], betas[-1])
+            )(asked, *arrived, summed, models[-1], alphas[-1], betas[-1])
             models.append(model)
             betas.append(beta)
     model, beta, share = call(
-        functools.partial(last_cell_kernel, peers), "cells_last", [SMEM] + ins + [VMEM] * 3,
-        [whole, tile, ((8, BS), F32, VMEM)], (), 0, 8 << 20,
-    )(asked, *arrived, models[-1], alphas[-1], betas[-1])
+        functools.partial(last_cell_kernel, peers, early), "cells_last",
+        [SMEM] + ins + [VMEM] * 4, [whole, tile, ((8, BS), F32, VMEM)], (), 0, 8 << 20,
+    )(asked, *arrived, summed, models[-1], alphas[-1], betas[-1])
     betas.append(beta)
+    scratch = [VMEM(whole[0], F32), pltpu.SemaphoreType.DMA((CHUNKS,))]
+    (estimate,) = call(
+        estimate_kernel, "estimate", [VMEM] * (3 * ITERS + 1), [(whole[0], F32, HBM)], scratch,
+        0, 6 << 20,
+    )(*models, *alphas, *betas)
     reach, shares = peers, [share]
     while reach > 1:
         share = sum(shares[1:], shares[0])
+        if reach < peers:
+            share, estimate = lax.optimization_barrier((share, estimate))
         low = max(reach // 4, 1)
         shares = [share] + [
             lax.ppermute(share, "pair", [(one, one ^ step) for one in range(peers)])
             for step in range(low, reach, low)
         ]
         reach = low
-    scratch = [VMEM(whole[0], F32), pltpu.SemaphoreType.DMA((CHUNKS,))]
-    (estimate,) = call(
-        estimate_kernel, "estimate", [VMEM] * (3 * ITERS + 1), [(whole[0], F32, HBM)], scratch,
-        0, 6 << 20,
-    )(*models, *alphas, *betas)
     (model_vec,) = call(
         model_kernel, "model", [VMEM] * (len(shares) + 2), [(whole[0], F32, HBM)], scratch,
         0, 4 << 20,

time: 174 us -> 175 us (level)
  Pallas kernels: 25.5 us -> 28.4 us
  waiting for transfers between devices: 41.8 us -> 39.8 us
    pallas_call x3 -> x6, Pallas kernels: 6.95 us -> 9.83 us  [the longest x1 2.35 us: on_device(): call(functools.partial(cell_kernel, peers, early), 'cells', [SMEM] + ins...]
    ppermute x75, waiting for transfers between devices: 39.7 us -> 37.1 us  [exchange(): lax.ppermute(value, 'pair', [(one, one ^ step) for one in range(peers)])]
  transfers between devices with their start and end apart: 81 -> 81, of which waited for: 32 -> 28; matrix products, arithmetic and copies ran while one was open for 0% -> 0% of each run, Pallas kernels for 3% -> 4%
where the time goes in v15:
time: 175 us; the launch traced here: 174 us
  starting transfers between devices  103 us (59%)
  waiting for transfers between devices  39.8 us (23%)
  Pallas kernels  28.4 us (16%)
    ppermute x75, starting transfers between devices, exchange(): lax.ppermute(value, 'pair', [(one, one ^ step) for one in range(peers)])  97.1 us
    ppermute x75, waiting for transfers between devices, exchange(): lax.ppermute(value, 'pair', [(one, one ^ step) for one in range(peers)])  37.1 us
    pallas_call x2, Pallas kernels, on_device(): call(functools.partial(pair_kernel, peers), 'pairs_last' if last else 'pa...  6.91 us
    ppermute x6, starting transfers between devices, on_device(): lax.ppermute(share, 'pair', [(one, one ^ step) for one in range(peers)])  6.37 us
    pallas_call x1, Pallas kernels, on_device(): call(functools.partial(start_kernel, peers), 'start', [SMEM, HBM, HBM, HB...  5.7 us
  transfers between devices with their start and end apart: 81, of which 28 were waited for; matrix products, arithmetic and copies ran while one was open for 0% of the time, Pallas kernels for 4%

profile of v15, /device:TPU:0, one launch (start us, length us, event | category | flops | bytes accessed | tf_op | source)
XLA Modules:
  0.0 174.2 jit_solution(15296710625279676911)
XLA Ops:
  0.6 5.7 %start.1 = (bf16[264,128]{1,0:T(8,128)(2,1)}, bf16[264,128]{1,0:T(8,128)(2,1)}, bf16[264,128]{1,0:T(8,128)(2,1)}, bf16[264,128]{1,0:T(8,128)(2,1)}, bf16[264,128...) custom-call(s32[1]{0:T(128)} %bitcast.me_ref, ...), custom_call_target="tpu_custom_call" | custom-call | flops 268435456 | bytes 6291456 | tf_op jit(solution)/shard_map/start/pallas_call | solution.py:434
  6.3 4.1 %collective-permute-start = (bf16[264,128]{1,0:T(8,128)(2,1)}, bf16[264,128]{1,0:T(8,128)(2,1)S(1)}, u32[]{:S(2)}, u32[]{:S(2)}) collective-permute-start(bf16[264,128]{1,0:T(8,128)(2,1)} %get-tuple-element.102), channel_id=1, source_target_pairs={{0,8},{1,9},{2,10},{3,11},{4,12},{5,13},{6,14},{7,15},{8,0},{9,1},... | collective-permute-start | bytes 202760 | tf_op jit(solution)/shard_map/ppermute | solution.py:429
  10.7 1.7 collective-permute-start.3
  12.4 2.6 %collective-permute-start.4 = (bf16[264,128]{1,0:T(8,128)(2,1)}, bf16[264,128]{1,0:T(8,128)(2,1)S(1)}, u32[]{:S(2)}, u32[]{:S(2)}) collective-permute-start(bf16[264,128]{1,0:T(8,128)(2,1)} %get-tuple-element.106), channel_id=1, source_target_pairs={{0,10},{1,11},{2,8},{3,9},{4,14},{5,15},{6,12},{7,13},{8,2},{9,3},... | collective-permute-start | bytes 202760 | tf_op jit(solution)/shard_map/ppermute | solution.py:429
  15.5 2.1 %collective-permute-start.6 = (bf16[264,128]{1,0:T(8,128)(2,1)}, bf16[264,128]{1,0:T(8,128)(2,1)S(1)}, u32[]{:S(2)}, u32[]{:S(2)}) collective-permute-start(bf16[264,128]{1,0:T(8,128)(2,1)} %get-tuple-element.108), channel_id=1, source_target_pairs={{0,11},{1,10},{2,9},{3,8},{4,15},{5,14},{6,13},{7,12},{8,3},{9,2},... | collective-permute-start | bytes 202760 | tf_op jit(solution)/shard_map/ppermute | solution.py:429
  17.6 4.4 %collective-permute-start.7 = (bf16[264,128]{1,0:T(8,128)(2,1)}, bf16[264,128]{1,0:T(8,128)(2,1)S(1)}, u32[]{:S(2)}, u32[]{:S(2)}) collective-permute-start(bf16[264,128]{1,0:T(8,128)(2,1)} %get-tuple-element.109), channel_id=1, source_target_pairs={{0,4},{1,5},{2,6},{3,7},{4,0},{5,1},{6,2},{7,3},{8,12},{9,13},{10,... | collective-permute-start | bytes 202760 | tf_op jit(solution)/shard_map/ppermute | solution.py:429
  22.4 4.4 %collective-permute-start.10 = (bf16[264,128]{1,0:T(8,128)(2,1)}, bf16[264,128]{1,0:T(8,128)(2,1)S(1)}, u32[]{:S(2)}, u32[]{:S(2)}) collective-permute-start(bf16[264,128]{1,0:T(8,128)(2,1)} %get-tuple-element.112), channel_id=1, source_target_pairs={{0,13},{1,12},{2,15},{3,14},{4,9},{5,8},{6,11},{7,10},{8,5},{9,4},... | collective-permute-start | bytes 202760 | tf_op jit(solution)/shard_map/ppermute | solution.py:429
  27.6 1.9 %collective-permute-start.12 = (bf16[264,128]{1,0:T(8,128)(2,1)}, bf16[264,128]{1,0:T(8,128)(2,1)S(1)}, u32[]{:S(2)}, u32[]{:S(2)}) collective-permute-start(bf16[264,128]{1,0:T(8,128)(2,1)} %get-tuple-element.114), channel_id=1, source_target_pairs={{0,14},{1,15},{2,12},{3,13},{4,10},{5,11},{6,8},{7,9},{8,6},{9,7},... | collective-permute-start | bytes 202760 | tf_op jit(solution)/shard_map/ppermute | solution.py:429
  29.8 3.4 %collective-permute-start.14 = (bf16[264,128]{1,0:T(8,128)(2,1)}, bf16[264,128]{1,0:T(8,128)(2,1)S(1)}, u32[]{:S(2)}, u32[]{:S(2)}) collective-permute-start(bf16[264,128]{1,0:T(8,128)(2,1)} %get-tuple-element.116), channel_id=1, source_target_pairs={{0,15},{1,14},{2,13},{3,12},{4,11},{5,10},{6,9},{7,8},{8,7},{9,6},... | collective-permute-start | bytes 202760 | tf_op jit(solution)/shard_map/ppermute | solution.py:429
  34.7 2.9 %keep.1 = (s32[128]{0:T(128)S(1)}, bf16[264,128]{1,0:T(8,128)(2,1)S(1)}, bf16[8,16,128,128]{3,2,1,0:T(8,128)(2,1)S(1)}) custom-call(s32[128]{0:T(128)S(1)} %copy-done.2, bf16[264,128]{1,0:T(8,128)(2,1)S(1)} %copy-done.1, bf16[8,16,128,128]{3,2,1,0:T(8,128)(2,1)} %rays_hbm.3), custom_call_target="tpu_custom_call" | custom-call | bytes 8388608 | tf_op jit(solution)/shard_map/keep/pallas_call | solution.py:446
  37.6 1.1 early_first.1.refs_16_
  38.7 2.2 %cells_first.1 = (f32[64,8192]{1,0:T(8,128)S(1)}, f32[64,128]{1,0:T(8,128)S(1)}, bf16[264,128]{1,0:T(8,128)(2,1)S(1)}, bf16[264,128]{1,0:T(8,128)(2,1)S(1)}, bf1...) custom-call(bf16[264,128]{1,0:T(8,128)(2,1)S(1)} %get-tuple-element., ...), custom_call_target="tpu_custom_call" | custom-call | bytes 6291456 | tf_op jit(solution)/shard_map/cells_first/pallas_call | solution.py:457
  41.7 2.4 %collective-permute-start.17 = (bf16[264,128]{1,0:T(8,128)(2,1)S(1)}, bf16[264,128]{1,0:T(8,128)(2,1)S(1)}, u32[]{:S(2)}, u32[]{:S(2)}) collective-permute-start(bf16[264,128]{1,0:T(8,128)(2,1)S(1)} %get-tuple-element.122), channel_id=1, source_target_pairs={{0,9},{1,8},{2,11},{3,10},{4,13},{5,12},{6,15},{7,14},{8,1},{9,0},... | collective-permute-start | bytes 202760 | tf_op jit(solution)/shard_map/ppermute | solution.py:429
  44.0 1.8 %collective-permute-start.19 = (bf16[264,128]{1,0:T(8,128)(2,1)S(1)}, bf16[264,128]{1,0:T(8,128)(2,1)S(1)}, u32[]{:S(2)}, u32[]{:S(2)}) collective-permute-start(bf16[264,128]{1,0:T(8,128)(2,1)S(1)} %get-tuple-element.124), channel_id=1, source_target_pairs={{0,10},{1,11},{2,8},{3,9},{4,14},{5,15},{6,12},{7,13},{8,2},{9,3},... | collective-permute-start | bytes 202760 | tf_op jit(solution)/shard_map/ppermute | solution.py:429
  45.9 3.9 %collective-permute-done.15.refs_1_ = bf16[264,128]{1,0:T(8,128)(2,1)S(1)} collective-permute-done((bf16[264,128]{1,0:T(8,128)(2,1)S(1)}, bf16[264,128]{1,0:T(8,128)(2,1)S(1)}, u32[]{:S(2)}, u32[]{:S(2)}) %collective-permute-start.15) | collective-permute-done | bytes 67616 | tf_op jit(solution)/shard_map/ppermute | solution.py:429
  51.3 4.0 %collective-permute-start.23 = (bf16[264,128]{1,0:T(8,128)(2,1)S(1)}, bf16[264,128]{1,0:T(8,128)(2,1)S(1)}, u32[]{:S(2)}, u32[]{:S(2)}) collective-permute-start(bf16[264,128]{1,0:T(8,128)(2,1)S(1)} %get-tuple-element.128), channel_id=1, source_target_pairs={{0,12},{1,13},{2,14},{3,15},{4,8},{5,9},{6,10},{7,11},{8,4},{9,5},... | collective-permute-start | bytes 202760 | tf_op jit(solution)/shard_map/ppermute | solution.py:429
  56.0 1.8 %collective-permute-start.26 = (bf16[264,128]{1,0:T(8,128)(2,1)S(1)}, bf16[264,128]{1,0:T(8,128)(2,1)S(1)}, u32[]{:S(2)}, u32[]{:S(2)}) collective-permute-start(bf16[264,128]{1,0:T(8,128)(2,1)S(1)} %get-tuple-element.131), channel_id=1, source_target_pairs={{0,6},{1,7},{2,4},{3,5},{4,2},{5,3},{6,0},{7,1},{8,14},{9,15},{10,... | collective-permute-start | bytes 202760 | tf_op jit(solution)/shard_map/ppermute | solution.py:429
  58.1 2.8 %collective-permute-start.27 = (bf16[264,128]{1,0:T(8,128)(2,1)S(1)}, bf16[264,128]{1,0:T(8,128)(2,1)S(1)}, u32[]{:S(2)}, u32[]{:S(2)}) collective-permute-start(bf16[264,128]{1,0:T(8,128)(2,1)S(1)} %get-tuple-element.132), channel_id=1, source_target_pairs={{0,14},{1,15},{2,12},{3,13},{4,10},{5,11},{6,8},{7,9},{8,6},{9,7},... | collective-permute-start | bytes 202760 | tf_op jit(solution)/shard_map/ppermute | solution.py:429
  63.2 2.5 %collective-permute-done.27.refs_13_ = bf16[264,128]{1,0:T(8,128)(2,1)S(1)} collective-permute-done((bf16[264,128]{1,0:T(8,128)(2,1)S(1)}, bf16[264,128]{1,0:T(8,128)(2,1)S(1)}, u32[]{:S(2)}, u32[]{:S(2)}) %collective-permute-start.27) | collective-permute-done | bytes 67616 | tf_op jit(solution)/shard_map/ppermute | solution.py:429
  66.4 1.9 %collective-permute-done.29.refs_15_ = bf16[264,128]{1,0:T(8,128)(2,1)S(1)} collective-permute-done((bf16[264,128]{1,0:T(8,128)(2,1)S(1)}, bf16[264,128]{1,0:T(8,128)(2,1)S(1)}, u32[]{:S(2)}, u32[]{:S(2)}) %collective-permute-start.29) | collective-permute-done | bytes 67616 | tf_op jit(solution)/shard_map/ppermute | solution.py:429
  68.3 3.5 %pairs.1 = (bf16[264,128]{1,0:T(8,128)(2,1)S(1)}, bf16[264,128]{1,0:T(8,128)(2,1)S(1)}, bf16[264,128]{1,0:T(8,128)(2,1)S(1)}, bf16[264,128]{1,0:T(8,128)(2,1)S(1...) custom-call(s32[128]{0:T(128)S(1)} %get-tuple-element.118.target_ref, ...), custom_call_target="tpu_custom_call" | custom-call | flops 536870912 | bytes 8388608 | tf_op jit(solution)/shard_map/pairs/pallas_call | solution.py:468
  72.7 2.1 %collective-permute-start.32 = (bf16[264,128]{1,0:T(8,128)(2,1)S(1)}, bf16[264,128]{1,0:T(8,128)(2,1)S(1)}, u32[]{:S(2)}, u32[]{:S(2)}) collective-permute-start(bf16[264,128]{1,0:T(8,128)(2,1)S(1)} %get-tuple-element.140), channel_id=1, source_target_pairs={{0,9},{1,8},{2,11},{3,10},{4,13},{5,12},{6,15},{7,14},{8,1},{9,0},... | collective-permute-start | bytes 202760 | tf_op jit(solution)/shard_map/ppermute | solution.py:429
  75.8 1.3 collective-permute-start.34
  77.1 2.1 %collective-permute-done.30.refs_2_.refs_1_ = bf16[264,128]{1,0:T(8,128)(2,1)S(1)} collective-permute-done((bf16[264,128]{1,0:T(8,128)(2,1)S(1)}, bf16[264,128]{1,0:T(8,128)(2,1)S(1)}, u32[]{:S(2)}, u32[]{:S(2)}) %collective-permute-start.30) | collective-permute-done | bytes 67616 | tf_op jit(solution)/shard_map/ppermute | solution.py:429
  79.2 1.3 collective-permute-start.36
  80.4 3.7 %collective-permute-start.37 = (bf16[264,128]{1,0:T(8,128)(2,1)S(1)}, bf16[264,128]{1,0:T(8,128)(2,1)S(1)}, u32[]{:S(2)}, u32[]{:S(2)}) collective-permute-start(bf16[264,128]{1,0:T(8,128)(2,1)S(1)} %get-tuple-element.145), channel_id=1, source_target_pairs={{0,4},{1,5},{2,6},{3,7},{4,0},{5,1},{6,2},{7,3},{8,12},{9,13},{10,... | collective-permute-start | bytes 202760 | tf_op jit(solution)/shard_map/ppermute | solution.py:429
  85.2 2.2 %collective-permute-start.40 = (bf16[264,128]{1,0:T(8,128)(2,1)S(1)}, bf16[264,128]{1,0:T(8,128)(2,1)S(1)}, u32[]{:S(2)}, u32[]{:S(2)}) collective-permute-start(bf16[264,128]{1,0:T(8,128)(2,1)S(1)} %get-tuple-element.148), channel_id=1, source_target_pairs={{0,13},{1,12},{2,15},{3,14},{4,9},{5,8},{6,11},{7,10},{8,5},{9,4},... | collective-permute-start | bytes 202760 | tf_op jit(solution)/shard_map/ppermute | solution.py:429
  87.4 2.8 %collective-permute-start.41 = (bf16[264,128]{1,0:T(8,128)(2,1)S(1)}, bf16[264,128]{1,0:T(8,128)(2,1)S(1)}, u32[]{:S(2)}, u32[]{:S(2)}) collective-permute-start(bf16[264,128]{1,0:T(8,128)(2,1)S(1)} %get-tuple-element.149), channel_id=1, source_target_pairs={{0,6},{1,7},{2,4},{3,5},{4,2},{5,3},{6,0},{7,1},{8,14},{9,15},{10,... | collective-permute-start | bytes 202760 | tf_op jit(solution)/shard_map/ppermute | solution.py:429
  91.3 2.6 %collective-permute-start.44 = (bf16[264,128]{1,0:T(8,128)(2,1)S(1)}, bf16[264,128]{1,0:T(8,128)(2,1)S(1)}, u32[]{:S(2)}, u32[]{:S(2)}) collective-permute-start(bf16[264,128]{1,0:T(8,128)(2,1)S(1)} %get-tuple-element.152), channel_id=1, source_target_pairs={{0,15},{1,14},{2,13},{3,12},{4,11},{5,10},{6,9},{7,8},{8,7},{9,6},... | collective-permute-start | bytes 202760 | tf_op jit(solution)/shard_map/ppermute | solution.py:429
  93.9 1.1 early.2.refs_16_
  95.1 2.5 %collective-permute-done.42.refs_13_ = bf16[264,128]{1,0:T(8,128)(2,1)S(1)} collective-permute-done((bf16[264,128]{1,0:T(8,128)(2,1)S(1)}, bf16[264,128]{1,0:T(8,128)(2,1)S(1)}, u32[]{:S(2)}, u32[]{:S(2)}) %collective-permute-start.42) | collective-permute-done | bytes 67616 | tf_op jit(solution)/shard_map/ppermute | solution.py:429
  98.4 2.4 %cells.1 = (f32[64,8192]{1,0:T(8,128)S(1)}, f32[64,128]{1,0:T(8,128)S(1)}, bf16[264,128]{1,0:T(8,128)(2,1)S(1)}, bf16[264,128]{1,0:T(8,128)(2,1)S(1)}, bf16[264,...) custom-call(s32[16,128]{1,0:T(8,128)S(1)} %get-tuple-element.117.ref, ...), custom_call_target="tpu_custom_call" | custom-call | bytes 8388608 | tf_op jit(solution)/shard_map/cells/pallas_call | solution.py:481
  101.4 1.9 %collective-permute-start.46 = (bf16[264,128]{1,0:T(8,128)(2,1)S(1)}, bf16[264,128]{1,0:T(8,128)(2,1)S(1)}, u32[]{:S(2)}, u32[]{:S(2)}) collective-permute-start(bf16[264,128]{1,0:T(8,128)(2,1)S(1)} %get-tuple-element.157), channel_id=1, source_target_pairs={{0,1},{1,0},{2,3},{3,2},{4,5},{5,4},{6,7},{7,6},{8,9},{9,8},{10,11... | collective-permute-start | bytes 202760 | tf_op jit(solution)/shard_map/ppermute | solution.py:429
  103.9 1.9 %collective-permute-start.48 = (bf16[264,128]{1,0:T(8,128)(2,1)S(1)}, bf16[264,128]{1,0:T(8,128)(2,1)S(1)}, u32[]{:S(2)}, u32[]{:S(2)}) collective-permute-start(bf16[264,128]{1,0:T(8,128)(2,1)S(1)} %get-tuple-element.159), channel_id=1, source_target_pairs={{0,2},{1,3},{2,0},{3,1},{4,6},{5,7},{6,4},{7,5},{8,10},{9,11},{10,... | collective-permute-start | bytes 202760 | tf_op jit(solution)/shard_map/ppermute | solution.py:429
  105.8 1.6 collective-permute-start.49
  107.4 2.3 %collective-permute-done.45.refs_1_ = bf16[264,128]{1,0:T(8,128)(2,1)S(1)} collective-permute-done((bf16[264,128]{1,0:T(8,128)(2,1)S(1)}, bf16[264,128]{1,0:T(8,128)(2,1)S(1)}, u32[]{:S(2)}, u32[]{:S(2)}) %collective-permute-start.45) | collective-permute-done | bytes 67616 | tf_op jit(solution)/shard_map/ppermute | solution.py:429
  109.6 2.6 %collective-permute-done.47.refs_3_ = bf16[264,128]{1,0:T(8,128)(2,1)S(1)} collective-permute-done((bf16[264,128]{1,0:T(8,128)(2,1)S(1)}, bf16[264,128]{1,0:T(8,128)(2,1)S(1)}, u32[]{:S(2)}, u32[]{:S(2)}) %collective-permute-start.47) | collective-permute-done | bytes 67616 | tf_op jit(solution)/shard_map/ppermute | solution.py:429
  112.2 1.3 collective-permute-start.52
  113.5 1.7 collective-permute-start.53
  115.2 1.7 collective-permute-start.55
  116.9 1.5 collective-permute-start.56
  119.0 1.8 %collective-permute-start.57 = (bf16[264,128]{1,0:T(8,128)(2,1)S(1)}, bf16[264,128]{1,0:T(8,128)(2,1)S(1)}, u32[]{:S(2)}, u32[]{:S(2)}) collective-permute-start(bf16[264,128]{1,0:T(8,128)(2,1)S(1)} %get-tuple-element.168), channel_id=1, source_target_pairs={{0,14},{1,15},{2,12},{3,13},{4,10},{5,11},{6,8},{7,9},{8,6},{9,7},... | collective-permute-start | bytes 202760 | tf_op jit(solution)/shard_map/ppermute | solution.py:429
  122.3 1.1 collective-permute-start.59
  124.2 2.1 %collective-permute-done.57.refs_13_ = bf16[264,128]{1,0:T(8,128)(2,1)S(1)} collective-permute-done((bf16[264,128]{1,0:T(8,128)(2,1)S(1)}, bf16[264,128]{1,0:T(8,128)(2,1)S(1)}, u32[]{:S(2)}, u32[]{:S(2)}) %collective-permute-start.57) | collective-permute-done | bytes 67616 | tf_op jit(solution)/shard_map/ppermute | solution.py:429
  127.3 2.0 %collective-permute-done.59.refs_15_ = bf16[264,128]{1,0:T(8,128)(2,1)S(1)} collective-permute-done((bf16[264,128]{1,0:T(8,128)(2,1)S(1)}, bf16[264,128]{1,0:T(8,128)(2,1)S(1)}, u32[]{:S(2)}, u32[]{:S(2)}) %collective-permute-start.59) | collective-permute-done | bytes 67616 | tf_op jit(solution)/shard_map/ppermute | solution.py:429
  129.3 3.5 %pairs_last.1 = (bf16[264,128]{1,0:T(8,128)(2,1)S(1)}, bf16[264,128]{1,0:T(8,128)(2,1)S(1)}, bf16[264,128]{1,0:T(8,128)(2,1)S(1)}, bf16[264,128]{1,0:T(8,128)(2,...) custom-call(s32[128]{0:T(128)S(1)} %get-tuple-element.118.target_ref, ...), custom_call_target="tpu_custom_call" | custom-call | flops 536870912 | bytes 8388608 | tf_op jit(solution)/shard_map/pairs_last/pallas_call | solution.py:468
  133.6 2.3 %collective-permute-start.62 = (bf16[264,128]{1,0:T(8,128)(2,1)S(1)}, bf16[264,128]{1,0:T(8,128)(2,1)S(1)}, u32[]{:S(2)}, u32[]{:S(2)}) collective-permute-start(bf16[264,128]{1,0:T(8,128)(2,1)S(1)} %get-tuple-element.176), channel_id=1, source_target_pairs={{0,9},{1,8},{2,11},{3,10},{4,13},{5,12},{6,15},{7,14},{8,1},{9,0},... | collective-permute-start | bytes 202760 | tf_op jit(solution)/shard_map/ppermute | solution.py:429
  136.7 1.4 collective-permute-start.64
  138.0 2.6 %collective-permute-done.60.refs_2_.refs_1_ = bf16[264,128]{1,0:T(8,128)(2,1)S(1)} collective-permute-done((bf16[264,128]{1,0:T(8,128)(2,1)S(1)}, bf16[264,128]{1,0:T(8,128)(2,1)S(1)}, u32[]{:S(2)}, u32[]{:S(2)}) %collective-permute-start.60) | collective-permute-done | bytes 67616 | tf_op jit(solution)/shard_map/ppermute | solution.py:429
  141.9 2.9 %collective-permute-start.67 = (bf16[264,128]{1,0:T(8,128)(2,1)S(1)}, bf16[264,128]{1,0:T(8,128)(2,1)S(1)}, u32[]{:S(2)}, u32[]{:S(2)}) collective-permute-start(bf16[264,128]{1,0:T(8,128)(2,1)S(1)} %get-tuple-element.181), channel_id=1, source_target_pairs={{0,4},{1,5},{2,6},{3,7},{4,0},{5,1},{6,2},{7,3},{8,12},{9,13},{10,... | collective-permute-start | bytes 202760 | tf_op jit(solution)/shard_map/ppermute | solution.py:429
  144.9 1.3 collective-permute-start.68
  146.2 1.9 %collective-permute-start.70 = (bf16[264,128]{1,0:T(8,128)(2,1)S(1)}, bf16[264,128]{1,0:T(8,128)(2,1)S(1)}, u32[]{:S(2)}, u32[]{:S(2)}) collective-permute-start(bf16[264,128]{1,0:T(8,128)(2,1)S(1)} %get-tuple-element.184), channel_id=1, source_target_pairs={{0,13},{1,12},{2,15},{3,14},{4,9},{5,8},{6,11},{7,10},{8,5},{9,4},... | collective-permute-start | bytes 202760 | tf_op jit(solution)/shard_map/ppermute | solution.py:429
  148.0 2.8 %collective-permute-start.71 = (bf16[264,128]{1,0:T(8,128)(2,1)S(1)}, bf16[264,128]{1,0:T(8,128)(2,1)S(1)}, u32[]{:S(2)}, u32[]{:S(2)}) collective-permute-start(bf16[264,128]{1,0:T(8,128)(2,1)S(1)} %get-tuple-element.185), channel_id=1, source_target_pairs={{0,6},{1,7},{2,4},{3,5},{4,2},{5,3},{6,0},{7,1},{8,14},{9,15},{10,... | collective-permute-start | bytes 202760 | tf_op jit(solution)/shard_map/ppermute | solution.py:429
  152.7 1.9 %collective-permute-start.74 = (bf16[264,128]{1,0:T(8,128)(2,1)S(1)}, bf16[264,128]{1,0:T(8,128)(2,1)S(1)}, u32[]{:S(2)}, u32[]{:S(2)}) collective-permute-start(bf16[264,128]{1,0:T(8,128)(2,1)S(1)} %get-tuple-element.188), channel_id=1, source_target_pairs={{0,15},{1,14},{2,13},{3,12},{4,11},{5,10},{6,9},{7,8},{8,7},{9,6},... | collective-permute-start | bytes 202760 | tf_op jit(solution)/shard_map/ppermute | solution.py:429
  154.6 1.1 early.3.refs_16_
  155.8 2.4 %collective-permute-done.72.refs_13_ = bf16[264,128]{1,0:T(8,128)(2,1)S(1)} collective-permute-done((bf16[264,128]{1,0:T(8,128)(2,1)S(1)}, bf16[264,128]{1,0:T(8,128)(2,1)S(1)}, u32[]{:S(2)}, u32[]{:S(2)}) %collective-permute-start.72) | collective-permute-done | bytes 67616 | tf_op jit(solution)/shard_map/ppermute | solution.py:429
  158.3 1.6 collective-permute-done.74.refs_15_
  159.9 2.0 %cells_last.1 = (f32[64,8192]{1,0:T(8,128)S(1)}, f32[64,128]{1,0:T(8,128)S(1)}, f32[8,128]{1,0:T(8,128)S(1)}) custom-call(s32[16,128]{1,0:T(8,128)S(1)} %get-tuple-element.117.refs_0_.asked_ref, bf16[264,128]{1,0:T(8,128)(2,1)S(1)} %get-tuple-element.173.refs_1_.refs_0_, bf16[264,128]{1,0:T(8,128)(2,1)S(1)} %collective-permute-done.60.refs_2_.refs_1_, ...), custom_call_target="tpu_custom_call" | custom-call | bytes 8388608 | tf_op jit(solution)/shard_map/cells_last/pallas_call | solution.py:487
  161.9 2.3 %collective-permute-start.77 = (f32[8,128]{1,0:T(8,128)S(1)}, f32[8,128]{1,0:T(8,128)S(1)}, u32[]{:S(2)}, u32[]{:S(2)}) collective-permute-start(f32[8,128]{1,0:T(8,128)S(1)} %get-tuple-element.191), channel_id=1, source_target_pairs={{0,12},{1,13},{2,14},{3,15},{4,8},{5,9},{6,10},{7,11},{8,4},{9,5},... | collective-permute-start | bytes 12296 | tf_op jit(solution)/shard_map/ppermute | solution.py:504
  164.3 2.0 %collective-permute-start.75 = (f32[8,128]{1,0:T(8,128)S(1)}, f32[8,128]{1,0:T(8,128)S(1)}, u32[]{:S(2)}, u32[]{:S(2)}) collective-permute-start(f32[8,128]{1,0:T(8,128)S(1)} %get-tuple-element.191), channel_id=1, source_target_pairs={{0,4},{1,5},{2,6},{3,7},{4,0},{5,1},{6,2},{7,3},{8,12},{9,13},{10,... | collective-permute-start | bytes 12296 | tf_op jit(solution)/shard_map/ppermute | solution.py:504
  166.4 1.5 estimate.1
  168.8 1.2 collective-permute-start.79
  170.7 1.2 collective-permute-done.80.refs_3_
  172.5 1.5 model.1
  (117 shorter events, 27.6 us)
Async XLA Ops:
  6.3 8.6 %collective-permute-start = (bf16[264,128]{1,0:T(8,128)(2,1)}, bf16[264,128]{1,0:T(8,128)(2,1)S(1)}, u32[]{:S(2)}, u32[]{:S(2)}) collective-permute-start(bf16[264,128]{1,0:T(8,128)(2,1)} %get-tuple-element.102), channel_id=1, source_target_pairs={{0,8},{1,9},{2,10},{3,11},{4,12},{5,13},{6,14},{7,15},{8,0},{9,1},... | collective-permute-start | bytes 202760 | tf_op jit(solution)/shard_map/ppermute | solution.py:429
  10.4 7.1 %collective-permute-start.2 = (bf16[264,128]{1,0:T(8,128)(2,1)}, bf16[264,128]{1,0:T(8,128)(2,1)S(1)}, u32[]{:S(2)}, u32[]{:S(2)}) collective-permute-start(bf16[264,128]{1,0:T(8,128)(2,1)} %get-tuple-element.104), channel_id=1, source_target_pairs={{0,9},{1,8},{2,11},{3,10},{4,13},{5,12},{6,15},{7,14},{8,1},{9,0},... | collective-permute-start | bytes 202760 | tf_op jit(solution)/shard_map/ppermute | solution.py:429
  10.7 11.3 %collective-permute-start.3 = (bf16[264,128]{1,0:T(8,128)(2,1)}, bf16[264,128]{1,0:T(8,128)(2,1)S(1)}, u32[]{:S(2)}, u32[]{:S(2)}) collective-permute-start(bf16[264,128]{1,0:T(8,128)(2,1)} %get-tuple-element.105), channel_id=1, source_target_pairs={{0,2},{1,3},{2,0},{3,1},{4,6},{5,7},{6,4},{7,5},{8,10},{9,11},{10,... | collective-permute-start | bytes 202760 | tf_op jit(solution)/shard_map/ppermute | solution.py:429
  12.4 9.6 %collective-permute-start.4 = (bf16[264,128]{1,0:T(8,128)(2,1)}, bf16[264,128]{1,0:T(8,128)(2,1)S(1)}, u32[]{:S(2)}, u32[]{:S(2)}) collective-permute-start(bf16[264,128]{1,0:T(8,128)(2,1)} %get-tuple-element.106), channel_id=1, source_target_pairs={{0,10},{1,11},{2,8},{3,9},{4,14},{5,15},{6,12},{7,13},{8,2},{9,3},... | collective-permute-start | bytes 202760 | tf_op jit(solution)/shard_map/ppermute | solution.py:429
  15.0 7.4 %collective-permute-start.5 = (bf16[264,128]{1,0:T(8,128)(2,1)}, bf16[264,128]{1,0:T(8,128)(2,1)S(1)}, u32[]{:S(2)}, u32[]{:S(2)}) collective-permute-start(bf16[264,128]{1,0:T(8,128)(2,1)} %get-tuple-element.107), channel_id=1, source_target_pairs={{0,3},{1,2},{2,1},{3,0},{4,7},{5,6},{6,5},{7,4},{8,11},{9,10},{10,... | collective-permute-start | bytes 202760 | tf_op jit(solution)/shard_map/ppermute | solution.py:429
  15.5 11.2 %collective-permute-start.6 = (bf16[264,128]{1,0:T(8,128)(2,1)}, bf16[264,128]{1,0:T(8,128)(2,1)S(1)}, u32[]{:S(2)}, u32[]{:S(2)}) collective-permute-start(bf16[264,128]{1,0:T(8,128)(2,1)} %get-tuple-element.108), channel_id=1, source_target_pairs={{0,11},{1,10},{2,9},{3,8},{4,15},{5,14},{6,13},{7,12},{8,3},{9,2},... | collective-permute-start | bytes 202760 | tf_op jit(solution)/shard_map/ppermute | solution.py:429
  17.6 10.0 %collective-permute-start.7 = (bf16[264,128]{1,0:T(8,128)(2,1)}, bf16[264,128]{1,0:T(8,128)(2,1)S(1)}, u32[]{:S(2)}, u32[]{:S(2)}) collective-permute-start(bf16[264,128]{1,0:T(8,128)(2,1)} %get-tuple-element.109), channel_id=1, source_target_pairs={{0,4},{1,5},{2,6},{3,7},{4,0},{5,1},{6,2},{7,3},{8,12},{9,13},{10,... | collective-permute-start | bytes 202760 | tf_op jit(solution)/shard_map/ppermute | solution.py:429
  21.9 7.5 %collective-permute-start.8 = (bf16[264,128]{1,0:T(8,128)(2,1)}, bf16[264,128]{1,0:T(8,128)(2,1)S(1)}, u32[]{:S(2)}, u32[]{:S(2)}) collective-permute-start(bf16[264,128]{1,0:T(8,128)(2,1)} %get-tuple-element.110), channel_id=1, source_target_pairs={{0,12},{1,13},{2,14},{3,15},{4,8},{5,9},{6,10},{7,11},{8,4},{9,5},... | collective-permute-start | bytes 202760 | tf_op jit(solution)/shard_map/ppermute | solution.py:429
  22.0 7.8 %collective-permute-start.9 = (bf16[264,128]{1,0:T(8,128)(2,1)}, bf16[264,128]{1,0:T(8,128)(2,1)S(1)}, u32[]{:S(2)}, u32[]{:S(2)}) collective-permute-start(bf16[264,128]{1,0:T(8,128)(2,1)} %get-tuple-element.111), channel_id=1, source_target_pairs={{0,5},{1,4},{2,7},{3,6},{4,1},{5,0},{6,3},{7,2},{8,13},{9,12},{10,... | collective-permute-start | bytes 202760 | tf_op jit(solution)/shard_map/ppermute | solution.py:429
  22.4 16.3 %collective-permute-start.10 = (bf16[264,128]{1,0:T(8,128)(2,1)}, bf16[264,128]{1,0:T(8,128)(2,1)S(1)}, u32[]{:S(2)}, u32[]{:S(2)}) collective-permute-start(bf16[264,128]{1,0:T(8,128)(2,1)} %get-tuple-element.112), channel_id=1, source_target_pairs={{0,13},{1,12},{2,15},{3,14},{4,9},{5,8},{6,11},{7,10},{8,5},{9,4},... | collective-permute-start | bytes 202760 | tf_op jit(solution)/shard_map/ppermute | solution.py:429
  26.7 11.9 %collective-permute-start.11 = (bf16[264,128]{1,0:T(8,128)(2,1)}, bf16[264,128]{1,0:T(8,128)(2,1)S(1)}, u32[]{:S(2)}, u32[]{:S(2)}) collective-permute-start(bf16[264,128]{1,0:T(8,128)(2,1)} %get-tuple-element.113), channel_id=1, source_target_pairs={{0,6},{1,7},{2,4},{3,5},{4,2},{5,3},{6,0},{7,1},{8,14},{9,15},{10,... | collective-permute-start | bytes 202760 | tf_op jit(solution)/shard_map/ppermute | solution.py:429
  27.6 11.1 %collective-permute-start.12 = (bf16[264,128]{1,0:T(8,128)(2,1)}, bf16[264,128]{1,0:T(8,128)(2,1)S(1)}, u32[]{:S(2)}, u32[]{:S(2)}) collective-permute-start(bf16[264,128]{1,0:T(8,128)(2,1)} %get-tuple-element.114), channel_id=1, source_target_pairs={{0,14},{1,15},{2,12},{3,13},{4,10},{5,11},{6,8},{7,9},{8,6},{9,7},... | collective-permute-start | bytes 202760 | tf_op jit(solution)/shard_map/ppermute | solution.py:429
  29.5 9.2 %collective-permute-start.13 = (bf16[264,128]{1,0:T(8,128)(2,1)}, bf16[264,128]{1,0:T(8,128)(2,1)S(1)}, u32[]{:S(2)}, u32[]{:S(2)}) collective-permute-start(bf16[264,128]{1,0:T(8,128)(2,1)} %get-tuple-element.115), channel_id=1, source_target_pairs={{0,7},{1,6},{2,5},{3,4},{4,3},{5,2},{6,1},{7,0},{8,15},{9,14},{10,... | collective-permute-start | bytes 202760 | tf_op jit(solution)/shard_map/ppermute | solution.py:429
  29.8 8.9 %collective-permute-start.14 = (bf16[264,128]{1,0:T(8,128)(2,1)}, bf16[264,128]{1,0:T(8,128)(2,1)S(1)}, u32[]{:S(2)}, u32[]{:S(2)}) collective-permute-start(bf16[264,128]{1,0:T(8,128)(2,1)} %get-tuple-element.116), channel_id=1, source_target_pairs={{0,15},{1,14},{2,13},{3,12},{4,11},{5,10},{6,9},{7,8},{8,7},{9,6},... | collective-permute-start | bytes 202760 | tf_op jit(solution)/shard_map/ppermute | solution.py:429
  40.9 8.8 %collective-permute-start.15 = (bf16[264,128]{1,0:T(8,128)(2,1)S(1)}, bf16[264,128]{1,0:T(8,128)(2,1)S(1)}, u32[]{:S(2)}, u32[]{:S(2)}) collective-permute-start(bf16[264,128]{1,0:T(8,128)(2,1)S(1)} %get-tuple-element.120), channel_id=1, source_target_pairs={{0,8},{1,9},{2,10},{3,11},{4,12},{5,13},{6,14},{7,15},{8,0},{9,1},... | collective-permute-start | bytes 202760 | tf_op jit(solution)/shard_map/ppermute | solution.py:429
  41.4 8.4 %collective-permute-start.16 = (bf16[264,128]{1,0:T(8,128)(2,1)S(1)}, bf16[264,128]{1,0:T(8,128)(2,1)S(1)}, u32[]{:S(2)}, u32[]{:S(2)}) collective-permute-start(bf16[264,128]{1,0:T(8,128)(2,1)S(1)} %get-tuple-element.121), channel_id=1, source_target_pairs={{0,1},{1,0},{2,3},{3,2},{4,5},{5,4},{6,7},{7,6},{8,9},{9,8},{10,11... | collective-permute-start | bytes 202760 | tf_op jit(solution)/shard_map/ppermute | solution.py:429
  41.7 9.6 %collective-permute-start.17 = (bf16[264,128]{1,0:T(8,128)(2,1)S(1)}, bf16[264,128]{1,0:T(8,128)(2,1)S(1)}, u32[]{:S(2)}, u32[]{:S(2)}) collective-permute-start(bf16[264,128]{1,0:T(8,128)(2,1)S(1)} %get-tuple-element.122), channel_id=1, source_target_pairs={{0,9},{1,8},{2,11},{3,10},{4,13},{5,12},{6,15},{7,14},{8,1},{9,0},... | collective-permute-start | bytes 202760 | tf_op jit(solution)/shard_map/ppermute | solution.py:429
  44.0 7.2 %collective-permute-start.18 = (bf16[264,128]{1,0:T(8,128)(2,1)S(1)}, bf16[264,128]{1,0:T(8,128)(2,1)S(1)}, u32[]{:S(2)}, u32[]{:S(2)}) collective-permute-start(bf16[264,128]{1,0:T(8,128)(2,1)S(1)} %get-tuple-element.123), channel_id=1, source_target_pairs={{0,2},{1,3},{2,0},{3,1},{4,6},{5,7},{6,4},{7,5},{8,10},{9,11},{10,... | collective-permute-start | bytes 202760 | tf_op jit(solution)/shard_map/ppermute | solution.py:429
  44.0 11.3 %collective-permute-start.19 = (bf16[264,128]{1,0:T(8,128)(2,1)S(1)}, bf16[264,128]{1,0:T(8,128)(2,1)S(1)}, u32[]{:S(2)}, u32[]{:S(2)}) collective-permute-start(bf16[264,128]{1,0:T(8,128)(2,1)S(1)} %get-tuple-element.124), channel_id=1, source_target_pairs={{0,10},{1,11},{2,8},{3,9},{4,14},{5,15},{6,12},{7,13},{8,2},{9,3},... | collective-permute-start | bytes 202760 | tf_op jit(solution)/shard_map/ppermute | solution.py:429
  51.3 6.8 %collective-permute-start.22 = (bf16[264,128]{1,0:T(8,128)(2,1)S(1)}, bf16[264,128]{1,0:T(8,128)(2,1)S(1)}, u32[]{:S(2)}, u32[]{:S(2)}) collective-permute-start(bf16[264,128]{1,0:T(8,128)(2,1)S(1)} %get-tuple-element.127), channel_id=1, source_target_pairs={{0,4},{1,5},{2,6},{3,7},{4,0},{5,1},{6,2},{7,3},{8,12},{9,13},{10,... | collective-permute-start | bytes 202760 | tf_op jit(solution)/shard_map/ppermute | solution.py:429
  51.3 9.6 %collective-permute-start.23 = (bf16[264,128]{1,0:T(8,128)(2,1)S(1)}, bf16[264,128]{1,0:T(8,128)(2,1)S(1)}, u32[]{:S(2)}, u32[]{:S(2)}) collective-permute-start(bf16[264,128]{1,0:T(8,128)(2,1)S(1)} %get-tuple-element.128), channel_id=1, source_target_pairs={{0,12},{1,13},{2,14},{3,15},{4,8},{5,9},{6,10},{7,11},{8,4},{9,5},... | collective-permute-start | bytes 202760 | tf_op jit(solution)/shard_map/ppermute | solution.py:429
  55.3 6.5 %collective-permute-start.24 = (bf16[264,128]{1,0:T(8,128)(2,1)S(1)}, bf16[264,128]{1,0:T(8,128)(2,1)S(1)}, u32[]{:S(2)}, u32[]{:S(2)}) collective-permute-start(bf16[264,128]{1,0:T(8,128)(2,1)S(1)} %get-tuple-element.129), channel_id=1, source_target_pairs={{0,5},{1,4},{2,7},{3,6},{4,1},{5,0},{6,3},{7,2},{8,13},{9,12},{10,... | collective-permute-start | bytes 202760 | tf_op jit(solution)/shard_map/ppermute | solution.py:429
  55.3 7.1 %collective-permute-start.25 = (bf16[264,128]{1,0:T(8,128)(2,1)S(1)}, bf16[264,128]{1,0:T(8,128)(2,1)S(1)}, u32[]{:S(2)}, u32[]{:S(2)}) collective-permute-start(bf16[264,128]{1,0:T(8,128)(2,1)S(1)} %get-tuple-element.130), channel_id=1, source_target_pairs={{0,13},{1,12},{2,15},{3,14},{4,9},{5,8},{6,11},{7,10},{8,5},{9,4},... | collective-permute-start | bytes 202760 | tf_op jit(solution)/shard_map/ppermute | solution.py:429
  56.0 7.2 %collective-permute-start.26 = (bf16[264,128]{1,0:T(8,128)(2,1)S(1)}, bf16[264,128]{1,0:T(8,128)(2,1)S(1)}, u32[]{:S(2)}, u32[]{:S(2)}) collective-permute-start(bf16[264,128]{1,0:T(8,128)(2,1)S(1)} %get-tuple-element.131), channel_id=1, source_target_pairs={{0,6},{1,7},{2,4},{3,5},{4,2},{5,3},{6,0},{7,1},{8,14},{9,15},{10,... | collective-permute-start | bytes 202760 | tf_op jit(solution)/shard_map/ppermute | solution.py:429
  58.1 7.6 %collective-permute-start.27 = (bf16[264,128]{1,0:T(8,128)(2,1)S(1)}, bf16[264,128]{1,0:T(8,128)(2,1)S(1)}, u32[]{:S(2)}, u32[]{:S(2)}) collective-permute-start(bf16[264,128]{1,0:T(8,128)(2,1)S(1)} %get-tuple-element.132), channel_id=1, source_target_pairs={{0,14},{1,15},{2,12},{3,13},{4,10},{5,11},{6,8},{7,9},{8,6},{9,7},... | collective-permute-start | bytes 202760 | tf_op jit(solution)/shard_map/ppermute | solution.py:429
  71.8 7.4 %collective-permute-start.30 = (bf16[264,128]{1,0:T(8,128)(2,1)S(1)}, bf16[264,128]{1,0:T(8,128)(2,1)S(1)}, u32[]{:S(2)}, u32[]{:S(2)}) collective-permute-start(bf16[264,128]{1,0:T(8,128)(2,1)S(1)} %get-tuple-element.138), channel_id=1, source_target_pairs={{0,8},{1,9},{2,10},{3,11},{4,12},{5,13},{6,14},{7,15},{8,0},{9,1},... | collective-permute-start | bytes 202760 | tf_op jit(solution)/shard_map/ppermute | solution.py:429
  72.6 6.6 %collective-permute-start.31 = (bf16[264,128]{1,0:T(8,128)(2,1)S(1)}, bf16[264,128]{1,0:T(8,128)(2,1)S(1)}, u32[]{:S(2)}, u32[]{:S(2)}) collective-permute-start(bf16[264,128]{1,0:T(8,128)(2,1)S(1)} %get-tuple-element.139), channel_id=1, source_target_pairs={{0,1},{1,0},{2,3},{3,2},{4,5},{5,4},{6,7},{7,6},{8,9},{9,8},{10,11... | collective-permute-start | bytes 202760 | tf_op jit(solution)/shard_map/ppermute | solution.py:429
  72.7 7.7 %collective-permute-start.32 = (bf16[264,128]{1,0:T(8,128)(2,1)S(1)}, bf16[264,128]{1,0:T(8,128)(2,1)S(1)}, u32[]{:S(2)}, u32[]{:S(2)}) collective-permute-start(bf16[264,128]{1,0:T(8,128)(2,1)S(1)} %get-tuple-element.140), channel_id=1, source_target_pairs={{0,9},{1,8},{2,11},{3,10},{4,13},{5,12},{6,15},{7,14},{8,1},{9,0},... | collective-permute-start | bytes 202760 | tf_op jit(solution)/shard_map/ppermute | solution.py:429
  74.9 9.3 %collective-permute-start.33 = (bf16[264,128]{1,0:T(8,128)(2,1)S(1)}, bf16[264,128]{1,0:T(8,128)(2,1)S(1)}, u32[]{:S(2)}, u32[]{:S(2)}) collective-permute-start(bf16[264,128]{1,0:T(8,128)(2,1)S(1)} %get-tuple-element.141), channel_id=1, source_target_pairs={{0,2},{1,3},{2,0},{3,1},{4,6},{5,7},{6,4},{7,5},{8,10},{9,11},{10,... | collective-permute-start | bytes 202760 | tf_op jit(solution)/shard_map/ppermute | solution.py:429
  75.8 9.0 %collective-permute-start.34 = (bf16[264,128]{1,0:T(8,128)(2,1)S(1)}, bf16[264,128]{1,0:T(8,128)(2,1)S(1)}, u32[]{:S(2)}, u32[]{:S(2)}) collective-permute-start(bf16[264,128]{1,0:T(8,128)(2,1)S(1)} %get-tuple-element.142), channel_id=1, source_target_pairs={{0,10},{1,11},{2,8},{3,9},{4,14},{5,15},{6,12},{7,13},{8,2},{9,3},... | collective-permute-start | bytes 202760 | tf_op jit(solution)/shard_map/ppermute | solution.py:429
  79.2 8.3 %collective-permute-start.36 = (bf16[264,128]{1,0:T(8,128)(2,1)S(1)}, bf16[264,128]{1,0:T(8,128)(2,1)S(1)}, u32[]{:S(2)}, u32[]{:S(2)}) collective-permute-start(bf16[264,128]{1,0:T(8,128)(2,1)S(1)} %get-tuple-element.144), channel_id=1, source_target_pairs={{0,11},{1,10},{2,9},{3,8},{4,15},{5,14},{6,13},{7,12},{8,3},{9,2},... | collective-permute-start | bytes 202760 | tf_op jit(solution)/shard_map/ppermute | solution.py:429
  80.4 9.8 %collective-permute-start.37 = (bf16[264,128]{1,0:T(8,128)(2,1)S(1)}, bf16[264,128]{1,0:T(8,128)(2,1)S(1)}, u32[]{:S(2)}, u32[]{:S(2)}) collective-permute-start(bf16[264,128]{1,0:T(8,128)(2,1)S(1)} %get-tuple-element.145), channel_id=1, source_target_pairs={{0,4},{1,5},{2,6},{3,7},{4,0},{5,1},{6,2},{7,3},{8,12},{9,13},{10,... | collective-permute-start | bytes 202760 | tf_op jit(solution)/shard_map/ppermute | solution.py:429
  84.1 7.1 %collective-permute-start.38 = (bf16[264,128]{1,0:T(8,128)(2,1)S(1)}, bf16[264,128]{1,0:T(8,128)(2,1)S(1)}, u32[]{:S(2)}, u32[]{:S(2)}) collective-permute-start(bf16[264,128]{1,0:T(8,128)(2,1)S(1)} %get-tuple-element.146), channel_id=1, source_target_pairs={{0,12},{1,13},{2,14},{3,15},{4,8},{5,9},{6,10},{7,11},{8,4},{9,5},... | collective-permute-start | bytes 202760 | tf_op jit(solution)/shard_map/ppermute | solution.py:429
  84.8 6.6 %collective-permute-start.39 = (bf16[264,128]{1,0:T(8,128)(2,1)S(1)}, bf16[264,128]{1,0:T(8,128)(2,1)S(1)}, u32[]{:S(2)}, u32[]{:S(2)}) collective-permute-start(bf16[264,128]{1,0:T(8,128)(2,1)S(1)} %get-tuple-element.147), channel_id=1, source_target_pairs={{0,5},{1,4},{2,7},{3,6},{4,1},{5,0},{6,3},{7,2},{8,13},{9,12},{10,... | collective-permute-start | bytes 202760 | tf_op jit(solution)/shard_map/ppermute | solution.py:429
  85.2 9.8 %collective-permute-start.40 = (bf16[264,128]{1,0:T(8,128)(2,1)S(1)}, bf16[264,128]{1,0:T(8,128)(2,1)S(1)}, u32[]{:S(2)}, u32[]{:S(2)}) collective-permute-start(bf16[264,128]{1,0:T(8,128)(2,1)S(1)} %get-tuple-element.148), channel_id=1, source_target_pairs={{0,13},{1,12},{2,15},{3,14},{4,9},{5,8},{6,11},{7,10},{8,5},{9,4},... | collective-permute-start | bytes 202760 | tf_op jit(solution)/shard_map/ppermute | solution.py:429
  87.4 7.6 %collective-permute-start.41 = (bf16[264,128]{1,0:T(8,128)(2,1)S(1)}, bf16[264,128]{1,0:T(8,128)(2,1)S(1)}, u32[]{:S(2)}, u32[]{:S(2)}) collective-permute-start(bf16[264,128]{1,0:T(8,128)(2,1)S(1)} %get-tuple-element.149), channel_id=1, source_target_pairs={{0,6},{1,7},{2,4},{3,5},{4,2},{5,3},{6,0},{7,1},{8,14},{9,15},{10,... | collective-permute-start | bytes 202760 | tf_op jit(solution)/shard_map/ppermute | solution.py:429
  90.2 7.3 %collective-permute-start.42 = (bf16[264,128]{1,0:T(8,128)(2,1)S(1)}, bf16[264,128]{1,0:T(8,128)(2,1)S(1)}, u32[]{:S(2)}, u32[]{:S(2)}) collective-permute-start(bf16[264,128]{1,0:T(8,128)(2,1)S(1)} %get-tuple-element.150), channel_id=1, source_target_pairs={{0,14},{1,15},{2,12},{3,13},{4,10},{5,11},{6,8},{7,9},{8,6},{9,7},... | collective-permute-start | bytes 202760 | tf_op jit(solution)/shard_map/ppermute | solution.py:429
  91.3 7.1 %collective-permute-start.44 = (bf16[264,128]{1,0:T(8,128)(2,1)S(1)}, bf16[264,128]{1,0:T(8,128)(2,1)S(1)}, u32[]{:S(2)}, u32[]{:S(2)}) collective-permute-start(bf16[264,128]{1,0:T(8,128)(2,1)S(1)} %get-tuple-element.152), channel_id=1, source_target_pairs={{0,15},{1,14},{2,13},{3,12},{4,11},{5,10},{6,9},{7,8},{8,7},{9,6},... | collective-permute-start | bytes 202760 | tf_op jit(solution)/shard_map/ppermute | solution.py:429
  100.7 8.9 %collective-permute-start.45 = (bf16[264,128]{1,0:T(8,128)(2,1)S(1)}, bf16[264,128]{1,0:T(8,128)(2,1)S(1)}, u32[]{:S(2)}, u32[]{:S(2)}) collective-permute-start(bf16[264,128]{1,0:T(8,128)(2,1)S(1)} %get-tuple-element.156), channel_id=1, source_target_pairs={{0,8},{1,9},{2,10},{3,11},{4,12},{5,13},{6,14},{7,15},{8,0},{9,1},... | collective-permute-start | bytes 202760 | tf_op jit(solution)/shard_map/ppermute | solution.py:429
  101.4 8.2 %collective-permute-start.46 = (bf16[264,128]{1,0:T(8,128)(2,1)S(1)}, bf16[264,128]{1,0:T(8,128)(2,1)S(1)}, u32[]{:S(2)}, u32[]{:S(2)}) collective-permute-start(bf16[264,128]{1,0:T(8,128)(2,1)S(1)} %get-tuple-element.157), channel_id=1, source_target_pairs={{0,1},{1,0},{2,3},{3,2},{4,5},{5,4},{6,7},{7,6},{8,9},{9,8},{10,11... | collective-permute-start | bytes 202760 | tf_op jit(solution)/shard_map/ppermute | solution.py:429
  103.4 8.9 %collective-permute-start.47 = (bf16[264,128]{1,0:T(8,128)(2,1)S(1)}, bf16[264,128]{1,0:T(8,128)(2,1)S(1)}, u32[]{:S(2)}, u32[]{:S(2)}) collective-permute-start(bf16[264,128]{1,0:T(8,128)(2,1)S(1)} %get-tuple-element.158), channel_id=1, source_target_pairs={{0,9},{1,8},{2,11},{3,10},{4,13},{5,12},{6,15},{7,14},{8,1},{9,0},... | collective-permute-start | bytes 202760 | tf_op jit(solution)/shard_map/ppermute | solution.py:429
  103.9 9.6 %collective-permute-start.48 = (bf16[264,128]{1,0:T(8,128)(2,1)S(1)}, bf16[264,128]{1,0:T(8,128)(2,1)S(1)}, u32[]{:S(2)}, u32[]{:S(2)}) collective-permute-start(bf16[264,128]{1,0:T(8,128)(2,1)S(1)} %get-tuple-element.159), channel_id=1, source_target_pairs={{0,2},{1,3},{2,0},{3,1},{4,6},{5,7},{6,4},{7,5},{8,10},{9,11},{10,... | collective-permute-start | bytes 202760 | tf_op jit(solution)/shard_map/ppermute | solution.py:429
  105.8 9.5 %collective-permute-start.49 = (bf16[264,128]{1,0:T(8,128)(2,1)S(1)}, bf16[264,128]{1,0:T(8,128)(2,1)S(1)}, u32[]{:S(2)}, u32[]{:S(2)}) collective-permute-start(bf16[264,128]{1,0:T(8,128)(2,1)S(1)} %get-tuple-element.160), channel_id=1, source_target_pairs={{0,10},{1,11},{2,8},{3,9},{4,14},{5,15},{6,12},{7,13},{8,2},{9,3},... | collective-permute-start | bytes 202760 | tf_op jit(solution)/shard_map/ppermute | solution.py:429
  109.6 7.3 %collective-permute-start.51 = (bf16[264,128]{1,0:T(8,128)(2,1)S(1)}, bf16[264,128]{1,0:T(8,128)(2,1)S(1)}, u32[]{:S(2)}, u32[]{:S(2)}) collective-permute-start(bf16[264,128]{1,0:T(8,128)(2,1)S(1)} %get-tuple-element.162), channel_id=1, source_target_pairs={{0,11},{1,10},{2,9},{3,8},{4,15},{5,14},{6,13},{7,12},{8,3},{9,2},... | collective-permute-start | bytes 202760 | tf_op jit(solution)/shard_map/ppermute | solution.py:429
  112.2 6.8 %collective-permute-start.52 = (bf16[264,128]{1,0:T(8,128)(2,1)S(1)}, bf16[264,128]{1,0:T(8,128)(2,1)S(1)}, u32[]{:S(2)}, u32[]{:S(2)}) collective-permute-start(bf16[264,128]{1,0:T(8,128)(2,1)S(1)} %get-tuple-element.163), channel_id=1, source_target_pairs={{0,4},{1,5},{2,6},{3,7},{4,0},{5,1},{6,2},{7,3},{8,12},{9,13},{10,... | collective-permute-start | bytes 202760 | tf_op jit(solution)/shard_map/ppermute | solution.py:429
  113.5 7.3 %collective-permute-start.53 = (bf16[264,128]{1,0:T(8,128)(2,1)S(1)}, bf16[264,128]{1,0:T(8,128)(2,1)S(1)}, u32[]{:S(2)}, u32[]{:S(2)}) collective-permute-start(bf16[264,128]{1,0:T(8,128)(2,1)S(1)} %get-tuple-element.164), channel_id=1, source_target_pairs={{0,12},{1,13},{2,14},{3,15},{4,8},{5,9},{6,10},{7,11},{8,4},{9,5},... | collective-permute-start | bytes 202760 | tf_op jit(solution)/shard_map/ppermute | solution.py:429
  115.2 7.1 %collective-permute-start.54 = (bf16[264,128]{1,0:T(8,128)(2,1)S(1)}, bf16[264,128]{1,0:T(8,128)(2,1)S(1)}, u32[]{:S(2)}, u32[]{:S(2)}) collective-permute-start(bf16[264,128]{1,0:T(8,128)(2,1)S(1)} %get-tuple-element.165), channel_id=1, source_target_pairs={{0,5},{1,4},{2,7},{3,6},{4,1},{5,0},{6,3},{7,2},{8,13},{9,12},{10,... | collective-permute-start | bytes 202760 | tf_op jit(solution)/shard_map/ppermute | solution.py:429
  115.2 8.2 %collective-permute-start.55 = (bf16[264,128]{1,0:T(8,128)(2,1)S(1)}, bf16[264,128]{1,0:T(8,128)(2,1)S(1)}, u32[]{:S(2)}, u32[]{:S(2)}) collective-permute-start(bf16[264,128]{1,0:T(8,128)(2,1)S(1)} %get-tuple-element.166), channel_id=1, source_target_pairs={{0,13},{1,12},{2,15},{3,14},{4,9},{5,8},{6,11},{7,10},{8,5},{9,4},... | collective-permute-start | bytes 202760 | tf_op jit(solution)/shard_map/ppermute | solution.py:429
  116.9 7.3 %collective-permute-start.56 = (bf16[264,128]{1,0:T(8,128)(2,1)S(1)}, bf16[264,128]{1,0:T(8,128)(2,1)S(1)}, u32[]{:S(2)}, u32[]{:S(2)}) collective-permute-start(bf16[264,128]{1,0:T(8,128)(2,1)S(1)} %get-tuple-element.167), channel_id=1, source_target_pairs={{0,6},{1,7},{2,4},{3,5},{4,2},{5,3},{6,0},{7,1},{8,14},{9,15},{10,... | collective-permute-start | bytes 202760 | tf_op jit(solution)/shard_map/ppermute | solution.py:429
  119.0 7.3 %collective-permute-start.57 = (bf16[264,128]{1,0:T(8,128)(2,1)S(1)}, bf16[264,128]{1,0:T(8,128)(2,1)S(1)}, u32[]{:S(2)}, u32[]{:S(2)}) collective-permute-start(bf16[264,128]{1,0:T(8,128)(2,1)S(1)} %get-tuple-element.168), channel_id=1, source_target_pairs={{0,14},{1,15},{2,12},{3,13},{4,10},{5,11},{6,8},{7,9},{8,6},{9,7},... | collective-permute-start | bytes 202760 | tf_op jit(solution)/shard_map/ppermute | solution.py:429
  122.3 6.9 %collective-permute-start.59 = (bf16[264,128]{1,0:T(8,128)(2,1)S(1)}, bf16[264,128]{1,0:T(8,128)(2,1)S(1)}, u32[]{:S(2)}, u32[]{:S(2)}) collective-permute-start(bf16[264,128]{1,0:T(8,128)(2,1)S(1)} %get-tuple-element.170), channel_id=1, source_target_pairs={{0,15},{1,14},{2,13},{3,12},{4,11},{5,10},{6,9},{7,8},{8,7},{9,6},... | collective-permute-start | bytes 202760 | tf_op jit(solution)/shard_map/ppermute | solution.py:429
  132.8 7.8 %collective-permute-start.60 = (bf16[264,128]{1,0:T(8,128)(2,1)S(1)}, bf16[264,128]{1,0:T(8,128)(2,1)S(1)}, u32[]{:S(2)}, u32[]{:S(2)}) collective-permute-start(bf16[264,128]{1,0:T(8,128)(2,1)S(1)} %get-tuple-element.174), channel_id=1, source_target_pairs={{0,8},{1,9},{2,10},{3,11},{4,12},{5,13},{6,14},{7,15},{8,0},{9,1},... | collective-permute-start | bytes 202760 | tf_op jit(solution)/shard_map/ppermute | solution.py:429
  133.5 7.1 %collective-permute-start.61 = (bf16[264,128]{1,0:T(8,128)(2,1)S(1)}, bf16[264,128]{1,0:T(8,128)(2,1)S(1)}, u32[]{:S(2)}, u32[]{:S(2)}) collective-permute-start(bf16[264,128]{1,0:T(8,128)(2,1)S(1)} %get-tuple-element.175), channel_id=1, source_target_pairs={{0,1},{1,0},{2,3},{3,2},{4,5},{5,4},{6,7},{7,6},{8,9},{9,8},{10,11... | collective-permute-start | bytes 202760 | tf_op jit(solution)/shard_map/ppermute | solution.py:429
  133.6 8.3 %collective-permute-start.62 = (bf16[264,128]{1,0:T(8,128)(2,1)S(1)}, bf16[264,128]{1,0:T(8,128)(2,1)S(1)}, u32[]{:S(2)}, u32[]{:S(2)}) collective-permute-start(bf16[264,128]{1,0:T(8,128)(2,1)S(1)} %get-tuple-element.176), channel_id=1, source_target_pairs={{0,9},{1,8},{2,11},{3,10},{4,13},{5,12},{6,15},{7,14},{8,1},{9,0},... | collective-permute-start | bytes 202760 | tf_op jit(solution)/shard_map/ppermute | solution.py:429
  135.9 9.0 %collective-permute-start.63 = (bf16[264,128]{1,0:T(8,128)(2,1)S(1)}, bf16[264,128]{1,0:T(8,128)(2,1)S(1)}, u32[]{:S(2)}, u32[]{:S(2)}) collective-permute-start(bf16[264,128]{1,0:T(8,128)(2,1)S(1)} %get-tuple-element.177), channel_id=1, source_target_pairs={{0,2},{1,3},{2,0},{3,1},{4,6},{5,7},{6,4},{7,5},{8,10},{9,11},{10,... | collective-permute-start | bytes 202760 | tf_op jit(solution)/shard_map/ppermute | solution.py:429
  136.7 9.5 %collective-permute-start.64 = (bf16[264,128]{1,0:T(8,128)(2,1)S(1)}, bf16[264,128]{1,0:T(8,128)(2,1)S(1)}, u32[]{:S(2)}, u32[]{:S(2)}) collective-permute-start(bf16[264,128]{1,0:T(8,128)(2,1)S(1)} %get-tuple-element.178), channel_id=1, source_target_pairs={{0,10},{1,11},{2,8},{3,9},{4,14},{5,15},{6,12},{7,13},{8,2},{9,3},... | collective-permute-start | bytes 202760 | tf_op jit(solution)/shard_map/ppermute | solution.py:429
  140.6 7.5 %collective-permute-start.66 = (bf16[264,128]{1,0:T(8,128)(2,1)S(1)}, bf16[264,128]{1,0:T(8,128)(2,1)S(1)}, u32[]{:S(2)}, u32[]{:S(2)}) collective-permute-start(bf16[264,128]{1,0:T(8,128)(2,1)S(1)} %get-tuple-element.180), channel_id=1, source_target_pairs={{0,11},{1,10},{2,9},{3,8},{4,15},{5,14},{6,13},{7,12},{8,3},{9,2},... | collective-permute-start | bytes 202760 | tf_op jit(solution)/shard_map/ppermute | solution.py:429
  141.9 8.9 %collective-permute-start.67 = (bf16[264,128]{1,0:T(8,128)(2,1)S(1)}, bf16[264,128]{1,0:T(8,128)(2,1)S(1)}, u32[]{:S(2)}, u32[]{:S(2)}) collective-permute-start(bf16[264,128]{1,0:T(8,128)(2,1)S(1)} %get-tuple-element.181), channel_id=1, source_target_pairs={{0,4},{1,5},{2,6},{3,7},{4,0},{5,1},{6,2},{7,3},{8,12},{9,13},{10,... | collective-permute-start | bytes 202760 | tf_op jit(solution)/shard_map/ppermute | solution.py:429
  144.9 7.0 %collective-permute-start.68 = (bf16[264,128]{1,0:T(8,128)(2,1)S(1)}, bf16[264,128]{1,0:T(8,128)(2,1)S(1)}, u32[]{:S(2)}, u32[]{:S(2)}) collective-permute-start(bf16[264,128]{1,0:T(8,128)(2,1)S(1)} %get-tuple-element.182), channel_id=1, source_target_pairs={{0,12},{1,13},{2,14},{3,15},{4,8},{5,9},{6,10},{7,11},{8,4},{9,5},... | collective-permute-start | bytes 202760 | tf_op jit(solution)/shard_map/ppermute | solution.py:429
  146.2 6.6 %collective-permute-start.69 = (bf16[264,128]{1,0:T(8,128)(2,1)S(1)}, bf16[264,128]{1,0:T(8,128)(2,1)S(1)}, u32[]{:S(2)}, u32[]{:S(2)}) collective-permute-start(bf16[264,128]{1,0:T(8,128)(2,1)S(1)} %get-tuple-element.183), channel_id=1, source_target_pairs={{0,5},{1,4},{2,7},{3,6},{4,1},{5,0},{6,3},{7,2},{8,13},{9,12},{10,... | collective-permute-start | bytes 202760 | tf_op jit(solution)/shard_map/ppermute | solution.py:429
  146.2 9.6 %collective-permute-start.70 = (bf16[264,128]{1,0:T(8,128)(2,1)S(1)}, bf16[264,128]{1,0:T(8,128)(2,1)S(1)}, u32[]{:S(2)}, u32[]{:S(2)}) collective-permute-start(bf16[264,128]{1,0:T(8,128)(2,1)S(1)} %get-tuple-element.184), channel_id=1, source_target_pairs={{0,13},{1,12},{2,15},{3,14},{4,9},{5,8},{6,11},{7,10},{8,5},{9,4},... | collective-permute-start | bytes 202760 | tf_op jit(solution)/shard_map/ppermute | solution.py:429
  148.0 7.7 %collective-permute-start.71 = (bf16[264,128]{1,0:T(8,128)(2,1)S(1)}, bf16[264,128]{1,0:T(8,128)(2,1)S(1)}, u32[]{:S(2)}, u32[]{:S(2)}) collective-permute-start(bf16[264,128]{1,0:T(8,128)(2,1)S(1)} %get-tuple-element.185), channel_id=1, source_target_pairs={{0,6},{1,7},{2,4},{3,5},{4,2},{5,3},{6,0},{7,1},{8,14},{9,15},{10,... | collective-permute-start | bytes 202760 | tf_op jit(solution)/shard_map/ppermute | solution.py:429
  150.8 7.3 %collective-permute-start.72 = (bf16[264,128]{1,0:T(8,128)(2,1)S(1)}, bf16[264,128]{1,0:T(8,128)(2,1)S(1)}, u32[]{:S(2)}, u32[]{:S(2)}) collective-permute-start(bf16[264,128]{1,0:T(8,128)(2,1)S(1)} %get-tuple-element.186), channel_id=1, source_target_pairs={{0,14},{1,15},{2,12},{3,13},{4,10},{5,11},{6,8},{7,9},{8,6},{9,7},... | collective-permute-start | bytes 202760 | tf_op jit(solution)/shard_map/ppermute | solution.py:429
  152.7 7.2 %collective-permute-start.74 = (bf16[264,128]{1,0:T(8,128)(2,1)S(1)}, bf16[264,128]{1,0:T(8,128)(2,1)S(1)}, u32[]{:S(2)}, u32[]{:S(2)}) collective-permute-start(bf16[264,128]{1,0:T(8,128)(2,1)S(1)} %get-tuple-element.188), channel_id=1, source_target_pairs={{0,15},{1,14},{2,13},{3,12},{4,11},{5,10},{6,9},{7,8},{8,7},{9,6},... | collective-permute-start | bytes 202760 | tf_op jit(solution)/shard_map/ppermute | solution.py:429
  (20 other events, 120.6 us)

commit v16 on v12

--- a/solution.py
+++ b/solution.py
@@ -19,6 +19,11 @@
 SMEM = pltpu.SMEM
 HBM = pltpu.HBM
 CHUNKS = 8
+
+
+def pairs_of(peers):
+    half = peers // 2
+    return [(half + step, step) for step in range(1, half)]
 
 
 def diagonal(cols):
@@ -88,7 +93,14 @@
 def start_kernel(peers, me_ref, cells_hbm, counts_hbm, times_hbm, rays_hbm, *refs):
     message_refs = refs[:peers]
     target_ref, total_ref, table_ref, used_ref, cells_ref, counts_ref = refs[peers : peers + 6]
-    times_ref, rays_ref, sems, ray_sems = refs[peers + 6 :]
+    times_ref, rays_ref, place_ref, sems, ray_sems = refs[peers + 6 :]
+    me = me_ref[0]
+    core = me % 2
+    place_ref[me] = 0
+    place_ref[me ^ (peers // 2)] = 1
+    for index, (far, near) in enumerate(pairs_of(peers), 1):
+        place_ref[me ^ far] = 2 * index + core
+        place_ref[me ^ near] = 2 * index + 1 - core
     pair_count, slot_count = rays_ref.shape[:2]
     cols = times_ref.shape[0]
     owned = CELL_DEV // BS
@@ -124,8 +136,7 @@
         count = counts_ref[pair]
         for slot in range(slot_count):
             cell = cells_ref[pair, slot]
-            apart = (cell // owned) ^ me_ref[0]
-            owner = apart * 2 - jnp.where(apart < peers // 2, 0, peers - 1)
+            owner = place_ref[cell // owned]
             local = cell % owned
             used = used_ref[owner]
             rank = used
@@ -397,13 +408,17 @@
     totals = VMEM((spots + 1, cols, BS), F32)
     flops = 2 * slots * BS * BS * cols
 
+    def send(value, steps):
+        return lax.ppermute(value, "pair", [(i, i ^ steps[i % 2]) for i in range(peers)])
+
     def exchange(values):
-        half = peers // 2
-        steps = [i // 2 + i % 2 * half for i in range(peers)]
-        return [values[0]] + [
-            lax.ppermute(value, "pair", [(one, one ^ step) for one in range(peers)])
-            for value, step in zip(values[1:], steps[1:])
-        ]
+        back = [values[0], send(values[1], (peers // 2, peers // 2))]
+        for index, (far, near) in enumerate(pairs_of(peers), 1):
+            two = [
+                send(values[2 * index], (far, near)), send(values[2 * index + 1], (near, far))
+            ]
+            back += two[::-1] if far % 2 else two
+        return back
 
     me = lax.axis_index("pair").astype(jnp.int32).reshape(1)
     *outgoing, target = call(
@@ -412,7 +427,7 @@
         [
             totals, SMEM((spots,), jnp.int32), SMEM((peers,), jnp.int32),
             SMEM(block_cells.shape, jnp.int32), SMEM(block_counts.shape, jnp.int32),
-            VMEM(times.shape, F32), VMEM(ray_blocks.shape, BF16),
+            VMEM(times.shape, F32), VMEM(ray_blocks.shape, BF16), SMEM((peers,), jnp.int32),
             pltpu.SemaphoreType.DMA((3,)), pltpu.SemaphoreType.DMA((pair_count,)),
         ],
         flops, 6 << 20, 60 << 20,

time: 174 us -> 177 us (1.017)
  starting transfers between devices: 104 us -> 120 us
  waiting for transfers between devices: 41.8 us -> 29.3 us
    ppermute x75, starting transfers between devices: 97.3 us -> 113 us  [send(): lax.ppermute(value, 'pair', [(i, i ^ steps[i % 2]) for i in range(peers)])]
    ppermute x75, waiting for transfers between devices: 39.7 us -> 26.4 us  [send(): lax.ppermute(value, 'pair', [(i, i ^ steps[i % 2]) for i in range(peers)])]
  transfers between devices with their start and end apart: 81 -> 81, of which waited for: 32 -> 31; matrix products, arithmetic and copies ran while one was open for 0% -> 0% of each run, Pallas kernels for 3% -> 3%
where the time goes in v16:
time: 177 us
  starting transfers between devices  120 us (68%)
  waiting for transfers between devices  29.3 us (17%)
  Pallas kernels  25 us (14%)
    ppermute x75, starting transfers between devices, send(): lax.ppermute(value, 'pair', [(i, i ^ steps[i % 2]) for i in range(peers)])  113 us
    ppermute x75, waiting for transfers between devices, send(): lax.ppermute(value, 'pair', [(i, i ^ steps[i % 2]) for i in range(peers)])  26.4 us
    ppermute x6, starting transfers between devices, on_device(): lax.ppermute(share, 'pair', [(one, one ^ step) for one in range(peers)])  6.93 us
    pallas_call x2, Pallas kernels, on_device(): call(functools.partial(pair_kernel, peers), 'pairs_last' if last else 'pa...  6.9 us
    pallas_call x1, Pallas kernels, on_device(): call(functools.partial(start_kernel, peers), 'start', [SMEM, HBM, HBM, HB...  5.37 us
  transfers between devices with their start and end apart: 81, of which 31 were waited for; matrix products, arithmetic and copies ran while one was open for 0% of the time, Pallas kernels for 3%

profile of v16, /device:TPU:0, one launch (start us, length us, event | category | flops | bytes accessed | tf_op | source)
XLA Modules:
  0.0 177.2 jit_solution(18284317792091982790)
XLA Ops:
  0.6 5.4 %start.1 = (bf16[264,128]{1,0:T(8,128)(2,1)}, bf16[264,128]{1,0:T(8,128)(2,1)}, bf16[264,128]{1,0:T(8,128)(2,1)}, bf16[264,128]{1,0:T(8,128)(2,1)}, bf16[264,128...) custom-call(s32[1]{0:T(128)} %bitcast.me_ref, ...), custom_call_target="tpu_custom_call" | custom-call | flops 268435456 | bytes 6291456 | tf_op jit(solution)/shard_map/start/pallas_call | solution.py:424
  6.0 4.1 %collective-permute-start = (bf16[264,128]{1,0:T(8,128)(2,1)}, bf16[264,128]{1,0:T(8,128)(2,1)S(1)}, u32[]{:S(2)}, u32[]{:S(2)}) collective-permute-start(bf16[264,128]{1,0:T(8,128)(2,1)} %get-tuple-element.100), channel_id=1, source_target_pairs={{0,8},{1,9},{2,10},{3,11},{4,12},{5,13},{6,14},{7,15},{8,0},{9,1},... | collective-permute-start | bytes 202760 | tf_op jit(solution)/shard_map/ppermute | solution.py:412
  10.1 2.6 %collective-permute-start.2 = (bf16[264,128]{1,0:T(8,128)(2,1)}, bf16[264,128]{1,0:T(8,128)(2,1)S(1)}, u32[]{:S(2)}, u32[]{:S(2)}) collective-permute-start(bf16[264,128]{1,0:T(8,128)(2,1)} %get-tuple-element.102), channel_id=1, source_target_pairs={{0,9},{1,0},{2,11},{3,2},{4,13},{5,4},{6,15},{7,6},{8,1},{9,8},{10... | collective-permute-start | bytes 202760 | tf_op jit(solution)/shard_map/ppermute | solution.py:412
  12.7 1.3 collective-permute-start.3
  15.2 2.4 %collective-permute-done.1.refs_2_ = bf16[264,128]{1,0:T(8,128)(2,1)S(1)} collective-permute-done((bf16[264,128]{1,0:T(8,128)(2,1)}, bf16[264,128]{1,0:T(8,128)(2,1)S(1)}, u32[]{:S(2)}, u32[]{:S(2)}) %collective-permute-start.1) | collective-permute-done | bytes 67616 | tf_op jit(solution)/shard_map/ppermute | solution.py:412
  17.8 4.1 %collective-permute-start.7 = (bf16[264,128]{1,0:T(8,128)(2,1)}, bf16[264,128]{1,0:T(8,128)(2,1)S(1)}, u32[]{:S(2)}, u32[]{:S(2)}) collective-permute-start(bf16[264,128]{1,0:T(8,128)(2,1)} %get-tuple-element.107), channel_id=1, source_target_pairs={{0,12},{1,5},{2,14},{3,7},{4,8},{5,1},{6,10},{7,3},{8,4},{9,13},{1... | collective-permute-start | bytes 202760 | tf_op jit(solution)/shard_map/ppermute | solution.py:412
  22.3 1.1 collective-permute-start.9
  23.4 2.5 %collective-permute-start.10 = (bf16[264,128]{1,0:T(8,128)(2,1)}, bf16[264,128]{1,0:T(8,128)(2,1)S(1)}, u32[]{:S(2)}, u32[]{:S(2)}) collective-permute-start(bf16[264,128]{1,0:T(8,128)(2,1)} %get-tuple-element.110), channel_id=1, source_target_pairs={{0,13},{1,4},{2,15},{3,6},{4,9},{5,0},{6,11},{7,2},{8,5},{9,12},{1... | collective-permute-start | bytes 202760 | tf_op jit(solution)/shard_map/ppermute | solution.py:412
  25.9 3.4 %collective-permute-start.11 = (bf16[264,128]{1,0:T(8,128)(2,1)}, bf16[264,128]{1,0:T(8,128)(2,1)S(1)}, u32[]{:S(2)}, u32[]{:S(2)}) collective-permute-start(bf16[264,128]{1,0:T(8,128)(2,1)} %get-tuple-element.111), channel_id=1, source_target_pairs={{0,14},{1,7},{2,12},{3,5},{4,10},{5,3},{6,8},{7,1},{8,6},{9,15},{1... | collective-permute-start | bytes 202760 | tf_op jit(solution)/shard_map/ppermute | solution.py:412
  29.6 4.4 %collective-permute-start.14 = (bf16[264,128]{1,0:T(8,128)(2,1)}, bf16[264,128]{1,0:T(8,128)(2,1)S(1)}, u32[]{:S(2)}, u32[]{:S(2)}) collective-permute-start(bf16[264,128]{1,0:T(8,128)(2,1)} %get-tuple-element.114), channel_id=1, source_target_pairs={{0,15},{1,6},{2,13},{3,4},{4,11},{5,2},{6,9},{7,0},{8,7},{9,14},{1... | collective-permute-start | bytes 202760 | tf_op jit(solution)/shard_map/ppermute | solution.py:412
  35.5 2.9 %keep.1 = (s32[128]{0:T(128)S(1)}, bf16[264,128]{1,0:T(8,128)(2,1)S(1)}, bf16[8,16,128,128]{3,2,1,0:T(8,128)(2,1)S(1)}) custom-call(s32[128]{0:T(128)S(1)} %copy-done.2, bf16[264,128]{1,0:T(8,128)(2,1)S(1)} %copy-done.1, bf16[8,16,128,128]{3,2,1,0:T(8,128)(2,1)} %rays_hbm.3), custom_call_target="tpu_custom_call" | custom-call | bytes 8388608 | tf_op jit(solution)/shard_map/keep/pallas_call | solution.py:436
  38.5 2.5 %cells_first.1 = (f32[64,8192]{1,0:T(8,128)S(1)}, f32[64,128]{1,0:T(8,128)S(1)}, bf16[264,128]{1,0:T(8,128)(2,1)S(1)}, bf16[264,128]{1,0:T(8,128)(2,1)S(1)}, bf1...) custom-call(bf16[264,128]{1,0:T(8,128)(2,1)S(1)} %get-tuple-element., ...), custom_call_target="tpu_custom_call" | custom-call | bytes 6291456 | tf_op jit(solution)/shard_map/cells_first/pallas_call | solution.py:441
  41.2 2.6 %collective-permute-start.17 = (bf16[264,128]{1,0:T(8,128)(2,1)S(1)}, bf16[264,128]{1,0:T(8,128)(2,1)S(1)}, u32[]{:S(2)}, u32[]{:S(2)}) collective-permute-start(bf16[264,128]{1,0:T(8,128)(2,1)S(1)} %get-tuple-element.121), channel_id=1, source_target_pairs={{0,9},{1,0},{2,11},{3,2},{4,13},{5,4},{6,15},{7,6},{8,1},{9,8},{10... | collective-permute-start | bytes 202760 | tf_op jit(solution)/shard_map/ppermute | solution.py:412
  43.8 3.6 %collective-permute-start.18 = (bf16[264,128]{1,0:T(8,128)(2,1)S(1)}, bf16[264,128]{1,0:T(8,128)(2,1)S(1)}, u32[]{:S(2)}, u32[]{:S(2)}) collective-permute-start(bf16[264,128]{1,0:T(8,128)(2,1)S(1)} %get-tuple-element.122), channel_id=1, source_target_pairs={{0,10},{1,3},{2,8},{3,1},{4,14},{5,7},{6,12},{7,5},{8,2},{9,11},{1... | collective-permute-start | bytes 202760 | tf_op jit(solution)/shard_map/ppermute | solution.py:412
  48.1 3.5 %collective-permute-start.21 = (bf16[264,128]{1,0:T(8,128)(2,1)S(1)}, bf16[264,128]{1,0:T(8,128)(2,1)S(1)}, u32[]{:S(2)}, u32[]{:S(2)}) collective-permute-start(bf16[264,128]{1,0:T(8,128)(2,1)S(1)} %get-tuple-element.125), channel_id=1, source_target_pairs={{0,11},{1,2},{2,9},{3,0},{4,15},{5,6},{6,13},{7,4},{8,3},{9,10},{1... | collective-permute-start | bytes 202760 | tf_op jit(solution)/shard_map/ppermute | solution.py:412
  54.0 1.6 collective-permute-start.24
  55.6 1.9 %collective-permute-start.25 = (bf16[264,128]{1,0:T(8,128)(2,1)S(1)}, bf16[264,128]{1,0:T(8,128)(2,1)S(1)}, u32[]{:S(2)}, u32[]{:S(2)}) collective-permute-start(bf16[264,128]{1,0:T(8,128)(2,1)S(1)} %get-tuple-element.129), channel_id=1, source_target_pairs={{0,13},{1,4},{2,15},{3,6},{4,9},{5,0},{6,11},{7,2},{8,5},{9,12},{1... | collective-permute-start | bytes 202760 | tf_op jit(solution)/shard_map/ppermute | solution.py:412
  57.5 4.4 %collective-permute-start.26 = (bf16[264,128]{1,0:T(8,128)(2,1)S(1)}, bf16[264,128]{1,0:T(8,128)(2,1)S(1)}, u32[]{:S(2)}, u32[]{:S(2)}) collective-permute-start(bf16[264,128]{1,0:T(8,128)(2,1)S(1)} %get-tuple-element.130), channel_id=1, source_target_pairs={{0,14},{1,7},{2,12},{3,5},{4,10},{5,3},{6,8},{7,1},{8,6},{9,15},{1... | collective-permute-start | bytes 202760 | tf_op jit(solution)/shard_map/ppermute | solution.py:412
  62.0 4.4 %collective-permute-start.29 = (bf16[264,128]{1,0:T(8,128)(2,1)S(1)}, bf16[264,128]{1,0:T(8,128)(2,1)S(1)}, u32[]{:S(2)}, u32[]{:S(2)}) collective-permute-start(bf16[264,128]{1,0:T(8,128)(2,1)S(1)} %get-tuple-element.133), channel_id=1, source_target_pairs={{0,15},{1,6},{2,13},{3,4},{4,11},{5,2},{6,9},{7,0},{8,7},{9,14},{1... | collective-permute-start | bytes 202760 | tf_op jit(solution)/shard_map/ppermute | solution.py:412
  66.4 1.3 collective-permute-done.27.refs_13_
  68.7 3.4 %pairs.1 = (bf16[264,128]{1,0:T(8,128)(2,1)S(1)}, bf16[264,128]{1,0:T(8,128)(2,1)S(1)}, bf16[264,128]{1,0:T(8,128)(2,1)S(1)}, bf16[264,128]{1,0:T(8,128)(2,1)S(1...) custom-call(s32[128]{0:T(128)S(1)} %get-tuple-element.117.target_ref, ...), custom_call_target="tpu_custom_call" | custom-call | flops 536870912 | bytes 8388608 | tf_op jit(solution)/shard_map/pairs/pallas_call | solution.py:452
  72.2 1.6 collective-permute-start.30
  73.7 1.3 collective-permute-start.31
  75.0 1.4 collective-permute-start.32
  76.4 1.3 collective-permute-start.33
  77.7 1.6 collective-permute-start.34
  79.3 1.6 collective-permute-done.30.refs_1_
  80.9 3.2 %collective-permute-done.31.refs_2_ = bf16[264,128]{1,0:T(8,128)(2,1)S(1)} collective-permute-done((bf16[264,128]{1,0:T(8,128)(2,1)S(1)}, bf16[264,128]{1,0:T(8,128)(2,1)S(1)}, u32[]{:S(2)}, u32[]{:S(2)}) %collective-permute-start.31) | collective-permute-done | bytes 67616 | tf_op jit(solution)/shard_map/ppermute | solution.py:412
  84.4 1.8 %collective-permute-start.37 = (bf16[264,128]{1,0:T(8,128)(2,1)S(1)}, bf16[264,128]{1,0:T(8,128)(2,1)S(1)}, u32[]{:S(2)}, u32[]{:S(2)}) collective-permute-start(bf16[264,128]{1,0:T(8,128)(2,1)S(1)} %get-tuple-element.144), channel_id=1, source_target_pairs={{0,12},{1,5},{2,14},{3,7},{4,8},{5,1},{6,10},{7,3},{8,4},{9,13},{1... | collective-permute-start | bytes 202760 | tf_op jit(solution)/shard_map/ppermute | solution.py:412
  86.8 3.1 %collective-permute-start.40 = (bf16[264,128]{1,0:T(8,128)(2,1)S(1)}, bf16[264,128]{1,0:T(8,128)(2,1)S(1)}, u32[]{:S(2)}, u32[]{:S(2)}) collective-permute-start(bf16[264,128]{1,0:T(8,128)(2,1)S(1)} %get-tuple-element.147), channel_id=1, source_target_pairs={{0,13},{1,4},{2,15},{3,6},{4,9},{5,0},{6,11},{7,2},{8,5},{9,12},{1... | collective-permute-start | bytes 202760 | tf_op jit(solution)/shard_map/ppermute | solution.py:412
  89.9 2.3 %collective-permute-start.41 = (bf16[264,128]{1,0:T(8,128)(2,1)S(1)}, bf16[264,128]{1,0:T(8,128)(2,1)S(1)}, u32[]{:S(2)}, u32[]{:S(2)}) collective-permute-start(bf16[264,128]{1,0:T(8,128)(2,1)S(1)} %get-tuple-element.148), channel_id=1, source_target_pairs={{0,14},{1,7},{2,12},{3,5},{4,10},{5,3},{6,8},{7,1},{8,6},{9,15},{1... | collective-permute-start | bytes 202760 | tf_op jit(solution)/shard_map/ppermute | solution.py:412
  92.9 4.2 %collective-permute-start.44 = (bf16[264,128]{1,0:T(8,128)(2,1)S(1)}, bf16[264,128]{1,0:T(8,128)(2,1)S(1)}, u32[]{:S(2)}, u32[]{:S(2)}) collective-permute-start(bf16[264,128]{1,0:T(8,128)(2,1)S(1)} %get-tuple-element.151), channel_id=1, source_target_pairs={{0,15},{1,6},{2,13},{3,4},{4,11},{5,2},{6,9},{7,0},{8,7},{9,14},{1... | collective-permute-start | bytes 202760 | tf_op jit(solution)/shard_map/ppermute | solution.py:412
  97.4 1.3 collective-permute-done.42.refs_13_
  99.8 2.2 %cells.1 = (f32[64,8192]{1,0:T(8,128)S(1)}, f32[64,128]{1,0:T(8,128)S(1)}, bf16[264,128]{1,0:T(8,128)(2,1)S(1)}, bf16[264,128]{1,0:T(8,128)(2,1)S(1)}, bf16[264,...) custom-call(s32[16,128]{1,0:T(8,128)S(1)} %get-tuple-element.116.ask, ...), custom_call_target="tpu_custom_call" | custom-call | bytes 8388608 | tf_op jit(solution)/shard_map/cells/pallas_call | solution.py:461
  102.0 1.1 collective-permute-start.45
  103.7 2.2 %collective-permute-start.47 = (bf16[264,128]{1,0:T(8,128)(2,1)S(1)}, bf16[264,128]{1,0:T(8,128)(2,1)S(1)}, u32[]{:S(2)}, u32[]{:S(2)}) collective-permute-start(bf16[264,128]{1,0:T(8,128)(2,1)S(1)} %get-tuple-element.157), channel_id=1, source_target_pairs={{0,9},{1,0},{2,11},{3,2},{4,13},{5,4},{6,15},{7,6},{8,1},{9,8},{10... | collective-permute-start | bytes 202760 | tf_op jit(solution)/shard_map/ppermute | solution.py:412
  105.8 2.5 %collective-permute-start.48 = (bf16[264,128]{1,0:T(8,128)(2,1)S(1)}, bf16[264,128]{1,0:T(8,128)(2,1)S(1)}, u32[]{:S(2)}, u32[]{:S(2)}) collective-permute-start(bf16[264,128]{1,0:T(8,128)(2,1)S(1)} %get-tuple-element.158), channel_id=1, source_target_pairs={{0,10},{1,3},{2,8},{3,1},{4,14},{5,7},{6,12},{7,5},{8,2},{9,11},{1... | collective-permute-start | bytes 202760 | tf_op jit(solution)/shard_map/ppermute | solution.py:412
  109.7 2.5 %collective-permute-start.50 = (bf16[264,128]{1,0:T(8,128)(2,1)S(1)}, bf16[264,128]{1,0:T(8,128)(2,1)S(1)}, u32[]{:S(2)}, u32[]{:S(2)}) collective-permute-start(bf16[264,128]{1,0:T(8,128)(2,1)S(1)} %get-tuple-element.160), channel_id=1, source_target_pairs={{0,3},{1,10},{2,1},{3,8},{4,7},{5,14},{6,5},{7,12},{8,11},{9,2},{1... | collective-permute-start | bytes 202760 | tf_op jit(solution)/shard_map/ppermute | solution.py:412
  112.1 2.1 %collective-permute-done.46.refs_2_ = bf16[264,128]{1,0:T(8,128)(2,1)S(1)} collective-permute-done((bf16[264,128]{1,0:T(8,128)(2,1)S(1)}, bf16[264,128]{1,0:T(8,128)(2,1)S(1)}, u32[]{:S(2)}, u32[]{:S(2)}) %collective-permute-start.46) | collective-permute-done | bytes 67616 | tf_op jit(solution)/shard_map/ppermute | solution.py:412
  114.3 2.5 %collective-permute-start.52 = (bf16[264,128]{1,0:T(8,128)(2,1)S(1)}, bf16[264,128]{1,0:T(8,128)(2,1)S(1)}, u32[]{:S(2)}, u32[]{:S(2)}) collective-permute-start(bf16[264,128]{1,0:T(8,128)(2,1)S(1)} %get-tuple-element.162), channel_id=1, source_target_pairs={{0,12},{1,5},{2,14},{3,7},{4,8},{5,1},{6,10},{7,3},{8,4},{9,13},{1... | collective-permute-start | bytes 202760 | tf_op jit(solution)/shard_map/ppermute | solution.py:412
  117.4 3.0 %collective-permute-start.55 = (bf16[264,128]{1,0:T(8,128)(2,1)S(1)}, bf16[264,128]{1,0:T(8,128)(2,1)S(1)}, u32[]{:S(2)}, u32[]{:S(2)}) collective-permute-start(bf16[264,128]{1,0:T(8,128)(2,1)S(1)} %get-tuple-element.165), channel_id=1, source_target_pairs={{0,13},{1,4},{2,15},{3,6},{4,9},{5,0},{6,11},{7,2},{8,5},{9,12},{1... | collective-permute-start | bytes 202760 | tf_op jit(solution)/shard_map/ppermute | solution.py:412
  120.4 2.4 %collective-permute-start.56 = (bf16[264,128]{1,0:T(8,128)(2,1)S(1)}, bf16[264,128]{1,0:T(8,128)(2,1)S(1)}, u32[]{:S(2)}, u32[]{:S(2)}) collective-permute-start(bf16[264,128]{1,0:T(8,128)(2,1)S(1)} %get-tuple-element.166), channel_id=1, source_target_pairs={{0,14},{1,7},{2,12},{3,5},{4,10},{5,3},{6,8},{7,1},{8,6},{9,15},{1... | collective-permute-start | bytes 202760 | tf_op jit(solution)/shard_map/ppermute | solution.py:412
  123.1 4.2 %collective-permute-start.59 = (bf16[264,128]{1,0:T(8,128)(2,1)S(1)}, bf16[264,128]{1,0:T(8,128)(2,1)S(1)}, u32[]{:S(2)}, u32[]{:S(2)}) collective-permute-start(bf16[264,128]{1,0:T(8,128)(2,1)S(1)} %get-tuple-element.169), channel_id=1, source_target_pairs={{0,15},{1,6},{2,13},{3,4},{4,11},{5,2},{6,9},{7,0},{8,7},{9,14},{1... | collective-permute-start | bytes 202760 | tf_op jit(solution)/shard_map/ppermute | solution.py:412
  128.7 1.1 collective-permute-done.58.refs_14_
  130.3 3.5 %pairs_last.1 = (bf16[264,128]{1,0:T(8,128)(2,1)S(1)}, bf16[264,128]{1,0:T(8,128)(2,1)S(1)}, bf16[264,128]{1,0:T(8,128)(2,1)S(1)}, bf16[264,128]{1,0:T(8,128)(2,...) custom-call(s32[128]{0:T(128)S(1)} %get-tuple-element.117.target_ref, ...), custom_call_target="tpu_custom_call" | custom-call | flops 536870912 | bytes 8388608 | tf_op jit(solution)/shard_map/pairs_last/pallas_call | solution.py:452
  133.7 1.1 collective-permute-start.60
  135.9 2.1 %collective-permute-start.62 = (bf16[264,128]{1,0:T(8,128)(2,1)S(1)}, bf16[264,128]{1,0:T(8,128)(2,1)S(1)}, u32[]{:S(2)}, u32[]{:S(2)}) collective-permute-start(bf16[264,128]{1,0:T(8,128)(2,1)S(1)} %get-tuple-element.176), channel_id=1, source_target_pairs={{0,9},{1,0},{2,11},{3,2},{4,13},{5,4},{6,15},{7,6},{8,1},{9,8},{10... | collective-permute-start | bytes 202760 | tf_op jit(solution)/shard_map/ppermute | solution.py:412
  138.0 1.8 %collective-permute-start.63 = (bf16[264,128]{1,0:T(8,128)(2,1)S(1)}, bf16[264,128]{1,0:T(8,128)(2,1)S(1)}, u32[]{:S(2)}, u32[]{:S(2)}) collective-permute-start(bf16[264,128]{1,0:T(8,128)(2,1)S(1)} %get-tuple-element.177), channel_id=1, source_target_pairs={{0,10},{1,3},{2,8},{3,1},{4,14},{5,7},{6,12},{7,5},{8,2},{9,11},{1... | collective-permute-start | bytes 202760 | tf_op jit(solution)/shard_map/ppermute | solution.py:412
  140.8 2.0 %collective-permute-done.60.refs_1_ = bf16[264,128]{1,0:T(8,128)(2,1)S(1)} collective-permute-done((bf16[264,128]{1,0:T(8,128)(2,1)S(1)}, bf16[264,128]{1,0:T(8,128)(2,1)S(1)}, u32[]{:S(2)}, u32[]{:S(2)}) %collective-permute-start.60) | collective-permute-done | bytes 67616 | tf_op jit(solution)/shard_map/ppermute | solution.py:412
  142.9 1.6 collective-permute-start.65
  145.2 1.2 collective-permute-start.66
  146.4 1.1 collective-permute-start.67
  147.6 1.4 collective-permute-start.69
  149.5 1.6 collective-permute-start.70
  151.2 4.0 %collective-permute-start.71 = (bf16[264,128]{1,0:T(8,128)(2,1)S(1)}, bf16[264,128]{1,0:T(8,128)(2,1)S(1)}, u32[]{:S(2)}, u32[]{:S(2)}) collective-permute-start(bf16[264,128]{1,0:T(8,128)(2,1)S(1)} %get-tuple-element.185), channel_id=1, source_target_pairs={{0,14},{1,7},{2,12},{3,5},{4,10},{5,3},{6,8},{7,1},{8,6},{9,15},{1... | collective-permute-start | bytes 202760 | tf_op jit(solution)/shard_map/ppermute | solution.py:412
  155.3 4.4 %collective-permute-start.74 = (bf16[264,128]{1,0:T(8,128)(2,1)S(1)}, bf16[264,128]{1,0:T(8,128)(2,1)S(1)}, u32[]{:S(2)}, u32[]{:S(2)}) collective-permute-start(bf16[264,128]{1,0:T(8,128)(2,1)S(1)} %get-tuple-element.188), channel_id=1, source_target_pairs={{0,15},{1,6},{2,13},{3,4},{4,11},{5,2},{6,9},{7,0},{8,7},{9,14},{1... | collective-permute-start | bytes 202760 | tf_op jit(solution)/shard_map/ppermute | solution.py:412
  159.8 1.5 collective-permute-done.72.refs_13_
  162.1 2.0 %cells_last.1 = (f32[64,8192]{1,0:T(8,128)S(1)}, f32[64,128]{1,0:T(8,128)S(1)}, f32[8,128]{1,0:T(8,128)S(1)}) custom-call(s32[16,128]{1,0:T(8,128)S(1)} %get-tuple-element.116.asked_ref, bf16[264,128]{1,0:T(8,128)(2,1)S(1)} %get-tuple-element.173.refs_0_, bf16[264,128]{1,0:T(8,128)(2,1)S(1)} %collective-permute-done.60.refs_1_, ...), custom_call_target="tpu_custom_call" | custom-call | bytes 8388608 | tf_op jit(solution)/shard_map/cells_last/pallas_call | solution.py:467
  164.1 1.7 collective-permute-start.77
  165.9 2.7 %collective-permute-start.75 = (f32[8,128]{1,0:T(8,128)S(1)}, f32[8,128]{1,0:T(8,128)S(1)}, u32[]{:S(2)}, u32[]{:S(2)}) collective-permute-start(f32[8,128]{1,0:T(8,128)S(1)} %get-tuple-element.190), channel_id=1, source_target_pairs={{0,4},{1,5},{2,6},{3,7},{4,0},{5,1},{6,2},{7,3},{8,12},{9,13},{10,... | collective-permute-start | bytes 12296 | tf_op jit(solution)/shard_map/ppermute | solution.py:477
  170.3 1.6 collective-permute-start.80
  172.8 1.5 estimate.1
  174.4 1.2 collective-permute-done.79.refs_2_
  175.6 1.5 model.1
  (114 shorter events, 22.6 us)
Async XLA Ops:
  6.0 8.3 %collective-permute-start = (bf16[264,128]{1,0:T(8,128)(2,1)}, bf16[264,128]{1,0:T(8,128)(2,1)S(1)}, u32[]{:S(2)}, u32[]{:S(2)}) collective-permute-start(bf16[264,128]{1,0:T(8,128)(2,1)} %get-tuple-element.100), channel_id=1, source_target_pairs={{0,8},{1,9},{2,10},{3,11},{4,12},{5,13},{6,14},{7,15},{8,0},{9,1},... | collective-permute-start | bytes 202760 | tf_op jit(solution)/shard_map/ppermute | solution.py:412
  10.1 7.5 %collective-permute-start.1 = (bf16[264,128]{1,0:T(8,128)(2,1)}, bf16[264,128]{1,0:T(8,128)(2,1)S(1)}, u32[]{:S(2)}, u32[]{:S(2)}) collective-permute-start(bf16[264,128]{1,0:T(8,128)(2,1)} %get-tuple-element.101), channel_id=1, source_target_pairs={{0,1},{1,8},{2,3},{3,10},{4,5},{5,12},{6,7},{7,14},{8,9},{9,0},{10... | collective-permute-start | bytes 202760 | tf_op jit(solution)/shard_map/ppermute | solution.py:412
  10.1 7.7 %collective-permute-start.2 = (bf16[264,128]{1,0:T(8,128)(2,1)}, bf16[264,128]{1,0:T(8,128)(2,1)S(1)}, u32[]{:S(2)}, u32[]{:S(2)}) collective-permute-start(bf16[264,128]{1,0:T(8,128)(2,1)} %get-tuple-element.102), channel_id=1, source_target_pairs={{0,9},{1,0},{2,11},{3,2},{4,13},{5,4},{6,15},{7,6},{8,1},{9,8},{10... | collective-permute-start | bytes 202760 | tf_op jit(solution)/shard_map/ppermute | solution.py:412
  12.7 9.6 %collective-permute-start.3 = (bf16[264,128]{1,0:T(8,128)(2,1)}, bf16[264,128]{1,0:T(8,128)(2,1)S(1)}, u32[]{:S(2)}, u32[]{:S(2)}) collective-permute-start(bf16[264,128]{1,0:T(8,128)(2,1)} %get-tuple-element.103), channel_id=1, source_target_pairs={{0,10},{1,3},{2,8},{3,1},{4,14},{5,7},{6,12},{7,5},{8,2},{9,11},{1... | collective-permute-start | bytes 202760 | tf_op jit(solution)/shard_map/ppermute | solution.py:412
  14.1 8.2 %collective-permute-start.4 = (bf16[264,128]{1,0:T(8,128)(2,1)}, bf16[264,128]{1,0:T(8,128)(2,1)S(1)}, u32[]{:S(2)}, u32[]{:S(2)}) collective-permute-start(bf16[264,128]{1,0:T(8,128)(2,1)} %get-tuple-element.104), channel_id=1, source_target_pairs={{0,2},{1,11},{2,0},{3,9},{4,6},{5,15},{6,4},{7,13},{8,10},{9,3},{1... | collective-permute-start | bytes 202760 | tf_op jit(solution)/shard_map/ppermute | solution.py:412
  14.3 9.1 %collective-permute-start.5 = (bf16[264,128]{1,0:T(8,128)(2,1)}, bf16[264,128]{1,0:T(8,128)(2,1)S(1)}, u32[]{:S(2)}, u32[]{:S(2)}) collective-permute-start(bf16[264,128]{1,0:T(8,128)(2,1)} %get-tuple-element.105), channel_id=1, source_target_pairs={{0,3},{1,10},{2,1},{3,8},{4,7},{5,14},{6,5},{7,12},{8,11},{9,2},{1... | collective-permute-start | bytes 202760 | tf_op jit(solution)/shard_map/ppermute | solution.py:412
  17.5 8.3 %collective-permute-start.6 = (bf16[264,128]{1,0:T(8,128)(2,1)}, bf16[264,128]{1,0:T(8,128)(2,1)S(1)}, u32[]{:S(2)}, u32[]{:S(2)}) collective-permute-start(bf16[264,128]{1,0:T(8,128)(2,1)} %get-tuple-element.106), channel_id=1, source_target_pairs={{0,11},{1,2},{2,9},{3,0},{4,15},{5,6},{6,13},{7,4},{8,3},{9,10},{1... | collective-permute-start | bytes 202760 | tf_op jit(solution)/shard_map/ppermute | solution.py:412
  17.8 11.4 %collective-permute-start.7 = (bf16[264,128]{1,0:T(8,128)(2,1)}, bf16[264,128]{1,0:T(8,128)(2,1)S(1)}, u32[]{:S(2)}, u32[]{:S(2)}) collective-permute-start(bf16[264,128]{1,0:T(8,128)(2,1)} %get-tuple-element.107), channel_id=1, source_target_pairs={{0,12},{1,5},{2,14},{3,7},{4,8},{5,1},{6,10},{7,3},{8,4},{9,13},{1... | collective-permute-start | bytes 202760 | tf_op jit(solution)/shard_map/ppermute | solution.py:412
  22.3 7.3 %collective-permute-start.8 = (bf16[264,128]{1,0:T(8,128)(2,1)}, bf16[264,128]{1,0:T(8,128)(2,1)S(1)}, u32[]{:S(2)}, u32[]{:S(2)}) collective-permute-start(bf16[264,128]{1,0:T(8,128)(2,1)} %get-tuple-element.108), channel_id=1, source_target_pairs={{0,4},{1,13},{2,6},{3,15},{4,0},{5,9},{6,2},{7,11},{8,12},{9,5},{1... | collective-permute-start | bytes 202760 | tf_op jit(solution)/shard_map/ppermute | solution.py:412
  22.3 7.3 %collective-permute-start.9 = (bf16[264,128]{1,0:T(8,128)(2,1)}, bf16[264,128]{1,0:T(8,128)(2,1)S(1)}, u32[]{:S(2)}, u32[]{:S(2)}) collective-permute-start(bf16[264,128]{1,0:T(8,128)(2,1)} %get-tuple-element.109), channel_id=1, source_target_pairs={{0,5},{1,12},{2,7},{3,14},{4,1},{5,8},{6,3},{7,10},{8,13},{9,4},{1... | collective-permute-start | bytes 202760 | tf_op jit(solution)/shard_map/ppermute | solution.py:412
  23.4 15.0 %collective-permute-start.10 = (bf16[264,128]{1,0:T(8,128)(2,1)}, bf16[264,128]{1,0:T(8,128)(2,1)S(1)}, u32[]{:S(2)}, u32[]{:S(2)}) collective-permute-start(bf16[264,128]{1,0:T(8,128)(2,1)} %get-tuple-element.110), channel_id=1, source_target_pairs={{0,13},{1,4},{2,15},{3,6},{4,9},{5,0},{6,11},{7,2},{8,5},{9,12},{1... | collective-permute-start | bytes 202760 | tf_op jit(solution)/shard_map/ppermute | solution.py:412
  25.9 12.6 %collective-permute-start.11 = (bf16[264,128]{1,0:T(8,128)(2,1)}, bf16[264,128]{1,0:T(8,128)(2,1)S(1)}, u32[]{:S(2)}, u32[]{:S(2)}) collective-permute-start(bf16[264,128]{1,0:T(8,128)(2,1)} %get-tuple-element.111), channel_id=1, source_target_pairs={{0,14},{1,7},{2,12},{3,5},{4,10},{5,3},{6,8},{7,1},{8,6},{9,15},{1... | collective-permute-start | bytes 202760 | tf_op jit(solution)/shard_map/ppermute | solution.py:412
  29.3 9.2 %collective-permute-start.12 = (bf16[264,128]{1,0:T(8,128)(2,1)}, bf16[264,128]{1,0:T(8,128)(2,1)S(1)}, u32[]{:S(2)}, u32[]{:S(2)}) collective-permute-start(bf16[264,128]{1,0:T(8,128)(2,1)} %get-tuple-element.112), channel_id=1, source_target_pairs={{0,6},{1,15},{2,4},{3,13},{4,2},{5,11},{6,0},{7,9},{8,14},{9,7},{1... | collective-permute-start | bytes 202760 | tf_op jit(solution)/shard_map/ppermute | solution.py:412
  29.6 8.9 %collective-permute-start.13 = (bf16[264,128]{1,0:T(8,128)(2,1)}, bf16[264,128]{1,0:T(8,128)(2,1)S(1)}, u32[]{:S(2)}, u32[]{:S(2)}) collective-permute-start(bf16[264,128]{1,0:T(8,128)(2,1)} %get-tuple-element.113), channel_id=1, source_target_pairs={{0,7},{1,14},{2,5},{3,12},{4,3},{5,10},{6,1},{7,8},{8,15},{9,6},{1... | collective-permute-start | bytes 202760 | tf_op jit(solution)/shard_map/ppermute | solution.py:412
  29.6 8.9 %collective-permute-start.14 = (bf16[264,128]{1,0:T(8,128)(2,1)}, bf16[264,128]{1,0:T(8,128)(2,1)S(1)}, u32[]{:S(2)}, u32[]{:S(2)}) collective-permute-start(bf16[264,128]{1,0:T(8,128)(2,1)} %get-tuple-element.114), channel_id=1, source_target_pairs={{0,15},{1,6},{2,13},{3,4},{4,11},{5,2},{6,9},{7,0},{8,7},{9,14},{1... | collective-permute-start | bytes 202760 | tf_op jit(solution)/shard_map/ppermute | solution.py:412
  41.0 7.1 %collective-permute-start.15 = (bf16[264,128]{1,0:T(8,128)(2,1)S(1)}, bf16[264,128]{1,0:T(8,128)(2,1)S(1)}, u32[]{:S(2)}, u32[]{:S(2)}) collective-permute-start(bf16[264,128]{1,0:T(8,128)(2,1)S(1)} %get-tuple-element.119), channel_id=1, source_target_pairs={{0,8},{1,9},{2,10},{3,11},{4,12},{5,13},{6,14},{7,15},{8,0},{9,1},... | collective-permute-start | bytes 202760 | tf_op jit(solution)/shard_map/ppermute | solution.py:412
  41.1 7.0 %collective-permute-start.16 = (bf16[264,128]{1,0:T(8,128)(2,1)S(1)}, bf16[264,128]{1,0:T(8,128)(2,1)S(1)}, u32[]{:S(2)}, u32[]{:S(2)}) collective-permute-start(bf16[264,128]{1,0:T(8,128)(2,1)S(1)} %get-tuple-element.120), channel_id=1, source_target_pairs={{0,1},{1,8},{2,3},{3,10},{4,5},{5,12},{6,7},{7,14},{8,9},{9,0},{10... | collective-permute-start | bytes 202760 | tf_op jit(solution)/shard_map/ppermute | solution.py:412
  41.2 10.5 %collective-permute-start.17 = (bf16[264,128]{1,0:T(8,128)(2,1)S(1)}, bf16[264,128]{1,0:T(8,128)(2,1)S(1)}, u32[]{:S(2)}, u32[]{:S(2)}) collective-permute-start(bf16[264,128]{1,0:T(8,128)(2,1)S(1)} %get-tuple-element.121), channel_id=1, source_target_pairs={{0,9},{1,0},{2,11},{3,2},{4,13},{5,4},{6,15},{7,6},{8,1},{9,8},{10... | collective-permute-start | bytes 202760 | tf_op jit(solution)/shard_map/ppermute | solution.py:412
  43.8 9.4 %collective-permute-start.18 = (bf16[264,128]{1,0:T(8,128)(2,1)S(1)}, bf16[264,128]{1,0:T(8,128)(2,1)S(1)}, u32[]{:S(2)}, u32[]{:S(2)}) collective-permute-start(bf16[264,128]{1,0:T(8,128)(2,1)S(1)} %get-tuple-element.122), channel_id=1, source_target_pairs={{0,10},{1,3},{2,8},{3,1},{4,14},{5,7},{6,12},{7,5},{8,2},{9,11},{1... | collective-permute-start | bytes 202760 | tf_op jit(solution)/shard_map/ppermute | solution.py:412
  47.4 6.6 %collective-permute-start.19 = (bf16[264,128]{1,0:T(8,128)(2,1)S(1)}, bf16[264,128]{1,0:T(8,128)(2,1)S(1)}, u32[]{:S(2)}, u32[]{:S(2)}) collective-permute-start(bf16[264,128]{1,0:T(8,128)(2,1)S(1)} %get-tuple-element.123), channel_id=1, source_target_pairs={{0,2},{1,11},{2,0},{3,9},{4,6},{5,15},{6,4},{7,13},{8,10},{9,3},{1... | collective-permute-start | bytes 202760 | tf_op jit(solution)/shard_map/ppermute | solution.py:412
  48.1 7.5 %collective-permute-start.20 = (bf16[264,128]{1,0:T(8,128)(2,1)S(1)}, bf16[264,128]{1,0:T(8,128)(2,1)S(1)}, u32[]{:S(2)}, u32[]{:S(2)}) collective-permute-start(bf16[264,128]{1,0:T(8,128)(2,1)S(1)} %get-tuple-element.124), channel_id=1, source_target_pairs={{0,3},{1,10},{2,1},{3,8},{4,7},{5,14},{6,5},{7,12},{8,11},{9,2},{1... | collective-permute-start | bytes 202760 | tf_op jit(solution)/shard_map/ppermute | solution.py:412
  48.1 9.4 %collective-permute-start.21 = (bf16[264,128]{1,0:T(8,128)(2,1)S(1)}, bf16[264,128]{1,0:T(8,128)(2,1)S(1)}, u32[]{:S(2)}, u32[]{:S(2)}) collective-permute-start(bf16[264,128]{1,0:T(8,128)(2,1)S(1)} %get-tuple-element.125), channel_id=1, source_target_pairs={{0,11},{1,2},{2,9},{3,0},{4,15},{5,6},{6,13},{7,4},{8,3},{9,10},{1... | collective-permute-start | bytes 202760 | tf_op jit(solution)/shard_map/ppermute | solution.py:412
  51.7 10.2 %collective-permute-start.22 = (bf16[264,128]{1,0:T(8,128)(2,1)S(1)}, bf16[264,128]{1,0:T(8,128)(2,1)S(1)}, u32[]{:S(2)}, u32[]{:S(2)}) collective-permute-start(bf16[264,128]{1,0:T(8,128)(2,1)S(1)} %get-tuple-element.126), channel_id=1, source_target_pairs={{0,12},{1,5},{2,14},{3,7},{4,8},{5,1},{6,10},{7,3},{8,4},{9,13},{1... | collective-permute-start | bytes 202760 | tf_op jit(solution)/shard_map/ppermute | solution.py:412
  53.2 8.7 %collective-permute-start.23 = (bf16[264,128]{1,0:T(8,128)(2,1)S(1)}, bf16[264,128]{1,0:T(8,128)(2,1)S(1)}, u32[]{:S(2)}, u32[]{:S(2)}) collective-permute-start(bf16[264,128]{1,0:T(8,128)(2,1)S(1)} %get-tuple-element.127), channel_id=1, source_target_pairs={{0,4},{1,13},{2,6},{3,15},{4,0},{5,9},{6,2},{7,11},{8,12},{9,5},{1... | collective-permute-start | bytes 202760 | tf_op jit(solution)/shard_map/ppermute | solution.py:412
  54.0 8.0 %collective-permute-start.24 = (bf16[264,128]{1,0:T(8,128)(2,1)S(1)}, bf16[264,128]{1,0:T(8,128)(2,1)S(1)}, u32[]{:S(2)}, u32[]{:S(2)}) collective-permute-start(bf16[264,128]{1,0:T(8,128)(2,1)S(1)} %get-tuple-element.128), channel_id=1, source_target_pairs={{0,5},{1,12},{2,7},{3,14},{4,1},{5,8},{6,3},{7,10},{8,13},{9,4},{1... | collective-permute-start | bytes 202760 | tf_op jit(solution)/shard_map/ppermute | solution.py:412
  55.6 10.8 %collective-permute-start.25 = (bf16[264,128]{1,0:T(8,128)(2,1)S(1)}, bf16[264,128]{1,0:T(8,128)(2,1)S(1)}, u32[]{:S(2)}, u32[]{:S(2)}) collective-permute-start(bf16[264,128]{1,0:T(8,128)(2,1)S(1)} %get-tuple-element.129), channel_id=1, source_target_pairs={{0,13},{1,4},{2,15},{3,6},{4,9},{5,0},{6,11},{7,2},{8,5},{9,12},{1... | collective-permute-start | bytes 202760 | tf_op jit(solution)/shard_map/ppermute | solution.py:412
  57.5 8.9 %collective-permute-start.26 = (bf16[264,128]{1,0:T(8,128)(2,1)S(1)}, bf16[264,128]{1,0:T(8,128)(2,1)S(1)}, u32[]{:S(2)}, u32[]{:S(2)}) collective-permute-start(bf16[264,128]{1,0:T(8,128)(2,1)S(1)} %get-tuple-element.130), channel_id=1, source_target_pairs={{0,14},{1,7},{2,12},{3,5},{4,10},{5,3},{6,8},{7,1},{8,6},{9,15},{1... | collective-permute-start | bytes 202760 | tf_op jit(solution)/shard_map/ppermute | solution.py:412
  61.9 6.8 %collective-permute-start.28 = (bf16[264,128]{1,0:T(8,128)(2,1)S(1)}, bf16[264,128]{1,0:T(8,128)(2,1)S(1)}, u32[]{:S(2)}, u32[]{:S(2)}) collective-permute-start(bf16[264,128]{1,0:T(8,128)(2,1)S(1)} %get-tuple-element.132), channel_id=1, source_target_pairs={{0,7},{1,14},{2,5},{3,12},{4,3},{5,10},{6,1},{7,8},{8,15},{9,6},{1... | collective-permute-start | bytes 202760 | tf_op jit(solution)/shard_map/ppermute | solution.py:412
  62.0 6.7 %collective-permute-start.29 = (bf16[264,128]{1,0:T(8,128)(2,1)S(1)}, bf16[264,128]{1,0:T(8,128)(2,1)S(1)}, u32[]{:S(2)}, u32[]{:S(2)}) collective-permute-start(bf16[264,128]{1,0:T(8,128)(2,1)S(1)} %get-tuple-element.133), channel_id=1, source_target_pairs={{0,15},{1,6},{2,13},{3,4},{4,11},{5,2},{6,9},{7,0},{8,7},{9,14},{1... | collective-permute-start | bytes 202760 | tf_op jit(solution)/shard_map/ppermute | solution.py:412
  72.2 8.7 %collective-permute-start.30 = (bf16[264,128]{1,0:T(8,128)(2,1)S(1)}, bf16[264,128]{1,0:T(8,128)(2,1)S(1)}, u32[]{:S(2)}, u32[]{:S(2)}) collective-permute-start(bf16[264,128]{1,0:T(8,128)(2,1)S(1)} %get-tuple-element.137), channel_id=1, source_target_pairs={{0,8},{1,9},{2,10},{3,11},{4,12},{5,13},{6,14},{7,15},{8,0},{9,1},... | collective-permute-start | bytes 202760 | tf_op jit(solution)/shard_map/ppermute | solution.py:412
  73.7 10.4 %collective-permute-start.31 = (bf16[264,128]{1,0:T(8,128)(2,1)S(1)}, bf16[264,128]{1,0:T(8,128)(2,1)S(1)}, u32[]{:S(2)}, u32[]{:S(2)}) collective-permute-start(bf16[264,128]{1,0:T(8,128)(2,1)S(1)} %get-tuple-element.138), channel_id=1, source_target_pairs={{0,1},{1,8},{2,3},{3,10},{4,5},{5,12},{6,7},{7,14},{8,9},{9,0},{10... | collective-permute-start | bytes 202760 | tf_op jit(solution)/shard_map/ppermute | solution.py:412
  75.0 9.4 %collective-permute-start.32 = (bf16[264,128]{1,0:T(8,128)(2,1)S(1)}, bf16[264,128]{1,0:T(8,128)(2,1)S(1)}, u32[]{:S(2)}, u32[]{:S(2)}) collective-permute-start(bf16[264,128]{1,0:T(8,128)(2,1)S(1)} %get-tuple-element.139), channel_id=1, source_target_pairs={{0,9},{1,0},{2,11},{3,2},{4,13},{5,4},{6,15},{7,6},{8,1},{9,8},{10... | collective-permute-start | bytes 202760 | tf_op jit(solution)/shard_map/ppermute | solution.py:412
  76.4 9.9 %collective-permute-start.33 = (bf16[264,128]{1,0:T(8,128)(2,1)S(1)}, bf16[264,128]{1,0:T(8,128)(2,1)S(1)}, u32[]{:S(2)}, u32[]{:S(2)}) collective-permute-start(bf16[264,128]{1,0:T(8,128)(2,1)S(1)} %get-tuple-element.140), channel_id=1, source_target_pairs={{0,10},{1,3},{2,8},{3,1},{4,14},{5,7},{6,12},{7,5},{8,2},{9,11},{1... | collective-permute-start | bytes 202760 | tf_op jit(solution)/shard_map/ppermute | solution.py:412
  77.7 8.6 %collective-permute-start.34 = (bf16[264,128]{1,0:T(8,128)(2,1)S(1)}, bf16[264,128]{1,0:T(8,128)(2,1)S(1)}, u32[]{:S(2)}, u32[]{:S(2)}) collective-permute-start(bf16[264,128]{1,0:T(8,128)(2,1)S(1)} %get-tuple-element.141), channel_id=1, source_target_pairs={{0,2},{1,11},{2,0},{3,9},{4,6},{5,15},{6,4},{7,13},{8,10},{9,3},{1... | collective-permute-start | bytes 202760 | tf_op jit(solution)/shard_map/ppermute | solution.py:412
  84.4 7.8 %collective-permute-start.37 = (bf16[264,128]{1,0:T(8,128)(2,1)S(1)}, bf16[264,128]{1,0:T(8,128)(2,1)S(1)}, u32[]{:S(2)}, u32[]{:S(2)}) collective-permute-start(bf16[264,128]{1,0:T(8,128)(2,1)S(1)} %get-tuple-element.144), channel_id=1, source_target_pairs={{0,12},{1,5},{2,14},{3,7},{4,8},{5,1},{6,10},{7,3},{8,4},{9,13},{1... | collective-permute-start | bytes 202760 | tf_op jit(solution)/shard_map/ppermute | solution.py:412
  86.3 6.6 %collective-permute-start.39 = (bf16[264,128]{1,0:T(8,128)(2,1)S(1)}, bf16[264,128]{1,0:T(8,128)(2,1)S(1)}, u32[]{:S(2)}, u32[]{:S(2)}) collective-permute-start(bf16[264,128]{1,0:T(8,128)(2,1)S(1)} %get-tuple-element.146), channel_id=1, source_target_pairs={{0,5},{1,12},{2,7},{3,14},{4,1},{5,8},{6,3},{7,10},{8,13},{9,4},{1... | collective-permute-start | bytes 202760 | tf_op jit(solution)/shard_map/ppermute | solution.py:412
  86.8 10.3 %collective-permute-start.40 = (bf16[264,128]{1,0:T(8,128)(2,1)S(1)}, bf16[264,128]{1,0:T(8,128)(2,1)S(1)}, u32[]{:S(2)}, u32[]{:S(2)}) collective-permute-start(bf16[264,128]{1,0:T(8,128)(2,1)S(1)} %get-tuple-element.147), channel_id=1, source_target_pairs={{0,13},{1,4},{2,15},{3,6},{4,9},{5,0},{6,11},{7,2},{8,5},{9,12},{1... | collective-permute-start | bytes 202760 | tf_op jit(solution)/shard_map/ppermute | solution.py:412
  89.9 7.5 %collective-permute-start.41 = (bf16[264,128]{1,0:T(8,128)(2,1)S(1)}, bf16[264,128]{1,0:T(8,128)(2,1)S(1)}, u32[]{:S(2)}, u32[]{:S(2)}) collective-permute-start(bf16[264,128]{1,0:T(8,128)(2,1)S(1)} %get-tuple-element.148), channel_id=1, source_target_pairs={{0,14},{1,7},{2,12},{3,5},{4,10},{5,3},{6,8},{7,1},{8,6},{9,15},{1... | collective-permute-start | bytes 202760 | tf_op jit(solution)/shard_map/ppermute | solution.py:412
  92.6 6.9 %collective-permute-start.43 = (bf16[264,128]{1,0:T(8,128)(2,1)S(1)}, bf16[264,128]{1,0:T(8,128)(2,1)S(1)}, u32[]{:S(2)}, u32[]{:S(2)}) collective-permute-start(bf16[264,128]{1,0:T(8,128)(2,1)S(1)} %get-tuple-element.150), channel_id=1, source_target_pairs={{0,7},{1,14},{2,5},{3,12},{4,3},{5,10},{6,1},{7,8},{8,15},{9,6},{1... | collective-permute-start | bytes 202760 | tf_op jit(solution)/shard_map/ppermute | solution.py:412
  92.9 6.9 %collective-permute-start.44 = (bf16[264,128]{1,0:T(8,128)(2,1)S(1)}, bf16[264,128]{1,0:T(8,128)(2,1)S(1)}, u32[]{:S(2)}, u32[]{:S(2)}) collective-permute-start(bf16[264,128]{1,0:T(8,128)(2,1)S(1)} %get-tuple-element.151), channel_id=1, source_target_pairs={{0,15},{1,6},{2,13},{3,4},{4,11},{5,2},{6,9},{7,0},{8,7},{9,14},{1... | collective-permute-start | bytes 202760 | tf_op jit(solution)/shard_map/ppermute | solution.py:412
  102.0 7.7 %collective-permute-start.45 = (bf16[264,128]{1,0:T(8,128)(2,1)S(1)}, bf16[264,128]{1,0:T(8,128)(2,1)S(1)}, u32[]{:S(2)}, u32[]{:S(2)}) collective-permute-start(bf16[264,128]{1,0:T(8,128)(2,1)S(1)} %get-tuple-element.155), channel_id=1, source_target_pairs={{0,8},{1,9},{2,10},{3,11},{4,12},{5,13},{6,14},{7,15},{8,0},{9,1},... | collective-permute-start | bytes 202760 | tf_op jit(solution)/shard_map/ppermute | solution.py:412
  103.1 11.1 %collective-permute-start.46 = (bf16[264,128]{1,0:T(8,128)(2,1)S(1)}, bf16[264,128]{1,0:T(8,128)(2,1)S(1)}, u32[]{:S(2)}, u32[]{:S(2)}) collective-permute-start(bf16[264,128]{1,0:T(8,128)(2,1)S(1)} %get-tuple-element.156), channel_id=1, source_target_pairs={{0,1},{1,8},{2,3},{3,10},{4,5},{5,12},{6,7},{7,14},{8,9},{9,0},{10... | collective-permute-start | bytes 202760 | tf_op jit(solution)/shard_map/ppermute | solution.py:412
  103.7 10.6 %collective-permute-start.47 = (bf16[264,128]{1,0:T(8,128)(2,1)S(1)}, bf16[264,128]{1,0:T(8,128)(2,1)S(1)}, u32[]{:S(2)}, u32[]{:S(2)}) collective-permute-start(bf16[264,128]{1,0:T(8,128)(2,1)S(1)} %get-tuple-element.157), channel_id=1, source_target_pairs={{0,9},{1,0},{2,11},{3,2},{4,13},{5,4},{6,15},{7,6},{8,1},{9,8},{10... | collective-permute-start | bytes 202760 | tf_op jit(solution)/shard_map/ppermute | solution.py:412
  105.8 10.9 %collective-permute-start.48 = (bf16[264,128]{1,0:T(8,128)(2,1)S(1)}, bf16[264,128]{1,0:T(8,128)(2,1)S(1)}, u32[]{:S(2)}, u32[]{:S(2)}) collective-permute-start(bf16[264,128]{1,0:T(8,128)(2,1)S(1)} %get-tuple-element.158), channel_id=1, source_target_pairs={{0,10},{1,3},{2,8},{3,1},{4,14},{5,7},{6,12},{7,5},{8,2},{9,11},{1... | collective-permute-start | bytes 202760 | tf_op jit(solution)/shard_map/ppermute | solution.py:412
  108.3 8.5 %collective-permute-start.49 = (bf16[264,128]{1,0:T(8,128)(2,1)S(1)}, bf16[264,128]{1,0:T(8,128)(2,1)S(1)}, u32[]{:S(2)}, u32[]{:S(2)}) collective-permute-start(bf16[264,128]{1,0:T(8,128)(2,1)S(1)} %get-tuple-element.159), channel_id=1, source_target_pairs={{0,2},{1,11},{2,0},{3,9},{4,6},{5,15},{6,4},{7,13},{8,10},{9,3},{1... | collective-permute-start | bytes 202760 | tf_op jit(solution)/shard_map/ppermute | solution.py:412
  109.7 7.8 %collective-permute-start.50 = (bf16[264,128]{1,0:T(8,128)(2,1)S(1)}, bf16[264,128]{1,0:T(8,128)(2,1)S(1)}, u32[]{:S(2)}, u32[]{:S(2)}) collective-permute-start(bf16[264,128]{1,0:T(8,128)(2,1)S(1)} %get-tuple-element.160), channel_id=1, source_target_pairs={{0,3},{1,10},{2,1},{3,8},{4,7},{5,14},{6,5},{7,12},{8,11},{9,2},{1... | collective-permute-start | bytes 202760 | tf_op jit(solution)/shard_map/ppermute | solution.py:412
  114.3 8.6 %collective-permute-start.52 = (bf16[264,128]{1,0:T(8,128)(2,1)S(1)}, bf16[264,128]{1,0:T(8,128)(2,1)S(1)}, u32[]{:S(2)}, u32[]{:S(2)}) collective-permute-start(bf16[264,128]{1,0:T(8,128)(2,1)S(1)} %get-tuple-element.162), channel_id=1, source_target_pairs={{0,12},{1,5},{2,14},{3,7},{4,8},{5,1},{6,10},{7,3},{8,4},{9,13},{1... | collective-permute-start | bytes 202760 | tf_op jit(solution)/shard_map/ppermute | solution.py:412
  117.4 9.9 %collective-permute-start.55 = (bf16[264,128]{1,0:T(8,128)(2,1)S(1)}, bf16[264,128]{1,0:T(8,128)(2,1)S(1)}, u32[]{:S(2)}, u32[]{:S(2)}) collective-permute-start(bf16[264,128]{1,0:T(8,128)(2,1)S(1)} %get-tuple-element.165), channel_id=1, source_target_pairs={{0,13},{1,4},{2,15},{3,6},{4,9},{5,0},{6,11},{7,2},{8,5},{9,12},{1... | collective-permute-start | bytes 202760 | tf_op jit(solution)/shard_map/ppermute | solution.py:412
  120.4 7.3 %collective-permute-start.56 = (bf16[264,128]{1,0:T(8,128)(2,1)S(1)}, bf16[264,128]{1,0:T(8,128)(2,1)S(1)}, u32[]{:S(2)}, u32[]{:S(2)}) collective-permute-start(bf16[264,128]{1,0:T(8,128)(2,1)S(1)} %get-tuple-element.166), channel_id=1, source_target_pairs={{0,14},{1,7},{2,12},{3,5},{4,10},{5,3},{6,8},{7,1},{8,6},{9,15},{1... | collective-permute-start | bytes 202760 | tf_op jit(solution)/shard_map/ppermute | solution.py:412
  122.9 6.9 %collective-permute-start.58 = (bf16[264,128]{1,0:T(8,128)(2,1)S(1)}, bf16[264,128]{1,0:T(8,128)(2,1)S(1)}, u32[]{:S(2)}, u32[]{:S(2)}) collective-permute-start(bf16[264,128]{1,0:T(8,128)(2,1)S(1)} %get-tuple-element.168), channel_id=1, source_target_pairs={{0,7},{1,14},{2,5},{3,12},{4,3},{5,10},{6,1},{7,8},{8,15},{9,6},{1... | collective-permute-start | bytes 202760 | tf_op jit(solution)/shard_map/ppermute | solution.py:412
  123.1 7.2 %collective-permute-start.59 = (bf16[264,128]{1,0:T(8,128)(2,1)S(1)}, bf16[264,128]{1,0:T(8,128)(2,1)S(1)}, u32[]{:S(2)}, u32[]{:S(2)}) collective-permute-start(bf16[264,128]{1,0:T(8,128)(2,1)S(1)} %get-tuple-element.169), channel_id=1, source_target_pairs={{0,15},{1,6},{2,13},{3,4},{4,11},{5,2},{6,9},{7,0},{8,7},{9,14},{1... | collective-permute-start | bytes 202760 | tf_op jit(solution)/shard_map/ppermute | solution.py:412
  133.7 9.1 %collective-permute-start.60 = (bf16[264,128]{1,0:T(8,128)(2,1)S(1)}, bf16[264,128]{1,0:T(8,128)(2,1)S(1)}, u32[]{:S(2)}, u32[]{:S(2)}) collective-permute-start(bf16[264,128]{1,0:T(8,128)(2,1)S(1)} %get-tuple-element.174), channel_id=1, source_target_pairs={{0,8},{1,9},{2,10},{3,11},{4,12},{5,13},{6,14},{7,15},{8,0},{9,1},... | collective-permute-start | bytes 202760 | tf_op jit(solution)/shard_map/ppermute | solution.py:412
  134.9 10.4 %collective-permute-start.61 = (bf16[264,128]{1,0:T(8,128)(2,1)S(1)}, bf16[264,128]{1,0:T(8,128)(2,1)S(1)}, u32[]{:S(2)}, u32[]{:S(2)}) collective-permute-start(bf16[264,128]{1,0:T(8,128)(2,1)S(1)} %get-tuple-element.175), channel_id=1, source_target_pairs={{0,1},{1,8},{2,3},{3,10},{4,5},{5,12},{6,7},{7,14},{8,9},{9,0},{10... | collective-permute-start | bytes 202760 | tf_op jit(solution)/shard_map/ppermute | solution.py:412
  135.9 10.5 %collective-permute-start.62 = (bf16[264,128]{1,0:T(8,128)(2,1)S(1)}, bf16[264,128]{1,0:T(8,128)(2,1)S(1)}, u32[]{:S(2)}, u32[]{:S(2)}) collective-permute-start(bf16[264,128]{1,0:T(8,128)(2,1)S(1)} %get-tuple-element.176), channel_id=1, source_target_pairs={{0,9},{1,0},{2,11},{3,2},{4,13},{5,4},{6,15},{7,6},{8,1},{9,8},{10... | collective-permute-start | bytes 202760 | tf_op jit(solution)/shard_map/ppermute | solution.py:412
  138.0 9.6 %collective-permute-start.63 = (bf16[264,128]{1,0:T(8,128)(2,1)S(1)}, bf16[264,128]{1,0:T(8,128)(2,1)S(1)}, u32[]{:S(2)}, u32[]{:S(2)}) collective-permute-start(bf16[264,128]{1,0:T(8,128)(2,1)S(1)} %get-tuple-element.177), channel_id=1, source_target_pairs={{0,10},{1,3},{2,8},{3,1},{4,14},{5,7},{6,12},{7,5},{8,2},{9,11},{1... | collective-permute-start | bytes 202760 | tf_op jit(solution)/shard_map/ppermute | solution.py:412
  139.8 7.8 %collective-permute-start.64 = (bf16[264,128]{1,0:T(8,128)(2,1)S(1)}, bf16[264,128]{1,0:T(8,128)(2,1)S(1)}, u32[]{:S(2)}, u32[]{:S(2)}) collective-permute-start(bf16[264,128]{1,0:T(8,128)(2,1)S(1)} %get-tuple-element.178), channel_id=1, source_target_pairs={{0,2},{1,11},{2,0},{3,9},{4,6},{5,15},{6,4},{7,13},{8,10},{9,3},{1... | collective-permute-start | bytes 202760 | tf_op jit(solution)/shard_map/ppermute | solution.py:412
  142.9 6.6 %collective-permute-start.65 = (bf16[264,128]{1,0:T(8,128)(2,1)S(1)}, bf16[264,128]{1,0:T(8,128)(2,1)S(1)}, u32[]{:S(2)}, u32[]{:S(2)}) collective-permute-start(bf16[264,128]{1,0:T(8,128)(2,1)S(1)} %get-tuple-element.179), channel_id=1, source_target_pairs={{0,3},{1,10},{2,1},{3,8},{4,7},{5,14},{6,5},{7,12},{8,11},{9,2},{1... | collective-permute-start | bytes 202760 | tf_op jit(solution)/shard_map/ppermute | solution.py:412
  146.4 8.8 %collective-permute-start.67 = (bf16[264,128]{1,0:T(8,128)(2,1)S(1)}, bf16[264,128]{1,0:T(8,128)(2,1)S(1)}, u32[]{:S(2)}, u32[]{:S(2)}) collective-permute-start(bf16[264,128]{1,0:T(8,128)(2,1)S(1)} %get-tuple-element.181), channel_id=1, source_target_pairs={{0,12},{1,5},{2,14},{3,7},{4,8},{5,1},{6,10},{7,3},{8,4},{9,13},{1... | collective-permute-start | bytes 202760 | tf_op jit(solution)/shard_map/ppermute | solution.py:412
  147.6 7.7 %collective-permute-start.68 = (bf16[264,128]{1,0:T(8,128)(2,1)S(1)}, bf16[264,128]{1,0:T(8,128)(2,1)S(1)}, u32[]{:S(2)}, u32[]{:S(2)}) collective-permute-start(bf16[264,128]{1,0:T(8,128)(2,1)S(1)} %get-tuple-element.182), channel_id=1, source_target_pairs={{0,4},{1,13},{2,6},{3,15},{4,0},{5,9},{6,2},{7,11},{8,12},{9,5},{1... | collective-permute-start | bytes 202760 | tf_op jit(solution)/shard_map/ppermute | solution.py:412
  147.6 7.7 %collective-permute-start.69 = (bf16[264,128]{1,0:T(8,128)(2,1)S(1)}, bf16[264,128]{1,0:T(8,128)(2,1)S(1)}, u32[]{:S(2)}, u32[]{:S(2)}) collective-permute-start(bf16[264,128]{1,0:T(8,128)(2,1)S(1)} %get-tuple-element.183), channel_id=1, source_target_pairs={{0,5},{1,12},{2,7},{3,14},{4,1},{5,8},{6,3},{7,10},{8,13},{9,4},{1... | collective-permute-start | bytes 202760 | tf_op jit(solution)/shard_map/ppermute | solution.py:412
  149.5 10.2 %collective-permute-start.70 = (bf16[264,128]{1,0:T(8,128)(2,1)S(1)}, bf16[264,128]{1,0:T(8,128)(2,1)S(1)}, u32[]{:S(2)}, u32[]{:S(2)}) collective-permute-start(bf16[264,128]{1,0:T(8,128)(2,1)S(1)} %get-tuple-element.184), channel_id=1, source_target_pairs={{0,13},{1,4},{2,15},{3,6},{4,9},{5,0},{6,11},{7,2},{8,5},{9,12},{1... | collective-permute-start | bytes 202760 | tf_op jit(solution)/shard_map/ppermute | solution.py:412
  151.2 8.6 %collective-permute-start.71 = (bf16[264,128]{1,0:T(8,128)(2,1)S(1)}, bf16[264,128]{1,0:T(8,128)(2,1)S(1)}, u32[]{:S(2)}, u32[]{:S(2)}) collective-permute-start(bf16[264,128]{1,0:T(8,128)(2,1)S(1)} %get-tuple-element.185), channel_id=1, source_target_pairs={{0,14},{1,7},{2,12},{3,5},{4,10},{5,3},{6,8},{7,1},{8,6},{9,15},{1... | collective-permute-start | bytes 202760 | tf_op jit(solution)/shard_map/ppermute | solution.py:412
  155.2 6.9 %collective-permute-start.73 = (bf16[264,128]{1,0:T(8,128)(2,1)S(1)}, bf16[264,128]{1,0:T(8,128)(2,1)S(1)}, u32[]{:S(2)}, u32[]{:S(2)}) collective-permute-start(bf16[264,128]{1,0:T(8,128)(2,1)S(1)} %get-tuple-element.187), channel_id=1, source_target_pairs={{0,7},{1,14},{2,5},{3,12},{4,3},{5,10},{6,1},{7,8},{8,15},{9,6},{1... | collective-permute-start | bytes 202760 | tf_op jit(solution)/shard_map/ppermute | solution.py:412
  155.3 6.8 %collective-permute-start.74 = (bf16[264,128]{1,0:T(8,128)(2,1)S(1)}, bf16[264,128]{1,0:T(8,128)(2,1)S(1)}, u32[]{:S(2)}, u32[]{:S(2)}) collective-permute-start(bf16[264,128]{1,0:T(8,128)(2,1)S(1)} %get-tuple-element.188), channel_id=1, source_target_pairs={{0,15},{1,6},{2,13},{3,4},{4,11},{5,2},{6,9},{7,0},{8,7},{9,14},{1... | collective-permute-start | bytes 202760 | tf_op jit(solution)/shard_map/ppermute | solution.py:412
  (20 other events, 126.2 us)

commit v17 on v14

--- a/solution.py
+++ b/solution.py
@@ -22,12 +22,9 @@
 
 
 def steps_of(peers):
-    near, far = list(range(1, peers // 2)), list(range(peers // 2, peers))
-    steps = [0]
-    while far:
-        steps += far[:2] + near[:1]
-        far, near = far[2:], near[1:]
-    return steps + near
+    half, quarter = peers // 2, peers // 4
+    near = [step for low in range(quarter) for step in (low, quarter + low)][1:]
+    return [0, half] + [step for low in near for step in (low, half + low)]
 
 
 def diagonal(cols):

time: 192 us -> 172 us (0.90)
  waiting for transfers between devices: 57 us -> 36.5 us
    ppermute x75, waiting for transfers between devices: 54.6 us -> 33.3 us  [exchange(): lax.ppermute(value, 'pair', [(one, one ^ step) for one in range(peers)])]
  transfers between devices with their start and end apart: 81 -> 81, of which waited for: 35 -> 30; matrix products, arithmetic and copies ran while one was open for 0% -> 0% of each run, Pallas kernels for 2% -> 3%
where the time goes in v17:
time: 172 us
  starting transfers between devices  108 us (63%)
  waiting for transfers between devices  36.5 us (21%)
  Pallas kernels  25.2 us (15%)
    ppermute x75, starting transfers between devices, exchange(): lax.ppermute(value, 'pair', [(one, one ^ step) for one in range(peers)])  102 us
    ppermute x75, waiting for transfers between devices, exchange(): lax.ppermute(value, 'pair', [(one, one ^ step) for one in range(peers)])  33.3 us
    pallas_call x2, Pallas kernels, on_device(): call(functools.partial(pair_kernel, peers), 'pairs_last' if last else 'pa...  6.9 us
    ppermute x6, starting transfers between devices, on_device(): lax.ppermute(share, 'pair', [(one, one ^ step) for one in range(peers)])  6.39 us
    pallas_call x1, Pallas kernels, on_device(): call(functools.partial(start_kernel, peers), 'start', [SMEM, HBM, HBM, HB...  5.39 us
  transfers between devices with their start and end apart: 81, of which 30 were waited for; matrix products, arithmetic and copies ran while one was open for 0% of the time, Pallas kernels for 3%

profile of v17, /device:TPU:0, one launch (start us, length us, event | category | flops | bytes accessed | tf_op | source)
XLA Modules:
  0.0 172.2 jit_solution(18169759856891184046)
XLA Ops:
  0.6 5.4 %start.1 = (bf16[264,128]{1,0:T(8,128)(2,1)}, bf16[264,128]{1,0:T(8,128)(2,1)}, bf16[264,128]{1,0:T(8,128)(2,1)}, bf16[264,128]{1,0:T(8,128)(2,1)}, bf16[264,128...) custom-call(s32[1]{0:T(128)} %bitcast.me_ref, ...), custom_call_target="tpu_custom_call" | custom-call | flops 268435456 | bytes 6291456 | tf_op jit(solution)/shard_map/start/pallas_call | solution.py:416
  6.0 4.1 %collective-permute-start = (bf16[264,128]{1,0:T(8,128)(2,1)}, bf16[264,128]{1,0:T(8,128)(2,1)S(1)}, u32[]{:S(2)}, u32[]{:S(2)}) collective-permute-start(bf16[264,128]{1,0:T(8,128)(2,1)} %get-tuple-element.100), channel_id=1, source_target_pairs={{0,8},{1,9},{2,10},{3,11},{4,12},{5,13},{6,14},{7,15},{8,0},{9,1},... | collective-permute-start | bytes 202760 | tf_op jit(solution)/shard_map/ppermute | solution.py:411
  10.2 1.5 collective-permute-start.1
  11.7 2.1 %collective-permute-start.4 = (bf16[264,128]{1,0:T(8,128)(2,1)}, bf16[264,128]{1,0:T(8,128)(2,1)S(1)}, u32[]{:S(2)}, u32[]{:S(2)}) collective-permute-start(bf16[264,128]{1,0:T(8,128)(2,1)} %get-tuple-element.104), channel_id=1, source_target_pairs={{0,9},{1,8},{2,11},{3,10},{4,13},{5,12},{6,15},{7,14},{8,1},{9,0},... | collective-permute-start | bytes 202760 | tf_op jit(solution)/shard_map/ppermute | solution.py:411
  13.8 2.0 %collective-permute-start.5 = (bf16[264,128]{1,0:T(8,128)(2,1)}, bf16[264,128]{1,0:T(8,128)(2,1)S(1)}, u32[]{:S(2)}, u32[]{:S(2)}) collective-permute-start(bf16[264,128]{1,0:T(8,128)(2,1)} %get-tuple-element.105), channel_id=1, source_target_pairs={{0,5},{1,4},{2,7},{3,6},{4,1},{5,0},{6,3},{7,2},{8,13},{9,12},{10,... | collective-permute-start | bytes 202760 | tf_op jit(solution)/shard_map/ppermute | solution.py:411
  15.8 1.5 collective-permute-start.6
  17.3 1.4 collective-permute-done.2.refs_3_
  18.7 1.6 collective-permute-start.7
  20.3 2.5 %collective-permute-start.8 = (bf16[264,128]{1,0:T(8,128)(2,1)}, bf16[264,128]{1,0:T(8,128)(2,1)S(1)}, u32[]{:S(2)}, u32[]{:S(2)}) collective-permute-start(bf16[264,128]{1,0:T(8,128)(2,1)} %get-tuple-element.108), channel_id=1, source_target_pairs={{0,10},{1,11},{2,8},{3,9},{4,14},{5,15},{6,12},{7,13},{8,2},{9,3},... | collective-permute-start | bytes 202760 | tf_op jit(solution)/shard_map/ppermute | solution.py:411
  23.9 2.7 %collective-permute-start.10 = (bf16[264,128]{1,0:T(8,128)(2,1)}, bf16[264,128]{1,0:T(8,128)(2,1)S(1)}, u32[]{:S(2)}, u32[]{:S(2)}) collective-permute-start(bf16[264,128]{1,0:T(8,128)(2,1)} %get-tuple-element.110), channel_id=1, source_target_pairs={{0,14},{1,15},{2,12},{3,13},{4,10},{5,11},{6,8},{7,9},{8,6},{9,7},... | collective-permute-start | bytes 202760 | tf_op jit(solution)/shard_map/ppermute | solution.py:411
  26.6 1.1 collective-permute-start.11
  29.3 3.6 %collective-permute-start.14 = (bf16[264,128]{1,0:T(8,128)(2,1)}, bf16[264,128]{1,0:T(8,128)(2,1)S(1)}, u32[]{:S(2)}, u32[]{:S(2)}) collective-permute-start(bf16[264,128]{1,0:T(8,128)(2,1)} %get-tuple-element.114), channel_id=1, source_target_pairs={{0,15},{1,14},{2,13},{3,12},{4,11},{5,10},{6,9},{7,8},{8,7},{9,6},... | collective-permute-start | bytes 202760 | tf_op jit(solution)/shard_map/ppermute | solution.py:411
  34.3 2.9 %keep.1 = (s32[128]{0:T(128)S(1)}, bf16[264,128]{1,0:T(8,128)(2,1)S(1)}, bf16[8,16,128,128]{3,2,1,0:T(8,128)(2,1)S(1)}) custom-call(s32[128]{0:T(128)S(1)} %copy-done.2, bf16[264,128]{1,0:T(8,128)(2,1)S(1)} %copy-done.1, bf16[8,16,128,128]{3,2,1,0:T(8,128)(2,1)} %rays_hbm.3), custom_call_target="tpu_custom_call" | custom-call | bytes 8388608 | tf_op jit(solution)/shard_map/keep/pallas_call | solution.py:428
  37.3 2.5 %cells_first.1 = (f32[64,8192]{1,0:T(8,128)S(1)}, f32[64,128]{1,0:T(8,128)S(1)}, bf16[264,128]{1,0:T(8,128)(2,1)S(1)}, bf16[264,128]{1,0:T(8,128)(2,1)S(1)}, bf1...) custom-call(bf16[264,128]{1,0:T(8,128)(2,1)S(1)} %get-tuple-element., ...), custom_call_target="tpu_custom_call" | custom-call | bytes 6291456 | tf_op jit(solution)/shard_map/cells_first/pallas_call | solution.py:433
  39.9 3.0 %collective-permute-start.16 = (bf16[264,128]{1,0:T(8,128)(2,1)S(1)}, bf16[264,128]{1,0:T(8,128)(2,1)S(1)}, u32[]{:S(2)}, u32[]{:S(2)}) collective-permute-start(bf16[264,128]{1,0:T(8,128)(2,1)S(1)} %get-tuple-element.120), channel_id=1, source_target_pairs={{0,4},{1,5},{2,6},{3,7},{4,0},{5,1},{6,2},{7,3},{8,12},{9,13},{10,... | collective-permute-start | bytes 202760 | tf_op jit(solution)/shard_map/ppermute | solution.py:411
  42.9 1.3 collective-permute-start.17
  44.5 2.4 %collective-permute-done.15.refs_1_ = bf16[264,128]{1,0:T(8,128)(2,1)S(1)} collective-permute-done((bf16[264,128]{1,0:T(8,128)(2,1)S(1)}, bf16[264,128]{1,0:T(8,128)(2,1)S(1)}, u32[]{:S(2)}, u32[]{:S(2)}) %collective-permute-start.15) | collective-permute-done | bytes 67616 | tf_op jit(solution)/shard_map/ppermute | solution.py:411
  47.0 1.4 collective-permute-start.21
  48.5 1.3 collective-permute-done.17.refs_3_
  49.8 3.5 %collective-permute-start.23 = (bf16[264,128]{1,0:T(8,128)(2,1)S(1)}, bf16[264,128]{1,0:T(8,128)(2,1)S(1)}, u32[]{:S(2)}, u32[]{:S(2)}) collective-permute-start(bf16[264,128]{1,0:T(8,128)(2,1)S(1)} %get-tuple-element.127), channel_id=1, source_target_pairs={{0,10},{1,11},{2,8},{3,9},{4,14},{5,15},{6,12},{7,13},{8,2},{9,3},... | collective-permute-start | bytes 202760 | tf_op jit(solution)/shard_map/ppermute | solution.py:411
  53.7 2.8 %collective-permute-start.25 = (bf16[264,128]{1,0:T(8,128)(2,1)S(1)}, bf16[264,128]{1,0:T(8,128)(2,1)S(1)}, u32[]{:S(2)}, u32[]{:S(2)}) collective-permute-start(bf16[264,128]{1,0:T(8,128)(2,1)S(1)} %get-tuple-element.129), channel_id=1, source_target_pairs={{0,14},{1,15},{2,12},{3,13},{4,10},{5,11},{6,8},{7,9},{8,6},{9,7},... | collective-permute-start | bytes 202760 | tf_op jit(solution)/shard_map/ppermute | solution.py:411
  56.5 2.3 %collective-permute-start.27 = (bf16[264,128]{1,0:T(8,128)(2,1)S(1)}, bf16[264,128]{1,0:T(8,128)(2,1)S(1)}, u32[]{:S(2)}, u32[]{:S(2)}) collective-permute-start(bf16[264,128]{1,0:T(8,128)(2,1)S(1)} %get-tuple-element.131), channel_id=1, source_target_pairs={{0,11},{1,10},{2,9},{3,8},{4,15},{5,14},{6,13},{7,12},{8,3},{9,2},... | collective-permute-start | bytes 202760 | tf_op jit(solution)/shard_map/ppermute | solution.py:411
  59.8 2.9 %collective-permute-start.29 = (bf16[264,128]{1,0:T(8,128)(2,1)S(1)}, bf16[264,128]{1,0:T(8,128)(2,1)S(1)}, u32[]{:S(2)}, u32[]{:S(2)}) collective-permute-start(bf16[264,128]{1,0:T(8,128)(2,1)S(1)} %get-tuple-element.133), channel_id=1, source_target_pairs={{0,15},{1,14},{2,13},{3,12},{4,11},{5,10},{6,9},{7,8},{8,7},{9,6},... | collective-permute-start | bytes 202760 | tf_op jit(solution)/shard_map/ppermute | solution.py:411
  63.0 1.7 %collective-permute-done.28.refs_14_ = bf16[264,128]{1,0:T(8,128)(2,1)S(1)} collective-permute-done((bf16[264,128]{1,0:T(8,128)(2,1)S(1)}, bf16[264,128]{1,0:T(8,128)(2,1)S(1)}, u32[]{:S(2)}, u32[]{:S(2)}) %collective-permute-start.28) | collective-permute-done | bytes 67616 | tf_op jit(solution)/shard_map/ppermute | solution.py:411
  64.7 1.6 collective-permute-done.29.refs_15_
  66.3 3.5 %pairs.1 = (bf16[264,128]{1,0:T(8,128)(2,1)S(1)}, bf16[264,128]{1,0:T(8,128)(2,1)S(1)}, bf16[264,128]{1,0:T(8,128)(2,1)S(1)}, bf16[264,128]{1,0:T(8,128)(2,1)S(1...) custom-call(s32[128]{0:T(128)S(1)} %get-tuple-element.117.target_ref, ...), custom_call_target="tpu_custom_call" | custom-call | flops 536870912 | bytes 8388608 | tf_op jit(solution)/shard_map/pairs/pallas_call | solution.py:444
  70.6 2.3 %collective-permute-start.31 = (bf16[264,128]{1,0:T(8,128)(2,1)S(1)}, bf16[264,128]{1,0:T(8,128)(2,1)S(1)}, u32[]{:S(2)}, u32[]{:S(2)}) collective-permute-start(bf16[264,128]{1,0:T(8,128)(2,1)S(1)} %get-tuple-element.138), channel_id=1, source_target_pairs={{0,4},{1,5},{2,6},{3,7},{4,0},{5,1},{6,2},{7,3},{8,12},{9,13},{10,... | collective-permute-start | bytes 202760 | tf_op jit(solution)/shard_map/ppermute | solution.py:411
  72.9 1.4 collective-permute-start.32
  74.4 2.4 %collective-permute-done.30.refs_1_ = bf16[264,128]{1,0:T(8,128)(2,1)S(1)} collective-permute-done((bf16[264,128]{1,0:T(8,128)(2,1)S(1)}, bf16[264,128]{1,0:T(8,128)(2,1)S(1)}, u32[]{:S(2)}, u32[]{:S(2)}) %collective-permute-start.30) | collective-permute-done | bytes 67616 | tf_op jit(solution)/shard_map/ppermute | solution.py:411
  79.9 3.9 %collective-permute-start.38 = (bf16[264,128]{1,0:T(8,128)(2,1)S(1)}, bf16[264,128]{1,0:T(8,128)(2,1)S(1)}, u32[]{:S(2)}, u32[]{:S(2)}) collective-permute-start(bf16[264,128]{1,0:T(8,128)(2,1)S(1)} %get-tuple-element.145), channel_id=1, source_target_pairs={{0,10},{1,11},{2,8},{3,9},{4,14},{5,15},{6,12},{7,13},{8,2},{9,3},... | collective-permute-start | bytes 202760 | tf_op jit(solution)/shard_map/ppermute | solution.py:411
  83.8 2.5 %collective-permute-start.40 = (bf16[264,128]{1,0:T(8,128)(2,1)S(1)}, bf16[264,128]{1,0:T(8,128)(2,1)S(1)}, u32[]{:S(2)}, u32[]{:S(2)}) collective-permute-start(bf16[264,128]{1,0:T(8,128)(2,1)S(1)} %get-tuple-element.147), channel_id=1, source_target_pairs={{0,14},{1,15},{2,12},{3,13},{4,10},{5,11},{6,8},{7,9},{8,6},{9,7},... | collective-permute-start | bytes 202760 | tf_op jit(solution)/shard_map/ppermute | solution.py:411
  86.3 1.1 collective-permute-start.41
  87.4 2.0 %collective-permute-start.42 = (bf16[264,128]{1,0:T(8,128)(2,1)S(1)}, bf16[264,128]{1,0:T(8,128)(2,1)S(1)}, u32[]{:S(2)}, u32[]{:S(2)}) collective-permute-start(bf16[264,128]{1,0:T(8,128)(2,1)S(1)} %get-tuple-element.149), channel_id=1, source_target_pairs={{0,11},{1,10},{2,9},{3,8},{4,15},{5,14},{6,13},{7,12},{8,3},{9,2},... | collective-permute-start | bytes 202760 | tf_op jit(solution)/shard_map/ppermute | solution.py:411
  90.1 2.4 %collective-permute-start.44 = (bf16[264,128]{1,0:T(8,128)(2,1)S(1)}, bf16[264,128]{1,0:T(8,128)(2,1)S(1)}, u32[]{:S(2)}, u32[]{:S(2)}) collective-permute-start(bf16[264,128]{1,0:T(8,128)(2,1)S(1)} %get-tuple-element.151), channel_id=1, source_target_pairs={{0,15},{1,14},{2,13},{3,12},{4,11},{5,10},{6,9},{7,8},{8,7},{9,6},... | collective-permute-start | bytes 202760 | tf_op jit(solution)/shard_map/ppermute | solution.py:411
  92.5 2.3 %collective-permute-done.42.refs_13_ = bf16[264,128]{1,0:T(8,128)(2,1)S(1)} collective-permute-done((bf16[264,128]{1,0:T(8,128)(2,1)S(1)}, bf16[264,128]{1,0:T(8,128)(2,1)S(1)}, u32[]{:S(2)}, u32[]{:S(2)}) %collective-permute-start.42) | collective-permute-done | bytes 67616 | tf_op jit(solution)/shard_map/ppermute | solution.py:411
  95.0 1.9 %collective-permute-done.44.refs_15_ = bf16[264,128]{1,0:T(8,128)(2,1)S(1)} collective-permute-done((bf16[264,128]{1,0:T(8,128)(2,1)S(1)}, bf16[264,128]{1,0:T(8,128)(2,1)S(1)}, u32[]{:S(2)}, u32[]{:S(2)}) %collective-permute-start.44) | collective-permute-done | bytes 67616 | tf_op jit(solution)/shard_map/ppermute | solution.py:411
  96.9 2.4 %cells.1 = (f32[64,8192]{1,0:T(8,128)S(1)}, f32[64,128]{1,0:T(8,128)S(1)}, bf16[264,128]{1,0:T(8,128)(2,1)S(1)}, bf16[264,128]{1,0:T(8,128)(2,1)S(1)}, bf16[264,...) custom-call(s32[16,128]{1,0:T(8,128)S(1)} %get-tuple-element.116.ask, ...), custom_call_target="tpu_custom_call" | custom-call | bytes 8388608 | tf_op jit(solution)/shard_map/cells/pallas_call | solution.py:453
  100.0 2.0 %collective-permute-start.46 = (bf16[264,128]{1,0:T(8,128)(2,1)S(1)}, bf16[264,128]{1,0:T(8,128)(2,1)S(1)}, u32[]{:S(2)}, u32[]{:S(2)}) collective-permute-start(bf16[264,128]{1,0:T(8,128)(2,1)S(1)} %get-tuple-element.156), channel_id=1, source_target_pairs={{0,4},{1,5},{2,6},{3,7},{4,0},{5,1},{6,2},{7,3},{8,12},{9,13},{10,... | collective-permute-start | bytes 202760 | tf_op jit(solution)/shard_map/ppermute | solution.py:411
  102.0 1.8 %collective-permute-start.47 = (bf16[264,128]{1,0:T(8,128)(2,1)S(1)}, bf16[264,128]{1,0:T(8,128)(2,1)S(1)}, u32[]{:S(2)}, u32[]{:S(2)}) collective-permute-start(bf16[264,128]{1,0:T(8,128)(2,1)S(1)} %get-tuple-element.157), channel_id=1, source_target_pairs={{0,12},{1,13},{2,14},{3,15},{4,8},{5,9},{6,10},{7,11},{8,4},{9,5},... | collective-permute-start | bytes 202760 | tf_op jit(solution)/shard_map/ppermute | solution.py:411
  103.8 3.0 %collective-permute-done.45.refs_1_ = bf16[264,128]{1,0:T(8,128)(2,1)S(1)} collective-permute-done((bf16[264,128]{1,0:T(8,128)(2,1)S(1)}, bf16[264,128]{1,0:T(8,128)(2,1)S(1)}, u32[]{:S(2)}, u32[]{:S(2)}) %collective-permute-start.45) | collective-permute-done | bytes 67616 | tf_op jit(solution)/shard_map/ppermute | solution.py:411
  106.8 4.1 %collective-permute-start.51 = (bf16[264,128]{1,0:T(8,128)(2,1)S(1)}, bf16[264,128]{1,0:T(8,128)(2,1)S(1)}, u32[]{:S(2)}, u32[]{:S(2)}) collective-permute-start(bf16[264,128]{1,0:T(8,128)(2,1)S(1)} %get-tuple-element.161), channel_id=1, source_target_pairs={{0,13},{1,12},{2,15},{3,14},{4,9},{5,8},{6,11},{7,10},{8,5},{9,4},... | collective-permute-start | bytes 202760 | tf_op jit(solution)/shard_map/ppermute | solution.py:411
  110.9 2.3 %collective-permute-start.53 = (bf16[264,128]{1,0:T(8,128)(2,1)S(1)}, bf16[264,128]{1,0:T(8,128)(2,1)S(1)}, u32[]{:S(2)}, u32[]{:S(2)}) collective-permute-start(bf16[264,128]{1,0:T(8,128)(2,1)S(1)} %get-tuple-element.163), channel_id=1, source_target_pairs={{0,10},{1,11},{2,8},{3,9},{4,14},{5,15},{6,12},{7,13},{8,2},{9,3},... | collective-permute-start | bytes 202760 | tf_op jit(solution)/shard_map/ppermute | solution.py:411
  113.7 4.0 %collective-permute-start.55 = (bf16[264,128]{1,0:T(8,128)(2,1)S(1)}, bf16[264,128]{1,0:T(8,128)(2,1)S(1)}, u32[]{:S(2)}, u32[]{:S(2)}) collective-permute-start(bf16[264,128]{1,0:T(8,128)(2,1)S(1)} %get-tuple-element.165), channel_id=1, source_target_pairs={{0,14},{1,15},{2,12},{3,13},{4,10},{5,11},{6,8},{7,9},{8,6},{9,7},... | collective-permute-start | bytes 202760 | tf_op jit(solution)/shard_map/ppermute | solution.py:411
  117.7 1.2 collective-permute-start.57
  119.8 4.0 %collective-permute-start.59 = (bf16[264,128]{1,0:T(8,128)(2,1)S(1)}, bf16[264,128]{1,0:T(8,128)(2,1)S(1)}, u32[]{:S(2)}, u32[]{:S(2)}) collective-permute-start(bf16[264,128]{1,0:T(8,128)(2,1)S(1)} %get-tuple-element.169), channel_id=1, source_target_pairs={{0,15},{1,14},{2,13},{3,12},{4,11},{5,10},{6,9},{7,8},{8,7},{9,6},... | collective-permute-start | bytes 202760 | tf_op jit(solution)/shard_map/ppermute | solution.py:411
  123.9 1.3 collective-permute-done.57.refs_13_
  125.2 2.1 %collective-permute-done.59.refs_15_ = bf16[264,128]{1,0:T(8,128)(2,1)S(1)} collective-permute-done((bf16[264,128]{1,0:T(8,128)(2,1)S(1)}, bf16[264,128]{1,0:T(8,128)(2,1)S(1)}, u32[]{:S(2)}, u32[]{:S(2)}) %collective-permute-start.59) | collective-permute-done | bytes 67616 | tf_op jit(solution)/shard_map/ppermute | solution.py:411
  127.3 3.4 %pairs_last.1 = (bf16[264,128]{1,0:T(8,128)(2,1)S(1)}, bf16[264,128]{1,0:T(8,128)(2,1)S(1)}, bf16[264,128]{1,0:T(8,128)(2,1)S(1)}, bf16[264,128]{1,0:T(8,128)(2,...) custom-call(s32[128]{0:T(128)S(1)} %get-tuple-element.117.target_ref, ...), custom_call_target="tpu_custom_call" | custom-call | flops 536870912 | bytes 8388608 | tf_op jit(solution)/shard_map/pairs_last/pallas_call | solution.py:444
  131.1 2.6 %collective-permute-start.61 = (bf16[264,128]{1,0:T(8,128)(2,1)S(1)}, bf16[264,128]{1,0:T(8,128)(2,1)S(1)}, u32[]{:S(2)}, u32[]{:S(2)}) collective-permute-start(bf16[264,128]{1,0:T(8,128)(2,1)S(1)} %get-tuple-element.175), channel_id=1, source_target_pairs={{0,4},{1,5},{2,6},{3,7},{4,0},{5,1},{6,2},{7,3},{8,12},{9,13},{10,... | collective-permute-start | bytes 202760 | tf_op jit(solution)/shard_map/ppermute | solution.py:411
  133.8 1.5 collective-permute-start.62
  135.3 2.4 %collective-permute-done.60.refs_1_ = bf16[264,128]{1,0:T(8,128)(2,1)S(1)} collective-permute-done((bf16[264,128]{1,0:T(8,128)(2,1)S(1)}, bf16[264,128]{1,0:T(8,128)(2,1)S(1)}, u32[]{:S(2)}, u32[]{:S(2)}) %collective-permute-start.60) | collective-permute-done | bytes 67616 | tf_op jit(solution)/shard_map/ppermute | solution.py:411
  138.1 1.5 collective-permute-start.66
  141.1 3.3 %collective-permute-start.68 = (bf16[264,128]{1,0:T(8,128)(2,1)S(1)}, bf16[264,128]{1,0:T(8,128)(2,1)S(1)}, u32[]{:S(2)}, u32[]{:S(2)}) collective-permute-start(bf16[264,128]{1,0:T(8,128)(2,1)S(1)} %get-tuple-element.182), channel_id=1, source_target_pairs={{0,10},{1,11},{2,8},{3,9},{4,14},{5,15},{6,12},{7,13},{8,2},{9,3},... | collective-permute-start | bytes 202760 | tf_op jit(solution)/shard_map/ppermute | solution.py:411
  144.9 2.3 %collective-permute-start.70 = (bf16[264,128]{1,0:T(8,128)(2,1)S(1)}, bf16[264,128]{1,0:T(8,128)(2,1)S(1)}, u32[]{:S(2)}, u32[]{:S(2)}) collective-permute-start(bf16[264,128]{1,0:T(8,128)(2,1)S(1)} %get-tuple-element.184), channel_id=1, source_target_pairs={{0,14},{1,15},{2,12},{3,13},{4,10},{5,11},{6,8},{7,9},{8,6},{9,7},... | collective-permute-start | bytes 202760 | tf_op jit(solution)/shard_map/ppermute | solution.py:411
  147.5 2.6 %collective-permute-start.72 = (bf16[264,128]{1,0:T(8,128)(2,1)S(1)}, bf16[264,128]{1,0:T(8,128)(2,1)S(1)}, u32[]{:S(2)}, u32[]{:S(2)}) collective-permute-start(bf16[264,128]{1,0:T(8,128)(2,1)S(1)} %get-tuple-element.186), channel_id=1, source_target_pairs={{0,11},{1,10},{2,9},{3,8},{4,15},{5,14},{6,13},{7,12},{8,3},{9,2},... | collective-permute-start | bytes 202760 | tf_op jit(solution)/shard_map/ppermute | solution.py:411
  150.7 2.8 %collective-permute-start.74 = (bf16[264,128]{1,0:T(8,128)(2,1)S(1)}, bf16[264,128]{1,0:T(8,128)(2,1)S(1)}, u32[]{:S(2)}, u32[]{:S(2)}) collective-permute-start(bf16[264,128]{1,0:T(8,128)(2,1)S(1)} %get-tuple-element.188), channel_id=1, source_target_pairs={{0,15},{1,14},{2,13},{3,12},{4,11},{5,10},{6,9},{7,8},{8,7},{9,6},... | collective-permute-start | bytes 202760 | tf_op jit(solution)/shard_map/ppermute | solution.py:411
  153.6 1.6 collective-permute-done.72.refs_13_
  157.3 2.0 %cells_last.1 = (f32[64,8192]{1,0:T(8,128)S(1)}, f32[64,128]{1,0:T(8,128)S(1)}, f32[8,128]{1,0:T(8,128)S(1)}) custom-call(s32[16,128]{1,0:T(8,128)S(1)} %get-tuple-element.116.asked_ref, bf16[264,128]{1,0:T(8,128)(2,1)S(1)} %get-tuple-element.173.refs_0_, bf16[264,128]{1,0:T(8,128)(2,1)S(1)} %collective-permute-done.60.refs_1_, ...), custom_call_target="tpu_custom_call" | custom-call | bytes 8388608 | tf_op jit(solution)/shard_map/cells_last/pallas_call | solution.py:459
  159.3 2.9 %collective-permute-start.77 = (f32[8,128]{1,0:T(8,128)S(1)}, f32[8,128]{1,0:T(8,128)S(1)}, u32[]{:S(2)}, u32[]{:S(2)}) collective-permute-start(f32[8,128]{1,0:T(8,128)S(1)} %get-tuple-element.190), channel_id=1, source_target_pairs={{0,12},{1,13},{2,14},{3,15},{4,8},{5,9},{6,10},{7,11},{8,4},{9,5},... | collective-permute-start | bytes 12296 | tf_op jit(solution)/shard_map/ppermute | solution.py:469
  162.3 1.5 collective-permute-start.75
  164.8 1.9 %collective-permute-done.76 = f32[8,128]{1,0:T(8,128)S(1)} collective-permute-done((f32[8,128]{1,0:T(8,128)S(1)}, f32[8,128]{1,0:T(8,128)S(1)}, u32[]{:S(2)}, u32[]{:S(2)}) %collective-permute-start.76) | collective-permute-done | bytes 4128 | tf_op jit(solution)/shard_map/ppermute | solution.py:469
  167.2 1.5 collective-permute-start.78
  168.7 1.5 estimate.1
  170.5 1.5 model.1
  (114 shorter events, 21.3 us)
Async XLA Ops:
  6.0 7.7 %collective-permute-start = (bf16[264,128]{1,0:T(8,128)(2,1)}, bf16[264,128]{1,0:T(8,128)(2,1)S(1)}, u32[]{:S(2)}, u32[]{:S(2)}) collective-permute-start(bf16[264,128]{1,0:T(8,128)(2,1)} %get-tuple-element.100), channel_id=1, source_target_pairs={{0,8},{1,9},{2,10},{3,11},{4,12},{5,13},{6,14},{7,15},{8,0},{9,1},... | collective-permute-start | bytes 202760 | tf_op jit(solution)/shard_map/ppermute | solution.py:411
  11.6 7.1 %collective-permute-start.2 = (bf16[264,128]{1,0:T(8,128)(2,1)}, bf16[264,128]{1,0:T(8,128)(2,1)S(1)}, u32[]{:S(2)}, u32[]{:S(2)}) collective-permute-start(bf16[264,128]{1,0:T(8,128)(2,1)} %get-tuple-element.102), channel_id=1, source_target_pairs={{0,12},{1,13},{2,14},{3,15},{4,8},{5,9},{6,10},{7,11},{8,4},{9,5},... | collective-permute-start | bytes 202760 | tf_op jit(solution)/shard_map/ppermute | solution.py:411
  11.7 8.6 %collective-permute-start.3 = (bf16[264,128]{1,0:T(8,128)(2,1)}, bf16[264,128]{1,0:T(8,128)(2,1)S(1)}, u32[]{:S(2)}, u32[]{:S(2)}) collective-permute-start(bf16[264,128]{1,0:T(8,128)(2,1)} %get-tuple-element.103), channel_id=1, source_target_pairs={{0,1},{1,0},{2,3},{3,2},{4,5},{5,4},{6,7},{7,6},{8,9},{9,8},{10,11... | collective-permute-start | bytes 202760 | tf_op jit(solution)/shard_map/ppermute | solution.py:411
  11.7 11.1 %collective-permute-start.4 = (bf16[264,128]{1,0:T(8,128)(2,1)}, bf16[264,128]{1,0:T(8,128)(2,1)S(1)}, u32[]{:S(2)}, u32[]{:S(2)}) collective-permute-start(bf16[264,128]{1,0:T(8,128)(2,1)} %get-tuple-element.104), channel_id=1, source_target_pairs={{0,9},{1,8},{2,11},{3,10},{4,13},{5,12},{6,15},{7,14},{8,1},{9,0},... | collective-permute-start | bytes 202760 | tf_op jit(solution)/shard_map/ppermute | solution.py:411
  13.8 10.1 %collective-permute-start.5 = (bf16[264,128]{1,0:T(8,128)(2,1)}, bf16[264,128]{1,0:T(8,128)(2,1)S(1)}, u32[]{:S(2)}, u32[]{:S(2)}) collective-permute-start(bf16[264,128]{1,0:T(8,128)(2,1)} %get-tuple-element.105), channel_id=1, source_target_pairs={{0,5},{1,4},{2,7},{3,6},{4,1},{5,0},{6,3},{7,2},{8,13},{9,12},{10,... | collective-permute-start | bytes 202760 | tf_op jit(solution)/shard_map/ppermute | solution.py:411
  15.8 10.9 %collective-permute-start.6 = (bf16[264,128]{1,0:T(8,128)(2,1)}, bf16[264,128]{1,0:T(8,128)(2,1)S(1)}, u32[]{:S(2)}, u32[]{:S(2)}) collective-permute-start(bf16[264,128]{1,0:T(8,128)(2,1)} %get-tuple-element.106), channel_id=1, source_target_pairs={{0,13},{1,12},{2,15},{3,14},{4,9},{5,8},{6,11},{7,10},{8,5},{9,4},... | collective-permute-start | bytes 202760 | tf_op jit(solution)/shard_map/ppermute | solution.py:411
  18.7 9.0 %collective-permute-start.7 = (bf16[264,128]{1,0:T(8,128)(2,1)}, bf16[264,128]{1,0:T(8,128)(2,1)S(1)}, u32[]{:S(2)}, u32[]{:S(2)}) collective-permute-start(bf16[264,128]{1,0:T(8,128)(2,1)} %get-tuple-element.107), channel_id=1, source_target_pairs={{0,2},{1,3},{2,0},{3,1},{4,6},{5,7},{6,4},{7,5},{8,10},{9,11},{10,... | collective-permute-start | bytes 202760 | tf_op jit(solution)/shard_map/ppermute | solution.py:411
  20.3 8.1 %collective-permute-start.8 = (bf16[264,128]{1,0:T(8,128)(2,1)}, bf16[264,128]{1,0:T(8,128)(2,1)S(1)}, u32[]{:S(2)}, u32[]{:S(2)}) collective-permute-start(bf16[264,128]{1,0:T(8,128)(2,1)} %get-tuple-element.108), channel_id=1, source_target_pairs={{0,10},{1,11},{2,8},{3,9},{4,14},{5,15},{6,12},{7,13},{8,2},{9,3},... | collective-permute-start | bytes 202760 | tf_op jit(solution)/shard_map/ppermute | solution.py:411
  22.8 6.4 %collective-permute-start.9 = (bf16[264,128]{1,0:T(8,128)(2,1)}, bf16[264,128]{1,0:T(8,128)(2,1)S(1)}, u32[]{:S(2)}, u32[]{:S(2)}) collective-permute-start(bf16[264,128]{1,0:T(8,128)(2,1)} %get-tuple-element.109), channel_id=1, source_target_pairs={{0,6},{1,7},{2,4},{3,5},{4,2},{5,3},{6,0},{7,1},{8,14},{9,15},{10,... | collective-permute-start | bytes 202760 | tf_op jit(solution)/shard_map/ppermute | solution.py:411
  23.9 13.3 %collective-permute-start.10 = (bf16[264,128]{1,0:T(8,128)(2,1)}, bf16[264,128]{1,0:T(8,128)(2,1)S(1)}, u32[]{:S(2)}, u32[]{:S(2)}) collective-permute-start(bf16[264,128]{1,0:T(8,128)(2,1)} %get-tuple-element.110), channel_id=1, source_target_pairs={{0,14},{1,15},{2,12},{3,13},{4,10},{5,11},{6,8},{7,9},{8,6},{9,7},... | collective-permute-start | bytes 202760 | tf_op jit(solution)/shard_map/ppermute | solution.py:411
  26.6 10.6 %collective-permute-start.11 = (bf16[264,128]{1,0:T(8,128)(2,1)}, bf16[264,128]{1,0:T(8,128)(2,1)S(1)}, u32[]{:S(2)}, u32[]{:S(2)}) collective-permute-start(bf16[264,128]{1,0:T(8,128)(2,1)} %get-tuple-element.111), channel_id=1, source_target_pairs={{0,3},{1,2},{2,1},{3,0},{4,7},{5,6},{6,5},{7,4},{8,11},{9,10},{10,... | collective-permute-start | bytes 202760 | tf_op jit(solution)/shard_map/ppermute | solution.py:411
  27.7 9.5 %collective-permute-start.12 = (bf16[264,128]{1,0:T(8,128)(2,1)}, bf16[264,128]{1,0:T(8,128)(2,1)S(1)}, u32[]{:S(2)}, u32[]{:S(2)}) collective-permute-start(bf16[264,128]{1,0:T(8,128)(2,1)} %get-tuple-element.112), channel_id=1, source_target_pairs={{0,11},{1,10},{2,9},{3,8},{4,15},{5,14},{6,13},{7,12},{8,3},{9,2},... | collective-permute-start | bytes 202760 | tf_op jit(solution)/shard_map/ppermute | solution.py:411
  28.4 8.8 %collective-permute-start.13 = (bf16[264,128]{1,0:T(8,128)(2,1)}, bf16[264,128]{1,0:T(8,128)(2,1)S(1)}, u32[]{:S(2)}, u32[]{:S(2)}) collective-permute-start(bf16[264,128]{1,0:T(8,128)(2,1)} %get-tuple-element.113), channel_id=1, source_target_pairs={{0,7},{1,6},{2,5},{3,4},{4,3},{5,2},{6,1},{7,0},{8,15},{9,14},{10,... | collective-permute-start | bytes 202760 | tf_op jit(solution)/shard_map/ppermute | solution.py:411
  29.3 8.0 %collective-permute-start.14 = (bf16[264,128]{1,0:T(8,128)(2,1)}, bf16[264,128]{1,0:T(8,128)(2,1)S(1)}, u32[]{:S(2)}, u32[]{:S(2)}) collective-permute-start(bf16[264,128]{1,0:T(8,128)(2,1)} %get-tuple-element.114), channel_id=1, source_target_pairs={{0,15},{1,14},{2,13},{3,12},{4,11},{5,10},{6,9},{7,8},{8,7},{9,6},... | collective-permute-start | bytes 202760 | tf_op jit(solution)/shard_map/ppermute | solution.py:411
  39.8 7.1 %collective-permute-start.15 = (bf16[264,128]{1,0:T(8,128)(2,1)S(1)}, bf16[264,128]{1,0:T(8,128)(2,1)S(1)}, u32[]{:S(2)}, u32[]{:S(2)}) collective-permute-start(bf16[264,128]{1,0:T(8,128)(2,1)S(1)} %get-tuple-element.119), channel_id=1, source_target_pairs={{0,8},{1,9},{2,10},{3,11},{4,12},{5,13},{6,14},{7,15},{8,0},{9,1},... | collective-permute-start | bytes 202760 | tf_op jit(solution)/shard_map/ppermute | solution.py:411
  39.9 7.2 %collective-permute-start.16 = (bf16[264,128]{1,0:T(8,128)(2,1)S(1)}, bf16[264,128]{1,0:T(8,128)(2,1)S(1)}, u32[]{:S(2)}, u32[]{:S(2)}) collective-permute-start(bf16[264,128]{1,0:T(8,128)(2,1)S(1)} %get-tuple-element.120), channel_id=1, source_target_pairs={{0,4},{1,5},{2,6},{3,7},{4,0},{5,1},{6,2},{7,3},{8,12},{9,13},{10,... | collective-permute-start | bytes 202760 | tf_op jit(solution)/shard_map/ppermute | solution.py:411
  42.9 6.8 %collective-permute-start.17 = (bf16[264,128]{1,0:T(8,128)(2,1)S(1)}, bf16[264,128]{1,0:T(8,128)(2,1)S(1)}, u32[]{:S(2)}, u32[]{:S(2)}) collective-permute-start(bf16[264,128]{1,0:T(8,128)(2,1)S(1)} %get-tuple-element.121), channel_id=1, source_target_pairs={{0,12},{1,13},{2,14},{3,15},{4,8},{5,9},{6,10},{7,11},{8,4},{9,5},... | collective-permute-start | bytes 202760 | tf_op jit(solution)/shard_map/ppermute | solution.py:411
  44.3 9.0 %collective-permute-start.19 = (bf16[264,128]{1,0:T(8,128)(2,1)S(1)}, bf16[264,128]{1,0:T(8,128)(2,1)S(1)}, u32[]{:S(2)}, u32[]{:S(2)}) collective-permute-start(bf16[264,128]{1,0:T(8,128)(2,1)S(1)} %get-tuple-element.123), channel_id=1, source_target_pairs={{0,9},{1,8},{2,11},{3,10},{4,13},{5,12},{6,15},{7,14},{8,1},{9,0},... | collective-permute-start | bytes 202760 | tf_op jit(solution)/shard_map/ppermute | solution.py:411
  46.9 6.8 %collective-permute-start.20 = (bf16[264,128]{1,0:T(8,128)(2,1)S(1)}, bf16[264,128]{1,0:T(8,128)(2,1)S(1)}, u32[]{:S(2)}, u32[]{:S(2)}) collective-permute-start(bf16[264,128]{1,0:T(8,128)(2,1)S(1)} %get-tuple-element.124), channel_id=1, source_target_pairs={{0,5},{1,4},{2,7},{3,6},{4,1},{5,0},{6,3},{7,2},{8,13},{9,12},{10,... | collective-permute-start | bytes 202760 | tf_op jit(solution)/shard_map/ppermute | solution.py:411
  47.0 9.5 %collective-permute-start.21 = (bf16[264,128]{1,0:T(8,128)(2,1)S(1)}, bf16[264,128]{1,0:T(8,128)(2,1)S(1)}, u32[]{:S(2)}, u32[]{:S(2)}) collective-permute-start(bf16[264,128]{1,0:T(8,128)(2,1)S(1)} %get-tuple-element.125), channel_id=1, source_target_pairs={{0,13},{1,12},{2,15},{3,14},{4,9},{5,8},{6,11},{7,10},{8,5},{9,4},... | collective-permute-start | bytes 202760 | tf_op jit(solution)/shard_map/ppermute | solution.py:411
  49.8 6.8 %collective-permute-start.22 = (bf16[264,128]{1,0:T(8,128)(2,1)S(1)}, bf16[264,128]{1,0:T(8,128)(2,1)S(1)}, u32[]{:S(2)}, u32[]{:S(2)}) collective-permute-start(bf16[264,128]{1,0:T(8,128)(2,1)S(1)} %get-tuple-element.126), channel_id=1, source_target_pairs={{0,2},{1,3},{2,0},{3,1},{4,6},{5,7},{6,4},{7,5},{8,10},{9,11},{10,... | collective-permute-start | bytes 202760 | tf_op jit(solution)/shard_map/ppermute | solution.py:411
  49.8 9.0 %collective-permute-start.23 = (bf16[264,128]{1,0:T(8,128)(2,1)S(1)}, bf16[264,128]{1,0:T(8,128)(2,1)S(1)}, u32[]{:S(2)}, u32[]{:S(2)}) collective-permute-start(bf16[264,128]{1,0:T(8,128)(2,1)S(1)} %get-tuple-element.127), channel_id=1, source_target_pairs={{0,10},{1,11},{2,8},{3,9},{4,14},{5,15},{6,12},{7,13},{8,2},{9,3},... | collective-permute-start | bytes 202760 | tf_op jit(solution)/shard_map/ppermute | solution.py:411
  53.2 6.6 %collective-permute-start.24 = (bf16[264,128]{1,0:T(8,128)(2,1)S(1)}, bf16[264,128]{1,0:T(8,128)(2,1)S(1)}, u32[]{:S(2)}, u32[]{:S(2)}) collective-permute-start(bf16[264,128]{1,0:T(8,128)(2,1)S(1)} %get-tuple-element.128), channel_id=1, source_target_pairs={{0,6},{1,7},{2,4},{3,5},{4,2},{5,3},{6,0},{7,1},{8,14},{9,15},{10,... | collective-permute-start | bytes 202760 | tf_op jit(solution)/shard_map/ppermute | solution.py:411
  53.7 9.0 %collective-permute-start.25 = (bf16[264,128]{1,0:T(8,128)(2,1)S(1)}, bf16[264,128]{1,0:T(8,128)(2,1)S(1)}, u32[]{:S(2)}, u32[]{:S(2)}) collective-permute-start(bf16[264,128]{1,0:T(8,128)(2,1)S(1)} %get-tuple-element.129), channel_id=1, source_target_pairs={{0,14},{1,15},{2,12},{3,13},{4,10},{5,11},{6,8},{7,9},{8,6},{9,7},... | collective-permute-start | bytes 202760 | tf_op jit(solution)/shard_map/ppermute | solution.py:411
  56.5 6.5 %collective-permute-start.27 = (bf16[264,128]{1,0:T(8,128)(2,1)S(1)}, bf16[264,128]{1,0:T(8,128)(2,1)S(1)}, u32[]{:S(2)}, u32[]{:S(2)}) collective-permute-start(bf16[264,128]{1,0:T(8,128)(2,1)S(1)} %get-tuple-element.131), channel_id=1, source_target_pairs={{0,11},{1,10},{2,9},{3,8},{4,15},{5,14},{6,13},{7,12},{8,3},{9,2},... | collective-permute-start | bytes 202760 | tf_op jit(solution)/shard_map/ppermute | solution.py:411
  59.8 6.5 %collective-permute-start.29 = (bf16[264,128]{1,0:T(8,128)(2,1)S(1)}, bf16[264,128]{1,0:T(8,128)(2,1)S(1)}, u32[]{:S(2)}, u32[]{:S(2)}) collective-permute-start(bf16[264,128]{1,0:T(8,128)(2,1)S(1)} %get-tuple-element.133), channel_id=1, source_target_pairs={{0,15},{1,14},{2,13},{3,12},{4,11},{5,10},{6,9},{7,8},{8,7},{9,6},... | collective-permute-start | bytes 202760 | tf_op jit(solution)/shard_map/ppermute | solution.py:411
  69.8 7.1 %collective-permute-start.30 = (bf16[264,128]{1,0:T(8,128)(2,1)S(1)}, bf16[264,128]{1,0:T(8,128)(2,1)S(1)}, u32[]{:S(2)}, u32[]{:S(2)}) collective-permute-start(bf16[264,128]{1,0:T(8,128)(2,1)S(1)} %get-tuple-element.137), channel_id=1, source_target_pairs={{0,8},{1,9},{2,10},{3,11},{4,12},{5,13},{6,14},{7,15},{8,0},{9,1},... | collective-permute-start | bytes 202760 | tf_op jit(solution)/shard_map/ppermute | solution.py:411
  70.6 7.3 %collective-permute-start.31 = (bf16[264,128]{1,0:T(8,128)(2,1)S(1)}, bf16[264,128]{1,0:T(8,128)(2,1)S(1)}, u32[]{:S(2)}, u32[]{:S(2)}) collective-permute-start(bf16[264,128]{1,0:T(8,128)(2,1)S(1)} %get-tuple-element.138), channel_id=1, source_target_pairs={{0,4},{1,5},{2,6},{3,7},{4,0},{5,1},{6,2},{7,3},{8,12},{9,13},{10,... | collective-permute-start | bytes 202760 | tf_op jit(solution)/shard_map/ppermute | solution.py:411
  72.9 6.7 %collective-permute-start.32 = (bf16[264,128]{1,0:T(8,128)(2,1)S(1)}, bf16[264,128]{1,0:T(8,128)(2,1)S(1)}, u32[]{:S(2)}, u32[]{:S(2)}) collective-permute-start(bf16[264,128]{1,0:T(8,128)(2,1)S(1)} %get-tuple-element.139), channel_id=1, source_target_pairs={{0,12},{1,13},{2,14},{3,15},{4,8},{5,9},{6,10},{7,11},{8,4},{9,5},... | collective-permute-start | bytes 202760 | tf_op jit(solution)/shard_map/ppermute | solution.py:411
  74.2 9.6 %collective-permute-start.34 = (bf16[264,128]{1,0:T(8,128)(2,1)S(1)}, bf16[264,128]{1,0:T(8,128)(2,1)S(1)}, u32[]{:S(2)}, u32[]{:S(2)}) collective-permute-start(bf16[264,128]{1,0:T(8,128)(2,1)S(1)} %get-tuple-element.141), channel_id=1, source_target_pairs={{0,9},{1,8},{2,11},{3,10},{4,13},{5,12},{6,15},{7,14},{8,1},{9,0},... | collective-permute-start | bytes 202760 | tf_op jit(solution)/shard_map/ppermute | solution.py:411
  76.8 7.0 %collective-permute-start.35 = (bf16[264,128]{1,0:T(8,128)(2,1)S(1)}, bf16[264,128]{1,0:T(8,128)(2,1)S(1)}, u32[]{:S(2)}, u32[]{:S(2)}) collective-permute-start(bf16[264,128]{1,0:T(8,128)(2,1)S(1)} %get-tuple-element.142), channel_id=1, source_target_pairs={{0,5},{1,4},{2,7},{3,6},{4,1},{5,0},{6,3},{7,2},{8,13},{9,12},{10,... | collective-permute-start | bytes 202760 | tf_op jit(solution)/shard_map/ppermute | solution.py:411
  77.9 8.4 %collective-permute-start.36 = (bf16[264,128]{1,0:T(8,128)(2,1)S(1)}, bf16[264,128]{1,0:T(8,128)(2,1)S(1)}, u32[]{:S(2)}, u32[]{:S(2)}) collective-permute-start(bf16[264,128]{1,0:T(8,128)(2,1)S(1)} %get-tuple-element.143), channel_id=1, source_target_pairs={{0,13},{1,12},{2,15},{3,14},{4,9},{5,8},{6,11},{7,10},{8,5},{9,4},... | collective-permute-start | bytes 202760 | tf_op jit(solution)/shard_map/ppermute | solution.py:411
  79.5 7.9 %collective-permute-start.37 = (bf16[264,128]{1,0:T(8,128)(2,1)S(1)}, bf16[264,128]{1,0:T(8,128)(2,1)S(1)}, u32[]{:S(2)}, u32[]{:S(2)}) collective-permute-start(bf16[264,128]{1,0:T(8,128)(2,1)S(1)} %get-tuple-element.144), channel_id=1, source_target_pairs={{0,2},{1,3},{2,0},{3,1},{4,6},{5,7},{6,4},{7,5},{8,10},{9,11},{10,... | collective-permute-start | bytes 202760 | tf_op jit(solution)/shard_map/ppermute | solution.py:411
  79.9 9.5 %collective-permute-start.38 = (bf16[264,128]{1,0:T(8,128)(2,1)S(1)}, bf16[264,128]{1,0:T(8,128)(2,1)S(1)}, u32[]{:S(2)}, u32[]{:S(2)}) collective-permute-start(bf16[264,128]{1,0:T(8,128)(2,1)S(1)} %get-tuple-element.145), channel_id=1, source_target_pairs={{0,10},{1,11},{2,8},{3,9},{4,14},{5,15},{6,12},{7,13},{8,2},{9,3},... | collective-permute-start | bytes 202760 | tf_op jit(solution)/shard_map/ppermute | solution.py:411
  83.8 6.3 %collective-permute-start.39 = (bf16[264,128]{1,0:T(8,128)(2,1)S(1)}, bf16[264,128]{1,0:T(8,128)(2,1)S(1)}, u32[]{:S(2)}, u32[]{:S(2)}) collective-permute-start(bf16[264,128]{1,0:T(8,128)(2,1)S(1)} %get-tuple-element.146), channel_id=1, source_target_pairs={{0,6},{1,7},{2,4},{3,5},{4,2},{5,3},{6,0},{7,1},{8,14},{9,15},{10,... | collective-permute-start | bytes 202760 | tf_op jit(solution)/shard_map/ppermute | solution.py:411
  83.8 8.7 %collective-permute-start.40 = (bf16[264,128]{1,0:T(8,128)(2,1)S(1)}, bf16[264,128]{1,0:T(8,128)(2,1)S(1)}, u32[]{:S(2)}, u32[]{:S(2)}) collective-permute-start(bf16[264,128]{1,0:T(8,128)(2,1)S(1)} %get-tuple-element.147), channel_id=1, source_target_pairs={{0,14},{1,15},{2,12},{3,13},{4,10},{5,11},{6,8},{7,9},{8,6},{9,7},... | collective-permute-start | bytes 202760 | tf_op jit(solution)/shard_map/ppermute | solution.py:411
  87.4 7.4 %collective-permute-start.42 = (bf16[264,128]{1,0:T(8,128)(2,1)S(1)}, bf16[264,128]{1,0:T(8,128)(2,1)S(1)}, u32[]{:S(2)}, u32[]{:S(2)}) collective-permute-start(bf16[264,128]{1,0:T(8,128)(2,1)S(1)} %get-tuple-element.149), channel_id=1, source_target_pairs={{0,11},{1,10},{2,9},{3,8},{4,15},{5,14},{6,13},{7,12},{8,3},{9,2},... | collective-permute-start | bytes 202760 | tf_op jit(solution)/shard_map/ppermute | solution.py:411
  90.1 6.8 %collective-permute-start.44 = (bf16[264,128]{1,0:T(8,128)(2,1)S(1)}, bf16[264,128]{1,0:T(8,128)(2,1)S(1)}, u32[]{:S(2)}, u32[]{:S(2)}) collective-permute-start(bf16[264,128]{1,0:T(8,128)(2,1)S(1)} %get-tuple-element.151), channel_id=1, source_target_pairs={{0,15},{1,14},{2,13},{3,12},{4,11},{5,10},{6,9},{7,8},{8,7},{9,6},... | collective-permute-start | bytes 202760 | tf_op jit(solution)/shard_map/ppermute | solution.py:411
  99.3 7.5 %collective-permute-start.45 = (bf16[264,128]{1,0:T(8,128)(2,1)S(1)}, bf16[264,128]{1,0:T(8,128)(2,1)S(1)}, u32[]{:S(2)}, u32[]{:S(2)}) collective-permute-start(bf16[264,128]{1,0:T(8,128)(2,1)S(1)} %get-tuple-element.155), channel_id=1, source_target_pairs={{0,8},{1,9},{2,10},{3,11},{4,12},{5,13},{6,14},{7,15},{8,0},{9,1},... | collective-permute-start | bytes 202760 | tf_op jit(solution)/shard_map/ppermute | solution.py:411
  100.0 6.8 %collective-permute-start.46 = (bf16[264,128]{1,0:T(8,128)(2,1)S(1)}, bf16[264,128]{1,0:T(8,128)(2,1)S(1)}, u32[]{:S(2)}, u32[]{:S(2)}) collective-permute-start(bf16[264,128]{1,0:T(8,128)(2,1)S(1)} %get-tuple-element.156), channel_id=1, source_target_pairs={{0,4},{1,5},{2,6},{3,7},{4,0},{5,1},{6,2},{7,3},{8,12},{9,13},{10,... | collective-permute-start | bytes 202760 | tf_op jit(solution)/shard_map/ppermute | solution.py:411
  102.0 8.9 %collective-permute-start.47 = (bf16[264,128]{1,0:T(8,128)(2,1)S(1)}, bf16[264,128]{1,0:T(8,128)(2,1)S(1)}, u32[]{:S(2)}, u32[]{:S(2)}) collective-permute-start(bf16[264,128]{1,0:T(8,128)(2,1)S(1)} %get-tuple-element.157), channel_id=1, source_target_pairs={{0,12},{1,13},{2,14},{3,15},{4,8},{5,9},{6,10},{7,11},{8,4},{9,5},... | collective-permute-start | bytes 202760 | tf_op jit(solution)/shard_map/ppermute | solution.py:411
  103.8 7.2 %collective-permute-start.48 = (bf16[264,128]{1,0:T(8,128)(2,1)S(1)}, bf16[264,128]{1,0:T(8,128)(2,1)S(1)}, u32[]{:S(2)}, u32[]{:S(2)}) collective-permute-start(bf16[264,128]{1,0:T(8,128)(2,1)S(1)} %get-tuple-element.158), channel_id=1, source_target_pairs={{0,1},{1,0},{2,3},{3,2},{4,5},{5,4},{6,7},{7,6},{8,9},{9,8},{10,11... | collective-permute-start | bytes 202760 | tf_op jit(solution)/shard_map/ppermute | solution.py:411
  103.8 9.5 %collective-permute-start.49 = (bf16[264,128]{1,0:T(8,128)(2,1)S(1)}, bf16[264,128]{1,0:T(8,128)(2,1)S(1)}, u32[]{:S(2)}, u32[]{:S(2)}) collective-permute-start(bf16[264,128]{1,0:T(8,128)(2,1)S(1)} %get-tuple-element.159), channel_id=1, source_target_pairs={{0,9},{1,8},{2,11},{3,10},{4,13},{5,12},{6,15},{7,14},{8,1},{9,0},... | collective-permute-start | bytes 202760 | tf_op jit(solution)/shard_map/ppermute | solution.py:411
  106.8 6.9 %collective-permute-start.50 = (bf16[264,128]{1,0:T(8,128)(2,1)S(1)}, bf16[264,128]{1,0:T(8,128)(2,1)S(1)}, u32[]{:S(2)}, u32[]{:S(2)}) collective-permute-start(bf16[264,128]{1,0:T(8,128)(2,1)S(1)} %get-tuple-element.160), channel_id=1, source_target_pairs={{0,5},{1,4},{2,7},{3,6},{4,1},{5,0},{6,3},{7,2},{8,13},{9,12},{10,... | collective-permute-start | bytes 202760 | tf_op jit(solution)/shard_map/ppermute | solution.py:411
  106.8 10.9 %collective-permute-start.51 = (bf16[264,128]{1,0:T(8,128)(2,1)S(1)}, bf16[264,128]{1,0:T(8,128)(2,1)S(1)}, u32[]{:S(2)}, u32[]{:S(2)}) collective-permute-start(bf16[264,128]{1,0:T(8,128)(2,1)S(1)} %get-tuple-element.161), channel_id=1, source_target_pairs={{0,13},{1,12},{2,15},{3,14},{4,9},{5,8},{6,11},{7,10},{8,5},{9,4},... | collective-permute-start | bytes 202760 | tf_op jit(solution)/shard_map/ppermute | solution.py:411
  110.9 6.8 %collective-permute-start.52 = (bf16[264,128]{1,0:T(8,128)(2,1)S(1)}, bf16[264,128]{1,0:T(8,128)(2,1)S(1)}, u32[]{:S(2)}, u32[]{:S(2)}) collective-permute-start(bf16[264,128]{1,0:T(8,128)(2,1)S(1)} %get-tuple-element.162), channel_id=1, source_target_pairs={{0,2},{1,3},{2,0},{3,1},{4,6},{5,7},{6,4},{7,5},{8,10},{9,11},{10,... | collective-permute-start | bytes 202760 | tf_op jit(solution)/shard_map/ppermute | solution.py:411
  110.9 7.9 %collective-permute-start.53 = (bf16[264,128]{1,0:T(8,128)(2,1)S(1)}, bf16[264,128]{1,0:T(8,128)(2,1)S(1)}, u32[]{:S(2)}, u32[]{:S(2)}) collective-permute-start(bf16[264,128]{1,0:T(8,128)(2,1)S(1)} %get-tuple-element.163), channel_id=1, source_target_pairs={{0,10},{1,11},{2,8},{3,9},{4,14},{5,15},{6,12},{7,13},{8,2},{9,3},... | collective-permute-start | bytes 202760 | tf_op jit(solution)/shard_map/ppermute | solution.py:411
  113.3 6.6 %collective-permute-start.54 = (bf16[264,128]{1,0:T(8,128)(2,1)S(1)}, bf16[264,128]{1,0:T(8,128)(2,1)S(1)}, u32[]{:S(2)}, u32[]{:S(2)}) collective-permute-start(bf16[264,128]{1,0:T(8,128)(2,1)S(1)} %get-tuple-element.164), channel_id=1, source_target_pairs={{0,6},{1,7},{2,4},{3,5},{4,2},{5,3},{6,0},{7,1},{8,14},{9,15},{10,... | collective-permute-start | bytes 202760 | tf_op jit(solution)/shard_map/ppermute | solution.py:411
  113.7 10.2 %collective-permute-start.55 = (bf16[264,128]{1,0:T(8,128)(2,1)S(1)}, bf16[264,128]{1,0:T(8,128)(2,1)S(1)}, u32[]{:S(2)}, u32[]{:S(2)}) collective-permute-start(bf16[264,128]{1,0:T(8,128)(2,1)S(1)} %get-tuple-element.165), channel_id=1, source_target_pairs={{0,14},{1,15},{2,12},{3,13},{4,10},{5,11},{6,8},{7,9},{8,6},{9,7},... | collective-permute-start | bytes 202760 | tf_op jit(solution)/shard_map/ppermute | solution.py:411
  117.7 7.5 %collective-permute-start.57 = (bf16[264,128]{1,0:T(8,128)(2,1)S(1)}, bf16[264,128]{1,0:T(8,128)(2,1)S(1)}, u32[]{:S(2)}, u32[]{:S(2)}) collective-permute-start(bf16[264,128]{1,0:T(8,128)(2,1)S(1)} %get-tuple-element.167), channel_id=1, source_target_pairs={{0,11},{1,10},{2,9},{3,8},{4,15},{5,14},{6,13},{7,12},{8,3},{9,2},... | collective-permute-start | bytes 202760 | tf_op jit(solution)/shard_map/ppermute | solution.py:411
  118.9 6.3 %collective-permute-start.58 = (bf16[264,128]{1,0:T(8,128)(2,1)S(1)}, bf16[264,128]{1,0:T(8,128)(2,1)S(1)}, u32[]{:S(2)}, u32[]{:S(2)}) collective-permute-start(bf16[264,128]{1,0:T(8,128)(2,1)S(1)} %get-tuple-element.168), channel_id=1, source_target_pairs={{0,7},{1,6},{2,5},{3,4},{4,3},{5,2},{6,1},{7,0},{8,15},{9,14},{10,... | collective-permute-start | bytes 202760 | tf_op jit(solution)/shard_map/ppermute | solution.py:411
  119.8 7.5 %collective-permute-start.59 = (bf16[264,128]{1,0:T(8,128)(2,1)S(1)}, bf16[264,128]{1,0:T(8,128)(2,1)S(1)}, u32[]{:S(2)}, u32[]{:S(2)}) collective-permute-start(bf16[264,128]{1,0:T(8,128)(2,1)S(1)} %get-tuple-element.169), channel_id=1, source_target_pairs={{0,15},{1,14},{2,13},{3,12},{4,11},{5,10},{6,9},{7,8},{8,7},{9,6},... | collective-permute-start | bytes 202760 | tf_op jit(solution)/shard_map/ppermute | solution.py:411
  130.8 7.0 %collective-permute-start.60 = (bf16[264,128]{1,0:T(8,128)(2,1)S(1)}, bf16[264,128]{1,0:T(8,128)(2,1)S(1)}, u32[]{:S(2)}, u32[]{:S(2)}) collective-permute-start(bf16[264,128]{1,0:T(8,128)(2,1)S(1)} %get-tuple-element.174), channel_id=1, source_target_pairs={{0,8},{1,9},{2,10},{3,11},{4,12},{5,13},{6,14},{7,15},{8,0},{9,1},... | collective-permute-start | bytes 202760 | tf_op jit(solution)/shard_map/ppermute | solution.py:411
  131.1 7.0 %collective-permute-start.61 = (bf16[264,128]{1,0:T(8,128)(2,1)S(1)}, bf16[264,128]{1,0:T(8,128)(2,1)S(1)}, u32[]{:S(2)}, u32[]{:S(2)}) collective-permute-start(bf16[264,128]{1,0:T(8,128)(2,1)S(1)} %get-tuple-element.175), channel_id=1, source_target_pairs={{0,4},{1,5},{2,6},{3,7},{4,0},{5,1},{6,2},{7,3},{8,12},{9,13},{10,... | collective-permute-start | bytes 202760 | tf_op jit(solution)/shard_map/ppermute | solution.py:411
  133.8 6.7 %collective-permute-start.62 = (bf16[264,128]{1,0:T(8,128)(2,1)S(1)}, bf16[264,128]{1,0:T(8,128)(2,1)S(1)}, u32[]{:S(2)}, u32[]{:S(2)}) collective-permute-start(bf16[264,128]{1,0:T(8,128)(2,1)S(1)} %get-tuple-element.176), channel_id=1, source_target_pairs={{0,12},{1,13},{2,14},{3,15},{4,8},{5,9},{6,10},{7,11},{8,4},{9,5},... | collective-permute-start | bytes 202760 | tf_op jit(solution)/shard_map/ppermute | solution.py:411
  135.2 9.3 %collective-permute-start.64 = (bf16[264,128]{1,0:T(8,128)(2,1)S(1)}, bf16[264,128]{1,0:T(8,128)(2,1)S(1)}, u32[]{:S(2)}, u32[]{:S(2)}) collective-permute-start(bf16[264,128]{1,0:T(8,128)(2,1)S(1)} %get-tuple-element.178), channel_id=1, source_target_pairs={{0,9},{1,8},{2,11},{3,10},{4,13},{5,12},{6,15},{7,14},{8,1},{9,0},... | collective-permute-start | bytes 202760 | tf_op jit(solution)/shard_map/ppermute | solution.py:411
  137.7 7.2 %collective-permute-start.65 = (bf16[264,128]{1,0:T(8,128)(2,1)S(1)}, bf16[264,128]{1,0:T(8,128)(2,1)S(1)}, u32[]{:S(2)}, u32[]{:S(2)}) collective-permute-start(bf16[264,128]{1,0:T(8,128)(2,1)S(1)} %get-tuple-element.179), channel_id=1, source_target_pairs={{0,5},{1,4},{2,7},{3,6},{4,1},{5,0},{6,3},{7,2},{8,13},{9,12},{10,... | collective-permute-start | bytes 202760 | tf_op jit(solution)/shard_map/ppermute | solution.py:411
  138.1 9.1 %collective-permute-start.66 = (bf16[264,128]{1,0:T(8,128)(2,1)S(1)}, bf16[264,128]{1,0:T(8,128)(2,1)S(1)}, u32[]{:S(2)}, u32[]{:S(2)}) collective-permute-start(bf16[264,128]{1,0:T(8,128)(2,1)S(1)} %get-tuple-element.180), channel_id=1, source_target_pairs={{0,13},{1,12},{2,15},{3,14},{4,9},{5,8},{6,11},{7,10},{8,5},{9,4},... | collective-permute-start | bytes 202760 | tf_op jit(solution)/shard_map/ppermute | solution.py:411
  140.4 7.0 %collective-permute-start.67 = (bf16[264,128]{1,0:T(8,128)(2,1)S(1)}, bf16[264,128]{1,0:T(8,128)(2,1)S(1)}, u32[]{:S(2)}, u32[]{:S(2)}) collective-permute-start(bf16[264,128]{1,0:T(8,128)(2,1)S(1)} %get-tuple-element.181), channel_id=1, source_target_pairs={{0,2},{1,3},{2,0},{3,1},{4,6},{5,7},{6,4},{7,5},{8,10},{9,11},{10,... | collective-permute-start | bytes 202760 | tf_op jit(solution)/shard_map/ppermute | solution.py:411
  141.1 9.0 %collective-permute-start.68 = (bf16[264,128]{1,0:T(8,128)(2,1)S(1)}, bf16[264,128]{1,0:T(8,128)(2,1)S(1)}, u32[]{:S(2)}, u32[]{:S(2)}) collective-permute-start(bf16[264,128]{1,0:T(8,128)(2,1)S(1)} %get-tuple-element.182), channel_id=1, source_target_pairs={{0,10},{1,11},{2,8},{3,9},{4,14},{5,15},{6,12},{7,13},{8,2},{9,3},... | collective-permute-start | bytes 202760 | tf_op jit(solution)/shard_map/ppermute | solution.py:411
  144.9 8.5 %collective-permute-start.70 = (bf16[264,128]{1,0:T(8,128)(2,1)S(1)}, bf16[264,128]{1,0:T(8,128)(2,1)S(1)}, u32[]{:S(2)}, u32[]{:S(2)}) collective-permute-start(bf16[264,128]{1,0:T(8,128)(2,1)S(1)} %get-tuple-element.184), channel_id=1, source_target_pairs={{0,14},{1,15},{2,12},{3,13},{4,10},{5,11},{6,8},{7,9},{8,6},{9,7},... | collective-permute-start | bytes 202760 | tf_op jit(solution)/shard_map/ppermute | solution.py:411
  147.2 6.4 %collective-permute-start.71 = (bf16[264,128]{1,0:T(8,128)(2,1)S(1)}, bf16[264,128]{1,0:T(8,128)(2,1)S(1)}, u32[]{:S(2)}, u32[]{:S(2)}) collective-permute-start(bf16[264,128]{1,0:T(8,128)(2,1)S(1)} %get-tuple-element.185), channel_id=1, source_target_pairs={{0,3},{1,2},{2,1},{3,0},{4,7},{5,6},{6,5},{7,4},{8,11},{9,10},{10,... | collective-permute-start | bytes 202760 | tf_op jit(solution)/shard_map/ppermute | solution.py:411
  147.5 7.7 %collective-permute-start.72 = (bf16[264,128]{1,0:T(8,128)(2,1)S(1)}, bf16[264,128]{1,0:T(8,128)(2,1)S(1)}, u32[]{:S(2)}, u32[]{:S(2)}) collective-permute-start(bf16[264,128]{1,0:T(8,128)(2,1)S(1)} %get-tuple-element.186), channel_id=1, source_target_pairs={{0,11},{1,10},{2,9},{3,8},{4,15},{5,14},{6,13},{7,12},{8,3},{9,2},... | collective-permute-start | bytes 202760 | tf_op jit(solution)/shard_map/ppermute | solution.py:411
  150.7 6.6 %collective-permute-start.74 = (bf16[264,128]{1,0:T(8,128)(2,1)S(1)}, bf16[264,128]{1,0:T(8,128)(2,1)S(1)}, u32[]{:S(2)}, u32[]{:S(2)}) collective-permute-start(bf16[264,128]{1,0:T(8,128)(2,1)S(1)} %get-tuple-element.188), channel_id=1, source_target_pairs={{0,15},{1,14},{2,13},{3,12},{4,11},{5,10},{6,9},{7,8},{8,7},{9,6},... | collective-permute-start | bytes 202760 | tf_op jit(solution)/shard_map/ppermute | solution.py:411
  (20 other events, 123.6 us)

commit v18 on v17

--- a/solution.py
+++ b/solution.py
@@ -461,20 +461,22 @@
         [whole, tile, ((8, BS), F32, VMEM)], (), 0, 8 << 20,
     )(asked, *arrived, models[-1], alphas[-1], betas[-1])
     betas.append(beta)
+    scratch = [VMEM(whole[0], F32), pltpu.SemaphoreType.DMA((CHUNKS,))]
+    (estimate,) = call(
+        estimate_kernel, "estimate", [VMEM] * (3 * ITERS + 1), [(whole[0], F32, HBM)], scratch,
+        0, 6 << 20,
+    )(*models, *alphas, *betas)
     reach, shares = peers, [share]
     while reach > 1:
         share = sum(shares[1:], shares[0])
-        low = max(reach // 4, 1)
+        if reach < peers:
+            share, estimate = lax.optimization_barrier((share, estimate))
+        low = reach // 2 if reach > 4 else 1
         shares = [share] + [
             lax.ppermute(share, "pair", [(one, one ^ step) for one in range(peers)])
             for step in range(low, reach, low)
         ]
         reach = low
-    scratch = [VMEM(whole[0], F32), pltpu.SemaphoreType.DMA((CHUNKS,))]
-    (estimate,) = call(
-        estimate_kernel, "estimate", [VMEM] * (3 * ITERS + 1), [(whole[0], F32, HBM)], scratch,
-        0, 6 << 20,
-    )(*models, *alphas, *betas)
     (model_vec,) = call(
         model_kernel, "model", [VMEM] * (len(shares) + 2), [(whole[0], F32, HBM)], scratch,
         0, 4 << 20,

time: 172 us -> 173 us (level)
  waiting for transfers between devices: 36.5 us -> 39 us
    ppermute x6 -> x5, waiting for transfers between devices: 3.23 us -> 6.81 us  [on_device(): lax.ppermute(share, 'pair', [(one, one ^ step) for one in range(peers)])]
    ppermute x6 -> x5, starting transfers between devices: 6.39 us -> 3.46 us  [on_device(): lax.ppermute(share, 'pair', [(one, one ^ step) for one in range(peers)])]
  transfers between devices with their start and end apart: 81 -> 80, of which waited for: 30 -> 30; matrix products, arithmetic and copies ran while one was open for 0% -> 0% of each run, Pallas kernels for 3% -> 3%
where the time goes in v18:
time: 173 us
  starting transfers between devices  107 us (62%)
  waiting for transfers between devices  39 us (23%)
  Pallas kernels  25.2 us (15%)
    ppermute x75, starting transfers between devices, exchange(): lax.ppermute(value, 'pair', [(one, one ^ step) for one in range(peers)])  103 us
    ppermute x75, waiting for transfers between devices, exchange(): lax.ppermute(value, 'pair', [(one, one ^ step) for one in range(peers)])  32.2 us
    pallas_call x2, Pallas kernels, on_device(): call(functools.partial(pair_kernel, peers), 'pairs_last' if last else 'pa...  6.89 us
    ppermute x5, waiting for transfers between devices, on_device(): lax.ppermute(share, 'pair', [(one, one ^ step) for one in range(peers)])  6.81 us
    pallas_call x1, Pallas kernels, on_device(): call(functools.partial(start_kernel, peers), 'start', [SMEM, HBM, HBM, HB...  5.37 us
    ppermute x5, starting transfers between devices, on_device(): lax.ppermute(share, 'pair', [(one, one ^ step) for one in range(peers)])  3.46 us
  transfers between devices with their start and end apart: 80, of which 30 were waited for; matrix products, arithmetic and copies ran while one was open for 0% of the time, Pallas kernels for 3%

profile of v18, /device:TPU:0, one launch (start us, length us, event | category | flops | bytes accessed | tf_op | source)
XLA Modules:
  0.0 173.4 jit_solution(11709203866772881215)
XLA Ops:
  0.6 5.4 %start.1 = (bf16[264,128]{1,0:T(8,128)(2,1)}, bf16[264,128]{1,0:T(8,128)(2,1)}, bf16[264,128]{1,0:T(8,128)(2,1)}, bf16[264,128]{1,0:T(8,128)(2,1)}, bf16[264,128...) custom-call(s32[1]{0:T(128)} %bitcast.me_ref, ...), custom_call_target="tpu_custom_call" | custom-call | flops 268435456 | bytes 6291456 | tf_op jit(solution)/shard_map/start/pallas_call | solution.py:416
  6.0 4.2 %collective-permute-start = (bf16[264,128]{1,0:T(8,128)(2,1)}, bf16[264,128]{1,0:T(8,128)(2,1)S(1)}, u32[]{:S(2)}, u32[]{:S(2)}) collective-permute-start(bf16[264,128]{1,0:T(8,128)(2,1)} %get-tuple-element.104), channel_id=1, source_target_pairs={{0,8},{1,9},{2,10},{3,11},{4,12},{5,13},{6,14},{7,15},{8,0},{9,1},... | collective-permute-start | bytes 202760 | tf_op jit(solution)/shard_map/ppermute | solution.py:411
  10.2 1.5 collective-permute-start.1
  11.7 2.1 %collective-permute-start.4 = (bf16[264,128]{1,0:T(8,128)(2,1)}, bf16[264,128]{1,0:T(8,128)(2,1)S(1)}, u32[]{:S(2)}, u32[]{:S(2)}) collective-permute-start(bf16[264,128]{1,0:T(8,128)(2,1)} %get-tuple-element.108), channel_id=1, source_target_pairs={{0,9},{1,8},{2,11},{3,10},{4,13},{5,12},{6,15},{7,14},{8,1},{9,0},... | collective-permute-start | bytes 202760 | tf_op jit(solution)/shard_map/ppermute | solution.py:411
  13.8 2.0 %collective-permute-start.5 = (bf16[264,128]{1,0:T(8,128)(2,1)}, bf16[264,128]{1,0:T(8,128)(2,1)S(1)}, u32[]{:S(2)}, u32[]{:S(2)}) collective-permute-start(bf16[264,128]{1,0:T(8,128)(2,1)} %get-tuple-element.109), channel_id=1, source_target_pairs={{0,5},{1,4},{2,7},{3,6},{4,1},{5,0},{6,3},{7,2},{8,13},{9,12},{10,... | collective-permute-start | bytes 202760 | tf_op jit(solution)/shard_map/ppermute | solution.py:411
  15.8 1.6 collective-permute-start.6
  17.4 1.4 collective-permute-done.2.refs_3_
  18.7 1.5 collective-permute-start.7
  20.3 2.6 %collective-permute-start.8 = (bf16[264,128]{1,0:T(8,128)(2,1)}, bf16[264,128]{1,0:T(8,128)(2,1)S(1)}, u32[]{:S(2)}, u32[]{:S(2)}) collective-permute-start(bf16[264,128]{1,0:T(8,128)(2,1)} %get-tuple-element.112), channel_id=1, source_target_pairs={{0,10},{1,11},{2,8},{3,9},{4,14},{5,15},{6,12},{7,13},{8,2},{9,3},... | collective-permute-start | bytes 202760 | tf_op jit(solution)/shard_map/ppermute | solution.py:411
  23.9 2.7 %collective-permute-start.10 = (bf16[264,128]{1,0:T(8,128)(2,1)}, bf16[264,128]{1,0:T(8,128)(2,1)S(1)}, u32[]{:S(2)}, u32[]{:S(2)}) collective-permute-start(bf16[264,128]{1,0:T(8,128)(2,1)} %get-tuple-element.114), channel_id=1, source_target_pairs={{0,14},{1,15},{2,12},{3,13},{4,10},{5,11},{6,8},{7,9},{8,6},{9,7},... | collective-permute-start | bytes 202760 | tf_op jit(solution)/shard_map/ppermute | solution.py:411
  29.3 3.6 %collective-permute-start.14 = (bf16[264,128]{1,0:T(8,128)(2,1)}, bf16[264,128]{1,0:T(8,128)(2,1)S(1)}, u32[]{:S(2)}, u32[]{:S(2)}) collective-permute-start(bf16[264,128]{1,0:T(8,128)(2,1)} %get-tuple-element.118), channel_id=1, source_target_pairs={{0,15},{1,14},{2,13},{3,12},{4,11},{5,10},{6,9},{7,8},{8,7},{9,6},... | collective-permute-start | bytes 202760 | tf_op jit(solution)/shard_map/ppermute | solution.py:411
  34.4 2.9 %keep.1 = (s32[128]{0:T(128)S(1)}, bf16[264,128]{1,0:T(8,128)(2,1)S(1)}, bf16[8,16,128,128]{3,2,1,0:T(8,128)(2,1)S(1)}) custom-call(s32[128]{0:T(128)S(1)} %copy-done.2, bf16[264,128]{1,0:T(8,128)(2,1)S(1)} %copy-done.1, bf16[8,16,128,128]{3,2,1,0:T(8,128)(2,1)} %rays_hbm.3), custom_call_target="tpu_custom_call" | custom-call | bytes 8388608 | tf_op jit(solution)/shard_map/keep/pallas_call | solution.py:428
  37.3 2.5 %cells_first.1 = (f32[64,8192]{1,0:T(8,128)S(1)}, f32[64,128]{1,0:T(8,128)S(1)}, bf16[264,128]{1,0:T(8,128)(2,1)S(1)}, bf16[264,128]{1,0:T(8,128)(2,1)S(1)}, bf1...) custom-call(bf16[264,128]{1,0:T(8,128)(2,1)S(1)} %get-tuple-element., ...), custom_call_target="tpu_custom_call" | custom-call | bytes 6291456 | tf_op jit(solution)/shard_map/cells_first/pallas_call | solution.py:433
  40.0 3.1 %collective-permute-start.16 = (bf16[264,128]{1,0:T(8,128)(2,1)S(1)}, bf16[264,128]{1,0:T(8,128)(2,1)S(1)}, u32[]{:S(2)}, u32[]{:S(2)}) collective-permute-start(bf16[264,128]{1,0:T(8,128)(2,1)S(1)} %get-tuple-element.123), channel_id=1, source_target_pairs={{0,4},{1,5},{2,6},{3,7},{4,0},{5,1},{6,2},{7,3},{8,12},{9,13},{10,... | collective-permute-start | bytes 202760 | tf_op jit(solution)/shard_map/ppermute | solution.py:411
  43.0 1.3 collective-permute-start.17
  44.6 2.1 %collective-permute-done.15.refs_1_ = bf16[264,128]{1,0:T(8,128)(2,1)S(1)} collective-permute-done((bf16[264,128]{1,0:T(8,128)(2,1)S(1)}, bf16[264,128]{1,0:T(8,128)(2,1)S(1)}, u32[]{:S(2)}, u32[]{:S(2)}) %collective-permute-start.15) | collective-permute-done | bytes 67616 | tf_op jit(solution)/shard_map/ppermute | solution.py:411
  47.2 1.4 collective-permute-start.21
  48.6 1.3 collective-permute-done.17.refs_3_
  49.9 3.4 %collective-permute-start.23 = (bf16[264,128]{1,0:T(8,128)(2,1)S(1)}, bf16[264,128]{1,0:T(8,128)(2,1)S(1)}, u32[]{:S(2)}, u32[]{:S(2)}) collective-permute-start(bf16[264,128]{1,0:T(8,128)(2,1)S(1)} %get-tuple-element.130), channel_id=1, source_target_pairs={{0,10},{1,11},{2,8},{3,9},{4,14},{5,15},{6,12},{7,13},{8,2},{9,3},... | collective-permute-start | bytes 202760 | tf_op jit(solution)/shard_map/ppermute | solution.py:411
  53.8 2.8 %collective-permute-start.25 = (bf16[264,128]{1,0:T(8,128)(2,1)S(1)}, bf16[264,128]{1,0:T(8,128)(2,1)S(1)}, u32[]{:S(2)}, u32[]{:S(2)}) collective-permute-start(bf16[264,128]{1,0:T(8,128)(2,1)S(1)} %get-tuple-element.132), channel_id=1, source_target_pairs={{0,14},{1,15},{2,12},{3,13},{4,10},{5,11},{6,8},{7,9},{8,6},{9,7},... | collective-permute-start | bytes 202760 | tf_op jit(solution)/shard_map/ppermute | solution.py:411
  56.7 2.3 %collective-permute-start.27 = (bf16[264,128]{1,0:T(8,128)(2,1)S(1)}, bf16[264,128]{1,0:T(8,128)(2,1)S(1)}, u32[]{:S(2)}, u32[]{:S(2)}) collective-permute-start(bf16[264,128]{1,0:T(8,128)(2,1)S(1)} %get-tuple-element.134), channel_id=1, source_target_pairs={{0,11},{1,10},{2,9},{3,8},{4,15},{5,14},{6,13},{7,12},{8,3},{9,2},... | collective-permute-start | bytes 202760 | tf_op jit(solution)/shard_map/ppermute | solution.py:411
  59.9 2.9 %collective-permute-start.29 = (bf16[264,128]{1,0:T(8,128)(2,1)S(1)}, bf16[264,128]{1,0:T(8,128)(2,1)S(1)}, u32[]{:S(2)}, u32[]{:S(2)}) collective-permute-start(bf16[264,128]{1,0:T(8,128)(2,1)S(1)} %get-tuple-element.136), channel_id=1, source_target_pairs={{0,15},{1,14},{2,13},{3,12},{4,11},{5,10},{6,9},{7,8},{8,7},{9,6},... | collective-permute-start | bytes 202760 | tf_op jit(solution)/shard_map/ppermute | solution.py:411
  63.1 1.8 %collective-permute-done.28.refs_14_ = bf16[264,128]{1,0:T(8,128)(2,1)S(1)} collective-permute-done((bf16[264,128]{1,0:T(8,128)(2,1)S(1)}, bf16[264,128]{1,0:T(8,128)(2,1)S(1)}, u32[]{:S(2)}, u32[]{:S(2)}) %collective-permute-start.28) | collective-permute-done | bytes 67616 | tf_op jit(solution)/shard_map/ppermute | solution.py:411
  64.9 1.6 collective-permute-done.29.refs_15_
  66.5 3.4 %pairs.1 = (bf16[264,128]{1,0:T(8,128)(2,1)S(1)}, bf16[264,128]{1,0:T(8,128)(2,1)S(1)}, bf16[264,128]{1,0:T(8,128)(2,1)S(1)}, bf16[264,128]{1,0:T(8,128)(2,1)S(1...) custom-call(s32[128]{0:T(128)S(1)} %get-tuple-element.120.target_ref, ...), custom_call_target="tpu_custom_call" | custom-call | flops 536870912 | bytes 8388608 | tf_op jit(solution)/shard_map/pairs/pallas_call | solution.py:444
  69.9 1.2 collective-permute-start.30
  71.1 1.9 %collective-permute-start.31 = (bf16[264,128]{1,0:T(8,128)(2,1)S(1)}, bf16[264,128]{1,0:T(8,128)(2,1)S(1)}, u32[]{:S(2)}, u32[]{:S(2)}) collective-permute-start(bf16[264,128]{1,0:T(8,128)(2,1)S(1)} %get-tuple-element.141), channel_id=1, source_target_pairs={{0,4},{1,5},{2,6},{3,7},{4,0},{5,1},{6,2},{7,3},{8,12},{9,13},{10,... | collective-permute-start | bytes 202760 | tf_op jit(solution)/shard_map/ppermute | solution.py:411
  73.0 1.4 collective-permute-start.32
  74.7 2.3 %collective-permute-done.30.refs_1_ = bf16[264,128]{1,0:T(8,128)(2,1)S(1)} collective-permute-done((bf16[264,128]{1,0:T(8,128)(2,1)S(1)}, bf16[264,128]{1,0:T(8,128)(2,1)S(1)}, u32[]{:S(2)}, u32[]{:S(2)}) %collective-permute-start.30) | collective-permute-done | bytes 67616 | tf_op jit(solution)/shard_map/ppermute | solution.py:411
  80.3 4.1 %collective-permute-start.38 = (bf16[264,128]{1,0:T(8,128)(2,1)S(1)}, bf16[264,128]{1,0:T(8,128)(2,1)S(1)}, u32[]{:S(2)}, u32[]{:S(2)}) collective-permute-start(bf16[264,128]{1,0:T(8,128)(2,1)S(1)} %get-tuple-element.148), channel_id=1, source_target_pairs={{0,10},{1,11},{2,8},{3,9},{4,14},{5,15},{6,12},{7,13},{8,2},{9,3},... | collective-permute-start | bytes 202760 | tf_op jit(solution)/shard_map/ppermute | solution.py:411
  84.3 2.1 %collective-permute-start.40 = (bf16[264,128]{1,0:T(8,128)(2,1)S(1)}, bf16[264,128]{1,0:T(8,128)(2,1)S(1)}, u32[]{:S(2)}, u32[]{:S(2)}) collective-permute-start(bf16[264,128]{1,0:T(8,128)(2,1)S(1)} %get-tuple-element.150), channel_id=1, source_target_pairs={{0,14},{1,15},{2,12},{3,13},{4,10},{5,11},{6,8},{7,9},{8,6},{9,7},... | collective-permute-start | bytes 202760 | tf_op jit(solution)/shard_map/ppermute | solution.py:411
  87.3 2.6 %collective-permute-start.42 = (bf16[264,128]{1,0:T(8,128)(2,1)S(1)}, bf16[264,128]{1,0:T(8,128)(2,1)S(1)}, u32[]{:S(2)}, u32[]{:S(2)}) collective-permute-start(bf16[264,128]{1,0:T(8,128)(2,1)S(1)} %get-tuple-element.152), channel_id=1, source_target_pairs={{0,11},{1,10},{2,9},{3,8},{4,15},{5,14},{6,13},{7,12},{8,3},{9,2},... | collective-permute-start | bytes 202760 | tf_op jit(solution)/shard_map/ppermute | solution.py:411
  90.1 3.2 %collective-permute-start.44 = (bf16[264,128]{1,0:T(8,128)(2,1)S(1)}, bf16[264,128]{1,0:T(8,128)(2,1)S(1)}, u32[]{:S(2)}, u32[]{:S(2)}) collective-permute-start(bf16[264,128]{1,0:T(8,128)(2,1)S(1)} %get-tuple-element.154), channel_id=1, source_target_pairs={{0,15},{1,14},{2,13},{3,12},{4,11},{5,10},{6,9},{7,8},{8,7},{9,6},... | collective-permute-start | bytes 202760 | tf_op jit(solution)/shard_map/ppermute | solution.py:411
  93.3 1.4 collective-permute-done.42.refs_13_
  96.8 2.4 %cells.1 = (f32[64,8192]{1,0:T(8,128)S(1)}, f32[64,128]{1,0:T(8,128)S(1)}, bf16[264,128]{1,0:T(8,128)(2,1)S(1)}, bf16[264,128]{1,0:T(8,128)(2,1)S(1)}, bf16[264,...) custom-call(s32[16,128]{1,0:T(8,128)S(1)} %get-tuple-element.119.ask, ...), custom_call_target="tpu_custom_call" | custom-call | bytes 8388608 | tf_op jit(solution)/shard_map/cells/pallas_call | solution.py:453
  100.0 1.9 %collective-permute-start.46 = (bf16[264,128]{1,0:T(8,128)(2,1)S(1)}, bf16[264,128]{1,0:T(8,128)(2,1)S(1)}, u32[]{:S(2)}, u32[]{:S(2)}) collective-permute-start(bf16[264,128]{1,0:T(8,128)(2,1)S(1)} %get-tuple-element.159), channel_id=1, source_target_pairs={{0,4},{1,5},{2,6},{3,7},{4,0},{5,1},{6,2},{7,3},{8,12},{9,13},{10,... | collective-permute-start | bytes 202760 | tf_op jit(solution)/shard_map/ppermute | solution.py:411
  101.9 1.8 %collective-permute-start.47 = (bf16[264,128]{1,0:T(8,128)(2,1)S(1)}, bf16[264,128]{1,0:T(8,128)(2,1)S(1)}, u32[]{:S(2)}, u32[]{:S(2)}) collective-permute-start(bf16[264,128]{1,0:T(8,128)(2,1)S(1)} %get-tuple-element.160), channel_id=1, source_target_pairs={{0,12},{1,13},{2,14},{3,15},{4,8},{5,9},{6,10},{7,11},{8,4},{9,5},... | collective-permute-start | bytes 202760 | tf_op jit(solution)/shard_map/ppermute | solution.py:411
  103.7 3.2 %collective-permute-done.45.refs_1_ = bf16[264,128]{1,0:T(8,128)(2,1)S(1)} collective-permute-done((bf16[264,128]{1,0:T(8,128)(2,1)S(1)}, bf16[264,128]{1,0:T(8,128)(2,1)S(1)}, u32[]{:S(2)}, u32[]{:S(2)}) %collective-permute-start.45) | collective-permute-done | bytes 67616 | tf_op jit(solution)/shard_map/ppermute | solution.py:411
  106.9 4.0 %collective-permute-start.51 = (bf16[264,128]{1,0:T(8,128)(2,1)S(1)}, bf16[264,128]{1,0:T(8,128)(2,1)S(1)}, u32[]{:S(2)}, u32[]{:S(2)}) collective-permute-start(bf16[264,128]{1,0:T(8,128)(2,1)S(1)} %get-tuple-element.164), channel_id=1, source_target_pairs={{0,13},{1,12},{2,15},{3,14},{4,9},{5,8},{6,11},{7,10},{8,5},{9,4},... | collective-permute-start | bytes 202760 | tf_op jit(solution)/shard_map/ppermute | solution.py:411
  111.6 1.7 collective-permute-start.53
  114.1 3.5 %collective-permute-start.55 = (bf16[264,128]{1,0:T(8,128)(2,1)S(1)}, bf16[264,128]{1,0:T(8,128)(2,1)S(1)}, u32[]{:S(2)}, u32[]{:S(2)}) collective-permute-start(bf16[264,128]{1,0:T(8,128)(2,1)S(1)} %get-tuple-element.168), channel_id=1, source_target_pairs={{0,14},{1,15},{2,12},{3,13},{4,10},{5,11},{6,8},{7,9},{8,6},{9,7},... | collective-permute-start | bytes 202760 | tf_op jit(solution)/shard_map/ppermute | solution.py:411
  117.7 1.2 collective-permute-start.57
  120.2 3.7 %collective-permute-start.59 = (bf16[264,128]{1,0:T(8,128)(2,1)S(1)}, bf16[264,128]{1,0:T(8,128)(2,1)S(1)}, u32[]{:S(2)}, u32[]{:S(2)}) collective-permute-start(bf16[264,128]{1,0:T(8,128)(2,1)S(1)} %get-tuple-element.172), channel_id=1, source_target_pairs={{0,15},{1,14},{2,13},{3,12},{4,11},{5,10},{6,9},{7,8},{8,7},{9,6},... | collective-permute-start | bytes 202760 | tf_op jit(solution)/shard_map/ppermute | solution.py:411
  123.9 1.5 collective-permute-done.57.refs_13_
  125.9 1.4 collective-permute-done.59.refs_15_
  127.3 3.4 %pairs_last.1 = (bf16[264,128]{1,0:T(8,128)(2,1)S(1)}, bf16[264,128]{1,0:T(8,128)(2,1)S(1)}, bf16[264,128]{1,0:T(8,128)(2,1)S(1)}, bf16[264,128]{1,0:T(8,128)(2,...) custom-call(s32[128]{0:T(128)S(1)} %get-tuple-element.120.target_ref, ...), custom_call_target="tpu_custom_call" | custom-call | flops 536870912 | bytes 8388608 | tf_op jit(solution)/shard_map/pairs_last/pallas_call | solution.py:444
  131.1 2.2 %collective-permute-start.61 = (bf16[264,128]{1,0:T(8,128)(2,1)S(1)}, bf16[264,128]{1,0:T(8,128)(2,1)S(1)}, u32[]{:S(2)}, u32[]{:S(2)}) collective-permute-start(bf16[264,128]{1,0:T(8,128)(2,1)S(1)} %get-tuple-element.177), channel_id=1, source_target_pairs={{0,4},{1,5},{2,6},{3,7},{4,0},{5,1},{6,2},{7,3},{8,12},{9,13},{10,... | collective-permute-start | bytes 202760 | tf_op jit(solution)/shard_map/ppermute | solution.py:411
  133.3 1.9 %collective-permute-start.62 = (bf16[264,128]{1,0:T(8,128)(2,1)S(1)}, bf16[264,128]{1,0:T(8,128)(2,1)S(1)}, u32[]{:S(2)}, u32[]{:S(2)}) collective-permute-start(bf16[264,128]{1,0:T(8,128)(2,1)S(1)} %get-tuple-element.178), channel_id=1, source_target_pairs={{0,12},{1,13},{2,14},{3,15},{4,8},{5,9},{6,10},{7,11},{8,4},{9,5},... | collective-permute-start | bytes 202760 | tf_op jit(solution)/shard_map/ppermute | solution.py:411
  135.2 2.2 %collective-permute-done.60.refs_1_ = bf16[264,128]{1,0:T(8,128)(2,1)S(1)} collective-permute-done((bf16[264,128]{1,0:T(8,128)(2,1)S(1)}, bf16[264,128]{1,0:T(8,128)(2,1)S(1)}, u32[]{:S(2)}, u32[]{:S(2)}) %collective-permute-start.60) | collective-permute-done | bytes 67616 | tf_op jit(solution)/shard_map/ppermute | solution.py:411
  137.5 2.3 %collective-permute-start.66 = (bf16[264,128]{1,0:T(8,128)(2,1)S(1)}, bf16[264,128]{1,0:T(8,128)(2,1)S(1)}, u32[]{:S(2)}, u32[]{:S(2)}) collective-permute-start(bf16[264,128]{1,0:T(8,128)(2,1)S(1)} %get-tuple-element.182), channel_id=1, source_target_pairs={{0,13},{1,12},{2,15},{3,14},{4,9},{5,8},{6,11},{7,10},{8,5},{9,4},... | collective-permute-start | bytes 202760 | tf_op jit(solution)/shard_map/ppermute | solution.py:411
  140.1 1.2 collective-permute-start.67
  141.3 3.1 %collective-permute-start.68 = (bf16[264,128]{1,0:T(8,128)(2,1)S(1)}, bf16[264,128]{1,0:T(8,128)(2,1)S(1)}, u32[]{:S(2)}, u32[]{:S(2)}) collective-permute-start(bf16[264,128]{1,0:T(8,128)(2,1)S(1)} %get-tuple-element.184), channel_id=1, source_target_pairs={{0,10},{1,11},{2,8},{3,9},{4,14},{5,15},{6,12},{7,13},{8,2},{9,3},... | collective-permute-start | bytes 202760 | tf_op jit(solution)/shard_map/ppermute | solution.py:411
  145.1 2.5 %collective-permute-start.70 = (bf16[264,128]{1,0:T(8,128)(2,1)S(1)}, bf16[264,128]{1,0:T(8,128)(2,1)S(1)}, u32[]{:S(2)}, u32[]{:S(2)}) collective-permute-start(bf16[264,128]{1,0:T(8,128)(2,1)S(1)} %get-tuple-element.186), channel_id=1, source_target_pairs={{0,14},{1,15},{2,12},{3,13},{4,10},{5,11},{6,8},{7,9},{8,6},{9,7},... | collective-permute-start | bytes 202760 | tf_op jit(solution)/shard_map/ppermute | solution.py:411
  147.6 2.4 %collective-permute-start.72 = (bf16[264,128]{1,0:T(8,128)(2,1)S(1)}, bf16[264,128]{1,0:T(8,128)(2,1)S(1)}, u32[]{:S(2)}, u32[]{:S(2)}) collective-permute-start(bf16[264,128]{1,0:T(8,128)(2,1)S(1)} %get-tuple-element.188), channel_id=1, source_target_pairs={{0,11},{1,10},{2,9},{3,8},{4,15},{5,14},{6,13},{7,12},{8,3},{9,2},... | collective-permute-start | bytes 202760 | tf_op jit(solution)/shard_map/ppermute | solution.py:411
  151.1 2.7 %collective-permute-start.74 = (bf16[264,128]{1,0:T(8,128)(2,1)S(1)}, bf16[264,128]{1,0:T(8,128)(2,1)S(1)}, u32[]{:S(2)}, u32[]{:S(2)}) collective-permute-start(bf16[264,128]{1,0:T(8,128)(2,1)S(1)} %get-tuple-element.190), channel_id=1, source_target_pairs={{0,15},{1,14},{2,13},{3,12},{4,11},{5,10},{6,9},{7,8},{8,7},{9,6},... | collective-permute-start | bytes 202760 | tf_op jit(solution)/shard_map/ppermute | solution.py:411
  153.8 1.6 collective-permute-done.72.refs_13_
  156.1 1.7 collective-permute-done.74.refs_15_
  157.9 2.0 %cells_last.1 = (f32[64,8192]{1,0:T(8,128)S(1)}, f32[64,128]{1,0:T(8,128)S(1)}, f32[8,128]{1,0:T(8,128)S(1)}) custom-call(s32[16,128]{1,0:T(8,128)S(1)} %get-tuple-element.119.asked_ref, bf16[264,128]{1,0:T(8,128)(2,1)S(1)} %get-tuple-element.175.refs_0_, bf16[264,128]{1,0:T(8,128)(2,1)S(1)} %collective-permute-done.60.refs_1_, ...), custom_call_target="tpu_custom_call" | custom-call | bytes 8388608 | tf_op jit(solution)/shard_map/cells_last/pallas_call | solution.py:459
  159.9 1.5 collective-permute-start.75
  161.3 1.5 estimate.1
  162.9 1.6 collective-permute-done.75
  164.6 3.5 %collective-permute-done.76 = f32[8,128]{1,0:T(8,128)S(1)} collective-permute-done((f32[8,128]{1,0:T(8,128)S(1)}, f32[8,128]{1,0:T(8,128)S(1)}, u32[]{:S(2)}, u32[]{:S(2)}) %collective-permute-start.76) | collective-permute-done | bytes 4128 | tf_op jit(solution)/shard_map/ppermute | solution.py:476
  169.9 1.2 collective-permute-done.79.refs_3_
  171.7 1.5 model.1
  (113 shorter events, 24.8 us)
Async XLA Ops:
  6.0 7.8 %collective-permute-start = (bf16[264,128]{1,0:T(8,128)(2,1)}, bf16[264,128]{1,0:T(8,128)(2,1)S(1)}, u32[]{:S(2)}, u32[]{:S(2)}) collective-permute-start(bf16[264,128]{1,0:T(8,128)(2,1)} %get-tuple-element.104), channel_id=1, source_target_pairs={{0,8},{1,9},{2,10},{3,11},{4,12},{5,13},{6,14},{7,15},{8,0},{9,1},... | collective-permute-start | bytes 202760 | tf_op jit(solution)/shard_map/ppermute | solution.py:411
  11.7 7.1 %collective-permute-start.2 = (bf16[264,128]{1,0:T(8,128)(2,1)}, bf16[264,128]{1,0:T(8,128)(2,1)S(1)}, u32[]{:S(2)}, u32[]{:S(2)}) collective-permute-start(bf16[264,128]{1,0:T(8,128)(2,1)} %get-tuple-element.106), channel_id=1, source_target_pairs={{0,12},{1,13},{2,14},{3,15},{4,8},{5,9},{6,10},{7,11},{8,4},{9,5},... | collective-permute-start | bytes 202760 | tf_op jit(solution)/shard_map/ppermute | solution.py:411
  11.7 8.5 %collective-permute-start.3 = (bf16[264,128]{1,0:T(8,128)(2,1)}, bf16[264,128]{1,0:T(8,128)(2,1)S(1)}, u32[]{:S(2)}, u32[]{:S(2)}) collective-permute-start(bf16[264,128]{1,0:T(8,128)(2,1)} %get-tuple-element.107), channel_id=1, source_target_pairs={{0,1},{1,0},{2,3},{3,2},{4,5},{5,4},{6,7},{7,6},{8,9},{9,8},{10,11... | collective-permute-start | bytes 202760 | tf_op jit(solution)/shard_map/ppermute | solution.py:411
  11.7 11.1 %collective-permute-start.4 = (bf16[264,128]{1,0:T(8,128)(2,1)}, bf16[264,128]{1,0:T(8,128)(2,1)S(1)}, u32[]{:S(2)}, u32[]{:S(2)}) collective-permute-start(bf16[264,128]{1,0:T(8,128)(2,1)} %get-tuple-element.108), channel_id=1, source_target_pairs={{0,9},{1,8},{2,11},{3,10},{4,13},{5,12},{6,15},{7,14},{8,1},{9,0},... | collective-permute-start | bytes 202760 | tf_op jit(solution)/shard_map/ppermute | solution.py:411
  13.8 10.1 %collective-permute-start.5 = (bf16[264,128]{1,0:T(8,128)(2,1)}, bf16[264,128]{1,0:T(8,128)(2,1)S(1)}, u32[]{:S(2)}, u32[]{:S(2)}) collective-permute-start(bf16[264,128]{1,0:T(8,128)(2,1)} %get-tuple-element.109), channel_id=1, source_target_pairs={{0,5},{1,4},{2,7},{3,6},{4,1},{5,0},{6,3},{7,2},{8,13},{9,12},{10,... | collective-permute-start | bytes 202760 | tf_op jit(solution)/shard_map/ppermute | solution.py:411
  15.8 10.8 %collective-permute-start.6 = (bf16[264,128]{1,0:T(8,128)(2,1)}, bf16[264,128]{1,0:T(8,128)(2,1)S(1)}, u32[]{:S(2)}, u32[]{:S(2)}) collective-permute-start(bf16[264,128]{1,0:T(8,128)(2,1)} %get-tuple-element.110), channel_id=1, source_target_pairs={{0,13},{1,12},{2,15},{3,14},{4,9},{5,8},{6,11},{7,10},{8,5},{9,4},... | collective-permute-start | bytes 202760 | tf_op jit(solution)/shard_map/ppermute | solution.py:411
  18.7 9.0 %collective-permute-start.7 = (bf16[264,128]{1,0:T(8,128)(2,1)}, bf16[264,128]{1,0:T(8,128)(2,1)S(1)}, u32[]{:S(2)}, u32[]{:S(2)}) collective-permute-start(bf16[264,128]{1,0:T(8,128)(2,1)} %get-tuple-element.111), channel_id=1, source_target_pairs={{0,2},{1,3},{2,0},{3,1},{4,6},{5,7},{6,4},{7,5},{8,10},{9,11},{10,... | collective-permute-start | bytes 202760 | tf_op jit(solution)/shard_map/ppermute | solution.py:411
  20.3 8.2 %collective-permute-start.8 = (bf16[264,128]{1,0:T(8,128)(2,1)}, bf16[264,128]{1,0:T(8,128)(2,1)S(1)}, u32[]{:S(2)}, u32[]{:S(2)}) collective-permute-start(bf16[264,128]{1,0:T(8,128)(2,1)} %get-tuple-element.112), channel_id=1, source_target_pairs={{0,10},{1,11},{2,8},{3,9},{4,14},{5,15},{6,12},{7,13},{8,2},{9,3},... | collective-permute-start | bytes 202760 | tf_op jit(solution)/shard_map/ppermute | solution.py:411
  22.9 6.4 %collective-permute-start.9 = (bf16[264,128]{1,0:T(8,128)(2,1)}, bf16[264,128]{1,0:T(8,128)(2,1)S(1)}, u32[]{:S(2)}, u32[]{:S(2)}) collective-permute-start(bf16[264,128]{1,0:T(8,128)(2,1)} %get-tuple-element.113), channel_id=1, source_target_pairs={{0,6},{1,7},{2,4},{3,5},{4,2},{5,3},{6,0},{7,1},{8,14},{9,15},{10,... | collective-permute-start | bytes 202760 | tf_op jit(solution)/shard_map/ppermute | solution.py:411
  23.9 13.4 %collective-permute-start.10 = (bf16[264,128]{1,0:T(8,128)(2,1)}, bf16[264,128]{1,0:T(8,128)(2,1)S(1)}, u32[]{:S(2)}, u32[]{:S(2)}) collective-permute-start(bf16[264,128]{1,0:T(8,128)(2,1)} %get-tuple-element.114), channel_id=1, source_target_pairs={{0,14},{1,15},{2,12},{3,13},{4,10},{5,11},{6,8},{7,9},{8,6},{9,7},... | collective-permute-start | bytes 202760 | tf_op jit(solution)/shard_map/ppermute | solution.py:411
  26.6 10.7 %collective-permute-start.11 = (bf16[264,128]{1,0:T(8,128)(2,1)}, bf16[264,128]{1,0:T(8,128)(2,1)S(1)}, u32[]{:S(2)}, u32[]{:S(2)}) collective-permute-start(bf16[264,128]{1,0:T(8,128)(2,1)} %get-tuple-element.115), channel_id=1, source_target_pairs={{0,3},{1,2},{2,1},{3,0},{4,7},{5,6},{6,5},{7,4},{8,11},{9,10},{10,... | collective-permute-start | bytes 202760 | tf_op jit(solution)/shard_map/ppermute | solution.py:411
  27.7 9.6 %collective-permute-start.12 = (bf16[264,128]{1,0:T(8,128)(2,1)}, bf16[264,128]{1,0:T(8,128)(2,1)S(1)}, u32[]{:S(2)}, u32[]{:S(2)}) collective-permute-start(bf16[264,128]{1,0:T(8,128)(2,1)} %get-tuple-element.116), channel_id=1, source_target_pairs={{0,11},{1,10},{2,9},{3,8},{4,15},{5,14},{6,13},{7,12},{8,3},{9,2},... | collective-permute-start | bytes 202760 | tf_op jit(solution)/shard_map/ppermute | solution.py:411
  28.4 8.9 %collective-permute-start.13 = (bf16[264,128]{1,0:T(8,128)(2,1)}, bf16[264,128]{1,0:T(8,128)(2,1)S(1)}, u32[]{:S(2)}, u32[]{:S(2)}) collective-permute-start(bf16[264,128]{1,0:T(8,128)(2,1)} %get-tuple-element.117), channel_id=1, source_target_pairs={{0,7},{1,6},{2,5},{3,4},{4,3},{5,2},{6,1},{7,0},{8,15},{9,14},{10,... | collective-permute-start | bytes 202760 | tf_op jit(solution)/shard_map/ppermute | solution.py:411
  29.3 8.1 %collective-permute-start.14 = (bf16[264,128]{1,0:T(8,128)(2,1)}, bf16[264,128]{1,0:T(8,128)(2,1)S(1)}, u32[]{:S(2)}, u32[]{:S(2)}) collective-permute-start(bf16[264,128]{1,0:T(8,128)(2,1)} %get-tuple-element.118), channel_id=1, source_target_pairs={{0,15},{1,14},{2,13},{3,12},{4,11},{5,10},{6,9},{7,8},{8,7},{9,6},... | collective-permute-start | bytes 202760 | tf_op jit(solution)/shard_map/ppermute | solution.py:411
  39.9 6.9 %collective-permute-start.15 = (bf16[264,128]{1,0:T(8,128)(2,1)S(1)}, bf16[264,128]{1,0:T(8,128)(2,1)S(1)}, u32[]{:S(2)}, u32[]{:S(2)}) collective-permute-start(bf16[264,128]{1,0:T(8,128)(2,1)S(1)} %get-tuple-element.122), channel_id=1, source_target_pairs={{0,8},{1,9},{2,10},{3,11},{4,12},{5,13},{6,14},{7,15},{8,0},{9,1},... | collective-permute-start | bytes 202760 | tf_op jit(solution)/shard_map/ppermute | solution.py:411
  40.0 7.2 %collective-permute-start.16 = (bf16[264,128]{1,0:T(8,128)(2,1)S(1)}, bf16[264,128]{1,0:T(8,128)(2,1)S(1)}, u32[]{:S(2)}, u32[]{:S(2)}) collective-permute-start(bf16[264,128]{1,0:T(8,128)(2,1)S(1)} %get-tuple-element.123), channel_id=1, source_target_pairs={{0,4},{1,5},{2,6},{3,7},{4,0},{5,1},{6,2},{7,3},{8,12},{9,13},{10,... | collective-permute-start | bytes 202760 | tf_op jit(solution)/shard_map/ppermute | solution.py:411
  43.0 6.8 %collective-permute-start.17 = (bf16[264,128]{1,0:T(8,128)(2,1)S(1)}, bf16[264,128]{1,0:T(8,128)(2,1)S(1)}, u32[]{:S(2)}, u32[]{:S(2)}) collective-permute-start(bf16[264,128]{1,0:T(8,128)(2,1)S(1)} %get-tuple-element.124), channel_id=1, source_target_pairs={{0,12},{1,13},{2,14},{3,15},{4,8},{5,9},{6,10},{7,11},{8,4},{9,5},... | collective-permute-start | bytes 202760 | tf_op jit(solution)/shard_map/ppermute | solution.py:411
  44.3 9.0 %collective-permute-start.19 = (bf16[264,128]{1,0:T(8,128)(2,1)S(1)}, bf16[264,128]{1,0:T(8,128)(2,1)S(1)}, u32[]{:S(2)}, u32[]{:S(2)}) collective-permute-start(bf16[264,128]{1,0:T(8,128)(2,1)S(1)} %get-tuple-element.126), channel_id=1, source_target_pairs={{0,9},{1,8},{2,11},{3,10},{4,13},{5,12},{6,15},{7,14},{8,1},{9,0},... | collective-permute-start | bytes 202760 | tf_op jit(solution)/shard_map/ppermute | solution.py:411
  46.7 7.1 %collective-permute-start.20 = (bf16[264,128]{1,0:T(8,128)(2,1)S(1)}, bf16[264,128]{1,0:T(8,128)(2,1)S(1)}, u32[]{:S(2)}, u32[]{:S(2)}) collective-permute-start(bf16[264,128]{1,0:T(8,128)(2,1)S(1)} %get-tuple-element.127), channel_id=1, source_target_pairs={{0,5},{1,4},{2,7},{3,6},{4,1},{5,0},{6,3},{7,2},{8,13},{9,12},{10,... | collective-permute-start | bytes 202760 | tf_op jit(solution)/shard_map/ppermute | solution.py:411
  47.2 9.5 %collective-permute-start.21 = (bf16[264,128]{1,0:T(8,128)(2,1)S(1)}, bf16[264,128]{1,0:T(8,128)(2,1)S(1)}, u32[]{:S(2)}, u32[]{:S(2)}) collective-permute-start(bf16[264,128]{1,0:T(8,128)(2,1)S(1)} %get-tuple-element.128), channel_id=1, source_target_pairs={{0,13},{1,12},{2,15},{3,14},{4,9},{5,8},{6,11},{7,10},{8,5},{9,4},... | collective-permute-start | bytes 202760 | tf_op jit(solution)/shard_map/ppermute | solution.py:411
  49.9 6.8 %collective-permute-start.22 = (bf16[264,128]{1,0:T(8,128)(2,1)S(1)}, bf16[264,128]{1,0:T(8,128)(2,1)S(1)}, u32[]{:S(2)}, u32[]{:S(2)}) collective-permute-start(bf16[264,128]{1,0:T(8,128)(2,1)S(1)} %get-tuple-element.129), channel_id=1, source_target_pairs={{0,2},{1,3},{2,0},{3,1},{4,6},{5,7},{6,4},{7,5},{8,10},{9,11},{10,... | collective-permute-start | bytes 202760 | tf_op jit(solution)/shard_map/ppermute | solution.py:411
  49.9 9.0 %collective-permute-start.23 = (bf16[264,128]{1,0:T(8,128)(2,1)S(1)}, bf16[264,128]{1,0:T(8,128)(2,1)S(1)}, u32[]{:S(2)}, u32[]{:S(2)}) collective-permute-start(bf16[264,128]{1,0:T(8,128)(2,1)S(1)} %get-tuple-element.130), channel_id=1, source_target_pairs={{0,10},{1,11},{2,8},{3,9},{4,14},{5,15},{6,12},{7,13},{8,2},{9,3},... | collective-permute-start | bytes 202760 | tf_op jit(solution)/shard_map/ppermute | solution.py:411
  53.3 6.6 %collective-permute-start.24 = (bf16[264,128]{1,0:T(8,128)(2,1)S(1)}, bf16[264,128]{1,0:T(8,128)(2,1)S(1)}, u32[]{:S(2)}, u32[]{:S(2)}) collective-permute-start(bf16[264,128]{1,0:T(8,128)(2,1)S(1)} %get-tuple-element.131), channel_id=1, source_target_pairs={{0,6},{1,7},{2,4},{3,5},{4,2},{5,3},{6,0},{7,1},{8,14},{9,15},{10,... | collective-permute-start | bytes 202760 | tf_op jit(solution)/shard_map/ppermute | solution.py:411
  53.8 9.0 %collective-permute-start.25 = (bf16[264,128]{1,0:T(8,128)(2,1)S(1)}, bf16[264,128]{1,0:T(8,128)(2,1)S(1)}, u32[]{:S(2)}, u32[]{:S(2)}) collective-permute-start(bf16[264,128]{1,0:T(8,128)(2,1)S(1)} %get-tuple-element.132), channel_id=1, source_target_pairs={{0,14},{1,15},{2,12},{3,13},{4,10},{5,11},{6,8},{7,9},{8,6},{9,7},... | collective-permute-start | bytes 202760 | tf_op jit(solution)/shard_map/ppermute | solution.py:411
  56.7 6.5 %collective-permute-start.27 = (bf16[264,128]{1,0:T(8,128)(2,1)S(1)}, bf16[264,128]{1,0:T(8,128)(2,1)S(1)}, u32[]{:S(2)}, u32[]{:S(2)}) collective-permute-start(bf16[264,128]{1,0:T(8,128)(2,1)S(1)} %get-tuple-element.134), channel_id=1, source_target_pairs={{0,11},{1,10},{2,9},{3,8},{4,15},{5,14},{6,13},{7,12},{8,3},{9,2},... | collective-permute-start | bytes 202760 | tf_op jit(solution)/shard_map/ppermute | solution.py:411
  59.9 6.6 %collective-permute-start.29 = (bf16[264,128]{1,0:T(8,128)(2,1)S(1)}, bf16[264,128]{1,0:T(8,128)(2,1)S(1)}, u32[]{:S(2)}, u32[]{:S(2)}) collective-permute-start(bf16[264,128]{1,0:T(8,128)(2,1)S(1)} %get-tuple-element.136), channel_id=1, source_target_pairs={{0,15},{1,14},{2,13},{3,12},{4,11},{5,10},{6,9},{7,8},{8,7},{9,6},... | collective-permute-start | bytes 202760 | tf_op jit(solution)/shard_map/ppermute | solution.py:411
  69.9 7.1 %collective-permute-start.30 = (bf16[264,128]{1,0:T(8,128)(2,1)S(1)}, bf16[264,128]{1,0:T(8,128)(2,1)S(1)}, u32[]{:S(2)}, u32[]{:S(2)}) collective-permute-start(bf16[264,128]{1,0:T(8,128)(2,1)S(1)} %get-tuple-element.140), channel_id=1, source_target_pairs={{0,8},{1,9},{2,10},{3,11},{4,12},{5,13},{6,14},{7,15},{8,0},{9,1},... | collective-permute-start | bytes 202760 | tf_op jit(solution)/shard_map/ppermute | solution.py:411
  71.1 6.9 %collective-permute-start.31 = (bf16[264,128]{1,0:T(8,128)(2,1)S(1)}, bf16[264,128]{1,0:T(8,128)(2,1)S(1)}, u32[]{:S(2)}, u32[]{:S(2)}) collective-permute-start(bf16[264,128]{1,0:T(8,128)(2,1)S(1)} %get-tuple-element.141), channel_id=1, source_target_pairs={{0,4},{1,5},{2,6},{3,7},{4,0},{5,1},{6,2},{7,3},{8,12},{9,13},{10,... | collective-permute-start | bytes 202760 | tf_op jit(solution)/shard_map/ppermute | solution.py:411
  73.0 6.7 %collective-permute-start.32 = (bf16[264,128]{1,0:T(8,128)(2,1)S(1)}, bf16[264,128]{1,0:T(8,128)(2,1)S(1)}, u32[]{:S(2)}, u32[]{:S(2)}) collective-permute-start(bf16[264,128]{1,0:T(8,128)(2,1)S(1)} %get-tuple-element.142), channel_id=1, source_target_pairs={{0,12},{1,13},{2,14},{3,15},{4,8},{5,9},{6,10},{7,11},{8,4},{9,5},... | collective-permute-start | bytes 202760 | tf_op jit(solution)/shard_map/ppermute | solution.py:411
  74.4 9.9 %collective-permute-start.34 = (bf16[264,128]{1,0:T(8,128)(2,1)S(1)}, bf16[264,128]{1,0:T(8,128)(2,1)S(1)}, u32[]{:S(2)}, u32[]{:S(2)}) collective-permute-start(bf16[264,128]{1,0:T(8,128)(2,1)S(1)} %get-tuple-element.144), channel_id=1, source_target_pairs={{0,9},{1,8},{2,11},{3,10},{4,13},{5,12},{6,15},{7,14},{8,1},{9,0},... | collective-permute-start | bytes 202760 | tf_op jit(solution)/shard_map/ppermute | solution.py:411
  77.0 7.3 %collective-permute-start.35 = (bf16[264,128]{1,0:T(8,128)(2,1)S(1)}, bf16[264,128]{1,0:T(8,128)(2,1)S(1)}, u32[]{:S(2)}, u32[]{:S(2)}) collective-permute-start(bf16[264,128]{1,0:T(8,128)(2,1)S(1)} %get-tuple-element.145), channel_id=1, source_target_pairs={{0,5},{1,4},{2,7},{3,6},{4,1},{5,0},{6,3},{7,2},{8,13},{9,12},{10,... | collective-permute-start | bytes 202760 | tf_op jit(solution)/shard_map/ppermute | solution.py:411
  78.0 8.5 %collective-permute-start.36 = (bf16[264,128]{1,0:T(8,128)(2,1)S(1)}, bf16[264,128]{1,0:T(8,128)(2,1)S(1)}, u32[]{:S(2)}, u32[]{:S(2)}) collective-permute-start(bf16[264,128]{1,0:T(8,128)(2,1)S(1)} %get-tuple-element.146), channel_id=1, source_target_pairs={{0,13},{1,12},{2,15},{3,14},{4,9},{5,8},{6,11},{7,10},{8,5},{9,4},... | collective-permute-start | bytes 202760 | tf_op jit(solution)/shard_map/ppermute | solution.py:411
  79.7 7.6 %collective-permute-start.37 = (bf16[264,128]{1,0:T(8,128)(2,1)S(1)}, bf16[264,128]{1,0:T(8,128)(2,1)S(1)}, u32[]{:S(2)}, u32[]{:S(2)}) collective-permute-start(bf16[264,128]{1,0:T(8,128)(2,1)S(1)} %get-tuple-element.147), channel_id=1, source_target_pairs={{0,2},{1,3},{2,0},{3,1},{4,6},{5,7},{6,4},{7,5},{8,10},{9,11},{10,... | collective-permute-start | bytes 202760 | tf_op jit(solution)/shard_map/ppermute | solution.py:411
  80.3 9.7 %collective-permute-start.38 = (bf16[264,128]{1,0:T(8,128)(2,1)S(1)}, bf16[264,128]{1,0:T(8,128)(2,1)S(1)}, u32[]{:S(2)}, u32[]{:S(2)}) collective-permute-start(bf16[264,128]{1,0:T(8,128)(2,1)S(1)} %get-tuple-element.148), channel_id=1, source_target_pairs={{0,10},{1,11},{2,8},{3,9},{4,14},{5,15},{6,12},{7,13},{8,2},{9,3},... | collective-permute-start | bytes 202760 | tf_op jit(solution)/shard_map/ppermute | solution.py:411
  84.3 8.9 %collective-permute-start.40 = (bf16[264,128]{1,0:T(8,128)(2,1)S(1)}, bf16[264,128]{1,0:T(8,128)(2,1)S(1)}, u32[]{:S(2)}, u32[]{:S(2)}) collective-permute-start(bf16[264,128]{1,0:T(8,128)(2,1)S(1)} %get-tuple-element.150), channel_id=1, source_target_pairs={{0,14},{1,15},{2,12},{3,13},{4,10},{5,11},{6,8},{7,9},{8,6},{9,7},... | collective-permute-start | bytes 202760 | tf_op jit(solution)/shard_map/ppermute | solution.py:411
  86.5 6.8 %collective-permute-start.41 = (bf16[264,128]{1,0:T(8,128)(2,1)S(1)}, bf16[264,128]{1,0:T(8,128)(2,1)S(1)}, u32[]{:S(2)}, u32[]{:S(2)}) collective-permute-start(bf16[264,128]{1,0:T(8,128)(2,1)S(1)} %get-tuple-element.151), channel_id=1, source_target_pairs={{0,3},{1,2},{2,1},{3,0},{4,7},{5,6},{6,5},{7,4},{8,11},{9,10},{10,... | collective-permute-start | bytes 202760 | tf_op jit(solution)/shard_map/ppermute | solution.py:411
  87.3 7.4 %collective-permute-start.42 = (bf16[264,128]{1,0:T(8,128)(2,1)S(1)}, bf16[264,128]{1,0:T(8,128)(2,1)S(1)}, u32[]{:S(2)}, u32[]{:S(2)}) collective-permute-start(bf16[264,128]{1,0:T(8,128)(2,1)S(1)} %get-tuple-element.152), channel_id=1, source_target_pairs={{0,11},{1,10},{2,9},{3,8},{4,15},{5,14},{6,13},{7,12},{8,3},{9,2},... | collective-permute-start | bytes 202760 | tf_op jit(solution)/shard_map/ppermute | solution.py:411
  90.1 6.6 %collective-permute-start.44 = (bf16[264,128]{1,0:T(8,128)(2,1)S(1)}, bf16[264,128]{1,0:T(8,128)(2,1)S(1)}, u32[]{:S(2)}, u32[]{:S(2)}) collective-permute-start(bf16[264,128]{1,0:T(8,128)(2,1)S(1)} %get-tuple-element.154), channel_id=1, source_target_pairs={{0,15},{1,14},{2,13},{3,12},{4,11},{5,10},{6,9},{7,8},{8,7},{9,6},... | collective-permute-start | bytes 202760 | tf_op jit(solution)/shard_map/ppermute | solution.py:411
  99.2 7.7 %collective-permute-start.45 = (bf16[264,128]{1,0:T(8,128)(2,1)S(1)}, bf16[264,128]{1,0:T(8,128)(2,1)S(1)}, u32[]{:S(2)}, u32[]{:S(2)}) collective-permute-start(bf16[264,128]{1,0:T(8,128)(2,1)S(1)} %get-tuple-element.158), channel_id=1, source_target_pairs={{0,8},{1,9},{2,10},{3,11},{4,12},{5,13},{6,14},{7,15},{8,0},{9,1},... | collective-permute-start | bytes 202760 | tf_op jit(solution)/shard_map/ppermute | solution.py:411
  100.0 6.9 %collective-permute-start.46 = (bf16[264,128]{1,0:T(8,128)(2,1)S(1)}, bf16[264,128]{1,0:T(8,128)(2,1)S(1)}, u32[]{:S(2)}, u32[]{:S(2)}) collective-permute-start(bf16[264,128]{1,0:T(8,128)(2,1)S(1)} %get-tuple-element.159), channel_id=1, source_target_pairs={{0,4},{1,5},{2,6},{3,7},{4,0},{5,1},{6,2},{7,3},{8,12},{9,13},{10,... | collective-permute-start | bytes 202760 | tf_op jit(solution)/shard_map/ppermute | solution.py:411
  101.9 9.0 %collective-permute-start.47 = (bf16[264,128]{1,0:T(8,128)(2,1)S(1)}, bf16[264,128]{1,0:T(8,128)(2,1)S(1)}, u32[]{:S(2)}, u32[]{:S(2)}) collective-permute-start(bf16[264,128]{1,0:T(8,128)(2,1)S(1)} %get-tuple-element.160), channel_id=1, source_target_pairs={{0,12},{1,13},{2,14},{3,15},{4,8},{5,9},{6,10},{7,11},{8,4},{9,5},... | collective-permute-start | bytes 202760 | tf_op jit(solution)/shard_map/ppermute | solution.py:411
  103.7 7.9 %collective-permute-start.48 = (bf16[264,128]{1,0:T(8,128)(2,1)S(1)}, bf16[264,128]{1,0:T(8,128)(2,1)S(1)}, u32[]{:S(2)}, u32[]{:S(2)}) collective-permute-start(bf16[264,128]{1,0:T(8,128)(2,1)S(1)} %get-tuple-element.161), channel_id=1, source_target_pairs={{0,1},{1,0},{2,3},{3,2},{4,5},{5,4},{6,7},{7,6},{8,9},{9,8},{10,11... | collective-permute-start | bytes 202760 | tf_op jit(solution)/shard_map/ppermute | solution.py:411
  103.7 9.6 %collective-permute-start.49 = (bf16[264,128]{1,0:T(8,128)(2,1)S(1)}, bf16[264,128]{1,0:T(8,128)(2,1)S(1)}, u32[]{:S(2)}, u32[]{:S(2)}) collective-permute-start(bf16[264,128]{1,0:T(8,128)(2,1)S(1)} %get-tuple-element.162), channel_id=1, source_target_pairs={{0,9},{1,8},{2,11},{3,10},{4,13},{5,12},{6,15},{7,14},{8,1},{9,0},... | collective-permute-start | bytes 202760 | tf_op jit(solution)/shard_map/ppermute | solution.py:411
  106.9 7.3 %collective-permute-start.50 = (bf16[264,128]{1,0:T(8,128)(2,1)S(1)}, bf16[264,128]{1,0:T(8,128)(2,1)S(1)}, u32[]{:S(2)}, u32[]{:S(2)}) collective-permute-start(bf16[264,128]{1,0:T(8,128)(2,1)S(1)} %get-tuple-element.163), channel_id=1, source_target_pairs={{0,5},{1,4},{2,7},{3,6},{4,1},{5,0},{6,3},{7,2},{8,13},{9,12},{10,... | collective-permute-start | bytes 202760 | tf_op jit(solution)/shard_map/ppermute | solution.py:411
  106.9 10.8 %collective-permute-start.51 = (bf16[264,128]{1,0:T(8,128)(2,1)S(1)}, bf16[264,128]{1,0:T(8,128)(2,1)S(1)}, u32[]{:S(2)}, u32[]{:S(2)}) collective-permute-start(bf16[264,128]{1,0:T(8,128)(2,1)S(1)} %get-tuple-element.164), channel_id=1, source_target_pairs={{0,13},{1,12},{2,15},{3,14},{4,9},{5,8},{6,11},{7,10},{8,5},{9,4},... | collective-permute-start | bytes 202760 | tf_op jit(solution)/shard_map/ppermute | solution.py:411
  110.9 6.8 %collective-permute-start.52 = (bf16[264,128]{1,0:T(8,128)(2,1)S(1)}, bf16[264,128]{1,0:T(8,128)(2,1)S(1)}, u32[]{:S(2)}, u32[]{:S(2)}) collective-permute-start(bf16[264,128]{1,0:T(8,128)(2,1)S(1)} %get-tuple-element.165), channel_id=1, source_target_pairs={{0,2},{1,3},{2,0},{3,1},{4,6},{5,7},{6,4},{7,5},{8,10},{9,11},{10,... | collective-permute-start | bytes 202760 | tf_op jit(solution)/shard_map/ppermute | solution.py:411
  111.6 8.1 %collective-permute-start.53 = (bf16[264,128]{1,0:T(8,128)(2,1)S(1)}, bf16[264,128]{1,0:T(8,128)(2,1)S(1)}, u32[]{:S(2)}, u32[]{:S(2)}) collective-permute-start(bf16[264,128]{1,0:T(8,128)(2,1)S(1)} %get-tuple-element.166), channel_id=1, source_target_pairs={{0,10},{1,11},{2,8},{3,9},{4,14},{5,15},{6,12},{7,13},{8,2},{9,3},... | collective-permute-start | bytes 202760 | tf_op jit(solution)/shard_map/ppermute | solution.py:411
  113.2 6.9 %collective-permute-start.54 = (bf16[264,128]{1,0:T(8,128)(2,1)S(1)}, bf16[264,128]{1,0:T(8,128)(2,1)S(1)}, u32[]{:S(2)}, u32[]{:S(2)}) collective-permute-start(bf16[264,128]{1,0:T(8,128)(2,1)S(1)} %get-tuple-element.167), channel_id=1, source_target_pairs={{0,6},{1,7},{2,4},{3,5},{4,2},{5,3},{6,0},{7,1},{8,14},{9,15},{10,... | collective-permute-start | bytes 202760 | tf_op jit(solution)/shard_map/ppermute | solution.py:411
  114.1 9.7 %collective-permute-start.55 = (bf16[264,128]{1,0:T(8,128)(2,1)S(1)}, bf16[264,128]{1,0:T(8,128)(2,1)S(1)}, u32[]{:S(2)}, u32[]{:S(2)}) collective-permute-start(bf16[264,128]{1,0:T(8,128)(2,1)S(1)} %get-tuple-element.168), channel_id=1, source_target_pairs={{0,14},{1,15},{2,12},{3,13},{4,10},{5,11},{6,8},{7,9},{8,6},{9,7},... | collective-permute-start | bytes 202760 | tf_op jit(solution)/shard_map/ppermute | solution.py:411
  117.7 7.7 %collective-permute-start.57 = (bf16[264,128]{1,0:T(8,128)(2,1)S(1)}, bf16[264,128]{1,0:T(8,128)(2,1)S(1)}, u32[]{:S(2)}, u32[]{:S(2)}) collective-permute-start(bf16[264,128]{1,0:T(8,128)(2,1)S(1)} %get-tuple-element.170), channel_id=1, source_target_pairs={{0,11},{1,10},{2,9},{3,8},{4,15},{5,14},{6,13},{7,12},{8,3},{9,2},... | collective-permute-start | bytes 202760 | tf_op jit(solution)/shard_map/ppermute | solution.py:411
  120.2 7.1 %collective-permute-start.59 = (bf16[264,128]{1,0:T(8,128)(2,1)S(1)}, bf16[264,128]{1,0:T(8,128)(2,1)S(1)}, u32[]{:S(2)}, u32[]{:S(2)}) collective-permute-start(bf16[264,128]{1,0:T(8,128)(2,1)S(1)} %get-tuple-element.172), channel_id=1, source_target_pairs={{0,15},{1,14},{2,13},{3,12},{4,11},{5,10},{6,9},{7,8},{8,7},{9,6},... | collective-permute-start | bytes 202760 | tf_op jit(solution)/shard_map/ppermute | solution.py:411
  130.7 6.7 %collective-permute-start.60 = (bf16[264,128]{1,0:T(8,128)(2,1)S(1)}, bf16[264,128]{1,0:T(8,128)(2,1)S(1)}, u32[]{:S(2)}, u32[]{:S(2)}) collective-permute-start(bf16[264,128]{1,0:T(8,128)(2,1)S(1)} %get-tuple-element.176), channel_id=1, source_target_pairs={{0,8},{1,9},{2,10},{3,11},{4,12},{5,13},{6,14},{7,15},{8,0},{9,1},... | collective-permute-start | bytes 202760 | tf_op jit(solution)/shard_map/ppermute | solution.py:411
  131.1 6.4 %collective-permute-start.61 = (bf16[264,128]{1,0:T(8,128)(2,1)S(1)}, bf16[264,128]{1,0:T(8,128)(2,1)S(1)}, u32[]{:S(2)}, u32[]{:S(2)}) collective-permute-start(bf16[264,128]{1,0:T(8,128)(2,1)S(1)} %get-tuple-element.177), channel_id=1, source_target_pairs={{0,4},{1,5},{2,6},{3,7},{4,0},{5,1},{6,2},{7,3},{8,12},{9,13},{10,... | collective-permute-start | bytes 202760 | tf_op jit(solution)/shard_map/ppermute | solution.py:411
  133.3 6.7 %collective-permute-start.62 = (bf16[264,128]{1,0:T(8,128)(2,1)S(1)}, bf16[264,128]{1,0:T(8,128)(2,1)S(1)}, u32[]{:S(2)}, u32[]{:S(2)}) collective-permute-start(bf16[264,128]{1,0:T(8,128)(2,1)S(1)} %get-tuple-element.178), channel_id=1, source_target_pairs={{0,12},{1,13},{2,14},{3,15},{4,8},{5,9},{6,10},{7,11},{8,4},{9,5},... | collective-permute-start | bytes 202760 | tf_op jit(solution)/shard_map/ppermute | solution.py:411
  135.2 9.2 %collective-permute-start.64 = (bf16[264,128]{1,0:T(8,128)(2,1)S(1)}, bf16[264,128]{1,0:T(8,128)(2,1)S(1)}, u32[]{:S(2)}, u32[]{:S(2)}) collective-permute-start(bf16[264,128]{1,0:T(8,128)(2,1)S(1)} %get-tuple-element.180), channel_id=1, source_target_pairs={{0,9},{1,8},{2,11},{3,10},{4,13},{5,12},{6,15},{7,14},{8,1},{9,0},... | collective-permute-start | bytes 202760 | tf_op jit(solution)/shard_map/ppermute | solution.py:411
  137.5 7.6 %collective-permute-start.65 = (bf16[264,128]{1,0:T(8,128)(2,1)S(1)}, bf16[264,128]{1,0:T(8,128)(2,1)S(1)}, u32[]{:S(2)}, u32[]{:S(2)}) collective-permute-start(bf16[264,128]{1,0:T(8,128)(2,1)S(1)} %get-tuple-element.181), channel_id=1, source_target_pairs={{0,5},{1,4},{2,7},{3,6},{4,1},{5,0},{6,3},{7,2},{8,13},{9,12},{10,... | collective-permute-start | bytes 202760 | tf_op jit(solution)/shard_map/ppermute | solution.py:411
  137.5 10.1 %collective-permute-start.66 = (bf16[264,128]{1,0:T(8,128)(2,1)S(1)}, bf16[264,128]{1,0:T(8,128)(2,1)S(1)}, u32[]{:S(2)}, u32[]{:S(2)}) collective-permute-start(bf16[264,128]{1,0:T(8,128)(2,1)S(1)} %get-tuple-element.182), channel_id=1, source_target_pairs={{0,13},{1,12},{2,15},{3,14},{4,9},{5,8},{6,11},{7,10},{8,5},{9,4},... | collective-permute-start | bytes 202760 | tf_op jit(solution)/shard_map/ppermute | solution.py:411
  140.1 7.5 %collective-permute-start.67 = (bf16[264,128]{1,0:T(8,128)(2,1)S(1)}, bf16[264,128]{1,0:T(8,128)(2,1)S(1)}, u32[]{:S(2)}, u32[]{:S(2)}) collective-permute-start(bf16[264,128]{1,0:T(8,128)(2,1)S(1)} %get-tuple-element.183), channel_id=1, source_target_pairs={{0,2},{1,3},{2,0},{3,1},{4,6},{5,7},{6,4},{7,5},{8,10},{9,11},{10,... | collective-permute-start | bytes 202760 | tf_op jit(solution)/shard_map/ppermute | solution.py:411
  141.3 8.7 %collective-permute-start.68 = (bf16[264,128]{1,0:T(8,128)(2,1)S(1)}, bf16[264,128]{1,0:T(8,128)(2,1)S(1)}, u32[]{:S(2)}, u32[]{:S(2)}) collective-permute-start(bf16[264,128]{1,0:T(8,128)(2,1)S(1)} %get-tuple-element.184), channel_id=1, source_target_pairs={{0,10},{1,11},{2,8},{3,9},{4,14},{5,15},{6,12},{7,13},{8,2},{9,3},... | collective-permute-start | bytes 202760 | tf_op jit(solution)/shard_map/ppermute | solution.py:411
  144.4 6.7 %collective-permute-start.69 = (bf16[264,128]{1,0:T(8,128)(2,1)S(1)}, bf16[264,128]{1,0:T(8,128)(2,1)S(1)}, u32[]{:S(2)}, u32[]{:S(2)}) collective-permute-start(bf16[264,128]{1,0:T(8,128)(2,1)S(1)} %get-tuple-element.185), channel_id=1, source_target_pairs={{0,6},{1,7},{2,4},{3,5},{4,2},{5,3},{6,0},{7,1},{8,14},{9,15},{10,... | collective-permute-start | bytes 202760 | tf_op jit(solution)/shard_map/ppermute | solution.py:411
  145.1 8.7 %collective-permute-start.70 = (bf16[264,128]{1,0:T(8,128)(2,1)S(1)}, bf16[264,128]{1,0:T(8,128)(2,1)S(1)}, u32[]{:S(2)}, u32[]{:S(2)}) collective-permute-start(bf16[264,128]{1,0:T(8,128)(2,1)S(1)} %get-tuple-element.186), channel_id=1, source_target_pairs={{0,14},{1,15},{2,12},{3,13},{4,10},{5,11},{6,8},{7,9},{8,6},{9,7},... | collective-permute-start | bytes 202760 | tf_op jit(solution)/shard_map/ppermute | solution.py:411
  147.5 6.2 %collective-permute-start.71 = (bf16[264,128]{1,0:T(8,128)(2,1)S(1)}, bf16[264,128]{1,0:T(8,128)(2,1)S(1)}, u32[]{:S(2)}, u32[]{:S(2)}) collective-permute-start(bf16[264,128]{1,0:T(8,128)(2,1)S(1)} %get-tuple-element.187), channel_id=1, source_target_pairs={{0,3},{1,2},{2,1},{3,0},{4,7},{5,6},{6,5},{7,4},{8,11},{9,10},{10,... | collective-permute-start | bytes 202760 | tf_op jit(solution)/shard_map/ppermute | solution.py:411
  147.6 7.8 %collective-permute-start.72 = (bf16[264,128]{1,0:T(8,128)(2,1)S(1)}, bf16[264,128]{1,0:T(8,128)(2,1)S(1)}, u32[]{:S(2)}, u32[]{:S(2)}) collective-permute-start(bf16[264,128]{1,0:T(8,128)(2,1)S(1)} %get-tuple-element.188), channel_id=1, source_target_pairs={{0,11},{1,10},{2,9},{3,8},{4,15},{5,14},{6,13},{7,12},{8,3},{9,2},... | collective-permute-start | bytes 202760 | tf_op jit(solution)/shard_map/ppermute | solution.py:411
  151.1 6.8 %collective-permute-start.74 = (bf16[264,128]{1,0:T(8,128)(2,1)S(1)}, bf16[264,128]{1,0:T(8,128)(2,1)S(1)}, u32[]{:S(2)}, u32[]{:S(2)}) collective-permute-start(bf16[264,128]{1,0:T(8,128)(2,1)S(1)} %get-tuple-element.190), channel_id=1, source_target_pairs={{0,15},{1,14},{2,13},{3,12},{4,11},{5,10},{6,9},{7,8},{8,7},{9,6},... | collective-permute-start | bytes 202760 | tf_op jit(solution)/shard_map/ppermute | solution.py:411
  (19 other events, 116.7 us)

commit v19 on v17

--- a/solution.py
+++ b/solution.py
@@ -56,7 +56,7 @@
     return pl.ds(pl.multiple_of(block * BS, BS), BS)
 
 
-def transposed(data_ref, rays_ref, before, target_ref, total_ref, message_refs):
+def transposed(data_ref, rays_ref, begin, before, target_ref, total_ref, message_refs):
     pair_count, slot_count = rays_ref.shape[:2]
     cols = data_ref.shape[0]
     spots = len(message_refs) * BCAP
@@ -66,6 +66,7 @@
         return carry
 
     lax.fori_loop(0, spots, clear, 0, unroll=8)
+    begin()
 
     def one_pair(pair, carry):
         before(pair)
@@ -125,9 +126,6 @@
         return carry
 
     lax.fori_loop(0, peers, clear, 0)
-    for copy in copies:
-        copy.wait()
-
     def find_places(pair):
         count = counts_ref[pair]
         for slot in range(slot_count):
@@ -148,17 +146,22 @@
         find_places(pair)
         ray_copy(pair).wait()
 
-    transposed(times_ref, rays_ref, before, target_ref, total_ref, message_refs)
-    squares = jnp.zeros((cols, BS), F32)
-    for pair in range(pair_count):
-        part = times_ref[:, pair * BS : (pair + 1) * BS]
-        squares += part * part
-    tail = squares_tail(squares)
+    def begin():
+        for copy in copies:
+            copy.wait()
+        squares = jnp.zeros((cols, BS), F32)
+        for pair in range(pair_count):
+            values = times_ref[:, pair * BS : (pair + 1) * BS]
+            squares += values * values
+        tail = squares_tail(squares).astype(BF16)
+        for message_ref in message_refs:
+            message_ref[BCAP * cols :, :] = tail
+
+    transposed(times_ref, rays_ref, begin, before, target_ref, total_ref, message_refs)
     place = lax.broadcasted_iota(jnp.int32, (TAIL, BS), 0)
     lane = lax.broadcasted_iota(jnp.int32, (TAIL, BS), 1)
-
     for peer, message_ref in enumerate(message_refs):
-        rows = tail
+        rows = message_ref[BCAP * cols :, :].astype(F32)
         for rank in range(BCAP):
             asked = table_ref[peer * BCAP + rank].astype(F32)
             rows = jnp.where((place == 3) & (lane == rank), asked, rows)
@@ -213,10 +216,12 @@
         return squares + raw * raw
 
     squares = lax.fori_loop(0, pair_count, one_pair, jnp.zeros((cols, BS), F32), unroll=True)
-    transposed(raw_ref, rays_ref, lambda pair: None, target_ref, total_ref, message_refs)
     tail = squares_tail(squares).astype(BF16)
     for message_ref in message_refs:
         message_ref[BCAP * cols :, :] = tail
+    transposed(
+        raw_ref, rays_ref, lambda: None, lambda pair: None, target_ref, total_ref, message_refs
+    )
 
 
 def gathered(arrived_refs, asked_ref, model_ref):

time: 172 us -> 172 us (level)
  transfers between devices with their start and end apart: 81 -> 81, of which waited for: 30 -> 31; matrix products, arithmetic and copies ran while one was open for 0% -> 0% of each run, Pallas kernels for 3% -> 3%
where the time goes in v19:
time: 172 us; the launch traced here: 171 us
  starting transfers between devices  108 us (63%)
  waiting for transfers between devices  35.2 us (20%)
  Pallas kernels  25.2 us (15%)
    ppermute x75, starting transfers between devices, exchange(): lax.ppermute(value, 'pair', [(one, one ^ step) for one in range(peers)])  102 us
    ppermute x75, waiting for transfers between devices, exchange(): lax.ppermute(value, 'pair', [(one, one ^ step) for one in range(peers)])  32.8 us
    pallas_call x2, Pallas kernels, on_device(): call(functools.partial(pair_kernel, peers), 'pairs_last' if last else 'pa...  7.1 us
    ppermute x6, starting transfers between devices, on_device(): lax.ppermute(share, 'pair', [(one, one ^ step) for one in range(peers)])  6.37 us
    pallas_call x1, Pallas kernels, on_device(): call(functools.partial(start_kernel, peers), 'start', [SMEM, HBM, HBM, HB...  5.19 us
  transfers between devices with their start and end apart: 81, of which 31 were waited for; matrix products, arithmetic and copies ran while one was open for 0% of the time, Pallas kernels for 3%

profile of v19, /device:TPU:0, one launch (start us, length us, event | category | flops | bytes accessed | tf_op | source)
XLA Modules:
  0.0 171.2 jit_solution(11644865643639949171)
XLA Ops:
  0.6 5.2 %start.1 = (bf16[264,128]{1,0:T(8,128)(2,1)}, bf16[264,128]{1,0:T(8,128)(2,1)}, bf16[264,128]{1,0:T(8,128)(2,1)}, bf16[264,128]{1,0:T(8,128)(2,1)}, bf16[264,128...) custom-call(s32[1]{0:T(128)} %bitcast.me_ref, ...), custom_call_target="tpu_custom_call" | custom-call | flops 268435456 | bytes 6291456 | tf_op jit(solution)/shard_map/start/pallas_call | solution.py:421
  5.8 4.1 %collective-permute-start = (bf16[264,128]{1,0:T(8,128)(2,1)}, bf16[264,128]{1,0:T(8,128)(2,1)S(1)}, u32[]{:S(2)}, u32[]{:S(2)}) collective-permute-start(bf16[264,128]{1,0:T(8,128)(2,1)} %get-tuple-element.100), channel_id=1, source_target_pairs={{0,8},{1,9},{2,10},{3,11},{4,12},{5,13},{6,14},{7,15},{8,0},{9,1},... | collective-permute-start | bytes 202760 | tf_op jit(solution)/shard_map/ppermute | solution.py:416
  9.9 1.6 collective-permute-start.1
  11.5 2.0 %collective-permute-start.4 = (bf16[264,128]{1,0:T(8,128)(2,1)}, bf16[264,128]{1,0:T(8,128)(2,1)S(1)}, u32[]{:S(2)}, u32[]{:S(2)}) collective-permute-start(bf16[264,128]{1,0:T(8,128)(2,1)} %get-tuple-element.104), channel_id=1, source_target_pairs={{0,9},{1,8},{2,11},{3,10},{4,13},{5,12},{6,15},{7,14},{8,1},{9,0},... | collective-permute-start | bytes 202760 | tf_op jit(solution)/shard_map/ppermute | solution.py:416
  13.6 2.1 %collective-permute-start.5 = (bf16[264,128]{1,0:T(8,128)(2,1)}, bf16[264,128]{1,0:T(8,128)(2,1)S(1)}, u32[]{:S(2)}, u32[]{:S(2)}) collective-permute-start(bf16[264,128]{1,0:T(8,128)(2,1)} %get-tuple-element.105), channel_id=1, source_target_pairs={{0,5},{1,4},{2,7},{3,6},{4,1},{5,0},{6,3},{7,2},{8,13},{9,12},{10,... | collective-permute-start | bytes 202760 | tf_op jit(solution)/shard_map/ppermute | solution.py:416
  15.6 1.5 collective-permute-start.6
  17.1 1.5 collective-permute-done.2.refs_3_
  18.6 1.5 collective-permute-start.7
  20.1 2.5 %collective-permute-start.8 = (bf16[264,128]{1,0:T(8,128)(2,1)}, bf16[264,128]{1,0:T(8,128)(2,1)S(1)}, u32[]{:S(2)}, u32[]{:S(2)}) collective-permute-start(bf16[264,128]{1,0:T(8,128)(2,1)} %get-tuple-element.108), channel_id=1, source_target_pairs={{0,10},{1,11},{2,8},{3,9},{4,14},{5,15},{6,12},{7,13},{8,2},{9,3},... | collective-permute-start | bytes 202760 | tf_op jit(solution)/shard_map/ppermute | solution.py:416
  23.7 2.7 %collective-permute-start.10 = (bf16[264,128]{1,0:T(8,128)(2,1)}, bf16[264,128]{1,0:T(8,128)(2,1)S(1)}, u32[]{:S(2)}, u32[]{:S(2)}) collective-permute-start(bf16[264,128]{1,0:T(8,128)(2,1)} %get-tuple-element.110), channel_id=1, source_target_pairs={{0,14},{1,15},{2,12},{3,13},{4,10},{5,11},{6,8},{7,9},{8,6},{9,7},... | collective-permute-start | bytes 202760 | tf_op jit(solution)/shard_map/ppermute | solution.py:416
  26.4 1.1 collective-permute-start.11
  29.0 3.6 %collective-permute-start.14 = (bf16[264,128]{1,0:T(8,128)(2,1)}, bf16[264,128]{1,0:T(8,128)(2,1)S(1)}, u32[]{:S(2)}, u32[]{:S(2)}) collective-permute-start(bf16[264,128]{1,0:T(8,128)(2,1)} %get-tuple-element.114), channel_id=1, source_target_pairs={{0,15},{1,14},{2,13},{3,12},{4,11},{5,10},{6,9},{7,8},{8,7},{9,6},... | collective-permute-start | bytes 202760 | tf_op jit(solution)/shard_map/ppermute | solution.py:416
  34.1 2.9 %keep.1 = (s32[128]{0:T(128)S(1)}, bf16[264,128]{1,0:T(8,128)(2,1)S(1)}, bf16[8,16,128,128]{3,2,1,0:T(8,128)(2,1)S(1)}) custom-call(s32[128]{0:T(128)S(1)} %copy-done.2, bf16[264,128]{1,0:T(8,128)(2,1)S(1)} %copy-done.1, bf16[8,16,128,128]{3,2,1,0:T(8,128)(2,1)} %rays_hbm.3), custom_call_target="tpu_custom_call" | custom-call | bytes 8388608 | tf_op jit(solution)/shard_map/keep/pallas_call | solution.py:433
  37.0 2.5 %cells_first.1 = (f32[64,8192]{1,0:T(8,128)S(1)}, f32[64,128]{1,0:T(8,128)S(1)}, bf16[264,128]{1,0:T(8,128)(2,1)S(1)}, bf16[264,128]{1,0:T(8,128)(2,1)S(1)}, bf1...) custom-call(bf16[264,128]{1,0:T(8,128)(2,1)S(1)} %get-tuple-element., ...), custom_call_target="tpu_custom_call" | custom-call | bytes 6291456 | tf_op jit(solution)/shard_map/cells_first/pallas_call | solution.py:438
  39.7 3.1 %collective-permute-start.16 = (bf16[264,128]{1,0:T(8,128)(2,1)S(1)}, bf16[264,128]{1,0:T(8,128)(2,1)S(1)}, u32[]{:S(2)}, u32[]{:S(2)}) collective-permute-start(bf16[264,128]{1,0:T(8,128)(2,1)S(1)} %get-tuple-element.120), channel_id=1, source_target_pairs={{0,4},{1,5},{2,6},{3,7},{4,0},{5,1},{6,2},{7,3},{8,12},{9,13},{10,... | collective-permute-start | bytes 202760 | tf_op jit(solution)/shard_map/ppermute | solution.py:416
  42.8 1.2 collective-permute-start.17
  44.4 2.2 %collective-permute-done.15.refs_1_ = bf16[264,128]{1,0:T(8,128)(2,1)S(1)} collective-permute-done((bf16[264,128]{1,0:T(8,128)(2,1)S(1)}, bf16[264,128]{1,0:T(8,128)(2,1)S(1)}, u32[]{:S(2)}, u32[]{:S(2)}) %collective-permute-start.15) | collective-permute-done | bytes 67616 | tf_op jit(solution)/shard_map/ppermute | solution.py:416
  46.9 1.3 collective-permute-start.21
  48.3 1.4 collective-permute-done.17.refs_3_
  49.7 3.4 %collective-permute-start.23 = (bf16[264,128]{1,0:T(8,128)(2,1)S(1)}, bf16[264,128]{1,0:T(8,128)(2,1)S(1)}, u32[]{:S(2)}, u32[]{:S(2)}) collective-permute-start(bf16[264,128]{1,0:T(8,128)(2,1)S(1)} %get-tuple-element.127), channel_id=1, source_target_pairs={{0,10},{1,11},{2,8},{3,9},{4,14},{5,15},{6,12},{7,13},{8,2},{9,3},... | collective-permute-start | bytes 202760 | tf_op jit(solution)/shard_map/ppermute | solution.py:416
  53.6 2.8 %collective-permute-start.25 = (bf16[264,128]{1,0:T(8,128)(2,1)S(1)}, bf16[264,128]{1,0:T(8,128)(2,1)S(1)}, u32[]{:S(2)}, u32[]{:S(2)}) collective-permute-start(bf16[264,128]{1,0:T(8,128)(2,1)S(1)} %get-tuple-element.129), channel_id=1, source_target_pairs={{0,14},{1,15},{2,12},{3,13},{4,10},{5,11},{6,8},{7,9},{8,6},{9,7},... | collective-permute-start | bytes 202760 | tf_op jit(solution)/shard_map/ppermute | solution.py:416
  56.4 2.3 %collective-permute-start.27 = (bf16[264,128]{1,0:T(8,128)(2,1)S(1)}, bf16[264,128]{1,0:T(8,128)(2,1)S(1)}, u32[]{:S(2)}, u32[]{:S(2)}) collective-permute-start(bf16[264,128]{1,0:T(8,128)(2,1)S(1)} %get-tuple-element.131), channel_id=1, source_target_pairs={{0,11},{1,10},{2,9},{3,8},{4,15},{5,14},{6,13},{7,12},{8,3},{9,2},... | collective-permute-start | bytes 202760 | tf_op jit(solution)/shard_map/ppermute | solution.py:416
  59.6 3.0 %collective-permute-start.29 = (bf16[264,128]{1,0:T(8,128)(2,1)S(1)}, bf16[264,128]{1,0:T(8,128)(2,1)S(1)}, u32[]{:S(2)}, u32[]{:S(2)}) collective-permute-start(bf16[264,128]{1,0:T(8,128)(2,1)S(1)} %get-tuple-element.133), channel_id=1, source_target_pairs={{0,15},{1,14},{2,13},{3,12},{4,11},{5,10},{6,9},{7,8},{8,7},{9,6},... | collective-permute-start | bytes 202760 | tf_op jit(solution)/shard_map/ppermute | solution.py:416
  63.0 1.6 collective-permute-done.28.refs_14_
  64.6 1.6 collective-permute-done.29.refs_15_
  66.2 3.6 %pairs.1 = (bf16[264,128]{1,0:T(8,128)(2,1)S(1)}, bf16[264,128]{1,0:T(8,128)(2,1)S(1)}, bf16[264,128]{1,0:T(8,128)(2,1)S(1)}, bf16[264,128]{1,0:T(8,128)(2,1)S(1...) custom-call(s32[128]{0:T(128)S(1)} %get-tuple-element.117.target_ref, ...), custom_call_target="tpu_custom_call" | custom-call | flops 536870912 | bytes 8388608 | tf_op jit(solution)/shard_map/pairs/pallas_call | solution.py:449
  70.4 2.5 %collective-permute-start.31 = (bf16[264,128]{1,0:T(8,128)(2,1)S(1)}, bf16[264,128]{1,0:T(8,128)(2,1)S(1)}, u32[]{:S(2)}, u32[]{:S(2)}) collective-permute-start(bf16[264,128]{1,0:T(8,128)(2,1)S(1)} %get-tuple-element.138), channel_id=1, source_target_pairs={{0,4},{1,5},{2,6},{3,7},{4,0},{5,1},{6,2},{7,3},{8,12},{9,13},{10,... | collective-permute-start | bytes 202760 | tf_op jit(solution)/shard_map/ppermute | solution.py:416
  72.9 1.3 collective-permute-start.32
  74.5 2.4 %collective-permute-done.30.refs_1_ = bf16[264,128]{1,0:T(8,128)(2,1)S(1)} collective-permute-done((bf16[264,128]{1,0:T(8,128)(2,1)S(1)}, bf16[264,128]{1,0:T(8,128)(2,1)S(1)}, u32[]{:S(2)}, u32[]{:S(2)}) %collective-permute-start.30) | collective-permute-done | bytes 67616 | tf_op jit(solution)/shard_map/ppermute | solution.py:416
  77.0 1.7 collective-permute-start.36
  80.0 3.7 %collective-permute-start.38 = (bf16[264,128]{1,0:T(8,128)(2,1)S(1)}, bf16[264,128]{1,0:T(8,128)(2,1)S(1)}, u32[]{:S(2)}, u32[]{:S(2)}) collective-permute-start(bf16[264,128]{1,0:T(8,128)(2,1)S(1)} %get-tuple-element.145), channel_id=1, source_target_pairs={{0,10},{1,11},{2,8},{3,9},{4,14},{5,15},{6,12},{7,13},{8,2},{9,3},... | collective-permute-start | bytes 202760 | tf_op jit(solution)/shard_map/ppermute | solution.py:416
  84.1 2.3 %collective-permute-start.40 = (bf16[264,128]{1,0:T(8,128)(2,1)S(1)}, bf16[264,128]{1,0:T(8,128)(2,1)S(1)}, u32[]{:S(2)}, u32[]{:S(2)}) collective-permute-start(bf16[264,128]{1,0:T(8,128)(2,1)S(1)} %get-tuple-element.147), channel_id=1, source_target_pairs={{0,14},{1,15},{2,12},{3,13},{4,10},{5,11},{6,8},{7,9},{8,6},{9,7},... | collective-permute-start | bytes 202760 | tf_op jit(solution)/shard_map/ppermute | solution.py:416
  87.1 2.5 %collective-permute-start.42 = (bf16[264,128]{1,0:T(8,128)(2,1)S(1)}, bf16[264,128]{1,0:T(8,128)(2,1)S(1)}, u32[]{:S(2)}, u32[]{:S(2)}) collective-permute-start(bf16[264,128]{1,0:T(8,128)(2,1)S(1)} %get-tuple-element.149), channel_id=1, source_target_pairs={{0,11},{1,10},{2,9},{3,8},{4,15},{5,14},{6,13},{7,12},{8,3},{9,2},... | collective-permute-start | bytes 202760 | tf_op jit(solution)/shard_map/ppermute | solution.py:416
  89.9 2.6 %collective-permute-start.44 = (bf16[264,128]{1,0:T(8,128)(2,1)S(1)}, bf16[264,128]{1,0:T(8,128)(2,1)S(1)}, u32[]{:S(2)}, u32[]{:S(2)}) collective-permute-start(bf16[264,128]{1,0:T(8,128)(2,1)S(1)} %get-tuple-element.151), channel_id=1, source_target_pairs={{0,15},{1,14},{2,13},{3,12},{4,11},{5,10},{6,9},{7,8},{8,7},{9,6},... | collective-permute-start | bytes 202760 | tf_op jit(solution)/shard_map/ppermute | solution.py:416
  92.7 1.8 %collective-permute-done.42.refs_13_ = bf16[264,128]{1,0:T(8,128)(2,1)S(1)} collective-permute-done((bf16[264,128]{1,0:T(8,128)(2,1)S(1)}, bf16[264,128]{1,0:T(8,128)(2,1)S(1)}, u32[]{:S(2)}, u32[]{:S(2)}) %collective-permute-start.42) | collective-permute-done | bytes 67616 | tf_op jit(solution)/shard_map/ppermute | solution.py:416
  94.5 1.1 collective-permute-done.43.refs_14_
  96.4 2.4 %cells.1 = (f32[64,8192]{1,0:T(8,128)S(1)}, f32[64,128]{1,0:T(8,128)S(1)}, bf16[264,128]{1,0:T(8,128)(2,1)S(1)}, bf16[264,128]{1,0:T(8,128)(2,1)S(1)}, bf16[264,...) custom-call(s32[16,128]{1,0:T(8,128)S(1)} %get-tuple-element.116.ask, ...), custom_call_target="tpu_custom_call" | custom-call | bytes 8388608 | tf_op jit(solution)/shard_map/cells/pallas_call | solution.py:458
  99.6 2.1 %collective-permute-start.46 = (bf16[264,128]{1,0:T(8,128)(2,1)S(1)}, bf16[264,128]{1,0:T(8,128)(2,1)S(1)}, u32[]{:S(2)}, u32[]{:S(2)}) collective-permute-start(bf16[264,128]{1,0:T(8,128)(2,1)S(1)} %get-tuple-element.156), channel_id=1, source_target_pairs={{0,4},{1,5},{2,6},{3,7},{4,0},{5,1},{6,2},{7,3},{8,12},{9,13},{10,... | collective-permute-start | bytes 202760 | tf_op jit(solution)/shard_map/ppermute | solution.py:416
  101.7 1.6 collective-permute-start.47
  103.4 2.9 %collective-permute-done.45.refs_1_ = bf16[264,128]{1,0:T(8,128)(2,1)S(1)} collective-permute-done((bf16[264,128]{1,0:T(8,128)(2,1)S(1)}, bf16[264,128]{1,0:T(8,128)(2,1)S(1)}, u32[]{:S(2)}, u32[]{:S(2)}) %collective-permute-start.45) | collective-permute-done | bytes 67616 | tf_op jit(solution)/shard_map/ppermute | solution.py:416
  106.4 4.1 %collective-permute-start.51 = (bf16[264,128]{1,0:T(8,128)(2,1)S(1)}, bf16[264,128]{1,0:T(8,128)(2,1)S(1)}, u32[]{:S(2)}, u32[]{:S(2)}) collective-permute-start(bf16[264,128]{1,0:T(8,128)(2,1)S(1)} %get-tuple-element.161), channel_id=1, source_target_pairs={{0,13},{1,12},{2,15},{3,14},{4,9},{5,8},{6,11},{7,10},{8,5},{9,4},... | collective-permute-start | bytes 202760 | tf_op jit(solution)/shard_map/ppermute | solution.py:416
  110.5 2.3 %collective-permute-start.53 = (bf16[264,128]{1,0:T(8,128)(2,1)S(1)}, bf16[264,128]{1,0:T(8,128)(2,1)S(1)}, u32[]{:S(2)}, u32[]{:S(2)}) collective-permute-start(bf16[264,128]{1,0:T(8,128)(2,1)S(1)} %get-tuple-element.163), channel_id=1, source_target_pairs={{0,10},{1,11},{2,8},{3,9},{4,14},{5,15},{6,12},{7,13},{8,2},{9,3},... | collective-permute-start | bytes 202760 | tf_op jit(solution)/shard_map/ppermute | solution.py:416
  113.8 3.5 %collective-permute-start.55 = (bf16[264,128]{1,0:T(8,128)(2,1)S(1)}, bf16[264,128]{1,0:T(8,128)(2,1)S(1)}, u32[]{:S(2)}, u32[]{:S(2)}) collective-permute-start(bf16[264,128]{1,0:T(8,128)(2,1)S(1)} %get-tuple-element.165), channel_id=1, source_target_pairs={{0,14},{1,15},{2,12},{3,13},{4,10},{5,11},{6,8},{7,9},{8,6},{9,7},... | collective-permute-start | bytes 202760 | tf_op jit(solution)/shard_map/ppermute | solution.py:416
  117.3 1.2 collective-permute-start.57
  119.7 3.8 %collective-permute-start.59 = (bf16[264,128]{1,0:T(8,128)(2,1)S(1)}, bf16[264,128]{1,0:T(8,128)(2,1)S(1)}, u32[]{:S(2)}, u32[]{:S(2)}) collective-permute-start(bf16[264,128]{1,0:T(8,128)(2,1)S(1)} %get-tuple-element.169), channel_id=1, source_target_pairs={{0,15},{1,14},{2,13},{3,12},{4,11},{5,10},{6,9},{7,8},{8,7},{9,6},... | collective-permute-start | bytes 202760 | tf_op jit(solution)/shard_map/ppermute | solution.py:416
  123.5 1.4 collective-permute-done.57.refs_13_
  125.1 1.8 %collective-permute-done.59.refs_15_ = bf16[264,128]{1,0:T(8,128)(2,1)S(1)} collective-permute-done((bf16[264,128]{1,0:T(8,128)(2,1)S(1)}, bf16[264,128]{1,0:T(8,128)(2,1)S(1)}, u32[]{:S(2)}, u32[]{:S(2)}) %collective-permute-start.59) | collective-permute-done | bytes 67616 | tf_op jit(solution)/shard_map/ppermute | solution.py:416
  126.9 3.6 %pairs_last.1 = (bf16[264,128]{1,0:T(8,128)(2,1)S(1)}, bf16[264,128]{1,0:T(8,128)(2,1)S(1)}, bf16[264,128]{1,0:T(8,128)(2,1)S(1)}, bf16[264,128]{1,0:T(8,128)(2,...) custom-call(s32[128]{0:T(128)S(1)} %get-tuple-element.117.target_ref, ...), custom_call_target="tpu_custom_call" | custom-call | flops 536870912 | bytes 8388608 | tf_op jit(solution)/shard_map/pairs_last/pallas_call | solution.py:449
  130.9 2.6 %collective-permute-start.61 = (bf16[264,128]{1,0:T(8,128)(2,1)S(1)}, bf16[264,128]{1,0:T(8,128)(2,1)S(1)}, u32[]{:S(2)}, u32[]{:S(2)}) collective-permute-start(bf16[264,128]{1,0:T(8,128)(2,1)S(1)} %get-tuple-element.175), channel_id=1, source_target_pairs={{0,4},{1,5},{2,6},{3,7},{4,0},{5,1},{6,2},{7,3},{8,12},{9,13},{10,... | collective-permute-start | bytes 202760 | tf_op jit(solution)/shard_map/ppermute | solution.py:416
  133.5 1.5 collective-permute-start.62
  135.1 2.4 %collective-permute-done.60.refs_1_ = bf16[264,128]{1,0:T(8,128)(2,1)S(1)} collective-permute-done((bf16[264,128]{1,0:T(8,128)(2,1)S(1)}, bf16[264,128]{1,0:T(8,128)(2,1)S(1)}, u32[]{:S(2)}, u32[]{:S(2)}) %collective-permute-start.60) | collective-permute-done | bytes 67616 | tf_op jit(solution)/shard_map/ppermute | solution.py:416
  140.8 3.4 %collective-permute-start.68 = (bf16[264,128]{1,0:T(8,128)(2,1)S(1)}, bf16[264,128]{1,0:T(8,128)(2,1)S(1)}, u32[]{:S(2)}, u32[]{:S(2)}) collective-permute-start(bf16[264,128]{1,0:T(8,128)(2,1)S(1)} %get-tuple-element.182), channel_id=1, source_target_pairs={{0,10},{1,11},{2,8},{3,9},{4,14},{5,15},{6,12},{7,13},{8,2},{9,3},... | collective-permute-start | bytes 202760 | tf_op jit(solution)/shard_map/ppermute | solution.py:416
  144.7 2.3 %collective-permute-start.70 = (bf16[264,128]{1,0:T(8,128)(2,1)S(1)}, bf16[264,128]{1,0:T(8,128)(2,1)S(1)}, u32[]{:S(2)}, u32[]{:S(2)}) collective-permute-start(bf16[264,128]{1,0:T(8,128)(2,1)S(1)} %get-tuple-element.184), channel_id=1, source_target_pairs={{0,14},{1,15},{2,12},{3,13},{4,10},{5,11},{6,8},{7,9},{8,6},{9,7},... | collective-permute-start | bytes 202760 | tf_op jit(solution)/shard_map/ppermute | solution.py:416
  147.5 2.2 %collective-permute-start.72 = (bf16[264,128]{1,0:T(8,128)(2,1)S(1)}, bf16[264,128]{1,0:T(8,128)(2,1)S(1)}, u32[]{:S(2)}, u32[]{:S(2)}) collective-permute-start(bf16[264,128]{1,0:T(8,128)(2,1)S(1)} %get-tuple-element.186), channel_id=1, source_target_pairs={{0,11},{1,10},{2,9},{3,8},{4,15},{5,14},{6,13},{7,12},{8,3},{9,2},... | collective-permute-start | bytes 202760 | tf_op jit(solution)/shard_map/ppermute | solution.py:416
  150.5 2.6 %collective-permute-start.74 = (bf16[264,128]{1,0:T(8,128)(2,1)S(1)}, bf16[264,128]{1,0:T(8,128)(2,1)S(1)}, u32[]{:S(2)}, u32[]{:S(2)}) collective-permute-start(bf16[264,128]{1,0:T(8,128)(2,1)S(1)} %get-tuple-element.188), channel_id=1, source_target_pairs={{0,15},{1,14},{2,13},{3,12},{4,11},{5,10},{6,9},{7,8},{8,7},{9,6},... | collective-permute-start | bytes 202760 | tf_op jit(solution)/shard_map/ppermute | solution.py:416
  153.3 1.6 collective-permute-done.72.refs_13_
  155.8 1.3 collective-permute-done.74.refs_15_
  157.1 2.0 %cells_last.1 = (f32[64,8192]{1,0:T(8,128)S(1)}, f32[64,128]{1,0:T(8,128)S(1)}, f32[8,128]{1,0:T(8,128)S(1)}) custom-call(s32[16,128]{1,0:T(8,128)S(1)} %get-tuple-element.116.asked_ref, bf16[264,128]{1,0:T(8,128)(2,1)S(1)} %get-tuple-element.173.refs_0_, bf16[264,128]{1,0:T(8,128)(2,1)S(1)} %collective-permute-done.60.refs_1_, ...), custom_call_target="tpu_custom_call" | custom-call | bytes 8388608 | tf_op jit(solution)/shard_map/cells_last/pallas_call | solution.py:464
  159.1 2.1 %collective-permute-start.77 = (f32[8,128]{1,0:T(8,128)S(1)}, f32[8,128]{1,0:T(8,128)S(1)}, u32[]{:S(2)}, u32[]{:S(2)}) collective-permute-start(f32[8,128]{1,0:T(8,128)S(1)} %get-tuple-element.190), channel_id=1, source_target_pairs={{0,12},{1,13},{2,14},{3,15},{4,8},{5,9},{6,10},{7,11},{8,4},{9,5},... | collective-permute-start | bytes 12296 | tf_op jit(solution)/shard_map/ppermute | solution.py:474
  161.5 2.1 %collective-permute-start.75 = (f32[8,128]{1,0:T(8,128)S(1)}, f32[8,128]{1,0:T(8,128)S(1)}, u32[]{:S(2)}, u32[]{:S(2)}) collective-permute-start(f32[8,128]{1,0:T(8,128)S(1)} %get-tuple-element.190), channel_id=1, source_target_pairs={{0,4},{1,5},{2,6},{3,7},{4,0},{5,1},{6,2},{7,3},{8,12},{9,13},{10,... | collective-permute-start | bytes 12296 | tf_op jit(solution)/shard_map/ppermute | solution.py:474
  164.6 1.2 collective-permute-done.76
  165.8 1.2 collective-permute-start.79
  167.7 1.5 estimate.1
  169.5 1.5 model.1
  (114 shorter events, 23.7 us)
Async XLA Ops:
  5.8 7.7 %collective-permute-start = (bf16[264,128]{1,0:T(8,128)(2,1)}, bf16[264,128]{1,0:T(8,128)(2,1)S(1)}, u32[]{:S(2)}, u32[]{:S(2)}) collective-permute-start(bf16[264,128]{1,0:T(8,128)(2,1)} %get-tuple-element.100), channel_id=1, source_target_pairs={{0,8},{1,9},{2,10},{3,11},{4,12},{5,13},{6,14},{7,15},{8,0},{9,1},... | collective-permute-start | bytes 202760 | tf_op jit(solution)/shard_map/ppermute | solution.py:416
  11.5 7.1 %collective-permute-start.2 = (bf16[264,128]{1,0:T(8,128)(2,1)}, bf16[264,128]{1,0:T(8,128)(2,1)S(1)}, u32[]{:S(2)}, u32[]{:S(2)}) collective-permute-start(bf16[264,128]{1,0:T(8,128)(2,1)} %get-tuple-element.102), channel_id=1, source_target_pairs={{0,12},{1,13},{2,14},{3,15},{4,8},{5,9},{6,10},{7,11},{8,4},{9,5},... | collective-permute-start | bytes 202760 | tf_op jit(solution)/shard_map/ppermute | solution.py:416
  11.5 8.6 %collective-permute-start.3 = (bf16[264,128]{1,0:T(8,128)(2,1)}, bf16[264,128]{1,0:T(8,128)(2,1)S(1)}, u32[]{:S(2)}, u32[]{:S(2)}) collective-permute-start(bf16[264,128]{1,0:T(8,128)(2,1)} %get-tuple-element.103), channel_id=1, source_target_pairs={{0,1},{1,0},{2,3},{3,2},{4,5},{5,4},{6,7},{7,6},{8,9},{9,8},{10,11... | collective-permute-start | bytes 202760 | tf_op jit(solution)/shard_map/ppermute | solution.py:416
  11.5 11.1 %collective-permute-start.4 = (bf16[264,128]{1,0:T(8,128)(2,1)}, bf16[264,128]{1,0:T(8,128)(2,1)S(1)}, u32[]{:S(2)}, u32[]{:S(2)}) collective-permute-start(bf16[264,128]{1,0:T(8,128)(2,1)} %get-tuple-element.104), channel_id=1, source_target_pairs={{0,9},{1,8},{2,11},{3,10},{4,13},{5,12},{6,15},{7,14},{8,1},{9,0},... | collective-permute-start | bytes 202760 | tf_op jit(solution)/shard_map/ppermute | solution.py:416
  13.6 10.1 %collective-permute-start.5 = (bf16[264,128]{1,0:T(8,128)(2,1)}, bf16[264,128]{1,0:T(8,128)(2,1)S(1)}, u32[]{:S(2)}, u32[]{:S(2)}) collective-permute-start(bf16[264,128]{1,0:T(8,128)(2,1)} %get-tuple-element.105), channel_id=1, source_target_pairs={{0,5},{1,4},{2,7},{3,6},{4,1},{5,0},{6,3},{7,2},{8,13},{9,12},{10,... | collective-permute-start | bytes 202760 | tf_op jit(solution)/shard_map/ppermute | solution.py:416
  15.6 10.8 %collective-permute-start.6 = (bf16[264,128]{1,0:T(8,128)(2,1)}, bf16[264,128]{1,0:T(8,128)(2,1)S(1)}, u32[]{:S(2)}, u32[]{:S(2)}) collective-permute-start(bf16[264,128]{1,0:T(8,128)(2,1)} %get-tuple-element.106), channel_id=1, source_target_pairs={{0,13},{1,12},{2,15},{3,14},{4,9},{5,8},{6,11},{7,10},{8,5},{9,4},... | collective-permute-start | bytes 202760 | tf_op jit(solution)/shard_map/ppermute | solution.py:416
  18.6 8.9 %collective-permute-start.7 = (bf16[264,128]{1,0:T(8,128)(2,1)}, bf16[264,128]{1,0:T(8,128)(2,1)S(1)}, u32[]{:S(2)}, u32[]{:S(2)}) collective-permute-start(bf16[264,128]{1,0:T(8,128)(2,1)} %get-tuple-element.107), channel_id=1, source_target_pairs={{0,2},{1,3},{2,0},{3,1},{4,6},{5,7},{6,4},{7,5},{8,10},{9,11},{10,... | collective-permute-start | bytes 202760 | tf_op jit(solution)/shard_map/ppermute | solution.py:416
  20.1 8.1 %collective-permute-start.8 = (bf16[264,128]{1,0:T(8,128)(2,1)}, bf16[264,128]{1,0:T(8,128)(2,1)S(1)}, u32[]{:S(2)}, u32[]{:S(2)}) collective-permute-start(bf16[264,128]{1,0:T(8,128)(2,1)} %get-tuple-element.108), channel_id=1, source_target_pairs={{0,10},{1,11},{2,8},{3,9},{4,14},{5,15},{6,12},{7,13},{8,2},{9,3},... | collective-permute-start | bytes 202760 | tf_op jit(solution)/shard_map/ppermute | solution.py:416
  22.6 6.4 %collective-permute-start.9 = (bf16[264,128]{1,0:T(8,128)(2,1)}, bf16[264,128]{1,0:T(8,128)(2,1)S(1)}, u32[]{:S(2)}, u32[]{:S(2)}) collective-permute-start(bf16[264,128]{1,0:T(8,128)(2,1)} %get-tuple-element.109), channel_id=1, source_target_pairs={{0,6},{1,7},{2,4},{3,5},{4,2},{5,3},{6,0},{7,1},{8,14},{9,15},{10,... | collective-permute-start | bytes 202760 | tf_op jit(solution)/shard_map/ppermute | solution.py:416
  23.7 13.3 %collective-permute-start.10 = (bf16[264,128]{1,0:T(8,128)(2,1)}, bf16[264,128]{1,0:T(8,128)(2,1)S(1)}, u32[]{:S(2)}, u32[]{:S(2)}) collective-permute-start(bf16[264,128]{1,0:T(8,128)(2,1)} %get-tuple-element.110), channel_id=1, source_target_pairs={{0,14},{1,15},{2,12},{3,13},{4,10},{5,11},{6,8},{7,9},{8,6},{9,7},... | collective-permute-start | bytes 202760 | tf_op jit(solution)/shard_map/ppermute | solution.py:416
  26.4 10.6 %collective-permute-start.11 = (bf16[264,128]{1,0:T(8,128)(2,1)}, bf16[264,128]{1,0:T(8,128)(2,1)S(1)}, u32[]{:S(2)}, u32[]{:S(2)}) collective-permute-start(bf16[264,128]{1,0:T(8,128)(2,1)} %get-tuple-element.111), channel_id=1, source_target_pairs={{0,3},{1,2},{2,1},{3,0},{4,7},{5,6},{6,5},{7,4},{8,11},{9,10},{10,... | collective-permute-start | bytes 202760 | tf_op jit(solution)/shard_map/ppermute | solution.py:416
  27.5 9.5 %collective-permute-start.12 = (bf16[264,128]{1,0:T(8,128)(2,1)}, bf16[264,128]{1,0:T(8,128)(2,1)S(1)}, u32[]{:S(2)}, u32[]{:S(2)}) collective-permute-start(bf16[264,128]{1,0:T(8,128)(2,1)} %get-tuple-element.112), channel_id=1, source_target_pairs={{0,11},{1,10},{2,9},{3,8},{4,15},{5,14},{6,13},{7,12},{8,3},{9,2},... | collective-permute-start | bytes 202760 | tf_op jit(solution)/shard_map/ppermute | solution.py:416
  28.2 8.8 %collective-permute-start.13 = (bf16[264,128]{1,0:T(8,128)(2,1)}, bf16[264,128]{1,0:T(8,128)(2,1)S(1)}, u32[]{:S(2)}, u32[]{:S(2)}) collective-permute-start(bf16[264,128]{1,0:T(8,128)(2,1)} %get-tuple-element.113), channel_id=1, source_target_pairs={{0,7},{1,6},{2,5},{3,4},{4,3},{5,2},{6,1},{7,0},{8,15},{9,14},{10,... | collective-permute-start | bytes 202760 | tf_op jit(solution)/shard_map/ppermute | solution.py:416
  29.0 8.0 %collective-permute-start.14 = (bf16[264,128]{1,0:T(8,128)(2,1)}, bf16[264,128]{1,0:T(8,128)(2,1)S(1)}, u32[]{:S(2)}, u32[]{:S(2)}) collective-permute-start(bf16[264,128]{1,0:T(8,128)(2,1)} %get-tuple-element.114), channel_id=1, source_target_pairs={{0,15},{1,14},{2,13},{3,12},{4,11},{5,10},{6,9},{7,8},{8,7},{9,6},... | collective-permute-start | bytes 202760 | tf_op jit(solution)/shard_map/ppermute | solution.py:416
  39.6 7.0 %collective-permute-start.15 = (bf16[264,128]{1,0:T(8,128)(2,1)S(1)}, bf16[264,128]{1,0:T(8,128)(2,1)S(1)}, u32[]{:S(2)}, u32[]{:S(2)}) collective-permute-start(bf16[264,128]{1,0:T(8,128)(2,1)S(1)} %get-tuple-element.119), channel_id=1, source_target_pairs={{0,8},{1,9},{2,10},{3,11},{4,12},{5,13},{6,14},{7,15},{8,0},{9,1},... | collective-permute-start | bytes 202760 | tf_op jit(solution)/shard_map/ppermute | solution.py:416
  39.7 7.2 %collective-permute-start.16 = (bf16[264,128]{1,0:T(8,128)(2,1)S(1)}, bf16[264,128]{1,0:T(8,128)(2,1)S(1)}, u32[]{:S(2)}, u32[]{:S(2)}) collective-permute-start(bf16[264,128]{1,0:T(8,128)(2,1)S(1)} %get-tuple-element.120), channel_id=1, source_target_pairs={{0,4},{1,5},{2,6},{3,7},{4,0},{5,1},{6,2},{7,3},{8,12},{9,13},{10,... | collective-permute-start | bytes 202760 | tf_op jit(solution)/shard_map/ppermute | solution.py:416
  42.8 6.8 %collective-permute-start.17 = (bf16[264,128]{1,0:T(8,128)(2,1)S(1)}, bf16[264,128]{1,0:T(8,128)(2,1)S(1)}, u32[]{:S(2)}, u32[]{:S(2)}) collective-permute-start(bf16[264,128]{1,0:T(8,128)(2,1)S(1)} %get-tuple-element.121), channel_id=1, source_target_pairs={{0,12},{1,13},{2,14},{3,15},{4,8},{5,9},{6,10},{7,11},{8,4},{9,5},... | collective-permute-start | bytes 202760 | tf_op jit(solution)/shard_map/ppermute | solution.py:416
  44.0 9.1 %collective-permute-start.19 = (bf16[264,128]{1,0:T(8,128)(2,1)S(1)}, bf16[264,128]{1,0:T(8,128)(2,1)S(1)}, u32[]{:S(2)}, u32[]{:S(2)}) collective-permute-start(bf16[264,128]{1,0:T(8,128)(2,1)S(1)} %get-tuple-element.123), channel_id=1, source_target_pairs={{0,9},{1,8},{2,11},{3,10},{4,13},{5,12},{6,15},{7,14},{8,1},{9,0},... | collective-permute-start | bytes 202760 | tf_op jit(solution)/shard_map/ppermute | solution.py:416
  46.5 7.0 %collective-permute-start.20 = (bf16[264,128]{1,0:T(8,128)(2,1)S(1)}, bf16[264,128]{1,0:T(8,128)(2,1)S(1)}, u32[]{:S(2)}, u32[]{:S(2)}) collective-permute-start(bf16[264,128]{1,0:T(8,128)(2,1)S(1)} %get-tuple-element.124), channel_id=1, source_target_pairs={{0,5},{1,4},{2,7},{3,6},{4,1},{5,0},{6,3},{7,2},{8,13},{9,12},{10,... | collective-permute-start | bytes 202760 | tf_op jit(solution)/shard_map/ppermute | solution.py:416
  46.9 9.5 %collective-permute-start.21 = (bf16[264,128]{1,0:T(8,128)(2,1)S(1)}, bf16[264,128]{1,0:T(8,128)(2,1)S(1)}, u32[]{:S(2)}, u32[]{:S(2)}) collective-permute-start(bf16[264,128]{1,0:T(8,128)(2,1)S(1)} %get-tuple-element.125), channel_id=1, source_target_pairs={{0,13},{1,12},{2,15},{3,14},{4,9},{5,8},{6,11},{7,10},{8,5},{9,4},... | collective-permute-start | bytes 202760 | tf_op jit(solution)/shard_map/ppermute | solution.py:416
  49.6 6.8 %collective-permute-start.22 = (bf16[264,128]{1,0:T(8,128)(2,1)S(1)}, bf16[264,128]{1,0:T(8,128)(2,1)S(1)}, u32[]{:S(2)}, u32[]{:S(2)}) collective-permute-start(bf16[264,128]{1,0:T(8,128)(2,1)S(1)} %get-tuple-element.126), channel_id=1, source_target_pairs={{0,2},{1,3},{2,0},{3,1},{4,6},{5,7},{6,4},{7,5},{8,10},{9,11},{10,... | collective-permute-start | bytes 202760 | tf_op jit(solution)/shard_map/ppermute | solution.py:416
  49.7 9.0 %collective-permute-start.23 = (bf16[264,128]{1,0:T(8,128)(2,1)S(1)}, bf16[264,128]{1,0:T(8,128)(2,1)S(1)}, u32[]{:S(2)}, u32[]{:S(2)}) collective-permute-start(bf16[264,128]{1,0:T(8,128)(2,1)S(1)} %get-tuple-element.127), channel_id=1, source_target_pairs={{0,10},{1,11},{2,8},{3,9},{4,14},{5,15},{6,12},{7,13},{8,2},{9,3},... | collective-permute-start | bytes 202760 | tf_op jit(solution)/shard_map/ppermute | solution.py:416
  53.1 6.5 %collective-permute-start.24 = (bf16[264,128]{1,0:T(8,128)(2,1)S(1)}, bf16[264,128]{1,0:T(8,128)(2,1)S(1)}, u32[]{:S(2)}, u32[]{:S(2)}) collective-permute-start(bf16[264,128]{1,0:T(8,128)(2,1)S(1)} %get-tuple-element.128), channel_id=1, source_target_pairs={{0,6},{1,7},{2,4},{3,5},{4,2},{5,3},{6,0},{7,1},{8,14},{9,15},{10,... | collective-permute-start | bytes 202760 | tf_op jit(solution)/shard_map/ppermute | solution.py:416
  53.6 9.0 %collective-permute-start.25 = (bf16[264,128]{1,0:T(8,128)(2,1)S(1)}, bf16[264,128]{1,0:T(8,128)(2,1)S(1)}, u32[]{:S(2)}, u32[]{:S(2)}) collective-permute-start(bf16[264,128]{1,0:T(8,128)(2,1)S(1)} %get-tuple-element.129), channel_id=1, source_target_pairs={{0,14},{1,15},{2,12},{3,13},{4,10},{5,11},{6,8},{7,9},{8,6},{9,7},... | collective-permute-start | bytes 202760 | tf_op jit(solution)/shard_map/ppermute | solution.py:416
  56.4 6.6 %collective-permute-start.27 = (bf16[264,128]{1,0:T(8,128)(2,1)S(1)}, bf16[264,128]{1,0:T(8,128)(2,1)S(1)}, u32[]{:S(2)}, u32[]{:S(2)}) collective-permute-start(bf16[264,128]{1,0:T(8,128)(2,1)S(1)} %get-tuple-element.131), channel_id=1, source_target_pairs={{0,11},{1,10},{2,9},{3,8},{4,15},{5,14},{6,13},{7,12},{8,3},{9,2},... | collective-permute-start | bytes 202760 | tf_op jit(solution)/shard_map/ppermute | solution.py:416
  59.6 6.6 %collective-permute-start.29 = (bf16[264,128]{1,0:T(8,128)(2,1)S(1)}, bf16[264,128]{1,0:T(8,128)(2,1)S(1)}, u32[]{:S(2)}, u32[]{:S(2)}) collective-permute-start(bf16[264,128]{1,0:T(8,128)(2,1)S(1)} %get-tuple-element.133), channel_id=1, source_target_pairs={{0,15},{1,14},{2,13},{3,12},{4,11},{5,10},{6,9},{7,8},{8,7},{9,6},... | collective-permute-start | bytes 202760 | tf_op jit(solution)/shard_map/ppermute | solution.py:416
  69.8 7.1 %collective-permute-start.30 = (bf16[264,128]{1,0:T(8,128)(2,1)S(1)}, bf16[264,128]{1,0:T(8,128)(2,1)S(1)}, u32[]{:S(2)}, u32[]{:S(2)}) collective-permute-start(bf16[264,128]{1,0:T(8,128)(2,1)S(1)} %get-tuple-element.137), channel_id=1, source_target_pairs={{0,8},{1,9},{2,10},{3,11},{4,12},{5,13},{6,14},{7,15},{8,0},{9,1},... | collective-permute-start | bytes 202760 | tf_op jit(solution)/shard_map/ppermute | solution.py:416
  70.4 6.7 %collective-permute-start.31 = (bf16[264,128]{1,0:T(8,128)(2,1)S(1)}, bf16[264,128]{1,0:T(8,128)(2,1)S(1)}, u32[]{:S(2)}, u32[]{:S(2)}) collective-permute-start(bf16[264,128]{1,0:T(8,128)(2,1)S(1)} %get-tuple-element.138), channel_id=1, source_target_pairs={{0,4},{1,5},{2,6},{3,7},{4,0},{5,1},{6,2},{7,3},{8,12},{9,13},{10,... | collective-permute-start | bytes 202760 | tf_op jit(solution)/shard_map/ppermute | solution.py:416
  72.9 6.7 %collective-permute-start.32 = (bf16[264,128]{1,0:T(8,128)(2,1)S(1)}, bf16[264,128]{1,0:T(8,128)(2,1)S(1)}, u32[]{:S(2)}, u32[]{:S(2)}) collective-permute-start(bf16[264,128]{1,0:T(8,128)(2,1)S(1)} %get-tuple-element.139), channel_id=1, source_target_pairs={{0,12},{1,13},{2,14},{3,15},{4,8},{5,9},{6,10},{7,11},{8,4},{9,5},... | collective-permute-start | bytes 202760 | tf_op jit(solution)/shard_map/ppermute | solution.py:416
  74.2 9.8 %collective-permute-start.34 = (bf16[264,128]{1,0:T(8,128)(2,1)S(1)}, bf16[264,128]{1,0:T(8,128)(2,1)S(1)}, u32[]{:S(2)}, u32[]{:S(2)}) collective-permute-start(bf16[264,128]{1,0:T(8,128)(2,1)S(1)} %get-tuple-element.141), channel_id=1, source_target_pairs={{0,9},{1,8},{2,11},{3,10},{4,13},{5,12},{6,15},{7,14},{8,1},{9,0},... | collective-permute-start | bytes 202760 | tf_op jit(solution)/shard_map/ppermute | solution.py:416
  76.9 7.1 %collective-permute-start.35 = (bf16[264,128]{1,0:T(8,128)(2,1)S(1)}, bf16[264,128]{1,0:T(8,128)(2,1)S(1)}, u32[]{:S(2)}, u32[]{:S(2)}) collective-permute-start(bf16[264,128]{1,0:T(8,128)(2,1)S(1)} %get-tuple-element.142), channel_id=1, source_target_pairs={{0,5},{1,4},{2,7},{3,6},{4,1},{5,0},{6,3},{7,2},{8,13},{9,12},{10,... | collective-permute-start | bytes 202760 | tf_op jit(solution)/shard_map/ppermute | solution.py:416
  77.0 9.3 %collective-permute-start.36 = (bf16[264,128]{1,0:T(8,128)(2,1)S(1)}, bf16[264,128]{1,0:T(8,128)(2,1)S(1)}, u32[]{:S(2)}, u32[]{:S(2)}) collective-permute-start(bf16[264,128]{1,0:T(8,128)(2,1)S(1)} %get-tuple-element.143), channel_id=1, source_target_pairs={{0,13},{1,12},{2,15},{3,14},{4,9},{5,8},{6,11},{7,10},{8,5},{9,4},... | collective-permute-start | bytes 202760 | tf_op jit(solution)/shard_map/ppermute | solution.py:416
  79.6 7.5 %collective-permute-start.37 = (bf16[264,128]{1,0:T(8,128)(2,1)S(1)}, bf16[264,128]{1,0:T(8,128)(2,1)S(1)}, u32[]{:S(2)}, u32[]{:S(2)}) collective-permute-start(bf16[264,128]{1,0:T(8,128)(2,1)S(1)} %get-tuple-element.144), channel_id=1, source_target_pairs={{0,2},{1,3},{2,0},{3,1},{4,6},{5,7},{6,4},{7,5},{8,10},{9,11},{10,... | collective-permute-start | bytes 202760 | tf_op jit(solution)/shard_map/ppermute | solution.py:416
  80.0 9.7 %collective-permute-start.38 = (bf16[264,128]{1,0:T(8,128)(2,1)S(1)}, bf16[264,128]{1,0:T(8,128)(2,1)S(1)}, u32[]{:S(2)}, u32[]{:S(2)}) collective-permute-start(bf16[264,128]{1,0:T(8,128)(2,1)S(1)} %get-tuple-element.145), channel_id=1, source_target_pairs={{0,10},{1,11},{2,8},{3,9},{4,14},{5,15},{6,12},{7,13},{8,2},{9,3},... | collective-permute-start | bytes 202760 | tf_op jit(solution)/shard_map/ppermute | solution.py:416
  84.1 8.5 %collective-permute-start.40 = (bf16[264,128]{1,0:T(8,128)(2,1)S(1)}, bf16[264,128]{1,0:T(8,128)(2,1)S(1)}, u32[]{:S(2)}, u32[]{:S(2)}) collective-permute-start(bf16[264,128]{1,0:T(8,128)(2,1)S(1)} %get-tuple-element.147), channel_id=1, source_target_pairs={{0,14},{1,15},{2,12},{3,13},{4,10},{5,11},{6,8},{7,9},{8,6},{9,7},... | collective-permute-start | bytes 202760 | tf_op jit(solution)/shard_map/ppermute | solution.py:416
  86.3 6.3 %collective-permute-start.41 = (bf16[264,128]{1,0:T(8,128)(2,1)S(1)}, bf16[264,128]{1,0:T(8,128)(2,1)S(1)}, u32[]{:S(2)}, u32[]{:S(2)}) collective-permute-start(bf16[264,128]{1,0:T(8,128)(2,1)S(1)} %get-tuple-element.148), channel_id=1, source_target_pairs={{0,3},{1,2},{2,1},{3,0},{4,7},{5,6},{6,5},{7,4},{8,11},{9,10},{10,... | collective-permute-start | bytes 202760 | tf_op jit(solution)/shard_map/ppermute | solution.py:416
  87.1 7.3 %collective-permute-start.42 = (bf16[264,128]{1,0:T(8,128)(2,1)S(1)}, bf16[264,128]{1,0:T(8,128)(2,1)S(1)}, u32[]{:S(2)}, u32[]{:S(2)}) collective-permute-start(bf16[264,128]{1,0:T(8,128)(2,1)S(1)} %get-tuple-element.149), channel_id=1, source_target_pairs={{0,11},{1,10},{2,9},{3,8},{4,15},{5,14},{6,13},{7,12},{8,3},{9,2},... | collective-permute-start | bytes 202760 | tf_op jit(solution)/shard_map/ppermute | solution.py:416
  89.9 6.5 %collective-permute-start.44 = (bf16[264,128]{1,0:T(8,128)(2,1)S(1)}, bf16[264,128]{1,0:T(8,128)(2,1)S(1)}, u32[]{:S(2)}, u32[]{:S(2)}) collective-permute-start(bf16[264,128]{1,0:T(8,128)(2,1)S(1)} %get-tuple-element.151), channel_id=1, source_target_pairs={{0,15},{1,14},{2,13},{3,12},{4,11},{5,10},{6,9},{7,8},{8,7},{9,6},... | collective-permute-start | bytes 202760 | tf_op jit(solution)/shard_map/ppermute | solution.py:416
  98.9 7.5 %collective-permute-start.45 = (bf16[264,128]{1,0:T(8,128)(2,1)S(1)}, bf16[264,128]{1,0:T(8,128)(2,1)S(1)}, u32[]{:S(2)}, u32[]{:S(2)}) collective-permute-start(bf16[264,128]{1,0:T(8,128)(2,1)S(1)} %get-tuple-element.155), channel_id=1, source_target_pairs={{0,8},{1,9},{2,10},{3,11},{4,12},{5,13},{6,14},{7,15},{8,0},{9,1},... | collective-permute-start | bytes 202760 | tf_op jit(solution)/shard_map/ppermute | solution.py:416
  99.6 6.8 %collective-permute-start.46 = (bf16[264,128]{1,0:T(8,128)(2,1)S(1)}, bf16[264,128]{1,0:T(8,128)(2,1)S(1)}, u32[]{:S(2)}, u32[]{:S(2)}) collective-permute-start(bf16[264,128]{1,0:T(8,128)(2,1)S(1)} %get-tuple-element.156), channel_id=1, source_target_pairs={{0,4},{1,5},{2,6},{3,7},{4,0},{5,1},{6,2},{7,3},{8,12},{9,13},{10,... | collective-permute-start | bytes 202760 | tf_op jit(solution)/shard_map/ppermute | solution.py:416
  101.7 8.8 %collective-permute-start.47 = (bf16[264,128]{1,0:T(8,128)(2,1)S(1)}, bf16[264,128]{1,0:T(8,128)(2,1)S(1)}, u32[]{:S(2)}, u32[]{:S(2)}) collective-permute-start(bf16[264,128]{1,0:T(8,128)(2,1)S(1)} %get-tuple-element.157), channel_id=1, source_target_pairs={{0,12},{1,13},{2,14},{3,15},{4,8},{5,9},{6,10},{7,11},{8,4},{9,5},... | collective-permute-start | bytes 202760 | tf_op jit(solution)/shard_map/ppermute | solution.py:416
  103.3 7.2 %collective-permute-start.48 = (bf16[264,128]{1,0:T(8,128)(2,1)S(1)}, bf16[264,128]{1,0:T(8,128)(2,1)S(1)}, u32[]{:S(2)}, u32[]{:S(2)}) collective-permute-start(bf16[264,128]{1,0:T(8,128)(2,1)S(1)} %get-tuple-element.158), channel_id=1, source_target_pairs={{0,1},{1,0},{2,3},{3,2},{4,5},{5,4},{6,7},{7,6},{8,9},{9,8},{10,11... | collective-permute-start | bytes 202760 | tf_op jit(solution)/shard_map/ppermute | solution.py:416
  103.3 9.6 %collective-permute-start.49 = (bf16[264,128]{1,0:T(8,128)(2,1)S(1)}, bf16[264,128]{1,0:T(8,128)(2,1)S(1)}, u32[]{:S(2)}, u32[]{:S(2)}) collective-permute-start(bf16[264,128]{1,0:T(8,128)(2,1)S(1)} %get-tuple-element.159), channel_id=1, source_target_pairs={{0,9},{1,8},{2,11},{3,10},{4,13},{5,12},{6,15},{7,14},{8,1},{9,0},... | collective-permute-start | bytes 202760 | tf_op jit(solution)/shard_map/ppermute | solution.py:416
  106.4 7.4 %collective-permute-start.50 = (bf16[264,128]{1,0:T(8,128)(2,1)S(1)}, bf16[264,128]{1,0:T(8,128)(2,1)S(1)}, u32[]{:S(2)}, u32[]{:S(2)}) collective-permute-start(bf16[264,128]{1,0:T(8,128)(2,1)S(1)} %get-tuple-element.160), channel_id=1, source_target_pairs={{0,5},{1,4},{2,7},{3,6},{4,1},{5,0},{6,3},{7,2},{8,13},{9,12},{10,... | collective-permute-start | bytes 202760 | tf_op jit(solution)/shard_map/ppermute | solution.py:416
  106.4 10.9 %collective-permute-start.51 = (bf16[264,128]{1,0:T(8,128)(2,1)S(1)}, bf16[264,128]{1,0:T(8,128)(2,1)S(1)}, u32[]{:S(2)}, u32[]{:S(2)}) collective-permute-start(bf16[264,128]{1,0:T(8,128)(2,1)S(1)} %get-tuple-element.161), channel_id=1, source_target_pairs={{0,13},{1,12},{2,15},{3,14},{4,9},{5,8},{6,11},{7,10},{8,5},{9,4},... | collective-permute-start | bytes 202760 | tf_op jit(solution)/shard_map/ppermute | solution.py:416
  110.5 6.8 %collective-permute-start.52 = (bf16[264,128]{1,0:T(8,128)(2,1)S(1)}, bf16[264,128]{1,0:T(8,128)(2,1)S(1)}, u32[]{:S(2)}, u32[]{:S(2)}) collective-permute-start(bf16[264,128]{1,0:T(8,128)(2,1)S(1)} %get-tuple-element.162), channel_id=1, source_target_pairs={{0,2},{1,3},{2,0},{3,1},{4,6},{5,7},{6,4},{7,5},{8,10},{9,11},{10,... | collective-permute-start | bytes 202760 | tf_op jit(solution)/shard_map/ppermute | solution.py:416
  110.5 8.5 %collective-permute-start.53 = (bf16[264,128]{1,0:T(8,128)(2,1)S(1)}, bf16[264,128]{1,0:T(8,128)(2,1)S(1)}, u32[]{:S(2)}, u32[]{:S(2)}) collective-permute-start(bf16[264,128]{1,0:T(8,128)(2,1)S(1)} %get-tuple-element.163), channel_id=1, source_target_pairs={{0,10},{1,11},{2,8},{3,9},{4,14},{5,15},{6,12},{7,13},{8,2},{9,3},... | collective-permute-start | bytes 202760 | tf_op jit(solution)/shard_map/ppermute | solution.py:416
  112.9 6.8 %collective-permute-start.54 = (bf16[264,128]{1,0:T(8,128)(2,1)S(1)}, bf16[264,128]{1,0:T(8,128)(2,1)S(1)}, u32[]{:S(2)}, u32[]{:S(2)}) collective-permute-start(bf16[264,128]{1,0:T(8,128)(2,1)S(1)} %get-tuple-element.164), channel_id=1, source_target_pairs={{0,6},{1,7},{2,4},{3,5},{4,2},{5,3},{6,0},{7,1},{8,14},{9,15},{10,... | collective-permute-start | bytes 202760 | tf_op jit(solution)/shard_map/ppermute | solution.py:416
  113.8 9.7 %collective-permute-start.55 = (bf16[264,128]{1,0:T(8,128)(2,1)S(1)}, bf16[264,128]{1,0:T(8,128)(2,1)S(1)}, u32[]{:S(2)}, u32[]{:S(2)}) collective-permute-start(bf16[264,128]{1,0:T(8,128)(2,1)S(1)} %get-tuple-element.165), channel_id=1, source_target_pairs={{0,14},{1,15},{2,12},{3,13},{4,10},{5,11},{6,8},{7,9},{8,6},{9,7},... | collective-permute-start | bytes 202760 | tf_op jit(solution)/shard_map/ppermute | solution.py:416
  117.3 7.6 %collective-permute-start.57 = (bf16[264,128]{1,0:T(8,128)(2,1)S(1)}, bf16[264,128]{1,0:T(8,128)(2,1)S(1)}, u32[]{:S(2)}, u32[]{:S(2)}) collective-permute-start(bf16[264,128]{1,0:T(8,128)(2,1)S(1)} %get-tuple-element.167), channel_id=1, source_target_pairs={{0,11},{1,10},{2,9},{3,8},{4,15},{5,14},{6,13},{7,12},{8,3},{9,2},... | collective-permute-start | bytes 202760 | tf_op jit(solution)/shard_map/ppermute | solution.py:416
  119.7 7.2 %collective-permute-start.59 = (bf16[264,128]{1,0:T(8,128)(2,1)S(1)}, bf16[264,128]{1,0:T(8,128)(2,1)S(1)}, u32[]{:S(2)}, u32[]{:S(2)}) collective-permute-start(bf16[264,128]{1,0:T(8,128)(2,1)S(1)} %get-tuple-element.169), channel_id=1, source_target_pairs={{0,15},{1,14},{2,13},{3,12},{4,11},{5,10},{6,9},{7,8},{8,7},{9,6},... | collective-permute-start | bytes 202760 | tf_op jit(solution)/shard_map/ppermute | solution.py:416
  130.5 7.0 %collective-permute-start.60 = (bf16[264,128]{1,0:T(8,128)(2,1)S(1)}, bf16[264,128]{1,0:T(8,128)(2,1)S(1)}, u32[]{:S(2)}, u32[]{:S(2)}) collective-permute-start(bf16[264,128]{1,0:T(8,128)(2,1)S(1)} %get-tuple-element.174), channel_id=1, source_target_pairs={{0,8},{1,9},{2,10},{3,11},{4,12},{5,13},{6,14},{7,15},{8,0},{9,1},... | collective-permute-start | bytes 202760 | tf_op jit(solution)/shard_map/ppermute | solution.py:416
  130.9 7.5 %collective-permute-start.61 = (bf16[264,128]{1,0:T(8,128)(2,1)S(1)}, bf16[264,128]{1,0:T(8,128)(2,1)S(1)}, u32[]{:S(2)}, u32[]{:S(2)}) collective-permute-start(bf16[264,128]{1,0:T(8,128)(2,1)S(1)} %get-tuple-element.175), channel_id=1, source_target_pairs={{0,4},{1,5},{2,6},{3,7},{4,0},{5,1},{6,2},{7,3},{8,12},{9,13},{10,... | collective-permute-start | bytes 202760 | tf_op jit(solution)/shard_map/ppermute | solution.py:416
  133.5 6.7 %collective-permute-start.62 = (bf16[264,128]{1,0:T(8,128)(2,1)S(1)}, bf16[264,128]{1,0:T(8,128)(2,1)S(1)}, u32[]{:S(2)}, u32[]{:S(2)}) collective-permute-start(bf16[264,128]{1,0:T(8,128)(2,1)S(1)} %get-tuple-element.176), channel_id=1, source_target_pairs={{0,12},{1,13},{2,14},{3,15},{4,8},{5,9},{6,10},{7,11},{8,4},{9,5},... | collective-permute-start | bytes 202760 | tf_op jit(solution)/shard_map/ppermute | solution.py:416
  134.9 9.2 %collective-permute-start.64 = (bf16[264,128]{1,0:T(8,128)(2,1)S(1)}, bf16[264,128]{1,0:T(8,128)(2,1)S(1)}, u32[]{:S(2)}, u32[]{:S(2)}) collective-permute-start(bf16[264,128]{1,0:T(8,128)(2,1)S(1)} %get-tuple-element.178), channel_id=1, source_target_pairs={{0,9},{1,8},{2,11},{3,10},{4,13},{5,12},{6,15},{7,14},{8,1},{9,0},... | collective-permute-start | bytes 202760 | tf_op jit(solution)/shard_map/ppermute | solution.py:416
  137.5 7.1 %collective-permute-start.65 = (bf16[264,128]{1,0:T(8,128)(2,1)S(1)}, bf16[264,128]{1,0:T(8,128)(2,1)S(1)}, u32[]{:S(2)}, u32[]{:S(2)}) collective-permute-start(bf16[264,128]{1,0:T(8,128)(2,1)S(1)} %get-tuple-element.179), channel_id=1, source_target_pairs={{0,5},{1,4},{2,7},{3,6},{4,1},{5,0},{6,3},{7,2},{8,13},{9,12},{10,... | collective-permute-start | bytes 202760 | tf_op jit(solution)/shard_map/ppermute | solution.py:416
  138.4 8.6 %collective-permute-start.66 = (bf16[264,128]{1,0:T(8,128)(2,1)S(1)}, bf16[264,128]{1,0:T(8,128)(2,1)S(1)}, u32[]{:S(2)}, u32[]{:S(2)}) collective-permute-start(bf16[264,128]{1,0:T(8,128)(2,1)S(1)} %get-tuple-element.180), channel_id=1, source_target_pairs={{0,13},{1,12},{2,15},{3,14},{4,9},{5,8},{6,11},{7,10},{8,5},{9,4},... | collective-permute-start | bytes 202760 | tf_op jit(solution)/shard_map/ppermute | solution.py:416
  140.2 7.4 %collective-permute-start.67 = (bf16[264,128]{1,0:T(8,128)(2,1)S(1)}, bf16[264,128]{1,0:T(8,128)(2,1)S(1)}, u32[]{:S(2)}, u32[]{:S(2)}) collective-permute-start(bf16[264,128]{1,0:T(8,128)(2,1)S(1)} %get-tuple-element.181), channel_id=1, source_target_pairs={{0,2},{1,3},{2,0},{3,1},{4,6},{5,7},{6,4},{7,5},{8,10},{9,11},{10,... | collective-permute-start | bytes 202760 | tf_op jit(solution)/shard_map/ppermute | solution.py:416
  140.8 9.0 %collective-permute-start.68 = (bf16[264,128]{1,0:T(8,128)(2,1)S(1)}, bf16[264,128]{1,0:T(8,128)(2,1)S(1)}, u32[]{:S(2)}, u32[]{:S(2)}) collective-permute-start(bf16[264,128]{1,0:T(8,128)(2,1)S(1)} %get-tuple-element.182), channel_id=1, source_target_pairs={{0,10},{1,11},{2,8},{3,9},{4,14},{5,15},{6,12},{7,13},{8,2},{9,3},... | collective-permute-start | bytes 202760 | tf_op jit(solution)/shard_map/ppermute | solution.py:416
  144.2 6.3 %collective-permute-start.69 = (bf16[264,128]{1,0:T(8,128)(2,1)S(1)}, bf16[264,128]{1,0:T(8,128)(2,1)S(1)}, u32[]{:S(2)}, u32[]{:S(2)}) collective-permute-start(bf16[264,128]{1,0:T(8,128)(2,1)S(1)} %get-tuple-element.183), channel_id=1, source_target_pairs={{0,6},{1,7},{2,4},{3,5},{4,2},{5,3},{6,0},{7,1},{8,14},{9,15},{10,... | collective-permute-start | bytes 202760 | tf_op jit(solution)/shard_map/ppermute | solution.py:416
  144.7 8.5 %collective-permute-start.70 = (bf16[264,128]{1,0:T(8,128)(2,1)S(1)}, bf16[264,128]{1,0:T(8,128)(2,1)S(1)}, u32[]{:S(2)}, u32[]{:S(2)}) collective-permute-start(bf16[264,128]{1,0:T(8,128)(2,1)S(1)} %get-tuple-element.184), channel_id=1, source_target_pairs={{0,14},{1,15},{2,12},{3,13},{4,10},{5,11},{6,8},{7,9},{8,6},{9,7},... | collective-permute-start | bytes 202760 | tf_op jit(solution)/shard_map/ppermute | solution.py:416
  146.9 6.4 %collective-permute-start.71 = (bf16[264,128]{1,0:T(8,128)(2,1)S(1)}, bf16[264,128]{1,0:T(8,128)(2,1)S(1)}, u32[]{:S(2)}, u32[]{:S(2)}) collective-permute-start(bf16[264,128]{1,0:T(8,128)(2,1)S(1)} %get-tuple-element.185), channel_id=1, source_target_pairs={{0,3},{1,2},{2,1},{3,0},{4,7},{5,6},{6,5},{7,4},{8,11},{9,10},{10,... | collective-permute-start | bytes 202760 | tf_op jit(solution)/shard_map/ppermute | solution.py:416
  147.5 7.4 %collective-permute-start.72 = (bf16[264,128]{1,0:T(8,128)(2,1)S(1)}, bf16[264,128]{1,0:T(8,128)(2,1)S(1)}, u32[]{:S(2)}, u32[]{:S(2)}) collective-permute-start(bf16[264,128]{1,0:T(8,128)(2,1)S(1)} %get-tuple-element.186), channel_id=1, source_target_pairs={{0,11},{1,10},{2,9},{3,8},{4,15},{5,14},{6,13},{7,12},{8,3},{9,2},... | collective-permute-start | bytes 202760 | tf_op jit(solution)/shard_map/ppermute | solution.py:416
  150.5 6.6 %collective-permute-start.74 = (bf16[264,128]{1,0:T(8,128)(2,1)S(1)}, bf16[264,128]{1,0:T(8,128)(2,1)S(1)}, u32[]{:S(2)}, u32[]{:S(2)}) collective-permute-start(bf16[264,128]{1,0:T(8,128)(2,1)S(1)} %get-tuple-element.188), channel_id=1, source_target_pairs={{0,15},{1,14},{2,13},{3,12},{4,11},{5,10},{6,9},{7,8},{8,7},{9,6},... | collective-permute-start | bytes 202760 | tf_op jit(solution)/shard_map/ppermute | solution.py:416
  (20 other events, 122.7 us)

commit v20 on v17

--- a/solution.py
+++ b/solution.py
@@ -24,7 +24,8 @@
 def steps_of(peers):
     half, quarter = peers // 2, peers // 4
     near = [step for low in range(quarter) for step in (low, quarter + low)][1:]
-    return [0, half] + [step for low in near for step in (low, half + low)]
+    far = half + quarter
+    return [0, far] + [step for low in near for step in (low, far ^ low)]
 
 
 def diagonal(cols):

time: 172 us -> 174 us (1.012)
  starting transfers between devices: 108 us -> 111 us
    ppermute x75, starting transfers between devices: 102 us -> 104 us  [exchange(): lax.ppermute(value, 'pair', [(one, one ^ step) for one in range(peers)])]
  transfers between devices with their start and end apart: 81 -> 81, of which waited for: 30 -> 32; matrix products, arithmetic and copies ran while one was open for 0% -> 0% of each run, Pallas kernels for 3% -> 3%
where the time goes in v20:
time: 174 us
  starting transfers between devices  111 us (64%)
  waiting for transfers between devices  36.3 us (21%)
  Pallas kernels  25.2 us (14%)
    ppermute x75, starting transfers between devices, exchange(): lax.ppermute(value, 'pair', [(one, one ^ step) for one in range(peers)])  104 us
    ppermute x75, waiting for transfers between devices, exchange(): lax.ppermute(value, 'pair', [(one, one ^ step) for one in range(peers)])  34.4 us
    pallas_call x2, Pallas kernels, on_device(): call(functools.partial(pair_kernel, peers), 'pairs_last' if last else 'pa...  6.92 us
    ppermute x6, starting transfers between devices, on_device(): lax.ppermute(share, 'pair', [(one, one ^ step) for one in range(peers)])  6.31 us
    pallas_call x1, Pallas kernels, on_device(): call(functools.partial(start_kernel, peers), 'start', [SMEM, HBM, HBM, HB...  5.42 us
  transfers between devices with their start and end apart: 81, of which 32 were waited for; matrix products, arithmetic and copies ran while one was open for 0% of the time, Pallas kernels for 3%

profile of v20, /device:TPU:0, one launch (start us, length us, event | category | flops | bytes accessed | tf_op | source)
XLA Modules:
  0.0 174.5 jit_solution(15217125698058814130)
XLA Ops:
  0.6 5.4 %start.1 = (bf16[264,128]{1,0:T(8,128)(2,1)}, bf16[264,128]{1,0:T(8,128)(2,1)}, bf16[264,128]{1,0:T(8,128)(2,1)}, bf16[264,128]{1,0:T(8,128)(2,1)}, bf16[264,128...) custom-call(s32[1]{0:T(128)} %bitcast.me_ref, ...), custom_call_target="tpu_custom_call" | custom-call | flops 268435456 | bytes 6291456 | tf_op jit(solution)/shard_map/start/pallas_call | solution.py:417
  6.1 5.1 %collective-permute-start = (bf16[264,128]{1,0:T(8,128)(2,1)}, bf16[264,128]{1,0:T(8,128)(2,1)S(1)}, u32[]{:S(2)}, u32[]{:S(2)}) collective-permute-start(bf16[264,128]{1,0:T(8,128)(2,1)} %get-tuple-element.100), channel_id=1, source_target_pairs={{0,12},{1,13},{2,14},{3,15},{4,8},{5,9},{6,10},{7,11},{8,4},{9,5},... | collective-permute-start | bytes 202760 | tf_op jit(solution)/shard_map/ppermute | solution.py:412
  11.8 3.9 %collective-permute-start.4 = (bf16[264,128]{1,0:T(8,128)(2,1)}, bf16[264,128]{1,0:T(8,128)(2,1)S(1)}, u32[]{:S(2)}, u32[]{:S(2)}) collective-permute-start(bf16[264,128]{1,0:T(8,128)(2,1)} %get-tuple-element.104), channel_id=1, source_target_pairs={{0,13},{1,12},{2,15},{3,14},{4,9},{5,8},{6,11},{7,10},{8,5},{9,4},... | collective-permute-start | bytes 202760 | tf_op jit(solution)/shard_map/ppermute | solution.py:412
  16.1 2.4 %collective-permute-start.6 = (bf16[264,128]{1,0:T(8,128)(2,1)}, bf16[264,128]{1,0:T(8,128)(2,1)S(1)}, u32[]{:S(2)}, u32[]{:S(2)}) collective-permute-start(bf16[264,128]{1,0:T(8,128)(2,1)} %get-tuple-element.106), channel_id=1, source_target_pairs={{0,9},{1,8},{2,11},{3,10},{4,13},{5,12},{6,15},{7,14},{8,1},{9,0},... | collective-permute-start | bytes 202760 | tf_op jit(solution)/shard_map/ppermute | solution.py:412
  18.5 1.2 collective-permute-done.2.refs_3_
  19.7 1.6 collective-permute-start.7
  21.3 1.9 %collective-permute-start.8 = (bf16[264,128]{1,0:T(8,128)(2,1)}, bf16[264,128]{1,0:T(8,128)(2,1)S(1)}, u32[]{:S(2)}, u32[]{:S(2)}) collective-permute-start(bf16[264,128]{1,0:T(8,128)(2,1)} %get-tuple-element.108), channel_id=1, source_target_pairs={{0,14},{1,15},{2,12},{3,13},{4,10},{5,11},{6,8},{7,9},{8,6},{9,7},... | collective-permute-start | bytes 202760 | tf_op jit(solution)/shard_map/ppermute | solution.py:412
  23.1 3.3 %collective-permute-start.10 = (bf16[264,128]{1,0:T(8,128)(2,1)}, bf16[264,128]{1,0:T(8,128)(2,1)S(1)}, u32[]{:S(2)}, u32[]{:S(2)}) collective-permute-start(bf16[264,128]{1,0:T(8,128)(2,1)} %get-tuple-element.110), channel_id=1, source_target_pairs={{0,10},{1,11},{2,8},{3,9},{4,14},{5,15},{6,12},{7,13},{8,2},{9,3},... | collective-permute-start | bytes 202760 | tf_op jit(solution)/shard_map/ppermute | solution.py:412
  26.4 3.2 %collective-permute-start.12 = (bf16[264,128]{1,0:T(8,128)(2,1)}, bf16[264,128]{1,0:T(8,128)(2,1)S(1)}, u32[]{:S(2)}, u32[]{:S(2)}) collective-permute-start(bf16[264,128]{1,0:T(8,128)(2,1)} %get-tuple-element.112), channel_id=1, source_target_pairs={{0,15},{1,14},{2,13},{3,12},{4,11},{5,10},{6,9},{7,8},{8,7},{9,6},... | collective-permute-start | bytes 202760 | tf_op jit(solution)/shard_map/ppermute | solution.py:412
  30.0 2.6 %collective-permute-start.14 = (bf16[264,128]{1,0:T(8,128)(2,1)}, bf16[264,128]{1,0:T(8,128)(2,1)S(1)}, u32[]{:S(2)}, u32[]{:S(2)}) collective-permute-start(bf16[264,128]{1,0:T(8,128)(2,1)} %get-tuple-element.114), channel_id=1, source_target_pairs={{0,11},{1,10},{2,9},{3,8},{4,15},{5,14},{6,13},{7,12},{8,3},{9,2},... | collective-permute-start | bytes 202760 | tf_op jit(solution)/shard_map/ppermute | solution.py:412
  34.1 2.9 %keep.1 = (s32[128]{0:T(128)S(1)}, bf16[264,128]{1,0:T(8,128)(2,1)S(1)}, bf16[8,16,128,128]{3,2,1,0:T(8,128)(2,1)S(1)}) custom-call(s32[128]{0:T(128)S(1)} %copy-done.2, bf16[264,128]{1,0:T(8,128)(2,1)S(1)} %copy-done.1, bf16[8,16,128,128]{3,2,1,0:T(8,128)(2,1)} %rays_hbm.3), custom_call_target="tpu_custom_call" | custom-call | bytes 8388608 | tf_op jit(solution)/shard_map/keep/pallas_call | solution.py:429
  37.3 2.5 %cells_first.1 = (f32[64,8192]{1,0:T(8,128)S(1)}, f32[64,128]{1,0:T(8,128)S(1)}, bf16[264,128]{1,0:T(8,128)(2,1)S(1)}, bf16[264,128]{1,0:T(8,128)(2,1)S(1)}, bf1...) custom-call(bf16[264,128]{1,0:T(8,128)(2,1)S(1)} %get-tuple-element., ...), custom_call_target="tpu_custom_call" | custom-call | bytes 6291456 | tf_op jit(solution)/shard_map/cells_first/pallas_call | solution.py:434
  39.8 1.9 %collective-permute-start.15 = (bf16[264,128]{1,0:T(8,128)(2,1)S(1)}, bf16[264,128]{1,0:T(8,128)(2,1)S(1)}, u32[]{:S(2)}, u32[]{:S(2)}) collective-permute-start(bf16[264,128]{1,0:T(8,128)(2,1)S(1)} %get-tuple-element.119), channel_id=1, source_target_pairs={{0,12},{1,13},{2,14},{3,15},{4,8},{5,9},{6,10},{7,11},{8,4},{9,5},... | collective-permute-start | bytes 202760 | tf_op jit(solution)/shard_map/ppermute | solution.py:412
  41.7 2.5 %collective-permute-start.17 = (bf16[264,128]{1,0:T(8,128)(2,1)S(1)}, bf16[264,128]{1,0:T(8,128)(2,1)S(1)}, u32[]{:S(2)}, u32[]{:S(2)}) collective-permute-start(bf16[264,128]{1,0:T(8,128)(2,1)S(1)} %get-tuple-element.121), channel_id=1, source_target_pairs={{0,8},{1,9},{2,10},{3,11},{4,12},{5,13},{6,14},{7,15},{8,0},{9,1},... | collective-permute-start | bytes 202760 | tf_op jit(solution)/shard_map/ppermute | solution.py:412
  44.2 1.9 %collective-permute-start.19 = (bf16[264,128]{1,0:T(8,128)(2,1)S(1)}, bf16[264,128]{1,0:T(8,128)(2,1)S(1)}, u32[]{:S(2)}, u32[]{:S(2)}) collective-permute-start(bf16[264,128]{1,0:T(8,128)(2,1)S(1)} %get-tuple-element.123), channel_id=1, source_target_pairs={{0,13},{1,12},{2,15},{3,14},{4,9},{5,8},{6,11},{7,10},{8,5},{9,4},... | collective-permute-start | bytes 202760 | tf_op jit(solution)/shard_map/ppermute | solution.py:412
  46.6 1.4 collective-permute-done.16.refs_2_
  48.6 1.8 %collective-permute-done.17.refs_3_ = bf16[264,128]{1,0:T(8,128)(2,1)S(1)} collective-permute-done((bf16[264,128]{1,0:T(8,128)(2,1)S(1)}, bf16[264,128]{1,0:T(8,128)(2,1)S(1)}, u32[]{:S(2)}, u32[]{:S(2)}) %collective-permute-start.17) | collective-permute-done | bytes 67616 | tf_op jit(solution)/shard_map/ppermute | solution.py:412
  50.4 3.3 %collective-permute-start.23 = (bf16[264,128]{1,0:T(8,128)(2,1)S(1)}, bf16[264,128]{1,0:T(8,128)(2,1)S(1)}, u32[]{:S(2)}, u32[]{:S(2)}) collective-permute-start(bf16[264,128]{1,0:T(8,128)(2,1)S(1)} %get-tuple-element.127), channel_id=1, source_target_pairs={{0,14},{1,15},{2,12},{3,13},{4,10},{5,11},{6,8},{7,9},{8,6},{9,7},... | collective-permute-start | bytes 202760 | tf_op jit(solution)/shard_map/ppermute | solution.py:412
  53.7 3.4 %collective-permute-start.25 = (bf16[264,128]{1,0:T(8,128)(2,1)S(1)}, bf16[264,128]{1,0:T(8,128)(2,1)S(1)}, u32[]{:S(2)}, u32[]{:S(2)}) collective-permute-start(bf16[264,128]{1,0:T(8,128)(2,1)S(1)} %get-tuple-element.129), channel_id=1, source_target_pairs={{0,10},{1,11},{2,8},{3,9},{4,14},{5,15},{6,12},{7,13},{8,2},{9,3},... | collective-permute-start | bytes 202760 | tf_op jit(solution)/shard_map/ppermute | solution.py:412
  57.2 3.0 %collective-permute-start.27 = (bf16[264,128]{1,0:T(8,128)(2,1)S(1)}, bf16[264,128]{1,0:T(8,128)(2,1)S(1)}, u32[]{:S(2)}, u32[]{:S(2)}) collective-permute-start(bf16[264,128]{1,0:T(8,128)(2,1)S(1)} %get-tuple-element.131), channel_id=1, source_target_pairs={{0,15},{1,14},{2,13},{3,12},{4,11},{5,10},{6,9},{7,8},{8,7},{9,6},... | collective-permute-start | bytes 202760 | tf_op jit(solution)/shard_map/ppermute | solution.py:412
  60.2 3.2 %collective-permute-start.29 = (bf16[264,128]{1,0:T(8,128)(2,1)S(1)}, bf16[264,128]{1,0:T(8,128)(2,1)S(1)}, u32[]{:S(2)}, u32[]{:S(2)}) collective-permute-start(bf16[264,128]{1,0:T(8,128)(2,1)S(1)} %get-tuple-element.133), channel_id=1, source_target_pairs={{0,11},{1,10},{2,9},{3,8},{4,15},{5,14},{6,13},{7,12},{8,3},{9,2},... | collective-permute-start | bytes 202760 | tf_op jit(solution)/shard_map/ppermute | solution.py:412
  64.2 2.8 %collective-permute-done.28.refs_14_ = bf16[264,128]{1,0:T(8,128)(2,1)S(1)} collective-permute-done((bf16[264,128]{1,0:T(8,128)(2,1)S(1)}, bf16[264,128]{1,0:T(8,128)(2,1)S(1)}, u32[]{:S(2)}, u32[]{:S(2)}) %collective-permute-start.28) | collective-permute-done | bytes 67616 | tf_op jit(solution)/shard_map/ppermute | solution.py:412
  67.1 3.5 %pairs.1 = (bf16[264,128]{1,0:T(8,128)(2,1)S(1)}, bf16[264,128]{1,0:T(8,128)(2,1)S(1)}, bf16[264,128]{1,0:T(8,128)(2,1)S(1)}, bf16[264,128]{1,0:T(8,128)(2,1)S(1...) custom-call(s32[128]{0:T(128)S(1)} %get-tuple-element.117.target_ref, ...), custom_call_target="tpu_custom_call" | custom-call | flops 536870912 | bytes 8388608 | tf_op jit(solution)/shard_map/pairs/pallas_call | solution.py:445
  70.5 2.0 %collective-permute-start.30 = (bf16[264,128]{1,0:T(8,128)(2,1)S(1)}, bf16[264,128]{1,0:T(8,128)(2,1)S(1)}, u32[]{:S(2)}, u32[]{:S(2)}) collective-permute-start(bf16[264,128]{1,0:T(8,128)(2,1)S(1)} %get-tuple-element.137), channel_id=1, source_target_pairs={{0,12},{1,13},{2,14},{3,15},{4,8},{5,9},{6,10},{7,11},{8,4},{9,5},... | collective-permute-start | bytes 202760 | tf_op jit(solution)/shard_map/ppermute | solution.py:412
  72.5 2.4 %collective-permute-start.32 = (bf16[264,128]{1,0:T(8,128)(2,1)S(1)}, bf16[264,128]{1,0:T(8,128)(2,1)S(1)}, u32[]{:S(2)}, u32[]{:S(2)}) collective-permute-start(bf16[264,128]{1,0:T(8,128)(2,1)S(1)} %get-tuple-element.139), channel_id=1, source_target_pairs={{0,8},{1,9},{2,10},{3,11},{4,12},{5,13},{6,14},{7,15},{8,0},{9,1},... | collective-permute-start | bytes 202760 | tf_op jit(solution)/shard_map/ppermute | solution.py:412
  75.0 2.1 %collective-permute-start.34 = (bf16[264,128]{1,0:T(8,128)(2,1)S(1)}, bf16[264,128]{1,0:T(8,128)(2,1)S(1)}, u32[]{:S(2)}, u32[]{:S(2)}) collective-permute-start(bf16[264,128]{1,0:T(8,128)(2,1)S(1)} %get-tuple-element.141), channel_id=1, source_target_pairs={{0,13},{1,12},{2,15},{3,14},{4,9},{5,8},{6,11},{7,10},{8,5},{9,4},... | collective-permute-start | bytes 202760 | tf_op jit(solution)/shard_map/ppermute | solution.py:412
  77.1 1.7 collective-permute-done.31.refs_2_
  79.7 1.2 collective-permute-done.32.refs_3_
  80.9 1.1 collective-permute-start.37
  82.0 2.5 %collective-permute-start.38 = (bf16[264,128]{1,0:T(8,128)(2,1)S(1)}, bf16[264,128]{1,0:T(8,128)(2,1)S(1)}, u32[]{:S(2)}, u32[]{:S(2)}) collective-permute-start(bf16[264,128]{1,0:T(8,128)(2,1)S(1)} %get-tuple-element.145), channel_id=1, source_target_pairs={{0,14},{1,15},{2,12},{3,13},{4,10},{5,11},{6,8},{7,9},{8,6},{9,7},... | collective-permute-start | bytes 202760 | tf_op jit(solution)/shard_map/ppermute | solution.py:412
  84.6 3.1 %collective-permute-start.40 = (bf16[264,128]{1,0:T(8,128)(2,1)S(1)}, bf16[264,128]{1,0:T(8,128)(2,1)S(1)}, u32[]{:S(2)}, u32[]{:S(2)}) collective-permute-start(bf16[264,128]{1,0:T(8,128)(2,1)S(1)} %get-tuple-element.147), channel_id=1, source_target_pairs={{0,10},{1,11},{2,8},{3,9},{4,14},{5,15},{6,12},{7,13},{8,2},{9,3},... | collective-permute-start | bytes 202760 | tf_op jit(solution)/shard_map/ppermute | solution.py:412
  87.7 3.4 %collective-permute-start.42 = (bf16[264,128]{1,0:T(8,128)(2,1)S(1)}, bf16[264,128]{1,0:T(8,128)(2,1)S(1)}, u32[]{:S(2)}, u32[]{:S(2)}) collective-permute-start(bf16[264,128]{1,0:T(8,128)(2,1)S(1)} %get-tuple-element.149), channel_id=1, source_target_pairs={{0,15},{1,14},{2,13},{3,12},{4,11},{5,10},{6,9},{7,8},{8,7},{9,6},... | collective-permute-start | bytes 202760 | tf_op jit(solution)/shard_map/ppermute | solution.py:412
  91.7 2.1 %collective-permute-start.44 = (bf16[264,128]{1,0:T(8,128)(2,1)S(1)}, bf16[264,128]{1,0:T(8,128)(2,1)S(1)}, u32[]{:S(2)}, u32[]{:S(2)}) collective-permute-start(bf16[264,128]{1,0:T(8,128)(2,1)S(1)} %get-tuple-element.151), channel_id=1, source_target_pairs={{0,11},{1,10},{2,9},{3,8},{4,15},{5,14},{6,13},{7,12},{8,3},{9,2},... | collective-permute-start | bytes 202760 | tf_op jit(solution)/shard_map/ppermute | solution.py:412
  94.2 2.9 %collective-permute-done.43.refs_14_ = bf16[264,128]{1,0:T(8,128)(2,1)S(1)} collective-permute-done((bf16[264,128]{1,0:T(8,128)(2,1)S(1)}, bf16[264,128]{1,0:T(8,128)(2,1)S(1)}, u32[]{:S(2)}, u32[]{:S(2)}) %collective-permute-start.43) | collective-permute-done | bytes 67616 | tf_op jit(solution)/shard_map/ppermute | solution.py:412
  97.1 2.0 %collective-permute-done.44.refs_15_ = bf16[264,128]{1,0:T(8,128)(2,1)S(1)} collective-permute-done((bf16[264,128]{1,0:T(8,128)(2,1)S(1)}, bf16[264,128]{1,0:T(8,128)(2,1)S(1)}, u32[]{:S(2)}, u32[]{:S(2)}) %collective-permute-start.44) | collective-permute-done | bytes 67616 | tf_op jit(solution)/shard_map/ppermute | solution.py:412
  99.1 2.4 %cells.1 = (f32[64,8192]{1,0:T(8,128)S(1)}, f32[64,128]{1,0:T(8,128)S(1)}, bf16[264,128]{1,0:T(8,128)(2,1)S(1)}, bf16[264,128]{1,0:T(8,128)(2,1)S(1)}, bf16[264,...) custom-call(s32[16,128]{1,0:T(8,128)S(1)} %get-tuple-element.116.ask, ...), custom_call_target="tpu_custom_call" | custom-call | bytes 8388608 | tf_op jit(solution)/shard_map/cells/pallas_call | solution.py:454
  102.4 3.5 %collective-permute-start.47 = (bf16[264,128]{1,0:T(8,128)(2,1)S(1)}, bf16[264,128]{1,0:T(8,128)(2,1)S(1)}, u32[]{:S(2)}, u32[]{:S(2)}) collective-permute-start(bf16[264,128]{1,0:T(8,128)(2,1)S(1)} %get-tuple-element.157), channel_id=1, source_target_pairs={{0,8},{1,9},{2,10},{3,11},{4,12},{5,13},{6,14},{7,15},{8,0},{9,1},... | collective-permute-start | bytes 202760 | tf_op jit(solution)/shard_map/ppermute | solution.py:412
  106.9 1.4 collective-permute-done.45.refs_1_
  108.7 1.5 collective-permute-start.51
  110.9 1.7 collective-permute-start.52
  112.6 2.7 %collective-permute-start.53 = (bf16[264,128]{1,0:T(8,128)(2,1)S(1)}, bf16[264,128]{1,0:T(8,128)(2,1)S(1)}, u32[]{:S(2)}, u32[]{:S(2)}) collective-permute-start(bf16[264,128]{1,0:T(8,128)(2,1)S(1)} %get-tuple-element.163), channel_id=1, source_target_pairs={{0,14},{1,15},{2,12},{3,13},{4,10},{5,11},{6,8},{7,9},{8,6},{9,7},... | collective-permute-start | bytes 202760 | tf_op jit(solution)/shard_map/ppermute | solution.py:412
  115.3 2.3 %collective-permute-start.55 = (bf16[264,128]{1,0:T(8,128)(2,1)S(1)}, bf16[264,128]{1,0:T(8,128)(2,1)S(1)}, u32[]{:S(2)}, u32[]{:S(2)}) collective-permute-start(bf16[264,128]{1,0:T(8,128)(2,1)S(1)} %get-tuple-element.165), channel_id=1, source_target_pairs={{0,10},{1,11},{2,8},{3,9},{4,14},{5,15},{6,12},{7,13},{8,2},{9,3},... | collective-permute-start | bytes 202760 | tf_op jit(solution)/shard_map/ppermute | solution.py:412
  117.7 4.2 %collective-permute-start.57 = (bf16[264,128]{1,0:T(8,128)(2,1)S(1)}, bf16[264,128]{1,0:T(8,128)(2,1)S(1)}, u32[]{:S(2)}, u32[]{:S(2)}) collective-permute-start(bf16[264,128]{1,0:T(8,128)(2,1)S(1)} %get-tuple-element.167), channel_id=1, source_target_pairs={{0,15},{1,14},{2,13},{3,12},{4,11},{5,10},{6,9},{7,8},{8,7},{9,6},... | collective-permute-start | bytes 202760 | tf_op jit(solution)/shard_map/ppermute | solution.py:412
  121.8 2.0 %collective-permute-start.59 = (bf16[264,128]{1,0:T(8,128)(2,1)S(1)}, bf16[264,128]{1,0:T(8,128)(2,1)S(1)}, u32[]{:S(2)}, u32[]{:S(2)}) collective-permute-start(bf16[264,128]{1,0:T(8,128)(2,1)S(1)} %get-tuple-element.169), channel_id=1, source_target_pairs={{0,11},{1,10},{2,9},{3,8},{4,15},{5,14},{6,13},{7,12},{8,3},{9,2},... | collective-permute-start | bytes 202760 | tf_op jit(solution)/shard_map/ppermute | solution.py:412
  124.2 3.9 %collective-permute-done.58.refs_14_ = bf16[264,128]{1,0:T(8,128)(2,1)S(1)} collective-permute-done((bf16[264,128]{1,0:T(8,128)(2,1)S(1)}, bf16[264,128]{1,0:T(8,128)(2,1)S(1)}, u32[]{:S(2)}, u32[]{:S(2)}) %collective-permute-start.58) | collective-permute-done | bytes 67616 | tf_op jit(solution)/shard_map/ppermute | solution.py:412
  128.1 1.1 collective-permute-done.59.refs_15_
  129.2 3.5 %pairs_last.1 = (bf16[264,128]{1,0:T(8,128)(2,1)S(1)}, bf16[264,128]{1,0:T(8,128)(2,1)S(1)}, bf16[264,128]{1,0:T(8,128)(2,1)S(1)}, bf16[264,128]{1,0:T(8,128)(2,...) custom-call(s32[128]{0:T(128)S(1)} %get-tuple-element.117.target_ref, ...), custom_call_target="tpu_custom_call" | custom-call | flops 536870912 | bytes 8388608 | tf_op jit(solution)/shard_map/pairs_last/pallas_call | solution.py:445
  132.7 1.5 collective-permute-start.60
  134.2 2.9 %collective-permute-start.62 = (bf16[264,128]{1,0:T(8,128)(2,1)S(1)}, bf16[264,128]{1,0:T(8,128)(2,1)S(1)}, u32[]{:S(2)}, u32[]{:S(2)}) collective-permute-start(bf16[264,128]{1,0:T(8,128)(2,1)S(1)} %get-tuple-element.176), channel_id=1, source_target_pairs={{0,8},{1,9},{2,10},{3,11},{4,12},{5,13},{6,14},{7,15},{8,0},{9,1},... | collective-permute-start | bytes 202760 | tf_op jit(solution)/shard_map/ppermute | solution.py:412
  137.2 1.6 collective-permute-start.64
  139.9 1.4 collective-permute-start.66
  141.8 2.8 %collective-permute-start.67 = (bf16[264,128]{1,0:T(8,128)(2,1)S(1)}, bf16[264,128]{1,0:T(8,128)(2,1)S(1)}, u32[]{:S(2)}, u32[]{:S(2)}) collective-permute-start(bf16[264,128]{1,0:T(8,128)(2,1)S(1)} %get-tuple-element.181), channel_id=1, source_target_pairs={{0,2},{1,3},{2,0},{3,1},{4,6},{5,7},{6,4},{7,5},{8,10},{9,11},{10,... | collective-permute-start | bytes 202760 | tf_op jit(solution)/shard_map/ppermute | solution.py:412
  144.6 1.9 %collective-permute-start.68 = (bf16[264,128]{1,0:T(8,128)(2,1)S(1)}, bf16[264,128]{1,0:T(8,128)(2,1)S(1)}, u32[]{:S(2)}, u32[]{:S(2)}) collective-permute-start(bf16[264,128]{1,0:T(8,128)(2,1)S(1)} %get-tuple-element.182), channel_id=1, source_target_pairs={{0,14},{1,15},{2,12},{3,13},{4,10},{5,11},{6,8},{7,9},{8,6},{9,7},... | collective-permute-start | bytes 202760 | tf_op jit(solution)/shard_map/ppermute | solution.py:412
  146.5 2.9 %collective-permute-start.70 = (bf16[264,128]{1,0:T(8,128)(2,1)S(1)}, bf16[264,128]{1,0:T(8,128)(2,1)S(1)}, u32[]{:S(2)}, u32[]{:S(2)}) collective-permute-start(bf16[264,128]{1,0:T(8,128)(2,1)S(1)} %get-tuple-element.184), channel_id=1, source_target_pairs={{0,10},{1,11},{2,8},{3,9},{4,14},{5,15},{6,12},{7,13},{8,2},{9,3},... | collective-permute-start | bytes 202760 | tf_op jit(solution)/shard_map/ppermute | solution.py:412
  149.4 3.6 %collective-permute-start.72 = (bf16[264,128]{1,0:T(8,128)(2,1)S(1)}, bf16[264,128]{1,0:T(8,128)(2,1)S(1)}, u32[]{:S(2)}, u32[]{:S(2)}) collective-permute-start(bf16[264,128]{1,0:T(8,128)(2,1)S(1)} %get-tuple-element.186), channel_id=1, source_target_pairs={{0,15},{1,14},{2,13},{3,12},{4,11},{5,10},{6,9},{7,8},{8,7},{9,6},... | collective-permute-start | bytes 202760 | tf_op jit(solution)/shard_map/ppermute | solution.py:412
  153.9 1.7 collective-permute-start.74
  156.0 3.6 %collective-permute-done.73.refs_14_ = bf16[264,128]{1,0:T(8,128)(2,1)S(1)} collective-permute-done((bf16[264,128]{1,0:T(8,128)(2,1)S(1)}, bf16[264,128]{1,0:T(8,128)(2,1)S(1)}, u32[]{:S(2)}, u32[]{:S(2)}) %collective-permute-start.73) | collective-permute-done | bytes 67616 | tf_op jit(solution)/shard_map/ppermute | solution.py:412
  159.5 1.5 collective-permute-done.74.refs_15_
  161.0 2.0 %cells_last.1 = (f32[64,8192]{1,0:T(8,128)S(1)}, f32[64,128]{1,0:T(8,128)S(1)}, f32[8,128]{1,0:T(8,128)S(1)}) custom-call(s32[16,128]{1,0:T(8,128)S(1)} %get-tuple-element.116.asked_ref, bf16[264,128]{1,0:T(8,128)(2,1)S(1)} %get-tuple-element.173.refs_0_, bf16[264,128]{1,0:T(8,128)(2,1)S(1)} %collective-permute-done.60.refs_1_, ...), custom_call_target="tpu_custom_call" | custom-call | bytes 8388608 | tf_op jit(solution)/shard_map/cells_last/pallas_call | solution.py:460
  163.1 1.1 collective-permute-start.77
  164.1 3.4 %collective-permute-start.75 = (f32[8,128]{1,0:T(8,128)S(1)}, f32[8,128]{1,0:T(8,128)S(1)}, u32[]{:S(2)}, u32[]{:S(2)}) collective-permute-start(f32[8,128]{1,0:T(8,128)S(1)} %get-tuple-element.190), channel_id=1, source_target_pairs={{0,4},{1,5},{2,6},{3,7},{4,0},{5,1},{6,2},{7,3},{8,12},{9,13},{10,... | collective-permute-start | bytes 12296 | tf_op jit(solution)/shard_map/ppermute | solution.py:470
  169.8 1.2 collective-permute-start.78
  171.0 1.5 estimate.1
  172.8 1.5 model.1
  (114 shorter events, 15.8 us)
Async XLA Ops:
  6.1 9.6 %collective-permute-start = (bf16[264,128]{1,0:T(8,128)(2,1)}, bf16[264,128]{1,0:T(8,128)(2,1)S(1)}, u32[]{:S(2)}, u32[]{:S(2)}) collective-permute-start(bf16[264,128]{1,0:T(8,128)(2,1)} %get-tuple-element.100), channel_id=1, source_target_pairs={{0,12},{1,13},{2,14},{3,15},{4,8},{5,9},{6,10},{7,11},{8,4},{9,5},... | collective-permute-start | bytes 202760 | tf_op jit(solution)/shard_map/ppermute | solution.py:412
  11.1 8.5 %collective-permute-start.2 = (bf16[264,128]{1,0:T(8,128)(2,1)}, bf16[264,128]{1,0:T(8,128)(2,1)S(1)}, u32[]{:S(2)}, u32[]{:S(2)}) collective-permute-start(bf16[264,128]{1,0:T(8,128)(2,1)} %get-tuple-element.102), channel_id=1, source_target_pairs={{0,8},{1,9},{2,10},{3,11},{4,12},{5,13},{6,14},{7,15},{8,0},{9,1},... | collective-permute-start | bytes 202760 | tf_op jit(solution)/shard_map/ppermute | solution.py:412
  11.8 9.5 %collective-permute-start.3 = (bf16[264,128]{1,0:T(8,128)(2,1)}, bf16[264,128]{1,0:T(8,128)(2,1)S(1)}, u32[]{:S(2)}, u32[]{:S(2)}) collective-permute-start(bf16[264,128]{1,0:T(8,128)(2,1)} %get-tuple-element.103), channel_id=1, source_target_pairs={{0,1},{1,0},{2,3},{3,2},{4,5},{5,4},{6,7},{7,6},{8,9},{9,8},{10,11... | collective-permute-start | bytes 202760 | tf_op jit(solution)/shard_map/ppermute | solution.py:412
  11.8 11.3 %collective-permute-start.4 = (bf16[264,128]{1,0:T(8,128)(2,1)}, bf16[264,128]{1,0:T(8,128)(2,1)S(1)}, u32[]{:S(2)}, u32[]{:S(2)}) collective-permute-start(bf16[264,128]{1,0:T(8,128)(2,1)} %get-tuple-element.104), channel_id=1, source_target_pairs={{0,13},{1,12},{2,15},{3,14},{4,9},{5,8},{6,11},{7,10},{8,5},{9,4},... | collective-permute-start | bytes 202760 | tf_op jit(solution)/shard_map/ppermute | solution.py:412
  15.6 7.5 %collective-permute-start.5 = (bf16[264,128]{1,0:T(8,128)(2,1)}, bf16[264,128]{1,0:T(8,128)(2,1)S(1)}, u32[]{:S(2)}, u32[]{:S(2)}) collective-permute-start(bf16[264,128]{1,0:T(8,128)(2,1)} %get-tuple-element.105), channel_id=1, source_target_pairs={{0,5},{1,4},{2,7},{3,6},{4,1},{5,0},{6,3},{7,2},{8,13},{9,12},{10,... | collective-permute-start | bytes 202760 | tf_op jit(solution)/shard_map/ppermute | solution.py:412
  16.1 10.3 %collective-permute-start.6 = (bf16[264,128]{1,0:T(8,128)(2,1)}, bf16[264,128]{1,0:T(8,128)(2,1)S(1)}, u32[]{:S(2)}, u32[]{:S(2)}) collective-permute-start(bf16[264,128]{1,0:T(8,128)(2,1)} %get-tuple-element.106), channel_id=1, source_target_pairs={{0,9},{1,8},{2,11},{3,10},{4,13},{5,12},{6,15},{7,14},{8,1},{9,0},... | collective-permute-start | bytes 202760 | tf_op jit(solution)/shard_map/ppermute | solution.py:412
  19.7 6.8 %collective-permute-start.7 = (bf16[264,128]{1,0:T(8,128)(2,1)}, bf16[264,128]{1,0:T(8,128)(2,1)S(1)}, u32[]{:S(2)}, u32[]{:S(2)}) collective-permute-start(bf16[264,128]{1,0:T(8,128)(2,1)} %get-tuple-element.107), channel_id=1, source_target_pairs={{0,2},{1,3},{2,0},{3,1},{4,6},{5,7},{6,4},{7,5},{8,10},{9,11},{10,... | collective-permute-start | bytes 202760 | tf_op jit(solution)/shard_map/ppermute | solution.py:412
  21.3 8.4 %collective-permute-start.8 = (bf16[264,128]{1,0:T(8,128)(2,1)}, bf16[264,128]{1,0:T(8,128)(2,1)S(1)}, u32[]{:S(2)}, u32[]{:S(2)}) collective-permute-start(bf16[264,128]{1,0:T(8,128)(2,1)} %get-tuple-element.108), channel_id=1, source_target_pairs={{0,14},{1,15},{2,12},{3,13},{4,10},{5,11},{6,8},{7,9},{8,6},{9,7},... | collective-permute-start | bytes 202760 | tf_op jit(solution)/shard_map/ppermute | solution.py:412
  23.1 6.9 %collective-permute-start.9 = (bf16[264,128]{1,0:T(8,128)(2,1)}, bf16[264,128]{1,0:T(8,128)(2,1)S(1)}, u32[]{:S(2)}, u32[]{:S(2)}) collective-permute-start(bf16[264,128]{1,0:T(8,128)(2,1)} %get-tuple-element.109), channel_id=1, source_target_pairs={{0,6},{1,7},{2,4},{3,5},{4,2},{5,3},{6,0},{7,1},{8,14},{9,15},{10,... | collective-permute-start | bytes 202760 | tf_op jit(solution)/shard_map/ppermute | solution.py:412
  23.1 13.9 %collective-permute-start.10 = (bf16[264,128]{1,0:T(8,128)(2,1)}, bf16[264,128]{1,0:T(8,128)(2,1)S(1)}, u32[]{:S(2)}, u32[]{:S(2)}) collective-permute-start(bf16[264,128]{1,0:T(8,128)(2,1)} %get-tuple-element.110), channel_id=1, source_target_pairs={{0,10},{1,11},{2,8},{3,9},{4,14},{5,15},{6,12},{7,13},{8,2},{9,3},... | collective-permute-start | bytes 202760 | tf_op jit(solution)/shard_map/ppermute | solution.py:412
  26.4 10.6 %collective-permute-start.11 = (bf16[264,128]{1,0:T(8,128)(2,1)}, bf16[264,128]{1,0:T(8,128)(2,1)S(1)}, u32[]{:S(2)}, u32[]{:S(2)}) collective-permute-start(bf16[264,128]{1,0:T(8,128)(2,1)} %get-tuple-element.111), channel_id=1, source_target_pairs={{0,3},{1,2},{2,1},{3,0},{4,7},{5,6},{6,5},{7,4},{8,11},{9,10},{10,... | collective-permute-start | bytes 202760 | tf_op jit(solution)/shard_map/ppermute | solution.py:412
  26.4 10.6 %collective-permute-start.12 = (bf16[264,128]{1,0:T(8,128)(2,1)}, bf16[264,128]{1,0:T(8,128)(2,1)S(1)}, u32[]{:S(2)}, u32[]{:S(2)}) collective-permute-start(bf16[264,128]{1,0:T(8,128)(2,1)} %get-tuple-element.112), channel_id=1, source_target_pairs={{0,15},{1,14},{2,13},{3,12},{4,11},{5,10},{6,9},{7,8},{8,7},{9,6},... | collective-permute-start | bytes 202760 | tf_op jit(solution)/shard_map/ppermute | solution.py:412
  29.6 7.7 %collective-permute-start.13 = (bf16[264,128]{1,0:T(8,128)(2,1)}, bf16[264,128]{1,0:T(8,128)(2,1)S(1)}, u32[]{:S(2)}, u32[]{:S(2)}) collective-permute-start(bf16[264,128]{1,0:T(8,128)(2,1)} %get-tuple-element.113), channel_id=1, source_target_pairs={{0,7},{1,6},{2,5},{3,4},{4,3},{5,2},{6,1},{7,0},{8,15},{9,14},{10,... | collective-permute-start | bytes 202760 | tf_op jit(solution)/shard_map/ppermute | solution.py:412
  30.0 7.3 %collective-permute-start.14 = (bf16[264,128]{1,0:T(8,128)(2,1)}, bf16[264,128]{1,0:T(8,128)(2,1)S(1)}, u32[]{:S(2)}, u32[]{:S(2)}) collective-permute-start(bf16[264,128]{1,0:T(8,128)(2,1)} %get-tuple-element.114), channel_id=1, source_target_pairs={{0,11},{1,10},{2,9},{3,8},{4,15},{5,14},{6,13},{7,12},{8,3},{9,2},... | collective-permute-start | bytes 202760 | tf_op jit(solution)/shard_map/ppermute | solution.py:412
  39.8 6.9 %collective-permute-start.15 = (bf16[264,128]{1,0:T(8,128)(2,1)S(1)}, bf16[264,128]{1,0:T(8,128)(2,1)S(1)}, u32[]{:S(2)}, u32[]{:S(2)}) collective-permute-start(bf16[264,128]{1,0:T(8,128)(2,1)S(1)} %get-tuple-element.119), channel_id=1, source_target_pairs={{0,12},{1,13},{2,14},{3,15},{4,8},{5,9},{6,10},{7,11},{8,4},{9,5},... | collective-permute-start | bytes 202760 | tf_op jit(solution)/shard_map/ppermute | solution.py:412
  41.7 6.3 %collective-permute-start.16 = (bf16[264,128]{1,0:T(8,128)(2,1)S(1)}, bf16[264,128]{1,0:T(8,128)(2,1)S(1)}, u32[]{:S(2)}, u32[]{:S(2)}) collective-permute-start(bf16[264,128]{1,0:T(8,128)(2,1)S(1)} %get-tuple-element.120), channel_id=1, source_target_pairs={{0,4},{1,5},{2,6},{3,7},{4,0},{5,1},{6,2},{7,3},{8,12},{9,13},{10,... | collective-permute-start | bytes 202760 | tf_op jit(solution)/shard_map/ppermute | solution.py:412
  41.7 8.7 %collective-permute-start.17 = (bf16[264,128]{1,0:T(8,128)(2,1)S(1)}, bf16[264,128]{1,0:T(8,128)(2,1)S(1)}, u32[]{:S(2)}, u32[]{:S(2)}) collective-permute-start(bf16[264,128]{1,0:T(8,128)(2,1)S(1)} %get-tuple-element.121), channel_id=1, source_target_pairs={{0,8},{1,9},{2,10},{3,11},{4,12},{5,13},{6,14},{7,15},{8,0},{9,1},... | collective-permute-start | bytes 202760 | tf_op jit(solution)/shard_map/ppermute | solution.py:412
  44.2 9.5 %collective-permute-start.19 = (bf16[264,128]{1,0:T(8,128)(2,1)S(1)}, bf16[264,128]{1,0:T(8,128)(2,1)S(1)}, u32[]{:S(2)}, u32[]{:S(2)}) collective-permute-start(bf16[264,128]{1,0:T(8,128)(2,1)S(1)} %get-tuple-element.123), channel_id=1, source_target_pairs={{0,13},{1,12},{2,15},{3,14},{4,9},{5,8},{6,11},{7,10},{8,5},{9,4},... | collective-permute-start | bytes 202760 | tf_op jit(solution)/shard_map/ppermute | solution.py:412
  46.6 7.1 %collective-permute-start.20 = (bf16[264,128]{1,0:T(8,128)(2,1)S(1)}, bf16[264,128]{1,0:T(8,128)(2,1)S(1)}, u32[]{:S(2)}, u32[]{:S(2)}) collective-permute-start(bf16[264,128]{1,0:T(8,128)(2,1)S(1)} %get-tuple-element.124), channel_id=1, source_target_pairs={{0,5},{1,4},{2,7},{3,6},{4,1},{5,0},{6,3},{7,2},{8,13},{9,12},{10,... | collective-permute-start | bytes 202760 | tf_op jit(solution)/shard_map/ppermute | solution.py:412
  48.0 9.1 %collective-permute-start.21 = (bf16[264,128]{1,0:T(8,128)(2,1)S(1)}, bf16[264,128]{1,0:T(8,128)(2,1)S(1)}, u32[]{:S(2)}, u32[]{:S(2)}) collective-permute-start(bf16[264,128]{1,0:T(8,128)(2,1)S(1)} %get-tuple-element.125), channel_id=1, source_target_pairs={{0,9},{1,8},{2,11},{3,10},{4,13},{5,12},{6,15},{7,14},{8,1},{9,0},... | collective-permute-start | bytes 202760 | tf_op jit(solution)/shard_map/ppermute | solution.py:412
  50.4 6.8 %collective-permute-start.22 = (bf16[264,128]{1,0:T(8,128)(2,1)S(1)}, bf16[264,128]{1,0:T(8,128)(2,1)S(1)}, u32[]{:S(2)}, u32[]{:S(2)}) collective-permute-start(bf16[264,128]{1,0:T(8,128)(2,1)S(1)} %get-tuple-element.126), channel_id=1, source_target_pairs={{0,2},{1,3},{2,0},{3,1},{4,6},{5,7},{6,4},{7,5},{8,10},{9,11},{10,... | collective-permute-start | bytes 202760 | tf_op jit(solution)/shard_map/ppermute | solution.py:412
  50.4 9.8 %collective-permute-start.23 = (bf16[264,128]{1,0:T(8,128)(2,1)S(1)}, bf16[264,128]{1,0:T(8,128)(2,1)S(1)}, u32[]{:S(2)}, u32[]{:S(2)}) collective-permute-start(bf16[264,128]{1,0:T(8,128)(2,1)S(1)} %get-tuple-element.127), channel_id=1, source_target_pairs={{0,14},{1,15},{2,12},{3,13},{4,10},{5,11},{6,8},{7,9},{8,6},{9,7},... | collective-permute-start | bytes 202760 | tf_op jit(solution)/shard_map/ppermute | solution.py:412
  53.7 6.5 %collective-permute-start.24 = (bf16[264,128]{1,0:T(8,128)(2,1)S(1)}, bf16[264,128]{1,0:T(8,128)(2,1)S(1)}, u32[]{:S(2)}, u32[]{:S(2)}) collective-permute-start(bf16[264,128]{1,0:T(8,128)(2,1)S(1)} %get-tuple-element.128), channel_id=1, source_target_pairs={{0,6},{1,7},{2,4},{3,5},{4,2},{5,3},{6,0},{7,1},{8,14},{9,15},{10,... | collective-permute-start | bytes 202760 | tf_op jit(solution)/shard_map/ppermute | solution.py:412
  53.7 9.6 %collective-permute-start.25 = (bf16[264,128]{1,0:T(8,128)(2,1)S(1)}, bf16[264,128]{1,0:T(8,128)(2,1)S(1)}, u32[]{:S(2)}, u32[]{:S(2)}) collective-permute-start(bf16[264,128]{1,0:T(8,128)(2,1)S(1)} %get-tuple-element.129), channel_id=1, source_target_pairs={{0,10},{1,11},{2,8},{3,9},{4,14},{5,15},{6,12},{7,13},{8,2},{9,3},... | collective-permute-start | bytes 202760 | tf_op jit(solution)/shard_map/ppermute | solution.py:412
  57.2 7.1 %collective-permute-start.27 = (bf16[264,128]{1,0:T(8,128)(2,1)S(1)}, bf16[264,128]{1,0:T(8,128)(2,1)S(1)}, u32[]{:S(2)}, u32[]{:S(2)}) collective-permute-start(bf16[264,128]{1,0:T(8,128)(2,1)S(1)} %get-tuple-element.131), channel_id=1, source_target_pairs={{0,15},{1,14},{2,13},{3,12},{4,11},{5,10},{6,9},{7,8},{8,7},{9,6},... | collective-permute-start | bytes 202760 | tf_op jit(solution)/shard_map/ppermute | solution.py:412
  60.2 6.9 %collective-permute-start.28 = (bf16[264,128]{1,0:T(8,128)(2,1)S(1)}, bf16[264,128]{1,0:T(8,128)(2,1)S(1)}, u32[]{:S(2)}, u32[]{:S(2)}) collective-permute-start(bf16[264,128]{1,0:T(8,128)(2,1)S(1)} %get-tuple-element.132), channel_id=1, source_target_pairs={{0,7},{1,6},{2,5},{3,4},{4,3},{5,2},{6,1},{7,0},{8,15},{9,14},{10,... | collective-permute-start | bytes 202760 | tf_op jit(solution)/shard_map/ppermute | solution.py:412
  60.2 6.9 %collective-permute-start.29 = (bf16[264,128]{1,0:T(8,128)(2,1)S(1)}, bf16[264,128]{1,0:T(8,128)(2,1)S(1)}, u32[]{:S(2)}, u32[]{:S(2)}) collective-permute-start(bf16[264,128]{1,0:T(8,128)(2,1)S(1)} %get-tuple-element.133), channel_id=1, source_target_pairs={{0,11},{1,10},{2,9},{3,8},{4,15},{5,14},{6,13},{7,12},{8,3},{9,2},... | collective-permute-start | bytes 202760 | tf_op jit(solution)/shard_map/ppermute | solution.py:412
  70.5 6.5 %collective-permute-start.30 = (bf16[264,128]{1,0:T(8,128)(2,1)S(1)}, bf16[264,128]{1,0:T(8,128)(2,1)S(1)}, u32[]{:S(2)}, u32[]{:S(2)}) collective-permute-start(bf16[264,128]{1,0:T(8,128)(2,1)S(1)} %get-tuple-element.137), channel_id=1, source_target_pairs={{0,12},{1,13},{2,14},{3,15},{4,8},{5,9},{6,10},{7,11},{8,4},{9,5},... | collective-permute-start | bytes 202760 | tf_op jit(solution)/shard_map/ppermute | solution.py:412
  72.5 8.3 %collective-permute-start.32 = (bf16[264,128]{1,0:T(8,128)(2,1)S(1)}, bf16[264,128]{1,0:T(8,128)(2,1)S(1)}, u32[]{:S(2)}, u32[]{:S(2)}) collective-permute-start(bf16[264,128]{1,0:T(8,128)(2,1)S(1)} %get-tuple-element.139), channel_id=1, source_target_pairs={{0,8},{1,9},{2,10},{3,11},{4,12},{5,13},{6,14},{7,15},{8,0},{9,1},... | collective-permute-start | bytes 202760 | tf_op jit(solution)/shard_map/ppermute | solution.py:412
  75.0 7.0 %collective-permute-start.33 = (bf16[264,128]{1,0:T(8,128)(2,1)S(1)}, bf16[264,128]{1,0:T(8,128)(2,1)S(1)}, u32[]{:S(2)}, u32[]{:S(2)}) collective-permute-start(bf16[264,128]{1,0:T(8,128)(2,1)S(1)} %get-tuple-element.140), channel_id=1, source_target_pairs={{0,1},{1,0},{2,3},{3,2},{4,5},{5,4},{6,7},{7,6},{8,9},{9,8},{10,11... | collective-permute-start | bytes 202760 | tf_op jit(solution)/shard_map/ppermute | solution.py:412
  75.0 9.6 %collective-permute-start.34 = (bf16[264,128]{1,0:T(8,128)(2,1)S(1)}, bf16[264,128]{1,0:T(8,128)(2,1)S(1)}, u32[]{:S(2)}, u32[]{:S(2)}) collective-permute-start(bf16[264,128]{1,0:T(8,128)(2,1)S(1)} %get-tuple-element.141), channel_id=1, source_target_pairs={{0,13},{1,12},{2,15},{3,14},{4,9},{5,8},{6,11},{7,10},{8,5},{9,4},... | collective-permute-start | bytes 202760 | tf_op jit(solution)/shard_map/ppermute | solution.py:412
  77.1 7.5 %collective-permute-start.35 = (bf16[264,128]{1,0:T(8,128)(2,1)S(1)}, bf16[264,128]{1,0:T(8,128)(2,1)S(1)}, u32[]{:S(2)}, u32[]{:S(2)}) collective-permute-start(bf16[264,128]{1,0:T(8,128)(2,1)S(1)} %get-tuple-element.142), channel_id=1, source_target_pairs={{0,5},{1,4},{2,7},{3,6},{4,1},{5,0},{6,3},{7,2},{8,13},{9,12},{10,... | collective-permute-start | bytes 202760 | tf_op jit(solution)/shard_map/ppermute | solution.py:412
  78.8 8.9 %collective-permute-start.36 = (bf16[264,128]{1,0:T(8,128)(2,1)S(1)}, bf16[264,128]{1,0:T(8,128)(2,1)S(1)}, u32[]{:S(2)}, u32[]{:S(2)}) collective-permute-start(bf16[264,128]{1,0:T(8,128)(2,1)S(1)} %get-tuple-element.143), channel_id=1, source_target_pairs={{0,9},{1,8},{2,11},{3,10},{4,13},{5,12},{6,15},{7,14},{8,1},{9,0},... | collective-permute-start | bytes 202760 | tf_op jit(solution)/shard_map/ppermute | solution.py:412
  80.9 6.8 %collective-permute-start.37 = (bf16[264,128]{1,0:T(8,128)(2,1)S(1)}, bf16[264,128]{1,0:T(8,128)(2,1)S(1)}, u32[]{:S(2)}, u32[]{:S(2)}) collective-permute-start(bf16[264,128]{1,0:T(8,128)(2,1)S(1)} %get-tuple-element.144), channel_id=1, source_target_pairs={{0,2},{1,3},{2,0},{3,1},{4,6},{5,7},{6,4},{7,5},{8,10},{9,11},{10,... | collective-permute-start | bytes 202760 | tf_op jit(solution)/shard_map/ppermute | solution.py:412
  82.0 9.0 %collective-permute-start.38 = (bf16[264,128]{1,0:T(8,128)(2,1)S(1)}, bf16[264,128]{1,0:T(8,128)(2,1)S(1)}, u32[]{:S(2)}, u32[]{:S(2)}) collective-permute-start(bf16[264,128]{1,0:T(8,128)(2,1)S(1)} %get-tuple-element.145), channel_id=1, source_target_pairs={{0,14},{1,15},{2,12},{3,13},{4,10},{5,11},{6,8},{7,9},{8,6},{9,7},... | collective-permute-start | bytes 202760 | tf_op jit(solution)/shard_map/ppermute | solution.py:412
  84.5 7.2 %collective-permute-start.39 = (bf16[264,128]{1,0:T(8,128)(2,1)S(1)}, bf16[264,128]{1,0:T(8,128)(2,1)S(1)}, u32[]{:S(2)}, u32[]{:S(2)}) collective-permute-start(bf16[264,128]{1,0:T(8,128)(2,1)S(1)} %get-tuple-element.146), channel_id=1, source_target_pairs={{0,6},{1,7},{2,4},{3,5},{4,2},{5,3},{6,0},{7,1},{8,14},{9,15},{10,... | collective-permute-start | bytes 202760 | tf_op jit(solution)/shard_map/ppermute | solution.py:412
  84.6 9.3 %collective-permute-start.40 = (bf16[264,128]{1,0:T(8,128)(2,1)S(1)}, bf16[264,128]{1,0:T(8,128)(2,1)S(1)}, u32[]{:S(2)}, u32[]{:S(2)}) collective-permute-start(bf16[264,128]{1,0:T(8,128)(2,1)S(1)} %get-tuple-element.147), channel_id=1, source_target_pairs={{0,10},{1,11},{2,8},{3,9},{4,14},{5,15},{6,12},{7,13},{8,2},{9,3},... | collective-permute-start | bytes 202760 | tf_op jit(solution)/shard_map/ppermute | solution.py:412
  87.7 6.5 %collective-permute-start.42 = (bf16[264,128]{1,0:T(8,128)(2,1)S(1)}, bf16[264,128]{1,0:T(8,128)(2,1)S(1)}, u32[]{:S(2)}, u32[]{:S(2)}) collective-permute-start(bf16[264,128]{1,0:T(8,128)(2,1)S(1)} %get-tuple-element.149), channel_id=1, source_target_pairs={{0,15},{1,14},{2,13},{3,12},{4,11},{5,10},{6,9},{7,8},{8,7},{9,6},... | collective-permute-start | bytes 202760 | tf_op jit(solution)/shard_map/ppermute | solution.py:412
  91.7 7.4 %collective-permute-start.44 = (bf16[264,128]{1,0:T(8,128)(2,1)S(1)}, bf16[264,128]{1,0:T(8,128)(2,1)S(1)}, u32[]{:S(2)}, u32[]{:S(2)}) collective-permute-start(bf16[264,128]{1,0:T(8,128)(2,1)S(1)} %get-tuple-element.151), channel_id=1, source_target_pairs={{0,11},{1,10},{2,9},{3,8},{4,15},{5,14},{6,13},{7,12},{8,3},{9,2},... | collective-permute-start | bytes 202760 | tf_op jit(solution)/shard_map/ppermute | solution.py:412
  101.5 6.9 %collective-permute-start.45 = (bf16[264,128]{1,0:T(8,128)(2,1)S(1)}, bf16[264,128]{1,0:T(8,128)(2,1)S(1)}, u32[]{:S(2)}, u32[]{:S(2)}) collective-permute-start(bf16[264,128]{1,0:T(8,128)(2,1)S(1)} %get-tuple-element.155), channel_id=1, source_target_pairs={{0,12},{1,13},{2,14},{3,15},{4,8},{5,9},{6,10},{7,11},{8,4},{9,5},... | collective-permute-start | bytes 202760 | tf_op jit(solution)/shard_map/ppermute | solution.py:412
  102.4 8.4 %collective-permute-start.47 = (bf16[264,128]{1,0:T(8,128)(2,1)S(1)}, bf16[264,128]{1,0:T(8,128)(2,1)S(1)}, u32[]{:S(2)}, u32[]{:S(2)}) collective-permute-start(bf16[264,128]{1,0:T(8,128)(2,1)S(1)} %get-tuple-element.157), channel_id=1, source_target_pairs={{0,8},{1,9},{2,10},{3,11},{4,12},{5,13},{6,14},{7,15},{8,0},{9,1},... | collective-permute-start | bytes 202760 | tf_op jit(solution)/shard_map/ppermute | solution.py:412
  105.9 6.7 %collective-permute-start.48 = (bf16[264,128]{1,0:T(8,128)(2,1)S(1)}, bf16[264,128]{1,0:T(8,128)(2,1)S(1)}, u32[]{:S(2)}, u32[]{:S(2)}) collective-permute-start(bf16[264,128]{1,0:T(8,128)(2,1)S(1)} %get-tuple-element.158), channel_id=1, source_target_pairs={{0,1},{1,0},{2,3},{3,2},{4,5},{5,4},{6,7},{7,6},{8,9},{9,8},{10,11... | collective-permute-start | bytes 202760 | tf_op jit(solution)/shard_map/ppermute | solution.py:412
  105.9 9.4 %collective-permute-start.49 = (bf16[264,128]{1,0:T(8,128)(2,1)S(1)}, bf16[264,128]{1,0:T(8,128)(2,1)S(1)}, u32[]{:S(2)}, u32[]{:S(2)}) collective-permute-start(bf16[264,128]{1,0:T(8,128)(2,1)S(1)} %get-tuple-element.159), channel_id=1, source_target_pairs={{0,13},{1,12},{2,15},{3,14},{4,9},{5,8},{6,11},{7,10},{8,5},{9,4},... | collective-permute-start | bytes 202760 | tf_op jit(solution)/shard_map/ppermute | solution.py:412
  108.4 7.0 %collective-permute-start.50 = (bf16[264,128]{1,0:T(8,128)(2,1)S(1)}, bf16[264,128]{1,0:T(8,128)(2,1)S(1)}, u32[]{:S(2)}, u32[]{:S(2)}) collective-permute-start(bf16[264,128]{1,0:T(8,128)(2,1)S(1)} %get-tuple-element.160), channel_id=1, source_target_pairs={{0,5},{1,4},{2,7},{3,6},{4,1},{5,0},{6,3},{7,2},{8,13},{9,12},{10,... | collective-permute-start | bytes 202760 | tf_op jit(solution)/shard_map/ppermute | solution.py:412
  108.7 8.9 %collective-permute-start.51 = (bf16[264,128]{1,0:T(8,128)(2,1)S(1)}, bf16[264,128]{1,0:T(8,128)(2,1)S(1)}, u32[]{:S(2)}, u32[]{:S(2)}) collective-permute-start(bf16[264,128]{1,0:T(8,128)(2,1)S(1)} %get-tuple-element.161), channel_id=1, source_target_pairs={{0,9},{1,8},{2,11},{3,10},{4,13},{5,12},{6,15},{7,14},{8,1},{9,0},... | collective-permute-start | bytes 202760 | tf_op jit(solution)/shard_map/ppermute | solution.py:412
  110.9 6.8 %collective-permute-start.52 = (bf16[264,128]{1,0:T(8,128)(2,1)S(1)}, bf16[264,128]{1,0:T(8,128)(2,1)S(1)}, u32[]{:S(2)}, u32[]{:S(2)}) collective-permute-start(bf16[264,128]{1,0:T(8,128)(2,1)S(1)} %get-tuple-element.162), channel_id=1, source_target_pairs={{0,2},{1,3},{2,0},{3,1},{4,6},{5,7},{6,4},{7,5},{8,10},{9,11},{10,... | collective-permute-start | bytes 202760 | tf_op jit(solution)/shard_map/ppermute | solution.py:412
  112.6 9.2 %collective-permute-start.53 = (bf16[264,128]{1,0:T(8,128)(2,1)S(1)}, bf16[264,128]{1,0:T(8,128)(2,1)S(1)}, u32[]{:S(2)}, u32[]{:S(2)}) collective-permute-start(bf16[264,128]{1,0:T(8,128)(2,1)S(1)} %get-tuple-element.163), channel_id=1, source_target_pairs={{0,14},{1,15},{2,12},{3,13},{4,10},{5,11},{6,8},{7,9},{8,6},{9,7},... | collective-permute-start | bytes 202760 | tf_op jit(solution)/shard_map/ppermute | solution.py:412
  115.3 6.5 %collective-permute-start.54 = (bf16[264,128]{1,0:T(8,128)(2,1)S(1)}, bf16[264,128]{1,0:T(8,128)(2,1)S(1)}, u32[]{:S(2)}, u32[]{:S(2)}) collective-permute-start(bf16[264,128]{1,0:T(8,128)(2,1)S(1)} %get-tuple-element.164), channel_id=1, source_target_pairs={{0,6},{1,7},{2,4},{3,5},{4,2},{5,3},{6,0},{7,1},{8,14},{9,15},{10,... | collective-permute-start | bytes 202760 | tf_op jit(solution)/shard_map/ppermute | solution.py:412
  115.3 8.5 %collective-permute-start.55 = (bf16[264,128]{1,0:T(8,128)(2,1)S(1)}, bf16[264,128]{1,0:T(8,128)(2,1)S(1)}, u32[]{:S(2)}, u32[]{:S(2)}) collective-permute-start(bf16[264,128]{1,0:T(8,128)(2,1)S(1)} %get-tuple-element.165), channel_id=1, source_target_pairs={{0,10},{1,11},{2,8},{3,9},{4,14},{5,15},{6,12},{7,13},{8,2},{9,3},... | collective-permute-start | bytes 202760 | tf_op jit(solution)/shard_map/ppermute | solution.py:412
  117.7 6.6 %collective-permute-start.57 = (bf16[264,128]{1,0:T(8,128)(2,1)S(1)}, bf16[264,128]{1,0:T(8,128)(2,1)S(1)}, u32[]{:S(2)}, u32[]{:S(2)}) collective-permute-start(bf16[264,128]{1,0:T(8,128)(2,1)S(1)} %get-tuple-element.167), channel_id=1, source_target_pairs={{0,15},{1,14},{2,13},{3,12},{4,11},{5,10},{6,9},{7,8},{8,7},{9,6},... | collective-permute-start | bytes 202760 | tf_op jit(solution)/shard_map/ppermute | solution.py:412
  121.8 7.4 %collective-permute-start.59 = (bf16[264,128]{1,0:T(8,128)(2,1)S(1)}, bf16[264,128]{1,0:T(8,128)(2,1)S(1)}, u32[]{:S(2)}, u32[]{:S(2)}) collective-permute-start(bf16[264,128]{1,0:T(8,128)(2,1)S(1)} %get-tuple-element.169), channel_id=1, source_target_pairs={{0,11},{1,10},{2,9},{3,8},{4,15},{5,14},{6,13},{7,12},{8,3},{9,2},... | collective-permute-start | bytes 202760 | tf_op jit(solution)/shard_map/ppermute | solution.py:412
  132.7 6.4 %collective-permute-start.60 = (bf16[264,128]{1,0:T(8,128)(2,1)S(1)}, bf16[264,128]{1,0:T(8,128)(2,1)S(1)}, u32[]{:S(2)}, u32[]{:S(2)}) collective-permute-start(bf16[264,128]{1,0:T(8,128)(2,1)S(1)} %get-tuple-element.174), channel_id=1, source_target_pairs={{0,12},{1,13},{2,14},{3,15},{4,8},{5,9},{6,10},{7,11},{8,4},{9,5},... | collective-permute-start | bytes 202760 | tf_op jit(solution)/shard_map/ppermute | solution.py:412
  134.2 7.5 %collective-permute-start.62 = (bf16[264,128]{1,0:T(8,128)(2,1)S(1)}, bf16[264,128]{1,0:T(8,128)(2,1)S(1)}, u32[]{:S(2)}, u32[]{:S(2)}) collective-permute-start(bf16[264,128]{1,0:T(8,128)(2,1)S(1)} %get-tuple-element.176), channel_id=1, source_target_pairs={{0,8},{1,9},{2,10},{3,11},{4,12},{5,13},{6,14},{7,15},{8,0},{9,1},... | collective-permute-start | bytes 202760 | tf_op jit(solution)/shard_map/ppermute | solution.py:412
  137.2 7.5 %collective-permute-start.63 = (bf16[264,128]{1,0:T(8,128)(2,1)S(1)}, bf16[264,128]{1,0:T(8,128)(2,1)S(1)}, u32[]{:S(2)}, u32[]{:S(2)}) collective-permute-start(bf16[264,128]{1,0:T(8,128)(2,1)S(1)} %get-tuple-element.177), channel_id=1, source_target_pairs={{0,1},{1,0},{2,3},{3,2},{4,5},{5,4},{6,7},{7,6},{8,9},{9,8},{10,11... | collective-permute-start | bytes 202760 | tf_op jit(solution)/shard_map/ppermute | solution.py:412
  137.2 9.3 %collective-permute-start.64 = (bf16[264,128]{1,0:T(8,128)(2,1)S(1)}, bf16[264,128]{1,0:T(8,128)(2,1)S(1)}, u32[]{:S(2)}, u32[]{:S(2)}) collective-permute-start(bf16[264,128]{1,0:T(8,128)(2,1)S(1)} %get-tuple-element.178), channel_id=1, source_target_pairs={{0,13},{1,12},{2,15},{3,14},{4,9},{5,8},{6,11},{7,10},{8,5},{9,4},... | collective-permute-start | bytes 202760 | tf_op jit(solution)/shard_map/ppermute | solution.py:412
  139.1 7.4 %collective-permute-start.65 = (bf16[264,128]{1,0:T(8,128)(2,1)S(1)}, bf16[264,128]{1,0:T(8,128)(2,1)S(1)}, u32[]{:S(2)}, u32[]{:S(2)}) collective-permute-start(bf16[264,128]{1,0:T(8,128)(2,1)S(1)} %get-tuple-element.179), channel_id=1, source_target_pairs={{0,5},{1,4},{2,7},{3,6},{4,1},{5,0},{6,3},{7,2},{8,13},{9,12},{10,... | collective-permute-start | bytes 202760 | tf_op jit(solution)/shard_map/ppermute | solution.py:412
  139.9 9.4 %collective-permute-start.66 = (bf16[264,128]{1,0:T(8,128)(2,1)S(1)}, bf16[264,128]{1,0:T(8,128)(2,1)S(1)}, u32[]{:S(2)}, u32[]{:S(2)}) collective-permute-start(bf16[264,128]{1,0:T(8,128)(2,1)S(1)} %get-tuple-element.180), channel_id=1, source_target_pairs={{0,9},{1,8},{2,11},{3,10},{4,13},{5,12},{6,15},{7,14},{8,1},{9,0},... | collective-permute-start | bytes 202760 | tf_op jit(solution)/shard_map/ppermute | solution.py:412
  141.8 7.6 %collective-permute-start.67 = (bf16[264,128]{1,0:T(8,128)(2,1)S(1)}, bf16[264,128]{1,0:T(8,128)(2,1)S(1)}, u32[]{:S(2)}, u32[]{:S(2)}) collective-permute-start(bf16[264,128]{1,0:T(8,128)(2,1)S(1)} %get-tuple-element.181), channel_id=1, source_target_pairs={{0,2},{1,3},{2,0},{3,1},{4,6},{5,7},{6,4},{7,5},{8,10},{9,11},{10,... | collective-permute-start | bytes 202760 | tf_op jit(solution)/shard_map/ppermute | solution.py:412
  144.6 8.4 %collective-permute-start.68 = (bf16[264,128]{1,0:T(8,128)(2,1)S(1)}, bf16[264,128]{1,0:T(8,128)(2,1)S(1)}, u32[]{:S(2)}, u32[]{:S(2)}) collective-permute-start(bf16[264,128]{1,0:T(8,128)(2,1)S(1)} %get-tuple-element.182), channel_id=1, source_target_pairs={{0,14},{1,15},{2,12},{3,13},{4,10},{5,11},{6,8},{7,9},{8,6},{9,7},... | collective-permute-start | bytes 202760 | tf_op jit(solution)/shard_map/ppermute | solution.py:412
  146.5 7.4 %collective-permute-start.69 = (bf16[264,128]{1,0:T(8,128)(2,1)S(1)}, bf16[264,128]{1,0:T(8,128)(2,1)S(1)}, u32[]{:S(2)}, u32[]{:S(2)}) collective-permute-start(bf16[264,128]{1,0:T(8,128)(2,1)S(1)} %get-tuple-element.183), channel_id=1, source_target_pairs={{0,6},{1,7},{2,4},{3,5},{4,2},{5,3},{6,0},{7,1},{8,14},{9,15},{10,... | collective-permute-start | bytes 202760 | tf_op jit(solution)/shard_map/ppermute | solution.py:412
  146.5 9.1 %collective-permute-start.70 = (bf16[264,128]{1,0:T(8,128)(2,1)S(1)}, bf16[264,128]{1,0:T(8,128)(2,1)S(1)}, u32[]{:S(2)}, u32[]{:S(2)}) collective-permute-start(bf16[264,128]{1,0:T(8,128)(2,1)S(1)} %get-tuple-element.184), channel_id=1, source_target_pairs={{0,10},{1,11},{2,8},{3,9},{4,14},{5,15},{6,12},{7,13},{8,2},{9,3},... | collective-permute-start | bytes 202760 | tf_op jit(solution)/shard_map/ppermute | solution.py:412
  149.4 6.6 %collective-permute-start.72 = (bf16[264,128]{1,0:T(8,128)(2,1)S(1)}, bf16[264,128]{1,0:T(8,128)(2,1)S(1)}, u32[]{:S(2)}, u32[]{:S(2)}) collective-permute-start(bf16[264,128]{1,0:T(8,128)(2,1)S(1)} %get-tuple-element.186), channel_id=1, source_target_pairs={{0,15},{1,14},{2,13},{3,12},{4,11},{5,10},{6,9},{7,8},{8,7},{9,6},... | collective-permute-start | bytes 202760 | tf_op jit(solution)/shard_map/ppermute | solution.py:412
  153.0 6.5 %collective-permute-start.73 = (bf16[264,128]{1,0:T(8,128)(2,1)S(1)}, bf16[264,128]{1,0:T(8,128)(2,1)S(1)}, u32[]{:S(2)}, u32[]{:S(2)}) collective-permute-start(bf16[264,128]{1,0:T(8,128)(2,1)S(1)} %get-tuple-element.187), channel_id=1, source_target_pairs={{0,7},{1,6},{2,5},{3,4},{4,3},{5,2},{6,1},{7,0},{8,15},{9,14},{10,... | collective-permute-start | bytes 202760 | tf_op jit(solution)/shard_map/ppermute | solution.py:412
  153.9 7.1 %collective-permute-start.74 = (bf16[264,128]{1,0:T(8,128)(2,1)S(1)}, bf16[264,128]{1,0:T(8,128)(2,1)S(1)}, u32[]{:S(2)}, u32[]{:S(2)}) collective-permute-start(bf16[264,128]{1,0:T(8,128)(2,1)S(1)} %get-tuple-element.188), channel_id=1, source_target_pairs={{0,11},{1,10},{2,9},{3,8},{4,15},{5,14},{6,13},{7,12},{8,3},{9,2},... | collective-permute-start | bytes 202760 | tf_op jit(solution)/shard_map/ppermute | solution.py:412
  (20 other events, 126.0 us)

commit v21 on v17

--- a/solution.py
+++ b/solution.py
@@ -23,7 +23,7 @@
 
 def steps_of(peers):
     half, quarter = peers // 2, peers // 4
-    near = [step for low in range(quarter) for step in (low, quarter + low)][1:]
+    near = [step for low in range(quarter) for step in (quarter + low, low) if step]
     return [0, half] + [step for low in near for step in (low, half + low)]
 
 

time: 172 us -> 172 us (level)
  waiting for transfers between devices: 36.5 us -> 34.2 us
  starting transfers between devices: 108 us -> 110 us
    ppermute x75, waiting for transfers between devices: 33.3 us -> 30.6 us  [exchange(): lax.ppermute(value, 'pair', [(one, one ^ step) for one in range(peers)])]
  transfers between devices with their start and end apart: 81 -> 81, of which waited for: 30 -> 28; matrix products, arithmetic and copies ran while one was open for 0% -> 0% of each run, Pallas kernels for 3% -> 3%
where the time goes in v21:
time: 172 us; the launch traced here: 171 us
  starting transfers between devices  110 us (64%)
  waiting for transfers between devices  34.2 us (20%)
  Pallas kernels  25.2 us (15%)
    ppermute x75, starting transfers between devices, exchange(): lax.ppermute(value, 'pair', [(one, one ^ step) for one in range(peers)])  103 us
    ppermute x75, waiting for transfers between devices, exchange(): lax.ppermute(value, 'pair', [(one, one ^ step) for one in range(peers)])  30.6 us
    pallas_call x2, Pallas kernels, on_device(): call(functools.partial(pair_kernel, peers), 'pairs_last' if last else 'pa...  6.9 us
    ppermute x6, starting transfers between devices, on_device(): lax.ppermute(share, 'pair', [(one, one ^ step) for one in range(peers)])  6.37 us
    pallas_call x1, Pallas kernels, on_device(): call(functools.partial(start_kernel, peers), 'start', [SMEM, HBM, HBM, HB...  5.4 us
    ppermute x6, waiting for transfers between devices, on_device(): lax.ppermute(share, 'pair', [(one, one ^ step) for one in range(peers)])  3.63 us
  transfers between devices with their start and end apart: 81, of which 28 were waited for; matrix products, arithmetic and copies ran while one was open for 0% of the time, Pallas kernels for 3%

profile of v21, /device:TPU:0, one launch (start us, length us, event | category | flops | bytes accessed | tf_op | source)
XLA Modules:
  0.0 171.5 jit_solution(6450631582326592906)
XLA Ops:
  0.6 5.4 %start.1 = (bf16[264,128]{1,0:T(8,128)(2,1)}, bf16[264,128]{1,0:T(8,128)(2,1)}, bf16[264,128]{1,0:T(8,128)(2,1)}, bf16[264,128]{1,0:T(8,128)(2,1)}, bf16[264,128...) custom-call(s32[1]{0:T(128)} %bitcast.me_ref, ...), custom_call_target="tpu_custom_call" | custom-call | flops 268435456 | bytes 6291456 | tf_op jit(solution)/shard_map/start/pallas_call | solution.py:416
  6.0 4.1 %collective-permute-start = (bf16[264,128]{1,0:T(8,128)(2,1)}, bf16[264,128]{1,0:T(8,128)(2,1)S(1)}, u32[]{:S(2)}, u32[]{:S(2)}) collective-permute-start(bf16[264,128]{1,0:T(8,128)(2,1)} %get-tuple-element.100), channel_id=1, source_target_pairs={{0,8},{1,9},{2,10},{3,11},{4,12},{5,13},{6,14},{7,15},{8,0},{9,1},... | collective-permute-start | bytes 202760 | tf_op jit(solution)/shard_map/ppermute | solution.py:411
  10.1 1.6 collective-permute-start.1
  11.7 3.1 %collective-permute-start.4 = (bf16[264,128]{1,0:T(8,128)(2,1)}, bf16[264,128]{1,0:T(8,128)(2,1)S(1)}, u32[]{:S(2)}, u32[]{:S(2)}) collective-permute-start(bf16[264,128]{1,0:T(8,128)(2,1)} %get-tuple-element.104), channel_id=1, source_target_pairs={{0,13},{1,12},{2,15},{3,14},{4,9},{5,8},{6,11},{7,10},{8,5},{9,4},... | collective-permute-start | bytes 202760 | tf_op jit(solution)/shard_map/ppermute | solution.py:411
  16.3 2.3 %collective-permute-done.2.refs_3_ = bf16[264,128]{1,0:T(8,128)(2,1)S(1)} collective-permute-done((bf16[264,128]{1,0:T(8,128)(2,1)}, bf16[264,128]{1,0:T(8,128)(2,1)S(1)}, u32[]{:S(2)}, u32[]{:S(2)}) %collective-permute-start.2) | collective-permute-done | bytes 67616 | tf_op jit(solution)/shard_map/ppermute | solution.py:411
  18.5 1.7 collective-permute-start.7
  20.2 2.2 %collective-permute-start.8 = (bf16[264,128]{1,0:T(8,128)(2,1)}, bf16[264,128]{1,0:T(8,128)(2,1)S(1)}, u32[]{:S(2)}, u32[]{:S(2)}) collective-permute-start(bf16[264,128]{1,0:T(8,128)(2,1)} %get-tuple-element.108), channel_id=1, source_target_pairs={{0,14},{1,15},{2,12},{3,13},{4,10},{5,11},{6,8},{7,9},{8,6},{9,7},... | collective-permute-start | bytes 202760 | tf_op jit(solution)/shard_map/ppermute | solution.py:411
  22.5 1.4 collective-permute-start.9
  25.5 3.5 %collective-permute-start.12 = (bf16[264,128]{1,0:T(8,128)(2,1)}, bf16[264,128]{1,0:T(8,128)(2,1)S(1)}, u32[]{:S(2)}, u32[]{:S(2)}) collective-permute-start(bf16[264,128]{1,0:T(8,128)(2,1)} %get-tuple-element.112), channel_id=1, source_target_pairs={{0,15},{1,14},{2,13},{3,12},{4,11},{5,10},{6,9},{7,8},{8,7},{9,6},... | collective-permute-start | bytes 202760 | tf_op jit(solution)/shard_map/ppermute | solution.py:411
  29.0 1.6 collective-permute-start.14
  32.0 2.9 %keep.1 = (s32[128]{0:T(128)S(1)}, bf16[264,128]{1,0:T(8,128)(2,1)S(1)}, bf16[8,16,128,128]{3,2,1,0:T(8,128)(2,1)S(1)}) custom-call(s32[128]{0:T(128)S(1)} %copy-done.2, bf16[264,128]{1,0:T(8,128)(2,1)S(1)} %copy-done.1, bf16[8,16,128,128]{3,2,1,0:T(8,128)(2,1)} %rays_hbm.3), custom_call_target="tpu_custom_call" | custom-call | bytes 8388608 | tf_op jit(solution)/shard_map/keep/pallas_call | solution.py:428
  36.2 2.5 %cells_first.1 = (f32[64,8192]{1,0:T(8,128)S(1)}, f32[64,128]{1,0:T(8,128)S(1)}, bf16[264,128]{1,0:T(8,128)(2,1)S(1)}, bf16[264,128]{1,0:T(8,128)(2,1)S(1)}, bf1...) custom-call(bf16[264,128]{1,0:T(8,128)(2,1)S(1)} %get-tuple-element., ...), custom_call_target="tpu_custom_call" | custom-call | bytes 6291456 | tf_op jit(solution)/shard_map/cells_first/pallas_call | solution.py:433
  38.7 1.4 collective-permute-start.15
  40.1 2.3 %collective-permute-start.16 = (bf16[264,128]{1,0:T(8,128)(2,1)S(1)}, bf16[264,128]{1,0:T(8,128)(2,1)S(1)}, u32[]{:S(2)}, u32[]{:S(2)}) collective-permute-start(bf16[264,128]{1,0:T(8,128)(2,1)S(1)} %get-tuple-element.120), channel_id=1, source_target_pairs={{0,4},{1,5},{2,6},{3,7},{4,0},{5,1},{6,2},{7,3},{8,12},{9,13},{10,... | collective-permute-start | bytes 202760 | tf_op jit(solution)/shard_map/ppermute | solution.py:411
  43.1 1.9 %collective-permute-start.19 = (bf16[264,128]{1,0:T(8,128)(2,1)S(1)}, bf16[264,128]{1,0:T(8,128)(2,1)S(1)}, u32[]{:S(2)}, u32[]{:S(2)}) collective-permute-start(bf16[264,128]{1,0:T(8,128)(2,1)S(1)} %get-tuple-element.123), channel_id=1, source_target_pairs={{0,13},{1,12},{2,15},{3,14},{4,9},{5,8},{6,11},{7,10},{8,5},{9,4},... | collective-permute-start | bytes 202760 | tf_op jit(solution)/shard_map/ppermute | solution.py:411
  46.6 2.6 %collective-permute-done.17.refs_3_ = bf16[264,128]{1,0:T(8,128)(2,1)S(1)} collective-permute-done((bf16[264,128]{1,0:T(8,128)(2,1)S(1)}, bf16[264,128]{1,0:T(8,128)(2,1)S(1)}, u32[]{:S(2)}, u32[]{:S(2)}) %collective-permute-start.17) | collective-permute-done | bytes 67616 | tf_op jit(solution)/shard_map/ppermute | solution.py:411
  49.6 2.5 %collective-permute-start.23 = (bf16[264,128]{1,0:T(8,128)(2,1)S(1)}, bf16[264,128]{1,0:T(8,128)(2,1)S(1)}, u32[]{:S(2)}, u32[]{:S(2)}) collective-permute-start(bf16[264,128]{1,0:T(8,128)(2,1)S(1)} %get-tuple-element.127), channel_id=1, source_target_pairs={{0,14},{1,15},{2,12},{3,13},{4,10},{5,11},{6,8},{7,9},{8,6},{9,7},... | collective-permute-start | bytes 202760 | tf_op jit(solution)/shard_map/ppermute | solution.py:411
  52.3 2.7 %collective-permute-start.25 = (bf16[264,128]{1,0:T(8,128)(2,1)S(1)}, bf16[264,128]{1,0:T(8,128)(2,1)S(1)}, u32[]{:S(2)}, u32[]{:S(2)}) collective-permute-start(bf16[264,128]{1,0:T(8,128)(2,1)S(1)} %get-tuple-element.129), channel_id=1, source_target_pairs={{0,10},{1,11},{2,8},{3,9},{4,14},{5,15},{6,12},{7,13},{8,2},{9,3},... | collective-permute-start | bytes 202760 | tf_op jit(solution)/shard_map/ppermute | solution.py:411
  55.1 3.4 %collective-permute-start.27 = (bf16[264,128]{1,0:T(8,128)(2,1)S(1)}, bf16[264,128]{1,0:T(8,128)(2,1)S(1)}, u32[]{:S(2)}, u32[]{:S(2)}) collective-permute-start(bf16[264,128]{1,0:T(8,128)(2,1)S(1)} %get-tuple-element.131), channel_id=1, source_target_pairs={{0,15},{1,14},{2,13},{3,12},{4,11},{5,10},{6,9},{7,8},{8,7},{9,6},... | collective-permute-start | bytes 202760 | tf_op jit(solution)/shard_map/ppermute | solution.py:411
  59.5 2.8 %collective-permute-start.29 = (bf16[264,128]{1,0:T(8,128)(2,1)S(1)}, bf16[264,128]{1,0:T(8,128)(2,1)S(1)}, u32[]{:S(2)}, u32[]{:S(2)}) collective-permute-start(bf16[264,128]{1,0:T(8,128)(2,1)S(1)} %get-tuple-element.133), channel_id=1, source_target_pairs={{0,11},{1,10},{2,9},{3,8},{4,15},{5,14},{6,13},{7,12},{8,3},{9,2},... | collective-permute-start | bytes 202760 | tf_op jit(solution)/shard_map/ppermute | solution.py:411
  62.3 1.7 %collective-permute-done.28.refs_14_ = bf16[264,128]{1,0:T(8,128)(2,1)S(1)} collective-permute-done((bf16[264,128]{1,0:T(8,128)(2,1)S(1)}, bf16[264,128]{1,0:T(8,128)(2,1)S(1)}, u32[]{:S(2)}, u32[]{:S(2)}) %collective-permute-start.28) | collective-permute-done | bytes 67616 | tf_op jit(solution)/shard_map/ppermute | solution.py:411
  64.0 2.3 %collective-permute-done.29.refs_15_ = bf16[264,128]{1,0:T(8,128)(2,1)S(1)} collective-permute-done((bf16[264,128]{1,0:T(8,128)(2,1)S(1)}, bf16[264,128]{1,0:T(8,128)(2,1)S(1)}, u32[]{:S(2)}, u32[]{:S(2)}) %collective-permute-start.29) | collective-permute-done | bytes 67616 | tf_op jit(solution)/shard_map/ppermute | solution.py:411
  66.3 3.5 %pairs.1 = (bf16[264,128]{1,0:T(8,128)(2,1)S(1)}, bf16[264,128]{1,0:T(8,128)(2,1)S(1)}, bf16[264,128]{1,0:T(8,128)(2,1)S(1)}, bf16[264,128]{1,0:T(8,128)(2,1)S(1...) custom-call(s32[128]{0:T(128)S(1)} %get-tuple-element.117.target_ref, ...), custom_call_target="tpu_custom_call" | custom-call | flops 536870912 | bytes 8388608 | tf_op jit(solution)/shard_map/pairs/pallas_call | solution.py:444
  69.8 3.3 %collective-permute-start.30 = (bf16[264,128]{1,0:T(8,128)(2,1)S(1)}, bf16[264,128]{1,0:T(8,128)(2,1)S(1)}, u32[]{:S(2)}, u32[]{:S(2)}) collective-permute-start(bf16[264,128]{1,0:T(8,128)(2,1)S(1)} %get-tuple-element.137), channel_id=1, source_target_pairs={{0,8},{1,9},{2,10},{3,11},{4,12},{5,13},{6,14},{7,15},{8,0},{9,1},... | collective-permute-start | bytes 202760 | tf_op jit(solution)/shard_map/ppermute | solution.py:411
  73.1 1.5 collective-permute-start.32
  74.6 3.1 %collective-permute-start.34 = (bf16[264,128]{1,0:T(8,128)(2,1)S(1)}, bf16[264,128]{1,0:T(8,128)(2,1)S(1)}, u32[]{:S(2)}, u32[]{:S(2)}) collective-permute-start(bf16[264,128]{1,0:T(8,128)(2,1)S(1)} %get-tuple-element.141), channel_id=1, source_target_pairs={{0,13},{1,12},{2,15},{3,14},{4,9},{5,8},{6,11},{7,10},{8,5},{9,4},... | collective-permute-start | bytes 202760 | tf_op jit(solution)/shard_map/ppermute | solution.py:411
  77.8 1.3 collective-permute-start.36
  80.3 3.1 %collective-permute-start.38 = (bf16[264,128]{1,0:T(8,128)(2,1)S(1)}, bf16[264,128]{1,0:T(8,128)(2,1)S(1)}, u32[]{:S(2)}, u32[]{:S(2)}) collective-permute-start(bf16[264,128]{1,0:T(8,128)(2,1)S(1)} %get-tuple-element.145), channel_id=1, source_target_pairs={{0,14},{1,15},{2,12},{3,13},{4,10},{5,11},{6,8},{7,9},{8,6},{9,7},... | collective-permute-start | bytes 202760 | tf_op jit(solution)/shard_map/ppermute | solution.py:411
  86.3 3.5 %collective-permute-start.42 = (bf16[264,128]{1,0:T(8,128)(2,1)S(1)}, bf16[264,128]{1,0:T(8,128)(2,1)S(1)}, u32[]{:S(2)}, u32[]{:S(2)}) collective-permute-start(bf16[264,128]{1,0:T(8,128)(2,1)S(1)} %get-tuple-element.149), channel_id=1, source_target_pairs={{0,15},{1,14},{2,13},{3,12},{4,11},{5,10},{6,9},{7,8},{8,7},{9,6},... | collective-permute-start | bytes 202760 | tf_op jit(solution)/shard_map/ppermute | solution.py:411
  91.5 1.5 collective-permute-done.42.refs_13_
  93.0 2.1 %collective-permute-done.43.refs_14_ = bf16[264,128]{1,0:T(8,128)(2,1)S(1)} collective-permute-done((bf16[264,128]{1,0:T(8,128)(2,1)S(1)}, bf16[264,128]{1,0:T(8,128)(2,1)S(1)}, u32[]{:S(2)}, u32[]{:S(2)}) %collective-permute-start.43) | collective-permute-done | bytes 67616 | tf_op jit(solution)/shard_map/ppermute | solution.py:411
  95.1 2.1 %collective-permute-done.44.refs_15_ = bf16[264,128]{1,0:T(8,128)(2,1)S(1)} collective-permute-done((bf16[264,128]{1,0:T(8,128)(2,1)S(1)}, bf16[264,128]{1,0:T(8,128)(2,1)S(1)}, u32[]{:S(2)}, u32[]{:S(2)}) %collective-permute-start.44) | collective-permute-done | bytes 67616 | tf_op jit(solution)/shard_map/ppermute | solution.py:411
  97.2 2.4 %cells.1 = (f32[64,8192]{1,0:T(8,128)S(1)}, f32[64,128]{1,0:T(8,128)S(1)}, bf16[264,128]{1,0:T(8,128)(2,1)S(1)}, bf16[264,128]{1,0:T(8,128)(2,1)S(1)}, bf16[264,...) custom-call(s32[16,128]{1,0:T(8,128)S(1)} %get-tuple-element.116.ask, ...), custom_call_target="tpu_custom_call" | custom-call | bytes 8388608 | tf_op jit(solution)/shard_map/cells/pallas_call | solution.py:453
  99.7 2.3 %collective-permute-start.46 = (bf16[264,128]{1,0:T(8,128)(2,1)S(1)}, bf16[264,128]{1,0:T(8,128)(2,1)S(1)}, u32[]{:S(2)}, u32[]{:S(2)}) collective-permute-start(bf16[264,128]{1,0:T(8,128)(2,1)S(1)} %get-tuple-element.156), channel_id=1, source_target_pairs={{0,4},{1,5},{2,6},{3,7},{4,0},{5,1},{6,2},{7,3},{8,12},{9,13},{10,... | collective-permute-start | bytes 202760 | tf_op jit(solution)/shard_map/ppermute | solution.py:411
  102.0 2.1 %collective-permute-start.47 = (bf16[264,128]{1,0:T(8,128)(2,1)S(1)}, bf16[264,128]{1,0:T(8,128)(2,1)S(1)}, u32[]{:S(2)}, u32[]{:S(2)}) collective-permute-start(bf16[264,128]{1,0:T(8,128)(2,1)S(1)} %get-tuple-element.157), channel_id=1, source_target_pairs={{0,12},{1,13},{2,14},{3,15},{4,8},{5,9},{6,10},{7,11},{8,4},{9,5},... | collective-permute-start | bytes 202760 | tf_op jit(solution)/shard_map/ppermute | solution.py:411
  104.6 1.0 collective-permute-done.45.refs_1_
  107.4 1.1 collective-permute-done.47.refs_3_
  108.5 2.1 %collective-permute-start.52 = (bf16[264,128]{1,0:T(8,128)(2,1)S(1)}, bf16[264,128]{1,0:T(8,128)(2,1)S(1)}, u32[]{:S(2)}, u32[]{:S(2)}) collective-permute-start(bf16[264,128]{1,0:T(8,128)(2,1)S(1)} %get-tuple-element.162), channel_id=1, source_target_pairs={{0,6},{1,7},{2,4},{3,5},{4,2},{5,3},{6,0},{7,1},{8,14},{9,15},{10,... | collective-permute-start | bytes 202760 | tf_op jit(solution)/shard_map/ppermute | solution.py:411
  110.6 2.1 %collective-permute-start.53 = (bf16[264,128]{1,0:T(8,128)(2,1)S(1)}, bf16[264,128]{1,0:T(8,128)(2,1)S(1)}, u32[]{:S(2)}, u32[]{:S(2)}) collective-permute-start(bf16[264,128]{1,0:T(8,128)(2,1)S(1)} %get-tuple-element.163), channel_id=1, source_target_pairs={{0,14},{1,15},{2,12},{3,13},{4,10},{5,11},{6,8},{7,9},{8,6},{9,7},... | collective-permute-start | bytes 202760 | tf_op jit(solution)/shard_map/ppermute | solution.py:411
  113.5 1.7 collective-permute-start.55
  116.0 3.3 %collective-permute-start.57 = (bf16[264,128]{1,0:T(8,128)(2,1)S(1)}, bf16[264,128]{1,0:T(8,128)(2,1)S(1)}, u32[]{:S(2)}, u32[]{:S(2)}) collective-permute-start(bf16[264,128]{1,0:T(8,128)(2,1)S(1)} %get-tuple-element.167), channel_id=1, source_target_pairs={{0,15},{1,14},{2,13},{3,12},{4,11},{5,10},{6,9},{7,8},{8,7},{9,6},... | collective-permute-start | bytes 202760 | tf_op jit(solution)/shard_map/ppermute | solution.py:411
  119.3 4.4 %collective-permute-start.59 = (bf16[264,128]{1,0:T(8,128)(2,1)S(1)}, bf16[264,128]{1,0:T(8,128)(2,1)S(1)}, u32[]{:S(2)}, u32[]{:S(2)}) collective-permute-start(bf16[264,128]{1,0:T(8,128)(2,1)S(1)} %get-tuple-element.169), channel_id=1, source_target_pairs={{0,11},{1,10},{2,9},{3,8},{4,15},{5,14},{6,13},{7,12},{8,3},{9,2},... | collective-permute-start | bytes 202760 | tf_op jit(solution)/shard_map/ppermute | solution.py:411
  124.5 2.6 %collective-permute-done.59.refs_15_ = bf16[264,128]{1,0:T(8,128)(2,1)S(1)} collective-permute-done((bf16[264,128]{1,0:T(8,128)(2,1)S(1)}, bf16[264,128]{1,0:T(8,128)(2,1)S(1)}, u32[]{:S(2)}, u32[]{:S(2)}) %collective-permute-start.59) | collective-permute-done | bytes 67616 | tf_op jit(solution)/shard_map/ppermute | solution.py:411
  127.1 3.5 %pairs_last.1 = (bf16[264,128]{1,0:T(8,128)(2,1)S(1)}, bf16[264,128]{1,0:T(8,128)(2,1)S(1)}, bf16[264,128]{1,0:T(8,128)(2,1)S(1)}, bf16[264,128]{1,0:T(8,128)(2,...) custom-call(s32[128]{0:T(128)S(1)} %get-tuple-element.117.target_ref, ...), custom_call_target="tpu_custom_call" | custom-call | flops 536870912 | bytes 8388608 | tf_op jit(solution)/shard_map/pairs_last/pallas_call | solution.py:444
  130.8 1.8 %collective-permute-start.61 = (bf16[264,128]{1,0:T(8,128)(2,1)S(1)}, bf16[264,128]{1,0:T(8,128)(2,1)S(1)}, u32[]{:S(2)}, u32[]{:S(2)}) collective-permute-start(bf16[264,128]{1,0:T(8,128)(2,1)S(1)} %get-tuple-element.175), channel_id=1, source_target_pairs={{0,4},{1,5},{2,6},{3,7},{4,0},{5,1},{6,2},{7,3},{8,12},{9,13},{10,... | collective-permute-start | bytes 202760 | tf_op jit(solution)/shard_map/ppermute | solution.py:411
  132.6 2.4 %collective-permute-start.62 = (bf16[264,128]{1,0:T(8,128)(2,1)S(1)}, bf16[264,128]{1,0:T(8,128)(2,1)S(1)}, u32[]{:S(2)}, u32[]{:S(2)}) collective-permute-start(bf16[264,128]{1,0:T(8,128)(2,1)S(1)} %get-tuple-element.176), channel_id=1, source_target_pairs={{0,12},{1,13},{2,14},{3,15},{4,8},{5,9},{6,10},{7,11},{8,4},{9,5},... | collective-permute-start | bytes 202760 | tf_op jit(solution)/shard_map/ppermute | solution.py:411
  135.5 1.1 collective-permute-done.60.refs_1_
  136.6 1.8 %collective-permute-start.66 = (bf16[264,128]{1,0:T(8,128)(2,1)S(1)}, bf16[264,128]{1,0:T(8,128)(2,1)S(1)}, u32[]{:S(2)}, u32[]{:S(2)}) collective-permute-start(bf16[264,128]{1,0:T(8,128)(2,1)S(1)} %get-tuple-element.180), channel_id=1, source_target_pairs={{0,9},{1,8},{2,11},{3,10},{4,13},{5,12},{6,15},{7,14},{8,1},{9,0},... | collective-permute-start | bytes 202760 | tf_op jit(solution)/shard_map/ppermute | solution.py:411
  138.3 1.1 collective-permute-done.62.refs_3_
  139.4 1.5 collective-permute-start.67
  141.0 2.2 %collective-permute-start.68 = (bf16[264,128]{1,0:T(8,128)(2,1)S(1)}, bf16[264,128]{1,0:T(8,128)(2,1)S(1)}, u32[]{:S(2)}, u32[]{:S(2)}) collective-permute-start(bf16[264,128]{1,0:T(8,128)(2,1)S(1)} %get-tuple-element.182), channel_id=1, source_target_pairs={{0,14},{1,15},{2,12},{3,13},{4,10},{5,11},{6,8},{7,9},{8,6},{9,7},... | collective-permute-start | bytes 202760 | tf_op jit(solution)/shard_map/ppermute | solution.py:411
  143.1 1.1 collective-permute-start.69
  144.3 1.7 collective-permute-start.70
  146.9 2.7 %collective-permute-start.72 = (bf16[264,128]{1,0:T(8,128)(2,1)S(1)}, bf16[264,128]{1,0:T(8,128)(2,1)S(1)}, u32[]{:S(2)}, u32[]{:S(2)}) collective-permute-start(bf16[264,128]{1,0:T(8,128)(2,1)S(1)} %get-tuple-element.186), channel_id=1, source_target_pairs={{0,15},{1,14},{2,13},{3,12},{4,11},{5,10},{6,9},{7,8},{8,7},{9,6},... | collective-permute-start | bytes 202760 | tf_op jit(solution)/shard_map/ppermute | solution.py:411
  149.7 3.6 %collective-permute-start.74 = (bf16[264,128]{1,0:T(8,128)(2,1)S(1)}, bf16[264,128]{1,0:T(8,128)(2,1)S(1)}, u32[]{:S(2)}, u32[]{:S(2)}) collective-permute-start(bf16[264,128]{1,0:T(8,128)(2,1)S(1)} %get-tuple-element.188), channel_id=1, source_target_pairs={{0,11},{1,10},{2,9},{3,8},{4,15},{5,14},{6,13},{7,12},{8,3},{9,2},... | collective-permute-start | bytes 202760 | tf_op jit(solution)/shard_map/ppermute | solution.py:411
  153.6 2.6 %collective-permute-done.73.refs_14_ = bf16[264,128]{1,0:T(8,128)(2,1)S(1)} collective-permute-done((bf16[264,128]{1,0:T(8,128)(2,1)S(1)}, bf16[264,128]{1,0:T(8,128)(2,1)S(1)}, u32[]{:S(2)}, u32[]{:S(2)}) %collective-permute-start.73) | collective-permute-done | bytes 67616 | tf_op jit(solution)/shard_map/ppermute | solution.py:411
  156.2 2.0 %cells_last.1 = (f32[64,8192]{1,0:T(8,128)S(1)}, f32[64,128]{1,0:T(8,128)S(1)}, f32[8,128]{1,0:T(8,128)S(1)}) custom-call(s32[16,128]{1,0:T(8,128)S(1)} %get-tuple-element.116.asked_ref, bf16[264,128]{1,0:T(8,128)(2,1)S(1)} %get-tuple-element.173.refs_0_, bf16[264,128]{1,0:T(8,128)(2,1)S(1)} %collective-permute-done.60.refs_1_, ...), custom_call_target="tpu_custom_call" | custom-call | bytes 8388608 | tf_op jit(solution)/shard_map/cells_last/pallas_call | solution.py:459
  158.2 3.3 %collective-permute-start.77 = (f32[8,128]{1,0:T(8,128)S(1)}, f32[8,128]{1,0:T(8,128)S(1)}, u32[]{:S(2)}, u32[]{:S(2)}) collective-permute-start(f32[8,128]{1,0:T(8,128)S(1)} %get-tuple-element.190), channel_id=1, source_target_pairs={{0,12},{1,13},{2,14},{3,15},{4,8},{5,9},{6,10},{7,11},{8,4},{9,5},... | collective-permute-start | bytes 12296 | tf_op jit(solution)/shard_map/ppermute | solution.py:469
  161.5 1.1 collective-permute-start.75
  162.7 1.0 collective-permute-done.77
  163.7 2.3 %collective-permute-done.76 = f32[8,128]{1,0:T(8,128)S(1)} collective-permute-done((f32[8,128]{1,0:T(8,128)S(1)}, f32[8,128]{1,0:T(8,128)S(1)}, u32[]{:S(2)}, u32[]{:S(2)}) %collective-permute-start.76) | collective-permute-done | bytes 4128 | tf_op jit(solution)/shard_map/ppermute | solution.py:469
  166.7 1.2 collective-permute-start.78
  168.0 1.5 estimate.1
  169.8 1.5 model.1
  (114 shorter events, 23.5 us)
Async XLA Ops:
  6.0 8.8 %collective-permute-start = (bf16[264,128]{1,0:T(8,128)(2,1)}, bf16[264,128]{1,0:T(8,128)(2,1)S(1)}, u32[]{:S(2)}, u32[]{:S(2)}) collective-permute-start(bf16[264,128]{1,0:T(8,128)(2,1)} %get-tuple-element.100), channel_id=1, source_target_pairs={{0,8},{1,9},{2,10},{3,11},{4,12},{5,13},{6,14},{7,15},{8,0},{9,1},... | collective-permute-start | bytes 202760 | tf_op jit(solution)/shard_map/ppermute | solution.py:411
  11.7 6.8 %collective-permute-start.2 = (bf16[264,128]{1,0:T(8,128)(2,1)}, bf16[264,128]{1,0:T(8,128)(2,1)S(1)}, u32[]{:S(2)}, u32[]{:S(2)}) collective-permute-start(bf16[264,128]{1,0:T(8,128)(2,1)} %get-tuple-element.102), channel_id=1, source_target_pairs={{0,12},{1,13},{2,14},{3,15},{4,8},{5,9},{6,10},{7,11},{8,4},{9,5},... | collective-permute-start | bytes 202760 | tf_op jit(solution)/shard_map/ppermute | solution.py:411
  11.7 8.5 %collective-permute-start.3 = (bf16[264,128]{1,0:T(8,128)(2,1)}, bf16[264,128]{1,0:T(8,128)(2,1)S(1)}, u32[]{:S(2)}, u32[]{:S(2)}) collective-permute-start(bf16[264,128]{1,0:T(8,128)(2,1)} %get-tuple-element.103), channel_id=1, source_target_pairs={{0,5},{1,4},{2,7},{3,6},{4,1},{5,0},{6,3},{7,2},{8,13},{9,12},{10,... | collective-permute-start | bytes 202760 | tf_op jit(solution)/shard_map/ppermute | solution.py:411
  11.7 10.7 %collective-permute-start.4 = (bf16[264,128]{1,0:T(8,128)(2,1)}, bf16[264,128]{1,0:T(8,128)(2,1)S(1)}, u32[]{:S(2)}, u32[]{:S(2)}) collective-permute-start(bf16[264,128]{1,0:T(8,128)(2,1)} %get-tuple-element.104), channel_id=1, source_target_pairs={{0,13},{1,12},{2,15},{3,14},{4,9},{5,8},{6,11},{7,10},{8,5},{9,4},... | collective-permute-start | bytes 202760 | tf_op jit(solution)/shard_map/ppermute | solution.py:411
  14.8 9.0 %collective-permute-start.5 = (bf16[264,128]{1,0:T(8,128)(2,1)}, bf16[264,128]{1,0:T(8,128)(2,1)S(1)}, u32[]{:S(2)}, u32[]{:S(2)}) collective-permute-start(bf16[264,128]{1,0:T(8,128)(2,1)} %get-tuple-element.105), channel_id=1, source_target_pairs={{0,1},{1,0},{2,3},{3,2},{4,5},{5,4},{6,7},{7,6},{8,9},{9,8},{10,11... | collective-permute-start | bytes 202760 | tf_op jit(solution)/shard_map/ppermute | solution.py:411
  15.7 9.1 %collective-permute-start.6 = (bf16[264,128]{1,0:T(8,128)(2,1)}, bf16[264,128]{1,0:T(8,128)(2,1)S(1)}, u32[]{:S(2)}, u32[]{:S(2)}) collective-permute-start(bf16[264,128]{1,0:T(8,128)(2,1)} %get-tuple-element.106), channel_id=1, source_target_pairs={{0,9},{1,8},{2,11},{3,10},{4,13},{5,12},{6,15},{7,14},{8,1},{9,0},... | collective-permute-start | bytes 202760 | tf_op jit(solution)/shard_map/ppermute | solution.py:411
  18.5 6.9 %collective-permute-start.7 = (bf16[264,128]{1,0:T(8,128)(2,1)}, bf16[264,128]{1,0:T(8,128)(2,1)S(1)}, u32[]{:S(2)}, u32[]{:S(2)}) collective-permute-start(bf16[264,128]{1,0:T(8,128)(2,1)} %get-tuple-element.107), channel_id=1, source_target_pairs={{0,6},{1,7},{2,4},{3,5},{4,2},{5,3},{6,0},{7,1},{8,14},{9,15},{10,... | collective-permute-start | bytes 202760 | tf_op jit(solution)/shard_map/ppermute | solution.py:411
  20.2 8.7 %collective-permute-start.8 = (bf16[264,128]{1,0:T(8,128)(2,1)}, bf16[264,128]{1,0:T(8,128)(2,1)S(1)}, u32[]{:S(2)}, u32[]{:S(2)}) collective-permute-start(bf16[264,128]{1,0:T(8,128)(2,1)} %get-tuple-element.108), channel_id=1, source_target_pairs={{0,14},{1,15},{2,12},{3,13},{4,10},{5,11},{6,8},{7,9},{8,6},{9,7},... | collective-permute-start | bytes 202760 | tf_op jit(solution)/shard_map/ppermute | solution.py:411
  22.5 6.5 %collective-permute-start.9 = (bf16[264,128]{1,0:T(8,128)(2,1)}, bf16[264,128]{1,0:T(8,128)(2,1)S(1)}, u32[]{:S(2)}, u32[]{:S(2)}) collective-permute-start(bf16[264,128]{1,0:T(8,128)(2,1)} %get-tuple-element.109), channel_id=1, source_target_pairs={{0,2},{1,3},{2,0},{3,1},{4,6},{5,7},{6,4},{7,5},{8,10},{9,11},{10,... | collective-permute-start | bytes 202760 | tf_op jit(solution)/shard_map/ppermute | solution.py:411
  23.8 11.1 %collective-permute-start.10 = (bf16[264,128]{1,0:T(8,128)(2,1)}, bf16[264,128]{1,0:T(8,128)(2,1)S(1)}, u32[]{:S(2)}, u32[]{:S(2)}) collective-permute-start(bf16[264,128]{1,0:T(8,128)(2,1)} %get-tuple-element.110), channel_id=1, source_target_pairs={{0,10},{1,11},{2,8},{3,9},{4,14},{5,15},{6,12},{7,13},{8,2},{9,3},... | collective-permute-start | bytes 202760 | tf_op jit(solution)/shard_map/ppermute | solution.py:411
  24.8 10.2 %collective-permute-start.11 = (bf16[264,128]{1,0:T(8,128)(2,1)}, bf16[264,128]{1,0:T(8,128)(2,1)S(1)}, u32[]{:S(2)}, u32[]{:S(2)}) collective-permute-start(bf16[264,128]{1,0:T(8,128)(2,1)} %get-tuple-element.111), channel_id=1, source_target_pairs={{0,7},{1,6},{2,5},{3,4},{4,3},{5,2},{6,1},{7,0},{8,15},{9,14},{10,... | collective-permute-start | bytes 202760 | tf_op jit(solution)/shard_map/ppermute | solution.py:411
  25.5 9.5 %collective-permute-start.12 = (bf16[264,128]{1,0:T(8,128)(2,1)}, bf16[264,128]{1,0:T(8,128)(2,1)S(1)}, u32[]{:S(2)}, u32[]{:S(2)}) collective-permute-start(bf16[264,128]{1,0:T(8,128)(2,1)} %get-tuple-element.112), channel_id=1, source_target_pairs={{0,15},{1,14},{2,13},{3,12},{4,11},{5,10},{6,9},{7,8},{8,7},{9,6},... | collective-permute-start | bytes 202760 | tf_op jit(solution)/shard_map/ppermute | solution.py:411
  29.0 6.6 %collective-permute-start.13 = (bf16[264,128]{1,0:T(8,128)(2,1)}, bf16[264,128]{1,0:T(8,128)(2,1)S(1)}, u32[]{:S(2)}, u32[]{:S(2)}) collective-permute-start(bf16[264,128]{1,0:T(8,128)(2,1)} %get-tuple-element.113), channel_id=1, source_target_pairs={{0,3},{1,2},{2,1},{3,0},{4,7},{5,6},{6,5},{7,4},{8,11},{9,10},{10,... | collective-permute-start | bytes 202760 | tf_op jit(solution)/shard_map/ppermute | solution.py:411
  29.0 7.2 %collective-permute-start.14 = (bf16[264,128]{1,0:T(8,128)(2,1)}, bf16[264,128]{1,0:T(8,128)(2,1)S(1)}, u32[]{:S(2)}, u32[]{:S(2)}) collective-permute-start(bf16[264,128]{1,0:T(8,128)(2,1)} %get-tuple-element.114), channel_id=1, source_target_pairs={{0,11},{1,10},{2,9},{3,8},{4,15},{5,14},{6,13},{7,12},{8,3},{9,2},... | collective-permute-start | bytes 202760 | tf_op jit(solution)/shard_map/ppermute | solution.py:411
  38.7 7.0 %collective-permute-start.15 = (bf16[264,128]{1,0:T(8,128)(2,1)S(1)}, bf16[264,128]{1,0:T(8,128)(2,1)S(1)}, u32[]{:S(2)}, u32[]{:S(2)}) collective-permute-start(bf16[264,128]{1,0:T(8,128)(2,1)S(1)} %get-tuple-element.119), channel_id=1, source_target_pairs={{0,8},{1,9},{2,10},{3,11},{4,12},{5,13},{6,14},{7,15},{8,0},{9,1},... | collective-permute-start | bytes 202760 | tf_op jit(solution)/shard_map/ppermute | solution.py:411
  40.1 6.2 %collective-permute-start.16 = (bf16[264,128]{1,0:T(8,128)(2,1)S(1)}, bf16[264,128]{1,0:T(8,128)(2,1)S(1)}, u32[]{:S(2)}, u32[]{:S(2)}) collective-permute-start(bf16[264,128]{1,0:T(8,128)(2,1)S(1)} %get-tuple-element.120), channel_id=1, source_target_pairs={{0,4},{1,5},{2,6},{3,7},{4,0},{5,1},{6,2},{7,3},{8,12},{9,13},{10,... | collective-permute-start | bytes 202760 | tf_op jit(solution)/shard_map/ppermute | solution.py:411
  42.4 6.8 %collective-permute-start.17 = (bf16[264,128]{1,0:T(8,128)(2,1)S(1)}, bf16[264,128]{1,0:T(8,128)(2,1)S(1)}, u32[]{:S(2)}, u32[]{:S(2)}) collective-permute-start(bf16[264,128]{1,0:T(8,128)(2,1)S(1)} %get-tuple-element.121), channel_id=1, source_target_pairs={{0,12},{1,13},{2,14},{3,15},{4,8},{5,9},{6,10},{7,11},{8,4},{9,5},... | collective-permute-start | bytes 202760 | tf_op jit(solution)/shard_map/ppermute | solution.py:411
  43.1 6.5 %collective-permute-start.18 = (bf16[264,128]{1,0:T(8,128)(2,1)S(1)}, bf16[264,128]{1,0:T(8,128)(2,1)S(1)}, u32[]{:S(2)}, u32[]{:S(2)}) collective-permute-start(bf16[264,128]{1,0:T(8,128)(2,1)S(1)} %get-tuple-element.122), channel_id=1, source_target_pairs={{0,5},{1,4},{2,7},{3,6},{4,1},{5,0},{6,3},{7,2},{8,13},{9,12},{10,... | collective-permute-start | bytes 202760 | tf_op jit(solution)/shard_map/ppermute | solution.py:411
  43.1 9.0 %collective-permute-start.19 = (bf16[264,128]{1,0:T(8,128)(2,1)S(1)}, bf16[264,128]{1,0:T(8,128)(2,1)S(1)}, u32[]{:S(2)}, u32[]{:S(2)}) collective-permute-start(bf16[264,128]{1,0:T(8,128)(2,1)S(1)} %get-tuple-element.123), channel_id=1, source_target_pairs={{0,13},{1,12},{2,15},{3,14},{4,9},{5,8},{6,11},{7,10},{8,5},{9,4},... | collective-permute-start | bytes 202760 | tf_op jit(solution)/shard_map/ppermute | solution.py:411
  45.7 6.7 %collective-permute-start.20 = (bf16[264,128]{1,0:T(8,128)(2,1)S(1)}, bf16[264,128]{1,0:T(8,128)(2,1)S(1)}, u32[]{:S(2)}, u32[]{:S(2)}) collective-permute-start(bf16[264,128]{1,0:T(8,128)(2,1)S(1)} %get-tuple-element.124), channel_id=1, source_target_pairs={{0,1},{1,0},{2,3},{3,2},{4,5},{5,4},{6,7},{7,6},{8,9},{9,8},{10,11... | collective-permute-start | bytes 202760 | tf_op jit(solution)/shard_map/ppermute | solution.py:411
  46.3 8.7 %collective-permute-start.21 = (bf16[264,128]{1,0:T(8,128)(2,1)S(1)}, bf16[264,128]{1,0:T(8,128)(2,1)S(1)}, u32[]{:S(2)}, u32[]{:S(2)}) collective-permute-start(bf16[264,128]{1,0:T(8,128)(2,1)S(1)} %get-tuple-element.125), channel_id=1, source_target_pairs={{0,9},{1,8},{2,11},{3,10},{4,13},{5,12},{6,15},{7,14},{8,1},{9,0},... | collective-permute-start | bytes 202760 | tf_op jit(solution)/shard_map/ppermute | solution.py:411
  49.6 9.0 %collective-permute-start.23 = (bf16[264,128]{1,0:T(8,128)(2,1)S(1)}, bf16[264,128]{1,0:T(8,128)(2,1)S(1)}, u32[]{:S(2)}, u32[]{:S(2)}) collective-permute-start(bf16[264,128]{1,0:T(8,128)(2,1)S(1)} %get-tuple-element.127), channel_id=1, source_target_pairs={{0,14},{1,15},{2,12},{3,13},{4,10},{5,11},{6,8},{7,9},{8,6},{9,7},... | collective-permute-start | bytes 202760 | tf_op jit(solution)/shard_map/ppermute | solution.py:411
  52.1 7.4 %collective-permute-start.24 = (bf16[264,128]{1,0:T(8,128)(2,1)S(1)}, bf16[264,128]{1,0:T(8,128)(2,1)S(1)}, u32[]{:S(2)}, u32[]{:S(2)}) collective-permute-start(bf16[264,128]{1,0:T(8,128)(2,1)S(1)} %get-tuple-element.128), channel_id=1, source_target_pairs={{0,2},{1,3},{2,0},{3,1},{4,6},{5,7},{6,4},{7,5},{8,10},{9,11},{10,... | collective-permute-start | bytes 202760 | tf_op jit(solution)/shard_map/ppermute | solution.py:411
  52.3 10.0 %collective-permute-start.25 = (bf16[264,128]{1,0:T(8,128)(2,1)S(1)}, bf16[264,128]{1,0:T(8,128)(2,1)S(1)}, u32[]{:S(2)}, u32[]{:S(2)}) collective-permute-start(bf16[264,128]{1,0:T(8,128)(2,1)S(1)} %get-tuple-element.129), channel_id=1, source_target_pairs={{0,10},{1,11},{2,8},{3,9},{4,14},{5,15},{6,12},{7,13},{8,2},{9,3},... | collective-permute-start | bytes 202760 | tf_op jit(solution)/shard_map/ppermute | solution.py:411
  55.0 7.3 %collective-permute-start.26 = (bf16[264,128]{1,0:T(8,128)(2,1)S(1)}, bf16[264,128]{1,0:T(8,128)(2,1)S(1)}, u32[]{:S(2)}, u32[]{:S(2)}) collective-permute-start(bf16[264,128]{1,0:T(8,128)(2,1)S(1)} %get-tuple-element.130), channel_id=1, source_target_pairs={{0,7},{1,6},{2,5},{3,4},{4,3},{5,2},{6,1},{7,0},{8,15},{9,14},{10,... | collective-permute-start | bytes 202760 | tf_op jit(solution)/shard_map/ppermute | solution.py:411
  55.1 7.2 %collective-permute-start.27 = (bf16[264,128]{1,0:T(8,128)(2,1)S(1)}, bf16[264,128]{1,0:T(8,128)(2,1)S(1)}, u32[]{:S(2)}, u32[]{:S(2)}) collective-permute-start(bf16[264,128]{1,0:T(8,128)(2,1)S(1)} %get-tuple-element.131), channel_id=1, source_target_pairs={{0,15},{1,14},{2,13},{3,12},{4,11},{5,10},{6,9},{7,8},{8,7},{9,6},... | collective-permute-start | bytes 202760 | tf_op jit(solution)/shard_map/ppermute | solution.py:411
  59.5 6.8 %collective-permute-start.29 = (bf16[264,128]{1,0:T(8,128)(2,1)S(1)}, bf16[264,128]{1,0:T(8,128)(2,1)S(1)}, u32[]{:S(2)}, u32[]{:S(2)}) collective-permute-start(bf16[264,128]{1,0:T(8,128)(2,1)S(1)} %get-tuple-element.133), channel_id=1, source_target_pairs={{0,11},{1,10},{2,9},{3,8},{4,15},{5,14},{6,13},{7,12},{8,3},{9,2},... | collective-permute-start | bytes 202760 | tf_op jit(solution)/shard_map/ppermute | solution.py:411
  69.8 7.9 %collective-permute-start.30 = (bf16[264,128]{1,0:T(8,128)(2,1)S(1)}, bf16[264,128]{1,0:T(8,128)(2,1)S(1)}, u32[]{:S(2)}, u32[]{:S(2)}) collective-permute-start(bf16[264,128]{1,0:T(8,128)(2,1)S(1)} %get-tuple-element.137), channel_id=1, source_target_pairs={{0,8},{1,9},{2,10},{3,11},{4,12},{5,13},{6,14},{7,15},{8,0},{9,1},... | collective-permute-start | bytes 202760 | tf_op jit(solution)/shard_map/ppermute | solution.py:411
  73.1 6.3 %collective-permute-start.32 = (bf16[264,128]{1,0:T(8,128)(2,1)S(1)}, bf16[264,128]{1,0:T(8,128)(2,1)S(1)}, u32[]{:S(2)}, u32[]{:S(2)}) collective-permute-start(bf16[264,128]{1,0:T(8,128)(2,1)S(1)} %get-tuple-element.139), channel_id=1, source_target_pairs={{0,12},{1,13},{2,14},{3,15},{4,8},{5,9},{6,10},{7,11},{8,4},{9,5},... | collective-permute-start | bytes 202760 | tf_op jit(solution)/shard_map/ppermute | solution.py:411
  74.6 8.7 %collective-permute-start.34 = (bf16[264,128]{1,0:T(8,128)(2,1)S(1)}, bf16[264,128]{1,0:T(8,128)(2,1)S(1)}, u32[]{:S(2)}, u32[]{:S(2)}) collective-permute-start(bf16[264,128]{1,0:T(8,128)(2,1)S(1)} %get-tuple-element.141), channel_id=1, source_target_pairs={{0,13},{1,12},{2,15},{3,14},{4,9},{5,8},{6,11},{7,10},{8,5},{9,4},... | collective-permute-start | bytes 202760 | tf_op jit(solution)/shard_map/ppermute | solution.py:411
  77.7 6.5 %collective-permute-start.35 = (bf16[264,128]{1,0:T(8,128)(2,1)S(1)}, bf16[264,128]{1,0:T(8,128)(2,1)S(1)}, u32[]{:S(2)}, u32[]{:S(2)}) collective-permute-start(bf16[264,128]{1,0:T(8,128)(2,1)S(1)} %get-tuple-element.142), channel_id=1, source_target_pairs={{0,1},{1,0},{2,3},{3,2},{4,5},{5,4},{6,7},{7,6},{8,9},{9,8},{10,11... | collective-permute-start | bytes 202760 | tf_op jit(solution)/shard_map/ppermute | solution.py:411
  77.8 8.0 %collective-permute-start.36 = (bf16[264,128]{1,0:T(8,128)(2,1)S(1)}, bf16[264,128]{1,0:T(8,128)(2,1)S(1)}, u32[]{:S(2)}, u32[]{:S(2)}) collective-permute-start(bf16[264,128]{1,0:T(8,128)(2,1)S(1)} %get-tuple-element.143), channel_id=1, source_target_pairs={{0,9},{1,8},{2,11},{3,10},{4,13},{5,12},{6,15},{7,14},{8,1},{9,0},... | collective-permute-start | bytes 202760 | tf_op jit(solution)/shard_map/ppermute | solution.py:411
  79.4 6.9 %collective-permute-start.37 = (bf16[264,128]{1,0:T(8,128)(2,1)S(1)}, bf16[264,128]{1,0:T(8,128)(2,1)S(1)}, u32[]{:S(2)}, u32[]{:S(2)}) collective-permute-start(bf16[264,128]{1,0:T(8,128)(2,1)S(1)} %get-tuple-element.144), channel_id=1, source_target_pairs={{0,6},{1,7},{2,4},{3,5},{4,2},{5,3},{6,0},{7,1},{8,14},{9,15},{10,... | collective-permute-start | bytes 202760 | tf_op jit(solution)/shard_map/ppermute | solution.py:411
  80.3 9.6 %collective-permute-start.38 = (bf16[264,128]{1,0:T(8,128)(2,1)S(1)}, bf16[264,128]{1,0:T(8,128)(2,1)S(1)}, u32[]{:S(2)}, u32[]{:S(2)}) collective-permute-start(bf16[264,128]{1,0:T(8,128)(2,1)S(1)} %get-tuple-element.145), channel_id=1, source_target_pairs={{0,14},{1,15},{2,12},{3,13},{4,10},{5,11},{6,8},{7,9},{8,6},{9,7},... | collective-permute-start | bytes 202760 | tf_op jit(solution)/shard_map/ppermute | solution.py:411
  83.3 7.0 %collective-permute-start.39 = (bf16[264,128]{1,0:T(8,128)(2,1)S(1)}, bf16[264,128]{1,0:T(8,128)(2,1)S(1)}, u32[]{:S(2)}, u32[]{:S(2)}) collective-permute-start(bf16[264,128]{1,0:T(8,128)(2,1)S(1)} %get-tuple-element.146), channel_id=1, source_target_pairs={{0,2},{1,3},{2,0},{3,1},{4,6},{5,7},{6,4},{7,5},{8,10},{9,11},{10,... | collective-permute-start | bytes 202760 | tf_op jit(solution)/shard_map/ppermute | solution.py:411
  84.2 6.9 %collective-permute-start.40 = (bf16[264,128]{1,0:T(8,128)(2,1)S(1)}, bf16[264,128]{1,0:T(8,128)(2,1)S(1)}, u32[]{:S(2)}, u32[]{:S(2)}) collective-permute-start(bf16[264,128]{1,0:T(8,128)(2,1)S(1)} %get-tuple-element.147), channel_id=1, source_target_pairs={{0,10},{1,11},{2,8},{3,9},{4,14},{5,15},{6,12},{7,13},{8,2},{9,3},... | collective-permute-start | bytes 202760 | tf_op jit(solution)/shard_map/ppermute | solution.py:411
  86.3 6.7 %collective-permute-start.42 = (bf16[264,128]{1,0:T(8,128)(2,1)S(1)}, bf16[264,128]{1,0:T(8,128)(2,1)S(1)}, u32[]{:S(2)}, u32[]{:S(2)}) collective-permute-start(bf16[264,128]{1,0:T(8,128)(2,1)S(1)} %get-tuple-element.149), channel_id=1, source_target_pairs={{0,15},{1,14},{2,13},{3,12},{4,11},{5,10},{6,9},{7,8},{8,7},{9,6},... | collective-permute-start | bytes 202760 | tf_op jit(solution)/shard_map/ppermute | solution.py:411
  90.3 6.9 %collective-permute-start.44 = (bf16[264,128]{1,0:T(8,128)(2,1)S(1)}, bf16[264,128]{1,0:T(8,128)(2,1)S(1)}, u32[]{:S(2)}, u32[]{:S(2)}) collective-permute-start(bf16[264,128]{1,0:T(8,128)(2,1)S(1)} %get-tuple-element.151), channel_id=1, source_target_pairs={{0,11},{1,10},{2,9},{3,8},{4,15},{5,14},{6,13},{7,12},{8,3},{9,2},... | collective-permute-start | bytes 202760 | tf_op jit(solution)/shard_map/ppermute | solution.py:411
  99.7 7.2 %collective-permute-start.46 = (bf16[264,128]{1,0:T(8,128)(2,1)S(1)}, bf16[264,128]{1,0:T(8,128)(2,1)S(1)}, u32[]{:S(2)}, u32[]{:S(2)}) collective-permute-start(bf16[264,128]{1,0:T(8,128)(2,1)S(1)} %get-tuple-element.156), channel_id=1, source_target_pairs={{0,4},{1,5},{2,6},{3,7},{4,0},{5,1},{6,2},{7,3},{8,12},{9,13},{10,... | collective-permute-start | bytes 202760 | tf_op jit(solution)/shard_map/ppermute | solution.py:411
  102.0 6.6 %collective-permute-start.47 = (bf16[264,128]{1,0:T(8,128)(2,1)S(1)}, bf16[264,128]{1,0:T(8,128)(2,1)S(1)}, u32[]{:S(2)}, u32[]{:S(2)}) collective-permute-start(bf16[264,128]{1,0:T(8,128)(2,1)S(1)} %get-tuple-element.157), channel_id=1, source_target_pairs={{0,12},{1,13},{2,14},{3,15},{4,8},{5,9},{6,10},{7,11},{8,4},{9,5},... | collective-permute-start | bytes 202760 | tf_op jit(solution)/shard_map/ppermute | solution.py:411
  104.1 6.6 %collective-permute-start.48 = (bf16[264,128]{1,0:T(8,128)(2,1)S(1)}, bf16[264,128]{1,0:T(8,128)(2,1)S(1)}, u32[]{:S(2)}, u32[]{:S(2)}) collective-permute-start(bf16[264,128]{1,0:T(8,128)(2,1)S(1)} %get-tuple-element.158), channel_id=1, source_target_pairs={{0,5},{1,4},{2,7},{3,6},{4,1},{5,0},{6,3},{7,2},{8,13},{9,12},{10,... | collective-permute-start | bytes 202760 | tf_op jit(solution)/shard_map/ppermute | solution.py:411
  104.1 8.7 %collective-permute-start.49 = (bf16[264,128]{1,0:T(8,128)(2,1)S(1)}, bf16[264,128]{1,0:T(8,128)(2,1)S(1)}, u32[]{:S(2)}, u32[]{:S(2)}) collective-permute-start(bf16[264,128]{1,0:T(8,128)(2,1)S(1)} %get-tuple-element.159), channel_id=1, source_target_pairs={{0,13},{1,12},{2,15},{3,14},{4,9},{5,8},{6,11},{7,10},{8,5},{9,4},... | collective-permute-start | bytes 202760 | tf_op jit(solution)/shard_map/ppermute | solution.py:411
  105.6 7.8 %collective-permute-start.50 = (bf16[264,128]{1,0:T(8,128)(2,1)S(1)}, bf16[264,128]{1,0:T(8,128)(2,1)S(1)}, u32[]{:S(2)}, u32[]{:S(2)}) collective-permute-start(bf16[264,128]{1,0:T(8,128)(2,1)S(1)} %get-tuple-element.160), channel_id=1, source_target_pairs={{0,1},{1,0},{2,3},{3,2},{4,5},{5,4},{6,7},{7,6},{8,9},{9,8},{10,11... | collective-permute-start | bytes 202760 | tf_op jit(solution)/shard_map/ppermute | solution.py:411
  106.9 8.3 %collective-permute-start.51 = (bf16[264,128]{1,0:T(8,128)(2,1)S(1)}, bf16[264,128]{1,0:T(8,128)(2,1)S(1)}, u32[]{:S(2)}, u32[]{:S(2)}) collective-permute-start(bf16[264,128]{1,0:T(8,128)(2,1)S(1)} %get-tuple-element.161), channel_id=1, source_target_pairs={{0,9},{1,8},{2,11},{3,10},{4,13},{5,12},{6,15},{7,14},{8,1},{9,0},... | collective-permute-start | bytes 202760 | tf_op jit(solution)/shard_map/ppermute | solution.py:411
  108.5 7.5 %collective-permute-start.52 = (bf16[264,128]{1,0:T(8,128)(2,1)S(1)}, bf16[264,128]{1,0:T(8,128)(2,1)S(1)}, u32[]{:S(2)}, u32[]{:S(2)}) collective-permute-start(bf16[264,128]{1,0:T(8,128)(2,1)S(1)} %get-tuple-element.162), channel_id=1, source_target_pairs={{0,6},{1,7},{2,4},{3,5},{4,2},{5,3},{6,0},{7,1},{8,14},{9,15},{10,... | collective-permute-start | bytes 202760 | tf_op jit(solution)/shard_map/ppermute | solution.py:411
  110.6 8.6 %collective-permute-start.53 = (bf16[264,128]{1,0:T(8,128)(2,1)S(1)}, bf16[264,128]{1,0:T(8,128)(2,1)S(1)}, u32[]{:S(2)}, u32[]{:S(2)}) collective-permute-start(bf16[264,128]{1,0:T(8,128)(2,1)S(1)} %get-tuple-element.163), channel_id=1, source_target_pairs={{0,14},{1,15},{2,12},{3,13},{4,10},{5,11},{6,8},{7,9},{8,6},{9,7},... | collective-permute-start | bytes 202760 | tf_op jit(solution)/shard_map/ppermute | solution.py:411
  112.8 6.5 %collective-permute-start.54 = (bf16[264,128]{1,0:T(8,128)(2,1)S(1)}, bf16[264,128]{1,0:T(8,128)(2,1)S(1)}, u32[]{:S(2)}, u32[]{:S(2)}) collective-permute-start(bf16[264,128]{1,0:T(8,128)(2,1)S(1)} %get-tuple-element.164), channel_id=1, source_target_pairs={{0,2},{1,3},{2,0},{3,1},{4,6},{5,7},{6,4},{7,5},{8,10},{9,11},{10,... | collective-permute-start | bytes 202760 | tf_op jit(solution)/shard_map/ppermute | solution.py:411
  113.5 10.2 %collective-permute-start.55 = (bf16[264,128]{1,0:T(8,128)(2,1)S(1)}, bf16[264,128]{1,0:T(8,128)(2,1)S(1)}, u32[]{:S(2)}, u32[]{:S(2)}) collective-permute-start(bf16[264,128]{1,0:T(8,128)(2,1)S(1)} %get-tuple-element.165), channel_id=1, source_target_pairs={{0,10},{1,11},{2,8},{3,9},{4,14},{5,15},{6,12},{7,13},{8,2},{9,3},... | collective-permute-start | bytes 202760 | tf_op jit(solution)/shard_map/ppermute | solution.py:411
  115.2 8.5 %collective-permute-start.56 = (bf16[264,128]{1,0:T(8,128)(2,1)S(1)}, bf16[264,128]{1,0:T(8,128)(2,1)S(1)}, u32[]{:S(2)}, u32[]{:S(2)}) collective-permute-start(bf16[264,128]{1,0:T(8,128)(2,1)S(1)} %get-tuple-element.166), channel_id=1, source_target_pairs={{0,7},{1,6},{2,5},{3,4},{4,3},{5,2},{6,1},{7,0},{8,15},{9,14},{10,... | collective-permute-start | bytes 202760 | tf_op jit(solution)/shard_map/ppermute | solution.py:411
  116.0 7.7 %collective-permute-start.57 = (bf16[264,128]{1,0:T(8,128)(2,1)S(1)}, bf16[264,128]{1,0:T(8,128)(2,1)S(1)}, u32[]{:S(2)}, u32[]{:S(2)}) collective-permute-start(bf16[264,128]{1,0:T(8,128)(2,1)S(1)} %get-tuple-element.167), channel_id=1, source_target_pairs={{0,15},{1,14},{2,13},{3,12},{4,11},{5,10},{6,9},{7,8},{8,7},{9,6},... | collective-permute-start | bytes 202760 | tf_op jit(solution)/shard_map/ppermute | solution.py:411
  119.3 7.8 %collective-permute-start.59 = (bf16[264,128]{1,0:T(8,128)(2,1)S(1)}, bf16[264,128]{1,0:T(8,128)(2,1)S(1)}, u32[]{:S(2)}, u32[]{:S(2)}) collective-permute-start(bf16[264,128]{1,0:T(8,128)(2,1)S(1)} %get-tuple-element.169), channel_id=1, source_target_pairs={{0,11},{1,10},{2,9},{3,8},{4,15},{5,14},{6,13},{7,12},{8,3},{9,2},... | collective-permute-start | bytes 202760 | tf_op jit(solution)/shard_map/ppermute | solution.py:411
  130.5 6.0 %collective-permute-start.60 = (bf16[264,128]{1,0:T(8,128)(2,1)S(1)}, bf16[264,128]{1,0:T(8,128)(2,1)S(1)}, u32[]{:S(2)}, u32[]{:S(2)}) collective-permute-start(bf16[264,128]{1,0:T(8,128)(2,1)S(1)} %get-tuple-element.174), channel_id=1, source_target_pairs={{0,8},{1,9},{2,10},{3,11},{4,12},{5,13},{6,14},{7,15},{8,0},{9,1},... | collective-permute-start | bytes 202760 | tf_op jit(solution)/shard_map/ppermute | solution.py:411
  132.6 6.8 %collective-permute-start.62 = (bf16[264,128]{1,0:T(8,128)(2,1)S(1)}, bf16[264,128]{1,0:T(8,128)(2,1)S(1)}, u32[]{:S(2)}, u32[]{:S(2)}) collective-permute-start(bf16[264,128]{1,0:T(8,128)(2,1)S(1)} %get-tuple-element.176), channel_id=1, source_target_pairs={{0,12},{1,13},{2,14},{3,15},{4,8},{5,9},{6,10},{7,11},{8,4},{9,5},... | collective-permute-start | bytes 202760 | tf_op jit(solution)/shard_map/ppermute | solution.py:411
  135.0 8.2 %collective-permute-start.64 = (bf16[264,128]{1,0:T(8,128)(2,1)S(1)}, bf16[264,128]{1,0:T(8,128)(2,1)S(1)}, u32[]{:S(2)}, u32[]{:S(2)}) collective-permute-start(bf16[264,128]{1,0:T(8,128)(2,1)S(1)} %get-tuple-element.178), channel_id=1, source_target_pairs={{0,13},{1,12},{2,15},{3,14},{4,9},{5,8},{6,11},{7,10},{8,5},{9,4},... | collective-permute-start | bytes 202760 | tf_op jit(solution)/shard_map/ppermute | solution.py:411
  136.6 7.7 %collective-permute-start.65 = (bf16[264,128]{1,0:T(8,128)(2,1)S(1)}, bf16[264,128]{1,0:T(8,128)(2,1)S(1)}, u32[]{:S(2)}, u32[]{:S(2)}) collective-permute-start(bf16[264,128]{1,0:T(8,128)(2,1)S(1)} %get-tuple-element.179), channel_id=1, source_target_pairs={{0,1},{1,0},{2,3},{3,2},{4,5},{5,4},{6,7},{7,6},{8,9},{9,8},{10,11... | collective-permute-start | bytes 202760 | tf_op jit(solution)/shard_map/ppermute | solution.py:411
  136.6 9.4 %collective-permute-start.66 = (bf16[264,128]{1,0:T(8,128)(2,1)S(1)}, bf16[264,128]{1,0:T(8,128)(2,1)S(1)}, u32[]{:S(2)}, u32[]{:S(2)}) collective-permute-start(bf16[264,128]{1,0:T(8,128)(2,1)S(1)} %get-tuple-element.180), channel_id=1, source_target_pairs={{0,9},{1,8},{2,11},{3,10},{4,13},{5,12},{6,15},{7,14},{8,1},{9,0},... | collective-permute-start | bytes 202760 | tf_op jit(solution)/shard_map/ppermute | solution.py:411
  139.4 7.5 %collective-permute-start.67 = (bf16[264,128]{1,0:T(8,128)(2,1)S(1)}, bf16[264,128]{1,0:T(8,128)(2,1)S(1)}, u32[]{:S(2)}, u32[]{:S(2)}) collective-permute-start(bf16[264,128]{1,0:T(8,128)(2,1)S(1)} %get-tuple-element.181), channel_id=1, source_target_pairs={{0,6},{1,7},{2,4},{3,5},{4,2},{5,3},{6,0},{7,1},{8,14},{9,15},{10,... | collective-permute-start | bytes 202760 | tf_op jit(solution)/shard_map/ppermute | solution.py:411
  141.0 8.7 %collective-permute-start.68 = (bf16[264,128]{1,0:T(8,128)(2,1)S(1)}, bf16[264,128]{1,0:T(8,128)(2,1)S(1)}, u32[]{:S(2)}, u32[]{:S(2)}) collective-permute-start(bf16[264,128]{1,0:T(8,128)(2,1)S(1)} %get-tuple-element.182), channel_id=1, source_target_pairs={{0,14},{1,15},{2,12},{3,13},{4,10},{5,11},{6,8},{7,9},{8,6},{9,7},... | collective-permute-start | bytes 202760 | tf_op jit(solution)/shard_map/ppermute | solution.py:411
  143.1 6.5 %collective-permute-start.69 = (bf16[264,128]{1,0:T(8,128)(2,1)S(1)}, bf16[264,128]{1,0:T(8,128)(2,1)S(1)}, u32[]{:S(2)}, u32[]{:S(2)}) collective-permute-start(bf16[264,128]{1,0:T(8,128)(2,1)S(1)} %get-tuple-element.183), channel_id=1, source_target_pairs={{0,2},{1,3},{2,0},{3,1},{4,6},{5,7},{6,4},{7,5},{8,10},{9,11},{10,... | collective-permute-start | bytes 202760 | tf_op jit(solution)/shard_map/ppermute | solution.py:411
  144.3 9.0 %collective-permute-start.70 = (bf16[264,128]{1,0:T(8,128)(2,1)S(1)}, bf16[264,128]{1,0:T(8,128)(2,1)S(1)}, u32[]{:S(2)}, u32[]{:S(2)}) collective-permute-start(bf16[264,128]{1,0:T(8,128)(2,1)S(1)} %get-tuple-element.184), channel_id=1, source_target_pairs={{0,10},{1,11},{2,8},{3,9},{4,14},{5,15},{6,12},{7,13},{8,2},{9,3},... | collective-permute-start | bytes 202760 | tf_op jit(solution)/shard_map/ppermute | solution.py:411
  146.0 7.3 %collective-permute-start.71 = (bf16[264,128]{1,0:T(8,128)(2,1)S(1)}, bf16[264,128]{1,0:T(8,128)(2,1)S(1)}, u32[]{:S(2)}, u32[]{:S(2)}) collective-permute-start(bf16[264,128]{1,0:T(8,128)(2,1)S(1)} %get-tuple-element.185), channel_id=1, source_target_pairs={{0,7},{1,6},{2,5},{3,4},{4,3},{5,2},{6,1},{7,0},{8,15},{9,14},{10,... | collective-permute-start | bytes 202760 | tf_op jit(solution)/shard_map/ppermute | solution.py:411
  146.9 6.6 %collective-permute-start.72 = (bf16[264,128]{1,0:T(8,128)(2,1)S(1)}, bf16[264,128]{1,0:T(8,128)(2,1)S(1)}, u32[]{:S(2)}, u32[]{:S(2)}) collective-permute-start(bf16[264,128]{1,0:T(8,128)(2,1)S(1)} %get-tuple-element.186), channel_id=1, source_target_pairs={{0,15},{1,14},{2,13},{3,12},{4,11},{5,10},{6,9},{7,8},{8,7},{9,6},... | collective-permute-start | bytes 202760 | tf_op jit(solution)/shard_map/ppermute | solution.py:411
  149.7 6.5 %collective-permute-start.73 = (bf16[264,128]{1,0:T(8,128)(2,1)S(1)}, bf16[264,128]{1,0:T(8,128)(2,1)S(1)}, u32[]{:S(2)}, u32[]{:S(2)}) collective-permute-start(bf16[264,128]{1,0:T(8,128)(2,1)S(1)} %get-tuple-element.187), channel_id=1, source_target_pairs={{0,3},{1,2},{2,1},{3,0},{4,7},{5,6},{6,5},{7,4},{8,11},{9,10},{10,... | collective-permute-start | bytes 202760 | tf_op jit(solution)/shard_map/ppermute | solution.py:411
  149.7 6.5 %collective-permute-start.74 = (bf16[264,128]{1,0:T(8,128)(2,1)S(1)}, bf16[264,128]{1,0:T(8,128)(2,1)S(1)}, u32[]{:S(2)}, u32[]{:S(2)}) collective-permute-start(bf16[264,128]{1,0:T(8,128)(2,1)S(1)} %get-tuple-element.188), channel_id=1, source_target_pairs={{0,11},{1,10},{2,9},{3,8},{4,15},{5,14},{6,13},{7,12},{8,3},{9,2},... | collective-permute-start | bytes 202760 | tf_op jit(solution)/shard_map/ppermute | solution.py:411
  (20 other events, 121.7 us)

commit v22 on v21

--- a/solution.py
+++ b/solution.py
@@ -23,7 +23,8 @@
 
 def steps_of(peers):
     half, quarter = peers // 2, peers // 4
-    near = [step for low in range(quarter) for step in (quarter + low, low) if step]
+    lows = [low ^ low // 2 for low in range(quarter)]
+    near = [step for low in lows for step in (low, quarter + low)][1:]
     return [0, half] + [step for low in near for step in (low, half + low)]
 
 
@@ -244,7 +245,7 @@
         values = model_ref[:, lanes(block)]
         return squares + values * values
 
-    return lax.fori_loop(0, cells // BS, one_block, jnp.zeros((cols, BS), F32), unroll=8)
+    return lax.fori_loop(0, cells // BS, one_block, jnp.zeros((cols, BS), F32), unroll=32)
 
 
 def first_cell_kernel(peers, *refs):
@@ -270,7 +271,7 @@
         model_ref[:, lanes(block)] = before_ref[:, lanes(block)] * -scale
         return carry
 
-    lax.fori_loop(0, model_ref.shape[1] // BS, one_block, 0, unroll=8)
+    lax.fori_loop(0, model_ref.shape[1] // BS, one_block, 0, unroll=32)
 
 
 def cell_kernel(peers, asked_ref, *refs):
@@ -315,7 +316,7 @@
 
     copies = []
     for chunk in range(CHUNKS):
-        lax.fori_loop(chunk * blocks, (chunk + 1) * blocks, one_block, 0, unroll=4)
+        lax.fori_loop(chunk * blocks, (chunk + 1) * blocks, one_block, 0, unroll=True)
         where = slice(chunk * blocks * BS, (chunk + 1) * blocks * BS)
         copies.append(
             pltpu.make_async_copy(
@@ -365,7 +366,7 @@
 
     copies = []
     for chunk in range(CHUNKS):
-        lax.fori_loop(chunk * blocks, (chunk + 1) * blocks, one_block, 0, unroll=4)
+        lax.fori_loop(chunk * blocks, (chunk + 1) * blocks, one_block, 0, unroll=True)
         where = slice(chunk * blocks * BS, (chunk + 1) * blocks * BS)
         copies.append(
             pltpu.make_async_copy(out_ref.at[:, where], out_hbm.at[:, where], sems.at[chunk])

time: 172 us -> 171 us (level)
  starting transfers between devices: 110 us -> 103 us
  waiting for transfers between devices: 34.2 us -> 40.8 us
    ppermute x75, waiting for transfers between devices: 30.6 us -> 37.9 us  [exchange(): lax.ppermute(value, 'pair', [(one, one ^ step) for one in range(peers)])]
    ppermute x75, starting transfers between devices: 103 us -> 96.4 us  [exchange(): lax.ppermute(value, 'pair', [(one, one ^ step) for one in range(peers)])]
  transfers between devices with their start and end apart: 81 -> 81, of which waited for: 28 -> 31; matrix products, arithmetic and copies ran while one was open for 0% -> 0% of each run, Pallas kernels for 3% -> 3%
where the time goes in v22:
time: 171 us
  starting transfers between devices  103 us (60%)
  waiting for transfers between devices  40.8 us (24%)
  Pallas kernels  24.7 us (14%)
    ppermute x75, starting transfers between devices, exchange(): lax.ppermute(value, 'pair', [(one, one ^ step) for one in range(peers)])  96.4 us
    ppermute x75, waiting for transfers between devices, exchange(): lax.ppermute(value, 'pair', [(one, one ^ step) for one in range(peers)])  37.9 us
    pallas_call x2, Pallas kernels, on_device(): call(functools.partial(pair_kernel, peers), 'pairs_last' if last else 'pa...  6.88 us
    ppermute x6, starting transfers between devices, on_device(): lax.ppermute(share, 'pair', [(one, one ^ step) for one in range(peers)])  6.37 us
    pallas_call x1, Pallas kernels, on_device(): call(functools.partial(start_kernel, peers), 'start', [SMEM, HBM, HBM, HB...  5.39 us
  transfers between devices with their start and end apart: 81, of which 31 were waited for; matrix products, arithmetic and copies ran while one was open for 0% of the time, Pallas kernels for 3%

profile of v22, /device:TPU:0, one launch (start us, length us, event | category | flops | bytes accessed | tf_op | source)
XLA Modules:
  0.0 170.7 jit_solution(13110471559201009045)
XLA Ops:
  0.6 5.4 %start.1 = (bf16[264,128]{1,0:T(8,128)(2,1)}, bf16[264,128]{1,0:T(8,128)(2,1)}, bf16[264,128]{1,0:T(8,128)(2,1)}, bf16[264,128]{1,0:T(8,128)(2,1)}, bf16[264,128...) custom-call(s32[1]{0:T(128)} %bitcast.me_ref, ...), custom_call_target="tpu_custom_call" | custom-call | flops 268435456 | bytes 6291456 | tf_op jit(solution)/shard_map/start/pallas_call | solution.py:417
  6.0 4.1 %collective-permute-start = (bf16[264,128]{1,0:T(8,128)(2,1)}, bf16[264,128]{1,0:T(8,128)(2,1)S(1)}, u32[]{:S(2)}, u32[]{:S(2)}) collective-permute-start(bf16[264,128]{1,0:T(8,128)(2,1)} %get-tuple-element.100), channel_id=1, source_target_pairs={{0,8},{1,9},{2,10},{3,11},{4,12},{5,13},{6,14},{7,15},{8,0},{9,1},... | collective-permute-start | bytes 202760 | tf_op jit(solution)/shard_map/ppermute | solution.py:412
  10.1 1.6 collective-permute-start.1
  11.8 2.0 %collective-permute-start.4 = (bf16[264,128]{1,0:T(8,128)(2,1)}, bf16[264,128]{1,0:T(8,128)(2,1)S(1)}, u32[]{:S(2)}, u32[]{:S(2)}) collective-permute-start(bf16[264,128]{1,0:T(8,128)(2,1)} %get-tuple-element.104), channel_id=1, source_target_pairs={{0,9},{1,8},{2,11},{3,10},{4,13},{5,12},{6,15},{7,14},{8,1},{9,0},... | collective-permute-start | bytes 202760 | tf_op jit(solution)/shard_map/ppermute | solution.py:412
  13.8 2.1 %collective-permute-start.5 = (bf16[264,128]{1,0:T(8,128)(2,1)}, bf16[264,128]{1,0:T(8,128)(2,1)S(1)}, u32[]{:S(2)}, u32[]{:S(2)}) collective-permute-start(bf16[264,128]{1,0:T(8,128)(2,1)} %get-tuple-element.105), channel_id=1, source_target_pairs={{0,5},{1,4},{2,7},{3,6},{4,1},{5,0},{6,3},{7,2},{8,13},{9,12},{10,... | collective-permute-start | bytes 202760 | tf_op jit(solution)/shard_map/ppermute | solution.py:412
  15.9 1.4 collective-permute-start.6
  17.3 1.5 collective-permute-done.2.refs_3_
  19.8 2.7 %collective-permute-start.8 = (bf16[264,128]{1,0:T(8,128)(2,1)}, bf16[264,128]{1,0:T(8,128)(2,1)S(1)}, u32[]{:S(2)}, u32[]{:S(2)}) collective-permute-start(bf16[264,128]{1,0:T(8,128)(2,1)} %get-tuple-element.108), channel_id=1, source_target_pairs={{0,11},{1,10},{2,9},{3,8},{4,15},{5,14},{6,13},{7,12},{8,3},{9,2},... | collective-permute-start | bytes 202760 | tf_op jit(solution)/shard_map/ppermute | solution.py:412
  22.9 2.9 %collective-permute-start.10 = (bf16[264,128]{1,0:T(8,128)(2,1)}, bf16[264,128]{1,0:T(8,128)(2,1)S(1)}, u32[]{:S(2)}, u32[]{:S(2)}) collective-permute-start(bf16[264,128]{1,0:T(8,128)(2,1)} %get-tuple-element.110), channel_id=1, source_target_pairs={{0,15},{1,14},{2,13},{3,12},{4,11},{5,10},{6,9},{7,8},{8,7},{9,6},... | collective-permute-start | bytes 202760 | tf_op jit(solution)/shard_map/ppermute | solution.py:412
  25.8 1.3 collective-permute-start.11
  28.1 1.6 collective-permute-start.13
  29.7 2.9 %collective-permute-start.14 = (bf16[264,128]{1,0:T(8,128)(2,1)}, bf16[264,128]{1,0:T(8,128)(2,1)S(1)}, u32[]{:S(2)}, u32[]{:S(2)}) collective-permute-start(bf16[264,128]{1,0:T(8,128)(2,1)} %get-tuple-element.114), channel_id=1, source_target_pairs={{0,14},{1,15},{2,12},{3,13},{4,10},{5,11},{6,8},{7,9},{8,6},{9,7},... | collective-permute-start | bytes 202760 | tf_op jit(solution)/shard_map/ppermute | solution.py:412
  34.1 2.9 %keep.1 = (s32[128]{0:T(128)S(1)}, bf16[264,128]{1,0:T(8,128)(2,1)S(1)}, bf16[8,16,128,128]{3,2,1,0:T(8,128)(2,1)S(1)}) custom-call(s32[128]{0:T(128)S(1)} %copy-done.2, bf16[264,128]{1,0:T(8,128)(2,1)S(1)} %copy-done.1, bf16[8,16,128,128]{3,2,1,0:T(8,128)(2,1)} %rays_hbm.3), custom_call_target="tpu_custom_call" | custom-call | bytes 8388608 | tf_op jit(solution)/shard_map/keep/pallas_call | solution.py:429
  37.3 2.4 %cells_first.1 = (f32[64,8192]{1,0:T(8,128)S(1)}, f32[64,128]{1,0:T(8,128)S(1)}, bf16[264,128]{1,0:T(8,128)(2,1)S(1)}, bf16[264,128]{1,0:T(8,128)(2,1)S(1)}, bf1...) custom-call(bf16[264,128]{1,0:T(8,128)(2,1)S(1)} %get-tuple-element., ...), custom_call_target="tpu_custom_call" | custom-call | bytes 6291456 | tf_op jit(solution)/shard_map/cells_first/pallas_call | solution.py:434
  39.7 1.8 %collective-permute-start.15 = (bf16[264,128]{1,0:T(8,128)(2,1)S(1)}, bf16[264,128]{1,0:T(8,128)(2,1)S(1)}, u32[]{:S(2)}, u32[]{:S(2)}) collective-permute-start(bf16[264,128]{1,0:T(8,128)(2,1)S(1)} %get-tuple-element.119), channel_id=1, source_target_pairs={{0,8},{1,9},{2,10},{3,11},{4,12},{5,13},{6,14},{7,15},{8,0},{9,1},... | collective-permute-start | bytes 202760 | tf_op jit(solution)/shard_map/ppermute | solution.py:412
  41.5 1.3 collective-permute-start.16
  42.7 1.4 collective-permute-start.17
  45.1 1.6 collective-permute-done.15.refs_1_
  46.9 1.5 collective-permute-start.21
  49.6 1.5 collective-permute-start.23
  53.5 2.2 %collective-permute-start.25 = (bf16[264,128]{1,0:T(8,128)(2,1)S(1)}, bf16[264,128]{1,0:T(8,128)(2,1)S(1)}, u32[]{:S(2)}, u32[]{:S(2)}) collective-permute-start(bf16[264,128]{1,0:T(8,128)(2,1)S(1)} %get-tuple-element.129), channel_id=1, source_target_pairs={{0,15},{1,14},{2,13},{3,12},{4,11},{5,10},{6,9},{7,8},{8,7},{9,6},... | collective-permute-start | bytes 202760 | tf_op jit(solution)/shard_map/ppermute | solution.py:412
  57.8 2.0 %collective-permute-start.28 = (bf16[264,128]{1,0:T(8,128)(2,1)S(1)}, bf16[264,128]{1,0:T(8,128)(2,1)S(1)}, u32[]{:S(2)}, u32[]{:S(2)}) collective-permute-start(bf16[264,128]{1,0:T(8,128)(2,1)S(1)} %get-tuple-element.132), channel_id=1, source_target_pairs={{0,6},{1,7},{2,4},{3,5},{4,2},{5,3},{6,0},{7,1},{8,14},{9,15},{10,... | collective-permute-start | bytes 202760 | tf_op jit(solution)/shard_map/ppermute | solution.py:412
  59.8 2.7 %collective-permute-start.29 = (bf16[264,128]{1,0:T(8,128)(2,1)S(1)}, bf16[264,128]{1,0:T(8,128)(2,1)S(1)}, u32[]{:S(2)}, u32[]{:S(2)}) collective-permute-start(bf16[264,128]{1,0:T(8,128)(2,1)S(1)} %get-tuple-element.133), channel_id=1, source_target_pairs={{0,14},{1,15},{2,12},{3,13},{4,10},{5,11},{6,8},{7,9},{8,6},{9,7},... | collective-permute-start | bytes 202760 | tf_op jit(solution)/shard_map/ppermute | solution.py:412
  62.5 1.9 %collective-permute-done.26.refs_12_ = bf16[264,128]{1,0:T(8,128)(2,1)S(1)} collective-permute-done((bf16[264,128]{1,0:T(8,128)(2,1)S(1)}, bf16[264,128]{1,0:T(8,128)(2,1)S(1)}, u32[]{:S(2)}, u32[]{:S(2)}) %collective-permute-start.26) | collective-permute-done | bytes 67616 | tf_op jit(solution)/shard_map/ppermute | solution.py:412
  64.3 2.4 %collective-permute-done.29.refs_15_ = bf16[264,128]{1,0:T(8,128)(2,1)S(1)} collective-permute-done((bf16[264,128]{1,0:T(8,128)(2,1)S(1)}, bf16[264,128]{1,0:T(8,128)(2,1)S(1)}, u32[]{:S(2)}, u32[]{:S(2)}) %collective-permute-start.29) | collective-permute-done | bytes 67616 | tf_op jit(solution)/shard_map/ppermute | solution.py:412
  66.7 3.4 %pairs.1 = (bf16[264,128]{1,0:T(8,128)(2,1)S(1)}, bf16[264,128]{1,0:T(8,128)(2,1)S(1)}, bf16[264,128]{1,0:T(8,128)(2,1)S(1)}, bf16[264,128]{1,0:T(8,128)(2,1)S(1...) custom-call(s32[128]{0:T(128)S(1)} %get-tuple-element.117.target_ref, ...), custom_call_target="tpu_custom_call" | custom-call | flops 536870912 | bytes 8388608 | tf_op jit(solution)/shard_map/pairs/pallas_call | solution.py:445
  70.3 2.7 %collective-permute-start.31 = (bf16[264,128]{1,0:T(8,128)(2,1)S(1)}, bf16[264,128]{1,0:T(8,128)(2,1)S(1)}, u32[]{:S(2)}, u32[]{:S(2)}) collective-permute-start(bf16[264,128]{1,0:T(8,128)(2,1)S(1)} %get-tuple-element.138), channel_id=1, source_target_pairs={{0,4},{1,5},{2,6},{3,7},{4,0},{5,1},{6,2},{7,3},{8,12},{9,13},{10,... | collective-permute-start | bytes 202760 | tf_op jit(solution)/shard_map/ppermute | solution.py:412
  73.0 1.7 collective-permute-start.32
  74.7 1.9 %collective-permute-done.30.refs_1_ = bf16[264,128]{1,0:T(8,128)(2,1)S(1)} collective-permute-done((bf16[264,128]{1,0:T(8,128)(2,1)S(1)}, bf16[264,128]{1,0:T(8,128)(2,1)S(1)}, u32[]{:S(2)}, u32[]{:S(2)}) %collective-permute-start.30) | collective-permute-done | bytes 67616 | tf_op jit(solution)/shard_map/ppermute | solution.py:412
  77.1 1.8 %collective-permute-start.36 = (bf16[264,128]{1,0:T(8,128)(2,1)S(1)}, bf16[264,128]{1,0:T(8,128)(2,1)S(1)}, u32[]{:S(2)}, u32[]{:S(2)}) collective-permute-start(bf16[264,128]{1,0:T(8,128)(2,1)S(1)} %get-tuple-element.143), channel_id=1, source_target_pairs={{0,13},{1,12},{2,15},{3,14},{4,9},{5,8},{6,11},{7,10},{8,5},{9,4},... | collective-permute-start | bytes 202760 | tf_op jit(solution)/shard_map/ppermute | solution.py:412
  83.7 2.2 %collective-permute-start.40 = (bf16[264,128]{1,0:T(8,128)(2,1)S(1)}, bf16[264,128]{1,0:T(8,128)(2,1)S(1)}, u32[]{:S(2)}, u32[]{:S(2)}) collective-permute-start(bf16[264,128]{1,0:T(8,128)(2,1)S(1)} %get-tuple-element.147), channel_id=1, source_target_pairs={{0,15},{1,14},{2,13},{3,12},{4,11},{5,10},{6,9},{7,8},{8,7},{9,6},... | collective-permute-start | bytes 202760 | tf_op jit(solution)/shard_map/ppermute | solution.py:412
  88.0 2.0 %collective-permute-start.43 = (bf16[264,128]{1,0:T(8,128)(2,1)S(1)}, bf16[264,128]{1,0:T(8,128)(2,1)S(1)}, u32[]{:S(2)}, u32[]{:S(2)}) collective-permute-start(bf16[264,128]{1,0:T(8,128)(2,1)S(1)} %get-tuple-element.150), channel_id=1, source_target_pairs={{0,6},{1,7},{2,4},{3,5},{4,2},{5,3},{6,0},{7,1},{8,14},{9,15},{10,... | collective-permute-start | bytes 202760 | tf_op jit(solution)/shard_map/ppermute | solution.py:412
  90.0 2.7 %collective-permute-start.44 = (bf16[264,128]{1,0:T(8,128)(2,1)S(1)}, bf16[264,128]{1,0:T(8,128)(2,1)S(1)}, u32[]{:S(2)}, u32[]{:S(2)}) collective-permute-start(bf16[264,128]{1,0:T(8,128)(2,1)S(1)} %get-tuple-element.151), channel_id=1, source_target_pairs={{0,14},{1,15},{2,12},{3,13},{4,10},{5,11},{6,8},{7,9},{8,6},{9,7},... | collective-permute-start | bytes 202760 | tf_op jit(solution)/shard_map/ppermute | solution.py:412
  92.7 1.9 %collective-permute-done.41.refs_12_ = bf16[264,128]{1,0:T(8,128)(2,1)S(1)} collective-permute-done((bf16[264,128]{1,0:T(8,128)(2,1)S(1)}, bf16[264,128]{1,0:T(8,128)(2,1)S(1)}, u32[]{:S(2)}, u32[]{:S(2)}) %collective-permute-start.41) | collective-permute-done | bytes 67616 | tf_op jit(solution)/shard_map/ppermute | solution.py:412
  94.6 2.3 %collective-permute-done.44.refs_15_ = bf16[264,128]{1,0:T(8,128)(2,1)S(1)} collective-permute-done((bf16[264,128]{1,0:T(8,128)(2,1)S(1)}, bf16[264,128]{1,0:T(8,128)(2,1)S(1)}, u32[]{:S(2)}, u32[]{:S(2)}) %collective-permute-start.44) | collective-permute-done | bytes 67616 | tf_op jit(solution)/shard_map/ppermute | solution.py:412
  97.0 2.3 %cells.1 = (f32[64,8192]{1,0:T(8,128)S(1)}, f32[64,128]{1,0:T(8,128)S(1)}, bf16[264,128]{1,0:T(8,128)(2,1)S(1)}, bf16[264,128]{1,0:T(8,128)(2,1)S(1)}, bf16[264,...) custom-call(s32[16,128]{1,0:T(8,128)S(1)} %get-tuple-element.116.ask, ...), custom_call_target="tpu_custom_call" | custom-call | bytes 8388608 | tf_op jit(solution)/shard_map/cells/pallas_call | solution.py:454
  99.6 2.6 %collective-permute-start.46 = (bf16[264,128]{1,0:T(8,128)(2,1)S(1)}, bf16[264,128]{1,0:T(8,128)(2,1)S(1)}, u32[]{:S(2)}, u32[]{:S(2)}) collective-permute-start(bf16[264,128]{1,0:T(8,128)(2,1)S(1)} %get-tuple-element.156), channel_id=1, source_target_pairs={{0,4},{1,5},{2,6},{3,7},{4,0},{5,1},{6,2},{7,3},{8,12},{9,13},{10,... | collective-permute-start | bytes 202760 | tf_op jit(solution)/shard_map/ppermute | solution.py:412
  102.2 1.5 collective-permute-start.47
  103.8 1.9 %collective-permute-done.45.refs_1_ = bf16[264,128]{1,0:T(8,128)(2,1)S(1)} collective-permute-done((bf16[264,128]{1,0:T(8,128)(2,1)S(1)}, bf16[264,128]{1,0:T(8,128)(2,1)S(1)}, u32[]{:S(2)}, u32[]{:S(2)}) %collective-permute-start.45) | collective-permute-done | bytes 67616 | tf_op jit(solution)/shard_map/ppermute | solution.py:412
  106.4 1.6 collective-permute-start.51
  113.0 2.2 %collective-permute-start.55 = (bf16[264,128]{1,0:T(8,128)(2,1)S(1)}, bf16[264,128]{1,0:T(8,128)(2,1)S(1)}, u32[]{:S(2)}, u32[]{:S(2)}) collective-permute-start(bf16[264,128]{1,0:T(8,128)(2,1)S(1)} %get-tuple-element.165), channel_id=1, source_target_pairs={{0,15},{1,14},{2,13},{3,12},{4,11},{5,10},{6,9},{7,8},{8,7},{9,6},... | collective-permute-start | bytes 202760 | tf_op jit(solution)/shard_map/ppermute | solution.py:412
  116.1 1.2 collective-permute-start.57
  117.4 1.9 %collective-permute-start.58 = (bf16[264,128]{1,0:T(8,128)(2,1)S(1)}, bf16[264,128]{1,0:T(8,128)(2,1)S(1)}, u32[]{:S(2)}, u32[]{:S(2)}) collective-permute-start(bf16[264,128]{1,0:T(8,128)(2,1)S(1)} %get-tuple-element.168), channel_id=1, source_target_pairs={{0,6},{1,7},{2,4},{3,5},{4,2},{5,3},{6,0},{7,1},{8,14},{9,15},{10,... | collective-permute-start | bytes 202760 | tf_op jit(solution)/shard_map/ppermute | solution.py:412
  119.3 2.7 %collective-permute-start.59 = (bf16[264,128]{1,0:T(8,128)(2,1)S(1)}, bf16[264,128]{1,0:T(8,128)(2,1)S(1)}, u32[]{:S(2)}, u32[]{:S(2)}) collective-permute-start(bf16[264,128]{1,0:T(8,128)(2,1)S(1)} %get-tuple-element.169), channel_id=1, source_target_pairs={{0,14},{1,15},{2,12},{3,13},{4,10},{5,11},{6,8},{7,9},{8,6},{9,7},... | collective-permute-start | bytes 202760 | tf_op jit(solution)/shard_map/ppermute | solution.py:412
  122.0 1.8 %collective-permute-done.56.refs_12_ = bf16[264,128]{1,0:T(8,128)(2,1)S(1)} collective-permute-done((bf16[264,128]{1,0:T(8,128)(2,1)S(1)}, bf16[264,128]{1,0:T(8,128)(2,1)S(1)}, u32[]{:S(2)}, u32[]{:S(2)}) %collective-permute-start.56) | collective-permute-done | bytes 67616 | tf_op jit(solution)/shard_map/ppermute | solution.py:412
  123.8 2.5 %collective-permute-done.59.refs_15_ = bf16[264,128]{1,0:T(8,128)(2,1)S(1)} collective-permute-done((bf16[264,128]{1,0:T(8,128)(2,1)S(1)}, bf16[264,128]{1,0:T(8,128)(2,1)S(1)}, u32[]{:S(2)}, u32[]{:S(2)}) %collective-permute-start.59) | collective-permute-done | bytes 67616 | tf_op jit(solution)/shard_map/ppermute | solution.py:412
  126.3 3.4 %pairs_last.1 = (bf16[264,128]{1,0:T(8,128)(2,1)S(1)}, bf16[264,128]{1,0:T(8,128)(2,1)S(1)}, bf16[264,128]{1,0:T(8,128)(2,1)S(1)}, bf16[264,128]{1,0:T(8,128)(2,...) custom-call(s32[128]{0:T(128)S(1)} %get-tuple-element.117.target_ref, ...), custom_call_target="tpu_custom_call" | custom-call | flops 536870912 | bytes 8388608 | tf_op jit(solution)/shard_map/pairs_last/pallas_call | solution.py:445
  129.8 2.7 %collective-permute-start.61 = (bf16[264,128]{1,0:T(8,128)(2,1)S(1)}, bf16[264,128]{1,0:T(8,128)(2,1)S(1)}, u32[]{:S(2)}, u32[]{:S(2)}) collective-permute-start(bf16[264,128]{1,0:T(8,128)(2,1)S(1)} %get-tuple-element.175), channel_id=1, source_target_pairs={{0,4},{1,5},{2,6},{3,7},{4,0},{5,1},{6,2},{7,3},{8,12},{9,13},{10,... | collective-permute-start | bytes 202760 | tf_op jit(solution)/shard_map/ppermute | solution.py:412
  132.5 1.7 collective-permute-start.62
  134.2 1.9 %collective-permute-done.60.refs_1_ = bf16[264,128]{1,0:T(8,128)(2,1)S(1)} collective-permute-done((bf16[264,128]{1,0:T(8,128)(2,1)S(1)}, bf16[264,128]{1,0:T(8,128)(2,1)S(1)}, u32[]{:S(2)}, u32[]{:S(2)}) %collective-permute-start.60) | collective-permute-done | bytes 67616 | tf_op jit(solution)/shard_map/ppermute | solution.py:412
  136.6 1.8 %collective-permute-start.66 = (bf16[264,128]{1,0:T(8,128)(2,1)S(1)}, bf16[264,128]{1,0:T(8,128)(2,1)S(1)}, u32[]{:S(2)}, u32[]{:S(2)}) collective-permute-start(bf16[264,128]{1,0:T(8,128)(2,1)S(1)} %get-tuple-element.180), channel_id=1, source_target_pairs={{0,13},{1,12},{2,15},{3,14},{4,9},{5,8},{6,11},{7,10},{8,5},{9,4},... | collective-permute-start | bytes 202760 | tf_op jit(solution)/shard_map/ppermute | solution.py:412
  139.2 1.2 collective-permute-start.68
  143.2 2.2 %collective-permute-start.70 = (bf16[264,128]{1,0:T(8,128)(2,1)S(1)}, bf16[264,128]{1,0:T(8,128)(2,1)S(1)}, u32[]{:S(2)}, u32[]{:S(2)}) collective-permute-start(bf16[264,128]{1,0:T(8,128)(2,1)S(1)} %get-tuple-element.184), channel_id=1, source_target_pairs={{0,15},{1,14},{2,13},{3,12},{4,11},{5,10},{6,9},{7,8},{8,7},{9,6},... | collective-permute-start | bytes 202760 | tf_op jit(solution)/shard_map/ppermute | solution.py:412
  146.6 1.3 collective-permute-start.72
  147.8 1.7 collective-permute-start.73
  149.5 2.7 %collective-permute-start.74 = (bf16[264,128]{1,0:T(8,128)(2,1)S(1)}, bf16[264,128]{1,0:T(8,128)(2,1)S(1)}, u32[]{:S(2)}, u32[]{:S(2)}) collective-permute-start(bf16[264,128]{1,0:T(8,128)(2,1)S(1)} %get-tuple-element.188), channel_id=1, source_target_pairs={{0,14},{1,15},{2,12},{3,13},{4,10},{5,11},{6,8},{7,9},{8,6},{9,7},... | collective-permute-start | bytes 202760 | tf_op jit(solution)/shard_map/ppermute | solution.py:412
  152.2 1.9 %collective-permute-done.71.refs_12_ = bf16[264,128]{1,0:T(8,128)(2,1)S(1)} collective-permute-done((bf16[264,128]{1,0:T(8,128)(2,1)S(1)}, bf16[264,128]{1,0:T(8,128)(2,1)S(1)}, u32[]{:S(2)}, u32[]{:S(2)}) %collective-permute-start.71) | collective-permute-done | bytes 67616 | tf_op jit(solution)/shard_map/ppermute | solution.py:412
  154.1 2.4 %collective-permute-done.74.refs_15_ = bf16[264,128]{1,0:T(8,128)(2,1)S(1)} collective-permute-done((bf16[264,128]{1,0:T(8,128)(2,1)S(1)}, bf16[264,128]{1,0:T(8,128)(2,1)S(1)}, u32[]{:S(2)}, u32[]{:S(2)}) %collective-permute-start.74) | collective-permute-done | bytes 67616 | tf_op jit(solution)/shard_map/ppermute | solution.py:412
  156.5 1.9 %cells_last.1 = (f32[64,8192]{1,0:T(8,128)S(1)}, f32[64,128]{1,0:T(8,128)S(1)}, f32[8,128]{1,0:T(8,128)S(1)}) custom-call(s32[16,128]{1,0:T(8,128)S(1)} %get-tuple-element.116.asked_ref, bf16[264,128]{1,0:T(8,128)(2,1)S(1)} %get-tuple-element.173.refs_0_, bf16[264,128]{1,0:T(8,128)(2,1)S(1)} %collective-permute-done.60.refs_1_, ...), custom_call_target="tpu_custom_call" | custom-call | bytes 8388608 | tf_op jit(solution)/shard_map/cells_last/pallas_call | solution.py:460
  158.4 2.4 %collective-permute-start.77 = (f32[8,128]{1,0:T(8,128)S(1)}, f32[8,128]{1,0:T(8,128)S(1)}, u32[]{:S(2)}, u32[]{:S(2)}) collective-permute-start(f32[8,128]{1,0:T(8,128)S(1)} %get-tuple-element.190), channel_id=1, source_target_pairs={{0,12},{1,13},{2,14},{3,15},{4,8},{5,9},{6,10},{7,11},{8,4},{9,5},... | collective-permute-start | bytes 12296 | tf_op jit(solution)/shard_map/ppermute | solution.py:470
  160.8 2.0 %collective-permute-start.75 = (f32[8,128]{1,0:T(8,128)S(1)}, f32[8,128]{1,0:T(8,128)S(1)}, u32[]{:S(2)}, u32[]{:S(2)}) collective-permute-start(f32[8,128]{1,0:T(8,128)S(1)} %get-tuple-element.190), channel_id=1, source_target_pairs={{0,4},{1,5},{2,6},{3,7},{4,0},{5,1},{6,2},{7,3},{8,12},{9,13},{10,... | collective-permute-start | bytes 12296 | tf_op jit(solution)/shard_map/ppermute | solution.py:470
  163.8 1.5 collective-permute-done.76
  167.2 1.5 estimate.1
  169.1 1.5 model.1
  (114 shorter events, 34.4 us)
Async XLA Ops:
  6.0 7.7 %collective-permute-start = (bf16[264,128]{1,0:T(8,128)(2,1)}, bf16[264,128]{1,0:T(8,128)(2,1)S(1)}, u32[]{:S(2)}, u32[]{:S(2)}) collective-permute-start(bf16[264,128]{1,0:T(8,128)(2,1)} %get-tuple-element.100), channel_id=1, source_target_pairs={{0,8},{1,9},{2,10},{3,11},{4,12},{5,13},{6,14},{7,15},{8,0},{9,1},... | collective-permute-start | bytes 202760 | tf_op jit(solution)/shard_map/ppermute | solution.py:412
  11.8 7.1 %collective-permute-start.2 = (bf16[264,128]{1,0:T(8,128)(2,1)}, bf16[264,128]{1,0:T(8,128)(2,1)S(1)}, u32[]{:S(2)}, u32[]{:S(2)}) collective-permute-start(bf16[264,128]{1,0:T(8,128)(2,1)} %get-tuple-element.102), channel_id=1, source_target_pairs={{0,12},{1,13},{2,14},{3,15},{4,8},{5,9},{6,10},{7,11},{8,4},{9,5},... | collective-permute-start | bytes 202760 | tf_op jit(solution)/shard_map/ppermute | solution.py:412
  11.8 8.1 %collective-permute-start.3 = (bf16[264,128]{1,0:T(8,128)(2,1)}, bf16[264,128]{1,0:T(8,128)(2,1)S(1)}, u32[]{:S(2)}, u32[]{:S(2)}) collective-permute-start(bf16[264,128]{1,0:T(8,128)(2,1)} %get-tuple-element.103), channel_id=1, source_target_pairs={{0,1},{1,0},{2,3},{3,2},{4,5},{5,4},{6,7},{7,6},{8,9},{9,8},{10,11... | collective-permute-start | bytes 202760 | tf_op jit(solution)/shard_map/ppermute | solution.py:412
  11.8 10.8 %collective-permute-start.4 = (bf16[264,128]{1,0:T(8,128)(2,1)}, bf16[264,128]{1,0:T(8,128)(2,1)S(1)}, u32[]{:S(2)}, u32[]{:S(2)}) collective-permute-start(bf16[264,128]{1,0:T(8,128)(2,1)} %get-tuple-element.104), channel_id=1, source_target_pairs={{0,9},{1,8},{2,11},{3,10},{4,13},{5,12},{6,15},{7,14},{8,1},{9,0},... | collective-permute-start | bytes 202760 | tf_op jit(solution)/shard_map/ppermute | solution.py:412
  13.8 9.2 %collective-permute-start.5 = (bf16[264,128]{1,0:T(8,128)(2,1)}, bf16[264,128]{1,0:T(8,128)(2,1)S(1)}, u32[]{:S(2)}, u32[]{:S(2)}) collective-permute-start(bf16[264,128]{1,0:T(8,128)(2,1)} %get-tuple-element.105), channel_id=1, source_target_pairs={{0,5},{1,4},{2,7},{3,6},{4,1},{5,0},{6,3},{7,2},{8,13},{9,12},{10,... | collective-permute-start | bytes 202760 | tf_op jit(solution)/shard_map/ppermute | solution.py:412
  15.9 10.0 %collective-permute-start.6 = (bf16[264,128]{1,0:T(8,128)(2,1)}, bf16[264,128]{1,0:T(8,128)(2,1)S(1)}, u32[]{:S(2)}, u32[]{:S(2)}) collective-permute-start(bf16[264,128]{1,0:T(8,128)(2,1)} %get-tuple-element.106), channel_id=1, source_target_pairs={{0,13},{1,12},{2,15},{3,14},{4,9},{5,8},{6,11},{7,10},{8,5},{9,4},... | collective-permute-start | bytes 202760 | tf_op jit(solution)/shard_map/ppermute | solution.py:412
  18.8 8.3 %collective-permute-start.7 = (bf16[264,128]{1,0:T(8,128)(2,1)}, bf16[264,128]{1,0:T(8,128)(2,1)S(1)}, u32[]{:S(2)}, u32[]{:S(2)}) collective-permute-start(bf16[264,128]{1,0:T(8,128)(2,1)} %get-tuple-element.107), channel_id=1, source_target_pairs={{0,3},{1,2},{2,1},{3,0},{4,7},{5,6},{6,5},{7,4},{8,11},{9,10},{10,... | collective-permute-start | bytes 202760 | tf_op jit(solution)/shard_map/ppermute | solution.py:412
  19.8 8.3 %collective-permute-start.8 = (bf16[264,128]{1,0:T(8,128)(2,1)}, bf16[264,128]{1,0:T(8,128)(2,1)S(1)}, u32[]{:S(2)}, u32[]{:S(2)}) collective-permute-start(bf16[264,128]{1,0:T(8,128)(2,1)} %get-tuple-element.108), channel_id=1, source_target_pairs={{0,11},{1,10},{2,9},{3,8},{4,15},{5,14},{6,13},{7,12},{8,3},{9,2},... | collective-permute-start | bytes 202760 | tf_op jit(solution)/shard_map/ppermute | solution.py:412
  22.5 7.2 %collective-permute-start.9 = (bf16[264,128]{1,0:T(8,128)(2,1)}, bf16[264,128]{1,0:T(8,128)(2,1)S(1)}, u32[]{:S(2)}, u32[]{:S(2)}) collective-permute-start(bf16[264,128]{1,0:T(8,128)(2,1)} %get-tuple-element.109), channel_id=1, source_target_pairs={{0,7},{1,6},{2,5},{3,4},{4,3},{5,2},{6,1},{7,0},{8,15},{9,14},{10,... | collective-permute-start | bytes 202760 | tf_op jit(solution)/shard_map/ppermute | solution.py:412
  22.9 14.1 %collective-permute-start.10 = (bf16[264,128]{1,0:T(8,128)(2,1)}, bf16[264,128]{1,0:T(8,128)(2,1)S(1)}, u32[]{:S(2)}, u32[]{:S(2)}) collective-permute-start(bf16[264,128]{1,0:T(8,128)(2,1)} %get-tuple-element.110), channel_id=1, source_target_pairs={{0,15},{1,14},{2,13},{3,12},{4,11},{5,10},{6,9},{7,8},{8,7},{9,6},... | collective-permute-start | bytes 202760 | tf_op jit(solution)/shard_map/ppermute | solution.py:412
  25.8 11.2 %collective-permute-start.11 = (bf16[264,128]{1,0:T(8,128)(2,1)}, bf16[264,128]{1,0:T(8,128)(2,1)S(1)}, u32[]{:S(2)}, u32[]{:S(2)}) collective-permute-start(bf16[264,128]{1,0:T(8,128)(2,1)} %get-tuple-element.111), channel_id=1, source_target_pairs={{0,2},{1,3},{2,0},{3,1},{4,6},{5,7},{6,4},{7,5},{8,10},{9,11},{10,... | collective-permute-start | bytes 202760 | tf_op jit(solution)/shard_map/ppermute | solution.py:412
  27.1 9.9 %collective-permute-start.12 = (bf16[264,128]{1,0:T(8,128)(2,1)}, bf16[264,128]{1,0:T(8,128)(2,1)S(1)}, u32[]{:S(2)}, u32[]{:S(2)}) collective-permute-start(bf16[264,128]{1,0:T(8,128)(2,1)} %get-tuple-element.112), channel_id=1, source_target_pairs={{0,10},{1,11},{2,8},{3,9},{4,14},{5,15},{6,12},{7,13},{8,2},{9,3},... | collective-permute-start | bytes 202760 | tf_op jit(solution)/shard_map/ppermute | solution.py:412
  28.1 8.9 %collective-permute-start.13 = (bf16[264,128]{1,0:T(8,128)(2,1)}, bf16[264,128]{1,0:T(8,128)(2,1)S(1)}, u32[]{:S(2)}, u32[]{:S(2)}) collective-permute-start(bf16[264,128]{1,0:T(8,128)(2,1)} %get-tuple-element.113), channel_id=1, source_target_pairs={{0,6},{1,7},{2,4},{3,5},{4,2},{5,3},{6,0},{7,1},{8,14},{9,15},{10,... | collective-permute-start | bytes 202760 | tf_op jit(solution)/shard_map/ppermute | solution.py:412
  29.7 7.5 %collective-permute-start.14 = (bf16[264,128]{1,0:T(8,128)(2,1)}, bf16[264,128]{1,0:T(8,128)(2,1)S(1)}, u32[]{:S(2)}, u32[]{:S(2)}) collective-permute-start(bf16[264,128]{1,0:T(8,128)(2,1)} %get-tuple-element.114), channel_id=1, source_target_pairs={{0,14},{1,15},{2,12},{3,13},{4,10},{5,11},{6,8},{7,9},{8,6},{9,7},... | collective-permute-start | bytes 202760 | tf_op jit(solution)/shard_map/ppermute | solution.py:412
  39.7 7.0 %collective-permute-start.15 = (bf16[264,128]{1,0:T(8,128)(2,1)S(1)}, bf16[264,128]{1,0:T(8,128)(2,1)S(1)}, u32[]{:S(2)}, u32[]{:S(2)}) collective-permute-start(bf16[264,128]{1,0:T(8,128)(2,1)S(1)} %get-tuple-element.119), channel_id=1, source_target_pairs={{0,8},{1,9},{2,10},{3,11},{4,12},{5,13},{6,14},{7,15},{8,0},{9,1},... | collective-permute-start | bytes 202760 | tf_op jit(solution)/shard_map/ppermute | solution.py:412
  42.7 6.8 %collective-permute-start.17 = (bf16[264,128]{1,0:T(8,128)(2,1)S(1)}, bf16[264,128]{1,0:T(8,128)(2,1)S(1)}, u32[]{:S(2)}, u32[]{:S(2)}) collective-permute-start(bf16[264,128]{1,0:T(8,128)(2,1)S(1)} %get-tuple-element.121), channel_id=1, source_target_pairs={{0,12},{1,13},{2,14},{3,15},{4,8},{5,9},{6,10},{7,11},{8,4},{9,5},... | collective-permute-start | bytes 202760 | tf_op jit(solution)/shard_map/ppermute | solution.py:412
  44.2 7.4 %collective-permute-start.19 = (bf16[264,128]{1,0:T(8,128)(2,1)S(1)}, bf16[264,128]{1,0:T(8,128)(2,1)S(1)}, u32[]{:S(2)}, u32[]{:S(2)}) collective-permute-start(bf16[264,128]{1,0:T(8,128)(2,1)S(1)} %get-tuple-element.123), channel_id=1, source_target_pairs={{0,9},{1,8},{2,11},{3,10},{4,13},{5,12},{6,15},{7,14},{8,1},{9,0},... | collective-permute-start | bytes 202760 | tf_op jit(solution)/shard_map/ppermute | solution.py:412
  46.7 6.8 %collective-permute-start.20 = (bf16[264,128]{1,0:T(8,128)(2,1)S(1)}, bf16[264,128]{1,0:T(8,128)(2,1)S(1)}, u32[]{:S(2)}, u32[]{:S(2)}) collective-permute-start(bf16[264,128]{1,0:T(8,128)(2,1)S(1)} %get-tuple-element.124), channel_id=1, source_target_pairs={{0,5},{1,4},{2,7},{3,6},{4,1},{5,0},{6,3},{7,2},{8,13},{9,12},{10,... | collective-permute-start | bytes 202760 | tf_op jit(solution)/shard_map/ppermute | solution.py:412
  46.9 8.8 %collective-permute-start.21 = (bf16[264,128]{1,0:T(8,128)(2,1)S(1)}, bf16[264,128]{1,0:T(8,128)(2,1)S(1)}, u32[]{:S(2)}, u32[]{:S(2)}) collective-permute-start(bf16[264,128]{1,0:T(8,128)(2,1)S(1)} %get-tuple-element.125), channel_id=1, source_target_pairs={{0,13},{1,12},{2,15},{3,14},{4,9},{5,8},{6,11},{7,10},{8,5},{9,4},... | collective-permute-start | bytes 202760 | tf_op jit(solution)/shard_map/ppermute | solution.py:412
  49.5 7.1 %collective-permute-start.22 = (bf16[264,128]{1,0:T(8,128)(2,1)S(1)}, bf16[264,128]{1,0:T(8,128)(2,1)S(1)}, u32[]{:S(2)}, u32[]{:S(2)}) collective-permute-start(bf16[264,128]{1,0:T(8,128)(2,1)S(1)} %get-tuple-element.126), channel_id=1, source_target_pairs={{0,3},{1,2},{2,1},{3,0},{4,7},{5,6},{6,5},{7,4},{8,11},{9,10},{10,... | collective-permute-start | bytes 202760 | tf_op jit(solution)/shard_map/ppermute | solution.py:412
  49.6 8.2 %collective-permute-start.23 = (bf16[264,128]{1,0:T(8,128)(2,1)S(1)}, bf16[264,128]{1,0:T(8,128)(2,1)S(1)}, u32[]{:S(2)}, u32[]{:S(2)}) collective-permute-start(bf16[264,128]{1,0:T(8,128)(2,1)S(1)} %get-tuple-element.127), channel_id=1, source_target_pairs={{0,11},{1,10},{2,9},{3,8},{4,15},{5,14},{6,13},{7,12},{8,3},{9,2},... | collective-permute-start | bytes 202760 | tf_op jit(solution)/shard_map/ppermute | solution.py:412
  51.5 8.2 %collective-permute-start.24 = (bf16[264,128]{1,0:T(8,128)(2,1)S(1)}, bf16[264,128]{1,0:T(8,128)(2,1)S(1)}, u32[]{:S(2)}, u32[]{:S(2)}) collective-permute-start(bf16[264,128]{1,0:T(8,128)(2,1)S(1)} %get-tuple-element.128), channel_id=1, source_target_pairs={{0,7},{1,6},{2,5},{3,4},{4,3},{5,2},{6,1},{7,0},{8,15},{9,14},{10,... | collective-permute-start | bytes 202760 | tf_op jit(solution)/shard_map/ppermute | solution.py:412
  53.5 9.0 %collective-permute-start.25 = (bf16[264,128]{1,0:T(8,128)(2,1)S(1)}, bf16[264,128]{1,0:T(8,128)(2,1)S(1)}, u32[]{:S(2)}, u32[]{:S(2)}) collective-permute-start(bf16[264,128]{1,0:T(8,128)(2,1)S(1)} %get-tuple-element.129), channel_id=1, source_target_pairs={{0,15},{1,14},{2,13},{3,12},{4,11},{5,10},{6,9},{7,8},{8,7},{9,6},... | collective-permute-start | bytes 202760 | tf_op jit(solution)/shard_map/ppermute | solution.py:412
  55.7 8.6 %collective-permute-start.26 = (bf16[264,128]{1,0:T(8,128)(2,1)S(1)}, bf16[264,128]{1,0:T(8,128)(2,1)S(1)}, u32[]{:S(2)}, u32[]{:S(2)}) collective-permute-start(bf16[264,128]{1,0:T(8,128)(2,1)S(1)} %get-tuple-element.130), channel_id=1, source_target_pairs={{0,2},{1,3},{2,0},{3,1},{4,6},{5,7},{6,4},{7,5},{8,10},{9,11},{10,... | collective-permute-start | bytes 202760 | tf_op jit(solution)/shard_map/ppermute | solution.py:412
  56.6 7.7 %collective-permute-start.27 = (bf16[264,128]{1,0:T(8,128)(2,1)S(1)}, bf16[264,128]{1,0:T(8,128)(2,1)S(1)}, u32[]{:S(2)}, u32[]{:S(2)}) collective-permute-start(bf16[264,128]{1,0:T(8,128)(2,1)S(1)} %get-tuple-element.131), channel_id=1, source_target_pairs={{0,10},{1,11},{2,8},{3,9},{4,14},{5,15},{6,12},{7,13},{8,2},{9,3},... | collective-permute-start | bytes 202760 | tf_op jit(solution)/shard_map/ppermute | solution.py:412
  57.8 6.6 %collective-permute-start.28 = (bf16[264,128]{1,0:T(8,128)(2,1)S(1)}, bf16[264,128]{1,0:T(8,128)(2,1)S(1)}, u32[]{:S(2)}, u32[]{:S(2)}) collective-permute-start(bf16[264,128]{1,0:T(8,128)(2,1)S(1)} %get-tuple-element.132), channel_id=1, source_target_pairs={{0,6},{1,7},{2,4},{3,5},{4,2},{5,3},{6,0},{7,1},{8,14},{9,15},{10,... | collective-permute-start | bytes 202760 | tf_op jit(solution)/shard_map/ppermute | solution.py:412
  59.8 7.0 %collective-permute-start.29 = (bf16[264,128]{1,0:T(8,128)(2,1)S(1)}, bf16[264,128]{1,0:T(8,128)(2,1)S(1)}, u32[]{:S(2)}, u32[]{:S(2)}) collective-permute-start(bf16[264,128]{1,0:T(8,128)(2,1)S(1)} %get-tuple-element.133), channel_id=1, source_target_pairs={{0,14},{1,15},{2,12},{3,13},{4,10},{5,11},{6,8},{7,9},{8,6},{9,7},... | collective-permute-start | bytes 202760 | tf_op jit(solution)/shard_map/ppermute | solution.py:412
  70.3 6.8 %collective-permute-start.31 = (bf16[264,128]{1,0:T(8,128)(2,1)S(1)}, bf16[264,128]{1,0:T(8,128)(2,1)S(1)}, u32[]{:S(2)}, u32[]{:S(2)}) collective-permute-start(bf16[264,128]{1,0:T(8,128)(2,1)S(1)} %get-tuple-element.138), channel_id=1, source_target_pairs={{0,4},{1,5},{2,6},{3,7},{4,0},{5,1},{6,2},{7,3},{8,12},{9,13},{10,... | collective-permute-start | bytes 202760 | tf_op jit(solution)/shard_map/ppermute | solution.py:412
  73.0 6.8 %collective-permute-start.32 = (bf16[264,128]{1,0:T(8,128)(2,1)S(1)}, bf16[264,128]{1,0:T(8,128)(2,1)S(1)}, u32[]{:S(2)}, u32[]{:S(2)}) collective-permute-start(bf16[264,128]{1,0:T(8,128)(2,1)S(1)} %get-tuple-element.139), channel_id=1, source_target_pairs={{0,12},{1,13},{2,14},{3,15},{4,8},{5,9},{6,10},{7,11},{8,4},{9,5},... | collective-permute-start | bytes 202760 | tf_op jit(solution)/shard_map/ppermute | solution.py:412
  74.7 7.2 %collective-permute-start.34 = (bf16[264,128]{1,0:T(8,128)(2,1)S(1)}, bf16[264,128]{1,0:T(8,128)(2,1)S(1)}, u32[]{:S(2)}, u32[]{:S(2)}) collective-permute-start(bf16[264,128]{1,0:T(8,128)(2,1)S(1)} %get-tuple-element.141), channel_id=1, source_target_pairs={{0,9},{1,8},{2,11},{3,10},{4,13},{5,12},{6,15},{7,14},{8,1},{9,0},... | collective-permute-start | bytes 202760 | tf_op jit(solution)/shard_map/ppermute | solution.py:412
  76.6 7.2 %collective-permute-start.35 = (bf16[264,128]{1,0:T(8,128)(2,1)S(1)}, bf16[264,128]{1,0:T(8,128)(2,1)S(1)}, u32[]{:S(2)}, u32[]{:S(2)}) collective-permute-start(bf16[264,128]{1,0:T(8,128)(2,1)S(1)} %get-tuple-element.142), channel_id=1, source_target_pairs={{0,5},{1,4},{2,7},{3,6},{4,1},{5,0},{6,3},{7,2},{8,13},{9,12},{10,... | collective-permute-start | bytes 202760 | tf_op jit(solution)/shard_map/ppermute | solution.py:412
  77.1 8.8 %collective-permute-start.36 = (bf16[264,128]{1,0:T(8,128)(2,1)S(1)}, bf16[264,128]{1,0:T(8,128)(2,1)S(1)}, u32[]{:S(2)}, u32[]{:S(2)}) collective-permute-start(bf16[264,128]{1,0:T(8,128)(2,1)S(1)} %get-tuple-element.143), channel_id=1, source_target_pairs={{0,13},{1,12},{2,15},{3,14},{4,9},{5,8},{6,11},{7,10},{8,5},{9,4},... | collective-permute-start | bytes 202760 | tf_op jit(solution)/shard_map/ppermute | solution.py:412
  79.7 7.3 %collective-permute-start.37 = (bf16[264,128]{1,0:T(8,128)(2,1)S(1)}, bf16[264,128]{1,0:T(8,128)(2,1)S(1)}, u32[]{:S(2)}, u32[]{:S(2)}) collective-permute-start(bf16[264,128]{1,0:T(8,128)(2,1)S(1)} %get-tuple-element.144), channel_id=1, source_target_pairs={{0,3},{1,2},{2,1},{3,0},{4,7},{5,6},{6,5},{7,4},{8,11},{9,10},{10,... | collective-permute-start | bytes 202760 | tf_op jit(solution)/shard_map/ppermute | solution.py:412
  79.9 8.1 %collective-permute-start.38 = (bf16[264,128]{1,0:T(8,128)(2,1)S(1)}, bf16[264,128]{1,0:T(8,128)(2,1)S(1)}, u32[]{:S(2)}, u32[]{:S(2)}) collective-permute-start(bf16[264,128]{1,0:T(8,128)(2,1)S(1)} %get-tuple-element.145), channel_id=1, source_target_pairs={{0,11},{1,10},{2,9},{3,8},{4,15},{5,14},{6,13},{7,12},{8,3},{9,2},... | collective-permute-start | bytes 202760 | tf_op jit(solution)/shard_map/ppermute | solution.py:412
  81.8 8.2 %collective-permute-start.39 = (bf16[264,128]{1,0:T(8,128)(2,1)S(1)}, bf16[264,128]{1,0:T(8,128)(2,1)S(1)}, u32[]{:S(2)}, u32[]{:S(2)}) collective-permute-start(bf16[264,128]{1,0:T(8,128)(2,1)S(1)} %get-tuple-element.146), channel_id=1, source_target_pairs={{0,7},{1,6},{2,5},{3,4},{4,3},{5,2},{6,1},{7,0},{8,15},{9,14},{10,... | collective-permute-start | bytes 202760 | tf_op jit(solution)/shard_map/ppermute | solution.py:412
  83.7 9.0 %collective-permute-start.40 = (bf16[264,128]{1,0:T(8,128)(2,1)S(1)}, bf16[264,128]{1,0:T(8,128)(2,1)S(1)}, u32[]{:S(2)}, u32[]{:S(2)}) collective-permute-start(bf16[264,128]{1,0:T(8,128)(2,1)S(1)} %get-tuple-element.147), channel_id=1, source_target_pairs={{0,15},{1,14},{2,13},{3,12},{4,11},{5,10},{6,9},{7,8},{8,7},{9,6},... | collective-permute-start | bytes 202760 | tf_op jit(solution)/shard_map/ppermute | solution.py:412
  86.0 8.6 %collective-permute-start.41 = (bf16[264,128]{1,0:T(8,128)(2,1)S(1)}, bf16[264,128]{1,0:T(8,128)(2,1)S(1)}, u32[]{:S(2)}, u32[]{:S(2)}) collective-permute-start(bf16[264,128]{1,0:T(8,128)(2,1)S(1)} %get-tuple-element.148), channel_id=1, source_target_pairs={{0,2},{1,3},{2,0},{3,1},{4,6},{5,7},{6,4},{7,5},{8,10},{9,11},{10,... | collective-permute-start | bytes 202760 | tf_op jit(solution)/shard_map/ppermute | solution.py:412
  87.1 7.6 %collective-permute-start.42 = (bf16[264,128]{1,0:T(8,128)(2,1)S(1)}, bf16[264,128]{1,0:T(8,128)(2,1)S(1)}, u32[]{:S(2)}, u32[]{:S(2)}) collective-permute-start(bf16[264,128]{1,0:T(8,128)(2,1)S(1)} %get-tuple-element.149), channel_id=1, source_target_pairs={{0,10},{1,11},{2,8},{3,9},{4,14},{5,15},{6,12},{7,13},{8,2},{9,3},... | collective-permute-start | bytes 202760 | tf_op jit(solution)/shard_map/ppermute | solution.py:412
  88.0 6.6 %collective-permute-start.43 = (bf16[264,128]{1,0:T(8,128)(2,1)S(1)}, bf16[264,128]{1,0:T(8,128)(2,1)S(1)}, u32[]{:S(2)}, u32[]{:S(2)}) collective-permute-start(bf16[264,128]{1,0:T(8,128)(2,1)S(1)} %get-tuple-element.150), channel_id=1, source_target_pairs={{0,6},{1,7},{2,4},{3,5},{4,2},{5,3},{6,0},{7,1},{8,14},{9,15},{10,... | collective-permute-start | bytes 202760 | tf_op jit(solution)/shard_map/ppermute | solution.py:412
  90.0 7.0 %collective-permute-start.44 = (bf16[264,128]{1,0:T(8,128)(2,1)S(1)}, bf16[264,128]{1,0:T(8,128)(2,1)S(1)}, u32[]{:S(2)}, u32[]{:S(2)}) collective-permute-start(bf16[264,128]{1,0:T(8,128)(2,1)S(1)} %get-tuple-element.151), channel_id=1, source_target_pairs={{0,14},{1,15},{2,12},{3,13},{4,10},{5,11},{6,8},{7,9},{8,6},{9,7},... | collective-permute-start | bytes 202760 | tf_op jit(solution)/shard_map/ppermute | solution.py:412
  99.6 6.7 %collective-permute-start.46 = (bf16[264,128]{1,0:T(8,128)(2,1)S(1)}, bf16[264,128]{1,0:T(8,128)(2,1)S(1)}, u32[]{:S(2)}, u32[]{:S(2)}) collective-permute-start(bf16[264,128]{1,0:T(8,128)(2,1)S(1)} %get-tuple-element.156), channel_id=1, source_target_pairs={{0,4},{1,5},{2,6},{3,7},{4,0},{5,1},{6,2},{7,3},{8,12},{9,13},{10,... | collective-permute-start | bytes 202760 | tf_op jit(solution)/shard_map/ppermute | solution.py:412
  102.2 6.7 %collective-permute-start.47 = (bf16[264,128]{1,0:T(8,128)(2,1)S(1)}, bf16[264,128]{1,0:T(8,128)(2,1)S(1)}, u32[]{:S(2)}, u32[]{:S(2)}) collective-permute-start(bf16[264,128]{1,0:T(8,128)(2,1)S(1)} %get-tuple-element.157), channel_id=1, source_target_pairs={{0,12},{1,13},{2,14},{3,15},{4,8},{5,9},{6,10},{7,11},{8,4},{9,5},... | collective-permute-start | bytes 202760 | tf_op jit(solution)/shard_map/ppermute | solution.py:412
  103.7 7.3 %collective-permute-start.49 = (bf16[264,128]{1,0:T(8,128)(2,1)S(1)}, bf16[264,128]{1,0:T(8,128)(2,1)S(1)}, u32[]{:S(2)}, u32[]{:S(2)}) collective-permute-start(bf16[264,128]{1,0:T(8,128)(2,1)S(1)} %get-tuple-element.159), channel_id=1, source_target_pairs={{0,9},{1,8},{2,11},{3,10},{4,13},{5,12},{6,15},{7,14},{8,1},{9,0},... | collective-permute-start | bytes 202760 | tf_op jit(solution)/shard_map/ppermute | solution.py:412
  105.7 7.3 %collective-permute-start.50 = (bf16[264,128]{1,0:T(8,128)(2,1)S(1)}, bf16[264,128]{1,0:T(8,128)(2,1)S(1)}, u32[]{:S(2)}, u32[]{:S(2)}) collective-permute-start(bf16[264,128]{1,0:T(8,128)(2,1)S(1)} %get-tuple-element.160), channel_id=1, source_target_pairs={{0,5},{1,4},{2,7},{3,6},{4,1},{5,0},{6,3},{7,2},{8,13},{9,12},{10,... | collective-permute-start | bytes 202760 | tf_op jit(solution)/shard_map/ppermute | solution.py:412
  106.4 8.8 %collective-permute-start.51 = (bf16[264,128]{1,0:T(8,128)(2,1)S(1)}, bf16[264,128]{1,0:T(8,128)(2,1)S(1)}, u32[]{:S(2)}, u32[]{:S(2)}) collective-permute-start(bf16[264,128]{1,0:T(8,128)(2,1)S(1)} %get-tuple-element.161), channel_id=1, source_target_pairs={{0,13},{1,12},{2,15},{3,14},{4,9},{5,8},{6,11},{7,10},{8,5},{9,4},... | collective-permute-start | bytes 202760 | tf_op jit(solution)/shard_map/ppermute | solution.py:412
  109.0 7.1 %collective-permute-start.52 = (bf16[264,128]{1,0:T(8,128)(2,1)S(1)}, bf16[264,128]{1,0:T(8,128)(2,1)S(1)}, u32[]{:S(2)}, u32[]{:S(2)}) collective-permute-start(bf16[264,128]{1,0:T(8,128)(2,1)S(1)} %get-tuple-element.162), channel_id=1, source_target_pairs={{0,3},{1,2},{2,1},{3,0},{4,7},{5,6},{6,5},{7,4},{8,11},{9,10},{10,... | collective-permute-start | bytes 202760 | tf_op jit(solution)/shard_map/ppermute | solution.py:412
  109.0 8.4 %collective-permute-start.53 = (bf16[264,128]{1,0:T(8,128)(2,1)S(1)}, bf16[264,128]{1,0:T(8,128)(2,1)S(1)}, u32[]{:S(2)}, u32[]{:S(2)}) collective-permute-start(bf16[264,128]{1,0:T(8,128)(2,1)S(1)} %get-tuple-element.163), channel_id=1, source_target_pairs={{0,11},{1,10},{2,9},{3,8},{4,15},{5,14},{6,13},{7,12},{8,3},{9,2},... | collective-permute-start | bytes 202760 | tf_op jit(solution)/shard_map/ppermute | solution.py:412
  111.0 8.2 %collective-permute-start.54 = (bf16[264,128]{1,0:T(8,128)(2,1)S(1)}, bf16[264,128]{1,0:T(8,128)(2,1)S(1)}, u32[]{:S(2)}, u32[]{:S(2)}) collective-permute-start(bf16[264,128]{1,0:T(8,128)(2,1)S(1)} %get-tuple-element.164), channel_id=1, source_target_pairs={{0,7},{1,6},{2,5},{3,4},{4,3},{5,2},{6,1},{7,0},{8,15},{9,14},{10,... | collective-permute-start | bytes 202760 | tf_op jit(solution)/shard_map/ppermute | solution.py:412
  113.0 9.0 %collective-permute-start.55 = (bf16[264,128]{1,0:T(8,128)(2,1)S(1)}, bf16[264,128]{1,0:T(8,128)(2,1)S(1)}, u32[]{:S(2)}, u32[]{:S(2)}) collective-permute-start(bf16[264,128]{1,0:T(8,128)(2,1)S(1)} %get-tuple-element.165), channel_id=1, source_target_pairs={{0,15},{1,14},{2,13},{3,12},{4,11},{5,10},{6,9},{7,8},{8,7},{9,6},... | collective-permute-start | bytes 202760 | tf_op jit(solution)/shard_map/ppermute | solution.py:412
  115.2 8.6 %collective-permute-start.56 = (bf16[264,128]{1,0:T(8,128)(2,1)S(1)}, bf16[264,128]{1,0:T(8,128)(2,1)S(1)}, u32[]{:S(2)}, u32[]{:S(2)}) collective-permute-start(bf16[264,128]{1,0:T(8,128)(2,1)S(1)} %get-tuple-element.166), channel_id=1, source_target_pairs={{0,2},{1,3},{2,0},{3,1},{4,6},{5,7},{6,4},{7,5},{8,10},{9,11},{10,... | collective-permute-start | bytes 202760 | tf_op jit(solution)/shard_map/ppermute | solution.py:412
  116.1 7.7 %collective-permute-start.57 = (bf16[264,128]{1,0:T(8,128)(2,1)S(1)}, bf16[264,128]{1,0:T(8,128)(2,1)S(1)}, u32[]{:S(2)}, u32[]{:S(2)}) collective-permute-start(bf16[264,128]{1,0:T(8,128)(2,1)S(1)} %get-tuple-element.167), channel_id=1, source_target_pairs={{0,10},{1,11},{2,8},{3,9},{4,14},{5,15},{6,12},{7,13},{8,2},{9,3},... | collective-permute-start | bytes 202760 | tf_op jit(solution)/shard_map/ppermute | solution.py:412
  119.3 7.0 %collective-permute-start.59 = (bf16[264,128]{1,0:T(8,128)(2,1)S(1)}, bf16[264,128]{1,0:T(8,128)(2,1)S(1)}, u32[]{:S(2)}, u32[]{:S(2)}) collective-permute-start(bf16[264,128]{1,0:T(8,128)(2,1)S(1)} %get-tuple-element.169), channel_id=1, source_target_pairs={{0,14},{1,15},{2,12},{3,13},{4,10},{5,11},{6,8},{7,9},{8,6},{9,7},... | collective-permute-start | bytes 202760 | tf_op jit(solution)/shard_map/ppermute | solution.py:412
  129.8 6.8 %collective-permute-start.61 = (bf16[264,128]{1,0:T(8,128)(2,1)S(1)}, bf16[264,128]{1,0:T(8,128)(2,1)S(1)}, u32[]{:S(2)}, u32[]{:S(2)}) collective-permute-start(bf16[264,128]{1,0:T(8,128)(2,1)S(1)} %get-tuple-element.175), channel_id=1, source_target_pairs={{0,4},{1,5},{2,6},{3,7},{4,0},{5,1},{6,2},{7,3},{8,12},{9,13},{10,... | collective-permute-start | bytes 202760 | tf_op jit(solution)/shard_map/ppermute | solution.py:412
  132.5 6.7 %collective-permute-start.62 = (bf16[264,128]{1,0:T(8,128)(2,1)S(1)}, bf16[264,128]{1,0:T(8,128)(2,1)S(1)}, u32[]{:S(2)}, u32[]{:S(2)}) collective-permute-start(bf16[264,128]{1,0:T(8,128)(2,1)S(1)} %get-tuple-element.176), channel_id=1, source_target_pairs={{0,12},{1,13},{2,14},{3,15},{4,8},{5,9},{6,10},{7,11},{8,4},{9,5},... | collective-permute-start | bytes 202760 | tf_op jit(solution)/shard_map/ppermute | solution.py:412
  134.2 7.1 %collective-permute-start.64 = (bf16[264,128]{1,0:T(8,128)(2,1)S(1)}, bf16[264,128]{1,0:T(8,128)(2,1)S(1)}, u32[]{:S(2)}, u32[]{:S(2)}) collective-permute-start(bf16[264,128]{1,0:T(8,128)(2,1)S(1)} %get-tuple-element.178), channel_id=1, source_target_pairs={{0,9},{1,8},{2,11},{3,10},{4,13},{5,12},{6,15},{7,14},{8,1},{9,0},... | collective-permute-start | bytes 202760 | tf_op jit(solution)/shard_map/ppermute | solution.py:412
  136.1 7.2 %collective-permute-start.65 = (bf16[264,128]{1,0:T(8,128)(2,1)S(1)}, bf16[264,128]{1,0:T(8,128)(2,1)S(1)}, u32[]{:S(2)}, u32[]{:S(2)}) collective-permute-start(bf16[264,128]{1,0:T(8,128)(2,1)S(1)} %get-tuple-element.179), channel_id=1, source_target_pairs={{0,5},{1,4},{2,7},{3,6},{4,1},{5,0},{6,3},{7,2},{8,13},{9,12},{10,... | collective-permute-start | bytes 202760 | tf_op jit(solution)/shard_map/ppermute | solution.py:412
  136.6 8.8 %collective-permute-start.66 = (bf16[264,128]{1,0:T(8,128)(2,1)S(1)}, bf16[264,128]{1,0:T(8,128)(2,1)S(1)}, u32[]{:S(2)}, u32[]{:S(2)}) collective-permute-start(bf16[264,128]{1,0:T(8,128)(2,1)S(1)} %get-tuple-element.180), channel_id=1, source_target_pairs={{0,13},{1,12},{2,15},{3,14},{4,9},{5,8},{6,11},{7,10},{8,5},{9,4},... | collective-permute-start | bytes 202760 | tf_op jit(solution)/shard_map/ppermute | solution.py:412
  139.2 7.3 %collective-permute-start.67 = (bf16[264,128]{1,0:T(8,128)(2,1)S(1)}, bf16[264,128]{1,0:T(8,128)(2,1)S(1)}, u32[]{:S(2)}, u32[]{:S(2)}) collective-permute-start(bf16[264,128]{1,0:T(8,128)(2,1)S(1)} %get-tuple-element.181), channel_id=1, source_target_pairs={{0,3},{1,2},{2,1},{3,0},{4,7},{5,6},{6,5},{7,4},{8,11},{9,10},{10,... | collective-permute-start | bytes 202760 | tf_op jit(solution)/shard_map/ppermute | solution.py:412
  139.2 8.6 %collective-permute-start.68 = (bf16[264,128]{1,0:T(8,128)(2,1)S(1)}, bf16[264,128]{1,0:T(8,128)(2,1)S(1)}, u32[]{:S(2)}, u32[]{:S(2)}) collective-permute-start(bf16[264,128]{1,0:T(8,128)(2,1)S(1)} %get-tuple-element.182), channel_id=1, source_target_pairs={{0,11},{1,10},{2,9},{3,8},{4,15},{5,14},{6,13},{7,12},{8,3},{9,2},... | collective-permute-start | bytes 202760 | tf_op jit(solution)/shard_map/ppermute | solution.py:412
  141.3 8.2 %collective-permute-start.69 = (bf16[264,128]{1,0:T(8,128)(2,1)S(1)}, bf16[264,128]{1,0:T(8,128)(2,1)S(1)}, u32[]{:S(2)}, u32[]{:S(2)}) collective-permute-start(bf16[264,128]{1,0:T(8,128)(2,1)S(1)} %get-tuple-element.183), channel_id=1, source_target_pairs={{0,7},{1,6},{2,5},{3,4},{4,3},{5,2},{6,1},{7,0},{8,15},{9,14},{10,... | collective-permute-start | bytes 202760 | tf_op jit(solution)/shard_map/ppermute | solution.py:412
  143.2 9.0 %collective-permute-start.70 = (bf16[264,128]{1,0:T(8,128)(2,1)S(1)}, bf16[264,128]{1,0:T(8,128)(2,1)S(1)}, u32[]{:S(2)}, u32[]{:S(2)}) collective-permute-start(bf16[264,128]{1,0:T(8,128)(2,1)S(1)} %get-tuple-element.184), channel_id=1, source_target_pairs={{0,15},{1,14},{2,13},{3,12},{4,11},{5,10},{6,9},{7,8},{8,7},{9,6},... | collective-permute-start | bytes 202760 | tf_op jit(solution)/shard_map/ppermute | solution.py:412
  145.4 8.6 %collective-permute-start.71 = (bf16[264,128]{1,0:T(8,128)(2,1)S(1)}, bf16[264,128]{1,0:T(8,128)(2,1)S(1)}, u32[]{:S(2)}, u32[]{:S(2)}) collective-permute-start(bf16[264,128]{1,0:T(8,128)(2,1)S(1)} %get-tuple-element.185), channel_id=1, source_target_pairs={{0,2},{1,3},{2,0},{3,1},{4,6},{5,7},{6,4},{7,5},{8,10},{9,11},{10,... | collective-permute-start | bytes 202760 | tf_op jit(solution)/shard_map/ppermute | solution.py:412
  146.6 7.5 %collective-permute-start.72 = (bf16[264,128]{1,0:T(8,128)(2,1)S(1)}, bf16[264,128]{1,0:T(8,128)(2,1)S(1)}, u32[]{:S(2)}, u32[]{:S(2)}) collective-permute-start(bf16[264,128]{1,0:T(8,128)(2,1)S(1)} %get-tuple-element.186), channel_id=1, source_target_pairs={{0,10},{1,11},{2,8},{3,9},{4,14},{5,15},{6,12},{7,13},{8,2},{9,3},... | collective-permute-start | bytes 202760 | tf_op jit(solution)/shard_map/ppermute | solution.py:412
  149.5 7.0 %collective-permute-start.74 = (bf16[264,128]{1,0:T(8,128)(2,1)S(1)}, bf16[264,128]{1,0:T(8,128)(2,1)S(1)}, u32[]{:S(2)}, u32[]{:S(2)}) collective-permute-start(bf16[264,128]{1,0:T(8,128)(2,1)S(1)} %get-tuple-element.188), channel_id=1, source_target_pairs={{0,14},{1,15},{2,12},{3,13},{4,10},{5,11},{6,8},{7,9},{8,6},{9,7},... | collective-permute-start | bytes 202760 | tf_op jit(solution)/shard_map/ppermute | solution.py:412
  (20 other events, 122.6 us)

commit v23 on v19

--- a/solution.py
+++ b/solution.py
@@ -216,12 +216,12 @@
         return squares + raw * raw
 
     squares = lax.fori_loop(0, pair_count, one_pair, jnp.zeros((cols, BS), F32), unroll=True)
+    transposed(
+        raw_ref, rays_ref, lambda: None, lambda pair: None, target_ref, total_ref, message_refs
+    )
     tail = squares_tail(squares).astype(BF16)
     for message_ref in message_refs:
         message_ref[BCAP * cols :, :] = tail
-    transposed(
-        raw_ref, rays_ref, lambda: None, lambda pair: None, target_ref, total_ref, message_refs
-    )
 
 
 def gathered(arrived_refs, asked_ref, model_ref):
@@ -249,7 +249,7 @@
         values = model_ref[:, lanes(block)]
         return squares + values * values
 
-    return lax.fori_loop(0, cells // BS, one_block, jnp.zeros((cols, BS), F32), unroll=8)
+    return lax.fori_loop(0, cells // BS, one_block, jnp.zeros((cols, BS), F32), unroll=32)
 
 
 def first_cell_kernel(peers, *refs):
@@ -275,7 +275,7 @@
         model_ref[:, lanes(block)] = before_ref[:, lanes(block)] * -scale
         return carry
 
-    lax.fori_loop(0, model_ref.shape[1] // BS, one_block, 0, unroll=8)
+    lax.fori_loop(0, model_ref.shape[1] // BS, one_block, 0, unroll=32)
 
 
 def cell_kernel(peers, asked_ref, *refs):
@@ -320,7 +320,7 @@
 
     copies = []
     for chunk in range(CHUNKS):
-        lax.fori_loop(chunk * blocks, (chunk + 1) * blocks, one_block, 0, unroll=4)
+        lax.fori_loop(chunk * blocks, (chunk + 1) * blocks, one_block, 0, unroll=True)
         where = slice(chunk * blocks * BS, (chunk + 1) * blocks * BS)
         copies.append(
             pltpu.make_async_copy(
@@ -370,7 +370,7 @@
 
     copies = []
     for chunk in range(CHUNKS):
-        lax.fori_loop(chunk * blocks, (chunk + 1) * blocks, one_block, 0, unroll=4)
+        lax.fori_loop(chunk * blocks, (chunk + 1) * blocks, one_block, 0, unroll=True)
         where = slice(chunk * blocks * BS, (chunk + 1) * blocks * BS)
         copies.append(
             pltpu.make_async_copy(out_ref.at[:, where], out_hbm.at[:, where], sems.at[chunk])

time: 172 us -> 171 us (level)
  waiting for transfers between devices: 35.2 us -> 38.3 us
  starting transfers between devices: 108 us -> 106 us
    ppermute x75, waiting for transfers between devices: 32.8 us -> 36.3 us  [exchange(): lax.ppermute(value, 'pair', [(one, one ^ step) for one in range(peers)])]
    ppermute x75, starting transfers between devices: 102 us -> 99.4 us  [exchange(): lax.ppermute(value, 'pair', [(one, one ^ step) for one in range(peers)])]
where the time goes in v23:
time: 171 us
  starting transfers between devices  106 us (62%)
  waiting for transfers between devices  38.3 us (22%)
  Pallas kernels  24.6 us (14%)
    ppermute x75, starting transfers between devices, exchange(): lax.ppermute(value, 'pair', [(one, one ^ step) for one in range(peers)])  99.4 us
    ppermute x75, waiting for transfers between devices, exchange(): lax.ppermute(value, 'pair', [(one, one ^ step) for one in range(peers)])  36.3 us
    pallas_call x2, Pallas kernels, on_device(): call(functools.partial(pair_kernel, peers), 'pairs_last' if last else 'pa...  6.91 us
    ppermute x6, starting transfers between devices, on_device(): lax.ppermute(share, 'pair', [(one, one ^ step) for one in range(peers)])  6.31 us
    pallas_call x1, Pallas kernels, on_device(): call(functools.partial(start_kernel, peers), 'start', [SMEM, HBM, HBM, HB...  5.2 us
  transfers between devices with their start and end apart: 81, of which 31 were waited for; matrix products, arithmetic and copies ran while one was open for 0% of the time, Pallas kernels for 3%

profile of v23, /device:TPU:0, one launch (start us, length us, event | category | flops | bytes accessed | tf_op | source)
XLA Modules:
  0.0 171.0 jit_solution(9880832101536584214)
XLA Ops:
  0.6 5.2 %start.1 = (bf16[264,128]{1,0:T(8,128)(2,1)}, bf16[264,128]{1,0:T(8,128)(2,1)}, bf16[264,128]{1,0:T(8,128)(2,1)}, bf16[264,128]{1,0:T(8,128)(2,1)}, bf16[264,128...) custom-call(s32[1]{0:T(128)} %bitcast.me_ref, ...), custom_call_target="tpu_custom_call" | custom-call | flops 268435456 | bytes 6291456 | tf_op jit(solution)/shard_map/start/pallas_call | solution.py:421
  5.8 4.0 %collective-permute-start = (bf16[264,128]{1,0:T(8,128)(2,1)}, bf16[264,128]{1,0:T(8,128)(2,1)S(1)}, u32[]{:S(2)}, u32[]{:S(2)}) collective-permute-start(bf16[264,128]{1,0:T(8,128)(2,1)} %get-tuple-element.100), channel_id=1, source_target_pairs={{0,8},{1,9},{2,10},{3,11},{4,12},{5,13},{6,14},{7,15},{8,0},{9,1},... | collective-permute-start | bytes 202760 | tf_op jit(solution)/shard_map/ppermute | solution.py:416
  9.9 1.6 collective-permute-start.1
  11.5 2.0 %collective-permute-start.4 = (bf16[264,128]{1,0:T(8,128)(2,1)}, bf16[264,128]{1,0:T(8,128)(2,1)S(1)}, u32[]{:S(2)}, u32[]{:S(2)}) collective-permute-start(bf16[264,128]{1,0:T(8,128)(2,1)} %get-tuple-element.104), channel_id=1, source_target_pairs={{0,9},{1,8},{2,11},{3,10},{4,13},{5,12},{6,15},{7,14},{8,1},{9,0},... | collective-permute-start | bytes 202760 | tf_op jit(solution)/shard_map/ppermute | solution.py:416
  13.5 2.2 %collective-permute-start.5 = (bf16[264,128]{1,0:T(8,128)(2,1)}, bf16[264,128]{1,0:T(8,128)(2,1)S(1)}, u32[]{:S(2)}, u32[]{:S(2)}) collective-permute-start(bf16[264,128]{1,0:T(8,128)(2,1)} %get-tuple-element.105), channel_id=1, source_target_pairs={{0,5},{1,4},{2,7},{3,6},{4,1},{5,0},{6,3},{7,2},{8,13},{9,12},{10,... | collective-permute-start | bytes 202760 | tf_op jit(solution)/shard_map/ppermute | solution.py:416
  15.6 1.4 collective-permute-start.6
  17.1 1.5 collective-permute-done.2.refs_3_
  18.6 1.5 collective-permute-start.7
  20.0 2.5 %collective-permute-start.8 = (bf16[264,128]{1,0:T(8,128)(2,1)}, bf16[264,128]{1,0:T(8,128)(2,1)S(1)}, u32[]{:S(2)}, u32[]{:S(2)}) collective-permute-start(bf16[264,128]{1,0:T(8,128)(2,1)} %get-tuple-element.108), channel_id=1, source_target_pairs={{0,10},{1,11},{2,8},{3,9},{4,14},{5,15},{6,12},{7,13},{8,2},{9,3},... | collective-permute-start | bytes 202760 | tf_op jit(solution)/shard_map/ppermute | solution.py:416
  23.7 2.7 %collective-permute-start.10 = (bf16[264,128]{1,0:T(8,128)(2,1)}, bf16[264,128]{1,0:T(8,128)(2,1)S(1)}, u32[]{:S(2)}, u32[]{:S(2)}) collective-permute-start(bf16[264,128]{1,0:T(8,128)(2,1)} %get-tuple-element.110), channel_id=1, source_target_pairs={{0,14},{1,15},{2,12},{3,13},{4,10},{5,11},{6,8},{7,9},{8,6},{9,7},... | collective-permute-start | bytes 202760 | tf_op jit(solution)/shard_map/ppermute | solution.py:416
  29.1 3.6 %collective-permute-start.14 = (bf16[264,128]{1,0:T(8,128)(2,1)}, bf16[264,128]{1,0:T(8,128)(2,1)S(1)}, u32[]{:S(2)}, u32[]{:S(2)}) collective-permute-start(bf16[264,128]{1,0:T(8,128)(2,1)} %get-tuple-element.114), channel_id=1, source_target_pairs={{0,15},{1,14},{2,13},{3,12},{4,11},{5,10},{6,9},{7,8},{8,7},{9,6},... | collective-permute-start | bytes 202760 | tf_op jit(solution)/shard_map/ppermute | solution.py:416
  34.1 2.9 %keep.1 = (s32[128]{0:T(128)S(1)}, bf16[264,128]{1,0:T(8,128)(2,1)S(1)}, bf16[8,16,128,128]{3,2,1,0:T(8,128)(2,1)S(1)}) custom-call(s32[128]{0:T(128)S(1)} %copy-done.2, bf16[264,128]{1,0:T(8,128)(2,1)S(1)} %copy-done.1, bf16[8,16,128,128]{3,2,1,0:T(8,128)(2,1)} %rays_hbm.3), custom_call_target="tpu_custom_call" | custom-call | bytes 8388608 | tf_op jit(solution)/shard_map/keep/pallas_call | solution.py:433
  37.1 2.5 %cells_first.1 = (f32[64,8192]{1,0:T(8,128)S(1)}, f32[64,128]{1,0:T(8,128)S(1)}, bf16[264,128]{1,0:T(8,128)(2,1)S(1)}, bf16[264,128]{1,0:T(8,128)(2,1)S(1)}, bf1...) custom-call(bf16[264,128]{1,0:T(8,128)(2,1)S(1)} %get-tuple-element., ...), custom_call_target="tpu_custom_call" | custom-call | bytes 6291456 | tf_op jit(solution)/shard_map/cells_first/pallas_call | solution.py:438
  39.7 3.1 %collective-permute-start.16 = (bf16[264,128]{1,0:T(8,128)(2,1)S(1)}, bf16[264,128]{1,0:T(8,128)(2,1)S(1)}, u32[]{:S(2)}, u32[]{:S(2)}) collective-permute-start(bf16[264,128]{1,0:T(8,128)(2,1)S(1)} %get-tuple-element.120), channel_id=1, source_target_pairs={{0,4},{1,5},{2,6},{3,7},{4,0},{5,1},{6,2},{7,3},{8,12},{9,13},{10,... | collective-permute-start | bytes 202760 | tf_op jit(solution)/shard_map/ppermute | solution.py:416
  42.7 1.3 collective-permute-start.17
  44.3 2.4 %collective-permute-done.15.refs_1_ = bf16[264,128]{1,0:T(8,128)(2,1)S(1)} collective-permute-done((bf16[264,128]{1,0:T(8,128)(2,1)S(1)}, bf16[264,128]{1,0:T(8,128)(2,1)S(1)}, u32[]{:S(2)}, u32[]{:S(2)}) %collective-permute-start.15) | collective-permute-done | bytes 67616 | tf_op jit(solution)/shard_map/ppermute | solution.py:416
  46.8 1.4 collective-permute-start.21
  48.3 1.3 collective-permute-done.17.refs_3_
  49.6 3.5 %collective-permute-start.23 = (bf16[264,128]{1,0:T(8,128)(2,1)S(1)}, bf16[264,128]{1,0:T(8,128)(2,1)S(1)}, u32[]{:S(2)}, u32[]{:S(2)}) collective-permute-start(bf16[264,128]{1,0:T(8,128)(2,1)S(1)} %get-tuple-element.127), channel_id=1, source_target_pairs={{0,10},{1,11},{2,8},{3,9},{4,14},{5,15},{6,12},{7,13},{8,2},{9,3},... | collective-permute-start | bytes 202760 | tf_op jit(solution)/shard_map/ppermute | solution.py:416
  53.5 2.8 %collective-permute-start.25 = (bf16[264,128]{1,0:T(8,128)(2,1)S(1)}, bf16[264,128]{1,0:T(8,128)(2,1)S(1)}, u32[]{:S(2)}, u32[]{:S(2)}) collective-permute-start(bf16[264,128]{1,0:T(8,128)(2,1)S(1)} %get-tuple-element.129), channel_id=1, source_target_pairs={{0,14},{1,15},{2,12},{3,13},{4,10},{5,11},{6,8},{7,9},{8,6},{9,7},... | collective-permute-start | bytes 202760 | tf_op jit(solution)/shard_map/ppermute | solution.py:416
  56.3 2.3 %collective-permute-start.27 = (bf16[264,128]{1,0:T(8,128)(2,1)S(1)}, bf16[264,128]{1,0:T(8,128)(2,1)S(1)}, u32[]{:S(2)}, u32[]{:S(2)}) collective-permute-start(bf16[264,128]{1,0:T(8,128)(2,1)S(1)} %get-tuple-element.131), channel_id=1, source_target_pairs={{0,11},{1,10},{2,9},{3,8},{4,15},{5,14},{6,13},{7,12},{8,3},{9,2},... | collective-permute-start | bytes 202760 | tf_op jit(solution)/shard_map/ppermute | solution.py:416
  59.5 3.0 %collective-permute-start.29 = (bf16[264,128]{1,0:T(8,128)(2,1)S(1)}, bf16[264,128]{1,0:T(8,128)(2,1)S(1)}, u32[]{:S(2)}, u32[]{:S(2)}) collective-permute-start(bf16[264,128]{1,0:T(8,128)(2,1)S(1)} %get-tuple-element.133), channel_id=1, source_target_pairs={{0,15},{1,14},{2,13},{3,12},{4,11},{5,10},{6,9},{7,8},{8,7},{9,6},... | collective-permute-start | bytes 202760 | tf_op jit(solution)/shard_map/ppermute | solution.py:416
  62.5 2.0 %collective-permute-done.26.refs_12_ = bf16[264,128]{1,0:T(8,128)(2,1)S(1)} collective-permute-done((bf16[264,128]{1,0:T(8,128)(2,1)S(1)}, bf16[264,128]{1,0:T(8,128)(2,1)S(1)}, u32[]{:S(2)}, u32[]{:S(2)}) %collective-permute-start.26) | collective-permute-done | bytes 67616 | tf_op jit(solution)/shard_map/ppermute | solution.py:416
  64.5 1.6 collective-permute-done.29.refs_15_
  66.1 3.5 %pairs.1 = (bf16[264,128]{1,0:T(8,128)(2,1)S(1)}, bf16[264,128]{1,0:T(8,128)(2,1)S(1)}, bf16[264,128]{1,0:T(8,128)(2,1)S(1)}, bf16[264,128]{1,0:T(8,128)(2,1)S(1...) custom-call(s32[128]{0:T(128)S(1)} %get-tuple-element.117.target_ref, ...), custom_call_target="tpu_custom_call" | custom-call | flops 536870912 | bytes 8388608 | tf_op jit(solution)/shard_map/pairs/pallas_call | solution.py:449
  70.2 2.5 %collective-permute-start.31 = (bf16[264,128]{1,0:T(8,128)(2,1)S(1)}, bf16[264,128]{1,0:T(8,128)(2,1)S(1)}, u32[]{:S(2)}, u32[]{:S(2)}) collective-permute-start(bf16[264,128]{1,0:T(8,128)(2,1)S(1)} %get-tuple-element.138), channel_id=1, source_target_pairs={{0,4},{1,5},{2,6},{3,7},{4,0},{5,1},{6,2},{7,3},{8,12},{9,13},{10,... | collective-permute-start | bytes 202760 | tf_op jit(solution)/shard_map/ppermute | solution.py:416
  72.7 1.4 collective-permute-start.32
  74.2 2.4 %collective-permute-done.30.refs_1_ = bf16[264,128]{1,0:T(8,128)(2,1)S(1)} collective-permute-done((bf16[264,128]{1,0:T(8,128)(2,1)S(1)}, bf16[264,128]{1,0:T(8,128)(2,1)S(1)}, u32[]{:S(2)}, u32[]{:S(2)}) %collective-permute-start.30) | collective-permute-done | bytes 67616 | tf_op jit(solution)/shard_map/ppermute | solution.py:416
  79.9 3.6 %collective-permute-start.38 = (bf16[264,128]{1,0:T(8,128)(2,1)S(1)}, bf16[264,128]{1,0:T(8,128)(2,1)S(1)}, u32[]{:S(2)}, u32[]{:S(2)}) collective-permute-start(bf16[264,128]{1,0:T(8,128)(2,1)S(1)} %get-tuple-element.145), channel_id=1, source_target_pairs={{0,10},{1,11},{2,8},{3,9},{4,14},{5,15},{6,12},{7,13},{8,2},{9,3},... | collective-permute-start | bytes 202760 | tf_op jit(solution)/shard_map/ppermute | solution.py:416
  83.9 2.2 %collective-permute-start.40 = (bf16[264,128]{1,0:T(8,128)(2,1)S(1)}, bf16[264,128]{1,0:T(8,128)(2,1)S(1)}, u32[]{:S(2)}, u32[]{:S(2)}) collective-permute-start(bf16[264,128]{1,0:T(8,128)(2,1)S(1)} %get-tuple-element.147), channel_id=1, source_target_pairs={{0,14},{1,15},{2,12},{3,13},{4,10},{5,11},{6,8},{7,9},{8,6},{9,7},... | collective-permute-start | bytes 202760 | tf_op jit(solution)/shard_map/ppermute | solution.py:416
  86.9 2.6 %collective-permute-start.42 = (bf16[264,128]{1,0:T(8,128)(2,1)S(1)}, bf16[264,128]{1,0:T(8,128)(2,1)S(1)}, u32[]{:S(2)}, u32[]{:S(2)}) collective-permute-start(bf16[264,128]{1,0:T(8,128)(2,1)S(1)} %get-tuple-element.149), channel_id=1, source_target_pairs={{0,11},{1,10},{2,9},{3,8},{4,15},{5,14},{6,13},{7,12},{8,3},{9,2},... | collective-permute-start | bytes 202760 | tf_op jit(solution)/shard_map/ppermute | solution.py:416
  89.8 2.5 %collective-permute-start.44 = (bf16[264,128]{1,0:T(8,128)(2,1)S(1)}, bf16[264,128]{1,0:T(8,128)(2,1)S(1)}, u32[]{:S(2)}, u32[]{:S(2)}) collective-permute-start(bf16[264,128]{1,0:T(8,128)(2,1)S(1)} %get-tuple-element.151), channel_id=1, source_target_pairs={{0,15},{1,14},{2,13},{3,12},{4,11},{5,10},{6,9},{7,8},{8,7},{9,6},... | collective-permute-start | bytes 202760 | tf_op jit(solution)/shard_map/ppermute | solution.py:416
  92.6 1.4 collective-permute-done.42.refs_13_
  94.1 1.2 collective-permute-done.43.refs_14_
  96.3 2.2 %cells.1 = (f32[64,8192]{1,0:T(8,128)S(1)}, f32[64,128]{1,0:T(8,128)S(1)}, bf16[264,128]{1,0:T(8,128)(2,1)S(1)}, bf16[264,128]{1,0:T(8,128)(2,1)S(1)}, bf16[264,...) custom-call(s32[16,128]{1,0:T(8,128)S(1)} %get-tuple-element.116.ask, ...), custom_call_target="tpu_custom_call" | custom-call | bytes 8388608 | tf_op jit(solution)/shard_map/cells/pallas_call | solution.py:458
  99.4 1.9 %collective-permute-start.46 = (bf16[264,128]{1,0:T(8,128)(2,1)S(1)}, bf16[264,128]{1,0:T(8,128)(2,1)S(1)}, u32[]{:S(2)}, u32[]{:S(2)}) collective-permute-start(bf16[264,128]{1,0:T(8,128)(2,1)S(1)} %get-tuple-element.156), channel_id=1, source_target_pairs={{0,4},{1,5},{2,6},{3,7},{4,0},{5,1},{6,2},{7,3},{8,12},{9,13},{10,... | collective-permute-start | bytes 202760 | tf_op jit(solution)/shard_map/ppermute | solution.py:416
  101.3 1.7 %collective-permute-start.47 = (bf16[264,128]{1,0:T(8,128)(2,1)S(1)}, bf16[264,128]{1,0:T(8,128)(2,1)S(1)}, u32[]{:S(2)}, u32[]{:S(2)}) collective-permute-start(bf16[264,128]{1,0:T(8,128)(2,1)S(1)} %get-tuple-element.157), channel_id=1, source_target_pairs={{0,12},{1,13},{2,14},{3,15},{4,8},{5,9},{6,10},{7,11},{8,4},{9,5},... | collective-permute-start | bytes 202760 | tf_op jit(solution)/shard_map/ppermute | solution.py:416
  103.0 2.9 %collective-permute-done.45.refs_1_ = bf16[264,128]{1,0:T(8,128)(2,1)S(1)} collective-permute-done((bf16[264,128]{1,0:T(8,128)(2,1)S(1)}, bf16[264,128]{1,0:T(8,128)(2,1)S(1)}, u32[]{:S(2)}, u32[]{:S(2)}) %collective-permute-start.45) | collective-permute-done | bytes 67616 | tf_op jit(solution)/shard_map/ppermute | solution.py:416
  105.9 1.7 collective-permute-start.51
  108.1 1.6 collective-permute-start.52
  109.7 2.9 %collective-permute-start.53 = (bf16[264,128]{1,0:T(8,128)(2,1)S(1)}, bf16[264,128]{1,0:T(8,128)(2,1)S(1)}, u32[]{:S(2)}, u32[]{:S(2)}) collective-permute-start(bf16[264,128]{1,0:T(8,128)(2,1)S(1)} %get-tuple-element.163), channel_id=1, source_target_pairs={{0,10},{1,11},{2,8},{3,9},{4,14},{5,15},{6,12},{7,13},{8,2},{9,3},... | collective-permute-start | bytes 202760 | tf_op jit(solution)/shard_map/ppermute | solution.py:416
  113.7 1.6 collective-permute-start.55
  116.3 1.9 %collective-permute-start.57 = (bf16[264,128]{1,0:T(8,128)(2,1)S(1)}, bf16[264,128]{1,0:T(8,128)(2,1)S(1)}, u32[]{:S(2)}, u32[]{:S(2)}) collective-permute-start(bf16[264,128]{1,0:T(8,128)(2,1)S(1)} %get-tuple-element.167), channel_id=1, source_target_pairs={{0,11},{1,10},{2,9},{3,8},{4,15},{5,14},{6,13},{7,12},{8,3},{9,2},... | collective-permute-start | bytes 202760 | tf_op jit(solution)/shard_map/ppermute | solution.py:416
  119.4 2.3 %collective-permute-start.59 = (bf16[264,128]{1,0:T(8,128)(2,1)S(1)}, bf16[264,128]{1,0:T(8,128)(2,1)S(1)}, u32[]{:S(2)}, u32[]{:S(2)}) collective-permute-start(bf16[264,128]{1,0:T(8,128)(2,1)S(1)} %get-tuple-element.169), channel_id=1, source_target_pairs={{0,15},{1,14},{2,13},{3,12},{4,11},{5,10},{6,9},{7,8},{8,7},{9,6},... | collective-permute-start | bytes 202760 | tf_op jit(solution)/shard_map/ppermute | solution.py:416
  121.6 2.2 %collective-permute-done.57.refs_13_ = bf16[264,128]{1,0:T(8,128)(2,1)S(1)} collective-permute-done((bf16[264,128]{1,0:T(8,128)(2,1)S(1)}, bf16[264,128]{1,0:T(8,128)(2,1)S(1)}, u32[]{:S(2)}, u32[]{:S(2)}) %collective-permute-start.57) | collective-permute-done | bytes 67616 | tf_op jit(solution)/shard_map/ppermute | solution.py:416
  124.2 1.6 collective-permute-done.59.refs_15_
  125.9 3.5 %pairs_last.1 = (bf16[264,128]{1,0:T(8,128)(2,1)S(1)}, bf16[264,128]{1,0:T(8,128)(2,1)S(1)}, bf16[264,128]{1,0:T(8,128)(2,1)S(1)}, bf16[264,128]{1,0:T(8,128)(2,...) custom-call(s32[128]{0:T(128)S(1)} %get-tuple-element.117.target_ref, ...), custom_call_target="tpu_custom_call" | custom-call | flops 536870912 | bytes 8388608 | tf_op jit(solution)/shard_map/pairs_last/pallas_call | solution.py:449
  129.3 1.9 %collective-permute-start.60 = (bf16[264,128]{1,0:T(8,128)(2,1)S(1)}, bf16[264,128]{1,0:T(8,128)(2,1)S(1)}, u32[]{:S(2)}, u32[]{:S(2)}) collective-permute-start(bf16[264,128]{1,0:T(8,128)(2,1)S(1)} %get-tuple-element.174), channel_id=1, source_target_pairs={{0,8},{1,9},{2,10},{3,11},{4,12},{5,13},{6,14},{7,15},{8,0},{9,1},... | collective-permute-start | bytes 202760 | tf_op jit(solution)/shard_map/ppermute | solution.py:416
  132.0 1.8 %collective-permute-start.62 = (bf16[264,128]{1,0:T(8,128)(2,1)S(1)}, bf16[264,128]{1,0:T(8,128)(2,1)S(1)}, u32[]{:S(2)}, u32[]{:S(2)}) collective-permute-start(bf16[264,128]{1,0:T(8,128)(2,1)S(1)} %get-tuple-element.176), channel_id=1, source_target_pairs={{0,12},{1,13},{2,14},{3,15},{4,8},{5,9},{6,10},{7,11},{8,4},{9,5},... | collective-permute-start | bytes 202760 | tf_op jit(solution)/shard_map/ppermute | solution.py:416
  134.9 1.6 collective-permute-done.60.refs_1_
  136.5 1.4 collective-permute-done.61.refs_2_
  138.6 2.2 %collective-permute-start.67 = (bf16[264,128]{1,0:T(8,128)(2,1)S(1)}, bf16[264,128]{1,0:T(8,128)(2,1)S(1)}, u32[]{:S(2)}, u32[]{:S(2)}) collective-permute-start(bf16[264,128]{1,0:T(8,128)(2,1)S(1)} %get-tuple-element.181), channel_id=1, source_target_pairs={{0,2},{1,3},{2,0},{3,1},{4,6},{5,7},{6,4},{7,5},{8,10},{9,11},{10,... | collective-permute-start | bytes 202760 | tf_op jit(solution)/shard_map/ppermute | solution.py:416
  140.8 2.8 %collective-permute-start.68 = (bf16[264,128]{1,0:T(8,128)(2,1)S(1)}, bf16[264,128]{1,0:T(8,128)(2,1)S(1)}, u32[]{:S(2)}, u32[]{:S(2)}) collective-permute-start(bf16[264,128]{1,0:T(8,128)(2,1)S(1)} %get-tuple-element.182), channel_id=1, source_target_pairs={{0,10},{1,11},{2,8},{3,9},{4,14},{5,15},{6,12},{7,13},{8,2},{9,3},... | collective-permute-start | bytes 202760 | tf_op jit(solution)/shard_map/ppermute | solution.py:416
  143.7 2.6 %collective-permute-start.70 = (bf16[264,128]{1,0:T(8,128)(2,1)S(1)}, bf16[264,128]{1,0:T(8,128)(2,1)S(1)}, u32[]{:S(2)}, u32[]{:S(2)}) collective-permute-start(bf16[264,128]{1,0:T(8,128)(2,1)S(1)} %get-tuple-element.184), channel_id=1, source_target_pairs={{0,14},{1,15},{2,12},{3,13},{4,10},{5,11},{6,8},{7,9},{8,6},{9,7},... | collective-permute-start | bytes 202760 | tf_op jit(solution)/shard_map/ppermute | solution.py:416
  146.5 2.8 %collective-permute-start.72 = (bf16[264,128]{1,0:T(8,128)(2,1)S(1)}, bf16[264,128]{1,0:T(8,128)(2,1)S(1)}, u32[]{:S(2)}, u32[]{:S(2)}) collective-permute-start(bf16[264,128]{1,0:T(8,128)(2,1)S(1)} %get-tuple-element.186), channel_id=1, source_target_pairs={{0,11},{1,10},{2,9},{3,8},{4,15},{5,14},{6,13},{7,12},{8,3},{9,2},... | collective-permute-start | bytes 202760 | tf_op jit(solution)/shard_map/ppermute | solution.py:416
  149.6 1.5 collective-permute-done.69.refs_10_
  151.1 1.4 collective-permute-start.74
  152.5 2.4 %collective-permute-done.72.refs_13_ = bf16[264,128]{1,0:T(8,128)(2,1)S(1)} collective-permute-done((bf16[264,128]{1,0:T(8,128)(2,1)S(1)}, bf16[264,128]{1,0:T(8,128)(2,1)S(1)}, u32[]{:S(2)}, u32[]{:S(2)}) %collective-permute-start.72) | collective-permute-done | bytes 67616 | tf_op jit(solution)/shard_map/ppermute | solution.py:416
  155.7 2.0 %collective-permute-done.74.refs_15_ = bf16[264,128]{1,0:T(8,128)(2,1)S(1)} collective-permute-done((bf16[264,128]{1,0:T(8,128)(2,1)S(1)}, bf16[264,128]{1,0:T(8,128)(2,1)S(1)}, u32[]{:S(2)}, u32[]{:S(2)}) %collective-permute-start.74) | collective-permute-done | bytes 67616 | tf_op jit(solution)/shard_map/ppermute | solution.py:416
  157.8 1.9 %cells_last.1 = (f32[64,8192]{1,0:T(8,128)S(1)}, f32[64,128]{1,0:T(8,128)S(1)}, f32[8,128]{1,0:T(8,128)S(1)}) custom-call(s32[16,128]{1,0:T(8,128)S(1)} %get-tuple-element.116.asked_ref, bf16[264,128]{1,0:T(8,128)(2,1)S(1)} %get-tuple-element.173.refs_0_, bf16[264,128]{1,0:T(8,128)(2,1)S(1)} %collective-permute-done.60.refs_1_, ...), custom_call_target="tpu_custom_call" | custom-call | bytes 8388608 | tf_op jit(solution)/shard_map/cells_last/pallas_call | solution.py:464
  160.4 3.7 %collective-permute-start.75 = (f32[8,128]{1,0:T(8,128)S(1)}, f32[8,128]{1,0:T(8,128)S(1)}, u32[]{:S(2)}, u32[]{:S(2)}) collective-permute-start(f32[8,128]{1,0:T(8,128)S(1)} %get-tuple-element.190), channel_id=1, source_target_pairs={{0,4},{1,5},{2,6},{3,7},{4,0},{5,1},{6,2},{7,3},{8,12},{9,13},{10,... | collective-permute-start | bytes 12296 | tf_op jit(solution)/shard_map/ppermute | solution.py:474
  165.9 1.7 collective-permute-start.78
  167.6 1.5 estimate.1
  169.4 1.5 model.1
  (114 shorter events, 25.9 us)
Async XLA Ops:
  5.8 7.6 %collective-permute-start = (bf16[264,128]{1,0:T(8,128)(2,1)}, bf16[264,128]{1,0:T(8,128)(2,1)S(1)}, u32[]{:S(2)}, u32[]{:S(2)}) collective-permute-start(bf16[264,128]{1,0:T(8,128)(2,1)} %get-tuple-element.100), channel_id=1, source_target_pairs={{0,8},{1,9},{2,10},{3,11},{4,12},{5,13},{6,14},{7,15},{8,0},{9,1},... | collective-permute-start | bytes 202760 | tf_op jit(solution)/shard_map/ppermute | solution.py:416
  11.5 7.1 %collective-permute-start.2 = (bf16[264,128]{1,0:T(8,128)(2,1)}, bf16[264,128]{1,0:T(8,128)(2,1)S(1)}, u32[]{:S(2)}, u32[]{:S(2)}) collective-permute-start(bf16[264,128]{1,0:T(8,128)(2,1)} %get-tuple-element.102), channel_id=1, source_target_pairs={{0,12},{1,13},{2,14},{3,15},{4,8},{5,9},{6,10},{7,11},{8,4},{9,5},... | collective-permute-start | bytes 202760 | tf_op jit(solution)/shard_map/ppermute | solution.py:416
  11.5 8.5 %collective-permute-start.3 = (bf16[264,128]{1,0:T(8,128)(2,1)}, bf16[264,128]{1,0:T(8,128)(2,1)S(1)}, u32[]{:S(2)}, u32[]{:S(2)}) collective-permute-start(bf16[264,128]{1,0:T(8,128)(2,1)} %get-tuple-element.103), channel_id=1, source_target_pairs={{0,1},{1,0},{2,3},{3,2},{4,5},{5,4},{6,7},{7,6},{8,9},{9,8},{10,11... | collective-permute-start | bytes 202760 | tf_op jit(solution)/shard_map/ppermute | solution.py:416
  11.5 11.1 %collective-permute-start.4 = (bf16[264,128]{1,0:T(8,128)(2,1)}, bf16[264,128]{1,0:T(8,128)(2,1)S(1)}, u32[]{:S(2)}, u32[]{:S(2)}) collective-permute-start(bf16[264,128]{1,0:T(8,128)(2,1)} %get-tuple-element.104), channel_id=1, source_target_pairs={{0,9},{1,8},{2,11},{3,10},{4,13},{5,12},{6,15},{7,14},{8,1},{9,0},... | collective-permute-start | bytes 202760 | tf_op jit(solution)/shard_map/ppermute | solution.py:416
  13.5 10.2 %collective-permute-start.5 = (bf16[264,128]{1,0:T(8,128)(2,1)}, bf16[264,128]{1,0:T(8,128)(2,1)S(1)}, u32[]{:S(2)}, u32[]{:S(2)}) collective-permute-start(bf16[264,128]{1,0:T(8,128)(2,1)} %get-tuple-element.105), channel_id=1, source_target_pairs={{0,5},{1,4},{2,7},{3,6},{4,1},{5,0},{6,3},{7,2},{8,13},{9,12},{10,... | collective-permute-start | bytes 202760 | tf_op jit(solution)/shard_map/ppermute | solution.py:416
  15.6 10.8 %collective-permute-start.6 = (bf16[264,128]{1,0:T(8,128)(2,1)}, bf16[264,128]{1,0:T(8,128)(2,1)S(1)}, u32[]{:S(2)}, u32[]{:S(2)}) collective-permute-start(bf16[264,128]{1,0:T(8,128)(2,1)} %get-tuple-element.106), channel_id=1, source_target_pairs={{0,13},{1,12},{2,15},{3,14},{4,9},{5,8},{6,11},{7,10},{8,5},{9,4},... | collective-permute-start | bytes 202760 | tf_op jit(solution)/shard_map/ppermute | solution.py:416
  18.6 9.0 %collective-permute-start.7 = (bf16[264,128]{1,0:T(8,128)(2,1)}, bf16[264,128]{1,0:T(8,128)(2,1)S(1)}, u32[]{:S(2)}, u32[]{:S(2)}) collective-permute-start(bf16[264,128]{1,0:T(8,128)(2,1)} %get-tuple-element.107), channel_id=1, source_target_pairs={{0,2},{1,3},{2,0},{3,1},{4,6},{5,7},{6,4},{7,5},{8,10},{9,11},{10,... | collective-permute-start | bytes 202760 | tf_op jit(solution)/shard_map/ppermute | solution.py:416
  20.0 8.1 %collective-permute-start.8 = (bf16[264,128]{1,0:T(8,128)(2,1)}, bf16[264,128]{1,0:T(8,128)(2,1)S(1)}, u32[]{:S(2)}, u32[]{:S(2)}) collective-permute-start(bf16[264,128]{1,0:T(8,128)(2,1)} %get-tuple-element.108), channel_id=1, source_target_pairs={{0,10},{1,11},{2,8},{3,9},{4,14},{5,15},{6,12},{7,13},{8,2},{9,3},... | collective-permute-start | bytes 202760 | tf_op jit(solution)/shard_map/ppermute | solution.py:416
  22.6 6.5 %collective-permute-start.9 = (bf16[264,128]{1,0:T(8,128)(2,1)}, bf16[264,128]{1,0:T(8,128)(2,1)S(1)}, u32[]{:S(2)}, u32[]{:S(2)}) collective-permute-start(bf16[264,128]{1,0:T(8,128)(2,1)} %get-tuple-element.109), channel_id=1, source_target_pairs={{0,6},{1,7},{2,4},{3,5},{4,2},{5,3},{6,0},{7,1},{8,14},{9,15},{10,... | collective-permute-start | bytes 202760 | tf_op jit(solution)/shard_map/ppermute | solution.py:416
  23.7 13.3 %collective-permute-start.10 = (bf16[264,128]{1,0:T(8,128)(2,1)}, bf16[264,128]{1,0:T(8,128)(2,1)S(1)}, u32[]{:S(2)}, u32[]{:S(2)}) collective-permute-start(bf16[264,128]{1,0:T(8,128)(2,1)} %get-tuple-element.110), channel_id=1, source_target_pairs={{0,14},{1,15},{2,12},{3,13},{4,10},{5,11},{6,8},{7,9},{8,6},{9,7},... | collective-permute-start | bytes 202760 | tf_op jit(solution)/shard_map/ppermute | solution.py:416
  26.4 10.6 %collective-permute-start.11 = (bf16[264,128]{1,0:T(8,128)(2,1)}, bf16[264,128]{1,0:T(8,128)(2,1)S(1)}, u32[]{:S(2)}, u32[]{:S(2)}) collective-permute-start(bf16[264,128]{1,0:T(8,128)(2,1)} %get-tuple-element.111), channel_id=1, source_target_pairs={{0,3},{1,2},{2,1},{3,0},{4,7},{5,6},{6,5},{7,4},{8,11},{9,10},{10,... | collective-permute-start | bytes 202760 | tf_op jit(solution)/shard_map/ppermute | solution.py:416
  27.5 9.5 %collective-permute-start.12 = (bf16[264,128]{1,0:T(8,128)(2,1)}, bf16[264,128]{1,0:T(8,128)(2,1)S(1)}, u32[]{:S(2)}, u32[]{:S(2)}) collective-permute-start(bf16[264,128]{1,0:T(8,128)(2,1)} %get-tuple-element.112), channel_id=1, source_target_pairs={{0,11},{1,10},{2,9},{3,8},{4,15},{5,14},{6,13},{7,12},{8,3},{9,2},... | collective-permute-start | bytes 202760 | tf_op jit(solution)/shard_map/ppermute | solution.py:416
  28.2 8.9 %collective-permute-start.13 = (bf16[264,128]{1,0:T(8,128)(2,1)}, bf16[264,128]{1,0:T(8,128)(2,1)S(1)}, u32[]{:S(2)}, u32[]{:S(2)}) collective-permute-start(bf16[264,128]{1,0:T(8,128)(2,1)} %get-tuple-element.113), channel_id=1, source_target_pairs={{0,7},{1,6},{2,5},{3,4},{4,3},{5,2},{6,1},{7,0},{8,15},{9,14},{10,... | collective-permute-start | bytes 202760 | tf_op jit(solution)/shard_map/ppermute | solution.py:416
  29.1 8.0 %collective-permute-start.14 = (bf16[264,128]{1,0:T(8,128)(2,1)}, bf16[264,128]{1,0:T(8,128)(2,1)S(1)}, u32[]{:S(2)}, u32[]{:S(2)}) collective-permute-start(bf16[264,128]{1,0:T(8,128)(2,1)} %get-tuple-element.114), channel_id=1, source_target_pairs={{0,15},{1,14},{2,13},{3,12},{4,11},{5,10},{6,9},{7,8},{8,7},{9,6},... | collective-permute-start | bytes 202760 | tf_op jit(solution)/shard_map/ppermute | solution.py:416
  39.6 7.1 %collective-permute-start.15 = (bf16[264,128]{1,0:T(8,128)(2,1)S(1)}, bf16[264,128]{1,0:T(8,128)(2,1)S(1)}, u32[]{:S(2)}, u32[]{:S(2)}) collective-permute-start(bf16[264,128]{1,0:T(8,128)(2,1)S(1)} %get-tuple-element.119), channel_id=1, source_target_pairs={{0,8},{1,9},{2,10},{3,11},{4,12},{5,13},{6,14},{7,15},{8,0},{9,1},... | collective-permute-start | bytes 202760 | tf_op jit(solution)/shard_map/ppermute | solution.py:416
  39.7 7.2 %collective-permute-start.16 = (bf16[264,128]{1,0:T(8,128)(2,1)S(1)}, bf16[264,128]{1,0:T(8,128)(2,1)S(1)}, u32[]{:S(2)}, u32[]{:S(2)}) collective-permute-start(bf16[264,128]{1,0:T(8,128)(2,1)S(1)} %get-tuple-element.120), channel_id=1, source_target_pairs={{0,4},{1,5},{2,6},{3,7},{4,0},{5,1},{6,2},{7,3},{8,12},{9,13},{10,... | collective-permute-start | bytes 202760 | tf_op jit(solution)/shard_map/ppermute | solution.py:416
  42.7 6.8 %collective-permute-start.17 = (bf16[264,128]{1,0:T(8,128)(2,1)S(1)}, bf16[264,128]{1,0:T(8,128)(2,1)S(1)}, u32[]{:S(2)}, u32[]{:S(2)}) collective-permute-start(bf16[264,128]{1,0:T(8,128)(2,1)S(1)} %get-tuple-element.121), channel_id=1, source_target_pairs={{0,12},{1,13},{2,14},{3,15},{4,8},{5,9},{6,10},{7,11},{8,4},{9,5},... | collective-permute-start | bytes 202760 | tf_op jit(solution)/shard_map/ppermute | solution.py:416
  44.0 9.0 %collective-permute-start.19 = (bf16[264,128]{1,0:T(8,128)(2,1)S(1)}, bf16[264,128]{1,0:T(8,128)(2,1)S(1)}, u32[]{:S(2)}, u32[]{:S(2)}) collective-permute-start(bf16[264,128]{1,0:T(8,128)(2,1)S(1)} %get-tuple-element.123), channel_id=1, source_target_pairs={{0,9},{1,8},{2,11},{3,10},{4,13},{5,12},{6,15},{7,14},{8,1},{9,0},... | collective-permute-start | bytes 202760 | tf_op jit(solution)/shard_map/ppermute | solution.py:416
  46.7 6.8 %collective-permute-start.20 = (bf16[264,128]{1,0:T(8,128)(2,1)S(1)}, bf16[264,128]{1,0:T(8,128)(2,1)S(1)}, u32[]{:S(2)}, u32[]{:S(2)}) collective-permute-start(bf16[264,128]{1,0:T(8,128)(2,1)S(1)} %get-tuple-element.124), channel_id=1, source_target_pairs={{0,5},{1,4},{2,7},{3,6},{4,1},{5,0},{6,3},{7,2},{8,13},{9,12},{10,... | collective-permute-start | bytes 202760 | tf_op jit(solution)/shard_map/ppermute | solution.py:416
  46.8 9.5 %collective-permute-start.21 = (bf16[264,128]{1,0:T(8,128)(2,1)S(1)}, bf16[264,128]{1,0:T(8,128)(2,1)S(1)}, u32[]{:S(2)}, u32[]{:S(2)}) collective-permute-start(bf16[264,128]{1,0:T(8,128)(2,1)S(1)} %get-tuple-element.125), channel_id=1, source_target_pairs={{0,13},{1,12},{2,15},{3,14},{4,9},{5,8},{6,11},{7,10},{8,5},{9,4},... | collective-permute-start | bytes 202760 | tf_op jit(solution)/shard_map/ppermute | solution.py:416
  49.6 6.8 %collective-permute-start.22 = (bf16[264,128]{1,0:T(8,128)(2,1)S(1)}, bf16[264,128]{1,0:T(8,128)(2,1)S(1)}, u32[]{:S(2)}, u32[]{:S(2)}) collective-permute-start(bf16[264,128]{1,0:T(8,128)(2,1)S(1)} %get-tuple-element.126), channel_id=1, source_target_pairs={{0,2},{1,3},{2,0},{3,1},{4,6},{5,7},{6,4},{7,5},{8,10},{9,11},{10,... | collective-permute-start | bytes 202760 | tf_op jit(solution)/shard_map/ppermute | solution.py:416
  49.6 9.0 %collective-permute-start.23 = (bf16[264,128]{1,0:T(8,128)(2,1)S(1)}, bf16[264,128]{1,0:T(8,128)(2,1)S(1)}, u32[]{:S(2)}, u32[]{:S(2)}) collective-permute-start(bf16[264,128]{1,0:T(8,128)(2,1)S(1)} %get-tuple-element.127), channel_id=1, source_target_pairs={{0,10},{1,11},{2,8},{3,9},{4,14},{5,15},{6,12},{7,13},{8,2},{9,3},... | collective-permute-start | bytes 202760 | tf_op jit(solution)/shard_map/ppermute | solution.py:416
  53.5 9.0 %collective-permute-start.25 = (bf16[264,128]{1,0:T(8,128)(2,1)S(1)}, bf16[264,128]{1,0:T(8,128)(2,1)S(1)}, u32[]{:S(2)}, u32[]{:S(2)}) collective-permute-start(bf16[264,128]{1,0:T(8,128)(2,1)S(1)} %get-tuple-element.129), channel_id=1, source_target_pairs={{0,14},{1,15},{2,12},{3,13},{4,10},{5,11},{6,8},{7,9},{8,6},{9,7},... | collective-permute-start | bytes 202760 | tf_op jit(solution)/shard_map/ppermute | solution.py:416
  56.3 8.2 %collective-permute-start.26 = (bf16[264,128]{1,0:T(8,128)(2,1)S(1)}, bf16[264,128]{1,0:T(8,128)(2,1)S(1)}, u32[]{:S(2)}, u32[]{:S(2)}) collective-permute-start(bf16[264,128]{1,0:T(8,128)(2,1)S(1)} %get-tuple-element.130), channel_id=1, source_target_pairs={{0,3},{1,2},{2,1},{3,0},{4,7},{5,6},{6,5},{7,4},{8,11},{9,10},{10,... | collective-permute-start | bytes 202760 | tf_op jit(solution)/shard_map/ppermute | solution.py:416
  56.3 8.2 %collective-permute-start.27 = (bf16[264,128]{1,0:T(8,128)(2,1)S(1)}, bf16[264,128]{1,0:T(8,128)(2,1)S(1)}, u32[]{:S(2)}, u32[]{:S(2)}) collective-permute-start(bf16[264,128]{1,0:T(8,128)(2,1)S(1)} %get-tuple-element.131), channel_id=1, source_target_pairs={{0,11},{1,10},{2,9},{3,8},{4,15},{5,14},{6,13},{7,12},{8,3},{9,2},... | collective-permute-start | bytes 202760 | tf_op jit(solution)/shard_map/ppermute | solution.py:416
  59.5 6.6 %collective-permute-start.29 = (bf16[264,128]{1,0:T(8,128)(2,1)S(1)}, bf16[264,128]{1,0:T(8,128)(2,1)S(1)}, u32[]{:S(2)}, u32[]{:S(2)}) collective-permute-start(bf16[264,128]{1,0:T(8,128)(2,1)S(1)} %get-tuple-element.133), channel_id=1, source_target_pairs={{0,15},{1,14},{2,13},{3,12},{4,11},{5,10},{6,9},{7,8},{8,7},{9,6},... | collective-permute-start | bytes 202760 | tf_op jit(solution)/shard_map/ppermute | solution.py:416
  69.6 7.1 %collective-permute-start.30 = (bf16[264,128]{1,0:T(8,128)(2,1)S(1)}, bf16[264,128]{1,0:T(8,128)(2,1)S(1)}, u32[]{:S(2)}, u32[]{:S(2)}) collective-permute-start(bf16[264,128]{1,0:T(8,128)(2,1)S(1)} %get-tuple-element.137), channel_id=1, source_target_pairs={{0,8},{1,9},{2,10},{3,11},{4,12},{5,13},{6,14},{7,15},{8,0},{9,1},... | collective-permute-start | bytes 202760 | tf_op jit(solution)/shard_map/ppermute | solution.py:416
  70.2 7.5 %collective-permute-start.31 = (bf16[264,128]{1,0:T(8,128)(2,1)S(1)}, bf16[264,128]{1,0:T(8,128)(2,1)S(1)}, u32[]{:S(2)}, u32[]{:S(2)}) collective-permute-start(bf16[264,128]{1,0:T(8,128)(2,1)S(1)} %get-tuple-element.138), channel_id=1, source_target_pairs={{0,4},{1,5},{2,6},{3,7},{4,0},{5,1},{6,2},{7,3},{8,12},{9,13},{10,... | collective-permute-start | bytes 202760 | tf_op jit(solution)/shard_map/ppermute | solution.py:416
  72.7 6.7 %collective-permute-start.32 = (bf16[264,128]{1,0:T(8,128)(2,1)S(1)}, bf16[264,128]{1,0:T(8,128)(2,1)S(1)}, u32[]{:S(2)}, u32[]{:S(2)}) collective-permute-start(bf16[264,128]{1,0:T(8,128)(2,1)S(1)} %get-tuple-element.139), channel_id=1, source_target_pairs={{0,12},{1,13},{2,14},{3,15},{4,8},{5,9},{6,10},{7,11},{8,4},{9,5},... | collective-permute-start | bytes 202760 | tf_op jit(solution)/shard_map/ppermute | solution.py:416
  74.0 9.9 %collective-permute-start.34 = (bf16[264,128]{1,0:T(8,128)(2,1)S(1)}, bf16[264,128]{1,0:T(8,128)(2,1)S(1)}, u32[]{:S(2)}, u32[]{:S(2)}) collective-permute-start(bf16[264,128]{1,0:T(8,128)(2,1)S(1)} %get-tuple-element.141), channel_id=1, source_target_pairs={{0,9},{1,8},{2,11},{3,10},{4,13},{5,12},{6,15},{7,14},{8,1},{9,0},... | collective-permute-start | bytes 202760 | tf_op jit(solution)/shard_map/ppermute | solution.py:416
  76.7 7.3 %collective-permute-start.35 = (bf16[264,128]{1,0:T(8,128)(2,1)S(1)}, bf16[264,128]{1,0:T(8,128)(2,1)S(1)}, u32[]{:S(2)}, u32[]{:S(2)}) collective-permute-start(bf16[264,128]{1,0:T(8,128)(2,1)S(1)} %get-tuple-element.142), channel_id=1, source_target_pairs={{0,5},{1,4},{2,7},{3,6},{4,1},{5,0},{6,3},{7,2},{8,13},{9,12},{10,... | collective-permute-start | bytes 202760 | tf_op jit(solution)/shard_map/ppermute | solution.py:416
  77.6 8.5 %collective-permute-start.36 = (bf16[264,128]{1,0:T(8,128)(2,1)S(1)}, bf16[264,128]{1,0:T(8,128)(2,1)S(1)}, u32[]{:S(2)}, u32[]{:S(2)}) collective-permute-start(bf16[264,128]{1,0:T(8,128)(2,1)S(1)} %get-tuple-element.143), channel_id=1, source_target_pairs={{0,13},{1,12},{2,15},{3,14},{4,9},{5,8},{6,11},{7,10},{8,5},{9,4},... | collective-permute-start | bytes 202760 | tf_op jit(solution)/shard_map/ppermute | solution.py:416
  79.3 7.5 %collective-permute-start.37 = (bf16[264,128]{1,0:T(8,128)(2,1)S(1)}, bf16[264,128]{1,0:T(8,128)(2,1)S(1)}, u32[]{:S(2)}, u32[]{:S(2)}) collective-permute-start(bf16[264,128]{1,0:T(8,128)(2,1)S(1)} %get-tuple-element.144), channel_id=1, source_target_pairs={{0,2},{1,3},{2,0},{3,1},{4,6},{5,7},{6,4},{7,5},{8,10},{9,11},{10,... | collective-permute-start | bytes 202760 | tf_op jit(solution)/shard_map/ppermute | solution.py:416
  79.9 9.6 %collective-permute-start.38 = (bf16[264,128]{1,0:T(8,128)(2,1)S(1)}, bf16[264,128]{1,0:T(8,128)(2,1)S(1)}, u32[]{:S(2)}, u32[]{:S(2)}) collective-permute-start(bf16[264,128]{1,0:T(8,128)(2,1)S(1)} %get-tuple-element.145), channel_id=1, source_target_pairs={{0,10},{1,11},{2,8},{3,9},{4,14},{5,15},{6,12},{7,13},{8,2},{9,3},... | collective-permute-start | bytes 202760 | tf_op jit(solution)/shard_map/ppermute | solution.py:416
  83.9 8.4 %collective-permute-start.40 = (bf16[264,128]{1,0:T(8,128)(2,1)S(1)}, bf16[264,128]{1,0:T(8,128)(2,1)S(1)}, u32[]{:S(2)}, u32[]{:S(2)}) collective-permute-start(bf16[264,128]{1,0:T(8,128)(2,1)S(1)} %get-tuple-element.147), channel_id=1, source_target_pairs={{0,14},{1,15},{2,12},{3,13},{4,10},{5,11},{6,8},{7,9},{8,6},{9,7},... | collective-permute-start | bytes 202760 | tf_op jit(solution)/shard_map/ppermute | solution.py:416
  86.1 6.5 %collective-permute-start.41 = (bf16[264,128]{1,0:T(8,128)(2,1)S(1)}, bf16[264,128]{1,0:T(8,128)(2,1)S(1)}, u32[]{:S(2)}, u32[]{:S(2)}) collective-permute-start(bf16[264,128]{1,0:T(8,128)(2,1)S(1)} %get-tuple-element.148), channel_id=1, source_target_pairs={{0,3},{1,2},{2,1},{3,0},{4,7},{5,6},{6,5},{7,4},{8,11},{9,10},{10,... | collective-permute-start | bytes 202760 | tf_op jit(solution)/shard_map/ppermute | solution.py:416
  86.9 7.2 %collective-permute-start.42 = (bf16[264,128]{1,0:T(8,128)(2,1)S(1)}, bf16[264,128]{1,0:T(8,128)(2,1)S(1)}, u32[]{:S(2)}, u32[]{:S(2)}) collective-permute-start(bf16[264,128]{1,0:T(8,128)(2,1)S(1)} %get-tuple-element.149), channel_id=1, source_target_pairs={{0,11},{1,10},{2,9},{3,8},{4,15},{5,14},{6,13},{7,12},{8,3},{9,2},... | collective-permute-start | bytes 202760 | tf_op jit(solution)/shard_map/ppermute | solution.py:416
  89.8 6.5 %collective-permute-start.44 = (bf16[264,128]{1,0:T(8,128)(2,1)S(1)}, bf16[264,128]{1,0:T(8,128)(2,1)S(1)}, u32[]{:S(2)}, u32[]{:S(2)}) collective-permute-start(bf16[264,128]{1,0:T(8,128)(2,1)S(1)} %get-tuple-element.151), channel_id=1, source_target_pairs={{0,15},{1,14},{2,13},{3,12},{4,11},{5,10},{6,9},{7,8},{8,7},{9,6},... | collective-permute-start | bytes 202760 | tf_op jit(solution)/shard_map/ppermute | solution.py:416
  98.6 7.4 %collective-permute-start.45 = (bf16[264,128]{1,0:T(8,128)(2,1)S(1)}, bf16[264,128]{1,0:T(8,128)(2,1)S(1)}, u32[]{:S(2)}, u32[]{:S(2)}) collective-permute-start(bf16[264,128]{1,0:T(8,128)(2,1)S(1)} %get-tuple-element.155), channel_id=1, source_target_pairs={{0,8},{1,9},{2,10},{3,11},{4,12},{5,13},{6,14},{7,15},{8,0},{9,1},... | collective-permute-start | bytes 202760 | tf_op jit(solution)/shard_map/ppermute | solution.py:416
  99.4 6.5 %collective-permute-start.46 = (bf16[264,128]{1,0:T(8,128)(2,1)S(1)}, bf16[264,128]{1,0:T(8,128)(2,1)S(1)}, u32[]{:S(2)}, u32[]{:S(2)}) collective-permute-start(bf16[264,128]{1,0:T(8,128)(2,1)S(1)} %get-tuple-element.156), channel_id=1, source_target_pairs={{0,4},{1,5},{2,6},{3,7},{4,0},{5,1},{6,2},{7,3},{8,12},{9,13},{10,... | collective-permute-start | bytes 202760 | tf_op jit(solution)/shard_map/ppermute | solution.py:416
  101.3 6.8 %collective-permute-start.47 = (bf16[264,128]{1,0:T(8,128)(2,1)S(1)}, bf16[264,128]{1,0:T(8,128)(2,1)S(1)}, u32[]{:S(2)}, u32[]{:S(2)}) collective-permute-start(bf16[264,128]{1,0:T(8,128)(2,1)S(1)} %get-tuple-element.157), channel_id=1, source_target_pairs={{0,12},{1,13},{2,14},{3,15},{4,8},{5,9},{6,10},{7,11},{8,4},{9,5},... | collective-permute-start | bytes 202760 | tf_op jit(solution)/shard_map/ppermute | solution.py:416
  103.0 6.6 %collective-permute-start.48 = (bf16[264,128]{1,0:T(8,128)(2,1)S(1)}, bf16[264,128]{1,0:T(8,128)(2,1)S(1)}, u32[]{:S(2)}, u32[]{:S(2)}) collective-permute-start(bf16[264,128]{1,0:T(8,128)(2,1)S(1)} %get-tuple-element.158), channel_id=1, source_target_pairs={{0,1},{1,0},{2,3},{3,2},{4,5},{5,4},{6,7},{7,6},{8,9},{9,8},{10,11... | collective-permute-start | bytes 202760 | tf_op jit(solution)/shard_map/ppermute | solution.py:416
  103.0 9.6 %collective-permute-start.49 = (bf16[264,128]{1,0:T(8,128)(2,1)S(1)}, bf16[264,128]{1,0:T(8,128)(2,1)S(1)}, u32[]{:S(2)}, u32[]{:S(2)}) collective-permute-start(bf16[264,128]{1,0:T(8,128)(2,1)S(1)} %get-tuple-element.159), channel_id=1, source_target_pairs={{0,9},{1,8},{2,11},{3,10},{4,13},{5,12},{6,15},{7,14},{8,1},{9,0},... | collective-permute-start | bytes 202760 | tf_op jit(solution)/shard_map/ppermute | solution.py:416
  105.9 7.8 %collective-permute-start.50 = (bf16[264,128]{1,0:T(8,128)(2,1)S(1)}, bf16[264,128]{1,0:T(8,128)(2,1)S(1)}, u32[]{:S(2)}, u32[]{:S(2)}) collective-permute-start(bf16[264,128]{1,0:T(8,128)(2,1)S(1)} %get-tuple-element.160), channel_id=1, source_target_pairs={{0,5},{1,4},{2,7},{3,6},{4,1},{5,0},{6,3},{7,2},{8,13},{9,12},{10,... | collective-permute-start | bytes 202760 | tf_op jit(solution)/shard_map/ppermute | solution.py:416
  105.9 9.3 %collective-permute-start.51 = (bf16[264,128]{1,0:T(8,128)(2,1)S(1)}, bf16[264,128]{1,0:T(8,128)(2,1)S(1)}, u32[]{:S(2)}, u32[]{:S(2)}) collective-permute-start(bf16[264,128]{1,0:T(8,128)(2,1)S(1)} %get-tuple-element.161), channel_id=1, source_target_pairs={{0,13},{1,12},{2,15},{3,14},{4,9},{5,8},{6,11},{7,10},{8,5},{9,4},... | collective-permute-start | bytes 202760 | tf_op jit(solution)/shard_map/ppermute | solution.py:416
  108.1 8.2 %collective-permute-start.52 = (bf16[264,128]{1,0:T(8,128)(2,1)S(1)}, bf16[264,128]{1,0:T(8,128)(2,1)S(1)}, u32[]{:S(2)}, u32[]{:S(2)}) collective-permute-start(bf16[264,128]{1,0:T(8,128)(2,1)S(1)} %get-tuple-element.162), channel_id=1, source_target_pairs={{0,2},{1,3},{2,0},{3,1},{4,6},{5,7},{6,4},{7,5},{8,10},{9,11},{10,... | collective-permute-start | bytes 202760 | tf_op jit(solution)/shard_map/ppermute | solution.py:416
  109.7 8.5 %collective-permute-start.53 = (bf16[264,128]{1,0:T(8,128)(2,1)S(1)}, bf16[264,128]{1,0:T(8,128)(2,1)S(1)}, u32[]{:S(2)}, u32[]{:S(2)}) collective-permute-start(bf16[264,128]{1,0:T(8,128)(2,1)S(1)} %get-tuple-element.163), channel_id=1, source_target_pairs={{0,10},{1,11},{2,8},{3,9},{4,14},{5,15},{6,12},{7,13},{8,2},{9,3},... | collective-permute-start | bytes 202760 | tf_op jit(solution)/shard_map/ppermute | solution.py:416
  112.6 6.7 %collective-permute-start.54 = (bf16[264,128]{1,0:T(8,128)(2,1)S(1)}, bf16[264,128]{1,0:T(8,128)(2,1)S(1)}, u32[]{:S(2)}, u32[]{:S(2)}) collective-permute-start(bf16[264,128]{1,0:T(8,128)(2,1)S(1)} %get-tuple-element.164), channel_id=1, source_target_pairs={{0,6},{1,7},{2,4},{3,5},{4,2},{5,3},{6,0},{7,1},{8,14},{9,15},{10,... | collective-permute-start | bytes 202760 | tf_op jit(solution)/shard_map/ppermute | solution.py:416
  113.7 7.9 %collective-permute-start.55 = (bf16[264,128]{1,0:T(8,128)(2,1)S(1)}, bf16[264,128]{1,0:T(8,128)(2,1)S(1)}, u32[]{:S(2)}, u32[]{:S(2)}) collective-permute-start(bf16[264,128]{1,0:T(8,128)(2,1)S(1)} %get-tuple-element.165), channel_id=1, source_target_pairs={{0,14},{1,15},{2,12},{3,13},{4,10},{5,11},{6,8},{7,9},{8,6},{9,7},... | collective-permute-start | bytes 202760 | tf_op jit(solution)/shard_map/ppermute | solution.py:416
  116.3 7.5 %collective-permute-start.57 = (bf16[264,128]{1,0:T(8,128)(2,1)S(1)}, bf16[264,128]{1,0:T(8,128)(2,1)S(1)}, u32[]{:S(2)}, u32[]{:S(2)}) collective-permute-start(bf16[264,128]{1,0:T(8,128)(2,1)S(1)} %get-tuple-element.167), channel_id=1, source_target_pairs={{0,11},{1,10},{2,9},{3,8},{4,15},{5,14},{6,13},{7,12},{8,3},{9,2},... | collective-permute-start | bytes 202760 | tf_op jit(solution)/shard_map/ppermute | solution.py:416
  119.4 6.5 %collective-permute-start.59 = (bf16[264,128]{1,0:T(8,128)(2,1)S(1)}, bf16[264,128]{1,0:T(8,128)(2,1)S(1)}, u32[]{:S(2)}, u32[]{:S(2)}) collective-permute-start(bf16[264,128]{1,0:T(8,128)(2,1)S(1)} %get-tuple-element.169), channel_id=1, source_target_pairs={{0,15},{1,14},{2,13},{3,12},{4,11},{5,10},{6,9},{7,8},{8,7},{9,6},... | collective-permute-start | bytes 202760 | tf_op jit(solution)/shard_map/ppermute | solution.py:416
  129.3 7.1 %collective-permute-start.60 = (bf16[264,128]{1,0:T(8,128)(2,1)S(1)}, bf16[264,128]{1,0:T(8,128)(2,1)S(1)}, u32[]{:S(2)}, u32[]{:S(2)}) collective-permute-start(bf16[264,128]{1,0:T(8,128)(2,1)S(1)} %get-tuple-element.174), channel_id=1, source_target_pairs={{0,8},{1,9},{2,10},{3,11},{4,12},{5,13},{6,14},{7,15},{8,0},{9,1},... | collective-permute-start | bytes 202760 | tf_op jit(solution)/shard_map/ppermute | solution.py:416
  131.3 6.6 %collective-permute-start.61 = (bf16[264,128]{1,0:T(8,128)(2,1)S(1)}, bf16[264,128]{1,0:T(8,128)(2,1)S(1)}, u32[]{:S(2)}, u32[]{:S(2)}) collective-permute-start(bf16[264,128]{1,0:T(8,128)(2,1)S(1)} %get-tuple-element.175), channel_id=1, source_target_pairs={{0,4},{1,5},{2,6},{3,7},{4,0},{5,1},{6,2},{7,3},{8,12},{9,13},{10,... | collective-permute-start | bytes 202760 | tf_op jit(solution)/shard_map/ppermute | solution.py:416
  132.0 6.7 %collective-permute-start.62 = (bf16[264,128]{1,0:T(8,128)(2,1)S(1)}, bf16[264,128]{1,0:T(8,128)(2,1)S(1)}, u32[]{:S(2)}, u32[]{:S(2)}) collective-permute-start(bf16[264,128]{1,0:T(8,128)(2,1)S(1)} %get-tuple-element.176), channel_id=1, source_target_pairs={{0,12},{1,13},{2,14},{3,15},{4,8},{5,9},{6,10},{7,11},{8,4},{9,5},... | collective-permute-start | bytes 202760 | tf_op jit(solution)/shard_map/ppermute | solution.py:416
  133.8 7.0 %collective-permute-start.63 = (bf16[264,128]{1,0:T(8,128)(2,1)S(1)}, bf16[264,128]{1,0:T(8,128)(2,1)S(1)}, u32[]{:S(2)}, u32[]{:S(2)}) collective-permute-start(bf16[264,128]{1,0:T(8,128)(2,1)S(1)} %get-tuple-element.177), channel_id=1, source_target_pairs={{0,1},{1,0},{2,3},{3,2},{4,5},{5,4},{6,7},{7,6},{8,9},{9,8},{10,11... | collective-permute-start | bytes 202760 | tf_op jit(solution)/shard_map/ppermute | solution.py:416
  133.8 9.9 %collective-permute-start.64 = (bf16[264,128]{1,0:T(8,128)(2,1)S(1)}, bf16[264,128]{1,0:T(8,128)(2,1)S(1)}, u32[]{:S(2)}, u32[]{:S(2)}) collective-permute-start(bf16[264,128]{1,0:T(8,128)(2,1)S(1)} %get-tuple-element.178), channel_id=1, source_target_pairs={{0,9},{1,8},{2,11},{3,10},{4,13},{5,12},{6,15},{7,14},{8,1},{9,0},... | collective-permute-start | bytes 202760 | tf_op jit(solution)/shard_map/ppermute | solution.py:416
  136.5 7.3 %collective-permute-start.65 = (bf16[264,128]{1,0:T(8,128)(2,1)S(1)}, bf16[264,128]{1,0:T(8,128)(2,1)S(1)}, u32[]{:S(2)}, u32[]{:S(2)}) collective-permute-start(bf16[264,128]{1,0:T(8,128)(2,1)S(1)} %get-tuple-element.179), channel_id=1, source_target_pairs={{0,5},{1,4},{2,7},{3,6},{4,1},{5,0},{6,3},{7,2},{8,13},{9,12},{10,... | collective-permute-start | bytes 202760 | tf_op jit(solution)/shard_map/ppermute | solution.py:416
  137.9 8.4 %collective-permute-start.66 = (bf16[264,128]{1,0:T(8,128)(2,1)S(1)}, bf16[264,128]{1,0:T(8,128)(2,1)S(1)}, u32[]{:S(2)}, u32[]{:S(2)}) collective-permute-start(bf16[264,128]{1,0:T(8,128)(2,1)S(1)} %get-tuple-element.180), channel_id=1, source_target_pairs={{0,13},{1,12},{2,15},{3,14},{4,9},{5,8},{6,11},{7,10},{8,5},{9,4},... | collective-permute-start | bytes 202760 | tf_op jit(solution)/shard_map/ppermute | solution.py:416
  138.6 7.9 %collective-permute-start.67 = (bf16[264,128]{1,0:T(8,128)(2,1)S(1)}, bf16[264,128]{1,0:T(8,128)(2,1)S(1)}, u32[]{:S(2)}, u32[]{:S(2)}) collective-permute-start(bf16[264,128]{1,0:T(8,128)(2,1)S(1)} %get-tuple-element.181), channel_id=1, source_target_pairs={{0,2},{1,3},{2,0},{3,1},{4,6},{5,7},{6,4},{7,5},{8,10},{9,11},{10,... | collective-permute-start | bytes 202760 | tf_op jit(solution)/shard_map/ppermute | solution.py:416
  140.8 8.5 %collective-permute-start.68 = (bf16[264,128]{1,0:T(8,128)(2,1)S(1)}, bf16[264,128]{1,0:T(8,128)(2,1)S(1)}, u32[]{:S(2)}, u32[]{:S(2)}) collective-permute-start(bf16[264,128]{1,0:T(8,128)(2,1)S(1)} %get-tuple-element.182), channel_id=1, source_target_pairs={{0,10},{1,11},{2,8},{3,9},{4,14},{5,15},{6,12},{7,13},{8,2},{9,3},... | collective-permute-start | bytes 202760 | tf_op jit(solution)/shard_map/ppermute | solution.py:416
  143.7 7.4 %collective-permute-start.69 = (bf16[264,128]{1,0:T(8,128)(2,1)S(1)}, bf16[264,128]{1,0:T(8,128)(2,1)S(1)}, u32[]{:S(2)}, u32[]{:S(2)}) collective-permute-start(bf16[264,128]{1,0:T(8,128)(2,1)S(1)} %get-tuple-element.183), channel_id=1, source_target_pairs={{0,6},{1,7},{2,4},{3,5},{4,2},{5,3},{6,0},{7,1},{8,14},{9,15},{10,... | collective-permute-start | bytes 202760 | tf_op jit(solution)/shard_map/ppermute | solution.py:416
  143.7 8.8 %collective-permute-start.70 = (bf16[264,128]{1,0:T(8,128)(2,1)S(1)}, bf16[264,128]{1,0:T(8,128)(2,1)S(1)}, u32[]{:S(2)}, u32[]{:S(2)}) collective-permute-start(bf16[264,128]{1,0:T(8,128)(2,1)S(1)} %get-tuple-element.184), channel_id=1, source_target_pairs={{0,14},{1,15},{2,12},{3,13},{4,10},{5,11},{6,8},{7,9},{8,6},{9,7},... | collective-permute-start | bytes 202760 | tf_op jit(solution)/shard_map/ppermute | solution.py:416
  146.5 8.4 %collective-permute-start.72 = (bf16[264,128]{1,0:T(8,128)(2,1)S(1)}, bf16[264,128]{1,0:T(8,128)(2,1)S(1)}, u32[]{:S(2)}, u32[]{:S(2)}) collective-permute-start(bf16[264,128]{1,0:T(8,128)(2,1)S(1)} %get-tuple-element.186), channel_id=1, source_target_pairs={{0,11},{1,10},{2,9},{3,8},{4,15},{5,14},{6,13},{7,12},{8,3},{9,2},... | collective-permute-start | bytes 202760 | tf_op jit(solution)/shard_map/ppermute | solution.py:416
  151.1 6.7 %collective-permute-start.74 = (bf16[264,128]{1,0:T(8,128)(2,1)S(1)}, bf16[264,128]{1,0:T(8,128)(2,1)S(1)}, u32[]{:S(2)}, u32[]{:S(2)}) collective-permute-start(bf16[264,128]{1,0:T(8,128)(2,1)S(1)} %get-tuple-element.188), channel_id=1, source_target_pairs={{0,15},{1,14},{2,13},{3,12},{4,11},{5,10},{6,9},{7,8},{8,7},{9,6},... | collective-permute-start | bytes 202760 | tf_op jit(solution)/shard_map/ppermute | solution.py:416
  (20 other events, 125.8 us)

commit v24 on v23

--- a/solution.py
+++ b/solution.py
@@ -24,7 +24,7 @@
 def steps_of(peers):
     half, quarter = peers // 2, peers // 4
     near = [step for low in range(quarter) for step in (low, quarter + low)][1:]
-    return [0, half] + [step for low in near for step in (low, half + low)]
+    return [0] + [step for low in near for step in (low, half + low)] + [half]
 
 
 def diagonal(cols):

time: 171 us -> 176 us (1.029)
  starting transfers between devices: 106 us -> 118 us
  waiting for transfers between devices: 38.3 us -> 30.2 us
    ppermute x75, starting transfers between devices: 99.4 us -> 112 us  [exchange(): lax.ppermute(value, 'pair', [(one, one ^ step) for one in range(peers)])]
    ppermute x75, waiting for transfers between devices: 36.3 us -> 27.5 us  [exchange(): lax.ppermute(value, 'pair', [(one, one ^ step) for one in range(peers)])]
  transfers between devices with their start and end apart: 81 -> 81, of which waited for: 31 -> 20; matrix products, arithmetic and copies ran while one was open for 0% -> 0% of each run, Pallas kernels for 3% -> 2%
where the time goes in v24:
time: 176 us
  starting transfers between devices  118 us (67%)
  waiting for transfers between devices  30.2 us (17%)
  Pallas kernels  24.5 us (14%)
    ppermute x75, starting transfers between devices, exchange(): lax.ppermute(value, 'pair', [(one, one ^ step) for one in range(peers)])  112 us
    ppermute x75, waiting for transfers between devices, exchange(): lax.ppermute(value, 'pair', [(one, one ^ step) for one in range(peers)])  27.5 us
    pallas_call x2, Pallas kernels, on_device(): call(functools.partial(pair_kernel, peers), 'pairs_last' if last else 'pa...  6.91 us
    ppermute x6, starting transfers between devices, on_device(): lax.ppermute(share, 'pair', [(one, one ^ step) for one in range(peers)])  6.37 us
    pallas_call x1, Pallas kernels, on_device(): call(functools.partial(start_kernel, peers), 'start', [SMEM, HBM, HBM, HB...  5.2 us
  transfers between devices with their start and end apart: 81, of which 20 were waited for; matrix products, arithmetic and copies ran while one was open for 0% of the time, Pallas kernels for 2%

profile of v24, /device:TPU:0, one launch (start us, length us, event | category | flops | bytes accessed | tf_op | source)
XLA Modules:
  0.0 175.7 jit_solution(7174612892304669272)
XLA Ops:
  0.6 5.2 %start.1 = (bf16[264,128]{1,0:T(8,128)(2,1)}, bf16[264,128]{1,0:T(8,128)(2,1)}, bf16[264,128]{1,0:T(8,128)(2,1)}, bf16[264,128]{1,0:T(8,128)(2,1)}, bf16[264,128...) custom-call(s32[1]{0:T(128)} %bitcast.me_ref, ...), custom_call_target="tpu_custom_call" | custom-call | flops 268435456 | bytes 6291456 | tf_op jit(solution)/shard_map/start/pallas_call | solution.py:421
  5.8 3.1 %collective-permute-start = (bf16[264,128]{1,0:T(8,128)(2,1)}, bf16[264,128]{1,0:T(8,128)(2,1)S(1)}, u32[]{:S(2)}, u32[]{:S(2)}) collective-permute-start(bf16[264,128]{1,0:T(8,128)(2,1)} %get-tuple-element.100), channel_id=1, source_target_pairs={{0,4},{1,5},{2,6},{3,7},{4,0},{5,1},{6,2},{7,3},{8,12},{9,13},{10,... | collective-permute-start | bytes 202760 | tf_op jit(solution)/shard_map/ppermute | solution.py:416
  8.9 2.5 %collective-permute-start.1 = (bf16[264,128]{1,0:T(8,128)(2,1)}, bf16[264,128]{1,0:T(8,128)(2,1)S(1)}, u32[]{:S(2)}, u32[]{:S(2)}) collective-permute-start(bf16[264,128]{1,0:T(8,128)(2,1)} %get-tuple-element.101), channel_id=1, source_target_pairs={{0,12},{1,13},{2,14},{3,15},{4,8},{5,9},{6,10},{7,11},{8,4},{9,5},... | collective-permute-start | bytes 202760 | tf_op jit(solution)/shard_map/ppermute | solution.py:416
  11.6 1.4 collective-permute-start.4
  13.1 2.6 %collective-permute-start.5 = (bf16[264,128]{1,0:T(8,128)(2,1)}, bf16[264,128]{1,0:T(8,128)(2,1)S(1)}, u32[]{:S(2)}, u32[]{:S(2)}) collective-permute-start(bf16[264,128]{1,0:T(8,128)(2,1)} %get-tuple-element.105), channel_id=1, source_target_pairs={{0,13},{1,12},{2,15},{3,14},{4,9},{5,8},{6,11},{7,10},{8,5},{9,4},... | collective-permute-start | bytes 202760 | tf_op jit(solution)/shard_map/ppermute | solution.py:416
  15.7 1.4 collective-permute-start.6
  17.1 2.5 %collective-permute-start.7 = (bf16[264,128]{1,0:T(8,128)(2,1)}, bf16[264,128]{1,0:T(8,128)(2,1)S(1)}, u32[]{:S(2)}, u32[]{:S(2)}) collective-permute-start(bf16[264,128]{1,0:T(8,128)(2,1)} %get-tuple-element.107), channel_id=1, source_target_pairs={{0,10},{1,11},{2,8},{3,9},{4,14},{5,15},{6,12},{7,13},{8,2},{9,3},... | collective-permute-start | bytes 202760 | tf_op jit(solution)/shard_map/ppermute | solution.py:416
  19.6 1.7 collective-permute-start.8
  21.3 1.3 collective-permute-start.9
  23.5 1.6 collective-permute-start.11
  25.2 1.4 collective-permute-start.12
  26.5 2.6 %collective-permute-start.13 = (bf16[264,128]{1,0:T(8,128)(2,1)}, bf16[264,128]{1,0:T(8,128)(2,1)S(1)}, u32[]{:S(2)}, u32[]{:S(2)}) collective-permute-start(bf16[264,128]{1,0:T(8,128)(2,1)} %get-tuple-element.113), channel_id=1, source_target_pairs={{0,15},{1,14},{2,13},{3,12},{4,11},{5,10},{6,9},{7,8},{8,7},{9,6},... | collective-permute-start | bytes 202760 | tf_op jit(solution)/shard_map/ppermute | solution.py:416
  30.8 2.9 %keep.1 = (s32[128]{0:T(128)S(1)}, bf16[264,128]{1,0:T(8,128)(2,1)S(1)}, bf16[8,16,128,128]{3,2,1,0:T(8,128)(2,1)S(1)}) custom-call(s32[128]{0:T(128)S(1)} %copy-done.2, bf16[264,128]{1,0:T(8,128)(2,1)S(1)} %copy-done.1, bf16[8,16,128,128]{3,2,1,0:T(8,128)(2,1)} %rays_hbm.3), custom_call_target="tpu_custom_call" | custom-call | bytes 8388608 | tf_op jit(solution)/shard_map/keep/pallas_call | solution.py:433
  33.7 3.1 %collective-permute-done.14.refs_15_ = bf16[264,128]{1,0:T(8,128)(2,1)S(1)} collective-permute-done((bf16[264,128]{1,0:T(8,128)(2,1)}, bf16[264,128]{1,0:T(8,128)(2,1)S(1)}, u32[]{:S(2)}, u32[]{:S(2)}) %collective-permute-start.14) | collective-permute-done | bytes 67616 | tf_op jit(solution)/shard_map/ppermute | solution.py:416
  36.8 2.4 %cells_first.1 = (f32[64,8192]{1,0:T(8,128)S(1)}, f32[64,128]{1,0:T(8,128)S(1)}, bf16[264,128]{1,0:T(8,128)(2,1)S(1)}, bf16[264,128]{1,0:T(8,128)(2,1)S(1)}, bf1...) custom-call(bf16[264,128]{1,0:T(8,128)(2,1)S(1)} %get-tuple-element., ...), custom_call_target="tpu_custom_call" | custom-call | bytes 6291456 | tf_op jit(solution)/shard_map/cells_first/pallas_call | solution.py:438
  39.3 2.4 %collective-permute-start.16 = (bf16[264,128]{1,0:T(8,128)(2,1)S(1)}, bf16[264,128]{1,0:T(8,128)(2,1)S(1)}, u32[]{:S(2)}, u32[]{:S(2)}) collective-permute-start(bf16[264,128]{1,0:T(8,128)(2,1)S(1)} %get-tuple-element.120), channel_id=1, source_target_pairs={{0,12},{1,13},{2,14},{3,15},{4,8},{5,9},{6,10},{7,11},{8,4},{9,5},... | collective-permute-start | bytes 202760 | tf_op jit(solution)/shard_map/ppermute | solution.py:416
  43.6 2.4 %collective-permute-start.20 = (bf16[264,128]{1,0:T(8,128)(2,1)S(1)}, bf16[264,128]{1,0:T(8,128)(2,1)S(1)}, u32[]{:S(2)}, u32[]{:S(2)}) collective-permute-start(bf16[264,128]{1,0:T(8,128)(2,1)S(1)} %get-tuple-element.124), channel_id=1, source_target_pairs={{0,13},{1,12},{2,15},{3,14},{4,9},{5,8},{6,11},{7,10},{8,5},{9,4},... | collective-permute-start | bytes 202760 | tf_op jit(solution)/shard_map/ppermute | solution.py:416
  47.2 3.9 %collective-permute-start.22 = (bf16[264,128]{1,0:T(8,128)(2,1)S(1)}, bf16[264,128]{1,0:T(8,128)(2,1)S(1)}, u32[]{:S(2)}, u32[]{:S(2)}) collective-permute-start(bf16[264,128]{1,0:T(8,128)(2,1)S(1)} %get-tuple-element.126), channel_id=1, source_target_pairs={{0,10},{1,11},{2,8},{3,9},{4,14},{5,15},{6,12},{7,13},{8,2},{9,3},... | collective-permute-start | bytes 202760 | tf_op jit(solution)/shard_map/ppermute | solution.py:416
  51.1 2.6 %collective-permute-start.24 = (bf16[264,128]{1,0:T(8,128)(2,1)S(1)}, bf16[264,128]{1,0:T(8,128)(2,1)S(1)}, u32[]{:S(2)}, u32[]{:S(2)}) collective-permute-start(bf16[264,128]{1,0:T(8,128)(2,1)S(1)} %get-tuple-element.128), channel_id=1, source_target_pairs={{0,14},{1,15},{2,12},{3,13},{4,10},{5,11},{6,8},{7,9},{8,6},{9,7},... | collective-permute-start | bytes 202760 | tf_op jit(solution)/shard_map/ppermute | solution.py:416
  54.8 1.9 %collective-permute-start.26 = (bf16[264,128]{1,0:T(8,128)(2,1)S(1)}, bf16[264,128]{1,0:T(8,128)(2,1)S(1)}, u32[]{:S(2)}, u32[]{:S(2)}) collective-permute-start(bf16[264,128]{1,0:T(8,128)(2,1)S(1)} %get-tuple-element.130), channel_id=1, source_target_pairs={{0,11},{1,10},{2,9},{3,8},{4,15},{5,14},{6,13},{7,12},{8,3},{9,2},... | collective-permute-start | bytes 202760 | tf_op jit(solution)/shard_map/ppermute | solution.py:416
  57.6 2.3 %collective-permute-start.28 = (bf16[264,128]{1,0:T(8,128)(2,1)S(1)}, bf16[264,128]{1,0:T(8,128)(2,1)S(1)}, u32[]{:S(2)}, u32[]{:S(2)}) collective-permute-start(bf16[264,128]{1,0:T(8,128)(2,1)S(1)} %get-tuple-element.132), channel_id=1, source_target_pairs={{0,15},{1,14},{2,13},{3,12},{4,11},{5,10},{6,9},{7,8},{8,7},{9,6},... | collective-permute-start | bytes 202760 | tf_op jit(solution)/shard_map/ppermute | solution.py:416
  59.9 2.5 %collective-permute-start.29 = (bf16[264,128]{1,0:T(8,128)(2,1)S(1)}, bf16[264,128]{1,0:T(8,128)(2,1)S(1)}, u32[]{:S(2)}, u32[]{:S(2)}) collective-permute-start(bf16[264,128]{1,0:T(8,128)(2,1)S(1)} %get-tuple-element.133), channel_id=1, source_target_pairs={{0,8},{1,9},{2,10},{3,11},{4,12},{5,13},{6,14},{7,15},{8,0},{9,1},... | collective-permute-start | bytes 202760 | tf_op jit(solution)/shard_map/ppermute | solution.py:416
  62.9 1.7 collective-permute-done.28.refs_14_
  64.5 3.4 %collective-permute-done.29.refs_15_ = bf16[264,128]{1,0:T(8,128)(2,1)S(1)} collective-permute-done((bf16[264,128]{1,0:T(8,128)(2,1)S(1)}, bf16[264,128]{1,0:T(8,128)(2,1)S(1)}, u32[]{:S(2)}, u32[]{:S(2)}) %collective-permute-start.29) | collective-permute-done | bytes 67616 | tf_op jit(solution)/shard_map/ppermute | solution.py:416
  67.9 3.5 %pairs.1 = (bf16[264,128]{1,0:T(8,128)(2,1)S(1)}, bf16[264,128]{1,0:T(8,128)(2,1)S(1)}, bf16[264,128]{1,0:T(8,128)(2,1)S(1)}, bf16[264,128]{1,0:T(8,128)(2,1)S(1...) custom-call(s32[128]{0:T(128)S(1)} %get-tuple-element.117.target_ref, ...), custom_call_target="tpu_custom_call" | custom-call | flops 536870912 | bytes 8388608 | tf_op jit(solution)/shard_map/pairs/pallas_call | solution.py:449
  71.5 2.2 %collective-permute-start.31 = (bf16[264,128]{1,0:T(8,128)(2,1)S(1)}, bf16[264,128]{1,0:T(8,128)(2,1)S(1)}, u32[]{:S(2)}, u32[]{:S(2)}) collective-permute-start(bf16[264,128]{1,0:T(8,128)(2,1)S(1)} %get-tuple-element.138), channel_id=1, source_target_pairs={{0,12},{1,13},{2,14},{3,15},{4,8},{5,9},{6,10},{7,11},{8,4},{9,5},... | collective-permute-start | bytes 202760 | tf_op jit(solution)/shard_map/ppermute | solution.py:416
  73.7 1.4 collective-permute-start.33
  75.8 2.1 %collective-permute-start.35 = (bf16[264,128]{1,0:T(8,128)(2,1)S(1)}, bf16[264,128]{1,0:T(8,128)(2,1)S(1)}, u32[]{:S(2)}, u32[]{:S(2)}) collective-permute-start(bf16[264,128]{1,0:T(8,128)(2,1)S(1)} %get-tuple-element.142), channel_id=1, source_target_pairs={{0,13},{1,12},{2,15},{3,14},{4,9},{5,8},{6,11},{7,10},{8,5},{9,4},... | collective-permute-start | bytes 202760 | tf_op jit(solution)/shard_map/ppermute | solution.py:416
  78.6 3.9 %collective-permute-start.37 = (bf16[264,128]{1,0:T(8,128)(2,1)S(1)}, bf16[264,128]{1,0:T(8,128)(2,1)S(1)}, u32[]{:S(2)}, u32[]{:S(2)}) collective-permute-start(bf16[264,128]{1,0:T(8,128)(2,1)S(1)} %get-tuple-element.144), channel_id=1, source_target_pairs={{0,10},{1,11},{2,8},{3,9},{4,14},{5,15},{6,12},{7,13},{8,2},{9,3},... | collective-permute-start | bytes 202760 | tf_op jit(solution)/shard_map/ppermute | solution.py:416
  82.8 2.1 %collective-permute-start.39 = (bf16[264,128]{1,0:T(8,128)(2,1)S(1)}, bf16[264,128]{1,0:T(8,128)(2,1)S(1)}, u32[]{:S(2)}, u32[]{:S(2)}) collective-permute-start(bf16[264,128]{1,0:T(8,128)(2,1)S(1)} %get-tuple-element.146), channel_id=1, source_target_pairs={{0,14},{1,15},{2,12},{3,13},{4,10},{5,11},{6,8},{7,9},{8,6},{9,7},... | collective-permute-start | bytes 202760 | tf_op jit(solution)/shard_map/ppermute | solution.py:416
  86.2 1.9 %collective-permute-start.41 = (bf16[264,128]{1,0:T(8,128)(2,1)S(1)}, bf16[264,128]{1,0:T(8,128)(2,1)S(1)}, u32[]{:S(2)}, u32[]{:S(2)}) collective-permute-start(bf16[264,128]{1,0:T(8,128)(2,1)S(1)} %get-tuple-element.148), channel_id=1, source_target_pairs={{0,11},{1,10},{2,9},{3,8},{4,15},{5,14},{6,13},{7,12},{8,3},{9,2},... | collective-permute-start | bytes 202760 | tf_op jit(solution)/shard_map/ppermute | solution.py:416
  89.1 2.0 %collective-permute-start.43 = (bf16[264,128]{1,0:T(8,128)(2,1)S(1)}, bf16[264,128]{1,0:T(8,128)(2,1)S(1)}, u32[]{:S(2)}, u32[]{:S(2)}) collective-permute-start(bf16[264,128]{1,0:T(8,128)(2,1)S(1)} %get-tuple-element.150), channel_id=1, source_target_pairs={{0,15},{1,14},{2,13},{3,12},{4,11},{5,10},{6,9},{7,8},{8,7},{9,6},... | collective-permute-start | bytes 202760 | tf_op jit(solution)/shard_map/ppermute | solution.py:416
  91.1 1.6 collective-permute-start.44
  92.7 1.7 collective-permute-done.41.refs_12_
  94.5 1.5 collective-permute-done.43.refs_14_
  96.0 3.5 %collective-permute-done.44.refs_15_ = bf16[264,128]{1,0:T(8,128)(2,1)S(1)} collective-permute-done((bf16[264,128]{1,0:T(8,128)(2,1)S(1)}, bf16[264,128]{1,0:T(8,128)(2,1)S(1)}, u32[]{:S(2)}, u32[]{:S(2)}) %collective-permute-start.44) | collective-permute-done | bytes 67616 | tf_op jit(solution)/shard_map/ppermute | solution.py:416
  99.5 2.2 %cells.1 = (f32[64,8192]{1,0:T(8,128)S(1)}, f32[64,128]{1,0:T(8,128)S(1)}, bf16[264,128]{1,0:T(8,128)(2,1)S(1)}, bf16[264,128]{1,0:T(8,128)(2,1)S(1)}, bf16[264,...) custom-call(s32[16,128]{1,0:T(8,128)S(1)} %get-tuple-element.116.ask, ...), custom_call_target="tpu_custom_call" | custom-call | bytes 8388608 | tf_op jit(solution)/shard_map/cells/pallas_call | solution.py:458
  101.9 2.1 %collective-permute-start.46 = (bf16[264,128]{1,0:T(8,128)(2,1)S(1)}, bf16[264,128]{1,0:T(8,128)(2,1)S(1)}, u32[]{:S(2)}, u32[]{:S(2)}) collective-permute-start(bf16[264,128]{1,0:T(8,128)(2,1)S(1)} %get-tuple-element.156), channel_id=1, source_target_pairs={{0,12},{1,13},{2,14},{3,15},{4,8},{5,9},{6,10},{7,11},{8,4},{9,5},... | collective-permute-start | bytes 202760 | tf_op jit(solution)/shard_map/ppermute | solution.py:416
  104.0 1.5 collective-permute-start.48
  106.1 2.1 %collective-permute-start.50 = (bf16[264,128]{1,0:T(8,128)(2,1)S(1)}, bf16[264,128]{1,0:T(8,128)(2,1)S(1)}, u32[]{:S(2)}, u32[]{:S(2)}) collective-permute-start(bf16[264,128]{1,0:T(8,128)(2,1)S(1)} %get-tuple-element.160), channel_id=1, source_target_pairs={{0,13},{1,12},{2,15},{3,14},{4,9},{5,8},{6,11},{7,10},{8,5},{9,4},... | collective-permute-start | bytes 202760 | tf_op jit(solution)/shard_map/ppermute | solution.py:416
  109.4 3.6 %collective-permute-start.52 = (bf16[264,128]{1,0:T(8,128)(2,1)S(1)}, bf16[264,128]{1,0:T(8,128)(2,1)S(1)}, u32[]{:S(2)}, u32[]{:S(2)}) collective-permute-start(bf16[264,128]{1,0:T(8,128)(2,1)S(1)} %get-tuple-element.162), channel_id=1, source_target_pairs={{0,10},{1,11},{2,8},{3,9},{4,14},{5,15},{6,12},{7,13},{8,2},{9,3},... | collective-permute-start | bytes 202760 | tf_op jit(solution)/shard_map/ppermute | solution.py:416
  113.5 2.2 %collective-permute-start.54 = (bf16[264,128]{1,0:T(8,128)(2,1)S(1)}, bf16[264,128]{1,0:T(8,128)(2,1)S(1)}, u32[]{:S(2)}, u32[]{:S(2)}) collective-permute-start(bf16[264,128]{1,0:T(8,128)(2,1)S(1)} %get-tuple-element.164), channel_id=1, source_target_pairs={{0,14},{1,15},{2,12},{3,13},{4,10},{5,11},{6,8},{7,9},{8,6},{9,7},... | collective-permute-start | bytes 202760 | tf_op jit(solution)/shard_map/ppermute | solution.py:416
  116.7 1.9 %collective-permute-start.56 = (bf16[264,128]{1,0:T(8,128)(2,1)S(1)}, bf16[264,128]{1,0:T(8,128)(2,1)S(1)}, u32[]{:S(2)}, u32[]{:S(2)}) collective-permute-start(bf16[264,128]{1,0:T(8,128)(2,1)S(1)} %get-tuple-element.166), channel_id=1, source_target_pairs={{0,11},{1,10},{2,9},{3,8},{4,15},{5,14},{6,13},{7,12},{8,3},{9,2},... | collective-permute-start | bytes 202760 | tf_op jit(solution)/shard_map/ppermute | solution.py:416
  119.3 2.5 %collective-permute-start.58 = (bf16[264,128]{1,0:T(8,128)(2,1)S(1)}, bf16[264,128]{1,0:T(8,128)(2,1)S(1)}, u32[]{:S(2)}, u32[]{:S(2)}) collective-permute-start(bf16[264,128]{1,0:T(8,128)(2,1)S(1)} %get-tuple-element.168), channel_id=1, source_target_pairs={{0,15},{1,14},{2,13},{3,12},{4,11},{5,10},{6,9},{7,8},{8,7},{9,6},... | collective-permute-start | bytes 202760 | tf_op jit(solution)/shard_map/ppermute | solution.py:416
  121.9 1.4 collective-permute-start.59
  123.2 1.6 collective-permute-done.56.refs_12_
  124.8 1.6 collective-permute-done.58.refs_14_
  126.5 3.6 %collective-permute-done.59.refs_15_ = bf16[264,128]{1,0:T(8,128)(2,1)S(1)} collective-permute-done((bf16[264,128]{1,0:T(8,128)(2,1)S(1)}, bf16[264,128]{1,0:T(8,128)(2,1)S(1)}, u32[]{:S(2)}, u32[]{:S(2)}) %collective-permute-start.59) | collective-permute-done | bytes 67616 | tf_op jit(solution)/shard_map/ppermute | solution.py:416
  130.0 3.5 %pairs_last.1 = (bf16[264,128]{1,0:T(8,128)(2,1)S(1)}, bf16[264,128]{1,0:T(8,128)(2,1)S(1)}, bf16[264,128]{1,0:T(8,128)(2,1)S(1)}, bf16[264,128]{1,0:T(8,128)(2,...) custom-call(s32[128]{0:T(128)S(1)} %get-tuple-element.117.target_ref, ...), custom_call_target="tpu_custom_call" | custom-call | flops 536870912 | bytes 8388608 | tf_op jit(solution)/shard_map/pairs_last/pallas_call | solution.py:449
  133.5 2.0 %collective-permute-start.61 = (bf16[264,128]{1,0:T(8,128)(2,1)S(1)}, bf16[264,128]{1,0:T(8,128)(2,1)S(1)}, u32[]{:S(2)}, u32[]{:S(2)}) collective-permute-start(bf16[264,128]{1,0:T(8,128)(2,1)S(1)} %get-tuple-element.175), channel_id=1, source_target_pairs={{0,12},{1,13},{2,14},{3,15},{4,8},{5,9},{6,10},{7,11},{8,4},{9,5},... | collective-permute-start | bytes 202760 | tf_op jit(solution)/shard_map/ppermute | solution.py:416
  135.5 1.6 collective-permute-start.63
  137.8 1.9 %collective-permute-start.65 = (bf16[264,128]{1,0:T(8,128)(2,1)S(1)}, bf16[264,128]{1,0:T(8,128)(2,1)S(1)}, u32[]{:S(2)}, u32[]{:S(2)}) collective-permute-start(bf16[264,128]{1,0:T(8,128)(2,1)S(1)} %get-tuple-element.179), channel_id=1, source_target_pairs={{0,13},{1,12},{2,15},{3,14},{4,9},{5,8},{6,11},{7,10},{8,5},{9,4},... | collective-permute-start | bytes 202760 | tf_op jit(solution)/shard_map/ppermute | solution.py:416
  141.0 3.6 %collective-permute-start.67 = (bf16[264,128]{1,0:T(8,128)(2,1)S(1)}, bf16[264,128]{1,0:T(8,128)(2,1)S(1)}, u32[]{:S(2)}, u32[]{:S(2)}) collective-permute-start(bf16[264,128]{1,0:T(8,128)(2,1)S(1)} %get-tuple-element.181), channel_id=1, source_target_pairs={{0,10},{1,11},{2,8},{3,9},{4,14},{5,15},{6,12},{7,13},{8,2},{9,3},... | collective-permute-start | bytes 202760 | tf_op jit(solution)/shard_map/ppermute | solution.py:416
  144.6 2.7 %collective-permute-start.69 = (bf16[264,128]{1,0:T(8,128)(2,1)S(1)}, bf16[264,128]{1,0:T(8,128)(2,1)S(1)}, u32[]{:S(2)}, u32[]{:S(2)}) collective-permute-start(bf16[264,128]{1,0:T(8,128)(2,1)S(1)} %get-tuple-element.183), channel_id=1, source_target_pairs={{0,14},{1,15},{2,12},{3,13},{4,10},{5,11},{6,8},{7,9},{8,6},{9,7},... | collective-permute-start | bytes 202760 | tf_op jit(solution)/shard_map/ppermute | solution.py:416
  148.3 1.9 %collective-permute-start.71 = (bf16[264,128]{1,0:T(8,128)(2,1)S(1)}, bf16[264,128]{1,0:T(8,128)(2,1)S(1)}, u32[]{:S(2)}, u32[]{:S(2)}) collective-permute-start(bf16[264,128]{1,0:T(8,128)(2,1)S(1)} %get-tuple-element.185), channel_id=1, source_target_pairs={{0,11},{1,10},{2,9},{3,8},{4,15},{5,14},{6,13},{7,12},{8,3},{9,2},... | collective-permute-start | bytes 202760 | tf_op jit(solution)/shard_map/ppermute | solution.py:416
  151.2 2.3 %collective-permute-start.73 = (bf16[264,128]{1,0:T(8,128)(2,1)S(1)}, bf16[264,128]{1,0:T(8,128)(2,1)S(1)}, u32[]{:S(2)}, u32[]{:S(2)}) collective-permute-start(bf16[264,128]{1,0:T(8,128)(2,1)S(1)} %get-tuple-element.187), channel_id=1, source_target_pairs={{0,15},{1,14},{2,13},{3,12},{4,11},{5,10},{6,9},{7,8},{8,7},{9,6},... | collective-permute-start | bytes 202760 | tf_op jit(solution)/shard_map/ppermute | solution.py:416
  153.5 3.4 %collective-permute-start.74 = (bf16[264,128]{1,0:T(8,128)(2,1)S(1)}, bf16[264,128]{1,0:T(8,128)(2,1)S(1)}, u32[]{:S(2)}, u32[]{:S(2)}) collective-permute-start(bf16[264,128]{1,0:T(8,128)(2,1)S(1)} %get-tuple-element.188), channel_id=1, source_target_pairs={{0,8},{1,9},{2,10},{3,11},{4,12},{5,13},{6,14},{7,15},{8,0},{9,1},... | collective-permute-start | bytes 202760 | tf_op jit(solution)/shard_map/ppermute | solution.py:416
  156.9 1.4 collective-permute-done.73.refs_14_
  158.3 3.3 %collective-permute-done.74.refs_15_ = bf16[264,128]{1,0:T(8,128)(2,1)S(1)} collective-permute-done((bf16[264,128]{1,0:T(8,128)(2,1)S(1)}, bf16[264,128]{1,0:T(8,128)(2,1)S(1)}, u32[]{:S(2)}, u32[]{:S(2)}) %collective-permute-start.74) | collective-permute-done | bytes 67616 | tf_op jit(solution)/shard_map/ppermute | solution.py:416
  161.6 1.9 %cells_last.1 = (f32[64,8192]{1,0:T(8,128)S(1)}, f32[64,128]{1,0:T(8,128)S(1)}, f32[8,128]{1,0:T(8,128)S(1)}) custom-call(s32[16,128]{1,0:T(8,128)S(1)} %get-tuple-element.116.asked_ref, bf16[264,128]{1,0:T(8,128)(2,1)S(1)} %get-tuple-element.173.refs_0_, bf16[264,128]{1,0:T(8,128)(2,1)S(1)} %collective-permute-done.60.refs_1_, ...), custom_call_target="tpu_custom_call" | custom-call | bytes 8388608 | tf_op jit(solution)/shard_map/cells_last/pallas_call | solution.py:464
  163.5 2.3 %collective-permute-start.77 = (f32[8,128]{1,0:T(8,128)S(1)}, f32[8,128]{1,0:T(8,128)S(1)}, u32[]{:S(2)}, u32[]{:S(2)}) collective-permute-start(f32[8,128]{1,0:T(8,128)S(1)} %get-tuple-element.190), channel_id=1, source_target_pairs={{0,12},{1,13},{2,14},{3,15},{4,8},{5,9},{6,10},{7,11},{8,4},{9,5},... | collective-permute-start | bytes 12296 | tf_op jit(solution)/shard_map/ppermute | solution.py:474
  165.8 2.2 %collective-permute-start.75 = (f32[8,128]{1,0:T(8,128)S(1)}, f32[8,128]{1,0:T(8,128)S(1)}, u32[]{:S(2)}, u32[]{:S(2)}) collective-permute-start(f32[8,128]{1,0:T(8,128)S(1)} %get-tuple-element.190), channel_id=1, source_target_pairs={{0,4},{1,5},{2,6},{3,7},{4,0},{5,1},{6,2},{7,3},{8,12},{9,13},{10,... | collective-permute-start | bytes 12296 | tf_op jit(solution)/shard_map/ppermute | solution.py:474
  172.2 1.5 estimate.1
  174.0 1.5 model.1
  (114 shorter events, 25.1 us)
Async XLA Ops:
  5.8 7.2 %collective-permute-start = (bf16[264,128]{1,0:T(8,128)(2,1)}, bf16[264,128]{1,0:T(8,128)(2,1)S(1)}, u32[]{:S(2)}, u32[]{:S(2)}) collective-permute-start(bf16[264,128]{1,0:T(8,128)(2,1)} %get-tuple-element.100), channel_id=1, source_target_pairs={{0,4},{1,5},{2,6},{3,7},{4,0},{5,1},{6,2},{7,3},{8,12},{9,13},{10,... | collective-permute-start | bytes 202760 | tf_op jit(solution)/shard_map/ppermute | solution.py:416
  8.9 6.7 %collective-permute-start.1 = (bf16[264,128]{1,0:T(8,128)(2,1)}, bf16[264,128]{1,0:T(8,128)(2,1)S(1)}, u32[]{:S(2)}, u32[]{:S(2)}) collective-permute-start(bf16[264,128]{1,0:T(8,128)(2,1)} %get-tuple-element.101), channel_id=1, source_target_pairs={{0,12},{1,13},{2,14},{3,15},{4,8},{5,9},{6,10},{7,11},{8,4},{9,5},... | collective-permute-start | bytes 202760 | tf_op jit(solution)/shard_map/ppermute | solution.py:416
  11.4 8.1 %collective-permute-start.3 = (bf16[264,128]{1,0:T(8,128)(2,1)}, bf16[264,128]{1,0:T(8,128)(2,1)S(1)}, u32[]{:S(2)}, u32[]{:S(2)}) collective-permute-start(bf16[264,128]{1,0:T(8,128)(2,1)} %get-tuple-element.103), channel_id=1, source_target_pairs={{0,9},{1,8},{2,11},{3,10},{4,13},{5,12},{6,15},{7,14},{8,1},{9,0},... | collective-permute-start | bytes 202760 | tf_op jit(solution)/shard_map/ppermute | solution.py:416
  11.6 9.7 %collective-permute-start.4 = (bf16[264,128]{1,0:T(8,128)(2,1)}, bf16[264,128]{1,0:T(8,128)(2,1)S(1)}, u32[]{:S(2)}, u32[]{:S(2)}) collective-permute-start(bf16[264,128]{1,0:T(8,128)(2,1)} %get-tuple-element.104), channel_id=1, source_target_pairs={{0,5},{1,4},{2,7},{3,6},{4,1},{5,0},{6,3},{7,2},{8,13},{9,12},{10,... | collective-permute-start | bytes 202760 | tf_op jit(solution)/shard_map/ppermute | solution.py:416
  13.1 9.6 %collective-permute-start.5 = (bf16[264,128]{1,0:T(8,128)(2,1)}, bf16[264,128]{1,0:T(8,128)(2,1)S(1)}, u32[]{:S(2)}, u32[]{:S(2)}) collective-permute-start(bf16[264,128]{1,0:T(8,128)(2,1)} %get-tuple-element.105), channel_id=1, source_target_pairs={{0,13},{1,12},{2,15},{3,14},{4,9},{5,8},{6,11},{7,10},{8,5},{9,4},... | collective-permute-start | bytes 202760 | tf_op jit(solution)/shard_map/ppermute | solution.py:416
  15.7 7.9 %collective-permute-start.6 = (bf16[264,128]{1,0:T(8,128)(2,1)}, bf16[264,128]{1,0:T(8,128)(2,1)S(1)}, u32[]{:S(2)}, u32[]{:S(2)}) collective-permute-start(bf16[264,128]{1,0:T(8,128)(2,1)} %get-tuple-element.106), channel_id=1, source_target_pairs={{0,2},{1,3},{2,0},{3,1},{4,6},{5,7},{6,4},{7,5},{8,10},{9,11},{10,... | collective-permute-start | bytes 202760 | tf_op jit(solution)/shard_map/ppermute | solution.py:416
  17.1 8.1 %collective-permute-start.7 = (bf16[264,128]{1,0:T(8,128)(2,1)}, bf16[264,128]{1,0:T(8,128)(2,1)S(1)}, u32[]{:S(2)}, u32[]{:S(2)}) collective-permute-start(bf16[264,128]{1,0:T(8,128)(2,1)} %get-tuple-element.107), channel_id=1, source_target_pairs={{0,10},{1,11},{2,8},{3,9},{4,14},{5,15},{6,12},{7,13},{8,2},{9,3},... | collective-permute-start | bytes 202760 | tf_op jit(solution)/shard_map/ppermute | solution.py:416
  19.6 6.9 %collective-permute-start.8 = (bf16[264,128]{1,0:T(8,128)(2,1)}, bf16[264,128]{1,0:T(8,128)(2,1)S(1)}, u32[]{:S(2)}, u32[]{:S(2)}) collective-permute-start(bf16[264,128]{1,0:T(8,128)(2,1)} %get-tuple-element.108), channel_id=1, source_target_pairs={{0,6},{1,7},{2,4},{3,5},{4,2},{5,3},{6,0},{7,1},{8,14},{9,15},{10,... | collective-permute-start | bytes 202760 | tf_op jit(solution)/shard_map/ppermute | solution.py:416
  21.3 7.9 %collective-permute-start.9 = (bf16[264,128]{1,0:T(8,128)(2,1)}, bf16[264,128]{1,0:T(8,128)(2,1)S(1)}, u32[]{:S(2)}, u32[]{:S(2)}) collective-permute-start(bf16[264,128]{1,0:T(8,128)(2,1)} %get-tuple-element.109), channel_id=1, source_target_pairs={{0,14},{1,15},{2,12},{3,13},{4,10},{5,11},{6,8},{7,9},{8,6},{9,7},... | collective-permute-start | bytes 202760 | tf_op jit(solution)/shard_map/ppermute | solution.py:416
  22.6 11.1 %collective-permute-start.10 = (bf16[264,128]{1,0:T(8,128)(2,1)}, bf16[264,128]{1,0:T(8,128)(2,1)S(1)}, u32[]{:S(2)}, u32[]{:S(2)}) collective-permute-start(bf16[264,128]{1,0:T(8,128)(2,1)} %get-tuple-element.110), channel_id=1, source_target_pairs={{0,3},{1,2},{2,1},{3,0},{4,7},{5,6},{6,5},{7,4},{8,11},{9,10},{10,... | collective-permute-start | bytes 202760 | tf_op jit(solution)/shard_map/ppermute | solution.py:416
  23.5 10.1 %collective-permute-start.11 = (bf16[264,128]{1,0:T(8,128)(2,1)}, bf16[264,128]{1,0:T(8,128)(2,1)S(1)}, u32[]{:S(2)}, u32[]{:S(2)}) collective-permute-start(bf16[264,128]{1,0:T(8,128)(2,1)} %get-tuple-element.111), channel_id=1, source_target_pairs={{0,11},{1,10},{2,9},{3,8},{4,15},{5,14},{6,13},{7,12},{8,3},{9,2},... | collective-permute-start | bytes 202760 | tf_op jit(solution)/shard_map/ppermute | solution.py:416
  25.2 8.5 %collective-permute-start.12 = (bf16[264,128]{1,0:T(8,128)(2,1)}, bf16[264,128]{1,0:T(8,128)(2,1)S(1)}, u32[]{:S(2)}, u32[]{:S(2)}) collective-permute-start(bf16[264,128]{1,0:T(8,128)(2,1)} %get-tuple-element.112), channel_id=1, source_target_pairs={{0,7},{1,6},{2,5},{3,4},{4,3},{5,2},{6,1},{7,0},{8,15},{9,14},{10,... | collective-permute-start | bytes 202760 | tf_op jit(solution)/shard_map/ppermute | solution.py:416
  26.5 7.2 %collective-permute-start.13 = (bf16[264,128]{1,0:T(8,128)(2,1)}, bf16[264,128]{1,0:T(8,128)(2,1)S(1)}, u32[]{:S(2)}, u32[]{:S(2)}) collective-permute-start(bf16[264,128]{1,0:T(8,128)(2,1)} %get-tuple-element.113), channel_id=1, source_target_pairs={{0,15},{1,14},{2,13},{3,12},{4,11},{5,10},{6,9},{7,8},{8,7},{9,6},... | collective-permute-start | bytes 202760 | tf_op jit(solution)/shard_map/ppermute | solution.py:416
  29.1 7.7 %collective-permute-start.14 = (bf16[264,128]{1,0:T(8,128)(2,1)}, bf16[264,128]{1,0:T(8,128)(2,1)S(1)}, u32[]{:S(2)}, u32[]{:S(2)}) collective-permute-start(bf16[264,128]{1,0:T(8,128)(2,1)} %get-tuple-element.114), channel_id=1, source_target_pairs={{0,8},{1,9},{2,10},{3,11},{4,12},{5,13},{6,14},{7,15},{8,0},{9,1},... | collective-permute-start | bytes 202760 | tf_op jit(solution)/shard_map/ppermute | solution.py:416
  39.3 6.7 %collective-permute-start.16 = (bf16[264,128]{1,0:T(8,128)(2,1)S(1)}, bf16[264,128]{1,0:T(8,128)(2,1)S(1)}, u32[]{:S(2)}, u32[]{:S(2)}) collective-permute-start(bf16[264,128]{1,0:T(8,128)(2,1)S(1)} %get-tuple-element.120), channel_id=1, source_target_pairs={{0,12},{1,13},{2,14},{3,15},{4,8},{5,9},{6,10},{7,11},{8,4},{9,5},... | collective-permute-start | bytes 202760 | tf_op jit(solution)/shard_map/ppermute | solution.py:416
  41.8 9.4 %collective-permute-start.18 = (bf16[264,128]{1,0:T(8,128)(2,1)S(1)}, bf16[264,128]{1,0:T(8,128)(2,1)S(1)}, u32[]{:S(2)}, u32[]{:S(2)}) collective-permute-start(bf16[264,128]{1,0:T(8,128)(2,1)S(1)} %get-tuple-element.122), channel_id=1, source_target_pairs={{0,9},{1,8},{2,11},{3,10},{4,13},{5,12},{6,15},{7,14},{8,1},{9,0},... | collective-permute-start | bytes 202760 | tf_op jit(solution)/shard_map/ppermute | solution.py:416
  42.9 8.2 %collective-permute-start.19 = (bf16[264,128]{1,0:T(8,128)(2,1)S(1)}, bf16[264,128]{1,0:T(8,128)(2,1)S(1)}, u32[]{:S(2)}, u32[]{:S(2)}) collective-permute-start(bf16[264,128]{1,0:T(8,128)(2,1)S(1)} %get-tuple-element.123), channel_id=1, source_target_pairs={{0,5},{1,4},{2,7},{3,6},{4,1},{5,0},{6,3},{7,2},{8,13},{9,12},{10,... | collective-permute-start | bytes 202760 | tf_op jit(solution)/shard_map/ppermute | solution.py:416
  43.6 10.1 %collective-permute-start.20 = (bf16[264,128]{1,0:T(8,128)(2,1)S(1)}, bf16[264,128]{1,0:T(8,128)(2,1)S(1)}, u32[]{:S(2)}, u32[]{:S(2)}) collective-permute-start(bf16[264,128]{1,0:T(8,128)(2,1)S(1)} %get-tuple-element.124), channel_id=1, source_target_pairs={{0,13},{1,12},{2,15},{3,14},{4,9},{5,8},{6,11},{7,10},{8,5},{9,4},... | collective-permute-start | bytes 202760 | tf_op jit(solution)/shard_map/ppermute | solution.py:416
  46.0 8.8 %collective-permute-start.21 = (bf16[264,128]{1,0:T(8,128)(2,1)S(1)}, bf16[264,128]{1,0:T(8,128)(2,1)S(1)}, u32[]{:S(2)}, u32[]{:S(2)}) collective-permute-start(bf16[264,128]{1,0:T(8,128)(2,1)S(1)} %get-tuple-element.125), channel_id=1, source_target_pairs={{0,2},{1,3},{2,0},{3,1},{4,6},{5,7},{6,4},{7,5},{8,10},{9,11},{10,... | collective-permute-start | bytes 202760 | tf_op jit(solution)/shard_map/ppermute | solution.py:416
  47.2 9.5 %collective-permute-start.22 = (bf16[264,128]{1,0:T(8,128)(2,1)S(1)}, bf16[264,128]{1,0:T(8,128)(2,1)S(1)}, u32[]{:S(2)}, u32[]{:S(2)}) collective-permute-start(bf16[264,128]{1,0:T(8,128)(2,1)S(1)} %get-tuple-element.126), channel_id=1, source_target_pairs={{0,10},{1,11},{2,8},{3,9},{4,14},{5,15},{6,12},{7,13},{8,2},{9,3},... | collective-permute-start | bytes 202760 | tf_op jit(solution)/shard_map/ppermute | solution.py:416
  51.1 6.5 %collective-permute-start.23 = (bf16[264,128]{1,0:T(8,128)(2,1)S(1)}, bf16[264,128]{1,0:T(8,128)(2,1)S(1)}, u32[]{:S(2)}, u32[]{:S(2)}) collective-permute-start(bf16[264,128]{1,0:T(8,128)(2,1)S(1)} %get-tuple-element.127), channel_id=1, source_target_pairs={{0,6},{1,7},{2,4},{3,5},{4,2},{5,3},{6,0},{7,1},{8,14},{9,15},{10,... | collective-permute-start | bytes 202760 | tf_op jit(solution)/shard_map/ppermute | solution.py:416
  51.1 8.8 %collective-permute-start.24 = (bf16[264,128]{1,0:T(8,128)(2,1)S(1)}, bf16[264,128]{1,0:T(8,128)(2,1)S(1)}, u32[]{:S(2)}, u32[]{:S(2)}) collective-permute-start(bf16[264,128]{1,0:T(8,128)(2,1)S(1)} %get-tuple-element.128), channel_id=1, source_target_pairs={{0,14},{1,15},{2,12},{3,13},{4,10},{5,11},{6,8},{7,9},{8,6},{9,7},... | collective-permute-start | bytes 202760 | tf_op jit(solution)/shard_map/ppermute | solution.py:416
  53.7 8.7 %collective-permute-start.25 = (bf16[264,128]{1,0:T(8,128)(2,1)S(1)}, bf16[264,128]{1,0:T(8,128)(2,1)S(1)}, u32[]{:S(2)}, u32[]{:S(2)}) collective-permute-start(bf16[264,128]{1,0:T(8,128)(2,1)S(1)} %get-tuple-element.129), channel_id=1, source_target_pairs={{0,3},{1,2},{2,1},{3,0},{4,7},{5,6},{6,5},{7,4},{8,11},{9,10},{10,... | collective-permute-start | bytes 202760 | tf_op jit(solution)/shard_map/ppermute | solution.py:416
  54.8 7.7 %collective-permute-start.26 = (bf16[264,128]{1,0:T(8,128)(2,1)S(1)}, bf16[264,128]{1,0:T(8,128)(2,1)S(1)}, u32[]{:S(2)}, u32[]{:S(2)}) collective-permute-start(bf16[264,128]{1,0:T(8,128)(2,1)S(1)} %get-tuple-element.130), channel_id=1, source_target_pairs={{0,11},{1,10},{2,9},{3,8},{4,15},{5,14},{6,13},{7,12},{8,3},{9,2},... | collective-permute-start | bytes 202760 | tf_op jit(solution)/shard_map/ppermute | solution.py:416
  57.6 6.9 %collective-permute-start.28 = (bf16[264,128]{1,0:T(8,128)(2,1)S(1)}, bf16[264,128]{1,0:T(8,128)(2,1)S(1)}, u32[]{:S(2)}, u32[]{:S(2)}) collective-permute-start(bf16[264,128]{1,0:T(8,128)(2,1)S(1)} %get-tuple-element.132), channel_id=1, source_target_pairs={{0,15},{1,14},{2,13},{3,12},{4,11},{5,10},{6,9},{7,8},{8,7},{9,6},... | collective-permute-start | bytes 202760 | tf_op jit(solution)/shard_map/ppermute | solution.py:416
  59.9 8.0 %collective-permute-start.29 = (bf16[264,128]{1,0:T(8,128)(2,1)S(1)}, bf16[264,128]{1,0:T(8,128)(2,1)S(1)}, u32[]{:S(2)}, u32[]{:S(2)}) collective-permute-start(bf16[264,128]{1,0:T(8,128)(2,1)S(1)} %get-tuple-element.133), channel_id=1, source_target_pairs={{0,8},{1,9},{2,10},{3,11},{4,12},{5,13},{6,14},{7,15},{8,0},{9,1},... | collective-permute-start | bytes 202760 | tf_op jit(solution)/shard_map/ppermute | solution.py:416
  71.5 6.4 %collective-permute-start.31 = (bf16[264,128]{1,0:T(8,128)(2,1)S(1)}, bf16[264,128]{1,0:T(8,128)(2,1)S(1)}, u32[]{:S(2)}, u32[]{:S(2)}) collective-permute-start(bf16[264,128]{1,0:T(8,128)(2,1)S(1)} %get-tuple-element.138), channel_id=1, source_target_pairs={{0,12},{1,13},{2,14},{3,15},{4,8},{5,9},{6,10},{7,11},{8,4},{9,5},... | collective-permute-start | bytes 202760 | tf_op jit(solution)/shard_map/ppermute | solution.py:416
  73.7 8.9 %collective-permute-start.33 = (bf16[264,128]{1,0:T(8,128)(2,1)S(1)}, bf16[264,128]{1,0:T(8,128)(2,1)S(1)}, u32[]{:S(2)}, u32[]{:S(2)}) collective-permute-start(bf16[264,128]{1,0:T(8,128)(2,1)S(1)} %get-tuple-element.140), channel_id=1, source_target_pairs={{0,9},{1,8},{2,11},{3,10},{4,13},{5,12},{6,15},{7,14},{8,1},{9,0},... | collective-permute-start | bytes 202760 | tf_op jit(solution)/shard_map/ppermute | solution.py:416
  75.1 7.7 %collective-permute-start.34 = (bf16[264,128]{1,0:T(8,128)(2,1)S(1)}, bf16[264,128]{1,0:T(8,128)(2,1)S(1)}, u32[]{:S(2)}, u32[]{:S(2)}) collective-permute-start(bf16[264,128]{1,0:T(8,128)(2,1)S(1)} %get-tuple-element.141), channel_id=1, source_target_pairs={{0,5},{1,4},{2,7},{3,6},{4,1},{5,0},{6,3},{7,2},{8,13},{9,12},{10,... | collective-permute-start | bytes 202760 | tf_op jit(solution)/shard_map/ppermute | solution.py:416
  75.8 9.1 %collective-permute-start.35 = (bf16[264,128]{1,0:T(8,128)(2,1)S(1)}, bf16[264,128]{1,0:T(8,128)(2,1)S(1)}, u32[]{:S(2)}, u32[]{:S(2)}) collective-permute-start(bf16[264,128]{1,0:T(8,128)(2,1)S(1)} %get-tuple-element.142), channel_id=1, source_target_pairs={{0,13},{1,12},{2,15},{3,14},{4,9},{5,8},{6,11},{7,10},{8,5},{9,4},... | collective-permute-start | bytes 202760 | tf_op jit(solution)/shard_map/ppermute | solution.py:416
  77.9 8.3 %collective-permute-start.36 = (bf16[264,128]{1,0:T(8,128)(2,1)S(1)}, bf16[264,128]{1,0:T(8,128)(2,1)S(1)}, u32[]{:S(2)}, u32[]{:S(2)}) collective-permute-start(bf16[264,128]{1,0:T(8,128)(2,1)S(1)} %get-tuple-element.143), channel_id=1, source_target_pairs={{0,2},{1,3},{2,0},{3,1},{4,6},{5,7},{6,4},{7,5},{8,10},{9,11},{10,... | collective-permute-start | bytes 202760 | tf_op jit(solution)/shard_map/ppermute | solution.py:416
  78.6 9.5 %collective-permute-start.37 = (bf16[264,128]{1,0:T(8,128)(2,1)S(1)}, bf16[264,128]{1,0:T(8,128)(2,1)S(1)}, u32[]{:S(2)}, u32[]{:S(2)}) collective-permute-start(bf16[264,128]{1,0:T(8,128)(2,1)S(1)} %get-tuple-element.144), channel_id=1, source_target_pairs={{0,10},{1,11},{2,8},{3,9},{4,14},{5,15},{6,12},{7,13},{8,2},{9,3},... | collective-permute-start | bytes 202760 | tf_op jit(solution)/shard_map/ppermute | solution.py:416
  82.5 6.5 %collective-permute-start.38 = (bf16[264,128]{1,0:T(8,128)(2,1)S(1)}, bf16[264,128]{1,0:T(8,128)(2,1)S(1)}, u32[]{:S(2)}, u32[]{:S(2)}) collective-permute-start(bf16[264,128]{1,0:T(8,128)(2,1)S(1)} %get-tuple-element.145), channel_id=1, source_target_pairs={{0,6},{1,7},{2,4},{3,5},{4,2},{5,3},{6,0},{7,1},{8,14},{9,15},{10,... | collective-permute-start | bytes 202760 | tf_op jit(solution)/shard_map/ppermute | solution.py:416
  82.8 8.3 %collective-permute-start.39 = (bf16[264,128]{1,0:T(8,128)(2,1)S(1)}, bf16[264,128]{1,0:T(8,128)(2,1)S(1)}, u32[]{:S(2)}, u32[]{:S(2)}) collective-permute-start(bf16[264,128]{1,0:T(8,128)(2,1)S(1)} %get-tuple-element.146), channel_id=1, source_target_pairs={{0,14},{1,15},{2,12},{3,13},{4,10},{5,11},{6,8},{7,9},{8,6},{9,7},... | collective-permute-start | bytes 202760 | tf_op jit(solution)/shard_map/ppermute | solution.py:416
  84.9 7.8 %collective-permute-start.40 = (bf16[264,128]{1,0:T(8,128)(2,1)S(1)}, bf16[264,128]{1,0:T(8,128)(2,1)S(1)}, u32[]{:S(2)}, u32[]{:S(2)}) collective-permute-start(bf16[264,128]{1,0:T(8,128)(2,1)S(1)} %get-tuple-element.147), channel_id=1, source_target_pairs={{0,3},{1,2},{2,1},{3,0},{4,7},{5,6},{6,5},{7,4},{8,11},{9,10},{10,... | collective-permute-start | bytes 202760 | tf_op jit(solution)/shard_map/ppermute | solution.py:416
  86.2 8.2 %collective-permute-start.41 = (bf16[264,128]{1,0:T(8,128)(2,1)S(1)}, bf16[264,128]{1,0:T(8,128)(2,1)S(1)}, u32[]{:S(2)}, u32[]{:S(2)}) collective-permute-start(bf16[264,128]{1,0:T(8,128)(2,1)S(1)} %get-tuple-element.148), channel_id=1, source_target_pairs={{0,11},{1,10},{2,9},{3,8},{4,15},{5,14},{6,13},{7,12},{8,3},{9,2},... | collective-permute-start | bytes 202760 | tf_op jit(solution)/shard_map/ppermute | solution.py:416
  88.1 6.4 %collective-permute-start.42 = (bf16[264,128]{1,0:T(8,128)(2,1)S(1)}, bf16[264,128]{1,0:T(8,128)(2,1)S(1)}, u32[]{:S(2)}, u32[]{:S(2)}) collective-permute-start(bf16[264,128]{1,0:T(8,128)(2,1)S(1)} %get-tuple-element.149), channel_id=1, source_target_pairs={{0,7},{1,6},{2,5},{3,4},{4,3},{5,2},{6,1},{7,0},{8,15},{9,14},{10,... | collective-permute-start | bytes 202760 | tf_op jit(solution)/shard_map/ppermute | solution.py:416
  89.1 7.0 %collective-permute-start.43 = (bf16[264,128]{1,0:T(8,128)(2,1)S(1)}, bf16[264,128]{1,0:T(8,128)(2,1)S(1)}, u32[]{:S(2)}, u32[]{:S(2)}) collective-permute-start(bf16[264,128]{1,0:T(8,128)(2,1)S(1)} %get-tuple-element.150), channel_id=1, source_target_pairs={{0,15},{1,14},{2,13},{3,12},{4,11},{5,10},{6,9},{7,8},{8,7},{9,6},... | collective-permute-start | bytes 202760 | tf_op jit(solution)/shard_map/ppermute | solution.py:416
  91.1 8.4 %collective-permute-start.44 = (bf16[264,128]{1,0:T(8,128)(2,1)S(1)}, bf16[264,128]{1,0:T(8,128)(2,1)S(1)}, u32[]{:S(2)}, u32[]{:S(2)}) collective-permute-start(bf16[264,128]{1,0:T(8,128)(2,1)S(1)} %get-tuple-element.151), channel_id=1, source_target_pairs={{0,8},{1,9},{2,10},{3,11},{4,12},{5,13},{6,14},{7,15},{8,0},{9,1},... | collective-permute-start | bytes 202760 | tf_op jit(solution)/shard_map/ppermute | solution.py:416
  101.9 6.4 %collective-permute-start.46 = (bf16[264,128]{1,0:T(8,128)(2,1)S(1)}, bf16[264,128]{1,0:T(8,128)(2,1)S(1)}, u32[]{:S(2)}, u32[]{:S(2)}) collective-permute-start(bf16[264,128]{1,0:T(8,128)(2,1)S(1)} %get-tuple-element.156), channel_id=1, source_target_pairs={{0,12},{1,13},{2,14},{3,15},{4,8},{5,9},{6,10},{7,11},{8,4},{9,5},... | collective-permute-start | bytes 202760 | tf_op jit(solution)/shard_map/ppermute | solution.py:416
  104.0 9.0 %collective-permute-start.48 = (bf16[264,128]{1,0:T(8,128)(2,1)S(1)}, bf16[264,128]{1,0:T(8,128)(2,1)S(1)}, u32[]{:S(2)}, u32[]{:S(2)}) collective-permute-start(bf16[264,128]{1,0:T(8,128)(2,1)S(1)} %get-tuple-element.158), channel_id=1, source_target_pairs={{0,9},{1,8},{2,11},{3,10},{4,13},{5,12},{6,15},{7,14},{8,1},{9,0},... | collective-permute-start | bytes 202760 | tf_op jit(solution)/shard_map/ppermute | solution.py:416
  105.5 8.0 %collective-permute-start.49 = (bf16[264,128]{1,0:T(8,128)(2,1)S(1)}, bf16[264,128]{1,0:T(8,128)(2,1)S(1)}, u32[]{:S(2)}, u32[]{:S(2)}) collective-permute-start(bf16[264,128]{1,0:T(8,128)(2,1)S(1)} %get-tuple-element.159), channel_id=1, source_target_pairs={{0,5},{1,4},{2,7},{3,6},{4,1},{5,0},{6,3},{7,2},{8,13},{9,12},{10,... | collective-permute-start | bytes 202760 | tf_op jit(solution)/shard_map/ppermute | solution.py:416
  106.1 9.5 %collective-permute-start.50 = (bf16[264,128]{1,0:T(8,128)(2,1)S(1)}, bf16[264,128]{1,0:T(8,128)(2,1)S(1)}, u32[]{:S(2)}, u32[]{:S(2)}) collective-permute-start(bf16[264,128]{1,0:T(8,128)(2,1)S(1)} %get-tuple-element.160), channel_id=1, source_target_pairs={{0,13},{1,12},{2,15},{3,14},{4,9},{5,8},{6,11},{7,10},{8,5},{9,4},... | collective-permute-start | bytes 202760 | tf_op jit(solution)/shard_map/ppermute | solution.py:416
  108.2 8.4 %collective-permute-start.51 = (bf16[264,128]{1,0:T(8,128)(2,1)S(1)}, bf16[264,128]{1,0:T(8,128)(2,1)S(1)}, u32[]{:S(2)}, u32[]{:S(2)}) collective-permute-start(bf16[264,128]{1,0:T(8,128)(2,1)S(1)} %get-tuple-element.161), channel_id=1, source_target_pairs={{0,2},{1,3},{2,0},{3,1},{4,6},{5,7},{6,4},{7,5},{8,10},{9,11},{10,... | collective-permute-start | bytes 202760 | tf_op jit(solution)/shard_map/ppermute | solution.py:416
  109.4 9.2 %collective-permute-start.52 = (bf16[264,128]{1,0:T(8,128)(2,1)S(1)}, bf16[264,128]{1,0:T(8,128)(2,1)S(1)}, u32[]{:S(2)}, u32[]{:S(2)}) collective-permute-start(bf16[264,128]{1,0:T(8,128)(2,1)S(1)} %get-tuple-element.162), channel_id=1, source_target_pairs={{0,10},{1,11},{2,8},{3,9},{4,14},{5,15},{6,12},{7,13},{8,2},{9,3},... | collective-permute-start | bytes 202760 | tf_op jit(solution)/shard_map/ppermute | solution.py:416
  113.0 6.4 %collective-permute-start.53 = (bf16[264,128]{1,0:T(8,128)(2,1)S(1)}, bf16[264,128]{1,0:T(8,128)(2,1)S(1)}, u32[]{:S(2)}, u32[]{:S(2)}) collective-permute-start(bf16[264,128]{1,0:T(8,128)(2,1)S(1)} %get-tuple-element.163), channel_id=1, source_target_pairs={{0,6},{1,7},{2,4},{3,5},{4,2},{5,3},{6,0},{7,1},{8,14},{9,15},{10,... | collective-permute-start | bytes 202760 | tf_op jit(solution)/shard_map/ppermute | solution.py:416
  113.5 8.4 %collective-permute-start.54 = (bf16[264,128]{1,0:T(8,128)(2,1)S(1)}, bf16[264,128]{1,0:T(8,128)(2,1)S(1)}, u32[]{:S(2)}, u32[]{:S(2)}) collective-permute-start(bf16[264,128]{1,0:T(8,128)(2,1)S(1)} %get-tuple-element.164), channel_id=1, source_target_pairs={{0,14},{1,15},{2,12},{3,13},{4,10},{5,11},{6,8},{7,9},{8,6},{9,7},... | collective-permute-start | bytes 202760 | tf_op jit(solution)/shard_map/ppermute | solution.py:416
  115.7 7.6 %collective-permute-start.55 = (bf16[264,128]{1,0:T(8,128)(2,1)S(1)}, bf16[264,128]{1,0:T(8,128)(2,1)S(1)}, u32[]{:S(2)}, u32[]{:S(2)}) collective-permute-start(bf16[264,128]{1,0:T(8,128)(2,1)S(1)} %get-tuple-element.165), channel_id=1, source_target_pairs={{0,3},{1,2},{2,1},{3,0},{4,7},{5,6},{6,5},{7,4},{8,11},{9,10},{10,... | collective-permute-start | bytes 202760 | tf_op jit(solution)/shard_map/ppermute | solution.py:416
  116.7 8.1 %collective-permute-start.56 = (bf16[264,128]{1,0:T(8,128)(2,1)S(1)}, bf16[264,128]{1,0:T(8,128)(2,1)S(1)}, u32[]{:S(2)}, u32[]{:S(2)}) collective-permute-start(bf16[264,128]{1,0:T(8,128)(2,1)S(1)} %get-tuple-element.166), channel_id=1, source_target_pairs={{0,11},{1,10},{2,9},{3,8},{4,15},{5,14},{6,13},{7,12},{8,3},{9,2},... | collective-permute-start | bytes 202760 | tf_op jit(solution)/shard_map/ppermute | solution.py:416
  118.6 6.2 %collective-permute-start.57 = (bf16[264,128]{1,0:T(8,128)(2,1)S(1)}, bf16[264,128]{1,0:T(8,128)(2,1)S(1)}, u32[]{:S(2)}, u32[]{:S(2)}) collective-permute-start(bf16[264,128]{1,0:T(8,128)(2,1)S(1)} %get-tuple-element.167), channel_id=1, source_target_pairs={{0,7},{1,6},{2,5},{3,4},{4,3},{5,2},{6,1},{7,0},{8,15},{9,14},{10,... | collective-permute-start | bytes 202760 | tf_op jit(solution)/shard_map/ppermute | solution.py:416
  119.3 7.1 %collective-permute-start.58 = (bf16[264,128]{1,0:T(8,128)(2,1)S(1)}, bf16[264,128]{1,0:T(8,128)(2,1)S(1)}, u32[]{:S(2)}, u32[]{:S(2)}) collective-permute-start(bf16[264,128]{1,0:T(8,128)(2,1)S(1)} %get-tuple-element.168), channel_id=1, source_target_pairs={{0,15},{1,14},{2,13},{3,12},{4,11},{5,10},{6,9},{7,8},{8,7},{9,6},... | collective-permute-start | bytes 202760 | tf_op jit(solution)/shard_map/ppermute | solution.py:416
  121.9 8.1 %collective-permute-start.59 = (bf16[264,128]{1,0:T(8,128)(2,1)S(1)}, bf16[264,128]{1,0:T(8,128)(2,1)S(1)}, u32[]{:S(2)}, u32[]{:S(2)}) collective-permute-start(bf16[264,128]{1,0:T(8,128)(2,1)S(1)} %get-tuple-element.169), channel_id=1, source_target_pairs={{0,8},{1,9},{2,10},{3,11},{4,12},{5,13},{6,14},{7,15},{8,0},{9,1},... | collective-permute-start | bytes 202760 | tf_op jit(solution)/shard_map/ppermute | solution.py:416
  135.5 9.1 %collective-permute-start.63 = (bf16[264,128]{1,0:T(8,128)(2,1)S(1)}, bf16[264,128]{1,0:T(8,128)(2,1)S(1)}, u32[]{:S(2)}, u32[]{:S(2)}) collective-permute-start(bf16[264,128]{1,0:T(8,128)(2,1)S(1)} %get-tuple-element.177), channel_id=1, source_target_pairs={{0,9},{1,8},{2,11},{3,10},{4,13},{5,12},{6,15},{7,14},{8,1},{9,0},... | collective-permute-start | bytes 202760 | tf_op jit(solution)/shard_map/ppermute | solution.py:416
  137.1 7.5 %collective-permute-start.64 = (bf16[264,128]{1,0:T(8,128)(2,1)S(1)}, bf16[264,128]{1,0:T(8,128)(2,1)S(1)}, u32[]{:S(2)}, u32[]{:S(2)}) collective-permute-start(bf16[264,128]{1,0:T(8,128)(2,1)S(1)} %get-tuple-element.178), channel_id=1, source_target_pairs={{0,5},{1,4},{2,7},{3,6},{4,1},{5,0},{6,3},{7,2},{8,13},{9,12},{10,... | collective-permute-start | bytes 202760 | tf_op jit(solution)/shard_map/ppermute | solution.py:416
  137.8 9.5 %collective-permute-start.65 = (bf16[264,128]{1,0:T(8,128)(2,1)S(1)}, bf16[264,128]{1,0:T(8,128)(2,1)S(1)}, u32[]{:S(2)}, u32[]{:S(2)}) collective-permute-start(bf16[264,128]{1,0:T(8,128)(2,1)S(1)} %get-tuple-element.179), channel_id=1, source_target_pairs={{0,13},{1,12},{2,15},{3,14},{4,9},{5,8},{6,11},{7,10},{8,5},{9,4},... | collective-permute-start | bytes 202760 | tf_op jit(solution)/shard_map/ppermute | solution.py:416
  139.8 8.5 %collective-permute-start.66 = (bf16[264,128]{1,0:T(8,128)(2,1)S(1)}, bf16[264,128]{1,0:T(8,128)(2,1)S(1)}, u32[]{:S(2)}, u32[]{:S(2)}) collective-permute-start(bf16[264,128]{1,0:T(8,128)(2,1)S(1)} %get-tuple-element.180), channel_id=1, source_target_pairs={{0,2},{1,3},{2,0},{3,1},{4,6},{5,7},{6,4},{7,5},{8,10},{9,11},{10,... | collective-permute-start | bytes 202760 | tf_op jit(solution)/shard_map/ppermute | solution.py:416
  141.0 9.2 %collective-permute-start.67 = (bf16[264,128]{1,0:T(8,128)(2,1)S(1)}, bf16[264,128]{1,0:T(8,128)(2,1)S(1)}, u32[]{:S(2)}, u32[]{:S(2)}) collective-permute-start(bf16[264,128]{1,0:T(8,128)(2,1)S(1)} %get-tuple-element.181), channel_id=1, source_target_pairs={{0,10},{1,11},{2,8},{3,9},{4,14},{5,15},{6,12},{7,13},{8,2},{9,3},... | collective-permute-start | bytes 202760 | tf_op jit(solution)/shard_map/ppermute | solution.py:416
  144.6 6.6 %collective-permute-start.68 = (bf16[264,128]{1,0:T(8,128)(2,1)S(1)}, bf16[264,128]{1,0:T(8,128)(2,1)S(1)}, u32[]{:S(2)}, u32[]{:S(2)}) collective-permute-start(bf16[264,128]{1,0:T(8,128)(2,1)S(1)} %get-tuple-element.182), channel_id=1, source_target_pairs={{0,6},{1,7},{2,4},{3,5},{4,2},{5,3},{6,0},{7,1},{8,14},{9,15},{10,... | collective-permute-start | bytes 202760 | tf_op jit(solution)/shard_map/ppermute | solution.py:416
  144.6 8.9 %collective-permute-start.69 = (bf16[264,128]{1,0:T(8,128)(2,1)S(1)}, bf16[264,128]{1,0:T(8,128)(2,1)S(1)}, u32[]{:S(2)}, u32[]{:S(2)}) collective-permute-start(bf16[264,128]{1,0:T(8,128)(2,1)S(1)} %get-tuple-element.183), channel_id=1, source_target_pairs={{0,14},{1,15},{2,12},{3,13},{4,10},{5,11},{6,8},{7,9},{8,6},{9,7},... | collective-permute-start | bytes 202760 | tf_op jit(solution)/shard_map/ppermute | solution.py:416
  147.3 9.6 %collective-permute-start.70 = (bf16[264,128]{1,0:T(8,128)(2,1)S(1)}, bf16[264,128]{1,0:T(8,128)(2,1)S(1)}, u32[]{:S(2)}, u32[]{:S(2)}) collective-permute-start(bf16[264,128]{1,0:T(8,128)(2,1)S(1)} %get-tuple-element.184), channel_id=1, source_target_pairs={{0,3},{1,2},{2,1},{3,0},{4,7},{5,6},{6,5},{7,4},{8,11},{9,10},{10,... | collective-permute-start | bytes 202760 | tf_op jit(solution)/shard_map/ppermute | solution.py:416
  148.3 8.6 %collective-permute-start.71 = (bf16[264,128]{1,0:T(8,128)(2,1)S(1)}, bf16[264,128]{1,0:T(8,128)(2,1)S(1)}, u32[]{:S(2)}, u32[]{:S(2)}) collective-permute-start(bf16[264,128]{1,0:T(8,128)(2,1)S(1)} %get-tuple-element.185), channel_id=1, source_target_pairs={{0,11},{1,10},{2,9},{3,8},{4,15},{5,14},{6,13},{7,12},{8,3},{9,2},... | collective-permute-start | bytes 202760 | tf_op jit(solution)/shard_map/ppermute | solution.py:416
  150.2 6.7 %collective-permute-start.72 = (bf16[264,128]{1,0:T(8,128)(2,1)S(1)}, bf16[264,128]{1,0:T(8,128)(2,1)S(1)}, u32[]{:S(2)}, u32[]{:S(2)}) collective-permute-start(bf16[264,128]{1,0:T(8,128)(2,1)S(1)} %get-tuple-element.186), channel_id=1, source_target_pairs={{0,7},{1,6},{2,5},{3,4},{4,3},{5,2},{6,1},{7,0},{8,15},{9,14},{10,... | collective-permute-start | bytes 202760 | tf_op jit(solution)/shard_map/ppermute | solution.py:416
  151.2 7.1 %collective-permute-start.73 = (bf16[264,128]{1,0:T(8,128)(2,1)S(1)}, bf16[264,128]{1,0:T(8,128)(2,1)S(1)}, u32[]{:S(2)}, u32[]{:S(2)}) collective-permute-start(bf16[264,128]{1,0:T(8,128)(2,1)S(1)} %get-tuple-element.187), channel_id=1, source_target_pairs={{0,15},{1,14},{2,13},{3,12},{4,11},{5,10},{6,9},{7,8},{8,7},{9,6},... | collective-permute-start | bytes 202760 | tf_op jit(solution)/shard_map/ppermute | solution.py:416
  153.5 8.1 %collective-permute-start.74 = (bf16[264,128]{1,0:T(8,128)(2,1)S(1)}, bf16[264,128]{1,0:T(8,128)(2,1)S(1)}, u32[]{:S(2)}, u32[]{:S(2)}) collective-permute-start(bf16[264,128]{1,0:T(8,128)(2,1)S(1)} %get-tuple-element.188), channel_id=1, source_target_pairs={{0,8},{1,9},{2,10},{3,11},{4,12},{5,13},{6,14},{7,15},{8,0},{9,1},... | collective-permute-start | bytes 202760 | tf_op jit(solution)/shard_map/ppermute | solution.py:416
  (20 other events, 119.8 us)
